TPU v7x, 32 devices: a whole 2x2x4 slice. The times are simulated.
32 devices in a mesh: gx: 8 (over z, x), gy: 4 (over y, core).
Axes of the slice: x: 2, y: 2, z: 4, core: 2. Of those that a mesh axis runs over, the one named last changes fastest.
Arguments:
- source: float32 [8, 32, 64, 128], P(None, 'gx', 'gy'), may hold values from -30 to 30
- reaction: float32 [32, 64, 128], P('gx', 'gy'), may hold values from 0.02 to 2
- shifts: float32 [8], replicated, may hold values from 0.05 to 2
- shift_index: int32 [8], replicated, may hold values from 0 to 7, each once
- velocity: float32 [3], replicated, may hold values from -2 to 2
Outputs:
- solution: float32 [8, 32, 64, 128], P(None, 'gx', 'gy')
- residual: float32 [8, 32, 64, 128], P(None, 'gx', 'gy')
- residual_rms: float32 [8], replicated
Inputs may be any that keep to these rules, and one draw needn't show every extreme that they name: `shift_index`: each column takes a different shift.
All inputs are finite; a program needn't handle non-finite values.
Results may differ from a plain program's by a relative error of at most 0.00021.
Values sent between devices are 32-bit elements; how exact they have to be, the bound alone decides.
No kernel may reach another device: no remote copies, remote signals or barrier semaphores. Data moves between devices by JAX's collectives and lax.ppermute only.
A program may use at most 64 MiB of HBM per device.

v0:
```python
import jax
import jax.numpy as jnp
from jax import lax
from jax.sharding import PartitionSpec as P

LEVELS = 3
COARSE_SWEEPS = 6


DAMPING = 0.8
EPSILON = 1e-06


def with_halo(x, sides, width):
    for axis, dim in sides:
        peers, length = (lax.axis_size(axis), x.shape[dim])
        up = [(i, (i + 1) % peers) for i in range(peers - 1)]
        down = [(j, i) for i, j in up]
        last = lax.slice_in_dim(x, length - width, length, axis=dim)
        leading = lax.slice_in_dim(x, 0, width, axis=dim)
        before = lax.ppermute(last, axis, up)
        after = lax.ppermute(leading, axis, down)
        x = jnp.concatenate([before, x, after], axis=dim)
    return x


def select_shifts(shifts, shift_index):
    columns = jnp.arange(shifts.shape[0], dtype=jnp.int32)
    picked = jnp.where(shift_index[:, None] == columns[None, :], shifts[None, :], 0.0)
    return jnp.sum(picked, axis=1)


def coefficients(velocity, spacing):
    scale_a = 1.0 / (spacing * spacing)
    backward = scale_a + jnp.maximum(velocity, 0.0) / spacing
    forward = scale_a - jnp.minimum(velocity, 0.0) / spacing
    centre = 6.0 * scale_a + jnp.sum(jnp.abs(velocity)) / spacing
    return (backward, forward, centre)


def apply_stencil(padded, backward, forward, diagonal):
    middle = padded[:, 1:-1, 1:-1, :]
    along_z = jnp.pad(middle, ((0, 0), (0, 0), (0, 0), (1, 1)))
    others = backward[0] * padded[:, :-2, 1:-1, :] + forward[0] * padded[:, 2:, 1:-1, :]
    others = others + backward[1] * padded[:, 1:-1, :-2, :] + forward[1] * padded[:, 1:-1, 2:, :]
    others = others + backward[2] * along_z[:, :, :, :-2] + forward[2] * along_z[:, :, :, 2:]
    return diagonal * middle - others


def face_halo(iterate):
    return with_halo(iterate, (("gx", 1), ("gy", 2)), 1)


def coarsen(values):
    count, size_x, size_y, size_z = values.shape
    blocks = values.reshape(count, size_x // 2, 2, size_y // 2, 2, size_z // 2, 2)
    return jnp.sum(blocks, axis=(2, 4, 6)) * 0.125


def refine(values):
    return jnp.repeat(jnp.repeat(jnp.repeat(values, 2, 1), 2, 2), 2, 3)


def coarsest_solve(rhs_field, backward, forward, diagonal):
    iterate = DAMPING * rhs_field / diagonal
    for repeat in range(COARSE_SWEEPS - 1):
        applied = apply_stencil(face_halo(iterate), backward, forward, diagonal)
        iterate = iterate + DAMPING * (rhs_field - applied) / diagonal
    return iterate


def multigrid_cycle(level_index, rhs_field, reaction_l, shift_value, velocity):
    backward, forward, centre = coefficients(velocity, 2.0**level_index)
    diagonal = centre + reaction_l + shift_value[:, None, None, None]
    if level_index == LEVELS - 1:
        return coarsest_solve(rhs_field, backward, forward, diagonal)

    def operate(iterate):
        return apply_stencil(face_halo(iterate), backward, forward, diagonal)

    def smooth_step(iterate):
        return iterate + DAMPING * (rhs_field - operate(iterate)) / diagonal

    iterate = DAMPING * rhs_field / diagonal
    iterate = smooth_step(iterate)
    defect = rhs_field - operate(iterate)
    correction = multigrid_cycle(
        level_index + 1, coarsen(defect), coarsen(reaction_l), shift_value, velocity
    )
    iterate = iterate + refine(correction)
    iterate = smooth_step(iterate)
    iterate = smooth_step(iterate)
    return iterate


def body(source, reaction, shifts, shift_index, velocity):
    columns, cells_x, cells_y, cells_z = source.shape
    shift_value = select_shifts(shifts, shift_index)
    reaction_top = reaction[None]
    backward, forward, centre = coefficients(velocity, 1.0)
    diagonal = centre + reaction_top + shift_value[:, None, None, None]

    def operate(iterate):
        return apply_stencil(face_halo(iterate), backward, forward, diagonal)

    def smooth_step(iterate):
        return iterate + DAMPING * (source - operate(iterate)) / diagonal

    iterate = DAMPING * source / diagonal
    iterate = smooth_step(iterate)
    defect = source - operate(iterate)
    correction = multigrid_cycle(1, coarsen(defect), coarsen(reaction_top), shift_value, velocity)
    iterate = iterate + refine(correction)
    iterate = smooth_step(iterate)
    iterate = smooth_step(iterate)
    residual = source - operate(iterate)
    local_squares = jnp.sum(residual * residual, axis=(1, 2, 3))
    squares = lax.psum(local_squares, ("gx", "gy"))
    total_cells = cells_x * cells_y * cells_z * lax.axis_size("gx") * lax.axis_size("gy")
    residual_rms = jnp.sqrt(squares / total_cells + EPSILON)
    return (iterate, residual, residual_rms)


def solution(mesh):
    return jax.shard_map(
        body,
        mesh=mesh,
        in_specs=(P(None, "gx", "gy", None), P("gx", "gy", None), P(), P(), P()),
        out_specs=(P(None, "gx", "gy", None), P(None, "gx", "gy", None), P()),
        check_vma=False,
    )
```

profile of v0, /device:TPU:0, one launch (start us, length us, event | category | flops | bytes accessed | tf_op | source)
XLA Modules:
  0.0 342.3 jit_solution(17706087928771465481)
XLA Ops:
  5.3 4.8 %collective-permute-start = (f32[8,1,16,128]{3,2,1,0:T(8,128)S(1)}, f32[8,1,16,128]{3,2,1,0:T(8,128)S(1)}, u32[]{:S(2)}, u32[]{:S(2)}) collective-permute-start(f32[8,1,16,128]{3,2,1,0:T(8,128)S(1)} %get-tuple-element.38), channel_id=1, source_target_pairs={{0,4},{4,8},{8,12},{12,16},{16,20},{20,24},{24,28},{1,5},{5,9},{9,... | collective-permute-start | bytes 196616 | tf_op jit(solution)/shard_map/ppermute | solution.py:21
  12.0 4.3 %collective-permute-done.1 = f32[8,1,16,128]{3,2,1,0:T(8,128)S(1)} collective-permute-done((f32[8,1,16,128]{3,2,1,0:T(8,128)S(1)}, f32[8,1,16,128]{3,2,1,0:T(8,128)S(1)}, u32[]{:S(2)}, u32[]{:S(2)}) %collective-permute-start.1) | collective-permute-done | bytes 65568 | tf_op jit(solution)/shard_map/ppermute | solution.py:22
  22.5 5.0 %fusion.33 = f32[8,4,16,128]{3,2,1,0:T(8,128)S(1)} fusion(f32[8,4,16,128]{3,2,1,0:T(8,128)S(1)} %add_divide_fusion.3, f32[8,4,16,128]{3,2,1,0:T(8,128)} %param.5, f32[8,6,1,128]{3,2,1,0:T(1,128)S(1)} %copy.616, f32[8,1,16,128]{3,2,1,0:T(8,128)S(1)} %collective-permute-done.1, f32[8,1,16,128]{3,2,1,0:T(8,128)S(1)} %collective-permute-done, ...), kind=kLoop, calls=%fused_computation.60 | loop fusion | flops 1703936 | bytes 999480 | tf_op jit(solution)/shard_map/add | solution.py:107
  27.5 4.4 %collective-permute-start.4 = (f32[8,1,16,128]{3,2,1,0:T(8,128)S(1)}, f32[8,1,16,128]{3,2,1,0:T(8,128)S(1)}, u32[]{:S(2)}, u32[]{:S(2)}) collective-permute-start(f32[8,1,16,128]{3,2,1,0:T(8,128)S(1)} %get-tuple-element.36), channel_id=1, source_target_pairs={{0,4},{4,8},{8,12},{12,16},{16,20},{20,24},{24,28},{1,5},{5,9},{9,... | collective-permute-start | bytes 196616 | tf_op jit(solution)/shard_map/ppermute | solution.py:21
  45.3 4.0 %fusion.11 = f32[8,4,16,128]{3,2,1,0:T(8,128)S(1)} fusion(f32[8,4,16,128]{3,2,1,0:T(8,128)S(1)} %copy-done, f32[8,4,16,128]{3,2,1,0:T(8,128)S(1)} %fusion.33, f32[8,6,1,128]{3,2,1,0:T(1,128)S(1)} %copy.620, f32[8,1,16,128]{3,2,1,0:T(8,128)S(1)} %collective-permute-done.5, f32[8,1,16,128]{3,2,1,0:T(8,128)S(1)} %collective-permute-done.4, ...), kind=kLoop, calls=%fused_computation.38 | loop fusion | flops 1507328 | bytes 999480 | tf_op jit(solution)/shard_map/sub | solution.py:111
  52.0 4.8 %reduce_sum.87 = f32[8,2,8,64]{0,3,2,1:T(8,128)S(1)} reduce(f32[8,2,2,8,2,64,2]{0,6,5,4,3,2,1:T(2,128)} %bitcast.35, f32[]{:T(128)} %constant.14.clone.1), dimensions={2,4,6}, to_apply=%region_2.3 | reduce | flops 57344 | bytes 294916 | tf_op jit(solution)/shard_map/reduce_sum | solution.py:57
  62.1 4.2 %collective-permute-done.9 = f32[8,1,8,64]{3,2,1,0:T(8,128)S(1)} collective-permute-done((f32[8,1,8,64]{3,2,1,0:T(8,128)S(1)}, f32[8,1,8,64]{3,2,1,0:T(8,128)S(1)}, u32[]{:S(2)}, u32[]{:S(2)}) %collective-permute-start.9) | collective-permute-done | bytes 16416 | tf_op jit(solution)/shard_map/ppermute | solution.py:22
  77.3 4.4 %collective-permute-start.12 = (f32[8,1,8,64]{3,2,1,0:T(8,128)S(1)}, f32[8,1,8,64]{3,2,1,0:T(8,128)S(1)}, u32[]{:S(2)}, u32[]{:S(2)}) collective-permute-start(f32[8,1,8,64]{3,2,1,0:T(8,128)S(1)} %get-tuple-element.52), channel_id=1, source_target_pairs={{0,4},{4,8},{8,12},{12,16},{16,20},{20,24},{24,28},{1,5},{5,9},{9,... | collective-permute-start | bytes 49160 | tf_op jit(solution)/shard_map/ppermute | solution.py:21
  103.6 4.2 %collective-permute-done.17 = f32[8,1,4,32]{3,0,2,1:T(8,128)S(1)} collective-permute-done((f32[8,1,4,32]{3,0,2,1:T(8,128)S(1)}, f32[8,1,4,32]{3,0,2,1:T(8,128)S(1)}, u32[]{:S(2)}, u32[]{:S(2)}) %collective-permute-start.17) | collective-permute-done | bytes 4128 | tf_op jit(solution)/shard_map/ppermute | solution.py:22
  118.8 4.4 %collective-permute-start.20 = (f32[8,1,4,32]{3,0,2,1:T(8,128)S(1)}, f32[8,1,4,32]{3,0,2,1:T(8,128)S(1)}, u32[]{:S(2)}, u32[]{:S(2)}) collective-permute-start(f32[8,1,4,32]{3,0,2,1:T(8,128)S(1)} %fusion.125), channel_id=1, source_target_pairs={{0,4},{4,8},{8,12},{12,16},{16,20},{20,24},{24,28},{1,5},{5,9},{9,... | collective-permute-start | bytes 12296 | tf_op jit(solution)/shard_map/ppermute | solution.py:21
  124.6 4.2 %collective-permute-done.21 = f32[8,1,4,32]{3,0,2,1:T(8,128)S(1)} collective-permute-done((f32[8,1,4,32]{3,0,2,1:T(8,128)S(1)}, f32[8,1,4,32]{3,0,2,1:T(8,128)S(1)}, u32[]{:S(2)}, u32[]{:S(2)}) %collective-permute-start.21) | collective-permute-done | bytes 4128 | tf_op jit(solution)/shard_map/ppermute | solution.py:22
  135.7 3.9 %fusion.129 = f32[8,1,4,32]{3,0,2,1:T(8,128)S(1)} fusion(f32[8,1,4,32]{3,0,2,1:T(8,128)S(1)} %fusion.125, f32[8,3,1,32]{3,0,2,1:T(8,128)S(1)} %collective-permute-done.23, f32[8,1,4,32]{3,0,2,1:T(8,128)S(1)} %collective-permute-done.21, f32[8,1,4,32]{3,0,2,1:T(8,128)S(1)} %collective-permute-done.20, f32[8,3,1,32]{3,0,2,1:T(8,128)S(1)} %collective-permute-done.22, ...), kind=kLoop, calls=%fused_computation.256 | loop fusion | flops 25600 | bytes 27192 | tf_op jit(solution)/shard_map/add | solution.py:68
  144.5 4.2 %collective-permute-done.25 = f32[8,1,4,32]{3,0,2,1:T(8,128)S(1)} collective-permute-done((f32[8,1,4,32]{3,0,2,1:T(8,128)S(1)}, f32[8,1,4,32]{3,0,2,1:T(8,128)S(1)}, u32[]{:S(2)}, u32[]{:S(2)}) %collective-permute-start.25) | collective-permute-done | bytes 4128 | tf_op jit(solution)/shard_map/ppermute | solution.py:22
  164.6 4.2 %collective-permute-done.29 = f32[8,1,4,32]{3,0,2,1:T(8,128)S(1)} collective-permute-done((f32[8,1,4,32]{3,0,2,1:T(8,128)S(1)}, f32[8,1,4,32]{3,0,2,1:T(8,128)S(1)}, u32[]{:S(2)}, u32[]{:S(2)}) %collective-permute-start.29) | collective-permute-done | bytes 4128 | tf_op jit(solution)/shard_map/ppermute | solution.py:22
  184.0 4.2 %collective-permute-done.33 = f32[8,1,4,32]{3,0,2,1:T(8,128)S(1)} collective-permute-done((f32[8,1,4,32]{3,0,2,1:T(8,128)S(1)}, f32[8,1,4,32]{3,0,2,1:T(8,128)S(1)}, u32[]{:S(2)}, u32[]{:S(2)}) %collective-permute-start.33) | collective-permute-done | bytes 4128 | tf_op jit(solution)/shard_map/ppermute | solution.py:22
  203.8 4.2 %collective-permute-done.37 = f32[8,1,8,64]{3,2,1,0:T(8,128)S(1)} collective-permute-done((f32[8,1,8,64]{3,2,1,0:T(8,128)S(1)}, f32[8,1,8,64]{3,2,1,0:T(8,128)S(1)}, u32[]{:S(2)}, u32[]{:S(2)}) %collective-permute-start.37) | collective-permute-done | bytes 16416 | tf_op jit(solution)/shard_map/ppermute | solution.py:22
  223.3 4.2 %collective-permute-done.41 = f32[8,1,8,64]{3,2,1,0:T(8,128)S(1)} collective-permute-done((f32[8,1,8,64]{3,2,1,0:T(8,128)S(1)}, f32[8,1,8,64]{3,2,1,0:T(8,128)S(1)}, u32[]{:S(2)}, u32[]{:S(2)}) %collective-permute-start.41) | collective-permute-done | bytes 16416 | tf_op jit(solution)/shard_map/ppermute | solution.py:22
  246.6 4.3 %collective-permute-done.45 = f32[8,1,16,128]{3,2,1,0:T(8,128)S(1)} collective-permute-done((f32[8,1,16,128]{3,2,1,0:T(8,128)S(1)}, f32[8,1,16,128]{3,2,1,0:T(8,128)S(1)}, u32[]{:S(2)}, u32[]{:S(2)}) %collective-permute-start.45) | collective-permute-done | bytes 65568 | tf_op jit(solution)/shard_map/ppermute | solution.py:22
  258.0 4.0 %fusion.34 = f32[8,4,16,128]{3,2,1,0:T(8,128)S(1)} fusion(f32[8,4,16,128]{3,2,1,0:T(8,128)S(1)} %add.461, f32[8,4,16,128]{3,2,1,0:T(8,128)S(1)} %copy-done, f32[8,6,1,128]{3,2,1,0:T(1,128)S(1)} %copy.636, f32[8,1,16,128]{3,2,1,0:T(8,128)S(1)} %collective-permute-done.45, f32[8,1,16,128]{3,2,1,0:T(8,128)S(1)} %collective-permute-done.44, ...), kind=kLoop, calls=%fused_computation.61 | loop fusion | flops 1703936 | bytes 999480 | tf_op jit(solution)/shard_map/add | solution.py:107
  266.8 4.3 %collective-permute-done.49 = f32[8,1,16,128]{3,2,1,0:T(8,128)S(1)} collective-permute-done((f32[8,1,16,128]{3,2,1,0:T(8,128)S(1)}, f32[8,1,16,128]{3,2,1,0:T(8,128)S(1)}, u32[]{:S(2)}, u32[]{:S(2)}) %collective-permute-start.49) | collective-permute-done | bytes 65568 | tf_op jit(solution)/shard_map/ppermute | solution.py:22
  278.2 4.0 %fusion.35 = f32[8,4,16,128]{3,2,1,0:T(8,128)S(1)} fusion(f32[8,4,16,128]{3,2,1,0:T(8,128)S(1)} %fusion.34, f32[8,4,16,128]{3,2,1,0:T(8,128)S(1)} %copy-done, f32[8,6,1,128]{3,2,1,0:T(1,128)S(1)} %copy.640, f32[8,1,16,128]{3,2,1,0:T(8,128)S(1)} %collective-permute-done.49, f32[8,1,16,128]{3,2,1,0:T(8,128)S(1)} %collective-permute-done.48, ...), kind=kLoop, calls=%fused_computation.62 | loop fusion | flops 1703936 | bytes 999480 | tf_op jit(solution)/shard_map/add | solution.py:107
  287.0 4.3 %collective-permute-done.53 = f32[8,1,16,128]{3,2,1,0:T(8,128)S(1)} collective-permute-done((f32[8,1,16,128]{3,2,1,0:T(8,128)S(1)}, f32[8,1,16,128]{3,2,1,0:T(8,128)S(1)}, u32[]{:S(2)}, u32[]{:S(2)}) %collective-permute-start.53) | collective-permute-done | bytes 65568 | tf_op jit(solution)/shard_map/ppermute | solution.py:22
  298.4 4.7 %multiply_reduce_fusion = (f32[8]{0:T(128)S(1)}, f32[8,4,16,128]{3,2,1,0:T(8,128)}) fusion(f32[8,4,16,128]{3,2,1,0:T(8,128)S(1)} %copy-done, f32[]{:T(128)} %bitcast.5, f32[8,4,16,128]{3,2,1,0:T(8,128)S(1)} %fusion.35, f32[]{:T(128)} %bitcast.4, f32[8,6,1,128]{3,2,1,0:T(1,128)S(1)} %copy.644, f32[8,1,16,128]{3,2,1,0:T(8,128)S(1)} %collective-permute-done.53, ...), kind=kLoop, calls=%fused_computation.138 | loop fusion | flops 1638392 | bytes 999512 | tf_op jit(solution)/shard_map/reduce_sum | solution.py:117
  303.1 38.6 %psum.7 = f32[8]{0:T(128)S(1)} all-reduce(f32[8]{0:T(128)S(1)} %get-tuple-element.18), channel_id=1, replica_groups=mesh['gx'=8,'gy'=4] {'gx','gy'}, use_global_device_ids=true, to_apply=%region_9.10 | all-reduce | flops 8 | bytes 64 | tf_op jit(solution)/shard_map/psum | solution.py:118
  (186 shorter events, 200.8 us)
Async XLA Ops:
  5.3 6.7 %collective-permute-start = (f32[8,1,16,128]{3,2,1,0:T(8,128)S(1)}, f32[8,1,16,128]{3,2,1,0:T(8,128)S(1)}, u32[]{:S(2)}, u32[]{:S(2)}) collective-permute-start(f32[8,1,16,128]{3,2,1,0:T(8,128)S(1)} %get-tuple-element.38), channel_id=1, source_target_pairs={{0,4},{4,8},{8,12},{12,16},{16,20},{20,24},{24,28},{1,5},{5,9},{9,... | collective-permute-start | bytes 196616 | tf_op jit(solution)/shard_map/ppermute | solution.py:21
  10.1 6.2 %collective-permute-start.1 = (f32[8,1,16,128]{3,2,1,0:T(8,128)S(1)}, f32[8,1,16,128]{3,2,1,0:T(8,128)S(1)}, u32[]{:S(2)}, u32[]{:S(2)}) collective-permute-start(f32[8,1,16,128]{3,2,1,0:T(8,128)S(1)} %get-tuple-element.39), channel_id=1, source_target_pairs={{4,0},{8,4},{12,8},{16,12},{20,16},{24,20},{28,24},{5,1},{9,5},{13... | collective-permute-start | bytes 196616 | tf_op jit(solution)/shard_map/ppermute | solution.py:22
  17.6 4.8 %collective-permute-start.3 = (f32[8,6,1,128]{3,0,2,1:T(8,128)S(1)}, f32[8,6,1,128]{3,0,2,1:T(8,128)S(1)}, u32[]{:S(2)}, u32[]{:S(2)}) collective-permute-start(f32[8,6,1,128]{3,0,2,1:T(8,128)S(1)} %copy.615), channel_id=1, source_target_pairs={{1,0},{2,1},{3,2},{5,4},{6,5},{7,6},{9,8},{10,9},{11,10},{13,12},{... | collective-permute-start | bytes 73736 | tf_op jit(solution)/shard_map/ppermute | solution.py:22
  27.5 8.8 %collective-permute-start.4 = (f32[8,1,16,128]{3,2,1,0:T(8,128)S(1)}, f32[8,1,16,128]{3,2,1,0:T(8,128)S(1)}, u32[]{:S(2)}, u32[]{:S(2)}) collective-permute-start(f32[8,1,16,128]{3,2,1,0:T(8,128)S(1)} %get-tuple-element.36), channel_id=1, source_target_pairs={{0,4},{4,8},{8,12},{12,16},{16,20},{20,24},{24,28},{1,5},{5,9},{9,... | collective-permute-start | bytes 196616 | tf_op jit(solution)/shard_map/ppermute | solution.py:21
  31.9 6.3 %collective-permute-start.5 = (f32[8,1,16,128]{3,2,1,0:T(8,128)S(1)}, f32[8,1,16,128]{3,2,1,0:T(8,128)S(1)}, u32[]{:S(2)}, u32[]{:S(2)}) collective-permute-start(f32[8,1,16,128]{3,2,1,0:T(8,128)S(1)} %get-tuple-element.37), channel_id=1, source_target_pairs={{4,0},{8,4},{12,8},{16,12},{20,16},{24,20},{28,24},{5,1},{9,5},{13... | collective-permute-start | bytes 196616 | tf_op jit(solution)/shard_map/ppermute | solution.py:22
  57.1 5.0 %collective-permute-start.8 = (f32[8,1,8,64]{3,2,1,0:T(8,128)S(1)}, f32[8,1,8,64]{3,2,1,0:T(8,128)S(1)}, u32[]{:S(2)}, u32[]{:S(2)}) collective-permute-start(f32[8,1,8,64]{3,2,1,0:T(8,128)S(1)} %get-tuple-element.54), channel_id=1, source_target_pairs={{0,4},{4,8},{8,12},{12,16},{16,20},{20,24},{24,28},{1,5},{5,9},{9,... | collective-permute-start | bytes 49160 | tf_op jit(solution)/shard_map/ppermute | solution.py:21
  60.5 5.8 %collective-permute-start.9 = (f32[8,1,8,64]{3,2,1,0:T(8,128)S(1)}, f32[8,1,8,64]{3,2,1,0:T(8,128)S(1)}, u32[]{:S(2)}, u32[]{:S(2)}) collective-permute-start(f32[8,1,8,64]{3,2,1,0:T(8,128)S(1)} %get-tuple-element.55), channel_id=1, source_target_pairs={{4,0},{8,4},{12,8},{16,12},{20,16},{24,20},{28,24},{5,1},{9,5},{13... | collective-permute-start | bytes 49160 | tf_op jit(solution)/shard_map/ppermute | solution.py:22
  66.4 5.0 %collective-permute-start.10 = (f32[8,4,1,64]{3,2,1,0:T(1,128)S(1)}, f32[8,4,1,64]{3,2,1,0:T(1,128)S(1)}, u32[]{:S(2)}, u32[]{:S(2)}) collective-permute-start(f32[8,4,1,64]{3,2,1,0:T(1,128)S(1)} %get-tuple-element.46), channel_id=1, source_target_pairs={{0,1},{1,2},{2,3},{4,5},{5,6},{6,7},{8,9},{9,10},{10,11},{12,13},{... | collective-permute-start | bytes 24584 | tf_op jit(solution)/shard_map/ppermute | solution.py:21
  77.3 6.6 %collective-permute-start.12 = (f32[8,1,8,64]{3,2,1,0:T(8,128)S(1)}, f32[8,1,8,64]{3,2,1,0:T(8,128)S(1)}, u32[]{:S(2)}, u32[]{:S(2)}) collective-permute-start(f32[8,1,8,64]{3,2,1,0:T(8,128)S(1)} %get-tuple-element.52), channel_id=1, source_target_pairs={{0,4},{4,8},{8,12},{12,16},{16,20},{20,24},{24,28},{1,5},{5,9},{9,... | collective-permute-start | bytes 49160 | tf_op jit(solution)/shard_map/ppermute | solution.py:21
  81.6 5.8 %collective-permute-start.13 = (f32[8,1,8,64]{3,2,1,0:T(8,128)S(1)}, f32[8,1,8,64]{3,2,1,0:T(8,128)S(1)}, u32[]{:S(2)}, u32[]{:S(2)}) collective-permute-start(f32[8,1,8,64]{3,2,1,0:T(8,128)S(1)} %get-tuple-element.53), channel_id=1, source_target_pairs={{4,0},{8,4},{12,8},{16,12},{20,16},{24,20},{28,24},{5,1},{9,5},{13... | collective-permute-start | bytes 49160 | tf_op jit(solution)/shard_map/ppermute | solution.py:22
  102.2 5.6 %collective-permute-start.17 = (f32[8,1,4,32]{3,0,2,1:T(8,128)S(1)}, f32[8,1,4,32]{3,0,2,1:T(8,128)S(1)}, u32[]{:S(2)}, u32[]{:S(2)}) collective-permute-start(f32[8,1,4,32]{3,0,2,1:T(8,128)S(1)} %add_divide_fusion.13), channel_id=1, source_target_pairs={{4,0},{8,4},{12,8},{16,12},{20,16},{24,20},{28,24},{5,1},{9,5},{13... | collective-permute-start | bytes 12296 | tf_op jit(solution)/shard_map/ppermute | solution.py:22
  107.9 4.9 %collective-permute-start.18 = (f32[8,3,1,32]{3,0,2,1:T(8,128)S(1)}, f32[8,3,1,32]{3,0,2,1:T(8,128)S(1)}, u32[]{:S(2)}, u32[]{:S(2)}) collective-permute-start(f32[8,3,1,32]{3,0,2,1:T(8,128)S(1)} %get-tuple-element.64), channel_id=1, source_target_pairs={{0,1},{1,2},{2,3},{4,5},{5,6},{6,7},{8,9},{9,10},{10,11},{12,13},{... | collective-permute-start | bytes 9224 | tf_op jit(solution)/shard_map/ppermute | solution.py:21
  118.8 5.8 %collective-permute-start.20 = (f32[8,1,4,32]{3,0,2,1:T(8,128)S(1)}, f32[8,1,4,32]{3,0,2,1:T(8,128)S(1)}, u32[]{:S(2)}, u32[]{:S(2)}) collective-permute-start(f32[8,1,4,32]{3,0,2,1:T(8,128)S(1)} %fusion.125), channel_id=1, source_target_pairs={{0,4},{4,8},{8,12},{12,16},{16,20},{20,24},{24,28},{1,5},{5,9},{9,... | collective-permute-start | bytes 12296 | tf_op jit(solution)/shard_map/ppermute | solution.py:21
  123.1 5.6 %collective-permute-start.21 = (f32[8,1,4,32]{3,0,2,1:T(8,128)S(1)}, f32[8,1,4,32]{3,0,2,1:T(8,128)S(1)}, u32[]{:S(2)}, u32[]{:S(2)}) collective-permute-start(f32[8,1,4,32]{3,0,2,1:T(8,128)S(1)} %fusion.125), channel_id=1, source_target_pairs={{4,0},{8,4},{12,8},{16,12},{20,16},{24,20},{28,24},{5,1},{9,5},{13... | collective-permute-start | bytes 12296 | tf_op jit(solution)/shard_map/ppermute | solution.py:22
  139.7 4.8 %collective-permute-start.24 = (f32[8,1,4,32]{3,0,2,1:T(8,128)S(1)}, f32[8,1,4,32]{3,0,2,1:T(8,128)S(1)}, u32[]{:S(2)}, u32[]{:S(2)}) collective-permute-start(f32[8,1,4,32]{3,0,2,1:T(8,128)S(1)} %fusion.129), channel_id=1, source_target_pairs={{0,4},{4,8},{8,12},{12,16},{16,20},{20,24},{24,28},{1,5},{5,9},{9,... | collective-permute-start | bytes 12296 | tf_op jit(solution)/shard_map/ppermute | solution.py:21
  143.1 5.6 %collective-permute-start.25 = (f32[8,1,4,32]{3,0,2,1:T(8,128)S(1)}, f32[8,1,4,32]{3,0,2,1:T(8,128)S(1)}, u32[]{:S(2)}, u32[]{:S(2)}) collective-permute-start(f32[8,1,4,32]{3,0,2,1:T(8,128)S(1)} %fusion.129), channel_id=1, source_target_pairs={{4,0},{8,4},{12,8},{16,12},{20,16},{24,20},{28,24},{5,1},{9,5},{13... | collective-permute-start | bytes 12296 | tf_op jit(solution)/shard_map/ppermute | solution.py:22
  159.6 5.0 %collective-permute-start.28 = (f32[8,1,4,32]{3,0,2,1:T(8,128)S(1)}, f32[8,1,4,32]{3,0,2,1:T(8,128)S(1)}, u32[]{:S(2)}, u32[]{:S(2)}) collective-permute-start(f32[8,1,4,32]{3,0,2,1:T(8,128)S(1)} %fusion.133), channel_id=1, source_target_pairs={{0,4},{4,8},{8,12},{12,16},{16,20},{20,24},{24,28},{1,5},{5,9},{9,... | collective-permute-start | bytes 12296 | tf_op jit(solution)/shard_map/ppermute | solution.py:21
  163.2 5.6 %collective-permute-start.29 = (f32[8,1,4,32]{3,0,2,1:T(8,128)S(1)}, f32[8,1,4,32]{3,0,2,1:T(8,128)S(1)}, u32[]{:S(2)}, u32[]{:S(2)}) collective-permute-start(f32[8,1,4,32]{3,0,2,1:T(8,128)S(1)} %fusion.133), channel_id=1, source_target_pairs={{4,0},{8,4},{12,8},{16,12},{20,16},{24,20},{28,24},{5,1},{9,5},{13... | collective-permute-start | bytes 12296 | tf_op jit(solution)/shard_map/ppermute | solution.py:22
  182.5 5.6 %collective-permute-start.33 = (f32[8,1,4,32]{3,0,2,1:T(8,128)S(1)}, f32[8,1,4,32]{3,0,2,1:T(8,128)S(1)}, u32[]{:S(2)}, u32[]{:S(2)}) collective-permute-start(f32[8,1,4,32]{3,0,2,1:T(8,128)S(1)} %fusion.137), channel_id=1, source_target_pairs={{4,0},{8,4},{12,8},{16,12},{20,16},{24,20},{28,24},{5,1},{9,5},{13... | collective-permute-start | bytes 12296 | tf_op jit(solution)/shard_map/ppermute | solution.py:22
  202.2 5.8 %collective-permute-start.37 = (f32[8,1,8,64]{3,2,1,0:T(8,128)S(1)}, f32[8,1,8,64]{3,2,1,0:T(8,128)S(1)}, u32[]{:S(2)}, u32[]{:S(2)}) collective-permute-start(f32[8,1,8,64]{3,2,1,0:T(8,128)S(1)} %get-tuple-element.51), channel_id=1, source_target_pairs={{4,0},{8,4},{12,8},{16,12},{20,16},{24,20},{28,24},{5,1},{9,5},{13... | collective-permute-start | bytes 49160 | tf_op jit(solution)/shard_map/ppermute | solution.py:22
  221.7 5.8 %collective-permute-start.41 = (f32[8,1,8,64]{3,2,1,0:T(8,128)S(1)}, f32[8,1,8,64]{3,2,1,0:T(8,128)S(1)}, u32[]{:S(2)}, u32[]{:S(2)}) collective-permute-start(f32[8,1,8,64]{3,2,1,0:T(8,128)S(1)} %get-tuple-element.49), channel_id=1, source_target_pairs={{4,0},{8,4},{12,8},{16,12},{20,16},{24,20},{28,24},{5,1},{9,5},{13... | collective-permute-start | bytes 49160 | tf_op jit(solution)/shard_map/ppermute | solution.py:22
  244.8 6.2 %collective-permute-start.45 = (f32[8,1,16,128]{3,2,1,0:T(8,128)S(1)}, f32[8,1,16,128]{3,2,1,0:T(8,128)S(1)}, u32[]{:S(2)}, u32[]{:S(2)}) collective-permute-start(f32[8,1,16,128]{3,2,1,0:T(8,128)S(1)} %get-tuple-element.35), channel_id=1, source_target_pairs={{4,0},{8,4},{12,8},{16,12},{20,16},{24,20},{28,24},{5,1},{9,5},{13... | collective-permute-start | bytes 196616 | tf_op jit(solution)/shard_map/ppermute | solution.py:22
  264.9 6.2 %collective-permute-start.49 = (f32[8,1,16,128]{3,2,1,0:T(8,128)S(1)}, f32[8,1,16,128]{3,2,1,0:T(8,128)S(1)}, u32[]{:S(2)}, u32[]{:S(2)}) collective-permute-start(f32[8,1,16,128]{3,2,1,0:T(8,128)S(1)} %get-tuple-element.33), channel_id=1, source_target_pairs={{4,0},{8,4},{12,8},{16,12},{20,16},{24,20},{28,24},{5,1},{9,5},{13... | collective-permute-start | bytes 196616 | tf_op jit(solution)/shard_map/ppermute | solution.py:22
  285.1 6.2 %collective-permute-start.53 = (f32[8,1,16,128]{3,2,1,0:T(8,128)S(1)}, f32[8,1,16,128]{3,2,1,0:T(8,128)S(1)}, u32[]{:S(2)}, u32[]{:S(2)}) collective-permute-start(f32[8,1,16,128]{3,2,1,0:T(8,128)S(1)} %get-tuple-element.31), channel_id=1, source_target_pairs={{4,0},{8,4},{12,8},{16,12},{20,16},{24,20},{28,24},{5,1},{9,5},{13... | collective-permute-start | bytes 196616 | tf_op jit(solution)/shard_map/ppermute | solution.py:22
  (35 other events, 241.1 us)
where the time goes:
time: 345 us; the launch traced here: 342 us
  starting transfers between devices  125 us (36%)
  waiting for transfers between devices  96.8 us (28%)
  other arithmetic  67 us (19%)
  blocking collectives  38.6 us (11%)
  local copies, waits for them, and re-layouts  11.4 us (3%)
  between operations  3.62 us (1%)
    ppermute x28, waiting for transfers between devices, with_halo(): after = lax.ppermute(leading, axis, down)  92.9 us
    ppermute x28, starting transfers between devices, with_halo(): before = lax.ppermute(last, axis, up)  88.4 us
    psum x1, blocking collectives, body(): squares = lax.psum(local_squares, ('gx', 'gy'))  38.6 us
    ppermute x28, starting transfers between devices, with_halo(): after = lax.ppermute(leading, axis, down)  36.5 us
    add x5, other arithmetic, coarsest_solve(): iterate = iterate + DAMPING * (rhs_field - applied) / diagonal  19.7 us
    add x3, other arithmetic, smooth_step(): return iterate + DAMPING * (source - operate(iterate)) / diagonal  13 us
    add x3, other arithmetic, smooth_step(): return iterate + DAMPING * (rhs_field - operate(iterate)) / diagonal  11.5 us
    reduce_sum x6, other arithmetic, coarsen(): return jnp.sum(blocks, axis=(2, 4, 6)) * 0.125  9.19 us
  transfers between devices with their start and end apart: 56, of which 40 were waited for; matrix products, arithmetic and copies ran while one was open for 1% of the time, Pallas kernels for 0%

commit v1 on v0

--- a/solution.py
+++ b/solution.py
@@ -1,14 +1,19 @@
+import functools
+
 import jax
 import jax.numpy as jnp
 from jax import lax
+from jax.experimental import pallas as pl
+from jax.experimental.pallas import tpu as pltpu
 from jax.sharding import PartitionSpec as P
 
 LEVELS = 3
 COARSE_SWEEPS = 6
 
-
 DAMPING = 0.8
 EPSILON = 1e-06
+VMEM_LIMIT = 40 * 1024 * 1024
+LANES = 128
 
 
 def with_halo(x, sides, width):
@@ -93,27 +98,15 @@
     return iterate
 
 
-def body(source, reaction, shifts, shift_index, velocity):
+def halo_body(source, reaction, shifts, shift_index, velocity):
     columns, cells_x, cells_y, cells_z = source.shape
     shift_value = select_shifts(shifts, shift_index)
     reaction_top = reaction[None]
     backward, forward, centre = coefficients(velocity, 1.0)
     diagonal = centre + reaction_top + shift_value[:, None, None, None]
 
-    def operate(iterate):
-        return apply_stencil(face_halo(iterate), backward, forward, diagonal)
-
-    def smooth_step(iterate):
-        return iterate + DAMPING * (source - operate(iterate)) / diagonal
-
-    iterate = DAMPING * source / diagonal
-    iterate = smooth_step(iterate)
-    defect = source - operate(iterate)
-    correction = multigrid_cycle(1, coarsen(defect), coarsen(reaction_top), shift_value, velocity)
-    iterate = iterate + refine(correction)
-    iterate = smooth_step(iterate)
-    iterate = smooth_step(iterate)
-    residual = source - operate(iterate)
+    iterate = multigrid_cycle(0, source, reaction_top, shift_value, velocity)
+    residual = source - apply_stencil(face_halo(iterate), backward, forward, diagonal)
     local_squares = jnp.sum(residual * residual, axis=(1, 2, 3))
     squares = lax.psum(local_squares, ("gx", "gy"))
     total_cells = cells_x * cells_y * cells_z * lax.axis_size("gx") * lax.axis_size("gy")
@@ -121,7 +114,263 @@
     return (iterate, residual, residual_rms)
 
 
+def split_dot(values, matrix):
+    high = values.astype(jnp.bfloat16)
+    low = (values - high.astype(jnp.float32)).astype(jnp.bfloat16)
+    return jnp.dot(high, matrix, preferred_element_type=jnp.float32) + jnp.dot(
+        low, matrix, preferred_element_type=jnp.float32
+    )
+
+
+class Level:
+    def __init__(self, index, sizes, velocity_ref, shift, f, r, w):
+        self.nx, self.ny, self.nz = (s >> index for s in sizes)
+        self.f, self.r, self.w = f, r, w
+        spacing = 2.0**index
+        scale_a = 1.0 / (spacing * spacing)
+        inverse = 1.0 / spacing
+        speed = [velocity_ref[d] for d in range(3)]
+        self.backward = [scale_a + jnp.maximum(v, 0.0) * inverse for v in speed]
+        self.forward = [scale_a - jnp.minimum(v, 0.0) * inverse for v in speed]
+        total = jnp.abs(speed[0]) + jnp.abs(speed[1]) + jnp.abs(speed[2])
+        self.centre = 6.0 * scale_a + total * inverse + shift
+        lane = lax.broadcasted_iota(jnp.int32, (1, LANES), 1)
+        inside = lane < self.nz
+        self.low_z = jnp.where((lane > 0) & inside, self.backward[2], 0.0)
+        self.high_z = jnp.where(lane < self.nz - 1, self.forward[2], 0.0)
+
+    def plane(self, v, x):
+        return v[x + 1, pl.ds(8, self.ny), :]
+
+    def neighbours(self, v, x, middle):
+        ny = self.ny
+        out = self.backward[0] * v[x, pl.ds(8, ny), :]
+        out += self.forward[0] * v[x + 2, pl.ds(8, ny), :]
+        out += self.backward[1] * v[x + 1, pl.ds(7, ny), :]
+        out += self.forward[1] * v[x + 1, pl.ds(9, ny), :]
+        out += self.low_z * pltpu.roll(middle, 1, 1)
+        out += self.high_z * pltpu.roll(middle, LANES - 1, 1)
+        return out
+
+    def smooth(self, src, dst):
+        def step(x, carry):
+            middle = self.plane(src, x)
+            pulled = self.f[x] + self.neighbours(src, x, middle)
+            dst[x + 1, pl.ds(8, self.ny), :] = (1.0 - DAMPING) * middle + self.w[x] * pulled
+            return carry
+
+        lax.fori_loop(0, self.nx, step, 0)
+
+    def defect(self, v, x):
+        middle = self.plane(v, x)
+        pulled = self.f[x] + self.neighbours(v, x, middle)
+        return pulled - (self.r[x] + self.centre) * middle
+
+    def start(self, v):
+        def step(x, carry):
+            weight = DAMPING / (self.r[x] + self.centre)
+            self.w[x] = weight
+            v[x + 1, pl.ds(8, self.ny), :] = weight * self.f[x]
+            return carry
+
+        lax.fori_loop(0, self.nx, step, 0)
+
+    def pair_rows(self, tmp, values, slot):
+        rows = tmp.at[slot]
+        rows[pl.ds(0, self.ny), :] = values
+        half = self.ny // 2
+        return rows[pl.ds(0, half, stride=2), :] + rows[pl.ds(1, half, stride=2), :]
+
+    def coarsen_defect(self, v, tmp, pooled):
+        half = self.ny // 2
+
+        def step(x, carry):
+            both = self.defect(v, 2 * x) + self.defect(v, 2 * x + 1)
+            pooled[pl.ds(pl.multiple_of(x * half, 8), half), :] = self.pair_rows(tmp, both, 0)
+            return carry
+
+        lax.fori_loop(0, self.nx // 2, step, 0)
+
+    def coarsen_reaction(self, tmp, pooled):
+        half = self.ny // 2
+
+        def step(x, carry):
+            both = self.r[2 * x] + self.r[2 * x + 1]
+            pooled[pl.ds(pl.multiple_of(x * half, 8), half), :] = self.pair_rows(tmp, both, 1)
+            return carry
+
+        lax.fori_loop(0, self.nx // 2, step, 0)
+
+    def add_refined(self, v, spread, tmp):
+        half = self.ny // 2
+
+        def step(x, carry):
+            part = spread[pl.ds(pl.multiple_of(x * half, 8), half), :]
+            rows = tmp.at[0]
+            rows[pl.ds(0, half, stride=2), :] = part
+            rows[pl.ds(1, half, stride=2), :] = part
+            full = rows[pl.ds(0, self.ny), :]
+            for k in range(2):
+                v[2 * x + 1 + k, pl.ds(8, self.ny), :] += full
+            return carry
+
+        lax.fori_loop(0, self.nx // 2, step, 0)
+
+
+def zero_rim(v, nx, ny):
+    rows = v.shape[1]
+    blank = jnp.zeros((rows, LANES), jnp.float32)
+    v[0] = blank
+    v[nx + 1] = blank
+    edge = jnp.zeros((nx + 2, 8, LANES), jnp.float32)
+    v[:, pl.ds(0, 8), :] = edge
+    v[:, pl.ds(8 + ny, 8), :] = edge
+
+
+def cycle_kernel(
+    sizes, blocks, place_ref, shifts_ref, index_ref, velocity_ref, pool_ref, spread_ref, *refs
+):
+    gx_size, gy_size = blocks
+    nx, ny, nz = sizes
+    bx, by = nx // gx_size, ny // gy_size
+    pieces = refs[:gy_size]
+    out_ref = refs[gy_size]
+    f0, r0, w0, va, vb, f1, r1, w1, v1a, v1b, f2, r2, w2, v2a, v2b, pooled, tmp = refs[gy_size + 1 :]
+    column, row_block = place_ref[0], place_ref[1]
+    shift = shifts_ref[index_ref[column]]
+    pool, spread = pool_ref[...], spread_ref[...]
+
+    fine = Level(0, sizes, velocity_ref, shift, f0, r0, w0)
+    mid = Level(1, sizes, velocity_ref, shift, f1, r1, w1)
+    deep = Level(2, sizes, velocity_ref, shift, f2, r2, w2)
+    for v, level in ((va, fine), (vb, fine), (v1a, mid), (v1b, mid), (v2a, deep), (v2b, deep)):
+        zero_rim(v, level.nx, level.ny)
+
+    for j, piece in enumerate(pieces):
+        for i in range(gx_size):
+            f0[pl.ds(i * bx, bx), pl.ds(j * by, by), :] = piece[i, 0]
+            r0[pl.ds(i * bx, bx), pl.ds(j * by, by), :] = piece[i, 1]
+
+    rows1, rows2 = mid.nx * mid.ny, deep.nx * deep.ny
+    fine.start(va)
+    fine.smooth(va, vb)
+    fine.coarsen_defect(vb, tmp, pooled)
+    f1[...] = split_dot(pooled[pl.ds(0, rows1), :], pool).reshape(f1.shape)
+    fine.coarsen_reaction(tmp, pooled)
+    r1[...] = split_dot(pooled[pl.ds(0, rows1), :], pool).reshape(r1.shape)
+
+    mid.start(v1a)
+    mid.smooth(v1a, v1b)
+    mid.coarsen_defect(v1b, tmp, pooled)
+    f2[...] = split_dot(pooled[pl.ds(0, rows2), :], pool).reshape(f2.shape)
+    mid.coarsen_reaction(tmp, pooled)
+    r2[...] = split_dot(pooled[pl.ds(0, rows2), :], pool).reshape(r2.shape)
+
+    deep.start(v2a)
+    src, dst = v2a, v2b
+    for _ in range(COARSE_SWEEPS - 1):
+        deep.smooth(src, dst)
+        src, dst = dst, src
+
+    values = src[pl.ds(1, deep.nx), pl.ds(8, deep.ny), :].reshape(rows2, LANES)
+    pooled[pl.ds(0, rows2), :] = split_dot(values, spread)
+    mid.add_refined(v1b, pooled, tmp)
+    mid.smooth(v1b, v1a)
+    mid.smooth(v1a, v1b)
+    values = v1b[pl.ds(1, mid.nx), pl.ds(8, mid.ny), :].reshape(rows1, LANES)
+    pooled[pl.ds(0, rows1), :] = split_dot(values, spread)
+    fine.add_refined(vb, pooled, tmp)
+    fine.smooth(vb, va)
+    fine.smooth(va, vb)
+
+    area = bx * by
+    row0 = pl.multiple_of(row_block * by, 8)
+
+    def finish(i, total):
+        for k in range(bx):
+            x = i * bx + k
+            rest = fine.defect(vb, x)
+            total = total + jnp.sum((rest * rest).reshape(ny // 8, 8, LANES), axis=0)
+            tmp[0, pl.ds(0, ny), :] = rest
+            out_ref[i, pl.ds(k * by, by), :] = vb[x + 1, pl.ds(8 + row0, by), :]
+            out_ref[i, pl.ds(area + k * by, by), :] = tmp[0, pl.ds(row0, by), :]
+        return total
+
+    squares = lax.fori_loop(0, gx_size, finish, jnp.zeros((8, LANES), jnp.float32))
+    mean = jnp.sum(squares) / (nx * ny * nz) + EPSILON
+    rms = jnp.sqrt(jnp.full((8, LANES), mean, jnp.float32))
+    for i in range(gx_size):
+        out_ref[i, pl.ds(2 * area, 8), :] = rms
+
+
+def pooling_matrices():
+    row = lax.broadcasted_iota(jnp.int32, (LANES, LANES), 0)
+    col = lax.broadcasted_iota(jnp.int32, (LANES, LANES), 1)
+    pool = jnp.where(row // 2 == col, 0.125, 0.0).astype(jnp.bfloat16)
+    spread = jnp.where(col // 2 == row, 1.0, 0.0).astype(jnp.bfloat16)
+    return pool, spread
+
+
+def column_cycle(pieces, place, shifts, shift_index, velocity, sizes, blocks):
+    gx_size, gy_size = blocks
+    nx, ny, nz = sizes
+    area = (nx // gx_size) * (ny // gy_size)
+    f32 = jnp.float32
+
+    def grid(index):
+        return pltpu.VMEM((nx >> index, ny >> index, LANES), f32)
+
+    def rimmed(index):
+        return pltpu.VMEM(((nx >> index) + 2, (ny >> index) + 16, LANES), f32)
+
+    scratch = []
+    for index in range(LEVELS):
+        scratch += [grid(index)] * 3 + [rimmed(index)] * 2
+    scratch += [pltpu.VMEM(((nx // 2) * (ny // 2), LANES), f32), pltpu.VMEM((2, ny, LANES), f32)]
+    smem = pl.BlockSpec(memory_space=pltpu.SMEM)
+    vmem = pl.BlockSpec(memory_space=pltpu.VMEM)
+    pool, spread = pooling_matrices()
+    return pl.pallas_call(
+        functools.partial(cycle_kernel, sizes, blocks),
+        out_shape=jax.ShapeDtypeStruct((gx_size, 2 * area + 8, LANES), f32),
+        in_specs=[smem] * 4 + [vmem] * (2 + gy_size),
+        out_specs=vmem,
+        scratch_shapes=scratch,
+        compiler_params=pltpu.CompilerParams(vmem_limit_bytes=VMEM_LIMIT),
+        name="cycle",
+    )(place, shifts, shift_index, velocity, pool, spread, *pieces)
+
+
+def column_body(source, reaction, shifts, shift_index, velocity):
+    columns, bx, by, nz = source.shape
+    gx_size, gy_size = lax.axis_size("gx"), lax.axis_size("gy")
+    sizes = (bx * gx_size, by * gy_size, nz)
+    place = jnp.stack([lax.axis_index("gx"), lax.axis_index("gy")]).astype(jnp.int32)
+
+    both = jnp.stack([source, jnp.broadcast_to(reaction[None], source.shape)], axis=1)
+    mine = lax.all_to_all(both, "gx", 0, 0)
+    gathered = lax.all_gather(mine, "gy")
+    pieces = [gathered[j] for j in range(gy_size)]
+    results = column_cycle(
+        pieces, place, shifts, shift_index, velocity, sizes, (gx_size, gy_size)
+    )
+    back = lax.all_to_all(results, "gx", 0, 0)
+    area = bx * by
+    iterate = back[:, :area].reshape(source.shape)
+    residual = back[:, area : 2 * area].reshape(source.shape)
+    return iterate, residual, back[:, 2 * area, 0]
+
+
 def solution(mesh):
+    gx_size, gy_size = mesh.shape["gx"], mesh.shape["gy"]
+
+    def body(source, reaction, shifts, shift_index, velocity):
+        columns, bx, by, nz = source.shape
+        cells = bx * gx_size * by * gy_size
+        fits = nz == LANES and bx % 4 == 0 and by % 16 == 0 and cells * nz * 4 <= 2**20
+        plan = column_body if columns == gx_size and fits else halo_body
+        return plan(source, reaction, shifts, shift_index, velocity)
+
     return jax.shard_map(
         body,
         mesh=mesh,

time: 345 us -> 108 us (0.31)
  starting transfers between devices: 125 us -> 0.04 us
  waiting for transfers between devices: 96.8 us -> 21.5 us
  other arithmetic: 67 us -> 1.2 us
  Pallas kernels: 0 us -> 23 us
  between operations: 3.62 us -> 14.1 us
  local copies, waits for them, and re-layouts: 11.4 us -> 4.05 us
  blocking collectives: 38.6 us -> 43.4 us
    ppermute x56 -> x0, starting transfers between devices: 125 us -> none  [the longest x28 88.4 us: with_halo(): before = lax.ppermute(last, axis, up)]
    ppermute x56 -> x0, waiting for transfers between devices: 96.8 us -> none  [the longest x28 92.9 us: with_halo(): after = lax.ppermute(leading, axis, down)]
    add x16 -> x0, other arithmetic: 46.2 us -> none  [the longest x5 19.7 us: coarsest_solve(): iterate = iterate + DAMPING * (rhs_field - applied) / diagonal]
    all_to_all x0 -> x2, blocking collectives: none -> 43.4 us  [the longest x1 21.7 us: column_body(): mine = lax.all_to_all(both, 'gx', 0, 0)]
    psum x1 -> x0, blocking collectives: 38.6 us -> none  [body(): squares = lax.psum(local_squares, ('gx', 'gy'))]
    pallas_call x0 -> x1, Pallas kernels: none -> 23 us  [column_cycle(): pl.pallas_call(functools.partial(cycle_kernel, sizes, blocks), out_shape=...]
    all_gather x0 -> x1, waiting for transfers between devices: none -> 21.5 us  [column_body(): gathered = lax.all_gather(mine, 'gy')]
    reduce_sum x8 -> x0, other arithmetic: 14.8 us -> none  [the longest x6 9.19 us: coarsen(): return jnp.sum(blocks, axis=(2, 4, 6)) * 0.125]
  transfers between devices with their start and end apart: 56 -> 1, of which waited for: 40 -> 1; matrix products, arithmetic and copies ran while one was open for 1% -> 0% of each run, Pallas kernels for 0% -> 0%
where the time goes in v1:
time: 108 us; the launch traced here: 107 us
  blocking collectives  43.4 us (40%)
  Pallas kernels  23 us (21%)
  waiting for transfers between devices  21.5 us (20%)
  between operations  14.1 us (13%)
  local copies, waits for them, and re-layouts  4.05 us (4%)
  other arithmetic  1.2 us (1%)
    pallas_call x1, Pallas kernels, column_cycle(): pl.pallas_call(functools.partial(cycle_kernel, sizes, blocks), out_shape=...  23 us
    all_to_all x1, blocking collectives, column_body(): mine = lax.all_to_all(both, 'gx', 0, 0)  21.7 us
    all_to_all x1, blocking collectives, column_body(): back = lax.all_to_all(results, 'gx', 0, 0)  21.7 us
    all_gather x1, waiting for transfers between devices, column_body(): gathered = lax.all_gather(mine, 'gy')  21.5 us
  transfers between devices with their start and end apart: 1, of which 1 were waited for; matrix products, arithmetic and copies ran while one was open for 0% of the time, Pallas kernels for 0%

profile of v1, /device:TPU:0, one launch (start us, length us, event | category | flops | bytes accessed | tf_op | source)
XLA Modules:
  0.0 107.3 jit_solution(1007323847280718245)
XLA Ops:
  7.2 0.0 all-gather.3.cloned.1.call-start
  7.2 0.8 stack_broadcast_in_dim.2
  8.0 1.0 pad_maximum_fusion
  9.0 21.7 %all_to_all.10 = f32[8,2,4,16,128]{4,3,2,1,0:T(8,128)} all-to-all(f32[8,2,4,16,128]{4,3,2,1,0:T(8,128)S(1)} %pad_maximum_fusion), channel_id=1, replica_groups=mesh['gx'=8,'gy'=4] {'gx'}, dimensions={0} | all-to-all | bytes 1048576 | tf_op jit(solution)/shard_map/all_to_all | solution.py:351
  30.7 0.0 all-gather.3.cloned.1.call-update
  30.7 0.1 pad_add_fusion.place_ref
  30.8 0.1 select_convert_fusion
  30.9 0.0 copy-start
  30.9 0.0 copy-start.1
  31.0 0.0 copy-start.2
  31.0 21.5 %all-gather.3.cloned.1.call-done = f32[32,2,4,16,128]{4,3,2,1,0:T(8,128)} async-done(((f32[8,2,4,16,128]{4,3,2,1,0:T(8,128)}), f32[32,2,4,16,128]{4,3,2,1,0:T(8,128)}) %all-gather.3.cloned.1.call-update) | async-done | bytes 2097168 | tf_op jit(solution)/shard_map/all_gather | solution.py:352
  52.5 1.8 %fusion = (f32[8,2,4,16,128]{4,3,2,1,0:T(8,128)S(1)}, f32[8,2,4,16,128]{4,3,2,1,0:T(8,128)S(1)}, f32[8,2,4,16,128]{4,3,2,1,0:T(8,128)S(1)}, f32[8,2,4,16,128]{4,3,2,1,0:T(8,128)S(1)}) fusion(f32[32,2,4,16,128]{4,3,2,1,0:T(8,128)} %all-gather.3.cloned.1.call-done), kind=kLoop, calls=%fused_computation.12 | loop fusion | bytes 4194304 | tf_op jit(solution)/shard_map/slice | solution.py:353
  54.2 0.0 copy-done
  54.3 0.0 copy-done.1
  54.3 0.0 copy-done.2
  54.3 23.0 %cycle.1 = f32[8,136,128]{2,1,0:T(8,128)S(1)} custom-call(s32[2]{0:T(128)S(1)} %pad_add_fusion.place_ref, f32[8]{0:T(128)S(1)} %copy-done, s32[8]{0:T(128)S(1)} %copy-done.1, f32[3]{0:T(128)S(1)} %copy-done.2, bf16[128,128]{1,0:T(8,128)(2,1)S(1)} %get-tuple-element.10.pool_ref, bf16[128,128]{1,0:T(8,128)(2,1)S(1)} %get-tuple-element.9.spread_ref, ...), custom_call_target="tpu_custom_call" | custom-call | tf_op jit(solution)/shard_map/cycle/pallas_call | solution.py:333
  77.3 21.7 %all_to_all.11 = f32[8,136,128]{2,1,0:T(8,128)S(1)} all-to-all(f32[8,136,128]{2,1,0:T(8,128)S(1)} %cycle.1), channel_id=1, replica_groups=mesh['gx'=8,'gy'=4] {'gx'}, dimensions={0} | all-to-all | bytes 1114112 | tf_op jit(solution)/shard_map/all_to_all | solution.py:357
  98.9 0.8 fusion.1
  99.8 0.7 slice_reduce_fusion
  (2 shorter events, 0.0 us)
Async XLA Ops:
  7.2 45.3 %all-gather.3.cloned.1.call-start = ((), (), s32[]{:S(2)}) async-start(), calls=%async_computation.2 | async-start | bytes 2621440 | tf_op jit(solution)/shard_map/all_gather | solution.py:352
  30.9 23.3 %copy-start = (f32[8]{0:T(128)S(1)}, f32[8]{0:T(128)}, u32[]{:S(2)}) copy-start(f32[8]{0:T(128)} %shifts_ref.1) | copy-start | bytes 100
  30.9 23.3 %copy-start.1 = (s32[8]{0:T(128)S(1)}, s32[8]{0:T(128)}, u32[]{:S(2)}) copy-start(s32[8]{0:T(128)} %index_ref.1) | copy-start | bytes 100
  31.0 23.3 %copy-start.2 = (f32[3]{0:T(128)S(1)}, f32[3]{0:T(128)}, u32[]{:S(2)}) copy-start(f32[3]{0:T(128)} %velocity_ref.1) | copy-start | bytes 40
Sparse Core Ops, SparseCore 0:
  30.8 21.6 all-gather.2

commit v2 on v1

--- a/solution.py
+++ b/solution.py
@@ -14,6 +14,7 @@
 EPSILON = 1e-06
 VMEM_LIMIT = 40 * 1024 * 1024
 LANES = 128
+UNROLL = 4
 
 
 def with_halo(x, sides, width):
@@ -120,6 +121,17 @@
     return jnp.dot(high, matrix, preferred_element_type=jnp.float32) + jnp.dot(
         low, matrix, preferred_element_type=jnp.float32
     )
+
+
+def sweep(count, get, put):
+    def step(group, carry):
+        planes = [group * UNROLL + k for k in range(UNROLL)]
+        values = [get(x) for x in planes]
+        for x, value in zip(planes, values):
+            put(x, value)
+        return carry
+
+    lax.fori_loop(0, count // UNROLL, step, 0)
 
 
 class Level:
@@ -144,22 +156,21 @@
 
     def neighbours(self, v, x, middle):
         ny = self.ny
-        out = self.backward[0] * v[x, pl.ds(8, ny), :]
-        out += self.forward[0] * v[x + 2, pl.ds(8, ny), :]
-        out += self.backward[1] * v[x + 1, pl.ds(7, ny), :]
-        out += self.forward[1] * v[x + 1, pl.ds(9, ny), :]
-        out += self.low_z * pltpu.roll(middle, 1, 1)
-        out += self.high_z * pltpu.roll(middle, LANES - 1, 1)
-        return out
+        along_x = self.backward[0] * v[x, pl.ds(8, ny), :] + self.forward[0] * v[x + 2, pl.ds(8, ny), :]
+        along_y = self.backward[1] * v[x + 1, pl.ds(7, ny), :] + self.forward[1] * v[x + 1, pl.ds(9, ny), :]
+        along_z = self.low_z * pltpu.roll(middle, 1, 1) + self.high_z * pltpu.roll(middle, LANES - 1, 1)
+        return along_x + along_y + along_z
+
+    def smoothed(self, v, x):
+        middle = self.plane(v, x)
+        pulled = self.f[x] + self.neighbours(v, x, middle)
+        return (1.0 - DAMPING) * middle + self.w[x] * pulled
 
     def smooth(self, src, dst):
-        def step(x, carry):
-            middle = self.plane(src, x)
-            pulled = self.f[x] + self.neighbours(src, x, middle)
-            dst[x + 1, pl.ds(8, self.ny), :] = (1.0 - DAMPING) * middle + self.w[x] * pulled
-            return carry
-
-        lax.fori_loop(0, self.nx, step, 0)
+        def put(x, value):
+            dst[x + 1, pl.ds(8, self.ny), :] = value
+
+        sweep(self.nx, lambda x: self.smoothed(src, x), put)
 
     def defect(self, v, x):
         middle = self.plane(v, x)
@@ -167,54 +178,59 @@
         return pulled - (self.r[x] + self.centre) * middle
 
     def start(self, v):
-        def step(x, carry):
-            weight = DAMPING / (self.r[x] + self.centre)
+        def put(x, weight):
             self.w[x] = weight
             v[x + 1, pl.ds(8, self.ny), :] = weight * self.f[x]
-            return carry
-
-        lax.fori_loop(0, self.nx, step, 0)
-
-    def pair_rows(self, tmp, values, slot):
-        rows = tmp.at[slot]
-        rows[pl.ds(0, self.ny), :] = values
-        half = self.ny // 2
-        return rows[pl.ds(0, half, stride=2), :] + rows[pl.ds(1, half, stride=2), :]
-
-    def coarsen_defect(self, v, tmp, pooled):
-        half = self.ny // 2
-
-        def step(x, carry):
-            both = self.defect(v, 2 * x) + self.defect(v, 2 * x + 1)
-            pooled[pl.ds(pl.multiple_of(x * half, 8), half), :] = self.pair_rows(tmp, both, 0)
-            return carry
-
-        lax.fori_loop(0, self.nx // 2, step, 0)
-
-    def coarsen_reaction(self, tmp, pooled):
-        half = self.ny // 2
-
-        def step(x, carry):
-            both = self.r[2 * x] + self.r[2 * x + 1]
-            pooled[pl.ds(pl.multiple_of(x * half, 8), half), :] = self.pair_rows(tmp, both, 1)
-            return carry
-
-        lax.fori_loop(0, self.nx // 2, step, 0)
+
+        sweep(self.nx, lambda x: DAMPING / (self.r[x] + self.centre), put)
+
+    def pool_pairs(self, plane_of, tmp, pooled):
+        half, ny = self.ny // 2, self.ny
+
+        def put(x, value):
+            rows = tmp.at[lax.rem(x, UNROLL)]
+            rows[pl.ds(0, ny), :] = value
+            both = rows[pl.ds(0, half, stride=2), :] + rows[pl.ds(1, half, stride=2), :]
+            pooled[pl.ds(pl.multiple_of(x * half, 8), half), :] = both
+
+        sweep(self.nx // 2, lambda x: plane_of(2 * x) + plane_of(2 * x + 1), put)
 
     def add_refined(self, v, spread, tmp):
-        half = self.ny // 2
-
-        def step(x, carry):
+        half, ny = self.ny // 2, self.ny
+
+        def get(x):
             part = spread[pl.ds(pl.multiple_of(x * half, 8), half), :]
-            rows = tmp.at[0]
+            rows = tmp.at[lax.rem(x, UNROLL)]
             rows[pl.ds(0, half, stride=2), :] = part
             rows[pl.ds(1, half, stride=2), :] = part
-            full = rows[pl.ds(0, self.ny), :]
+            return rows[pl.ds(0, ny), :]
+
+        def put(x, value):
             for k in range(2):
-                v[2 * x + 1 + k, pl.ds(8, self.ny), :] += full
-            return carry
-
-        lax.fori_loop(0, self.nx // 2, step, 0)
+                v[2 * x + 1 + k, pl.ds(8, ny), :] += value
+
+        sweep(self.nx // 2, get, put)
+
+    def solve_in_registers(self):
+        row = lax.broadcasted_iota(jnp.int32, (self.ny, 1), 0)
+        low_y = jnp.where(row > 0, self.backward[1], 0.0)
+        high_y = jnp.where(row < self.ny - 1, self.forward[1], 0.0)
+        weight = [DAMPING / (self.r[x] + self.centre) for x in range(self.nx)]
+        rhs = [self.f[x] for x in range(self.nx)]
+        v = [w * f for w, f in zip(weight, rhs)]
+        for _ in range(COARSE_SWEEPS - 1):
+            new = []
+            for x, here in enumerate(v):
+                along_z = self.low_z * pltpu.roll(here, 1, 1) + self.high_z * pltpu.roll(here, LANES - 1, 1)
+                along_y = low_y * pltpu.roll(here, 1, 0) + high_y * pltpu.roll(here, self.ny - 1, 0)
+                pulled = rhs[x] + along_z + along_y
+                if x > 0:
+                    pulled += self.backward[0] * v[x - 1]
+                if x < self.nx - 1:
+                    pulled += self.forward[0] * v[x + 1]
+                new.append((1.0 - DAMPING) * here + weight[x] * pulled)
+            v = new
+        return jnp.concatenate(v, axis=0)
 
 
 def zero_rim(v, nx, ny):
@@ -235,44 +251,40 @@
     bx, by = nx // gx_size, ny // gy_size
     pieces = refs[:gy_size]
     out_ref = refs[gy_size]
-    f0, r0, w0, va, vb, f1, r1, w1, v1a, v1b, f2, r2, w2, v2a, v2b, pooled, tmp = refs[gy_size + 1 :]
+    f0, r0, w0, va, vb, f1, r1, w1, v1a, v1b, f2, r2, pooled, tmp = refs[gy_size + 1 :]
     column, row_block = place_ref[0], place_ref[1]
     shift = shifts_ref[index_ref[column]]
     pool, spread = pool_ref[...], spread_ref[...]
 
     fine = Level(0, sizes, velocity_ref, shift, f0, r0, w0)
     mid = Level(1, sizes, velocity_ref, shift, f1, r1, w1)
-    deep = Level(2, sizes, velocity_ref, shift, f2, r2, w2)
-    for v, level in ((va, fine), (vb, fine), (v1a, mid), (v1b, mid), (v2a, deep), (v2b, deep)):
+    deep = Level(2, sizes, velocity_ref, shift, f2, r2, None)
+    for v, level in ((va, fine), (vb, fine), (v1a, mid), (v1b, mid)):
         zero_rim(v, level.nx, level.ny)
 
-    for j, piece in enumerate(pieces):
+    for k, piece in enumerate(pieces):
+        rows = pl.ds(pl.multiple_of(place_ref[1 + k] * by, 8), by)
         for i in range(gx_size):
-            f0[pl.ds(i * bx, bx), pl.ds(j * by, by), :] = piece[i, 0]
-            r0[pl.ds(i * bx, bx), pl.ds(j * by, by), :] = piece[i, 1]
+            f0[pl.ds(i * bx, bx), rows, :] = piece[i, 0]
+            r0[pl.ds(i * bx, bx), rows, :] = piece[i, 1]
 
     rows1, rows2 = mid.nx * mid.ny, deep.nx * deep.ny
     fine.start(va)
     fine.smooth(va, vb)
-    fine.coarsen_defect(vb, tmp, pooled)
+    fine.pool_pairs(lambda x: fine.defect(vb, x), tmp, pooled)
     f1[...] = split_dot(pooled[pl.ds(0, rows1), :], pool).reshape(f1.shape)
-    fine.coarsen_reaction(tmp, pooled)
+    fine.pool_pairs(lambda x: r0[x], tmp, pooled)
     r1[...] = split_dot(pooled[pl.ds(0, rows1), :], pool).reshape(r1.shape)
 
     mid.start(v1a)
     mid.smooth(v1a, v1b)
-    mid.coarsen_defect(v1b, tmp, pooled)
+    mid.pool_pairs(lambda x: mid.defect(v1b, x), tmp, pooled)
     f2[...] = split_dot(pooled[pl.ds(0, rows2), :], pool).reshape(f2.shape)
-    mid.coarsen_reaction(tmp, pooled)
+    mid.pool_pairs(lambda x: r1[x], tmp, pooled)
     r2[...] = split_dot(pooled[pl.ds(0, rows2), :], pool).reshape(r2.shape)
 
-    deep.start(v2a)
-    src, dst = v2a, v2b
-    for _ in range(COARSE_SWEEPS - 1):
-        deep.smooth(src, dst)
-        src, dst = dst, src
-
-    values = src[pl.ds(1, deep.nx), pl.ds(8, deep.ny), :].reshape(rows2, LANES)
+    values = deep.solve_in_registers()
+
     pooled[pl.ds(0, rows2), :] = split_dot(values, spread)
     mid.add_refined(v1b, pooled, tmp)
     mid.smooth(v1b, v1a)
@@ -291,9 +303,11 @@
             x = i * bx + k
             rest = fine.defect(vb, x)
             total = total + jnp.sum((rest * rest).reshape(ny // 8, 8, LANES), axis=0)
-            tmp[0, pl.ds(0, ny), :] = rest
+            tmp[k, pl.ds(0, ny), :] = rest
+        for k in range(bx):
+            x = i * bx + k
             out_ref[i, pl.ds(k * by, by), :] = vb[x + 1, pl.ds(8 + row0, by), :]
-            out_ref[i, pl.ds(area + k * by, by), :] = tmp[0, pl.ds(row0, by), :]
+            out_ref[i, pl.ds(area + k * by, by), :] = tmp[k, pl.ds(row0, by), :]
         return total
 
     squares = lax.fori_loop(0, gx_size, finish, jnp.zeros((8, LANES), jnp.float32))
@@ -324,9 +338,10 @@
         return pltpu.VMEM(((nx >> index) + 2, (ny >> index) + 16, LANES), f32)
 
     scratch = []
-    for index in range(LEVELS):
+    for index in range(LEVELS - 1):
         scratch += [grid(index)] * 3 + [rimmed(index)] * 2
-    scratch += [pltpu.VMEM(((nx // 2) * (ny // 2), LANES), f32), pltpu.VMEM((2, ny, LANES), f32)]
+    scratch += [grid(LEVELS - 1)] * 2
+    scratch += [pltpu.VMEM(((nx // 2) * (ny // 2), LANES), f32), pltpu.VMEM((UNROLL, ny, LANES), f32)]
     smem = pl.BlockSpec(memory_space=pltpu.SMEM)
     vmem = pl.BlockSpec(memory_space=pltpu.VMEM)
     pool, spread = pooling_matrices()
@@ -345,12 +360,17 @@
     columns, bx, by, nz = source.shape
     gx_size, gy_size = lax.axis_size("gx"), lax.axis_size("gy")
     sizes = (bx * gx_size, by * gy_size, nz)
-    place = jnp.stack([lax.axis_index("gx"), lax.axis_index("gy")]).astype(jnp.int32)
-
     both = jnp.stack([source, jnp.broadcast_to(reaction[None], source.shape)], axis=1)
     mine = lax.all_to_all(both, "gx", 0, 0)
-    gathered = lax.all_gather(mine, "gy")
-    pieces = [gathered[j] for j in range(gy_size)]
+
+    row_block = lax.axis_index("gy")
+    pieces, owners, stride = [mine], [row_block], gy_size // 2
+    while stride:
+        pairs = [(i, i ^ stride) for i in range(gy_size)]
+        pieces = pieces + [lax.ppermute(piece, "gy", pairs) for piece in pieces]
+        owners = owners + [jnp.bitwise_xor(owner, stride) for owner in owners]
+        stride //= 2
+    place = jnp.stack([lax.axis_index("gx")] + owners).astype(jnp.int32)
     results = column_cycle(
         pieces, place, shifts, shift_index, velocity, sizes, (gx_size, gy_size)
     )
@@ -367,8 +387,10 @@
     def body(source, reaction, shifts, shift_index, velocity):
         columns, bx, by, nz = source.shape
         cells = bx * gx_size * by * gy_size
-        fits = nz == LANES and bx % 4 == 0 and by % 16 == 0 and cells * nz * 4 <= 2**20
-        plan = column_body if columns == gx_size and fits else halo_body
+        fits = nz == LANES and by % 16 == 0 and cells * nz * 4 <= 2**20
+        dealt = columns == gx_size and gx_size % UNROLL == 0 and bx == UNROLL
+        dealt = dealt and gy_size & (gy_size - 1) == 0
+        plan = column_body if dealt and fits else halo_body
         return plan(source, reaction, shifts, shift_index, velocity)
 
     return jax.shard_map(

time: 108 us -> 71 us (0.66)
  between operations: 14.1 us -> 0.69 us
  Pallas kernels: 23 us -> 10.5 us
  waiting for transfers between devices: 21.5 us -> 12.7 us
  starting transfers between devices: 0.04 us -> 1.52 us
  blocking collectives: 43.4 us -> 42 us
    all_gather x1 -> x0, waiting for transfers between devices: 21.5 us -> none  [column_body(): gathered = lax.all_gather(mine, 'gy')]
    ppermute x0 -> x3, waiting for transfers between devices: none -> 12.7 us  [column_body(): pieces = pieces + [lax.ppermute(piece, 'gy', pairs) for piece in pieces]]
    pallas_call x1, Pallas kernels: 23 us -> 10.5 us  [column_cycle(): pl.pallas_call(functools.partial(cycle_kernel, sizes, blocks), out_shape=...]
    slice x1 -> x0, local copies, waits for them, and re-layouts: 1.75 us -> none  [column_body(): pieces = [gathered[j] for j in range(gy_size)]]
    ppermute x0 -> x3, starting transfers between devices: none -> 1.52 us  [column_body(): pieces = pieces + [lax.ppermute(piece, 'gy', pairs) for piece in pieces]]
    all_to_all x1, blocking collectives: 21.7 us -> 20.4 us  [column_body(): back = lax.all_to_all(results, 'gx', 0, 0)]
  transfers between devices with their start and end apart: 1 -> 3, of which waited for: 1 -> 2; matrix products, arithmetic and copies ran while one was open for 0% -> 0% of each run, Pallas kernels for 0% -> 0%
where the time goes in v2:
time: 71 us; the launch traced here: 70.8 us
  blocking collectives  42 us (59%)
  waiting for transfers between devices  12.7 us (18%)
  Pallas kernels  10.5 us (15%)
  local copies, waits for them, and re-layouts  3.22 us (5%)
  starting transfers between devices  1.52 us (2%)
    all_to_all x1, blocking collectives, column_body(): mine = lax.all_to_all(both, 'gx', 0, 0)  21.6 us
    all_to_all x1, blocking collectives, column_body(): back = lax.all_to_all(results, 'gx', 0, 0)  20.4 us
    ppermute x3, waiting for transfers between devices, column_body(): pieces = pieces + [lax.ppermute(piece, 'gy', pairs) for piece in pieces]  12.7 us
    pallas_call x1, Pallas kernels, column_cycle(): pl.pallas_call(functools.partial(cycle_kernel, sizes, blocks), out_shape=...  10.5 us
    ppermute x3, starting transfers between devices, column_body(): pieces = pieces + [lax.ppermute(piece, 'gy', pairs) for piece in pieces]  1.52 us
  transfers between devices with their start and end apart: 3, of which 2 were waited for; matrix products, arithmetic and copies ran while one was open for 0% of the time, Pallas kernels for 0%

profile of v2, /device:TPU:0, one launch (start us, length us, event | category | flops | bytes accessed | tf_op | source)
XLA Modules:
  0.0 70.8 jit_solution(6780623795826251642)
XLA Ops:
  0.6 0.0 copy-start.3
  0.6 0.8 %stack_broadcast_in_dim.2 = f32[8,1,4,16,128]{4,3,2,1,0:T(8,128)S(1)} broadcast(f32[4,16,128]{2,1,0:T(8,128)} %param.6), dimensions={2,3,4} | broadcast | bytes 294912 | tf_op jit(solution)/shard_map/stack;broadcast_in_dim | solution.py:363
  1.5 0.1 copy-done.3
  1.6 21.6 %all_to_all.10.refs_0_ = f32[8,2,4,16,128]{4,3,2,1,0:T(8,128)S(1)} all-to-all(f32[8,2,4,16,128]{4,3,2,1,0:T(8,128)S(1)} %pad_maximum_fusion), channel_id=1, replica_groups=mesh['gx'=8,'gy'=4] {'gx'}, dimensions={0} | all-to-all | bytes 1048576 | tf_op jit(solution)/shard_map/all_to_all | solution.py:364
  23.2 1.5 %collective-permute-start = (f32[8,2,4,16,128]{4,3,2,1,0:T(8,128)S(1)}, f32[8,2,4,16,128]{4,3,2,1,0:T(8,128)S(1)}, u32[]{:S(2)}, u32[]{:S(2)}) collective-permute-start(f32[8,2,4,16,128]{4,3,2,1,0:T(8,128)S(1)} %all_to_all.10.refs_0_), channel_id=1, source_target_pairs={{0,2},{1,3},{2,0},{3,1},{4,6},{5,7},{6,4},{7,5},{8,10},{9,11},{10,... | collective-permute-start | bytes 1572872 | tf_op jit(solution)/shard_map/ppermute | solution.py:370
  24.7 0.0 collective-permute-start.1
  24.8 11.0 %collective-permute-done.refs_1_ = f32[8,2,4,16,128]{4,3,2,1,0:T(8,128)S(1)} collective-permute-done((f32[8,2,4,16,128]{4,3,2,1,0:T(8,128)S(1)}, f32[8,2,4,16,128]{4,3,2,1,0:T(8,128)S(1)}, u32[]{:S(2)}, u32[]{:S(2)}) %collective-permute-start) | collective-permute-done | bytes 524320 | tf_op jit(solution)/shard_map/ppermute | solution.py:370
  35.8 0.0 collective-permute-start.2
  35.8 0.1 stack.29.place_ref
  35.9 0.1 select_convert_fusion
  36.0 0.0 collective-permute-done.1.refs_2_
  36.0 1.7 %collective-permute-done.2.refs_3_ = f32[8,2,4,16,128]{4,3,2,1,0:T(8,128)S(1)} collective-permute-done((f32[8,2,4,16,128]{4,3,2,1,0:T(8,128)S(1)}, f32[8,2,4,16,128]{4,3,2,1,0:T(8,128)S(1)}, u32[]{:S(2)}, u32[]{:S(2)}) %collective-permute-start.2) | collective-permute-done | bytes 524320 | tf_op jit(solution)/shard_map/ppermute | solution.py:370
  37.7 0.0 copy-start
  37.7 0.0 copy-start.1
  37.7 0.0 copy-start.2
  37.7 0.6 copy-done
  38.3 0.0 copy-done.1
  38.3 0.0 copy-done.2
  38.4 10.5 %cycle.1 = f32[8,136,128]{2,1,0:T(8,128)S(1)} custom-call(s32[5]{0:T(128)S(1)} %stack.29.place_ref, f32[8]{0:T(128)S(1)} %copy-done, s32[8]{0:T(128)S(1)} %copy-done.1, f32[3]{0:T(128)S(1)} %copy-done.2, bf16[128,128]{1,0:T(8,128)(2,1)S(1)} %get-tuple-element.6.pool_ref, bf16[128,128]{1,0:T(8,128)(2,1)S(1)} %get-tuple-element.5.spread_ref, ...), custom_call_target="tpu_custom_call" | custom-call | tf_op jit(solution)/shard_map/cycle/pallas_call | solution.py:348
  48.8 20.4 %all_to_all.11 = f32[8,136,128]{2,1,0:T(8,128)S(1)} all-to-all(f32[8,136,128]{2,1,0:T(8,128)S(1)} %cycle.1), channel_id=1, replica_groups=mesh['gx'=8,'gy'=4] {'gx'}, dimensions={0} | all-to-all | bytes 1114112 | tf_op jit(solution)/shard_map/all_to_all | solution.py:377
  69.3 0.7 slice_reduce_fusion
  69.9 0.8 %fusion = (f32[8,64,128]{2,1,0:T(8,128)}, f32[8,64,128]{2,1,0:T(8,128)}) fusion(f32[8,136,128]{2,1,0:T(8,128)S(1)} %all_to_all.11), kind=kLoop, calls=%fused_computation.11 | loop fusion | bytes 1048576 | tf_op jit(solution)/shard_map/slice | solution.py:380
  (3 shorter events, 0.1 us)
Async XLA Ops:
  0.6 1.0 %copy-start.3 = (f32[8,4,16,128]{3,2,1,0:T(8,128)S(1)}, f32[8,4,16,128]{3,2,1,0:T(8,128)}, u32[]{:S(2)}) copy-start(f32[8,4,16,128]{3,2,1,0:T(8,128)} %param.5) | copy-start | bytes 786436
  23.2 12.5 %collective-permute-start = (f32[8,2,4,16,128]{4,3,2,1,0:T(8,128)S(1)}, f32[8,2,4,16,128]{4,3,2,1,0:T(8,128)S(1)}, u32[]{:S(2)}, u32[]{:S(2)}) collective-permute-start(f32[8,2,4,16,128]{4,3,2,1,0:T(8,128)S(1)} %all_to_all.10.refs_0_), channel_id=1, source_target_pairs={{0,2},{1,3},{2,0},{3,1},{4,6},{5,7},{6,4},{7,5},{8,10},{9,11},{10,... | collective-permute-start | bytes 1572872 | tf_op jit(solution)/shard_map/ppermute | solution.py:370
  24.7 11.2 %collective-permute-start.1 = (f32[8,2,4,16,128]{4,3,2,1,0:T(8,128)S(1)}, f32[8,2,4,16,128]{4,3,2,1,0:T(8,128)S(1)}, u32[]{:S(2)}, u32[]{:S(2)}) collective-permute-start(f32[8,2,4,16,128]{4,3,2,1,0:T(8,128)S(1)} %all_to_all.10.refs_0_), channel_id=1, source_target_pairs={{0,1},{1,0},{2,3},{3,2},{4,5},{5,4},{6,7},{7,6},{8,9},{9,8},{10,11... | collective-permute-start | bytes 1572872 | tf_op jit(solution)/shard_map/ppermute | solution.py:370
  35.8 1.9 %collective-permute-start.2 = (f32[8,2,4,16,128]{4,3,2,1,0:T(8,128)S(1)}, f32[8,2,4,16,128]{4,3,2,1,0:T(8,128)S(1)}, u32[]{:S(2)}, u32[]{:S(2)}) collective-permute-start(f32[8,2,4,16,128]{4,3,2,1,0:T(8,128)S(1)} %collective-permute-done.refs_1_), channel_id=1, source_target_pairs={{0,1},{1,0},{2,3},{3,2},{4,5},{5,4},{6,7},{7,6},{8,9},{9,8},{10,11... | collective-permute-start | bytes 1572872 | tf_op jit(solution)/shard_map/ppermute | solution.py:370
  37.7 0.7 copy-start
  37.7 0.7 copy-start.1
  37.7 0.7 copy-start.2

commit v3 on v2

--- a/solution.py
+++ b/solution.py
@@ -249,9 +249,9 @@
     gx_size, gy_size = blocks
     nx, ny, nz = sizes
     bx, by = nx // gx_size, ny // gy_size
-    pieces = refs[:gy_size]
-    out_ref = refs[gy_size]
-    f0, r0, w0, va, vb, f1, r1, w1, v1a, v1b, f2, r2, pooled, tmp = refs[gy_size + 1 :]
+    f_pieces, r_pieces = refs[:gy_size], refs[gy_size : 2 * gy_size]
+    out_refs = refs[2 * gy_size : 2 * gy_size + gx_size]
+    f0, r0, w0, va, vb, f1, r1, w1, v1a, v1b, f2, r2, pooled, tmp = refs[2 * gy_size + gx_size :]
     column, row_block = place_ref[0], place_ref[1]
     shift = shifts_ref[index_ref[column]]
     pool, spread = pool_ref[...], spread_ref[...]
@@ -262,11 +262,12 @@
     for v, level in ((va, fine), (vb, fine), (v1a, mid), (v1b, mid)):
         zero_rim(v, level.nx, level.ny)
 
-    for k, piece in enumerate(pieces):
-        rows = pl.ds(pl.multiple_of(place_ref[1 + k] * by, 8), by)
-        for i in range(gx_size):
-            f0[pl.ds(i * bx, bx), rows, :] = piece[i, 0]
-            r0[pl.ds(i * bx, bx), rows, :] = piece[i, 1]
+    for j, (f_piece, r_piece) in enumerate(zip(f_pieces, r_pieces)):
+        rows = pl.ds(pl.multiple_of(place_ref[1 + j] * by, 8), by)
+        for k in range(gx_size):
+            planes = pl.ds(lax.rem(column + gx_size - k, gx_size) * bx, bx)
+            f0[planes, rows, :] = f_piece[k]
+            r0[planes, rows, :] = r_piece[k]
 
     rows1, rows2 = mid.nx * mid.ny, deep.nx * deep.ny
     fine.start(va)
@@ -298,23 +299,45 @@
     area = bx * by
     row0 = pl.multiple_of(row_block * by, 8)
 
-    def finish(i, total):
-        for k in range(bx):
-            x = i * bx + k
-            rest = fine.defect(vb, x)
-            total = total + jnp.sum((rest * rest).reshape(ny // 8, 8, LANES), axis=0)
-            tmp[k, pl.ds(0, ny), :] = rest
-        for k in range(bx):
-            x = i * bx + k
-            out_ref[i, pl.ds(k * by, by), :] = vb[x + 1, pl.ds(8 + row0, by), :]
-            out_ref[i, pl.ds(area + k * by, by), :] = tmp[k, pl.ds(row0, by), :]
-        return total
-
-    squares = lax.fori_loop(0, gx_size, finish, jnp.zeros((8, LANES), jnp.float32))
-    mean = jnp.sum(squares) / (nx * ny * nz) + EPSILON
+    total = jnp.zeros((8, LANES), jnp.float32)
+    for k, out_ref in enumerate(out_refs):
+        first = lax.rem(column + k, gx_size) * bx
+        rest = [fine.defect(vb, first + p) for p in range(bx)]
+        for p in range(bx):
+            total = total + jnp.sum((rest[p] * rest[p]).reshape(ny // 8, 8, LANES), axis=0)
+            tmp[p, pl.ds(0, ny), :] = rest[p]
+        for p in range(bx):
+            out_ref[pl.ds(p * by, by), :] = vb[first + p + 1, pl.ds(8 + row0, by), :]
+            out_ref[pl.ds(area + p * by, by), :] = tmp[p, pl.ds(row0, by), :]
+    mean = jnp.sum(total) / (nx * ny * nz) + EPSILON
     rms = jnp.sqrt(jnp.full((8, LANES), mean, jnp.float32))
-    for i in range(gx_size):
-        out_ref[i, pl.ds(2 * area, 8), :] = rms
+    for out_ref in out_refs:
+        out_ref[pl.ds(2 * area, 8), :] = rms
+
+
+def collect_kernel(bx, by, place_ref, *refs):
+    count = len(refs) - 3
+    parts, (iterate_ref, residual_ref, rms_ref) = refs[:count], refs[count:]
+    area = bx * by
+    for k, part in enumerate(parts):
+        column = lax.rem(place_ref[0] + count - k, count)
+        iterate_ref[column] = part[pl.ds(0, area), :].reshape(bx, by, LANES)
+        residual_ref[column] = part[pl.ds(area, area), :].reshape(bx, by, LANES)
+        rms_ref[column] = jnp.max(part[pl.ds(2 * area, 8), :])
+
+
+def collect(parts, place, shape):
+    columns, bx, by, nz = shape
+    smem = pl.BlockSpec(memory_space=pltpu.SMEM)
+    vmem = pl.BlockSpec(memory_space=pltpu.VMEM)
+    block = jax.ShapeDtypeStruct(shape, jnp.float32)
+    return pl.pallas_call(
+        functools.partial(collect_kernel, bx, by),
+        out_shape=(block, block, jax.ShapeDtypeStruct((columns,), jnp.float32)),
+        in_specs=[smem] + [vmem] * len(parts),
+        out_specs=(vmem, vmem, smem),
+        name="collect",
+    )(place, *parts)
 
 
 def pooling_matrices():
@@ -347,38 +370,58 @@
     pool, spread = pooling_matrices()
     return pl.pallas_call(
         functools.partial(cycle_kernel, sizes, blocks),
-        out_shape=jax.ShapeDtypeStruct((gx_size, 2 * area + 8, LANES), f32),
-        in_specs=[smem] * 4 + [vmem] * (2 + gy_size),
-        out_specs=vmem,
+        out_shape=[jax.ShapeDtypeStruct((2 * area + 8, LANES), f32)] * gx_size,
+        in_specs=[smem] * 4 + [vmem] * (2 + 2 * gy_size),
+        out_specs=[vmem] * gx_size,
         scratch_shapes=scratch,
         compiler_params=pltpu.CompilerParams(vmem_limit_bytes=VMEM_LIMIT),
         name="cycle",
     )(place, shifts, shift_index, velocity, pool, spread, *pieces)
 
 
+def deal(block_for):
+    size = lax.axis_size("gx")
+    moved = [block_for(0)]
+    for k in range(1, size):
+        pairs = [(i, (i + k) % size) for i in range(size)]
+        moved.append(lax.ppermute(block_for(k), "gx", pairs))
+    return moved
+
+
+def gather_rows(piece):
+    size = lax.axis_size("gy")
+    pieces, stride = [piece], size // 2
+    while stride:
+        pairs = [(i, i ^ stride) for i in range(size)]
+        pieces = pieces + [lax.ppermute(p, "gy", pairs) for p in pieces]
+        stride //= 2
+    return pieces
+
+
+def row_owners():
+    owners, stride = [lax.axis_index("gy")], lax.axis_size("gy") // 2
+    while stride:
+        owners = owners + [jnp.bitwise_xor(owner, stride) for owner in owners]
+        stride //= 2
+    return owners
+
+
 def column_body(source, reaction, shifts, shift_index, velocity):
     columns, bx, by, nz = source.shape
     gx_size, gy_size = lax.axis_size("gx"), lax.axis_size("gy")
     sizes = (bx * gx_size, by * gy_size, nz)
-    both = jnp.stack([source, jnp.broadcast_to(reaction[None], source.shape)], axis=1)
-    mine = lax.all_to_all(both, "gx", 0, 0)
-
-    row_block = lax.axis_index("gy")
-    pieces, owners, stride = [mine], [row_block], gy_size // 2
-    while stride:
-        pairs = [(i, i ^ stride) for i in range(gy_size)]
-        pieces = pieces + [lax.ppermute(piece, "gy", pairs) for piece in pieces]
-        owners = owners + [jnp.bitwise_xor(owner, stride) for owner in owners]
-        stride //= 2
-    place = jnp.stack([lax.axis_index("gx")] + owners).astype(jnp.int32)
+    column = lax.axis_index("gx")
+    place = jnp.stack([column] + row_owners()).astype(jnp.int32)
+
+    def column_for(k):
+        return lax.dynamic_index_in_dim(source, lax.rem(column + k, columns), 0, keepdims=False)
+
+    r_pieces = gather_rows(jnp.stack(deal(lambda k: reaction)))
+    f_pieces = gather_rows(jnp.stack(deal(column_for)))
     results = column_cycle(
-        pieces, place, shifts, shift_index, velocity, sizes, (gx_size, gy_size)
+        f_pieces + r_pieces, place, shifts, shift_index, velocity, sizes, (gx_size, gy_size)
     )
-    back = lax.all_to_all(results, "gx", 0, 0)
-    area = bx * by
-    iterate = back[:, :area].reshape(source.shape)
-    residual = back[:, area : 2 * area].reshape(source.shape)
-    return iterate, residual, back[:, 2 * area, 0]
+    return collect(deal(lambda k: results[k]), place, source.shape)
 
 
 def solution(mesh):

time: 71 us -> 78.2 us (1.10)
  blocking collectives: 42 us -> 0 us
  starting transfers between devices: 1.52 us -> 30.9 us
  waiting for transfers between devices: 12.7 us -> 30.3 us
  Pallas kernels: 10.5 us -> 11.9 us
    all_to_all x2 -> x0, blocking collectives: 42 us -> none  [the longest x1 21.6 us: column_body(): mine = lax.all_to_all(both, 'gx', 0, 0)]
    ppermute x3 -> x27, starting transfers between devices: 1.52 us -> 30.9 us  [the longest x21 27.2 us: deal(): moved.append(lax.ppermute(block_for(k), 'gx', pairs))]
    ppermute x3 -> x27, waiting for transfers between devices: 12.7 us -> 30.3 us  [the longest x21 24.7 us: deal(): moved.append(lax.ppermute(block_for(k), 'gx', pairs))]
    pallas_call x0 -> x1, Pallas kernels: none -> 1.97 us  [collect(): pl.pallas_call(functools.partial(collect_kernel, bx, by), out_shape=(bloc...]
    unnamed x8 -> x39, local copies, waits for them, and re-layouts: 0.82 us -> 2.78 us
    slice x2 -> x0, local copies, waits for them, and re-layouts: 1.5 us -> none  [the longest x1 0.84 us: column_body(): residual = back[:, area:2 * area].reshape(source.shape)]
    squeeze x0 -> x1, local copies, waits for them, and re-layouts: none -> 0.89 us  [column_for(): lax.dynamic_index_in_dim(source, lax.rem(column + k, columns), 0, keepdim...]
    another operation x2 -> x3, local copies, waits for them, and re-layouts: 0.9 us -> 0.09 us  [the longest x1 0.09 us: column_body(): place = jnp.stack([column] + row_owners()).astype(jnp.int32)]
  transfers between devices with their start and end apart: 3 -> 27, of which waited for: 2 -> 10; matrix products, arithmetic and copies ran while one was open for 0% -> 1% of each run, Pallas kernels for 0% -> 0%
where the time goes in v3:
time: 78.2 us; the launch traced here: 77.8 us
  starting transfers between devices  30.9 us (40%)
  waiting for transfers between devices  30.3 us (39%)
  Pallas kernels  11.9 us (15%)
  local copies, waits for them, and re-layouts  3.76 us (5%)
  between operations  0.84 us (1%)
    ppermute x21, starting transfers between devices, deal(): moved.append(lax.ppermute(block_for(k), 'gx', pairs))  27.2 us
    ppermute x21, waiting for transfers between devices, deal(): moved.append(lax.ppermute(block_for(k), 'gx', pairs))  24.7 us
    pallas_call x1, Pallas kernels, column_cycle(): pl.pallas_call(functools.partial(cycle_kernel, sizes, blocks), out_shape=...  9.94 us
    ppermute x6, waiting for transfers between devices, gather_rows(): pieces = pieces + [lax.ppermute(p, 'gy', pairs) for p in pieces]  5.61 us
    ppermute x6, starting transfers between devices, gather_rows(): pieces = pieces + [lax.ppermute(p, 'gy', pairs) for p in pieces]  3.68 us
    unnamed x39, local copies, waits for them, and re-layouts  2.78 us
    pallas_call x1, Pallas kernels, collect(): pl.pallas_call(functools.partial(collect_kernel, bx, by), out_shape=(bloc...  1.97 us
  transfers between devices with their start and end apart: 27, of which 10 were waited for; matrix products, arithmetic and copies ran while one was open for 1% of the time, Pallas kernels for 0%

profile of v3, /device:TPU:0, one launch (start us, length us, event | category | flops | bytes accessed | tf_op | source)
XLA Modules:
  0.0 77.8 jit_solution(5899501684846287054)
XLA Ops:
  0.6 5.0 %collective-permute-start.14 = (f32[4,16,128]{2,1,0:T(8,128)}, f32[4,16,128]{2,1,0:T(8,128)S(1)}, u32[]{:S(2)}, u32[]{:S(2)}) collective-permute-start(f32[4,16,128]{2,1,0:T(8,128)} %param.6), channel_id=1, source_target_pairs={{0,20},{4,24},{8,28},{12,0},{16,4},{20,8},{24,12},{28,16},{1,21},{... | collective-permute-start | bytes 98312 | tf_op jit(solution)/shard_map/ppermute | solution.py:387
  6.0 1.7 %collective-permute-start.12 = (f32[4,16,128]{2,1,0:T(8,128)}, f32[4,16,128]{2,1,0:T(8,128)S(1)}, u32[]{:S(2)}, u32[]{:S(2)}) collective-permute-start(f32[4,16,128]{2,1,0:T(8,128)} %param.6), channel_id=1, source_target_pairs={{0,12},{4,16},{8,20},{12,24},{16,28},{20,0},{24,4},{28,8},{1,13},{... | collective-permute-start | bytes 98312 | tf_op jit(solution)/shard_map/ppermute | solution.py:387
  7.6 2.5 %collective-permute-start.11 = (f32[4,16,128]{2,1,0:T(8,128)}, f32[4,16,128]{2,1,0:T(8,128)S(1)}, u32[]{:S(2)}, u32[]{:S(2)}) collective-permute-start(f32[4,16,128]{2,1,0:T(8,128)} %param.6), channel_id=1, source_target_pairs={{0,8},{4,12},{8,16},{12,20},{16,24},{20,28},{24,0},{28,4},{1,9},{5... | collective-permute-start | bytes 98312 | tf_op jit(solution)/shard_map/ppermute | solution.py:387
  10.1 1.5 %collective-permute-start.10 = (f32[4,16,128]{2,1,0:T(8,128)}, f32[4,16,128]{2,1,0:T(8,128)S(1)}, u32[]{:S(2)}, u32[]{:S(2)}) collective-permute-start(f32[4,16,128]{2,1,0:T(8,128)} %param.6), channel_id=1, source_target_pairs={{0,4},{4,8},{8,12},{12,16},{16,20},{20,24},{24,28},{28,0},{1,5},{5... | collective-permute-start | bytes 98312 | tf_op jit(solution)/shard_map/ppermute | solution.py:387
  13.3 3.6 %collective-permute-done.10 = f32[4,16,128]{2,1,0:T(8,128)S(1)} collective-permute-done((f32[4,16,128]{2,1,0:T(8,128)}, f32[4,16,128]{2,1,0:T(8,128)S(1)}, u32[]{:S(2)}, u32[]{:S(2)}) %collective-permute-start.10) | collective-permute-done | bytes 32800 | tf_op jit(solution)/shard_map/ppermute | solution.py:387
  17.5 1.5 %collective-permute-start.6 = (f32[4,16,128]{2,1,0:T(8,128)S(1)}, f32[4,16,128]{2,1,0:T(8,128)S(1)}, u32[]{:S(2)}, u32[]{:S(2)}) collective-permute-start(f32[4,16,128]{2,1,0:T(8,128)S(1)} %get-tuple-element.19), channel_id=1, source_target_pairs={{0,28},{4,0},{8,4},{12,8},{16,12},{20,16},{24,20},{28,24},{1,29},{... | collective-permute-start | bytes 98312 | tf_op jit(solution)/shard_map/ppermute | solution.py:387
  19.0 1.2 %collective-permute-start.4 = (f32[4,16,128]{2,1,0:T(8,128)S(1)}, f32[4,16,128]{2,1,0:T(8,128)S(1)}, u32[]{:S(2)}, u32[]{:S(2)}) collective-permute-start(f32[4,16,128]{2,1,0:T(8,128)S(1)} %get-tuple-element.20), channel_id=1, source_target_pairs={{0,20},{4,24},{8,28},{12,0},{16,4},{20,8},{24,12},{28,16},{1,21},{... | collective-permute-start | bytes 98312 | tf_op jit(solution)/shard_map/ppermute | solution.py:387
  20.2 1.9 %collective-permute-start.3 = (f32[4,16,128]{2,1,0:T(8,128)S(1)}, f32[4,16,128]{2,1,0:T(8,128)S(1)}, u32[]{:S(2)}, u32[]{:S(2)}) collective-permute-start(f32[4,16,128]{2,1,0:T(8,128)S(1)} %get-tuple-element.21), channel_id=1, source_target_pairs={{0,16},{4,20},{8,24},{12,28},{16,0},{20,4},{24,8},{28,12},{1,17},{... | collective-permute-start | bytes 98312 | tf_op jit(solution)/shard_map/ppermute | solution.py:387
  22.0 2.8 %collective-permute-start.2 = (f32[4,16,128]{2,1,0:T(8,128)S(1)}, f32[4,16,128]{2,1,0:T(8,128)S(1)}, u32[]{:S(2)}, u32[]{:S(2)}) collective-permute-start(f32[4,16,128]{2,1,0:T(8,128)S(1)} %get-tuple-element.22), channel_id=1, source_target_pairs={{0,12},{4,16},{8,20},{12,24},{16,28},{20,0},{24,4},{28,8},{1,13},{... | collective-permute-start | bytes 98312 | tf_op jit(solution)/shard_map/ppermute | solution.py:387
  24.9 6.6 %collective-permute-done = f32[4,16,128]{2,1,0:T(8,128)S(1)} collective-permute-done((f32[4,16,128]{2,1,0:T(8,128)S(1)}, f32[4,16,128]{2,1,0:T(8,128)S(1)}, u32[]{:S(2)}, u32[]{:S(2)}) %collective-permute-start) | collective-permute-done | bytes 32800 | tf_op jit(solution)/shard_map/ppermute | solution.py:387
  31.5 5.7 %collective-permute-done.1 = f32[4,16,128]{2,1,0:T(8,128)S(1)} collective-permute-done((f32[4,16,128]{2,1,0:T(8,128)S(1)}, f32[4,16,128]{2,1,0:T(8,128)S(1)}, u32[]{:S(2)}, u32[]{:S(2)}) %collective-permute-start.1) | collective-permute-done | bytes 32800 | tf_op jit(solution)/shard_map/ppermute | solution.py:387
  37.2 1.6 %collective-permute-start.17 = (f32[8,4,16,128]{3,2,1,0:T(8,128)S(1)}, f32[8,4,16,128]{3,2,1,0:T(8,128)S(1)}, u32[]{:S(2)}, u32[]{:S(2)}) collective-permute-start(f32[8,4,16,128]{3,2,1,0:T(8,128)S(1)} %constant_dynamic-update-slice_fusion.8.refs_4_), channel_id=1, source_target_pairs={{0,2},{1,3},{2,0},{3,1},{4,6},{5,7},{6,4},{7,5},{8,10},{9,11},{10,... | collective-permute-start | bytes 786440 | tf_op jit(solution)/shard_map/ppermute | solution.py:396
  38.8 2.3 %collective-permute-done.5 = f32[4,16,128]{2,1,0:T(8,128)S(1)} collective-permute-done((f32[4,16,128]{2,1,0:T(8,128)S(1)}, f32[4,16,128]{2,1,0:T(8,128)S(1)}, u32[]{:S(2)}, u32[]{:S(2)}) %collective-permute-start.5) | collective-permute-done | bytes 32800 | tf_op jit(solution)/shard_map/ppermute | solution.py:387
  41.1 1.6 %collective-permute-start.7 = (f32[8,4,16,128]{3,2,1,0:T(8,128)S(1)}, f32[8,4,16,128]{3,2,1,0:T(8,128)S(1)}, u32[]{:S(2)}, u32[]{:S(2)}) collective-permute-start(f32[8,4,16,128]{3,2,1,0:T(8,128)S(1)} %constant_dynamic-update-slice_fusion.refs_0_), channel_id=1, source_target_pairs={{0,2},{1,3},{2,0},{3,1},{4,6},{5,7},{6,4},{7,5},{8,10},{9,11},{10,... | collective-permute-start | bytes 786440 | tf_op jit(solution)/shard_map/ppermute | solution.py:396
  43.6 3.9 %collective-permute-done.7.refs_1_ = f32[8,4,16,128]{3,2,1,0:T(8,128)S(1)} collective-permute-done((f32[8,4,16,128]{3,2,1,0:T(8,128)S(1)}, f32[8,4,16,128]{3,2,1,0:T(8,128)S(1)}, u32[]{:S(2)}, u32[]{:S(2)}) %collective-permute-start.7) | collective-permute-done | bytes 262176 | tf_op jit(solution)/shard_map/ppermute | solution.py:396
  47.8 1.3 %collective-permute-done.9.refs_3_ = f32[8,4,16,128]{3,2,1,0:T(8,128)S(1)} collective-permute-done((f32[8,4,16,128]{3,2,1,0:T(8,128)S(1)}, f32[8,4,16,128]{3,2,1,0:T(8,128)S(1)}, u32[]{:S(2)}, u32[]{:S(2)}) %collective-permute-start.9) | collective-permute-done | bytes 262176 | tf_op jit(solution)/shard_map/ppermute | solution.py:396
  49.8 9.9 %cycle.1 = (f32[136,128]{1,0:T(8,128)S(1)}, f32[136,128]{1,0:T(8,128)S(1)}, f32[136,128]{1,0:T(8,128)S(1)}, f32[136,128]{1,0:T(8,128)S(1)}, f32[136,128]{1,0:T(8...) custom-call(s32[5]{0:T(128)S(1)} %stack.75.place_ref, f32[8]{0:T(128)S(1)} %copy-done.2, ...), custom_call_target="tpu_custom_call" | custom-call | tf_op jit(solution)/shard_map/cycle/pallas_call | solution.py:371
  61.2 3.0 %collective-permute-start.22 = (f32[136,128]{1,0:T(8,128)S(1)}, f32[136,128]{1,0:T(8,128)S(1)}, u32[]{:S(2)}, u32[]{:S(2)}) collective-permute-start(f32[136,128]{1,0:T(8,128)S(1)} %get-tuple-element.14), channel_id=1, source_target_pairs={{0,12},{4,16},{8,20},{12,24},{16,28},{20,0},{24,4},{28,8},{1,13},{... | collective-permute-start | bytes 208904 | tf_op jit(solution)/shard_map/ppermute | solution.py:387
  64.2 2.3 %collective-permute-start.23 = (f32[136,128]{1,0:T(8,128)S(1)}, f32[136,128]{1,0:T(8,128)S(1)}, u32[]{:S(2)}, u32[]{:S(2)}) collective-permute-start(f32[136,128]{1,0:T(8,128)S(1)} %get-tuple-element.15), channel_id=1, source_target_pairs={{0,16},{4,20},{8,24},{12,28},{16,0},{20,4},{24,8},{28,12},{1,17},{... | collective-permute-start | bytes 208904 | tf_op jit(solution)/shard_map/ppermute | solution.py:387
  66.6 1.6 %collective-permute-done.20.refs_1_ = f32[136,128]{1,0:T(8,128)S(1)} collective-permute-done((f32[136,128]{1,0:T(8,128)S(1)}, f32[136,128]{1,0:T(8,128)S(1)}, u32[]{:S(2)}, u32[]{:S(2)}) %collective-permute-start.20) | collective-permute-done | bytes 69664 | tf_op jit(solution)/shard_map/ppermute | solution.py:387
  68.9 1.5 %collective-permute-start.26 = (f32[136,128]{1,0:T(8,128)S(1)}, f32[136,128]{1,0:T(8,128)S(1)}, u32[]{:S(2)}, u32[]{:S(2)}) collective-permute-start(f32[136,128]{1,0:T(8,128)S(1)} %get-tuple-element.18), channel_id=1, source_target_pairs={{0,28},{4,0},{8,4},{12,8},{16,12},{20,16},{24,20},{28,24},{1,29},{... | collective-permute-start | bytes 208904 | tf_op jit(solution)/shard_map/ppermute | solution.py:387
  70.3 3.1 %collective-permute-done.22.refs_3_ = f32[136,128]{1,0:T(8,128)S(1)} collective-permute-done((f32[136,128]{1,0:T(8,128)S(1)}, f32[136,128]{1,0:T(8,128)S(1)}, u32[]{:S(2)}, u32[]{:S(2)}) %collective-permute-start.22) | collective-permute-done | bytes 69664 | tf_op jit(solution)/shard_map/ppermute | solution.py:387
  73.5 1.7 %collective-permute-done.24.refs_5_ = f32[136,128]{1,0:T(8,128)S(1)} collective-permute-done((f32[136,128]{1,0:T(8,128)S(1)}, f32[136,128]{1,0:T(8,128)S(1)}, u32[]{:S(2)}, u32[]{:S(2)}) %collective-permute-start.24) | collective-permute-done | bytes 69664 | tf_op jit(solution)/shard_map/ppermute | solution.py:387
  75.9 2.0 %collect.1 = (f32[8,4,16,128]{3,2,1,0:T(8,128)}, f32[8,4,16,128]{3,2,1,0:T(8,128)}, f32[8]{0:T(128)}) custom-call(s32[5]{0:T(128)} %copy-done.1, f32[136,128]{1,0:T(8,128)} %copy-done, f32[136,128]{1,0:T(8,128)} %copy-done.5, f32[136,128]{1,0:T(8,128)} %copy-done.6, f32[136,128]{1,0:T(8,128)} %copy-done.7, f32[136,128]{1,0:T(8,128)} %copy-done.8, ...), custom_call_target="tpu_custom_call" | custom-call | tf_op jit(solution)/shard_map/collect/pallas_call | solution.py:334
  (78 shorter events, 7.3 us)
Async XLA Ops:
  0.6 19.5 %collective-permute-start.14 = (f32[4,16,128]{2,1,0:T(8,128)}, f32[4,16,128]{2,1,0:T(8,128)S(1)}, u32[]{:S(2)}, u32[]{:S(2)}) collective-permute-start(f32[4,16,128]{2,1,0:T(8,128)} %param.6), channel_id=1, source_target_pairs={{0,20},{4,24},{8,28},{12,0},{16,4},{20,8},{24,12},{28,16},{1,21},{... | collective-permute-start | bytes 98312 | tf_op jit(solution)/shard_map/ppermute | solution.py:387
  5.6 13.3 %collective-permute-start.13 = (f32[4,16,128]{2,1,0:T(8,128)}, f32[4,16,128]{2,1,0:T(8,128)S(1)}, u32[]{:S(2)}, u32[]{:S(2)}) collective-permute-start(f32[4,16,128]{2,1,0:T(8,128)} %param.6), channel_id=1, source_target_pairs={{0,16},{4,20},{8,24},{12,28},{16,0},{20,4},{24,8},{28,12},{1,17},{... | collective-permute-start | bytes 98312 | tf_op jit(solution)/shard_map/ppermute | solution.py:387
  6.0 11.5 %collective-permute-start.12 = (f32[4,16,128]{2,1,0:T(8,128)}, f32[4,16,128]{2,1,0:T(8,128)S(1)}, u32[]{:S(2)}, u32[]{:S(2)}) collective-permute-start(f32[4,16,128]{2,1,0:T(8,128)} %param.6), channel_id=1, source_target_pairs={{0,12},{4,16},{8,20},{12,24},{16,28},{20,0},{24,4},{28,8},{1,13},{... | collective-permute-start | bytes 98312 | tf_op jit(solution)/shard_map/ppermute | solution.py:387
  7.6 9.8 %collective-permute-start.11 = (f32[4,16,128]{2,1,0:T(8,128)}, f32[4,16,128]{2,1,0:T(8,128)S(1)}, u32[]{:S(2)}, u32[]{:S(2)}) collective-permute-start(f32[4,16,128]{2,1,0:T(8,128)} %param.6), channel_id=1, source_target_pairs={{0,8},{4,12},{8,16},{12,20},{16,24},{20,28},{24,0},{28,4},{1,9},{5... | collective-permute-start | bytes 98312 | tf_op jit(solution)/shard_map/ppermute | solution.py:387
  10.1 6.8 %collective-permute-start.10 = (f32[4,16,128]{2,1,0:T(8,128)}, f32[4,16,128]{2,1,0:T(8,128)S(1)}, u32[]{:S(2)}, u32[]{:S(2)}) collective-permute-start(f32[4,16,128]{2,1,0:T(8,128)} %param.6), channel_id=1, source_target_pairs={{0,4},{4,8},{8,12},{12,16},{16,20},{20,24},{24,28},{28,0},{1,5},{5... | collective-permute-start | bytes 98312 | tf_op jit(solution)/shard_map/ppermute | solution.py:387
  16.9 7.9 %collective-permute-start.16 = (f32[4,16,128]{2,1,0:T(8,128)S(1)}, f32[4,16,128]{2,1,0:T(8,128)S(1)}, u32[]{:S(2)}, u32[]{:S(2)}) collective-permute-start(f32[4,16,128]{2,1,0:T(8,128)S(1)} %copy-done.12), channel_id=1, source_target_pairs={{0,28},{4,0},{8,4},{12,8},{16,12},{20,16},{24,20},{28,24},{1,29},{... | collective-permute-start | bytes 98312 | tf_op jit(solution)/shard_map/ppermute | solution.py:387
  17.4 4.6 %collective-permute-start.15 = (f32[4,16,128]{2,1,0:T(8,128)S(1)}, f32[4,16,128]{2,1,0:T(8,128)S(1)}, u32[]{:S(2)}, u32[]{:S(2)}) collective-permute-start(f32[4,16,128]{2,1,0:T(8,128)S(1)} %copy-done.12), channel_id=1, source_target_pairs={{0,24},{4,28},{8,0},{12,4},{16,8},{20,12},{24,16},{28,20},{1,25},{... | collective-permute-start | bytes 98312 | tf_op jit(solution)/shard_map/ppermute | solution.py:387
  17.5 23.7 %collective-permute-start.6 = (f32[4,16,128]{2,1,0:T(8,128)S(1)}, f32[4,16,128]{2,1,0:T(8,128)S(1)}, u32[]{:S(2)}, u32[]{:S(2)}) collective-permute-start(f32[4,16,128]{2,1,0:T(8,128)S(1)} %get-tuple-element.19), channel_id=1, source_target_pairs={{0,28},{4,0},{8,4},{12,8},{16,12},{20,16},{24,20},{28,24},{1,29},{... | collective-permute-start | bytes 98312 | tf_op jit(solution)/shard_map/ppermute | solution.py:387
  19.0 19.8 %collective-permute-start.4 = (f32[4,16,128]{2,1,0:T(8,128)S(1)}, f32[4,16,128]{2,1,0:T(8,128)S(1)}, u32[]{:S(2)}, u32[]{:S(2)}) collective-permute-start(f32[4,16,128]{2,1,0:T(8,128)S(1)} %get-tuple-element.20), channel_id=1, source_target_pairs={{0,20},{4,24},{8,28},{12,0},{16,4},{20,8},{24,12},{28,16},{1,21},{... | collective-permute-start | bytes 98312 | tf_op jit(solution)/shard_map/ppermute | solution.py:387
  20.2 18.6 %collective-permute-start.3 = (f32[4,16,128]{2,1,0:T(8,128)S(1)}, f32[4,16,128]{2,1,0:T(8,128)S(1)}, u32[]{:S(2)}, u32[]{:S(2)}) collective-permute-start(f32[4,16,128]{2,1,0:T(8,128)S(1)} %get-tuple-element.21), channel_id=1, source_target_pairs={{0,16},{4,20},{8,24},{12,28},{16,0},{20,4},{24,8},{28,12},{1,17},{... | collective-permute-start | bytes 98312 | tf_op jit(solution)/shard_map/ppermute | solution.py:387
  22.0 15.2 %collective-permute-start.2 = (f32[4,16,128]{2,1,0:T(8,128)S(1)}, f32[4,16,128]{2,1,0:T(8,128)S(1)}, u32[]{:S(2)}, u32[]{:S(2)}) collective-permute-start(f32[4,16,128]{2,1,0:T(8,128)S(1)} %get-tuple-element.22), channel_id=1, source_target_pairs={{0,12},{4,16},{8,20},{12,24},{16,28},{20,0},{24,4},{28,8},{1,13},{... | collective-permute-start | bytes 98312 | tf_op jit(solution)/shard_map/ppermute | solution.py:387
  24.9 6.6 %collective-permute-start = (f32[4,16,128]{2,1,0:T(8,128)S(1)}, f32[4,16,128]{2,1,0:T(8,128)S(1)}, u32[]{:S(2)}, u32[]{:S(2)}) collective-permute-start(f32[4,16,128]{2,1,0:T(8,128)S(1)} %get-tuple-element.24), channel_id=1, source_target_pairs={{0,4},{4,8},{8,12},{12,16},{16,20},{20,24},{24,28},{28,0},{1,5},{5... | collective-permute-start | bytes 98312 | tf_op jit(solution)/shard_map/ppermute | solution.py:387
  31.5 5.7 %collective-permute-start.1 = (f32[4,16,128]{2,1,0:T(8,128)S(1)}, f32[4,16,128]{2,1,0:T(8,128)S(1)}, u32[]{:S(2)}, u32[]{:S(2)}) collective-permute-start(f32[4,16,128]{2,1,0:T(8,128)S(1)} %get-tuple-element.23), channel_id=1, source_target_pairs={{0,8},{4,12},{8,16},{12,20},{16,24},{20,28},{24,0},{28,4},{1,9},{5... | collective-permute-start | bytes 98312 | tf_op jit(solution)/shard_map/ppermute | solution.py:387
  37.2 6.4 %collective-permute-start.17 = (f32[8,4,16,128]{3,2,1,0:T(8,128)S(1)}, f32[8,4,16,128]{3,2,1,0:T(8,128)S(1)}, u32[]{:S(2)}, u32[]{:S(2)}) collective-permute-start(f32[8,4,16,128]{3,2,1,0:T(8,128)S(1)} %constant_dynamic-update-slice_fusion.8.refs_4_), channel_id=1, source_target_pairs={{0,2},{1,3},{2,0},{3,1},{4,6},{5,7},{6,4},{7,5},{8,10},{9,11},{10,... | collective-permute-start | bytes 786440 | tf_op jit(solution)/shard_map/ppermute | solution.py:396
  41.1 6.4 %collective-permute-start.7 = (f32[8,4,16,128]{3,2,1,0:T(8,128)S(1)}, f32[8,4,16,128]{3,2,1,0:T(8,128)S(1)}, u32[]{:S(2)}, u32[]{:S(2)}) collective-permute-start(f32[8,4,16,128]{3,2,1,0:T(8,128)S(1)} %constant_dynamic-update-slice_fusion.refs_0_), channel_id=1, source_target_pairs={{0,2},{1,3},{2,0},{3,1},{4,6},{5,7},{6,4},{7,5},{8,10},{9,11},{10,... | collective-permute-start | bytes 786440 | tf_op jit(solution)/shard_map/ppermute | solution.py:396
  42.7 5.1 %collective-permute-start.18 = (f32[8,4,16,128]{3,2,1,0:T(8,128)S(1)}, f32[8,4,16,128]{3,2,1,0:T(8,128)S(1)}, u32[]{:S(2)}, u32[]{:S(2)}) collective-permute-start(f32[8,4,16,128]{3,2,1,0:T(8,128)S(1)} %constant_dynamic-update-slice_fusion.8.refs_4_), channel_id=1, source_target_pairs={{0,1},{1,0},{2,3},{3,2},{4,5},{5,4},{6,7},{7,6},{8,9},{9,8},{10,11... | collective-permute-start | bytes 786440 | tf_op jit(solution)/shard_map/ppermute | solution.py:396
  42.7 5.1 %collective-permute-start.8 = (f32[8,4,16,128]{3,2,1,0:T(8,128)S(1)}, f32[8,4,16,128]{3,2,1,0:T(8,128)S(1)}, u32[]{:S(2)}, u32[]{:S(2)}) collective-permute-start(f32[8,4,16,128]{3,2,1,0:T(8,128)S(1)} %constant_dynamic-update-slice_fusion.refs_0_), channel_id=1, source_target_pairs={{0,1},{1,0},{2,3},{3,2},{4,5},{5,4},{6,7},{7,6},{8,9},{9,8},{10,11... | collective-permute-start | bytes 786440 | tf_op jit(solution)/shard_map/ppermute | solution.py:396
  60.4 7.8 %collective-permute-start.20 = (f32[136,128]{1,0:T(8,128)S(1)}, f32[136,128]{1,0:T(8,128)S(1)}, u32[]{:S(2)}, u32[]{:S(2)}) collective-permute-start(f32[136,128]{1,0:T(8,128)S(1)} %get-tuple-element.12), channel_id=1, source_target_pairs={{0,4},{4,8},{8,12},{12,16},{16,20},{20,24},{24,28},{28,0},{1,5},{5... | collective-permute-start | bytes 208904 | tf_op jit(solution)/shard_map/ppermute | solution.py:387
  60.4 8.5 %collective-permute-start.21 = (f32[136,128]{1,0:T(8,128)S(1)}, f32[136,128]{1,0:T(8,128)S(1)}, u32[]{:S(2)}, u32[]{:S(2)}) collective-permute-start(f32[136,128]{1,0:T(8,128)S(1)} %get-tuple-element.13), channel_id=1, source_target_pairs={{0,8},{4,12},{8,16},{12,20},{16,24},{20,28},{24,0},{28,4},{1,9},{5... | collective-permute-start | bytes 208904 | tf_op jit(solution)/shard_map/ppermute | solution.py:387
  61.2 12.2 %collective-permute-start.22 = (f32[136,128]{1,0:T(8,128)S(1)}, f32[136,128]{1,0:T(8,128)S(1)}, u32[]{:S(2)}, u32[]{:S(2)}) collective-permute-start(f32[136,128]{1,0:T(8,128)S(1)} %get-tuple-element.14), channel_id=1, source_target_pairs={{0,12},{4,16},{8,20},{12,24},{16,28},{20,0},{24,4},{28,8},{1,13},{... | collective-permute-start | bytes 208904 | tf_op jit(solution)/shard_map/ppermute | solution.py:387
  64.2 9.3 %collective-permute-start.23 = (f32[136,128]{1,0:T(8,128)S(1)}, f32[136,128]{1,0:T(8,128)S(1)}, u32[]{:S(2)}, u32[]{:S(2)}) collective-permute-start(f32[136,128]{1,0:T(8,128)S(1)} %get-tuple-element.15), channel_id=1, source_target_pairs={{0,16},{4,20},{8,24},{12,28},{16,0},{20,4},{24,8},{28,12},{1,17},{... | collective-permute-start | bytes 208904 | tf_op jit(solution)/shard_map/ppermute | solution.py:387
  66.5 8.7 %collective-permute-start.24 = (f32[136,128]{1,0:T(8,128)S(1)}, f32[136,128]{1,0:T(8,128)S(1)}, u32[]{:S(2)}, u32[]{:S(2)}) collective-permute-start(f32[136,128]{1,0:T(8,128)S(1)} %get-tuple-element.16), channel_id=1, source_target_pairs={{0,20},{4,24},{8,28},{12,0},{16,4},{20,8},{24,12},{28,16},{1,21},{... | collective-permute-start | bytes 208904 | tf_op jit(solution)/shard_map/ppermute | solution.py:387
  68.2 7.0 %collective-permute-start.25 = (f32[136,128]{1,0:T(8,128)S(1)}, f32[136,128]{1,0:T(8,128)S(1)}, u32[]{:S(2)}, u32[]{:S(2)}) collective-permute-start(f32[136,128]{1,0:T(8,128)S(1)} %get-tuple-element.17), channel_id=1, source_target_pairs={{0,24},{4,28},{8,0},{12,4},{16,8},{20,12},{24,16},{28,20},{1,25},{... | collective-permute-start | bytes 208904 | tf_op jit(solution)/shard_map/ppermute | solution.py:387
  68.9 6.3 %collective-permute-start.26 = (f32[136,128]{1,0:T(8,128)S(1)}, f32[136,128]{1,0:T(8,128)S(1)}, u32[]{:S(2)}, u32[]{:S(2)}) collective-permute-start(f32[136,128]{1,0:T(8,128)S(1)} %get-tuple-element.18), channel_id=1, source_target_pairs={{0,28},{4,0},{8,4},{12,8},{16,12},{20,16},{24,20},{28,24},{1,29},{... | collective-permute-start | bytes 208904 | tf_op jit(solution)/shard_map/ppermute | solution.py:387
  (16 other events, 33.4 us)

commit v4 on v0

--- a/solution.py
+++ b/solution.py
@@ -1,14 +1,22 @@
+import functools
+
 import jax
 import jax.numpy as jnp
 from jax import lax
+from jax.experimental import pallas as pl
+from jax.experimental.pallas import tpu as pltpu
 from jax.sharding import PartitionSpec as P
 
 LEVELS = 3
 COARSE_SWEEPS = 6
 
-
 DAMPING = 0.8
 EPSILON = 1e-06
+VMEM_LIMIT = 32 * 1024 * 1024
+LANES = 128
+GROUP = 4
+SLAB = 8
+HALO = 4
 
 
 def with_halo(x, sides, width):
@@ -93,27 +101,15 @@
     return iterate
 
 
-def body(source, reaction, shifts, shift_index, velocity):
+def halo_body(source, reaction, shifts, shift_index, velocity):
     columns, cells_x, cells_y, cells_z = source.shape
     shift_value = select_shifts(shifts, shift_index)
     reaction_top = reaction[None]
     backward, forward, centre = coefficients(velocity, 1.0)
     diagonal = centre + reaction_top + shift_value[:, None, None, None]
 
-    def operate(iterate):
-        return apply_stencil(face_halo(iterate), backward, forward, diagonal)
-
-    def smooth_step(iterate):
-        return iterate + DAMPING * (source - operate(iterate)) / diagonal
-
-    iterate = DAMPING * source / diagonal
-    iterate = smooth_step(iterate)
-    defect = source - operate(iterate)
-    correction = multigrid_cycle(1, coarsen(defect), coarsen(reaction_top), shift_value, velocity)
-    iterate = iterate + refine(correction)
-    iterate = smooth_step(iterate)
-    iterate = smooth_step(iterate)
-    residual = source - operate(iterate)
+    iterate = multigrid_cycle(0, source, reaction_top, shift_value, velocity)
+    residual = source - apply_stencil(face_halo(iterate), backward, forward, diagonal)
     local_squares = jnp.sum(residual * residual, axis=(1, 2, 3))
     squares = lax.psum(local_squares, ("gx", "gy"))
     total_cells = cells_x * cells_y * cells_z * lax.axis_size("gx") * lax.axis_size("gy")
@@ -121,7 +117,409 @@
     return (iterate, residual, residual_rms)
 
 
+def split_dot(values, matrix):
+    high = values.astype(jnp.bfloat16)
+    low = (values - high.astype(jnp.float32)).astype(jnp.bfloat16)
+    return jnp.dot(high, matrix, preferred_element_type=jnp.float32) + jnp.dot(
+        low, matrix, preferred_element_type=jnp.float32
+    )
+
+
+def sweep(planes, get, put):
+    planes = list(planes)
+    for first in range(0, len(planes), GROUP):
+        group = planes[first : first + GROUP]
+        values = [get(x) for x in group]
+        for x, value in zip(group, values):
+            put(x, value)
+
+
+class Level:
+    def __init__(self, index, ny, nz, rim, velocity_ref, shift, f, r, w):
+        self.ny, self.nz, self.rim = ny, nz, rim
+        self.f, self.r, self.w = f, r, w
+        spacing = 2.0**index
+        scale_a = 1.0 / (spacing * spacing)
+        inverse = 1.0 / spacing
+        speed = [velocity_ref[d] for d in range(3)]
+        self.backward = [scale_a + jnp.maximum(v, 0.0) * inverse for v in speed]
+        self.forward = [scale_a - jnp.minimum(v, 0.0) * inverse for v in speed]
+        total = jnp.abs(speed[0]) + jnp.abs(speed[1]) + jnp.abs(speed[2])
+        self.centre = 6.0 * scale_a + total * inverse + shift
+        lane = lax.broadcasted_iota(jnp.int32, (1, LANES), 1)
+        inside = lane < nz
+        self.low_z = jnp.where((lane > 0) & inside, self.backward[2], 0.0)
+        self.high_z = jnp.where(lane < nz - 1, self.forward[2], 0.0)
+
+    def plane(self, v, x):
+        return v[x + self.rim, pl.ds(8, self.ny), :]
+
+    def put(self, v):
+        def write(x, value):
+            v[x + self.rim, pl.ds(8, self.ny), :] = value
+
+        return write
+
+    def along_z(self, middle):
+        return self.low_z * pltpu.roll(middle, 1, 1) + self.high_z * pltpu.roll(middle, LANES - 1, 1)
+
+    def neighbours(self, v, x, middle):
+        at, ny = x + self.rim, self.ny
+        along_x = self.backward[0] * v[at - 1, pl.ds(8, ny), :] + self.forward[0] * v[at + 1, pl.ds(8, ny), :]
+        along_y = self.backward[1] * v[at, pl.ds(7, ny), :] + self.forward[1] * v[at, pl.ds(9, ny), :]
+        return along_x + along_y + self.along_z(middle)
+
+    def smoothed(self, v, x):
+        middle = self.plane(v, x)
+        pulled = self.f[x] + self.neighbours(v, x, middle)
+        return (1.0 - DAMPING) * middle + self.w[x] * pulled
+
+    def smooth(self, src, dst, planes):
+        sweep(planes, lambda x: self.smoothed(src, x), self.put(dst))
+
+    def defect(self, v, x):
+        middle = self.plane(v, x)
+        pulled = self.f[x] + self.neighbours(v, x, middle)
+        return pulled - (self.r[x] + self.centre) * middle
+
+    def pool_rows(self, value, rows):
+        half, ny = self.ny // 2, self.ny
+        rows[pl.ds(0, ny), :] = value
+        return rows[pl.ds(0, half, stride=2), :] + rows[pl.ds(1, half, stride=2), :]
+
+    def spread_rows(self, part, rows):
+        half, ny = self.ny // 2, self.ny
+        rows[pl.ds(0, half, stride=2), :] = part
+        rows[pl.ds(1, half, stride=2), :] = part
+        return rows[pl.ds(0, ny), :]
+
+    def solve_in_registers(self, rhs, reaction):
+        row = lax.broadcasted_iota(jnp.int32, (self.ny, 1), 0)
+        low_y = jnp.where(row > 0, self.backward[1], 0.0)
+        high_y = jnp.where(row < self.ny - 1, self.forward[1], 0.0)
+        weight = [DAMPING / (r + self.centre) for r in reaction]
+        v = [w * f for w, f in zip(weight, rhs)]
+        for _ in range(COARSE_SWEEPS - 1):
+            new = []
+            for x, here in enumerate(v):
+                along_y = low_y * pltpu.roll(here, 1, 0) + high_y * pltpu.roll(here, self.ny - 1, 0)
+                pulled = rhs[x] + self.along_z(here) + along_y
+                if x > 0:
+                    pulled += self.backward[0] * v[x - 1]
+                if x < len(v) - 1:
+                    pulled += self.forward[0] * v[x + 1]
+                new.append((1.0 - DAMPING) * here + weight[x] * pulled)
+            v = new
+        return jnp.concatenate(v, axis=0)
+
+
+def zero_rows(v, ny):
+    edge = jnp.zeros((v.shape[0], 8, LANES), jnp.float32)
+    v[:, pl.ds(0, 8), :] = edge
+    v[:, pl.ds(8 + ny, 8), :] = edge
+
+
+def pool_matrix(offset):
+    row = lax.broadcasted_iota(jnp.int32, (LANES, LANES), 0)
+    col = lax.broadcasted_iota(jnp.int32, (LANES, LANES), 1)
+    return jnp.where(row // 2 + offset == col, 0.125, 0.0).astype(jnp.bfloat16)
+
+
+def spread_matrix():
+    row = lax.broadcasted_iota(jnp.int32, (LANES, LANES), 0)
+    col = lax.broadcasted_iota(jnp.int32, (LANES, LANES), 1)
+    return jnp.where(col // 2 == row, 1.0, 0.0).astype(jnp.bfloat16)
+
+
+def pack_kernel(place_ref, source_ref, reaction_ref, *out_refs):
+    for k, out_ref in enumerate(out_refs):
+        out_ref[0] = source_ref[jnp.bitwise_xor(place_ref[0], k)]
+        out_ref[1] = reaction_ref[...]
+
+
+def arrange_kernel(gy_size, place_ref, *refs):
+    pieces, (low_ref, high_ref, both) = refs[:-3], refs[-3:]
+    _, bx, by, _ = pieces[0].shape
+    for k, piece in enumerate(pieces):
+        owner = jnp.bitwise_xor(place_ref[0], k)
+        planes = pl.ds((owner // gy_size) * bx, bx)
+        rows = pl.ds(pl.multiple_of(lax.rem(owner, gy_size) * by, 8), by)
+        both[:, planes, rows, :] = piece[...]
+    low_ref[...] = both[:, pl.ds(0, HALO)]
+    high_ref[...] = both[:, pl.ds(HALO, HALO)]
+
+
+def pre_kernel(slabs, place_ref, shifts_ref, index_ref, velocity_ref, *refs):
+    pool_ref, pool_up_ref = refs[:2]
+    parts = refs[2:6]
+    f, r, w, v1, coarse_ref, v0, tmp, pooled = refs[6:]
+    ny = f.shape[1]
+    slab = place_ref[1]
+    shift = shifts_ref[index_ref[place_ref[0]]]
+    fine = Level(0, ny, LANES, 0, velocity_ref, shift, f, r, w)
+    zero_rows(v0, ny)
+    zero_rows(v1, ny)
+    count = SLAB + 2 * HALO
+    inside = [jnp.where(slab > 0, DAMPING, 0.0)] * HALO
+    inside += [DAMPING] * SLAB
+    inside += [jnp.where(slab < slabs - 1, DAMPING, 0.0)] * HALO
+
+    def begin(x):
+        part, at = parts[x // HALO], x % HALO
+        return part[0, at], part[1, at]
+
+    def put(x, pair):
+        f[x], r[x] = pair
+        weight = inside[x] / (pair[1] + fine.centre)
+        w[x] = weight
+        v0[x, pl.ds(8, ny), :] = weight * pair[0]
+
+    sweep(range(count), begin, put)
+    fine.smooth(v0, v1, range(1, count - 1))
+    half = ny // 2
+
+    def coarsened(x):
+        at = HALO + 2 * x
+        return fine.defect(v1, at) + fine.defect(v1, at + 1), r[at] + r[at + 1]
+
+    def put_pooled(x, pair):
+        for n in range(2):
+            pooled[n, pl.ds(x * half, half), :] = fine.pool_rows(pair[n], tmp.at[2 * x + n])
+
+    sweep(range(SLAB // 2), coarsened, put_pooled)
+    packed = split_dot(pooled[0], pool_ref[...]) + split_dot(pooled[1], pool_up_ref[...])
+    coarse_ref[...] = packed.reshape(coarse_ref.shape)
+
+
+def post_kernel(grid, gy_size, bx, by, place_ref, shifts_ref, index_ref, velocity_ref, *refs):
+    slabs, nx, ny, nz = grid
+    pool_ref, spread_ref, f, r, w, v1 = refs[:6]
+    coarse = refs[6 : 6 + slabs]
+    columns = SLAB // bx * gy_size
+    out_refs = refs[6 + slabs : 6 + slabs + columns]
+    va, vb, f1, r1, w1, v1a, v1b, pooled, tmp = refs[6 + slabs + columns :]
+    pool, spread = pool_ref[...], spread_ref[...]
+    slab = place_ref[1]
+    shift = shifts_ref[index_ref[place_ref[0]]]
+    rim = HALO // 2
+    nx1, ny1, nx2, ny2 = nx // 2, ny // 2, nx // 4, ny // 4
+    fine = Level(0, ny, nz, 0, velocity_ref, shift, f, r, w)
+    mid = Level(1, ny1, nz // 2, rim, velocity_ref, shift, f1, r1, w1)
+    deep = Level(2, ny2, nz // 4, 0, velocity_ref, shift, None, None, None)
+    for v in (va, vb):
+        zero_rows(v, ny)
+    for v in (v1a, v1b):
+        zero_rows(v, ny1)
+        blank = jnp.zeros((rim,) + v.shape[1:], jnp.float32)
+        v[pl.ds(0, rim)] = blank
+        v[pl.ds(rim + nx1, rim)] = blank
+
+    lower = lax.broadcasted_iota(jnp.int32, (1, LANES), 1) < LANES // 2
+    own = SLAB // 2
+    for k in range(slabs):
+        first = jnp.bitwise_xor(slab, k) * own
+        both = coarse[k][...]
+        f1[pl.ds(first, own)] = jnp.where(lower, both, 0.0)
+        r1[pl.ds(first, own)] = jnp.where(lower, pltpu.roll(both, LANES // 2, 2), 0.0)
+
+    def put_start(x, weight):
+        w1[x] = weight
+        v1a[x + rim, pl.ds(8, ny1), :] = weight * f1[x]
+
+    sweep(range(nx1), lambda x: DAMPING / (r1[x] + mid.centre), put_start)
+    mid.smooth(v1a, v1b, range(nx1))
+
+    def coarsened(x):
+        return mid.defect(v1b, 2 * x) + mid.defect(v1b, 2 * x + 1), r1[2 * x] + r1[2 * x + 1]
+
+    rows2 = nx2 * ny2
+
+    def put_pooled(x, pair):
+        for n in range(2):
+            value = mid.pool_rows(pair[n], tmp.at[2 * x + n])
+            pooled[pl.ds(n * rows2 + x * ny2, ny2), :] = value
+
+    sweep(range(nx2), coarsened, put_pooled)
+    deeper = split_dot(pooled[pl.ds(0, 2 * rows2), :], pool)
+    planes = [deeper[n * ny2 : (n + 1) * ny2] for n in range(2 * nx2)]
+    values = deep.solve_in_registers(planes[:nx2], planes[nx2:])
+
+    pooled[pl.ds(0, rows2), :] = split_dot(values, spread)
+
+    def refined1(x):
+        return mid.spread_rows(pooled[pl.ds(x * ny2, ny2), :], tmp.at[x])
+
+    def put_refined1(x, value):
+        for n in range(2):
+            v1b[2 * x + n + rim, pl.ds(8, ny1), :] += value
+
+    sweep(range(nx2), refined1, put_refined1)
+    mid.smooth(v1b, v1a, range(nx1))
+    mid.smooth(v1a, v1b, range(nx1))
+
+    window = own + 2 * rim
+    values = v1b[pl.ds(slab * own, window), pl.ds(8, ny1), :].reshape(window * ny1, LANES)
+    pooled[pl.ds(0, window * ny1), :] = split_dot(values, spread)
+    count = SLAB + 2 * HALO
+
+    def refined(x):
+        return fine.spread_rows(pooled[pl.ds(x * ny1, ny1), :], tmp.at[x])
+
+    def put_refined(x, value):
+        for at in (2 * x, 2 * x + 1):
+            if 0 < at < count - 1:
+                va[at, pl.ds(8, ny), :] = v1[at, pl.ds(8, ny), :] + value
+
+    sweep(range(window), refined, put_refined)
+    fine.smooth(va, vb, range(2, count - 2))
+    fine.smooth(vb, va, range(3, count - 3))
+
+    total = jnp.zeros((8, LANES), jnp.float32)
+    for x in range(SLAB):
+        rest = fine.defect(va, HALO + x)
+        total = total + jnp.sum((rest * rest).reshape(ny // 8, 8, LANES), axis=0)
+        tmp[x] = rest
+    squares = jnp.full((8, LANES), jnp.sum(total), jnp.float32)
+    area = bx * by
+    for k, out_ref in enumerate(out_refs):
+        owner = jnp.bitwise_xor(place_ref[0], k)
+        first = (owner // gy_size) * bx
+        row = pl.multiple_of(lax.rem(owner, gy_size) * by, 8)
+        for p in range(bx):
+            out_ref[pl.ds(p * by, by), :] = va[HALO + first + p, pl.ds(8 + row, by), :]
+            out_ref[pl.ds(area + p * by, by), :] = tmp[first + p, pl.ds(row, by), :]
+        out_ref[pl.ds(2 * area, 8), :] = squares
+
+
+def collect_kernel(bx, by, place_ref, *refs):
+    parts, (iterate_ref, residual_ref) = refs[:-2], refs[-2:]
+    area = bx * by
+    for k, part in enumerate(parts):
+        column = jnp.bitwise_xor(place_ref[0], k)
+        iterate_ref[column] = part[pl.ds(0, area), :].reshape(bx, by, LANES)
+        residual_ref[column] = part[pl.ds(area, area), :].reshape(bx, by, LANES)
+
+
+SMEM = pl.BlockSpec(memory_space=pltpu.SMEM)
+VMEM = pl.BlockSpec(memory_space=pltpu.VMEM)
+
+
+def local_kernel(kernel, name, scalars, arrays, outs, scratch=()):
+    return pl.pallas_call(
+        kernel,
+        out_shape=[jax.ShapeDtypeStruct(shape, jnp.float32) for shape in outs],
+        in_specs=[SMEM] * len(scalars) + [VMEM] * len(arrays),
+        out_specs=[VMEM] * len(outs),
+        scratch_shapes=[pltpu.VMEM(shape, jnp.float32) for shape in scratch],
+        compiler_params=pltpu.CompilerParams(vmem_limit_bytes=VMEM_LIMIT),
+        name=name,
+    )(*scalars, *arrays)
+
+
+def swap_in_plane(pieces, columns):
+    devices = lax.axis_size("gx") * lax.axis_size("gy")
+    moved = [pieces[0]]
+    for k in range(1, columns):
+        pairs = [(i, i ^ k) for i in range(devices)]
+        moved.append(lax.ppermute(pieces[k], ("gx", "gy"), pairs))
+    return moved
+
+
+def swap_slabs(piece, step, slabs):
+    size = lax.axis_size("gx")
+    moved = [piece]
+    for k in range(1, slabs):
+        pairs = [(i, i ^ (k * step)) for i in range(size)]
+        moved.append(lax.ppermute(piece, "gx", pairs))
+    return moved
+
+
+def column_body(source, reaction, shifts, shift_index, velocity):
+    columns, bx, by, nz = source.shape
+    gx_size, gy_size = lax.axis_size("gx"), lax.axis_size("gy")
+    nx, ny = bx * gx_size, by * gy_size
+    step = columns // gy_size
+    slabs = gx_size // step
+    along, across = lax.axis_index("gx"), lax.axis_index("gy")
+    column = lax.rem(along, step) * gy_size + across
+    place = jnp.stack([column, along // step]).astype(jnp.int32)
+    scalars = (place, shifts, shift_index, velocity)
+    count = SLAB + 2 * HALO
+    area = bx * by
+
+    pieces = local_kernel(
+        pack_kernel, "pack", (place,), (source, reaction), [(2, bx, by, nz)] * columns
+    )
+    pieces = swap_in_plane(pieces, columns)
+    low, high = local_kernel(
+        functools.partial(arrange_kernel, gy_size),
+        "arrange",
+        (place,),
+        pieces,
+        [(2, HALO, ny, nz)] * 2,
+        [(2, SLAB, ny, nz)],
+    )
+    before = lax.ppermute(high, "gx", [(i, i + step) for i in range(gx_size - step)])
+    after = lax.ppermute(low, "gx", [(i + step, i) for i in range(gx_size - step)])
+
+    grid, rimmed = (count, ny, nz), (count, ny + 16, nz)
+    f, r, w, v1, coarse = local_kernel(
+        functools.partial(pre_kernel, slabs),
+        "pre",
+        scalars,
+        (pool_matrix(0), pool_matrix(LANES // 2), before, low, high, after),
+        [grid, grid, grid, rimmed, (SLAB // 2, ny // 2, nz)],
+        [rimmed, (SLAB, ny, nz), (2, SLAB // 2 * ny // 2, nz)],
+    )
+    gathered = swap_slabs(coarse, step, slabs)
+
+    coarse_grid = (nx // 2, ny // 2, nz)
+    coarse_rimmed = (nx // 2 + HALO, ny // 2 + 16, nz)
+    rows = max((SLAB // 2 + HALO) * ny // 2, nx // 4 * ny // 2)
+    results = local_kernel(
+        functools.partial(post_kernel, (slabs, nx, ny, nz), gy_size, bx, by),
+        "post",
+        scalars,
+        (pool_matrix(0), spread_matrix(), f, r, w, v1, *gathered),
+        [(2 * area + 8, nz)] * columns,
+        [rimmed] * 2 + [coarse_grid] * 3 + [coarse_rimmed] * 2 + [(rows, nz), (nx // 2, ny, nz)],
+    )
+    parts = swap_in_plane(results, columns)
+
+    squares = jnp.stack([part[2 * area, 0] for part in parts])
+    total = sum(swap_slabs(squares, step, slabs))
+    rms = jnp.sqrt(total / (nx * ny * nz) + EPSILON)
+    slots = jnp.arange(columns, dtype=jnp.int32)
+    mine = jnp.bitwise_xor(slots, column)[None, :] == slots[:, None]
+    residual_rms = jnp.sum(jnp.where(mine, rms[None, :], 0.0), axis=1)
+    iterate, residual = local_kernel(
+        functools.partial(collect_kernel, bx, by), "collect", (place,), parts, [source.shape] * 2
+    )
+    return iterate, residual, residual_rms
+
+
+def power_of_two(n):
+    return n > 0 and n & (n - 1) == 0
+
+
+def column_plan_fits(columns, bx, by, nz, gx_size, gy_size):
+    if columns % gy_size or gx_size % (columns // gy_size):
+        return False
+    step = columns // gy_size
+    slabs, ny = gx_size // step, by * gy_size
+    whole = power_of_two(columns) and power_of_two(step) and power_of_two(slabs)
+    small = slabs * ny * nz <= 2**15
+    return whole and small and bx * step == SLAB and nz == LANES and by % 16 == 0
+
+
 def solution(mesh):
+    gx_size, gy_size = mesh.shape["gx"], mesh.shape["gy"]
+
+    def body(source, reaction, shifts, shift_index, velocity):
+        fits = column_plan_fits(*source.shape, gx_size, gy_size)
+        plan = column_body if fits else halo_body
+        return plan(source, reaction, shifts, shift_index, velocity)
+
     return jax.shard_map(
         body,
         mesh=mesh,

time: 345 us -> 67.3 us (0.20)
  starting transfers between devices: 125 us -> 27.5 us
  waiting for transfers between devices: 96.8 us -> 19.4 us
  other arithmetic: 67 us -> 0.85 us
  blocking collectives: 38.6 us -> 0 us
  Pallas kernels: 0 us -> 6.83 us
    ppermute x56 -> x22, starting transfers between devices: 125 us -> 27.5 us  [the longest x14 13.9 us: swap_in_plane(): moved.append(lax.ppermute(pieces[k], ('gx', 'gy'), pairs))]
    ppermute x56 -> x22, waiting for transfers between devices: 96.8 us -> 19.4 us  [the longest x14 5.71 us: swap_in_plane(): moved.append(lax.ppermute(pieces[k], ('gx', 'gy'), pairs))]
    add x16 -> x0, other arithmetic: 46.2 us -> none  [the longest x5 19.7 us: coarsest_solve(): iterate = iterate + DAMPING * (rhs_field - applied) / diagonal]
    psum x1 -> x0, blocking collectives: 38.6 us -> none  [body(): squares = lax.psum(local_squares, ('gx', 'gy'))]
    reduce_sum x8 -> x1, other arithmetic: 14.8 us -> 0.63 us  [column_body(): residual_rms = jnp.sum(jnp.where(mine, rms[None, :], 0.0), axis=1)]
    pallas_call x0 -> x5, Pallas kernels: none -> 6.83 us  [local_kernel(): pl.pallas_call(kernel, out_shape=[jax.ShapeDtypeStruct(shape, jnp.float32...]
    sub x1 -> x0, other arithmetic: 3.99 us -> none  [body(): defect = source - operate(iterate)]
  transfers between devices with their start and end apart: 56 -> 22, of which waited for: 40 -> 10; matrix products, arithmetic and copies ran while one was open for 1% -> 6% of each run, Pallas kernels for 0% -> 2%
where the time goes in v4:
time: 67.3 us; the launch traced here: 66.9 us
  starting transfers between devices  27.5 us (41%)
  waiting for transfers between devices  19.4 us (29%)
  local copies, waits for them, and re-layouts  11.6 us (17%)
  Pallas kernels  6.83 us (10%)
  other arithmetic  0.85 us (1%)
  between operations  0.76 us (1%)
    ppermute x14, starting transfers between devices, swap_in_plane(): moved.append(lax.ppermute(pieces[k], ('gx', 'gy'), pairs))  13.9 us
    ppermute x6, starting transfers between devices, swap_slabs(): moved.append(lax.ppermute(piece, 'gx', pairs))  8.84 us
    pallas_call x5, Pallas kernels, local_kernel(): pl.pallas_call(kernel, out_shape=[jax.ShapeDtypeStruct(shape, jnp.float32...  6.83 us
    ppermute x14, waiting for transfers between devices, swap_in_plane(): moved.append(lax.ppermute(pieces[k], ('gx', 'gy'), pairs))  5.71 us
    ppermute x6, waiting for transfers between devices, swap_slabs(): moved.append(lax.ppermute(piece, 'gx', pairs))  5.15 us
    another operation x1, local copies, waits for them, and re-layouts, column_body(): squares = jnp.stack([part[2 * area, 0] for part in parts])  5.07 us
    ppermute x1, waiting for transfers between devices, column_body(): lax.ppermute(high, 'gx', [(i, i + step) for i in range(gx_size - step)])  4.37 us
    slice x8, local copies, waits for them, and re-layouts, column_body(): squares = jnp.stack([part[2 * area, 0] for part in parts])  4.26 us
  transfers between devices with their start and end apart: 22, of which 10 were waited for; matrix products, arithmetic and copies ran while one was open for 6% of the time, Pallas kernels for 2%

profile of v4, /device:TPU:0, one launch (start us, length us, event | category | flops | bytes accessed | tf_op | source)
XLA Modules:
  0.0 66.9 jit_solution(7006162135919306940)
XLA Ops:
  3.4 2.6 %collective-permute-start.1 = (f32[2,4,16,128]{3,2,1,0:T(8,128)S(1)}, f32[2,4,16,128]{3,2,1,0:T(8,128)S(1)}, u32[]{:S(2)}, u32[]{:S(2)}) collective-permute-start(f32[2,4,16,128]{3,2,1,0:T(8,128)S(1)} %get-tuple-element.30), channel_id=1, source_target_pairs={{0,2},{1,3},{2,0},{3,1},{4,6},{5,7},{6,4},{7,5},{8,10},{9,11},{10,... | collective-permute-start | bytes 196616 | tf_op jit(solution)/shard_map/ppermute | solution.py:424
  6.1 1.7 %collective-permute-start.3 = (f32[2,4,16,128]{3,2,1,0:T(8,128)S(1)}, f32[2,4,16,128]{3,2,1,0:T(8,128)S(1)}, u32[]{:S(2)}, u32[]{:S(2)}) collective-permute-start(f32[2,4,16,128]{3,2,1,0:T(8,128)S(1)} %get-tuple-element.32), channel_id=1, source_target_pairs={{0,4},{1,5},{2,6},{3,7},{4,0},{5,1},{6,2},{7,3},{8,12},{9,13},{10,... | collective-permute-start | bytes 196616 | tf_op jit(solution)/shard_map/ppermute | solution.py:424
  7.8 2.6 %collective-permute-start.5 = (f32[2,4,16,128]{3,2,1,0:T(8,128)S(1)}, f32[2,4,16,128]{3,2,1,0:T(8,128)S(1)}, u32[]{:S(2)}, u32[]{:S(2)}) collective-permute-start(f32[2,4,16,128]{3,2,1,0:T(8,128)S(1)} %get-tuple-element.34), channel_id=1, source_target_pairs={{0,6},{1,7},{2,4},{3,5},{4,2},{5,3},{6,0},{7,1},{8,14},{9,15},{10,... | collective-permute-start | bytes 196616 | tf_op jit(solution)/shard_map/ppermute | solution.py:424
  10.7 1.3 %collective-permute-done.4.refs_5_ = f32[2,4,16,128]{3,2,1,0:T(8,128)S(1)} collective-permute-done((f32[2,4,16,128]{3,2,1,0:T(8,128)S(1)}, f32[2,4,16,128]{3,2,1,0:T(8,128)S(1)}, u32[]{:S(2)}, u32[]{:S(2)}) %collective-permute-start.4) | collective-permute-done | bytes 65568 | tf_op jit(solution)/shard_map/ppermute | solution.py:424
  12.0 2.7 %collective-permute-done.5.refs_6_ = f32[2,4,16,128]{3,2,1,0:T(8,128)S(1)} collective-permute-done((f32[2,4,16,128]{3,2,1,0:T(8,128)S(1)}, f32[2,4,16,128]{3,2,1,0:T(8,128)S(1)}, u32[]{:S(2)}, u32[]{:S(2)}) %collective-permute-start.5) | collective-permute-done | bytes 65568 | tf_op jit(solution)/shard_map/ppermute | solution.py:424
  16.5 3.5 %collective-permute-start.7 = (f32[2,4,64,128]{3,2,1,0:T(8,128)S(1)}, f32[2,4,64,128]{3,2,1,0:T(8,128)S(1)}, u32[]{:S(2)}, u32[]{:S(2)}) collective-permute-start(f32[2,4,64,128]{3,2,1,0:T(8,128)S(1)} %get-tuple-element.36.refs_4_), channel_id=1, source_target_pairs={{0,8},{4,12},{8,16},{12,20},{16,24},{20,28},{1,9},{5,13},{9,17},{1... | collective-permute-start | bytes 786440 | tf_op jit(solution)/shard_map/ppermute | solution.py:462
  20.0 1.3 %collective-permute-start.8 = (f32[2,4,64,128]{3,2,1,0:T(8,128)S(1)}, f32[2,4,64,128]{3,2,1,0:T(8,128)S(1)}, u32[]{:S(2)}, u32[]{:S(2)}) collective-permute-start(f32[2,4,64,128]{3,2,1,0:T(8,128)S(1)} %get-tuple-element.37.refs_3_), channel_id=1, source_target_pairs={{8,0},{12,4},{16,8},{20,12},{24,16},{28,20},{9,1},{13,5},{17,9},{2... | collective-permute-start | bytes 786440 | tf_op jit(solution)/shard_map/ppermute | solution.py:463
  21.4 4.4 %collective-permute-done.7.refs_2_ = f32[2,4,64,128]{3,2,1,0:T(8,128)S(1)} collective-permute-done((f32[2,4,64,128]{3,2,1,0:T(8,128)S(1)}, f32[2,4,64,128]{3,2,1,0:T(8,128)S(1)}, u32[]{:S(2)}, u32[]{:S(2)}) %collective-permute-start.7) | collective-permute-done | bytes 262176 | tf_op jit(solution)/shard_map/ppermute | solution.py:462
  25.8 4.1 %collective-permute-done.8.refs_5_ = f32[2,4,64,128]{3,2,1,0:T(8,128)S(1)} collective-permute-done((f32[2,4,64,128]{3,2,1,0:T(8,128)S(1)}, f32[2,4,64,128]{3,2,1,0:T(8,128)S(1)}, u32[]{:S(2)}, u32[]{:S(2)}) %collective-permute-start.8) | collective-permute-done | bytes 262176 | tf_op jit(solution)/shard_map/ppermute | solution.py:463
  30.6 1.2 %pre.1 = (f32[16,64,128]{2,1,0:T(8,128)S(1)}, f32[16,64,128]{2,1,0:T(8,128)S(1)}, f32[16,64,128]{2,1,0:T(8,128)S(1)}, f32[16,80,128]{2,1,0:T(8,128)S(1)}, f32[4,32,128]{2,1,0:T(8,128)S(1)}) custom-call(s32[2]{0:T(128)S(1)} %pad_add_fusion.place_ref, f32[8]{0:T(128)S(1)} %copy-done.2, s32[8]{0:T(128)S(1)} %copy-done.3, f32[3]{0:T(128)S(1)} %copy-done.4, ...), custom_call_target="tpu_custom_call" | custom-call | tf_op jit(solution)/shard_map/pre/pallas_call | solution.py:408
  31.8 1.6 %collective-permute-start.11 = (f32[4,32,128]{2,1,0:T(8,128)S(1)}, f32[4,32,128]{2,1,0:T(8,128)S(1)}, u32[]{:S(2)}, u32[]{:S(2)}) collective-permute-start(f32[4,32,128]{2,1,0:T(8,128)S(1)} %get-tuple-element.42.refs_6_), channel_id=1, source_target_pairs={{0,24},{4,28},{8,16},{12,20},{16,8},{20,12},{24,0},{28,4},{1,25},{... | collective-permute-start | bytes 196616 | tf_op jit(solution)/shard_map/ppermute | solution.py:433
  33.5 1.5 %collective-permute-start.10 = (f32[4,32,128]{2,1,0:T(8,128)S(1)}, f32[4,32,128]{2,1,0:T(8,128)S(1)}, u32[]{:S(2)}, u32[]{:S(2)}) collective-permute-start(f32[4,32,128]{2,1,0:T(8,128)S(1)} %get-tuple-element.42.refs_6_), channel_id=1, source_target_pairs={{0,16},{4,20},{8,24},{12,28},{16,0},{20,4},{24,8},{28,12},{1,17},{... | collective-permute-start | bytes 196616 | tf_op jit(solution)/shard_map/ppermute | solution.py:433
  34.9 1.4 %collective-permute-start.9 = (f32[4,32,128]{2,1,0:T(8,128)S(1)}, f32[4,32,128]{2,1,0:T(8,128)S(1)}, u32[]{:S(2)}, u32[]{:S(2)}) collective-permute-start(f32[4,32,128]{2,1,0:T(8,128)S(1)} %get-tuple-element.42.refs_6_), channel_id=1, source_target_pairs={{0,8},{4,12},{8,0},{12,4},{16,24},{20,28},{24,16},{28,20},{1,9},{5... | collective-permute-start | bytes 196616 | tf_op jit(solution)/shard_map/ppermute | solution.py:433
  36.3 2.3 %collective-permute-done.11.refs_9_ = f32[4,32,128]{2,1,0:T(8,128)S(1)} collective-permute-done((f32[4,32,128]{2,1,0:T(8,128)S(1)}, f32[4,32,128]{2,1,0:T(8,128)S(1)}, u32[]{:S(2)}, u32[]{:S(2)}) %collective-permute-start.11) | collective-permute-done | bytes 65568 | tf_op jit(solution)/shard_map/ppermute | solution.py:433
  38.6 1.6 %collective-permute-done.10.refs_8_ = f32[4,32,128]{2,1,0:T(8,128)S(1)} collective-permute-done((f32[4,32,128]{2,1,0:T(8,128)S(1)}, f32[4,32,128]{2,1,0:T(8,128)S(1)}, u32[]{:S(2)}, u32[]{:S(2)}) %collective-permute-start.10) | collective-permute-done | bytes 65568 | tf_op jit(solution)/shard_map/ppermute | solution.py:433
  40.2 3.0 %post.1 = (f32[136,128]{1,0:T(8,128)S(1)}, f32[136,128]{1,0:T(8,128)S(1)}, f32[136,128]{1,0:T(8,128)S(1)}, f32[136,128]{1,0:T(8,128)S(1)}, f32[136,128]{1,0:T(8,...) custom-call(s32[2]{0:T(128)S(1)} %pad_add_fusion.place_ref, f32[8]{0:T(128)S(1)} %copy-done.2, ...), custom_call_target="tpu_custom_call" | custom-call | tf_op jit(solution)/shard_map/post/pallas_call | solution.py:408
  43.8 1.4 %collective-permute-start.14 = (f32[136,128]{1,0:T(8,128)S(1)}, f32[136,128]{1,0:T(8,128)S(1)}, u32[]{:S(2)}, u32[]{:S(2)}) collective-permute-start(f32[136,128]{1,0:T(8,128)S(1)} %get-tuple-element.46), channel_id=1, source_target_pairs={{0,3},{1,2},{2,1},{3,0},{4,7},{5,6},{6,5},{7,4},{8,11},{9,10},{10,... | collective-permute-start | bytes 208904 | tf_op jit(solution)/shard_map/ppermute | solution.py:424
  45.1 1.5 %collective-permute-start.15 = (f32[136,128]{1,0:T(8,128)S(1)}, f32[136,128]{1,0:T(8,128)S(1)}, u32[]{:S(2)}, u32[]{:S(2)}) collective-permute-start(f32[136,128]{1,0:T(8,128)S(1)} %get-tuple-element.47), channel_id=1, source_target_pairs={{0,4},{1,5},{2,6},{3,7},{4,0},{5,1},{6,2},{7,3},{8,12},{9,13},{10,... | collective-permute-start | bytes 208904 | tf_op jit(solution)/shard_map/ppermute | solution.py:424
  46.8 1.3 %collective-permute-start.17 = (f32[136,128]{1,0:T(8,128)S(1)}, f32[136,128]{1,0:T(8,128)S(1)}, u32[]{:S(2)}, u32[]{:S(2)}) collective-permute-start(f32[136,128]{1,0:T(8,128)S(1)} %get-tuple-element.49), channel_id=1, source_target_pairs={{0,6},{1,7},{2,4},{3,5},{4,2},{5,3},{6,0},{7,1},{8,14},{9,15},{10,... | collective-permute-start | bytes 208904 | tf_op jit(solution)/shard_map/ppermute | solution.py:424
  54.2 5.1 %stack.15 = f32[8]{0:T(128)S(1)} concatenate(f32[1]{0:T(128)} %bitcast.2, f32[1]{0:T(128)} %bitcast.3, f32[1]{0:T(128)} %bitcast.4, f32[1]{0:T(128)} %bitcast.5, f32[1]{0:T(128)} %bitcast.6, f32[1]{0:T(128)} %bitcast.7, f32[1]{0:T(128)} %bitcast.8, f32[1]{0:T(128)} %bitcast.9), dimensions={0} | concatenate | bytes 64 | tf_op jit(solution)/shard_map/stack | solution.py:489
  59.3 2.6 %collective-permute-start.21 = (f32[8]{0:T(128)S(1)}, f32[8]{0:T(128)S(1)}, u32[]{:S(2)}, u32[]{:S(2)}) collective-permute-start(f32[8]{0:T(128)S(1)} %stack.15), channel_id=1, source_target_pairs={{0,24},{4,28},{8,16},{12,20},{16,8},{20,12},{24,0},{28,4},{1,25},{... | collective-permute-start | bytes 104 | tf_op jit(solution)/shard_map/ppermute | solution.py:433
  61.9 1.8 %collective-permute-start.19 = (f32[8]{0:T(128)S(1)}, f32[8]{0:T(128)S(1)}, u32[]{:S(2)}, u32[]{:S(2)}) collective-permute-start(f32[8]{0:T(128)S(1)} %stack.15), channel_id=1, source_target_pairs={{0,8},{4,12},{8,0},{12,4},{16,24},{20,28},{24,16},{28,20},{1,9},{5... | collective-permute-start | bytes 104 | tf_op jit(solution)/shard_map/ppermute | solution.py:433
  63.7 1.4 %collect.1 = (f32[8,4,16,128]{3,2,1,0:T(8,128)}, f32[8,4,16,128]{3,2,1,0:T(8,128)}) custom-call(s32[2]{0:T(128)S(1)} %pad_add_fusion.place_ref, f32[136,128]{1,0:T(8,128)S(1)} %get-tuple-element.43.refs_0_, f32[136,128]{1,0:T(8,128)S(1)} %collective-permute-done.12.refs_1_, f32[136,128]{1,0:T(8,128)S(1)} %collective-permute-done.13.refs_2_, ...), custom_call_target="tpu_custom_call" | custom-call | tf_op jit(solution)/shard_map/collect/pallas_call | solution.py:408
  65.0 1.3 %collective-permute-done.20 = f32[8]{0:T(128)S(1)} collective-permute-done((f32[8]{0:T(128)S(1)}, f32[8]{0:T(128)S(1)}, u32[]{:S(2)}, u32[]{:S(2)}) %collective-permute-start.20) | collective-permute-done | bytes 64 | tf_op jit(solution)/shard_map/ppermute | solution.py:433
  (51 shorter events, 13.1 us)
Async XLA Ops:
  0.6 0.8 %copy-start.1 = (f32[4,16,128]{2,1,0:T(8,128)S(1)}, f32[4,16,128]{2,1,0:T(8,128)}, u32[]{:S(2)}) copy-start(f32[4,16,128]{2,1,0:T(8,128)} %reaction_ref.1) | copy-start | bytes 98308
  1.4 0.9 %copy-start = (f32[8,4,16,128]{3,2,1,0:T(8,128)S(1)}, f32[8,4,16,128]{3,2,1,0:T(8,128)}, u32[]{:S(2)}) copy-start(f32[8,4,16,128]{3,2,1,0:T(8,128)} %source_ref.1) | copy-start | bytes 786436
  2.9 4.9 %collective-permute-start = (f32[2,4,16,128]{3,2,1,0:T(8,128)S(1)}, f32[2,4,16,128]{3,2,1,0:T(8,128)S(1)}, u32[]{:S(2)}, u32[]{:S(2)}) collective-permute-start(f32[2,4,16,128]{3,2,1,0:T(8,128)S(1)} %get-tuple-element.29), channel_id=1, source_target_pairs={{0,1},{1,0},{2,3},{3,2},{4,5},{5,4},{6,7},{7,6},{8,9},{9,8},{10,11... | collective-permute-start | bytes 196616 | tf_op jit(solution)/shard_map/ppermute | solution.py:424
  3.4 7.0 %collective-permute-start.1 = (f32[2,4,16,128]{3,2,1,0:T(8,128)S(1)}, f32[2,4,16,128]{3,2,1,0:T(8,128)S(1)}, u32[]{:S(2)}, u32[]{:S(2)}) collective-permute-start(f32[2,4,16,128]{3,2,1,0:T(8,128)S(1)} %get-tuple-element.30), channel_id=1, source_target_pairs={{0,2},{1,3},{2,0},{3,1},{4,6},{5,7},{6,4},{7,5},{8,10},{9,11},{10,... | collective-permute-start | bytes 196616 | tf_op jit(solution)/shard_map/ppermute | solution.py:424
  6.0 4.6 %collective-permute-start.2 = (f32[2,4,16,128]{3,2,1,0:T(8,128)S(1)}, f32[2,4,16,128]{3,2,1,0:T(8,128)S(1)}, u32[]{:S(2)}, u32[]{:S(2)}) collective-permute-start(f32[2,4,16,128]{3,2,1,0:T(8,128)S(1)} %get-tuple-element.31), channel_id=1, source_target_pairs={{0,3},{1,2},{2,1},{3,0},{4,7},{5,6},{6,5},{7,4},{8,11},{9,10},{10,... | collective-permute-start | bytes 196616 | tf_op jit(solution)/shard_map/ppermute | solution.py:424
  6.1 4.6 %collective-permute-start.3 = (f32[2,4,16,128]{3,2,1,0:T(8,128)S(1)}, f32[2,4,16,128]{3,2,1,0:T(8,128)S(1)}, u32[]{:S(2)}, u32[]{:S(2)}) collective-permute-start(f32[2,4,16,128]{3,2,1,0:T(8,128)S(1)} %get-tuple-element.32), channel_id=1, source_target_pairs={{0,4},{1,5},{2,6},{3,7},{4,0},{5,1},{6,2},{7,3},{8,12},{9,13},{10,... | collective-permute-start | bytes 196616 | tf_op jit(solution)/shard_map/ppermute | solution.py:424
  7.8 4.2 %collective-permute-start.4 = (f32[2,4,16,128]{3,2,1,0:T(8,128)S(1)}, f32[2,4,16,128]{3,2,1,0:T(8,128)S(1)}, u32[]{:S(2)}, u32[]{:S(2)}) collective-permute-start(f32[2,4,16,128]{3,2,1,0:T(8,128)S(1)} %get-tuple-element.33), channel_id=1, source_target_pairs={{0,5},{1,4},{2,7},{3,6},{4,1},{5,0},{6,3},{7,2},{8,13},{9,12},{10,... | collective-permute-start | bytes 196616 | tf_op jit(solution)/shard_map/ppermute | solution.py:424
  7.8 6.9 %collective-permute-start.5 = (f32[2,4,16,128]{3,2,1,0:T(8,128)S(1)}, f32[2,4,16,128]{3,2,1,0:T(8,128)S(1)}, u32[]{:S(2)}, u32[]{:S(2)}) collective-permute-start(f32[2,4,16,128]{3,2,1,0:T(8,128)S(1)} %get-tuple-element.34), channel_id=1, source_target_pairs={{0,6},{1,7},{2,4},{3,5},{4,2},{5,3},{6,0},{7,1},{8,14},{9,15},{10,... | collective-permute-start | bytes 196616 | tf_op jit(solution)/shard_map/ppermute | solution.py:424
  10.5 5.4 %collective-permute-start.6 = (f32[2,4,16,128]{3,2,1,0:T(8,128)S(1)}, f32[2,4,16,128]{3,2,1,0:T(8,128)S(1)}, u32[]{:S(2)}, u32[]{:S(2)}) collective-permute-start(f32[2,4,16,128]{3,2,1,0:T(8,128)S(1)} %get-tuple-element.35), channel_id=1, source_target_pairs={{0,7},{1,6},{2,5},{3,4},{4,3},{5,2},{6,1},{7,0},{8,15},{9,14},{10,... | collective-permute-start | bytes 196616 | tf_op jit(solution)/shard_map/ppermute | solution.py:424
  16.5 9.3 %collective-permute-start.7 = (f32[2,4,64,128]{3,2,1,0:T(8,128)S(1)}, f32[2,4,64,128]{3,2,1,0:T(8,128)S(1)}, u32[]{:S(2)}, u32[]{:S(2)}) collective-permute-start(f32[2,4,64,128]{3,2,1,0:T(8,128)S(1)} %get-tuple-element.36.refs_4_), channel_id=1, source_target_pairs={{0,8},{4,12},{8,16},{12,20},{16,24},{20,28},{1,9},{5,13},{9,17},{1... | collective-permute-start | bytes 786440 | tf_op jit(solution)/shard_map/ppermute | solution.py:462
  20.0 9.9 %collective-permute-start.8 = (f32[2,4,64,128]{3,2,1,0:T(8,128)S(1)}, f32[2,4,64,128]{3,2,1,0:T(8,128)S(1)}, u32[]{:S(2)}, u32[]{:S(2)}) collective-permute-start(f32[2,4,64,128]{3,2,1,0:T(8,128)S(1)} %get-tuple-element.37.refs_3_), channel_id=1, source_target_pairs={{8,0},{12,4},{16,8},{20,12},{24,16},{28,20},{9,1},{13,5},{17,9},{2... | collective-permute-start | bytes 786440 | tf_op jit(solution)/shard_map/ppermute | solution.py:463
  31.8 6.8 %collective-permute-start.11 = (f32[4,32,128]{2,1,0:T(8,128)S(1)}, f32[4,32,128]{2,1,0:T(8,128)S(1)}, u32[]{:S(2)}, u32[]{:S(2)}) collective-permute-start(f32[4,32,128]{2,1,0:T(8,128)S(1)} %get-tuple-element.42.refs_6_), channel_id=1, source_target_pairs={{0,24},{4,28},{8,16},{12,20},{16,8},{20,12},{24,0},{28,4},{1,25},{... | collective-permute-start | bytes 196616 | tf_op jit(solution)/shard_map/ppermute | solution.py:433
  33.5 6.7 %collective-permute-start.10 = (f32[4,32,128]{2,1,0:T(8,128)S(1)}, f32[4,32,128]{2,1,0:T(8,128)S(1)}, u32[]{:S(2)}, u32[]{:S(2)}) collective-permute-start(f32[4,32,128]{2,1,0:T(8,128)S(1)} %get-tuple-element.42.refs_6_), channel_id=1, source_target_pairs={{0,16},{4,20},{8,24},{12,28},{16,0},{20,4},{24,8},{28,12},{1,17},{... | collective-permute-start | bytes 196616 | tf_op jit(solution)/shard_map/ppermute | solution.py:433
  34.9 5.2 %collective-permute-start.9 = (f32[4,32,128]{2,1,0:T(8,128)S(1)}, f32[4,32,128]{2,1,0:T(8,128)S(1)}, u32[]{:S(2)}, u32[]{:S(2)}) collective-permute-start(f32[4,32,128]{2,1,0:T(8,128)S(1)} %get-tuple-element.42.refs_6_), channel_id=1, source_target_pairs={{0,8},{4,12},{8,0},{12,4},{16,24},{20,28},{24,16},{28,20},{1,9},{5... | collective-permute-start | bytes 196616 | tf_op jit(solution)/shard_map/ppermute | solution.py:433
  43.2 3.6 %collective-permute-start.12 = (f32[136,128]{1,0:T(8,128)S(1)}, f32[136,128]{1,0:T(8,128)S(1)}, u32[]{:S(2)}, u32[]{:S(2)}) collective-permute-start(f32[136,128]{1,0:T(8,128)S(1)} %get-tuple-element.44), channel_id=1, source_target_pairs={{0,1},{1,0},{2,3},{3,2},{4,5},{5,4},{6,7},{7,6},{8,9},{9,8},{10,11... | collective-permute-start | bytes 208904 | tf_op jit(solution)/shard_map/ppermute | solution.py:424
  43.3 5.0 %collective-permute-start.13 = (f32[136,128]{1,0:T(8,128)S(1)}, f32[136,128]{1,0:T(8,128)S(1)}, u32[]{:S(2)}, u32[]{:S(2)}) collective-permute-start(f32[136,128]{1,0:T(8,128)S(1)} %get-tuple-element.45), channel_id=1, source_target_pairs={{0,2},{1,3},{2,0},{3,1},{4,6},{5,7},{6,4},{7,5},{8,10},{9,11},{10,... | collective-permute-start | bytes 208904 | tf_op jit(solution)/shard_map/ppermute | solution.py:424
  43.8 7.3 %collective-permute-start.14 = (f32[136,128]{1,0:T(8,128)S(1)}, f32[136,128]{1,0:T(8,128)S(1)}, u32[]{:S(2)}, u32[]{:S(2)}) collective-permute-start(f32[136,128]{1,0:T(8,128)S(1)} %get-tuple-element.46), channel_id=1, source_target_pairs={{0,3},{1,2},{2,1},{3,0},{4,7},{5,6},{6,5},{7,4},{8,11},{9,10},{10,... | collective-permute-start | bytes 208904 | tf_op jit(solution)/shard_map/ppermute | solution.py:424
  45.1 6.5 %collective-permute-start.15 = (f32[136,128]{1,0:T(8,128)S(1)}, f32[136,128]{1,0:T(8,128)S(1)}, u32[]{:S(2)}, u32[]{:S(2)}) collective-permute-start(f32[136,128]{1,0:T(8,128)S(1)} %get-tuple-element.47), channel_id=1, source_target_pairs={{0,4},{1,5},{2,6},{3,7},{4,0},{5,1},{6,2},{7,3},{8,12},{9,13},{10,... | collective-permute-start | bytes 208904 | tf_op jit(solution)/shard_map/ppermute | solution.py:424
  46.6 5.6 %collective-permute-start.16 = (f32[136,128]{1,0:T(8,128)S(1)}, f32[136,128]{1,0:T(8,128)S(1)}, u32[]{:S(2)}, u32[]{:S(2)}) collective-permute-start(f32[136,128]{1,0:T(8,128)S(1)} %get-tuple-element.48), channel_id=1, source_target_pairs={{0,5},{1,4},{2,7},{3,6},{4,1},{5,0},{6,3},{7,2},{8,13},{9,12},{10,... | collective-permute-start | bytes 208904 | tf_op jit(solution)/shard_map/ppermute | solution.py:424
  46.8 5.9 %collective-permute-start.17 = (f32[136,128]{1,0:T(8,128)S(1)}, f32[136,128]{1,0:T(8,128)S(1)}, u32[]{:S(2)}, u32[]{:S(2)}) collective-permute-start(f32[136,128]{1,0:T(8,128)S(1)} %get-tuple-element.49), channel_id=1, source_target_pairs={{0,6},{1,7},{2,4},{3,5},{4,2},{5,3},{6,0},{7,1},{8,14},{9,15},{10,... | collective-permute-start | bytes 208904 | tf_op jit(solution)/shard_map/ppermute | solution.py:424
  48.3 5.4 %collective-permute-start.18 = (f32[136,128]{1,0:T(8,128)S(1)}, f32[136,128]{1,0:T(8,128)S(1)}, u32[]{:S(2)}, u32[]{:S(2)}) collective-permute-start(f32[136,128]{1,0:T(8,128)S(1)} %get-tuple-element.50), channel_id=1, source_target_pairs={{0,7},{1,6},{2,5},{3,4},{4,3},{5,2},{6,1},{7,0},{8,15},{9,14},{10,... | collective-permute-start | bytes 208904 | tf_op jit(solution)/shard_map/ppermute | solution.py:424
  59.3 5.8 %collective-permute-start.21 = (f32[8]{0:T(128)S(1)}, f32[8]{0:T(128)S(1)}, u32[]{:S(2)}, u32[]{:S(2)}) collective-permute-start(f32[8]{0:T(128)S(1)} %stack.15), channel_id=1, source_target_pairs={{0,24},{4,28},{8,16},{12,20},{16,8},{20,12},{24,0},{28,4},{1,25},{... | collective-permute-start | bytes 104 | tf_op jit(solution)/shard_map/ppermute | solution.py:433
  61.8 4.4 %collective-permute-start.20 = (f32[8]{0:T(128)S(1)}, f32[8]{0:T(128)S(1)}, u32[]{:S(2)}, u32[]{:S(2)}) collective-permute-start(f32[8]{0:T(128)S(1)} %stack.15), channel_id=1, source_target_pairs={{0,16},{4,20},{8,24},{12,28},{16,0},{20,4},{24,8},{28,12},{1,17},{... | collective-permute-start | bytes 104 | tf_op jit(solution)/shard_map/ppermute | solution.py:433
  61.9 4.4 %collective-permute-start.19 = (f32[8]{0:T(128)S(1)}, f32[8]{0:T(128)S(1)}, u32[]{:S(2)}, u32[]{:S(2)}) collective-permute-start(f32[8]{0:T(128)S(1)} %stack.15), channel_id=1, source_target_pairs={{0,8},{4,12},{8,0},{12,4},{16,24},{20,28},{24,16},{28,20},{1,9},{5... | collective-permute-start | bytes 104 | tf_op jit(solution)/shard_map/ppermute | solution.py:433
  (3 other events, 2.0 us)

commit v5 on v4

--- a/solution.py
+++ b/solution.py
@@ -231,50 +231,67 @@
     return jnp.where(col // 2 == row, 1.0, 0.0).astype(jnp.bfloat16)
 
 
-def pack_kernel(place_ref, source_ref, reaction_ref, *out_refs):
-    for k, out_ref in enumerate(out_refs):
-        out_ref[0] = source_ref[jnp.bitwise_xor(place_ref[0], k)]
-        out_ref[1] = reaction_ref[...]
-
-
-def arrange_kernel(gy_size, place_ref, *refs):
-    pieces, (low_ref, high_ref, both) = refs[:-3], refs[-3:]
-    _, bx, by, _ = pieces[0].shape
-    for k, piece in enumerate(pieces):
-        owner = jnp.bitwise_xor(place_ref[0], k)
-        planes = pl.ds((owner // gy_size) * bx, bx)
-        rows = pl.ds(pl.multiple_of(lax.rem(owner, gy_size) * by, 8), by)
-        both[:, planes, rows, :] = piece[...]
-    low_ref[...] = both[:, pl.ds(0, HALO)]
-    high_ref[...] = both[:, pl.ds(HALO, HALO)]
-
-
-def pre_kernel(slabs, place_ref, shifts_ref, index_ref, velocity_ref, *refs):
+def pack_kernel(place_ref, source_ref, reaction_ref, out_ref, sems):
+    columns = out_ref.shape[0] - 1
+    other = jnp.bitwise_xor(place_ref[0], 1) & 1
+    copies = [pltpu.make_async_copy(reaction_ref, out_ref.at[columns], sems.at[columns])]
+    for i in range(columns):
+        copies.append(pltpu.make_async_copy(source_ref.at[2 * i + other], out_ref.at[i], sems.at[i]))
+    for copy in copies:
+        copy.start()
+    for copy in copies:
+        copy.wait()
+
+
+def merge_kernel(place_ref, source_ref, reaction_ref, theirs_ref, *out_refs):
+    chip, core = place_ref[0] // 2, place_ref[0] & 1
+    columns, by = theirs_ref.shape[0] - 1, source_ref.shape[2]
+    mine = pl.ds(pl.multiple_of(core * by, 8), by)
+    theirs = pl.ds(pl.multiple_of((1 - core) * by, 8), by)
+    for m, out_ref in enumerate(out_refs):
+        target = jnp.bitwise_xor(chip, m)
+        out_ref[0, :, mine, :] = source_ref[2 * target + core]
+        out_ref[0, :, theirs, :] = theirs_ref[target]
+        out_ref[1, :, mine, :] = reaction_ref[...]
+        out_ref[1, :, theirs, :] = theirs_ref[columns]
+
+
+def squares_kernel(row, *refs):
+    for k, part in enumerate(refs[:-1]):
+        refs[-1][pl.ds(k, 1), :] = part[pl.ds(row, 1), :]
+
+
+def pre_kernel(slabs, chips_y, place_ref, shifts_ref, index_ref, velocity_ref, *refs):
     pool_ref, pool_up_ref = refs[:2]
-    parts = refs[2:6]
-    f, r, w, v1, coarse_ref, v0, tmp, pooled = refs[6:]
+    parts, refs = refs[2:-8], refs[-8:]
+    f, r, w, v1, coarse_ref, v0, tmp, pooled = refs
     ny = f.shape[1]
-    slab = place_ref[1]
+    chip, slab = place_ref[0] // 2, place_ref[1]
     shift = shifts_ref[index_ref[place_ref[0]]]
     fine = Level(0, ny, LANES, 0, velocity_ref, shift, f, r, w)
     zero_rows(v0, ny)
     zero_rows(v1, ny)
     count = SLAB + 2 * HALO
+
+    chips = len(parts) // 2
+    rows = parts[0].shape[2]
+    for k, part in enumerate(parts):
+        owner = jnp.bitwise_xor(chip, k % chips)
+        x = owner // chips_y
+        first = HALO * (1 + x) if k < chips else (HALO + SLAB) * (1 - x)
+        to = pl.ds(pl.multiple_of(lax.rem(owner, chips_y) * rows, 8), rows)
+        f[pl.ds(first, HALO), to, :] = part[0]
+        r[pl.ds(first, HALO), to, :] = part[1]
+
     inside = [jnp.where(slab > 0, DAMPING, 0.0)] * HALO
     inside += [DAMPING] * SLAB
     inside += [jnp.where(slab < slabs - 1, DAMPING, 0.0)] * HALO
 
-    def begin(x):
-        part, at = parts[x // HALO], x % HALO
-        return part[0, at], part[1, at]
-
-    def put(x, pair):
-        f[x], r[x] = pair
-        weight = inside[x] / (pair[1] + fine.centre)
+    def put(x, weight):
         w[x] = weight
-        v0[x, pl.ds(8, ny), :] = weight * pair[0]
-
-    sweep(range(count), begin, put)
+        v0[x, pl.ds(8, ny), :] = weight * f[x]
+
+    sweep(range(count), lambda x: inside[x] / (r[x] + fine.centre), put)
     fine.smooth(v0, v1, range(1, count - 1))
     half = ny // 2
 
@@ -400,6 +417,7 @@
         residual_ref[column] = part[pl.ds(area, area), :].reshape(bx, by, LANES)
 
 
+HBM = pl.BlockSpec(memory_space=pltpu.HBM)
 SMEM = pl.BlockSpec(memory_space=pltpu.SMEM)
 VMEM = pl.BlockSpec(memory_space=pltpu.VMEM)
 
@@ -416,12 +434,26 @@
     )(*scalars, *arrays)
 
 
-def swap_in_plane(pieces, columns):
+def swap_in_plane(pieces, unit):
     devices = lax.axis_size("gx") * lax.axis_size("gy")
     moved = [pieces[0]]
-    for k in range(1, columns):
-        pairs = [(i, i ^ k) for i in range(devices)]
+    for k in range(1, len(pieces)):
+        pairs = [(i, i ^ (k * unit)) for i in range(devices)]
         moved.append(lax.ppermute(pieces[k], ("gx", "gy"), pairs))
+    return moved
+
+
+def send_beside(pieces, columns, chips_y):
+    devices = lax.axis_size("gx") * lax.axis_size("gy")
+    moved = []
+    for m, piece in enumerate(pieces):
+        pairs = []
+        for i in range(devices):
+            up = (i % columns) // 2 // chips_y
+            target = (i ^ (2 * m)) + (columns if up else -columns)
+            if 0 <= target < devices:
+                pairs.append((i, target))
+        moved.append(lax.ppermute(piece, ("gx", "gy"), pairs))
     return moved
 
 
@@ -447,27 +479,32 @@
     count = SLAB + 2 * HALO
     area = bx * by
 
-    pieces = local_kernel(
-        pack_kernel, "pack", (place,), (source, reaction), [(2, bx, by, nz)] * columns
-    )
-    pieces = swap_in_plane(pieces, columns)
-    low, high = local_kernel(
-        functools.partial(arrange_kernel, gy_size),
-        "arrange",
+    chips, chips_y = columns // 2, gy_size // 2
+    packed = pl.pallas_call(
+        pack_kernel,
+        out_shape=jax.ShapeDtypeStruct((chips + 1, bx, by, nz), jnp.float32),
+        in_specs=[SMEM, HBM, HBM],
+        out_specs=VMEM,
+        scratch_shapes=[pltpu.SemaphoreType.DMA((chips + 1,))],
+        compiler_params=pltpu.CompilerParams(vmem_limit_bytes=63 * 1024 * 1024),
+        name="pack",
+    )(place, source, reaction)
+    theirs = lax.ppermute(packed, "gy", [(i, i ^ 1) for i in range(gy_size)])
+    blocks = local_kernel(
+        merge_kernel,
+        "merge",
         (place,),
-        pieces,
-        [(2, HALO, ny, nz)] * 2,
-        [(2, SLAB, ny, nz)],
-    )
-    before = lax.ppermute(high, "gx", [(i, i + step) for i in range(gx_size - step)])
-    after = lax.ppermute(low, "gx", [(i + step, i) for i in range(gx_size - step)])
+        (source, reaction, theirs),
+        [(2, bx, 2 * by, nz)] * chips,
+    )
+    parts = swap_in_plane(blocks, 2) + send_beside(blocks, columns, chips_y)
 
     grid, rimmed = (count, ny, nz), (count, ny + 16, nz)
     f, r, w, v1, coarse = local_kernel(
-        functools.partial(pre_kernel, slabs),
+        functools.partial(pre_kernel, slabs, chips_y),
         "pre",
         scalars,
-        (pool_matrix(0), pool_matrix(LANES // 2), before, low, high, after),
+        (pool_matrix(0), pool_matrix(LANES // 2), *parts),
         [grid, grid, grid, rimmed, (SLAB // 2, ny // 2, nz)],
         [rimmed, (SLAB, ny, nz), (2, SLAB // 2 * ny // 2, nz)],
     )
@@ -484,11 +521,13 @@
         [(2 * area + 8, nz)] * columns,
         [rimmed] * 2 + [coarse_grid] * 3 + [coarse_rimmed] * 2 + [(rows, nz), (nx // 2, ny, nz)],
     )
-    parts = swap_in_plane(results, columns)
-
-    squares = jnp.stack([part[2 * area, 0] for part in parts])
+    parts = swap_in_plane(results, 1)
+
+    (squares,) = local_kernel(
+        functools.partial(squares_kernel, 2 * area), "squares", (), parts, [(columns, nz)]
+    )
     total = sum(swap_slabs(squares, step, slabs))
-    rms = jnp.sqrt(total / (nx * ny * nz) + EPSILON)
+    rms = jnp.sqrt(total[:, 0] / (nx * ny * nz) + EPSILON)
     slots = jnp.arange(columns, dtype=jnp.int32)
     mine = jnp.bitwise_xor(slots, column)[None, :] == slots[:, None]
     residual_rms = jnp.sum(jnp.where(mine, rms[None, :], 0.0), axis=1)
@@ -509,7 +548,8 @@
     slabs, ny = gx_size // step, by * gy_size
     whole = power_of_two(columns) and power_of_two(step) and power_of_two(slabs)
     small = slabs * ny * nz <= 2**15
-    return whole and small and bx * step == SLAB and nz == LANES and by % 16 == 0
+    paired = step == 2 and bx == HALO and gy_size % 2 == 0
+    return whole and small and paired and bx * step == SLAB and nz == LANES and by % 16 == 0
 
 
 def solution(mesh):

time: 67.3 us -> 64.9 us (0.964)
  local copies, waits for them, and re-layouts: 11.6 us -> 0.7 us
  starting transfers between devices: 27.5 us -> 35.5 us
  waiting for transfers between devices: 19.4 us -> 17.3 us
  Pallas kernels: 6.83 us -> 8.74 us
  other arithmetic: 0.85 us -> 1.54 us
    ppermute x14 -> x10, starting transfers between devices: 13.9 us -> 21.7 us  [swap_in_plane(): moved.append(lax.ppermute(pieces[k], ('gx', 'gy'), pairs))]
    ppermute x2 -> x5, waiting for transfers between devices: 8.5 us -> 1.25 us  [the longest x1 1.24 us: column_body(): theirs = lax.ppermute(packed, 'gy', [(i, i ^ 1) for i in range(gy_size)])]
    another operation x1 -> x0, local copies, waits for them, and re-layouts: 5.07 us -> none  [column_body(): squares = jnp.stack([part[2 * area, 0] for part in parts])]
    slice x8 -> x0, local copies, waits for them, and re-layouts: 4.26 us -> none  [column_body(): squares = jnp.stack([part[2 * area, 0] for part in parts])]
    ppermute x14 -> x10, waiting for transfers between devices: 5.71 us -> 9.58 us  [swap_in_plane(): moved.append(lax.ppermute(pieces[k], ('gx', 'gy'), pairs))]
    pallas_call x0 -> x1, Pallas kernels: none -> 2.33 us  [column_body(): pl.pallas_call(pack_kernel, out_shape=jax.ShapeDtypeStruct((chips + 1, bx...]
    unnamed x10 -> x12, local copies, waits for them, and re-layouts: 2.29 us -> 0.7 us
    ppermute x6, waiting for transfers between devices: 5.15 us -> 6.48 us  [swap_slabs(): moved.append(lax.ppermute(piece, 'gx', pairs))]
  transfers between devices with their start and end apart: 22 -> 21, of which waited for: 10 -> 9; matrix products, arithmetic and copies ran while one was open for 6% -> 0% of each run, Pallas kernels for 2% -> 2%
where the time goes in v5:
time: 64.9 us; the launch traced here: 64.6 us
  starting transfers between devices  35.5 us (55%)
  waiting for transfers between devices  17.3 us (27%)
  Pallas kernels  8.74 us (13%)
  other arithmetic  1.54 us (2%)
  between operations  0.79 us (1%)
  local copies, waits for them, and re-layouts  0.7 us (1%)
    ppermute x10, starting transfers between devices, swap_in_plane(): moved.append(lax.ppermute(pieces[k], ('gx', 'gy'), pairs))  21.7 us
    ppermute x10, waiting for transfers between devices, swap_in_plane(): moved.append(lax.ppermute(pieces[k], ('gx', 'gy'), pairs))  9.58 us
    ppermute x6, starting transfers between devices, swap_slabs(): moved.append(lax.ppermute(piece, 'gx', pairs))  9.4 us
    ppermute x6, waiting for transfers between devices, swap_slabs(): moved.append(lax.ppermute(piece, 'gx', pairs))  6.48 us
    pallas_call x5, Pallas kernels, local_kernel(): pl.pallas_call(kernel, out_shape=[jax.ShapeDtypeStruct(shape, jnp.float32...  6.42 us
    ppermute x4, starting transfers between devices, send_beside(): moved.append(lax.ppermute(piece, ('gx', 'gy'), pairs))  3.9 us
    pallas_call x1, Pallas kernels, column_body(): pl.pallas_call(pack_kernel, out_shape=jax.ShapeDtypeStruct((chips + 1, bx...  2.33 us
  transfers between devices with their start and end apart: 21, of which 9 were waited for; matrix products, arithmetic and copies ran while one was open for 0% of the time, Pallas kernels for 2%

profile of v5, /device:TPU:0, one launch (start us, length us, event | category | flops | bytes accessed | tf_op | source)
XLA Modules:
  0.0 64.6 jit_solution(5698357320222366455)
XLA Ops:
  1.3 2.3 %pack.1 = f32[5,4,16,128]{3,2,1,0:T(8,128)} custom-call(s32[2]{0:T(128)} %pad_add_fusion.place_ref, f32[8,4,16,128]{3,2,1,0:T(8,128)} %source_ref.3, f32[4,16,128]{2,1,0:T(8,128)} %reaction_ref.3), custom_call_target="tpu_custom_call" | custom-call | tf_op jit(solution)/shard_map/pack/pallas_call | solution.py:483
  4.2 1.2 %collective-permute-done.theirs_ref = f32[5,4,16,128]{3,2,1,0:T(8,128)S(1)} collective-permute-done((f32[5,4,16,128]{3,2,1,0:T(8,128)}, f32[5,4,16,128]{3,2,1,0:T(8,128)S(1)}, u32[]{:S(2)}, u32[]{:S(2)}) %collective-permute-start) | collective-permute-done | bytes 163872 | tf_op jit(solution)/shard_map/ppermute | solution.py:492
  6.0 1.3 %collective-permute-start.4 = (f32[2,4,32,128]{3,2,1,0:T(8,128)S(1)}, f32[2,4,32,128]{3,2,1,0:T(8,128)S(1)}, u32[]{:S(2)}, u32[]{:S(2)}) collective-permute-start(f32[2,4,32,128]{3,2,1,0:T(8,128)S(1)} %get-tuple-element.22.refs_2_), channel_id=1, source_target_pairs={{4,12},{5,13},{6,14},{7,15},{8,0},{9,1},{10,2},{11,3},{12,20},{13,... | collective-permute-start | bytes 393224 | tf_op jit(solution)/shard_map/ppermute | solution.py:456
  7.3 1.3 %collective-permute-start.5 = (f32[2,4,32,128]{3,2,1,0:T(8,128)S(1)}, f32[2,4,32,128]{3,2,1,0:T(8,128)S(1)}, u32[]{:S(2)}, u32[]{:S(2)}) collective-permute-start(f32[2,4,32,128]{3,2,1,0:T(8,128)S(1)} %get-tuple-element.23), channel_id=1, source_target_pairs={{4,14},{5,15},{6,12},{7,13},{8,2},{9,3},{10,0},{11,1},{12,22},{13,... | collective-permute-start | bytes 393224 | tf_op jit(solution)/shard_map/ppermute | solution.py:456
  8.6 3.0 %collective-permute-start.1 = (f32[2,4,32,128]{3,2,1,0:T(8,128)S(1)}, f32[2,4,32,128]{3,2,1,0:T(8,128)S(1)}, u32[]{:S(2)}, u32[]{:S(2)}) collective-permute-start(f32[2,4,32,128]{3,2,1,0:T(8,128)S(1)} %get-tuple-element.23), channel_id=1, source_target_pairs={{0,2},{1,3},{2,0},{3,1},{4,6},{5,7},{6,4},{7,5},{8,10},{9,11},{10,... | collective-permute-start | bytes 393224 | tf_op jit(solution)/shard_map/ppermute | solution.py:442
  12.2 7.1 %collective-permute-start.2 = (f32[2,4,32,128]{3,2,1,0:T(8,128)S(1)}, f32[2,4,32,128]{3,2,1,0:T(8,128)S(1)}, u32[]{:S(2)}, u32[]{:S(2)}) collective-permute-start(f32[2,4,32,128]{3,2,1,0:T(8,128)S(1)} %get-tuple-element.24), channel_id=1, source_target_pairs={{0,4},{1,5},{2,6},{3,7},{4,0},{5,1},{6,2},{7,3},{8,12},{9,13},{10,... | collective-permute-start | bytes 393224 | tf_op jit(solution)/shard_map/ppermute | solution.py:442
  20.1 5.2 %collective-permute-start.3 = (f32[2,4,32,128]{3,2,1,0:T(8,128)S(1)}, f32[2,4,32,128]{3,2,1,0:T(8,128)S(1)}, u32[]{:S(2)}, u32[]{:S(2)}) collective-permute-start(f32[2,4,32,128]{3,2,1,0:T(8,128)S(1)} %get-tuple-element.25), channel_id=1, source_target_pairs={{0,6},{1,7},{2,4},{3,5},{4,2},{5,3},{6,0},{7,1},{8,14},{9,15},{10,... | collective-permute-start | bytes 393224 | tf_op jit(solution)/shard_map/ppermute | solution.py:442
  25.4 2.7 %collective-permute-done.2.refs_4_ = f32[2,4,32,128]{3,2,1,0:T(8,128)S(1)} collective-permute-done((f32[2,4,32,128]{3,2,1,0:T(8,128)S(1)}, f32[2,4,32,128]{3,2,1,0:T(8,128)S(1)}, u32[]{:S(2)}, u32[]{:S(2)}) %collective-permute-start.2) | collective-permute-done | bytes 131104 | tf_op jit(solution)/shard_map/ppermute | solution.py:442
  28.2 1.8 %collective-permute-done.3.refs_5_ = f32[2,4,32,128]{3,2,1,0:T(8,128)S(1)} collective-permute-done((f32[2,4,32,128]{3,2,1,0:T(8,128)S(1)}, f32[2,4,32,128]{3,2,1,0:T(8,128)S(1)}, u32[]{:S(2)}, u32[]{:S(2)}) %collective-permute-start.3) | collective-permute-done | bytes 131104 | tf_op jit(solution)/shard_map/ppermute | solution.py:442
  30.7 1.4 %pre.1 = (f32[16,64,128]{2,1,0:T(8,128)S(1)}, f32[16,64,128]{2,1,0:T(8,128)S(1)}, f32[16,64,128]{2,1,0:T(8,128)S(1)}, f32[16,80,128]{2,1,0:T(8,128)S(1)}, f32[4,32,128]{2,1,0:T(8,128)S(1)}) custom-call(s32[2]{0:T(128)S(1)} %copy-done.2, f32[8]{0:T(128)S(1)} %copy-done.3, s32[8]{0:T(128)S(1)} %copy-done.4, f32[3]{0:T(128)S(1)} %copy-done.5, ...), custom_call_target="tpu_custom_call" | custom-call | tf_op jit(solution)/shard_map/pre/pallas_call | solution.py:426
  32.1 4.4 %collective-permute-start.10 = (f32[4,32,128]{2,1,0:T(8,128)S(1)}, f32[4,32,128]{2,1,0:T(8,128)S(1)}, u32[]{:S(2)}, u32[]{:S(2)}) collective-permute-start(f32[4,32,128]{2,1,0:T(8,128)S(1)} %get-tuple-element.30.refs_6_), channel_id=1, source_target_pairs={{0,24},{4,28},{8,16},{12,20},{16,8},{20,12},{24,0},{28,4},{1,25},{... | collective-permute-start | bytes 196616 | tf_op jit(solution)/shard_map/ppermute | solution.py:465
  37.1 1.7 %collective-permute-done.10.refs_9_ = f32[4,32,128]{2,1,0:T(8,128)S(1)} collective-permute-done((f32[4,32,128]{2,1,0:T(8,128)S(1)}, f32[4,32,128]{2,1,0:T(8,128)S(1)}, u32[]{:S(2)}, u32[]{:S(2)}) %collective-permute-start.10) | collective-permute-done | bytes 65568 | tf_op jit(solution)/shard_map/ppermute | solution.py:465
  38.8 3.4 %collective-permute-done.9.refs_8_ = f32[4,32,128]{2,1,0:T(8,128)S(1)} collective-permute-done((f32[4,32,128]{2,1,0:T(8,128)S(1)}, f32[4,32,128]{2,1,0:T(8,128)S(1)}, u32[]{:S(2)}, u32[]{:S(2)}) %collective-permute-start.9) | collective-permute-done | bytes 65568 | tf_op jit(solution)/shard_map/ppermute | solution.py:465
  42.2 3.1 %post.1 = (f32[136,128]{1,0:T(8,128)S(1)}, f32[136,128]{1,0:T(8,128)S(1)}, f32[136,128]{1,0:T(8,128)S(1)}, f32[136,128]{1,0:T(8,128)S(1)}, f32[136,128]{1,0:T(8,...) custom-call(s32[2]{0:T(128)S(1)} %copy-done.2, f32[8]{0:T(128)S(1)} %copy-done.3, ...), custom_call_target="tpu_custom_call" | custom-call | tf_op jit(solution)/shard_map/post/pallas_call | solution.py:426
  45.4 1.1 %collective-permute-start.12 = (f32[136,128]{1,0:T(8,128)S(1)}, f32[136,128]{1,0:T(8,128)S(1)}, u32[]{:S(2)}, u32[]{:S(2)}) collective-permute-start(f32[136,128]{1,0:T(8,128)S(1)} %get-tuple-element.33), channel_id=1, source_target_pairs={{0,2},{1,3},{2,0},{3,1},{4,6},{5,7},{6,4},{7,5},{8,10},{9,11},{10,... | collective-permute-start | bytes 208904 | tf_op jit(solution)/shard_map/ppermute | solution.py:442
  47.3 1.7 %collective-permute-start.14 = (f32[136,128]{1,0:T(8,128)S(1)}, f32[136,128]{1,0:T(8,128)S(1)}, u32[]{:S(2)}, u32[]{:S(2)}) collective-permute-start(f32[136,128]{1,0:T(8,128)S(1)} %get-tuple-element.35), channel_id=1, source_target_pairs={{0,4},{1,5},{2,6},{3,7},{4,0},{5,1},{6,2},{7,3},{8,12},{9,13},{10,... | collective-permute-start | bytes 208904 | tf_op jit(solution)/shard_map/ppermute | solution.py:442
  49.0 2.1 %collective-permute-start.16 = (f32[136,128]{1,0:T(8,128)S(1)}, f32[136,128]{1,0:T(8,128)S(1)}, u32[]{:S(2)}, u32[]{:S(2)}) collective-permute-start(f32[136,128]{1,0:T(8,128)S(1)} %get-tuple-element.37), channel_id=1, source_target_pairs={{0,6},{1,7},{2,4},{3,5},{4,2},{5,3},{6,0},{7,1},{8,14},{9,15},{10,... | collective-permute-start | bytes 208904 | tf_op jit(solution)/shard_map/ppermute | solution.py:442
  51.7 1.6 %collective-permute-done.15.refs_5_ = f32[136,128]{1,0:T(8,128)S(1)} collective-permute-done((f32[136,128]{1,0:T(8,128)S(1)}, f32[136,128]{1,0:T(8,128)S(1)}, u32[]{:S(2)}, u32[]{:S(2)}) %collective-permute-start.15) | collective-permute-done | bytes 69664 | tf_op jit(solution)/shard_map/ppermute | solution.py:442
  53.3 2.4 %collective-permute-done.16.refs_6_ = f32[136,128]{1,0:T(8,128)S(1)} collective-permute-done((f32[136,128]{1,0:T(8,128)S(1)}, f32[136,128]{1,0:T(8,128)S(1)}, u32[]{:S(2)}, u32[]{:S(2)}) %collective-permute-start.16) | collective-permute-done | bytes 69664 | tf_op jit(solution)/shard_map/ppermute | solution.py:442
  55.7 1.0 %collective-permute-done.17.refs_7_ = f32[136,128]{1,0:T(8,128)S(1)} collective-permute-done((f32[136,128]{1,0:T(8,128)S(1)}, f32[136,128]{1,0:T(8,128)S(1)}, u32[]{:S(2)}, u32[]{:S(2)}) %collective-permute-start.17) | collective-permute-done | bytes 69664 | tf_op jit(solution)/shard_map/ppermute | solution.py:442
  56.7 2.6 %collective-permute-start.20 = (f32[8,128]{1,0:T(8,128)S(1)}, f32[8,128]{1,0:T(8,128)S(1)}, u32[]{:S(2)}, u32[]{:S(2)}) collective-permute-start(f32[8,128]{1,0:T(8,128)S(1)} %squares.1), channel_id=1, source_target_pairs={{0,24},{4,28},{8,16},{12,20},{16,8},{20,12},{24,0},{28,4},{1,25},{... | collective-permute-start | bytes 12296 | tf_op jit(solution)/shard_map/ppermute | solution.py:465
  59.3 1.8 %collective-permute-start.18 = (f32[8,128]{1,0:T(8,128)S(1)}, f32[8,128]{1,0:T(8,128)S(1)}, u32[]{:S(2)}, u32[]{:S(2)}) collective-permute-start(f32[8,128]{1,0:T(8,128)S(1)} %squares.1), channel_id=1, source_target_pairs={{0,8},{4,12},{8,0},{12,4},{16,24},{20,28},{24,16},{28,20},{1,9},{5... | collective-permute-start | bytes 12296 | tf_op jit(solution)/shard_map/ppermute | solution.py:465
  61.1 1.4 %collect.1 = (f32[8,4,16,128]{3,2,1,0:T(8,128)}, f32[8,4,16,128]{3,2,1,0:T(8,128)}) custom-call(s32[2]{0:T(128)S(1)} %copy-done.2, f32[136,128]{1,0:T(8,128)S(1)} %get-tuple-element.31.refs_0_, f32[136,128]{1,0:T(8,128)S(1)} %collective-permute-done.11.refs_1_, f32[136,128]{1,0:T(8,128)S(1)} %collective-permute-done.12.refs_2_, ...), custom_call_target="tpu_custom_call" | custom-call | tf_op jit(solution)/shard_map/collect/pallas_call | solution.py:426
  62.4 1.3 %collective-permute-done.19 = f32[8,128]{1,0:T(8,128)S(1)} collective-permute-done((f32[8,128]{1,0:T(8,128)S(1)}, f32[8,128]{1,0:T(8,128)S(1)}, u32[]{:S(2)}, u32[]{:S(2)}) %collective-permute-start.19) | collective-permute-done | bytes 4128 | tf_op jit(solution)/shard_map/ppermute | solution.py:465
  (44 shorter events, 6.7 us)
Async XLA Ops:
  0.6 4.8 %copy-start = (f32[8,4,16,128]{3,2,1,0:T(8,128)S(1)}, f32[8,4,16,128]{3,2,1,0:T(8,128)}, u32[]{:S(2)}) copy-start(f32[8,4,16,128]{3,2,1,0:T(8,128)} %source_ref.3) | copy-start | bytes 786436
  1.3 4.1 %copy-start.1 = (f32[4,16,128]{2,1,0:T(8,128)S(1)}, f32[4,16,128]{2,1,0:T(8,128)}, u32[]{:S(2)}) copy-start(f32[4,16,128]{2,1,0:T(8,128)} %reaction_ref.3) | copy-start | bytes 98308
  1.3 4.1 %copy-start.2 = (s32[2]{0:T(128)S(1)}, s32[2]{0:T(128)}, u32[]{:S(2)}) copy-start(s32[2]{0:T(128)} %pad_add_fusion.place_ref) | copy-start | bytes 28
  3.6 1.8 %collective-permute-start = (f32[5,4,16,128]{3,2,1,0:T(8,128)}, f32[5,4,16,128]{3,2,1,0:T(8,128)S(1)}, u32[]{:S(2)}, u32[]{:S(2)}) collective-permute-start(f32[5,4,16,128]{3,2,1,0:T(8,128)} %pack.1), channel_id=1, source_target_pairs={{0,1},{1,0},{2,3},{3,2},{4,5},{5,4},{6,7},{7,6},{8,9},{9,8},{10,11... | collective-permute-start | bytes 491528 | tf_op jit(solution)/shard_map/ppermute | solution.py:492
  6.0 13.4 %collective-permute-start.4 = (f32[2,4,32,128]{3,2,1,0:T(8,128)S(1)}, f32[2,4,32,128]{3,2,1,0:T(8,128)S(1)}, u32[]{:S(2)}, u32[]{:S(2)}) collective-permute-start(f32[2,4,32,128]{3,2,1,0:T(8,128)S(1)} %get-tuple-element.22.refs_2_), channel_id=1, source_target_pairs={{4,12},{5,13},{6,14},{7,15},{8,0},{9,1},{10,2},{11,3},{12,20},{13,... | collective-permute-start | bytes 393224 | tf_op jit(solution)/shard_map/ppermute | solution.py:456
  7.3 12.8 %collective-permute-start.5 = (f32[2,4,32,128]{3,2,1,0:T(8,128)S(1)}, f32[2,4,32,128]{3,2,1,0:T(8,128)S(1)}, u32[]{:S(2)}, u32[]{:S(2)}) collective-permute-start(f32[2,4,32,128]{3,2,1,0:T(8,128)S(1)} %get-tuple-element.23), channel_id=1, source_target_pairs={{4,14},{5,15},{6,12},{7,13},{8,2},{9,3},{10,0},{11,1},{12,22},{13,... | collective-permute-start | bytes 393224 | tf_op jit(solution)/shard_map/ppermute | solution.py:456
  8.6 16.8 %collective-permute-start.1 = (f32[2,4,32,128]{3,2,1,0:T(8,128)S(1)}, f32[2,4,32,128]{3,2,1,0:T(8,128)S(1)}, u32[]{:S(2)}, u32[]{:S(2)}) collective-permute-start(f32[2,4,32,128]{3,2,1,0:T(8,128)S(1)} %get-tuple-element.23), channel_id=1, source_target_pairs={{0,2},{1,3},{2,0},{3,1},{4,6},{5,7},{6,4},{7,5},{8,10},{9,11},{10,... | collective-permute-start | bytes 393224 | tf_op jit(solution)/shard_map/ppermute | solution.py:442
  11.6 13.9 %collective-permute-start.6 = (f32[2,4,32,128]{3,2,1,0:T(8,128)S(1)}, f32[2,4,32,128]{3,2,1,0:T(8,128)S(1)}, u32[]{:S(2)}, u32[]{:S(2)}) collective-permute-start(f32[2,4,32,128]{3,2,1,0:T(8,128)S(1)} %get-tuple-element.24), channel_id=1, source_target_pairs={{4,8},{5,9},{6,10},{7,11},{8,4},{9,5},{10,6},{11,7},{12,16},{13,17... | collective-permute-start | bytes 393224 | tf_op jit(solution)/shard_map/ppermute | solution.py:456
  12.2 15.9 %collective-permute-start.2 = (f32[2,4,32,128]{3,2,1,0:T(8,128)S(1)}, f32[2,4,32,128]{3,2,1,0:T(8,128)S(1)}, u32[]{:S(2)}, u32[]{:S(2)}) collective-permute-start(f32[2,4,32,128]{3,2,1,0:T(8,128)S(1)} %get-tuple-element.24), channel_id=1, source_target_pairs={{0,4},{1,5},{2,6},{3,7},{4,0},{5,1},{6,2},{7,3},{8,12},{9,13},{10,... | collective-permute-start | bytes 393224 | tf_op jit(solution)/shard_map/ppermute | solution.py:442
  19.4 8.8 %collective-permute-start.7 = (f32[2,4,32,128]{3,2,1,0:T(8,128)S(1)}, f32[2,4,32,128]{3,2,1,0:T(8,128)S(1)}, u32[]{:S(2)}, u32[]{:S(2)}) collective-permute-start(f32[2,4,32,128]{3,2,1,0:T(8,128)S(1)} %get-tuple-element.25), channel_id=1, source_target_pairs={{4,10},{5,11},{6,8},{7,9},{8,6},{9,7},{10,4},{11,5},{12,18},{13,19... | collective-permute-start | bytes 393224 | tf_op jit(solution)/shard_map/ppermute | solution.py:456
  20.1 10.0 %collective-permute-start.3 = (f32[2,4,32,128]{3,2,1,0:T(8,128)S(1)}, f32[2,4,32,128]{3,2,1,0:T(8,128)S(1)}, u32[]{:S(2)}, u32[]{:S(2)}) collective-permute-start(f32[2,4,32,128]{3,2,1,0:T(8,128)S(1)} %get-tuple-element.25), channel_id=1, source_target_pairs={{0,6},{1,7},{2,4},{3,5},{4,2},{5,3},{6,0},{7,1},{8,14},{9,15},{10,... | collective-permute-start | bytes 393224 | tf_op jit(solution)/shard_map/ppermute | solution.py:442
  32.1 6.7 %collective-permute-start.10 = (f32[4,32,128]{2,1,0:T(8,128)S(1)}, f32[4,32,128]{2,1,0:T(8,128)S(1)}, u32[]{:S(2)}, u32[]{:S(2)}) collective-permute-start(f32[4,32,128]{2,1,0:T(8,128)S(1)} %get-tuple-element.30.refs_6_), channel_id=1, source_target_pairs={{0,24},{4,28},{8,16},{12,20},{16,8},{20,12},{24,0},{28,4},{1,25},{... | collective-permute-start | bytes 196616 | tf_op jit(solution)/shard_map/ppermute | solution.py:465
  36.5 5.8 %collective-permute-start.9 = (f32[4,32,128]{2,1,0:T(8,128)S(1)}, f32[4,32,128]{2,1,0:T(8,128)S(1)}, u32[]{:S(2)}, u32[]{:S(2)}) collective-permute-start(f32[4,32,128]{2,1,0:T(8,128)S(1)} %get-tuple-element.30.refs_6_), channel_id=1, source_target_pairs={{0,16},{4,20},{8,24},{12,28},{16,0},{20,4},{24,8},{28,12},{1,17},{... | collective-permute-start | bytes 196616 | tf_op jit(solution)/shard_map/ppermute | solution.py:465
  36.7 5.6 %collective-permute-start.8 = (f32[4,32,128]{2,1,0:T(8,128)S(1)}, f32[4,32,128]{2,1,0:T(8,128)S(1)}, u32[]{:S(2)}, u32[]{:S(2)}) collective-permute-start(f32[4,32,128]{2,1,0:T(8,128)S(1)} %get-tuple-element.30.refs_6_), channel_id=1, source_target_pairs={{0,8},{4,12},{8,0},{12,4},{16,24},{20,28},{24,16},{28,20},{1,9},{5... | collective-permute-start | bytes 196616 | tf_op jit(solution)/shard_map/ppermute | solution.py:465
  45.3 3.7 %collective-permute-start.11 = (f32[136,128]{1,0:T(8,128)S(1)}, f32[136,128]{1,0:T(8,128)S(1)}, u32[]{:S(2)}, u32[]{:S(2)}) collective-permute-start(f32[136,128]{1,0:T(8,128)S(1)} %get-tuple-element.32), channel_id=1, source_target_pairs={{0,1},{1,0},{2,3},{3,2},{4,5},{5,4},{6,7},{7,6},{8,9},{9,8},{10,11... | collective-permute-start | bytes 208904 | tf_op jit(solution)/shard_map/ppermute | solution.py:442
  45.4 5.7 %collective-permute-start.12 = (f32[136,128]{1,0:T(8,128)S(1)}, f32[136,128]{1,0:T(8,128)S(1)}, u32[]{:S(2)}, u32[]{:S(2)}) collective-permute-start(f32[136,128]{1,0:T(8,128)S(1)} %get-tuple-element.33), channel_id=1, source_target_pairs={{0,2},{1,3},{2,0},{3,1},{4,6},{5,7},{6,4},{7,5},{8,10},{9,11},{10,... | collective-permute-start | bytes 208904 | tf_op jit(solution)/shard_map/ppermute | solution.py:442
  46.5 5.1 %collective-permute-start.13 = (f32[136,128]{1,0:T(8,128)S(1)}, f32[136,128]{1,0:T(8,128)S(1)}, u32[]{:S(2)}, u32[]{:S(2)}) collective-permute-start(f32[136,128]{1,0:T(8,128)S(1)} %get-tuple-element.34), channel_id=1, source_target_pairs={{0,3},{1,2},{2,1},{3,0},{4,7},{5,6},{6,5},{7,4},{8,11},{9,10},{10,... | collective-permute-start | bytes 208904 | tf_op jit(solution)/shard_map/ppermute | solution.py:442
  47.3 4.4 %collective-permute-start.14 = (f32[136,128]{1,0:T(8,128)S(1)}, f32[136,128]{1,0:T(8,128)S(1)}, u32[]{:S(2)}, u32[]{:S(2)}) collective-permute-start(f32[136,128]{1,0:T(8,128)S(1)} %get-tuple-element.35), channel_id=1, source_target_pairs={{0,4},{1,5},{2,6},{3,7},{4,0},{5,1},{6,2},{7,3},{8,12},{9,13},{10,... | collective-permute-start | bytes 208904 | tf_op jit(solution)/shard_map/ppermute | solution.py:442
  49.0 4.3 %collective-permute-start.15 = (f32[136,128]{1,0:T(8,128)S(1)}, f32[136,128]{1,0:T(8,128)S(1)}, u32[]{:S(2)}, u32[]{:S(2)}) collective-permute-start(f32[136,128]{1,0:T(8,128)S(1)} %get-tuple-element.36), channel_id=1, source_target_pairs={{0,5},{1,4},{2,7},{3,6},{4,1},{5,0},{6,3},{7,2},{8,13},{9,12},{10,... | collective-permute-start | bytes 208904 | tf_op jit(solution)/shard_map/ppermute | solution.py:442
  49.0 6.6 %collective-permute-start.16 = (f32[136,128]{1,0:T(8,128)S(1)}, f32[136,128]{1,0:T(8,128)S(1)}, u32[]{:S(2)}, u32[]{:S(2)}) collective-permute-start(f32[136,128]{1,0:T(8,128)S(1)} %get-tuple-element.37), channel_id=1, source_target_pairs={{0,6},{1,7},{2,4},{3,5},{4,2},{5,3},{6,0},{7,1},{8,14},{9,15},{10,... | collective-permute-start | bytes 208904 | tf_op jit(solution)/shard_map/ppermute | solution.py:442
  51.2 5.5 %collective-permute-start.17 = (f32[136,128]{1,0:T(8,128)S(1)}, f32[136,128]{1,0:T(8,128)S(1)}, u32[]{:S(2)}, u32[]{:S(2)}) collective-permute-start(f32[136,128]{1,0:T(8,128)S(1)} %get-tuple-element.38), channel_id=1, source_target_pairs={{0,7},{1,6},{2,5},{3,4},{4,3},{5,2},{6,1},{7,0},{8,15},{9,14},{10,... | collective-permute-start | bytes 208904 | tf_op jit(solution)/shard_map/ppermute | solution.py:442
  56.7 5.8 %collective-permute-start.20 = (f32[8,128]{1,0:T(8,128)S(1)}, f32[8,128]{1,0:T(8,128)S(1)}, u32[]{:S(2)}, u32[]{:S(2)}) collective-permute-start(f32[8,128]{1,0:T(8,128)S(1)} %squares.1), channel_id=1, source_target_pairs={{0,24},{4,28},{8,16},{12,20},{16,8},{20,12},{24,0},{28,4},{1,25},{... | collective-permute-start | bytes 12296 | tf_op jit(solution)/shard_map/ppermute | solution.py:465
  59.3 4.5 %collective-permute-start.19 = (f32[8,128]{1,0:T(8,128)S(1)}, f32[8,128]{1,0:T(8,128)S(1)}, u32[]{:S(2)}, u32[]{:S(2)}) collective-permute-start(f32[8,128]{1,0:T(8,128)S(1)} %squares.1), channel_id=1, source_target_pairs={{0,16},{4,20},{8,24},{12,28},{16,0},{20,4},{24,8},{28,12},{1,17},{... | collective-permute-start | bytes 12296 | tf_op jit(solution)/shard_map/ppermute | solution.py:465
  59.3 4.5 %collective-permute-start.18 = (f32[8,128]{1,0:T(8,128)S(1)}, f32[8,128]{1,0:T(8,128)S(1)}, u32[]{:S(2)}, u32[]{:S(2)}) collective-permute-start(f32[8,128]{1,0:T(8,128)S(1)} %squares.1), channel_id=1, source_target_pairs={{0,8},{4,12},{8,0},{12,4},{16,24},{20,28},{24,16},{28,20},{1,9},{5... | collective-permute-start | bytes 12296 | tf_op jit(solution)/shard_map/ppermute | solution.py:465
  (3 other events, 2.0 us)

commit v6 on v4

--- a/solution.py
+++ b/solution.py
@@ -135,13 +135,14 @@
 
 
 class Level:
-    def __init__(self, index, ny, nz, rim, velocity_ref, shift, f, r, w):
+    def __init__(self, index, ny, nz, rim, scalar_ref, f, r, w):
         self.ny, self.nz, self.rim = ny, nz, rim
         self.f, self.r, self.w = f, r, w
         spacing = 2.0**index
         scale_a = 1.0 / (spacing * spacing)
         inverse = 1.0 / spacing
-        speed = [velocity_ref[d] for d in range(3)]
+        shift = scalar_ref[0, 0]
+        speed = [scalar_ref[1 + d, 0] for d in range(3)]
         self.backward = [scale_a + jnp.maximum(v, 0.0) * inverse for v in speed]
         self.forward = [scale_a - jnp.minimum(v, 0.0) * inverse for v in speed]
         total = jnp.abs(speed[0]) + jnp.abs(speed[1]) + jnp.abs(speed[2])
@@ -231,32 +232,35 @@
     return jnp.where(col // 2 == row, 1.0, 0.0).astype(jnp.bfloat16)
 
 
-def pack_kernel(place_ref, source_ref, reaction_ref, *out_refs):
+def pack_kernel(first, place_ref, source_ref, reaction_ref, *out_refs):
     for k, out_ref in enumerate(out_refs):
-        out_ref[0] = source_ref[jnp.bitwise_xor(place_ref[0], k)]
+        out_ref[0] = source_ref[jnp.bitwise_xor(place_ref[0], first + k)]
         out_ref[1] = reaction_ref[...]
 
 
-def arrange_kernel(gy_size, place_ref, *refs):
-    pieces, (low_ref, high_ref, both) = refs[:-3], refs[-3:]
-    _, bx, by, _ = pieces[0].shape
-    for k, piece in enumerate(pieces):
-        owner = jnp.bitwise_xor(place_ref[0], k)
-        planes = pl.ds((owner // gy_size) * bx, bx)
+def pack_rest_kernel(first, place_ref, shifts_ref, index_ref, velocity_ref, source_ref, reaction_ref, _, *refs):
+    pack_kernel(first, place_ref, source_ref, reaction_ref, *refs[:-1])
+    scalars = [shifts_ref[index_ref[place_ref[0]]]] + [velocity_ref[d] for d in range(3)]
+    for n, scalar in enumerate(scalars):
+        refs[-1][pl.ds(n, 1), :] = jnp.full((1, LANES), scalar, jnp.float32)
+
+
+def arrange_kernel(gy_size, first, place_ref, *refs):
+    half_ref = refs[-1]
+    for k, piece in enumerate(refs[:-1]):
+        owner = jnp.bitwise_xor(place_ref[0], first + k)
+        by = piece.shape[2]
         rows = pl.ds(pl.multiple_of(lax.rem(owner, gy_size) * by, 8), by)
-        both[:, planes, rows, :] = piece[...]
-    low_ref[...] = both[:, pl.ds(0, HALO)]
-    high_ref[...] = both[:, pl.ds(HALO, HALO)]
-
-
-def pre_kernel(slabs, place_ref, shifts_ref, index_ref, velocity_ref, *refs):
+        half_ref[:, :, rows, :] = piece[...]
+
+
+def pre_kernel(slabs, gy_size, place_ref, scalar_ref, *refs):
     pool_ref, pool_up_ref = refs[:2]
     parts = refs[2:6]
     f, r, w, v1, coarse_ref, v0, tmp, pooled = refs[6:]
     ny = f.shape[1]
     slab = place_ref[1]
-    shift = shifts_ref[index_ref[place_ref[0]]]
-    fine = Level(0, ny, LANES, 0, velocity_ref, shift, f, r, w)
+    fine = Level(0, ny, LANES, 0, scalar_ref, f, r, w)
     zero_rows(v0, ny)
     zero_rows(v1, ny)
     count = SLAB + 2 * HALO
@@ -264,17 +268,17 @@
     inside += [DAMPING] * SLAB
     inside += [jnp.where(slab < slabs - 1, DAMPING, 0.0)] * HALO
 
-    def begin(x):
-        part, at = parts[x // HALO], x % HALO
-        return part[0, at], part[1, at]
-
-    def put(x, pair):
-        f[x], r[x] = pair
-        weight = inside[x] / (pair[1] + fine.centre)
+    x = place_ref[0] // gy_size
+    firsts = (HALO * (1 + x), HALO * (2 - x), (HALO + SLAB) * (1 - x), (HALO + SLAB) * x)
+    for part, first in zip(parts, firsts):
+        f[pl.ds(first, HALO)] = part[0]
+        r[pl.ds(first, HALO)] = part[1]
+
+    def put(x, weight):
         w[x] = weight
-        v0[x, pl.ds(8, ny), :] = weight * pair[0]
-
-    sweep(range(count), begin, put)
+        v0[x, pl.ds(8, ny), :] = weight * f[x]
+
+    sweep(range(count), lambda x: inside[x] / (r[x] + fine.centre), put)
     fine.smooth(v0, v1, range(1, count - 1))
     half = ny // 2
 
@@ -291,7 +295,7 @@
     coarse_ref[...] = packed.reshape(coarse_ref.shape)
 
 
-def post_kernel(grid, gy_size, bx, by, place_ref, shifts_ref, index_ref, velocity_ref, *refs):
+def post_kernel(grid, gy_size, bx, by, place_ref, scalar_ref, *refs):
     slabs, nx, ny, nz = grid
     pool_ref, spread_ref, f, r, w, v1 = refs[:6]
     coarse = refs[6 : 6 + slabs]
@@ -300,12 +304,11 @@
     va, vb, f1, r1, w1, v1a, v1b, pooled, tmp = refs[6 + slabs + columns :]
     pool, spread = pool_ref[...], spread_ref[...]
     slab = place_ref[1]
-    shift = shifts_ref[index_ref[place_ref[0]]]
     rim = HALO // 2
     nx1, ny1, nx2, ny2 = nx // 2, ny // 2, nx // 4, ny // 4
-    fine = Level(0, ny, nz, 0, velocity_ref, shift, f, r, w)
-    mid = Level(1, ny1, nz // 2, rim, velocity_ref, shift, f1, r1, w1)
-    deep = Level(2, ny2, nz // 4, 0, velocity_ref, shift, None, None, None)
+    fine = Level(0, ny, nz, 0, scalar_ref, f, r, w)
+    mid = Level(1, ny1, nz // 2, rim, scalar_ref, f1, r1, w1)
+    deep = Level(2, ny2, nz // 4, 0, scalar_ref, None, None, None)
     for v in (va, vb):
         zero_rows(v, ny)
     for v in (v1a, v1b):
@@ -400,6 +403,11 @@
         residual_ref[column] = part[pl.ds(area, area), :].reshape(bx, by, LANES)
 
 
+def squares_kernel(row, *refs):
+    for k, part in enumerate(refs[:-1]):
+        refs[-1][pl.ds(k, 1), :] = part[pl.ds(row, 1), :]
+
+
 SMEM = pl.BlockSpec(memory_space=pltpu.SMEM)
 VMEM = pl.BlockSpec(memory_space=pltpu.VMEM)
 
@@ -416,12 +424,12 @@
     )(*scalars, *arrays)
 
 
-def swap_in_plane(pieces, columns):
+def swap_in_plane(pieces, first):
     devices = lax.axis_size("gx") * lax.axis_size("gy")
-    moved = [pieces[0]]
-    for k in range(1, columns):
+    moved = []
+    for k, piece in enumerate(pieces, first):
         pairs = [(i, i ^ k) for i in range(devices)]
-        moved.append(lax.ppermute(pieces[k], ("gx", "gy"), pairs))
+        moved.append(lax.ppermute(piece, ("gx", "gy"), pairs) if k else piece)
     return moved
 
 
@@ -443,31 +451,47 @@
     along, across = lax.axis_index("gx"), lax.axis_index("gy")
     column = lax.rem(along, step) * gy_size + across
     place = jnp.stack([column, along // step]).astype(jnp.int32)
-    scalars = (place, shifts, shift_index, velocity)
     count = SLAB + 2 * HALO
     area = bx * by
 
+    piece = (2, bx, by, nz)
     pieces = local_kernel(
-        pack_kernel, "pack", (place,), (source, reaction), [(2, bx, by, nz)] * columns
-    )
-    pieces = swap_in_plane(pieces, columns)
-    low, high = local_kernel(
-        functools.partial(arrange_kernel, gy_size),
-        "arrange",
-        (place,),
-        pieces,
-        [(2, HALO, ny, nz)] * 2,
-        [(2, SLAB, ny, nz)],
-    )
-    before = lax.ppermute(high, "gx", [(i, i + step) for i in range(gx_size - step)])
-    after = lax.ppermute(low, "gx", [(i + step, i) for i in range(gx_size - step)])
+        functools.partial(pack_kernel, 0), "pack", (place,), (source, reaction), [piece] * gy_size
+    )
+    pieces = swap_in_plane(pieces, 0)
+    *rest, scalar_rows = local_kernel(
+        functools.partial(pack_rest_kernel, gy_size),
+        "pack_rest",
+        (place, shifts, shift_index, velocity),
+        (source, reaction, pieces[1]),
+        [piece] * gy_size + [(8, LANES)],
+    )
+    scalars = (place, scalar_rows)
+    pieces = pieces + swap_in_plane(rest, gy_size)
+    halves, beside = [], []
+    for n in range(2):
+        first = n * gy_size
+        (half,) = local_kernel(
+            functools.partial(arrange_kernel, gy_size, first),
+            "arrange",
+            (place,),
+            pieces[first : first + gy_size],
+            [(2, HALO, ny, nz)],
+        )
+        pairs = []
+        for i in range(gx_size):
+            target = i + step if i % step != n else i - step
+            if 0 <= target < gx_size:
+                pairs.append((i, target))
+        halves.append(half)
+        beside.append(lax.ppermute(half, "gx", pairs))
 
     grid, rimmed = (count, ny, nz), (count, ny + 16, nz)
     f, r, w, v1, coarse = local_kernel(
-        functools.partial(pre_kernel, slabs),
+        functools.partial(pre_kernel, slabs, gy_size),
         "pre",
         scalars,
-        (pool_matrix(0), pool_matrix(LANES // 2), before, low, high, after),
+        (pool_matrix(0), pool_matrix(LANES // 2), *halves, *beside),
         [grid, grid, grid, rimmed, (SLAB // 2, ny // 2, nz)],
         [rimmed, (SLAB, ny, nz), (2, SLAB // 2 * ny // 2, nz)],
     )
@@ -484,11 +508,13 @@
         [(2 * area + 8, nz)] * columns,
         [rimmed] * 2 + [coarse_grid] * 3 + [coarse_rimmed] * 2 + [(rows, nz), (nx // 2, ny, nz)],
     )
-    parts = swap_in_plane(results, columns)
-
-    squares = jnp.stack([part[2 * area, 0] for part in parts])
+    parts = swap_in_plane(results, 0)
+
+    (squares,) = local_kernel(
+        functools.partial(squares_kernel, 2 * area), "squares", (), parts, [(columns, nz)]
+    )
     total = sum(swap_slabs(squares, step, slabs))
-    rms = jnp.sqrt(total / (nx * ny * nz) + EPSILON)
+    rms = jnp.sqrt(total[:, 0] / (nx * ny * nz) + EPSILON)
     slots = jnp.arange(columns, dtype=jnp.int32)
     mine = jnp.bitwise_xor(slots, column)[None, :] == slots[:, None]
     residual_rms = jnp.sum(jnp.where(mine, rms[None, :], 0.0), axis=1)
@@ -509,7 +535,8 @@
     slabs, ny = gx_size // step, by * gy_size
     whole = power_of_two(columns) and power_of_two(step) and power_of_two(slabs)
     small = slabs * ny * nz <= 2**15
-    return whole and small and bx * step == SLAB and nz == LANES and by % 16 == 0
+    paired = step == 2 and bx == HALO
+    return whole and small and paired and bx * step == SLAB and nz == LANES and by % 16 == 0
 
 
 def solution(mesh):

time: 67.3 us -> 59.3 us (0.88)
  local copies, waits for them, and re-layouts: 11.6 us -> 1.62 us
  Pallas kernels: 6.83 us -> 8.21 us
    another operation x1 -> x0, local copies, waits for them, and re-layouts: 5.07 us -> none  [column_body(): squares = jnp.stack([part[2 * area, 0] for part in parts])]
    slice x8 -> x0, local copies, waits for them, and re-layouts: 4.26 us -> none  [column_body(): squares = jnp.stack([part[2 * area, 0] for part in parts])]
    pallas_call x5 -> x8, Pallas kernels: 6.83 us -> 8.21 us  [local_kernel(): pl.pallas_call(kernel, out_shape=[jax.ShapeDtypeStruct(shape, jnp.float32...]
    ppermute x6, starting transfers between devices: 8.84 us -> 9.6 us  [swap_slabs(): moved.append(lax.ppermute(piece, 'gx', pairs))]
    ppermute x6, waiting for transfers between devices: 5.15 us -> 5.88 us  [swap_slabs(): moved.append(lax.ppermute(piece, 'gx', pairs))]
    unnamed x10, local copies, waits for them, and re-layouts: 2.29 us -> 1.62 us
  transfers between devices with their start and end apart: 22 -> 22, of which waited for: 10 -> 12; matrix products, arithmetic and copies ran while one was open for 6% -> 0% of each run, Pallas kernels for 2% -> 5%
where the time goes in v6:
time: 59.3 us; the launch traced here: 59.1 us
  starting transfers between devices  28 us (47%)
  waiting for transfers between devices  19.5 us (33%)
  Pallas kernels  8.21 us (14%)
  local copies, waits for them, and re-layouts  1.62 us (3%)
  other arithmetic  0.97 us (2%)
  between operations  0.79 us (1%)
    ppermute x14, starting transfers between devices, swap_in_plane(): moved.append(lax.ppermute(piece, ('gx', 'gy'), pairs) if k else piece)  13.7 us
    ppermute x6, starting transfers between devices, swap_slabs(): moved.append(lax.ppermute(piece, 'gx', pairs))  9.6 us
    pallas_call x8, Pallas kernels, local_kernel(): pl.pallas_call(kernel, out_shape=[jax.ShapeDtypeStruct(shape, jnp.float32...  8.21 us
    ppermute x14, waiting for transfers between devices, swap_in_plane(): moved.append(lax.ppermute(piece, ('gx', 'gy'), pairs) if k else piece)  7.91 us
    ppermute x6, waiting for transfers between devices, swap_slabs(): moved.append(lax.ppermute(piece, 'gx', pairs))  5.88 us
    ppermute x2, waiting for transfers between devices, column_body(): beside.append(lax.ppermute(half, 'gx', pairs))  5.67 us
    ppermute x2, starting transfers between devices, column_body(): beside.append(lax.ppermute(half, 'gx', pairs))  4.79 us
    unnamed x10, local copies, waits for them, and re-layouts  1.62 us
  transfers between devices with their start and end apart: 22, of which 12 were waited for; matrix products, arithmetic and copies ran while one was open for 0% of the time, Pallas kernels for 5%

profile of v6, /device:TPU:0, one launch (start us, length us, event | category | flops | bytes accessed | tf_op | source)
XLA Modules:
  0.0 59.1 jit_solution(9194983045391814645)
XLA Ops:
  3.4 2.6 %collective-permute-start.1 = (f32[2,4,16,128]{3,2,1,0:T(8,128)S(1)}, f32[2,4,16,128]{3,2,1,0:T(8,128)S(1)}, u32[]{:S(2)}, u32[]{:S(2)}) collective-permute-start(f32[2,4,16,128]{3,2,1,0:T(8,128)S(1)} %get-tuple-element.30), channel_id=1, source_target_pairs={{0,2},{1,3},{2,0},{3,1},{4,6},{5,7},{6,4},{7,5},{8,10},{9,11},{10,... | collective-permute-start | bytes 196616 | tf_op jit(solution)/shard_map/ppermute | solution.py:432
  6.8 1.7 %collective-permute-start.3 = (f32[2,4,16,128]{3,2,1,0:T(8,128)S(1)}, f32[2,4,16,128]{3,2,1,0:T(8,128)S(1)}, u32[]{:S(2)}, u32[]{:S(2)}) collective-permute-start(f32[2,4,16,128]{3,2,1,0:T(8,128)S(1)} %get-tuple-element.32), channel_id=1, source_target_pairs={{0,4},{1,5},{2,6},{3,7},{4,0},{5,1},{6,2},{7,3},{8,12},{9,13},{10,... | collective-permute-start | bytes 196616 | tf_op jit(solution)/shard_map/ppermute | solution.py:432
  8.5 2.6 %collective-permute-start.5 = (f32[2,4,16,128]{3,2,1,0:T(8,128)S(1)}, f32[2,4,16,128]{3,2,1,0:T(8,128)S(1)}, u32[]{:S(2)}, u32[]{:S(2)}) collective-permute-start(f32[2,4,16,128]{3,2,1,0:T(8,128)S(1)} %get-tuple-element.34), channel_id=1, source_target_pairs={{0,6},{1,7},{2,4},{3,5},{4,2},{5,3},{6,0},{7,1},{8,14},{9,15},{10,... | collective-permute-start | bytes 196616 | tf_op jit(solution)/shard_map/ppermute | solution.py:432
  11.8 1.3 %collective-permute-start.7 = (f32[2,4,64,128]{3,2,1,0:T(8,128)S(1)}, f32[2,4,64,128]{3,2,1,0:T(8,128)S(1)}, u32[]{:S(2)}, u32[]{:S(2)}) collective-permute-start(f32[2,4,64,128]{3,2,1,0:T(8,128)S(1)} %arrange.2.refs_2_), channel_id=1, source_target_pairs={{4,12},{8,0},{12,20},{16,8},{20,28},{24,16},{5,13},{9,1},{13,21},{... | collective-permute-start | bytes 786440 | tf_op jit(solution)/shard_map/ppermute | solution.py:487
  13.1 2.2 %collective-permute-done.5.refs_2_ = f32[2,4,16,128]{3,2,1,0:T(8,128)S(1)} collective-permute-done((f32[2,4,16,128]{3,2,1,0:T(8,128)S(1)}, f32[2,4,16,128]{3,2,1,0:T(8,128)S(1)}, u32[]{:S(2)}, u32[]{:S(2)}) %collective-permute-start.5) | collective-permute-done | bytes 65568 | tf_op jit(solution)/shard_map/ppermute | solution.py:432
  15.4 1.1 %collective-permute-done.6.refs_3_ = f32[2,4,16,128]{3,2,1,0:T(8,128)S(1)} collective-permute-done((f32[2,4,16,128]{3,2,1,0:T(8,128)S(1)}, f32[2,4,16,128]{3,2,1,0:T(8,128)S(1)}, u32[]{:S(2)}, u32[]{:S(2)}) %collective-permute-start.6) | collective-permute-done | bytes 65568 | tf_op jit(solution)/shard_map/ppermute | solution.py:432
  17.1 3.5 %collective-permute-start.8 = (f32[2,4,64,128]{3,2,1,0:T(8,128)S(1)}, f32[2,4,64,128]{3,2,1,0:T(8,128)S(1)}, u32[]{:S(2)}, u32[]{:S(2)}) collective-permute-start(f32[2,4,64,128]{3,2,1,0:T(8,128)S(1)} %arrange.3.refs_3_), channel_id=1, source_target_pairs={{0,8},{8,16},{12,4},{16,24},{20,12},{28,20},{1,9},{9,17},{13,5},{1... | collective-permute-start | bytes 786440 | tf_op jit(solution)/shard_map/ppermute | solution.py:487
  20.7 2.0 %collective-permute-done.7.refs_4_ = f32[2,4,64,128]{3,2,1,0:T(8,128)S(1)} collective-permute-done((f32[2,4,64,128]{3,2,1,0:T(8,128)S(1)}, f32[2,4,64,128]{3,2,1,0:T(8,128)S(1)}, u32[]{:S(2)}, u32[]{:S(2)}) %collective-permute-start.7) | collective-permute-done | bytes 262176 | tf_op jit(solution)/shard_map/ppermute | solution.py:487
  22.7 3.7 %collective-permute-done.8.refs_5_ = f32[2,4,64,128]{3,2,1,0:T(8,128)S(1)} collective-permute-done((f32[2,4,64,128]{3,2,1,0:T(8,128)S(1)}, f32[2,4,64,128]{3,2,1,0:T(8,128)S(1)}, u32[]{:S(2)}, u32[]{:S(2)}) %collective-permute-start.8) | collective-permute-done | bytes 262176 | tf_op jit(solution)/shard_map/ppermute | solution.py:487
  26.4 1.4 %pre.1 = (f32[16,64,128]{2,1,0:T(8,128)S(1)}, f32[16,64,128]{2,1,0:T(8,128)S(1)}, f32[16,64,128]{2,1,0:T(8,128)S(1)}, f32[16,80,128]{2,1,0:T(8,128)S(1)}, f32[4,32,128]{2,1,0:T(8,128)S(1)}) custom-call(s32[2]{0:T(128)S(1)} %pad_add_fusion.place_ref, f32[8,128]{1,0:T(8,128)S(1)} %get-tuple-element.28.scalar_ref, ...), custom_call_target="tpu_custom_call" | custom-call | tf_op jit(solution)/shard_map/pre/pallas_call | solution.py:416
  27.8 4.6 %collective-permute-start.11 = (f32[4,32,128]{2,1,0:T(8,128)S(1)}, f32[4,32,128]{2,1,0:T(8,128)S(1)}, u32[]{:S(2)}, u32[]{:S(2)}) collective-permute-start(f32[4,32,128]{2,1,0:T(8,128)S(1)} %get-tuple-element.40.refs_6_), channel_id=1, source_target_pairs={{0,24},{4,28},{8,16},{12,20},{16,8},{20,12},{24,0},{28,4},{1,25},{... | collective-permute-start | bytes 196616 | tf_op jit(solution)/shard_map/ppermute | solution.py:441
  33.0 2.4 %collective-permute-done.11.refs_9_ = f32[4,32,128]{2,1,0:T(8,128)S(1)} collective-permute-done((f32[4,32,128]{2,1,0:T(8,128)S(1)}, f32[4,32,128]{2,1,0:T(8,128)S(1)}, u32[]{:S(2)}, u32[]{:S(2)}) %collective-permute-start.11) | collective-permute-done | bytes 65568 | tf_op jit(solution)/shard_map/ppermute | solution.py:441
  35.4 2.2 %collective-permute-done.10.refs_8_ = f32[4,32,128]{2,1,0:T(8,128)S(1)} collective-permute-done((f32[4,32,128]{2,1,0:T(8,128)S(1)}, f32[4,32,128]{2,1,0:T(8,128)S(1)}, u32[]{:S(2)}, u32[]{:S(2)}) %collective-permute-start.10) | collective-permute-done | bytes 65568 | tf_op jit(solution)/shard_map/ppermute | solution.py:441
  37.6 3.2 %post.1 = (f32[136,128]{1,0:T(8,128)S(1)}, f32[136,128]{1,0:T(8,128)S(1)}, f32[136,128]{1,0:T(8,128)S(1)}, f32[136,128]{1,0:T(8,128)S(1)}, f32[136,128]{1,0:T(8,...) custom-call(s32[2]{0:T(128)S(1)} %pad_add_fusion.place_ref, ...), custom_call_target="tpu_custom_call" | custom-call | tf_op jit(solution)/shard_map/post/pallas_call | solution.py:416
  41.4 1.4 %collective-permute-start.14 = (f32[136,128]{1,0:T(8,128)S(1)}, f32[136,128]{1,0:T(8,128)S(1)}, u32[]{:S(2)}, u32[]{:S(2)}) collective-permute-start(f32[136,128]{1,0:T(8,128)S(1)} %get-tuple-element.44), channel_id=1, source_target_pairs={{0,3},{1,2},{2,1},{3,0},{4,7},{5,6},{6,5},{7,4},{8,11},{9,10},{10,... | collective-permute-start | bytes 208904 | tf_op jit(solution)/shard_map/ppermute | solution.py:432
  42.7 1.2 %collective-permute-start.15 = (f32[136,128]{1,0:T(8,128)S(1)}, f32[136,128]{1,0:T(8,128)S(1)}, u32[]{:S(2)}, u32[]{:S(2)}) collective-permute-start(f32[136,128]{1,0:T(8,128)S(1)} %get-tuple-element.45), channel_id=1, source_target_pairs={{0,4},{1,5},{2,6},{3,7},{4,0},{5,1},{6,2},{7,3},{8,12},{9,13},{10,... | collective-permute-start | bytes 208904 | tf_op jit(solution)/shard_map/ppermute | solution.py:432
  44.4 1.1 %collective-permute-start.17 = (f32[136,128]{1,0:T(8,128)S(1)}, f32[136,128]{1,0:T(8,128)S(1)}, u32[]{:S(2)}, u32[]{:S(2)}) collective-permute-start(f32[136,128]{1,0:T(8,128)S(1)} %get-tuple-element.47), channel_id=1, source_target_pairs={{0,6},{1,7},{2,4},{3,5},{4,2},{5,3},{6,0},{7,1},{8,14},{9,15},{10,... | collective-permute-start | bytes 208904 | tf_op jit(solution)/shard_map/ppermute | solution.py:432
  45.9 1.2 %collective-permute-start.18 = (f32[136,128]{1,0:T(8,128)S(1)}, f32[136,128]{1,0:T(8,128)S(1)}, u32[]{:S(2)}, u32[]{:S(2)}) collective-permute-start(f32[136,128]{1,0:T(8,128)S(1)} %get-tuple-element.48), channel_id=1, source_target_pairs={{0,7},{1,6},{2,5},{3,4},{4,3},{5,2},{6,1},{7,0},{8,15},{9,14},{10,... | collective-permute-start | bytes 208904 | tf_op jit(solution)/shard_map/ppermute | solution.py:432
  48.4 1.8 %collective-permute-done.17.refs_6_ = f32[136,128]{1,0:T(8,128)S(1)} collective-permute-done((f32[136,128]{1,0:T(8,128)S(1)}, f32[136,128]{1,0:T(8,128)S(1)}, u32[]{:S(2)}, u32[]{:S(2)}) %collective-permute-start.17) | collective-permute-done | bytes 69664 | tf_op jit(solution)/shard_map/ppermute | solution.py:432
  50.2 1.1 %collective-permute-done.18.refs_7_ = f32[136,128]{1,0:T(8,128)S(1)} collective-permute-done((f32[136,128]{1,0:T(8,128)S(1)}, f32[136,128]{1,0:T(8,128)S(1)}, u32[]{:S(2)}, u32[]{:S(2)}) %collective-permute-start.18) | collective-permute-done | bytes 69664 | tf_op jit(solution)/shard_map/ppermute | solution.py:432
  51.3 2.5 %collective-permute-start.21 = (f32[8,128]{1,0:T(8,128)S(1)}, f32[8,128]{1,0:T(8,128)S(1)}, u32[]{:S(2)}, u32[]{:S(2)}) collective-permute-start(f32[8,128]{1,0:T(8,128)S(1)} %squares.1), channel_id=1, source_target_pairs={{0,24},{4,28},{8,16},{12,20},{16,8},{20,12},{24,0},{28,4},{1,25},{... | collective-permute-start | bytes 12296 | tf_op jit(solution)/shard_map/ppermute | solution.py:441
  53.8 1.9 %collective-permute-start.19 = (f32[8,128]{1,0:T(8,128)S(1)}, f32[8,128]{1,0:T(8,128)S(1)}, u32[]{:S(2)}, u32[]{:S(2)}) collective-permute-start(f32[8,128]{1,0:T(8,128)S(1)} %squares.1), channel_id=1, source_target_pairs={{0,8},{4,12},{8,0},{12,4},{16,24},{20,28},{24,16},{28,20},{1,9},{5... | collective-permute-start | bytes 12296 | tf_op jit(solution)/shard_map/ppermute | solution.py:441
  55.7 1.4 %collect.1 = (f32[8,4,16,128]{3,2,1,0:T(8,128)}, f32[8,4,16,128]{3,2,1,0:T(8,128)}) custom-call(s32[2]{0:T(128)S(1)} %pad_add_fusion.place_ref, f32[136,128]{1,0:T(8,128)S(1)} %get-tuple-element.41.refs_0_, f32[136,128]{1,0:T(8,128)S(1)} %collective-permute-done.12.refs_1_, f32[136,128]{1,0:T(8,128)S(1)} %collective-permute-done.13.refs_2_, ...), custom_call_target="tpu_custom_call" | custom-call | tf_op jit(solution)/shard_map/collect/pallas_call | solution.py:416
  57.1 1.3 %collective-permute-done.20 = f32[8,128]{1,0:T(8,128)S(1)} collective-permute-done((f32[8,128]{1,0:T(8,128)S(1)}, f32[8,128]{1,0:T(8,128)S(1)}, u32[]{:S(2)}, u32[]{:S(2)}) %collective-permute-start.20) | collective-permute-done | bytes 4128 | tf_op jit(solution)/shard_map/ppermute | solution.py:441
  (46 shorter events, 8.9 us)
Async XLA Ops:
  2.9 3.3 %collective-permute-start = (f32[2,4,16,128]{3,2,1,0:T(8,128)S(1)}, f32[2,4,16,128]{3,2,1,0:T(8,128)S(1)}, u32[]{:S(2)}, u32[]{:S(2)}) collective-permute-start(f32[2,4,16,128]{3,2,1,0:T(8,128)S(1)} %get-tuple-element.27), channel_id=1, source_target_pairs={{0,1},{1,0},{2,3},{3,2},{4,5},{5,4},{6,7},{7,6},{8,9},{9,8},{10,11... | collective-permute-start | bytes 196616 | tf_op jit(solution)/shard_map/ppermute | solution.py:432
  3.4 2.7 %copy-start.3 = (s32[8]{0:T(128)S(1)}, s32[8]{0:T(128)}, u32[]{:S(2)}) copy-start(s32[8]{0:T(128)} %index_ref.1) | copy-start | bytes 100
  3.4 2.8 %copy-start.4 = (f32[3]{0:T(128)S(1)}, f32[3]{0:T(128)}, u32[]{:S(2)}) copy-start(f32[3]{0:T(128)} %velocity_ref.1) | copy-start | bytes 40
  3.4 7.7 %collective-permute-start.1 = (f32[2,4,16,128]{3,2,1,0:T(8,128)S(1)}, f32[2,4,16,128]{3,2,1,0:T(8,128)S(1)}, u32[]{:S(2)}, u32[]{:S(2)}) collective-permute-start(f32[2,4,16,128]{3,2,1,0:T(8,128)S(1)} %get-tuple-element.30), channel_id=1, source_target_pairs={{0,2},{1,3},{2,0},{3,1},{4,6},{5,7},{6,4},{7,5},{8,10},{9,11},{10,... | collective-permute-start | bytes 196616 | tf_op jit(solution)/shard_map/ppermute | solution.py:432
  6.1 5.2 %collective-permute-start.2 = (f32[2,4,16,128]{3,2,1,0:T(8,128)S(1)}, f32[2,4,16,128]{3,2,1,0:T(8,128)S(1)}, u32[]{:S(2)}, u32[]{:S(2)}) collective-permute-start(f32[2,4,16,128]{3,2,1,0:T(8,128)S(1)} %get-tuple-element.31), channel_id=1, source_target_pairs={{0,3},{1,2},{2,1},{3,0},{4,7},{5,6},{6,5},{7,4},{8,11},{9,10},{10,... | collective-permute-start | bytes 196616 | tf_op jit(solution)/shard_map/ppermute | solution.py:432
  6.8 6.3 %collective-permute-start.3 = (f32[2,4,16,128]{3,2,1,0:T(8,128)S(1)}, f32[2,4,16,128]{3,2,1,0:T(8,128)S(1)}, u32[]{:S(2)}, u32[]{:S(2)}) collective-permute-start(f32[2,4,16,128]{3,2,1,0:T(8,128)S(1)} %get-tuple-element.32), channel_id=1, source_target_pairs={{0,4},{1,5},{2,6},{3,7},{4,0},{5,1},{6,2},{7,3},{8,12},{9,13},{10,... | collective-permute-start | bytes 196616 | tf_op jit(solution)/shard_map/ppermute | solution.py:432
  8.5 4.6 %collective-permute-start.4 = (f32[2,4,16,128]{3,2,1,0:T(8,128)S(1)}, f32[2,4,16,128]{3,2,1,0:T(8,128)S(1)}, u32[]{:S(2)}, u32[]{:S(2)}) collective-permute-start(f32[2,4,16,128]{3,2,1,0:T(8,128)S(1)} %get-tuple-element.33), channel_id=1, source_target_pairs={{0,5},{1,4},{2,7},{3,6},{4,1},{5,0},{6,3},{7,2},{8,13},{9,12},{10,... | collective-permute-start | bytes 196616 | tf_op jit(solution)/shard_map/ppermute | solution.py:432
  8.5 6.9 %collective-permute-start.5 = (f32[2,4,16,128]{3,2,1,0:T(8,128)S(1)}, f32[2,4,16,128]{3,2,1,0:T(8,128)S(1)}, u32[]{:S(2)}, u32[]{:S(2)}) collective-permute-start(f32[2,4,16,128]{3,2,1,0:T(8,128)S(1)} %get-tuple-element.34), channel_id=1, source_target_pairs={{0,6},{1,7},{2,4},{3,5},{4,2},{5,3},{6,0},{7,1},{8,14},{9,15},{10,... | collective-permute-start | bytes 196616 | tf_op jit(solution)/shard_map/ppermute | solution.py:432
  11.2 5.4 %collective-permute-start.6 = (f32[2,4,16,128]{3,2,1,0:T(8,128)S(1)}, f32[2,4,16,128]{3,2,1,0:T(8,128)S(1)}, u32[]{:S(2)}, u32[]{:S(2)}) collective-permute-start(f32[2,4,16,128]{3,2,1,0:T(8,128)S(1)} %get-tuple-element.35), channel_id=1, source_target_pairs={{0,7},{1,6},{2,5},{3,4},{4,3},{5,2},{6,1},{7,0},{8,15},{9,14},{10,... | collective-permute-start | bytes 196616 | tf_op jit(solution)/shard_map/ppermute | solution.py:432
  11.8 10.9 %collective-permute-start.7 = (f32[2,4,64,128]{3,2,1,0:T(8,128)S(1)}, f32[2,4,64,128]{3,2,1,0:T(8,128)S(1)}, u32[]{:S(2)}, u32[]{:S(2)}) collective-permute-start(f32[2,4,64,128]{3,2,1,0:T(8,128)S(1)} %arrange.2.refs_2_), channel_id=1, source_target_pairs={{4,12},{8,0},{12,20},{16,8},{20,28},{24,16},{5,13},{9,1},{13,21},{... | collective-permute-start | bytes 786440 | tf_op jit(solution)/shard_map/ppermute | solution.py:487
  17.1 9.3 %collective-permute-start.8 = (f32[2,4,64,128]{3,2,1,0:T(8,128)S(1)}, f32[2,4,64,128]{3,2,1,0:T(8,128)S(1)}, u32[]{:S(2)}, u32[]{:S(2)}) collective-permute-start(f32[2,4,64,128]{3,2,1,0:T(8,128)S(1)} %arrange.3.refs_3_), channel_id=1, source_target_pairs={{0,8},{8,16},{12,4},{16,24},{20,12},{28,20},{1,9},{9,17},{13,5},{1... | collective-permute-start | bytes 786440 | tf_op jit(solution)/shard_map/ppermute | solution.py:487
  27.8 7.6 %collective-permute-start.11 = (f32[4,32,128]{2,1,0:T(8,128)S(1)}, f32[4,32,128]{2,1,0:T(8,128)S(1)}, u32[]{:S(2)}, u32[]{:S(2)}) collective-permute-start(f32[4,32,128]{2,1,0:T(8,128)S(1)} %get-tuple-element.40.refs_6_), channel_id=1, source_target_pairs={{0,24},{4,28},{8,16},{12,20},{16,8},{20,12},{24,0},{28,4},{1,25},{... | collective-permute-start | bytes 196616 | tf_op jit(solution)/shard_map/ppermute | solution.py:441
  32.4 5.2 %collective-permute-start.10 = (f32[4,32,128]{2,1,0:T(8,128)S(1)}, f32[4,32,128]{2,1,0:T(8,128)S(1)}, u32[]{:S(2)}, u32[]{:S(2)}) collective-permute-start(f32[4,32,128]{2,1,0:T(8,128)S(1)} %get-tuple-element.40.refs_6_), channel_id=1, source_target_pairs={{0,16},{4,20},{8,24},{12,28},{16,0},{20,4},{24,8},{28,12},{1,17},{... | collective-permute-start | bytes 196616 | tf_op jit(solution)/shard_map/ppermute | solution.py:441
  32.4 5.2 %collective-permute-start.9 = (f32[4,32,128]{2,1,0:T(8,128)S(1)}, f32[4,32,128]{2,1,0:T(8,128)S(1)}, u32[]{:S(2)}, u32[]{:S(2)}) collective-permute-start(f32[4,32,128]{2,1,0:T(8,128)S(1)} %get-tuple-element.40.refs_6_), channel_id=1, source_target_pairs={{0,8},{4,12},{8,0},{12,4},{16,24},{20,28},{24,16},{28,20},{1,9},{5... | collective-permute-start | bytes 196616 | tf_op jit(solution)/shard_map/ppermute | solution.py:441
  40.8 3.6 %collective-permute-start.12 = (f32[136,128]{1,0:T(8,128)S(1)}, f32[136,128]{1,0:T(8,128)S(1)}, u32[]{:S(2)}, u32[]{:S(2)}) collective-permute-start(f32[136,128]{1,0:T(8,128)S(1)} %get-tuple-element.42), channel_id=1, source_target_pairs={{0,1},{1,0},{2,3},{3,2},{4,5},{5,4},{6,7},{7,6},{8,9},{9,8},{10,11... | collective-permute-start | bytes 208904 | tf_op jit(solution)/shard_map/ppermute | solution.py:432
  40.9 5.0 %collective-permute-start.13 = (f32[136,128]{1,0:T(8,128)S(1)}, f32[136,128]{1,0:T(8,128)S(1)}, u32[]{:S(2)}, u32[]{:S(2)}) collective-permute-start(f32[136,128]{1,0:T(8,128)S(1)} %get-tuple-element.43), channel_id=1, source_target_pairs={{0,2},{1,3},{2,0},{3,1},{4,6},{5,7},{6,4},{7,5},{8,10},{9,11},{10,... | collective-permute-start | bytes 208904 | tf_op jit(solution)/shard_map/ppermute | solution.py:432
  41.4 5.8 %collective-permute-start.14 = (f32[136,128]{1,0:T(8,128)S(1)}, f32[136,128]{1,0:T(8,128)S(1)}, u32[]{:S(2)}, u32[]{:S(2)}) collective-permute-start(f32[136,128]{1,0:T(8,128)S(1)} %get-tuple-element.44), channel_id=1, source_target_pairs={{0,3},{1,2},{2,1},{3,0},{4,7},{5,6},{6,5},{7,4},{8,11},{9,10},{10,... | collective-permute-start | bytes 208904 | tf_op jit(solution)/shard_map/ppermute | solution.py:432
  42.7 4.7 %collective-permute-start.15 = (f32[136,128]{1,0:T(8,128)S(1)}, f32[136,128]{1,0:T(8,128)S(1)}, u32[]{:S(2)}, u32[]{:S(2)}) collective-permute-start(f32[136,128]{1,0:T(8,128)S(1)} %get-tuple-element.45), channel_id=1, source_target_pairs={{0,4},{1,5},{2,6},{3,7},{4,0},{5,1},{6,2},{7,3},{8,12},{9,13},{10,... | collective-permute-start | bytes 208904 | tf_op jit(solution)/shard_map/ppermute | solution.py:432
  44.0 4.4 %collective-permute-start.16 = (f32[136,128]{1,0:T(8,128)S(1)}, f32[136,128]{1,0:T(8,128)S(1)}, u32[]{:S(2)}, u32[]{:S(2)}) collective-permute-start(f32[136,128]{1,0:T(8,128)S(1)} %get-tuple-element.46), channel_id=1, source_target_pairs={{0,5},{1,4},{2,7},{3,6},{4,1},{5,0},{6,3},{7,2},{8,13},{9,12},{10,... | collective-permute-start | bytes 208904 | tf_op jit(solution)/shard_map/ppermute | solution.py:432
  44.4 5.8 %collective-permute-start.17 = (f32[136,128]{1,0:T(8,128)S(1)}, f32[136,128]{1,0:T(8,128)S(1)}, u32[]{:S(2)}, u32[]{:S(2)}) collective-permute-start(f32[136,128]{1,0:T(8,128)S(1)} %get-tuple-element.47), channel_id=1, source_target_pairs={{0,6},{1,7},{2,4},{3,5},{4,2},{5,3},{6,0},{7,1},{8,14},{9,15},{10,... | collective-permute-start | bytes 208904 | tf_op jit(solution)/shard_map/ppermute | solution.py:432
  45.9 5.4 %collective-permute-start.18 = (f32[136,128]{1,0:T(8,128)S(1)}, f32[136,128]{1,0:T(8,128)S(1)}, u32[]{:S(2)}, u32[]{:S(2)}) collective-permute-start(f32[136,128]{1,0:T(8,128)S(1)} %get-tuple-element.48), channel_id=1, source_target_pairs={{0,7},{1,6},{2,5},{3,4},{4,3},{5,2},{6,1},{7,0},{8,15},{9,14},{10,... | collective-permute-start | bytes 208904 | tf_op jit(solution)/shard_map/ppermute | solution.py:432
  51.3 5.8 %collective-permute-start.21 = (f32[8,128]{1,0:T(8,128)S(1)}, f32[8,128]{1,0:T(8,128)S(1)}, u32[]{:S(2)}, u32[]{:S(2)}) collective-permute-start(f32[8,128]{1,0:T(8,128)S(1)} %squares.1), channel_id=1, source_target_pairs={{0,24},{4,28},{8,16},{12,20},{16,8},{20,12},{24,0},{28,4},{1,25},{... | collective-permute-start | bytes 12296 | tf_op jit(solution)/shard_map/ppermute | solution.py:441
  53.8 4.5 %collective-permute-start.20 = (f32[8,128]{1,0:T(8,128)S(1)}, f32[8,128]{1,0:T(8,128)S(1)}, u32[]{:S(2)}, u32[]{:S(2)}) collective-permute-start(f32[8,128]{1,0:T(8,128)S(1)} %squares.1), channel_id=1, source_target_pairs={{0,16},{4,20},{8,24},{12,28},{16,0},{20,4},{24,8},{28,12},{1,17},{... | collective-permute-start | bytes 12296 | tf_op jit(solution)/shard_map/ppermute | solution.py:441
  53.8 4.5 %collective-permute-start.19 = (f32[8,128]{1,0:T(8,128)S(1)}, f32[8,128]{1,0:T(8,128)S(1)}, u32[]{:S(2)}, u32[]{:S(2)}) collective-permute-start(f32[8,128]{1,0:T(8,128)S(1)} %squares.1), channel_id=1, source_target_pairs={{0,8},{4,12},{8,0},{12,4},{16,24},{20,28},{24,16},{28,20},{1,9},{5... | collective-permute-start | bytes 12296 | tf_op jit(solution)/shard_map/ppermute | solution.py:441
  (3 other events, 4.5 us)

commit v7 on v6

--- a/solution.py
+++ b/solution.py
@@ -232,26 +232,31 @@
     return jnp.where(col // 2 == row, 1.0, 0.0).astype(jnp.bfloat16)
 
 
-def pack_kernel(first, place_ref, source_ref, reaction_ref, *out_refs):
-    for k, out_ref in enumerate(out_refs):
-        out_ref[0] = source_ref[jnp.bitwise_xor(place_ref[0], first + k)]
-        out_ref[1] = reaction_ref[...]
-
-
-def pack_rest_kernel(first, place_ref, shifts_ref, index_ref, velocity_ref, source_ref, reaction_ref, _, *refs):
-    pack_kernel(first, place_ref, source_ref, reaction_ref, *refs[:-1])
+def merge_kernel(place_ref, shifts_ref, index_ref, velocity_ref, *refs):
+    source_ref, reaction_ref, other_source_ref, other_reaction_ref = refs[:4]
+    out_refs, scalar_ref = refs[4:-1], refs[-1]
+    chip, core = place_ref[0] // 2, place_ref[0] & 1
+    by = source_ref.shape[2]
+    mine = pl.ds(pl.multiple_of(core * by, 8), by)
+    theirs = pl.ds(pl.multiple_of((1 - core) * by, 8), by)
+    for m, out_ref in enumerate(out_refs):
+        column = 2 * jnp.bitwise_xor(chip, m) + core
+        out_ref[0, :, mine, :] = source_ref[column]
+        out_ref[0, :, theirs, :] = other_source_ref[column]
+        out_ref[1, :, mine, :] = reaction_ref[...]
+        out_ref[1, :, theirs, :] = other_reaction_ref[...]
     scalars = [shifts_ref[index_ref[place_ref[0]]]] + [velocity_ref[d] for d in range(3)]
     for n, scalar in enumerate(scalars):
-        refs[-1][pl.ds(n, 1), :] = jnp.full((1, LANES), scalar, jnp.float32)
-
-
-def arrange_kernel(gy_size, first, place_ref, *refs):
+        scalar_ref[pl.ds(n, 1), :] = jnp.full((1, LANES), scalar, jnp.float32)
+
+
+def arrange_kernel(chips_y, first, place_ref, *refs):
     half_ref = refs[-1]
-    for k, piece in enumerate(refs[:-1]):
-        owner = jnp.bitwise_xor(place_ref[0], first + k)
-        by = piece.shape[2]
-        rows = pl.ds(pl.multiple_of(lax.rem(owner, gy_size) * by, 8), by)
-        half_ref[:, :, rows, :] = piece[...]
+    for m, block in enumerate(refs[:-1]):
+        owner = jnp.bitwise_xor(place_ref[0] // 2, first + m)
+        size = block.shape[2]
+        rows = pl.ds(pl.multiple_of(lax.rem(owner, chips_y) * size, 8), size)
+        half_ref[:, :, rows, :] = block[...]
 
 
 def pre_kernel(slabs, gy_size, place_ref, scalar_ref, *refs):
@@ -424,12 +429,12 @@
     )(*scalars, *arrays)
 
 
-def swap_in_plane(pieces, first):
+def swap_in_plane(pieces, unit):
     devices = lax.axis_size("gx") * lax.axis_size("gy")
-    moved = []
-    for k, piece in enumerate(pieces, first):
-        pairs = [(i, i ^ k) for i in range(devices)]
-        moved.append(lax.ppermute(piece, ("gx", "gy"), pairs) if k else piece)
+    moved = [pieces[0]]
+    for k in range(1, len(pieces)):
+        pairs = [(i, i ^ (k * unit)) for i in range(devices)]
+        moved.append(lax.ppermute(pieces[k], ("gx", "gy"), pairs))
     return moved
 
 
@@ -454,28 +459,26 @@
     count = SLAB + 2 * HALO
     area = bx * by
 
-    piece = (2, bx, by, nz)
-    pieces = local_kernel(
-        functools.partial(pack_kernel, 0), "pack", (place,), (source, reaction), [piece] * gy_size
-    )
-    pieces = swap_in_plane(pieces, 0)
-    *rest, scalar_rows = local_kernel(
-        functools.partial(pack_rest_kernel, gy_size),
-        "pack_rest",
+    chips, chips_y = columns // 2, gy_size // 2
+    cores = [(i, i ^ 1) for i in range(gy_size)]
+    others = [lax.ppermute(source, "gy", cores), lax.ppermute(reaction, "gy", cores)]
+    *blocks, scalar_rows = local_kernel(
+        merge_kernel,
+        "merge",
         (place, shifts, shift_index, velocity),
-        (source, reaction, pieces[1]),
-        [piece] * gy_size + [(8, LANES)],
+        (source, reaction, *others),
+        [(2, bx, 2 * by, nz)] * chips + [(8, LANES)],
     )
     scalars = (place, scalar_rows)
-    pieces = pieces + swap_in_plane(rest, gy_size)
+    blocks = swap_in_plane(blocks, 2)
     halves, beside = [], []
     for n in range(2):
-        first = n * gy_size
+        first = n * chips_y
         (half,) = local_kernel(
-            functools.partial(arrange_kernel, gy_size, first),
+            functools.partial(arrange_kernel, chips_y, first),
             "arrange",
             (place,),
-            pieces[first : first + gy_size],
+            blocks[first : first + chips_y],
             [(2, HALO, ny, nz)],
         )
         pairs = []
@@ -508,7 +511,7 @@
         [(2 * area + 8, nz)] * columns,
         [rimmed] * 2 + [coarse_grid] * 3 + [coarse_rimmed] * 2 + [(rows, nz), (nx // 2, ny, nz)],
     )
-    parts = swap_in_plane(results, 0)
+    parts = swap_in_plane(results, 1)
 
     (squares,) = local_kernel(
         functools.partial(squares_kernel, 2 * area), "squares", (), parts, [(columns, nz)]
@@ -535,7 +538,7 @@
     slabs, ny = gx_size // step, by * gy_size
     whole = power_of_two(columns) and power_of_two(step) and power_of_two(slabs)
     small = slabs * ny * nz <= 2**15
-    paired = step == 2 and bx == HALO
+    paired = step == 2 and bx == HALO and gy_size % 2 == 0
     return whole and small and paired and bx * step == SLAB and nz == LANES and by % 16 == 0
 
 

time: 59.3 us -> 59.8 us (level)
  waiting for transfers between devices: 19.5 us -> 24.2 us
  starting transfers between devices: 28 us -> 25 us
  local copies, waits for them, and re-layouts: 1.62 us -> 0.96 us
    ppermute x14 -> x12, waiting for transfers between devices: 7.91 us -> 12.2 us  [the longest x10 11 us: swap_in_plane(): moved.append(lax.ppermute(pieces[k], ('gx', 'gy'), pairs))]
    ppermute x14 -> x12, starting transfers between devices: 13.7 us -> 11.4 us  [the longest x10 10.8 us: swap_in_plane(): moved.append(lax.ppermute(pieces[k], ('gx', 'gy'), pairs))]
    ppermute x2, waiting for transfers between devices: 5.67 us -> 7.63 us  [column_body(): beside.append(lax.ppermute(half, 'gx', pairs))]
    ppermute x6, waiting for transfers between devices: 5.88 us -> 4.39 us  [swap_slabs(): moved.append(lax.ppermute(piece, 'gx', pairs))]
    ppermute x6, starting transfers between devices: 9.6 us -> 8.84 us  [swap_slabs(): moved.append(lax.ppermute(piece, 'gx', pairs))]
    unnamed x10, local copies, waits for them, and re-layouts: 1.62 us -> 0.96 us
    pallas_call x8 -> x7, Pallas kernels: 8.21 us -> 7.68 us  [local_kernel(): pl.pallas_call(kernel, out_shape=[jax.ShapeDtypeStruct(shape, jnp.float32...]
  transfers between devices with their start and end apart: 22 -> 20, of which waited for: 12 -> 12; matrix products, arithmetic and copies ran while one was open for 0% -> 0% of each run, Pallas kernels for 5% -> 4%
where the time goes in v7:
time: 59.8 us; the launch traced here: 59.7 us
  starting transfers between devices  25 us (42%)
  waiting for transfers between devices  24.2 us (40%)
  Pallas kernels  7.68 us (13%)
  other arithmetic  0.97 us (2%)
  local copies, waits for them, and re-layouts  0.96 us (2%)
  between operations  0.78 us (1%)
    ppermute x10, waiting for transfers between devices, swap_in_plane(): moved.append(lax.ppermute(pieces[k], ('gx', 'gy'), pairs))  11 us
    ppermute x10, starting transfers between devices, swap_in_plane(): moved.append(lax.ppermute(pieces[k], ('gx', 'gy'), pairs))  10.8 us
    ppermute x6, starting transfers between devices, swap_slabs(): moved.append(lax.ppermute(piece, 'gx', pairs))  8.84 us
    pallas_call x7, Pallas kernels, local_kernel(): pl.pallas_call(kernel, out_shape=[jax.ShapeDtypeStruct(shape, jnp.float32...  7.68 us
    ppermute x2, waiting for transfers between devices, column_body(): beside.append(lax.ppermute(half, 'gx', pairs))  7.63 us
    ppermute x2, starting transfers between devices, column_body(): beside.append(lax.ppermute(half, 'gx', pairs))  4.79 us
    ppermute x6, waiting for transfers between devices, swap_slabs(): moved.append(lax.ppermute(piece, 'gx', pairs))  4.39 us
    ppermute x1, waiting for transfers between devices, column_body(): lax.ppermute(reaction, 'gy', cores)  1.26 us
  transfers between devices with their start and end apart: 20, of which 12 were waited for; matrix products, arithmetic and copies ran while one was open for 0% of the time, Pallas kernels for 4%

profile of v7, /device:TPU:0, one launch (start us, length us, event | category | flops | bytes accessed | tf_op | source)
XLA Modules:
  0.0 59.7 jit_solution(11868869683279202286)
XLA Ops:
  1.3 1.3 %collective-permute-done.1.refs_3_ = f32[4,16,128]{2,1,0:T(8,128)S(1)} collective-permute-done((f32[4,16,128]{2,1,0:T(8,128)}, f32[4,16,128]{2,1,0:T(8,128)S(1)}, u32[]{:S(2)}, u32[]{:S(2)}) %collective-permute-start.1) | collective-permute-done | bytes 32800 | tf_op jit(solution)/shard_map/ppermute | solution.py:464
  4.2 2.9 %collective-permute-start.3 = (f32[2,4,32,128]{3,2,1,0:T(8,128)S(1)}, f32[2,4,32,128]{3,2,1,0:T(8,128)S(1)}, u32[]{:S(2)}, u32[]{:S(2)}) collective-permute-start(f32[2,4,32,128]{3,2,1,0:T(8,128)S(1)} %get-tuple-element.26), channel_id=1, source_target_pairs={{0,4},{1,5},{2,6},{3,7},{4,0},{5,1},{6,2},{7,3},{8,12},{9,13},{10,... | collective-permute-start | bytes 393224 | tf_op jit(solution)/shard_map/ppermute | solution.py:437
  7.1 1.5 %collective-permute-start.4 = (f32[2,4,32,128]{3,2,1,0:T(8,128)S(1)}, f32[2,4,32,128]{3,2,1,0:T(8,128)S(1)}, u32[]{:S(2)}, u32[]{:S(2)}) collective-permute-start(f32[2,4,32,128]{3,2,1,0:T(8,128)S(1)} %get-tuple-element.27), channel_id=1, source_target_pairs={{0,6},{1,7},{2,4},{3,5},{4,2},{5,3},{6,0},{7,1},{8,14},{9,15},{10,... | collective-permute-start | bytes 393224 | tf_op jit(solution)/shard_map/ppermute | solution.py:437
  8.6 2.6 %collective-permute-done.3.refs_0_ = f32[2,4,32,128]{3,2,1,0:T(8,128)S(1)} collective-permute-done((f32[2,4,32,128]{3,2,1,0:T(8,128)S(1)}, f32[2,4,32,128]{3,2,1,0:T(8,128)S(1)}, u32[]{:S(2)}, u32[]{:S(2)}) %collective-permute-start.3) | collective-permute-done | bytes 131104 | tf_op jit(solution)/shard_map/ppermute | solution.py:437
  11.2 3.8 %collective-permute-done.4.refs_1_ = f32[2,4,32,128]{3,2,1,0:T(8,128)S(1)} collective-permute-done((f32[2,4,32,128]{3,2,1,0:T(8,128)S(1)}, f32[2,4,32,128]{3,2,1,0:T(8,128)S(1)}, u32[]{:S(2)}, u32[]{:S(2)}) %collective-permute-start.4) | collective-permute-done | bytes 131104 | tf_op jit(solution)/shard_map/ppermute | solution.py:437
  15.6 3.5 %collective-permute-start.6 = (f32[2,4,64,128]{3,2,1,0:T(8,128)S(1)}, f32[2,4,64,128]{3,2,1,0:T(8,128)S(1)}, u32[]{:S(2)}, u32[]{:S(2)}) collective-permute-start(f32[2,4,64,128]{3,2,1,0:T(8,128)S(1)} %arrange.3.refs_3_), channel_id=1, source_target_pairs={{0,8},{8,16},{12,4},{16,24},{20,12},{28,20},{1,9},{9,17},{13,5},{1... | collective-permute-start | bytes 786440 | tf_op jit(solution)/shard_map/ppermute | solution.py:490
  19.7 1.3 %collective-permute-start.5 = (f32[2,4,64,128]{3,2,1,0:T(8,128)S(1)}, f32[2,4,64,128]{3,2,1,0:T(8,128)S(1)}, u32[]{:S(2)}, u32[]{:S(2)}) collective-permute-start(f32[2,4,64,128]{3,2,1,0:T(8,128)S(1)} %arrange.2.refs_2_), channel_id=1, source_target_pairs={{4,12},{8,0},{12,20},{16,8},{20,28},{24,16},{5,13},{9,1},{13,21},{... | collective-permute-start | bytes 786440 | tf_op jit(solution)/shard_map/ppermute | solution.py:490
  21.1 2.9 %collective-permute-done.6.refs_5_ = f32[2,4,64,128]{3,2,1,0:T(8,128)S(1)} collective-permute-done((f32[2,4,64,128]{3,2,1,0:T(8,128)S(1)}, f32[2,4,64,128]{3,2,1,0:T(8,128)S(1)}, u32[]{:S(2)}, u32[]{:S(2)}) %collective-permute-start.6) | collective-permute-done | bytes 262176 | tf_op jit(solution)/shard_map/ppermute | solution.py:490
  24.0 4.7 %collective-permute-done.5.refs_4_ = f32[2,4,64,128]{3,2,1,0:T(8,128)S(1)} collective-permute-done((f32[2,4,64,128]{3,2,1,0:T(8,128)S(1)}, f32[2,4,64,128]{3,2,1,0:T(8,128)S(1)}, u32[]{:S(2)}, u32[]{:S(2)}) %collective-permute-start.5) | collective-permute-done | bytes 262176 | tf_op jit(solution)/shard_map/ppermute | solution.py:490
  28.8 1.4 %pre.1 = (f32[16,64,128]{2,1,0:T(8,128)S(1)}, f32[16,64,128]{2,1,0:T(8,128)S(1)}, f32[16,64,128]{2,1,0:T(8,128)S(1)}, f32[16,80,128]{2,1,0:T(8,128)S(1)}, f32[4,32,128]{2,1,0:T(8,128)S(1)}) custom-call(s32[2]{0:T(128)S(1)} %pad_add_fusion.place_ref, f32[8,128]{1,0:T(8,128)S(1)} %get-tuple-element.23.scalar_ref, ...), custom_call_target="tpu_custom_call" | custom-call | tf_op jit(solution)/shard_map/pre/pallas_call | solution.py:421
  30.2 1.6 %collective-permute-start.9 = (f32[4,32,128]{2,1,0:T(8,128)S(1)}, f32[4,32,128]{2,1,0:T(8,128)S(1)}, u32[]{:S(2)}, u32[]{:S(2)}) collective-permute-start(f32[4,32,128]{2,1,0:T(8,128)S(1)} %get-tuple-element.32.refs_6_), channel_id=1, source_target_pairs={{0,24},{4,28},{8,16},{12,20},{16,8},{20,12},{24,0},{28,4},{1,25},{... | collective-permute-start | bytes 196616 | tf_op jit(solution)/shard_map/ppermute | solution.py:446
  31.8 1.5 %collective-permute-start.8 = (f32[4,32,128]{2,1,0:T(8,128)S(1)}, f32[4,32,128]{2,1,0:T(8,128)S(1)}, u32[]{:S(2)}, u32[]{:S(2)}) collective-permute-start(f32[4,32,128]{2,1,0:T(8,128)S(1)} %get-tuple-element.32.refs_6_), channel_id=1, source_target_pairs={{0,16},{4,20},{8,24},{12,28},{16,0},{20,4},{24,8},{28,12},{1,17},{... | collective-permute-start | bytes 196616 | tf_op jit(solution)/shard_map/ppermute | solution.py:446
  33.3 1.4 %collective-permute-start.7 = (f32[4,32,128]{2,1,0:T(8,128)S(1)}, f32[4,32,128]{2,1,0:T(8,128)S(1)}, u32[]{:S(2)}, u32[]{:S(2)}) collective-permute-start(f32[4,32,128]{2,1,0:T(8,128)S(1)} %get-tuple-element.32.refs_6_), channel_id=1, source_target_pairs={{0,8},{4,12},{8,0},{12,4},{16,24},{20,28},{24,16},{28,20},{1,9},{5... | collective-permute-start | bytes 196616 | tf_op jit(solution)/shard_map/ppermute | solution.py:446
  34.6 1.7 %collective-permute-done.9.refs_9_ = f32[4,32,128]{2,1,0:T(8,128)S(1)} collective-permute-done((f32[4,32,128]{2,1,0:T(8,128)S(1)}, f32[4,32,128]{2,1,0:T(8,128)S(1)}, u32[]{:S(2)}, u32[]{:S(2)}) %collective-permute-start.9) | collective-permute-done | bytes 65568 | tf_op jit(solution)/shard_map/ppermute | solution.py:446
  37.7 3.2 %post.1 = (f32[136,128]{1,0:T(8,128)S(1)}, f32[136,128]{1,0:T(8,128)S(1)}, f32[136,128]{1,0:T(8,128)S(1)}, f32[136,128]{1,0:T(8,128)S(1)}, f32[136,128]{1,0:T(8,...) custom-call(s32[2]{0:T(128)S(1)} %pad_add_fusion.place_ref, ...), custom_call_target="tpu_custom_call" | custom-call | tf_op jit(solution)/shard_map/post/pallas_call | solution.py:421
  42.8 1.7 %collective-permute-start.13 = (f32[136,128]{1,0:T(8,128)S(1)}, f32[136,128]{1,0:T(8,128)S(1)}, u32[]{:S(2)}, u32[]{:S(2)}) collective-permute-start(f32[136,128]{1,0:T(8,128)S(1)} %get-tuple-element.37), channel_id=1, source_target_pairs={{0,4},{1,5},{2,6},{3,7},{4,0},{5,1},{6,2},{7,3},{8,12},{9,13},{10,... | collective-permute-start | bytes 208904 | tf_op jit(solution)/shard_map/ppermute | solution.py:437
  44.5 1.6 %collective-permute-start.15 = (f32[136,128]{1,0:T(8,128)S(1)}, f32[136,128]{1,0:T(8,128)S(1)}, u32[]{:S(2)}, u32[]{:S(2)}) collective-permute-start(f32[136,128]{1,0:T(8,128)S(1)} %get-tuple-element.39), channel_id=1, source_target_pairs={{0,6},{1,7},{2,4},{3,5},{4,2},{5,3},{6,0},{7,1},{8,14},{9,15},{10,... | collective-permute-start | bytes 208904 | tf_op jit(solution)/shard_map/ppermute | solution.py:437
  47.2 1.5 %collective-permute-done.14.refs_5_ = f32[136,128]{1,0:T(8,128)S(1)} collective-permute-done((f32[136,128]{1,0:T(8,128)S(1)}, f32[136,128]{1,0:T(8,128)S(1)}, u32[]{:S(2)}, u32[]{:S(2)}) %collective-permute-start.14) | collective-permute-done | bytes 69664 | tf_op jit(solution)/shard_map/ppermute | solution.py:437
  48.7 1.9 %collective-permute-done.15.refs_6_ = f32[136,128]{1,0:T(8,128)S(1)} collective-permute-done((f32[136,128]{1,0:T(8,128)S(1)}, f32[136,128]{1,0:T(8,128)S(1)}, u32[]{:S(2)}, u32[]{:S(2)}) %collective-permute-start.15) | collective-permute-done | bytes 69664 | tf_op jit(solution)/shard_map/ppermute | solution.py:437
  50.6 1.2 %collective-permute-done.16.refs_7_ = f32[136,128]{1,0:T(8,128)S(1)} collective-permute-done((f32[136,128]{1,0:T(8,128)S(1)}, f32[136,128]{1,0:T(8,128)S(1)}, u32[]{:S(2)}, u32[]{:S(2)}) %collective-permute-start.16) | collective-permute-done | bytes 69664 | tf_op jit(solution)/shard_map/ppermute | solution.py:437
  51.8 2.6 %collective-permute-start.19 = (f32[8,128]{1,0:T(8,128)S(1)}, f32[8,128]{1,0:T(8,128)S(1)}, u32[]{:S(2)}, u32[]{:S(2)}) collective-permute-start(f32[8,128]{1,0:T(8,128)S(1)} %squares.1), channel_id=1, source_target_pairs={{0,24},{4,28},{8,16},{12,20},{16,8},{20,12},{24,0},{28,4},{1,25},{... | collective-permute-start | bytes 12296 | tf_op jit(solution)/shard_map/ppermute | solution.py:446
  54.4 1.8 %collective-permute-start.17 = (f32[8,128]{1,0:T(8,128)S(1)}, f32[8,128]{1,0:T(8,128)S(1)}, u32[]{:S(2)}, u32[]{:S(2)}) collective-permute-start(f32[8,128]{1,0:T(8,128)S(1)} %squares.1), channel_id=1, source_target_pairs={{0,8},{4,12},{8,0},{12,4},{16,24},{20,28},{24,16},{28,20},{1,9},{5... | collective-permute-start | bytes 12296 | tf_op jit(solution)/shard_map/ppermute | solution.py:446
  56.2 1.4 %collect.1 = (f32[8,4,16,128]{3,2,1,0:T(8,128)}, f32[8,4,16,128]{3,2,1,0:T(8,128)}) custom-call(s32[2]{0:T(128)S(1)} %pad_add_fusion.place_ref, f32[136,128]{1,0:T(8,128)S(1)} %get-tuple-element.33.refs_0_, f32[136,128]{1,0:T(8,128)S(1)} %collective-permute-done.10.refs_1_, f32[136,128]{1,0:T(8,128)S(1)} %collective-permute-done.11.refs_2_, ...), custom_call_target="tpu_custom_call" | custom-call | tf_op jit(solution)/shard_map/collect/pallas_call | solution.py:421
  57.6 1.3 %collective-permute-done.18 = f32[8,128]{1,0:T(8,128)S(1)} collective-permute-done((f32[8,128]{1,0:T(8,128)S(1)}, f32[8,128]{1,0:T(8,128)S(1)}, u32[]{:S(2)}, u32[]{:S(2)}) %collective-permute-start.18) | collective-permute-done | bytes 4128 | tf_op jit(solution)/shard_map/ppermute | solution.py:446
  (41 shorter events, 8.8 us)
Async XLA Ops:
  0.6 2.0 %copy-start.1 = (f32[4,16,128]{2,1,0:T(8,128)S(1)}, f32[4,16,128]{2,1,0:T(8,128)}, u32[]{:S(2)}) copy-start(f32[4,16,128]{2,1,0:T(8,128)} %refs_1_.1) | copy-start | bytes 98308
  0.6 1.9 %collective-permute-start = (f32[8,4,16,128]{3,2,1,0:T(8,128)}, f32[8,4,16,128]{3,2,1,0:T(8,128)S(1)}, u32[]{:S(2)}, u32[]{:S(2)}) collective-permute-start(f32[8,4,16,128]{3,2,1,0:T(8,128)} %refs_0_.1), channel_id=1, source_target_pairs={{0,1},{1,0},{2,3},{3,2},{4,5},{5,4},{6,7},{7,6},{8,9},{9,8},{10,11... | collective-permute-start | bytes 786440 | tf_op jit(solution)/shard_map/ppermute | solution.py:464
  1.2 1.4 %collective-permute-start.1 = (f32[4,16,128]{2,1,0:T(8,128)}, f32[4,16,128]{2,1,0:T(8,128)S(1)}, u32[]{:S(2)}, u32[]{:S(2)}) collective-permute-start(f32[4,16,128]{2,1,0:T(8,128)} %refs_1_.1), channel_id=1, source_target_pairs={{0,1},{1,0},{2,3},{3,2},{4,5},{5,4},{6,7},{7,6},{8,9},{9,8},{10,11... | collective-permute-start | bytes 98312 | tf_op jit(solution)/shard_map/ppermute | solution.py:464
  1.2 1.3 %copy-start.2 = (f32[8]{0:T(128)S(1)}, f32[8]{0:T(128)}, u32[]{:S(2)}) copy-start(f32[8]{0:T(128)} %shifts_ref.1) | copy-start | bytes 100
  1.2 1.3 %copy-start.3 = (s32[8]{0:T(128)S(1)}, s32[8]{0:T(128)}, u32[]{:S(2)}) copy-start(s32[8]{0:T(128)} %index_ref.1) | copy-start | bytes 100
  1.2 1.4 %copy-start.4 = (f32[3]{0:T(128)S(1)}, f32[3]{0:T(128)}, u32[]{:S(2)}) copy-start(f32[3]{0:T(128)} %velocity_ref.1) | copy-start | bytes 40
  4.2 7.0 %collective-permute-start.3 = (f32[2,4,32,128]{3,2,1,0:T(8,128)S(1)}, f32[2,4,32,128]{3,2,1,0:T(8,128)S(1)}, u32[]{:S(2)}, u32[]{:S(2)}) collective-permute-start(f32[2,4,32,128]{3,2,1,0:T(8,128)S(1)} %get-tuple-element.26), channel_id=1, source_target_pairs={{0,4},{1,5},{2,6},{3,7},{4,0},{5,1},{6,2},{7,3},{8,12},{9,13},{10,... | collective-permute-start | bytes 393224 | tf_op jit(solution)/shard_map/ppermute | solution.py:437
  7.1 7.9 %collective-permute-start.4 = (f32[2,4,32,128]{3,2,1,0:T(8,128)S(1)}, f32[2,4,32,128]{3,2,1,0:T(8,128)S(1)}, u32[]{:S(2)}, u32[]{:S(2)}) collective-permute-start(f32[2,4,32,128]{3,2,1,0:T(8,128)S(1)} %get-tuple-element.27), channel_id=1, source_target_pairs={{0,6},{1,7},{2,4},{3,5},{4,2},{5,3},{6,0},{7,1},{8,14},{9,15},{10,... | collective-permute-start | bytes 393224 | tf_op jit(solution)/shard_map/ppermute | solution.py:437
  8.6 10.5 %collective-permute-start.2 = (f32[2,4,32,128]{3,2,1,0:T(8,128)S(1)}, f32[2,4,32,128]{3,2,1,0:T(8,128)S(1)}, u32[]{:S(2)}, u32[]{:S(2)}) collective-permute-start(f32[2,4,32,128]{3,2,1,0:T(8,128)S(1)} %get-tuple-element.25), channel_id=1, source_target_pairs={{0,2},{1,3},{2,0},{3,1},{4,6},{5,7},{6,4},{7,5},{8,10},{9,11},{10,... | collective-permute-start | bytes 393224 | tf_op jit(solution)/shard_map/ppermute | solution.py:437
  15.6 8.4 %collective-permute-start.6 = (f32[2,4,64,128]{3,2,1,0:T(8,128)S(1)}, f32[2,4,64,128]{3,2,1,0:T(8,128)S(1)}, u32[]{:S(2)}, u32[]{:S(2)}) collective-permute-start(f32[2,4,64,128]{3,2,1,0:T(8,128)S(1)} %arrange.3.refs_3_), channel_id=1, source_target_pairs={{0,8},{8,16},{12,4},{16,24},{20,12},{28,20},{1,9},{9,17},{13,5},{1... | collective-permute-start | bytes 786440 | tf_op jit(solution)/shard_map/ppermute | solution.py:490
  19.7 9.1 %collective-permute-start.5 = (f32[2,4,64,128]{3,2,1,0:T(8,128)S(1)}, f32[2,4,64,128]{3,2,1,0:T(8,128)S(1)}, u32[]{:S(2)}, u32[]{:S(2)}) collective-permute-start(f32[2,4,64,128]{3,2,1,0:T(8,128)S(1)} %arrange.2.refs_2_), channel_id=1, source_target_pairs={{4,12},{8,0},{12,20},{16,8},{20,28},{24,16},{5,13},{9,1},{13,21},{... | collective-permute-start | bytes 786440 | tf_op jit(solution)/shard_map/ppermute | solution.py:490
  30.2 6.1 %collective-permute-start.9 = (f32[4,32,128]{2,1,0:T(8,128)S(1)}, f32[4,32,128]{2,1,0:T(8,128)S(1)}, u32[]{:S(2)}, u32[]{:S(2)}) collective-permute-start(f32[4,32,128]{2,1,0:T(8,128)S(1)} %get-tuple-element.32.refs_6_), channel_id=1, source_target_pairs={{0,24},{4,28},{8,16},{12,20},{16,8},{20,12},{24,0},{28,4},{1,25},{... | collective-permute-start | bytes 196616 | tf_op jit(solution)/shard_map/ppermute | solution.py:446
  31.8 5.2 %collective-permute-start.8 = (f32[4,32,128]{2,1,0:T(8,128)S(1)}, f32[4,32,128]{2,1,0:T(8,128)S(1)}, u32[]{:S(2)}, u32[]{:S(2)}) collective-permute-start(f32[4,32,128]{2,1,0:T(8,128)S(1)} %get-tuple-element.32.refs_6_), channel_id=1, source_target_pairs={{0,16},{4,20},{8,24},{12,28},{16,0},{20,4},{24,8},{28,12},{1,17},{... | collective-permute-start | bytes 196616 | tf_op jit(solution)/shard_map/ppermute | solution.py:446
  33.3 4.4 %collective-permute-start.7 = (f32[4,32,128]{2,1,0:T(8,128)S(1)}, f32[4,32,128]{2,1,0:T(8,128)S(1)}, u32[]{:S(2)}, u32[]{:S(2)}) collective-permute-start(f32[4,32,128]{2,1,0:T(8,128)S(1)} %get-tuple-element.32.refs_6_), channel_id=1, source_target_pairs={{0,8},{4,12},{8,0},{12,4},{16,24},{20,28},{24,16},{28,20},{1,9},{5... | collective-permute-start | bytes 196616 | tf_op jit(solution)/shard_map/ppermute | solution.py:446
  40.9 3.7 %collective-permute-start.10 = (f32[136,128]{1,0:T(8,128)S(1)}, f32[136,128]{1,0:T(8,128)S(1)}, u32[]{:S(2)}, u32[]{:S(2)}) collective-permute-start(f32[136,128]{1,0:T(8,128)S(1)} %get-tuple-element.34), channel_id=1, source_target_pairs={{0,1},{1,0},{2,3},{3,2},{4,5},{5,4},{6,7},{7,6},{8,9},{9,8},{10,11... | collective-permute-start | bytes 208904 | tf_op jit(solution)/shard_map/ppermute | solution.py:437
  40.9 5.2 %collective-permute-start.11 = (f32[136,128]{1,0:T(8,128)S(1)}, f32[136,128]{1,0:T(8,128)S(1)}, u32[]{:S(2)}, u32[]{:S(2)}) collective-permute-start(f32[136,128]{1,0:T(8,128)S(1)} %get-tuple-element.35), channel_id=1, source_target_pairs={{0,2},{1,3},{2,0},{3,1},{4,6},{5,7},{6,4},{7,5},{8,10},{9,11},{10,... | collective-permute-start | bytes 208904 | tf_op jit(solution)/shard_map/ppermute | solution.py:437
  41.8 5.4 %collective-permute-start.12 = (f32[136,128]{1,0:T(8,128)S(1)}, f32[136,128]{1,0:T(8,128)S(1)}, u32[]{:S(2)}, u32[]{:S(2)}) collective-permute-start(f32[136,128]{1,0:T(8,128)S(1)} %get-tuple-element.36), channel_id=1, source_target_pairs={{0,3},{1,2},{2,1},{3,0},{4,7},{5,6},{6,5},{7,4},{8,11},{9,10},{10,... | collective-permute-start | bytes 208904 | tf_op jit(solution)/shard_map/ppermute | solution.py:437
  42.8 4.4 %collective-permute-start.13 = (f32[136,128]{1,0:T(8,128)S(1)}, f32[136,128]{1,0:T(8,128)S(1)}, u32[]{:S(2)}, u32[]{:S(2)}) collective-permute-start(f32[136,128]{1,0:T(8,128)S(1)} %get-tuple-element.37), channel_id=1, source_target_pairs={{0,4},{1,5},{2,6},{3,7},{4,0},{5,1},{6,2},{7,3},{8,12},{9,13},{10,... | collective-permute-start | bytes 208904 | tf_op jit(solution)/shard_map/ppermute | solution.py:437
  44.5 4.2 %collective-permute-start.14 = (f32[136,128]{1,0:T(8,128)S(1)}, f32[136,128]{1,0:T(8,128)S(1)}, u32[]{:S(2)}, u32[]{:S(2)}) collective-permute-start(f32[136,128]{1,0:T(8,128)S(1)} %get-tuple-element.38), channel_id=1, source_target_pairs={{0,5},{1,4},{2,7},{3,6},{4,1},{5,0},{6,3},{7,2},{8,13},{9,12},{10,... | collective-permute-start | bytes 208904 | tf_op jit(solution)/shard_map/ppermute | solution.py:437
  44.5 6.1 %collective-permute-start.15 = (f32[136,128]{1,0:T(8,128)S(1)}, f32[136,128]{1,0:T(8,128)S(1)}, u32[]{:S(2)}, u32[]{:S(2)}) collective-permute-start(f32[136,128]{1,0:T(8,128)S(1)} %get-tuple-element.39), channel_id=1, source_target_pairs={{0,6},{1,7},{2,4},{3,5},{4,2},{5,3},{6,0},{7,1},{8,14},{9,15},{10,... | collective-permute-start | bytes 208904 | tf_op jit(solution)/shard_map/ppermute | solution.py:437
  46.1 5.7 %collective-permute-start.16 = (f32[136,128]{1,0:T(8,128)S(1)}, f32[136,128]{1,0:T(8,128)S(1)}, u32[]{:S(2)}, u32[]{:S(2)}) collective-permute-start(f32[136,128]{1,0:T(8,128)S(1)} %get-tuple-element.40), channel_id=1, source_target_pairs={{0,7},{1,6},{2,5},{3,4},{4,3},{5,2},{6,1},{7,0},{8,15},{9,14},{10,... | collective-permute-start | bytes 208904 | tf_op jit(solution)/shard_map/ppermute | solution.py:437
  51.8 5.8 %collective-permute-start.19 = (f32[8,128]{1,0:T(8,128)S(1)}, f32[8,128]{1,0:T(8,128)S(1)}, u32[]{:S(2)}, u32[]{:S(2)}) collective-permute-start(f32[8,128]{1,0:T(8,128)S(1)} %squares.1), channel_id=1, source_target_pairs={{0,24},{4,28},{8,16},{12,20},{16,8},{20,12},{24,0},{28,4},{1,25},{... | collective-permute-start | bytes 12296 | tf_op jit(solution)/shard_map/ppermute | solution.py:446
  54.4 4.5 %collective-permute-start.18 = (f32[8,128]{1,0:T(8,128)S(1)}, f32[8,128]{1,0:T(8,128)S(1)}, u32[]{:S(2)}, u32[]{:S(2)}) collective-permute-start(f32[8,128]{1,0:T(8,128)S(1)} %squares.1), channel_id=1, source_target_pairs={{0,16},{4,20},{8,24},{12,28},{16,0},{20,4},{24,8},{28,12},{1,17},{... | collective-permute-start | bytes 12296 | tf_op jit(solution)/shard_map/ppermute | solution.py:446
  54.4 4.5 %collective-permute-start.17 = (f32[8,128]{1,0:T(8,128)S(1)}, f32[8,128]{1,0:T(8,128)S(1)}, u32[]{:S(2)}, u32[]{:S(2)}) collective-permute-start(f32[8,128]{1,0:T(8,128)S(1)} %squares.1), channel_id=1, source_target_pairs={{0,8},{4,12},{8,0},{12,4},{16,24},{20,28},{24,16},{28,20},{1,9},{5... | collective-permute-start | bytes 12296 | tf_op jit(solution)/shard_map/ppermute | solution.py:446
  (1 other events, 1.0 us)

commit v8 on v7

--- a/solution.py
+++ b/solution.py
@@ -232,39 +232,38 @@
     return jnp.where(col // 2 == row, 1.0, 0.0).astype(jnp.bfloat16)
 
 
-def merge_kernel(place_ref, shifts_ref, index_ref, velocity_ref, *refs):
-    source_ref, reaction_ref, other_source_ref, other_reaction_ref = refs[:4]
-    out_refs, scalar_ref = refs[4:-1], refs[-1]
+def merge_kernel(place_ref, mine_ref, theirs_ref, *out_refs):
     chip, core = place_ref[0] // 2, place_ref[0] & 1
-    by = source_ref.shape[2]
-    mine = pl.ds(pl.multiple_of(core * by, 8), by)
-    theirs = pl.ds(pl.multiple_of((1 - core) * by, 8), by)
-    for m, out_ref in enumerate(out_refs):
-        column = 2 * jnp.bitwise_xor(chip, m) + core
-        out_ref[0, :, mine, :] = source_ref[column]
-        out_ref[0, :, theirs, :] = other_source_ref[column]
-        out_ref[1, :, mine, :] = reaction_ref[...]
-        out_ref[1, :, theirs, :] = other_reaction_ref[...]
+    by = mine_ref.shape[2]
+    for first, ref in ((core * by, mine_ref), ((1 - core) * by, theirs_ref)):
+        rows = pl.ds(pl.multiple_of(first, 8), by)
+        for m, out_ref in enumerate(out_refs):
+            target = jnp.bitwise_xor(chip, m)
+            whole = ref.shape[0] > len(out_refs) + 1
+            out_ref[0, :, rows, :] = ref[2 * target + core if whole else target]
+            out_ref[1, :, rows, :] = ref[ref.shape[0] - 1]
+
+
+def pack_kernel(place_ref, block_ref, *refs):
+    out_ref = refs[-1]
+    other, chips = 1 - (place_ref[0] & 1), out_ref.shape[0] - 1
+    for n in range(chips):
+        out_ref[n] = block_ref[2 * n + other]
+    out_ref[chips] = block_ref[2 * chips]
+
+
+def scalars_kernel(place_ref, shifts_ref, index_ref, velocity_ref, out_ref):
     scalars = [shifts_ref[index_ref[place_ref[0]]]] + [velocity_ref[d] for d in range(3)]
     for n, scalar in enumerate(scalars):
-        scalar_ref[pl.ds(n, 1), :] = jnp.full((1, LANES), scalar, jnp.float32)
-
-
-def arrange_kernel(chips_y, first, place_ref, *refs):
-    half_ref = refs[-1]
-    for m, block in enumerate(refs[:-1]):
-        owner = jnp.bitwise_xor(place_ref[0] // 2, first + m)
-        size = block.shape[2]
-        rows = pl.ds(pl.multiple_of(lax.rem(owner, chips_y) * size, 8), size)
-        half_ref[:, :, rows, :] = block[...]
-
-
-def pre_kernel(slabs, gy_size, place_ref, scalar_ref, *refs):
+        out_ref[pl.ds(n, 1), :] = jnp.full((1, LANES), scalar, jnp.float32)
+
+
+def pre_kernel(slabs, chips_y, place_ref, scalar_ref, *refs):
     pool_ref, pool_up_ref = refs[:2]
-    parts = refs[2:6]
-    f, r, w, v1, coarse_ref, v0, tmp, pooled = refs[6:]
+    parts, refs = refs[2:-8], refs[-8:]
+    f, r, w, v1, coarse_ref, v0, tmp, pooled = refs
     ny = f.shape[1]
-    slab = place_ref[1]
+    chip, slab = place_ref[0] // 2, place_ref[1]
     fine = Level(0, ny, LANES, 0, scalar_ref, f, r, w)
     zero_rows(v0, ny)
     zero_rows(v1, ny)
@@ -273,11 +272,15 @@
     inside += [DAMPING] * SLAB
     inside += [jnp.where(slab < slabs - 1, DAMPING, 0.0)] * HALO
 
-    x = place_ref[0] // gy_size
-    firsts = (HALO * (1 + x), HALO * (2 - x), (HALO + SLAB) * (1 - x), (HALO + SLAB) * x)
-    for part, first in zip(parts, firsts):
-        f[pl.ds(first, HALO)] = part[0]
-        r[pl.ds(first, HALO)] = part[1]
+    chips = len(parts) // 2
+    rows = parts[0].shape[2]
+    for k, part in enumerate(parts):
+        owner = jnp.bitwise_xor(chip, k % chips)
+        x = owner // chips_y
+        first = HALO * (1 + x) if k < chips else (HALO + SLAB) * (1 - x)
+        to = pl.ds(pl.multiple_of(lax.rem(owner, chips_y) * rows, 8), rows)
+        f[pl.ds(first, HALO), to, :] = part[0]
+        r[pl.ds(first, HALO), to, :] = part[1]
 
     def put(x, weight):
         w[x] = weight
@@ -461,40 +464,34 @@
 
     chips, chips_y = columns // 2, gy_size // 2
     cores = [(i, i ^ 1) for i in range(gy_size)]
-    others = [lax.ppermute(source, "gy", cores), lax.ppermute(reaction, "gy", cores)]
-    *blocks, scalar_rows = local_kernel(
-        merge_kernel,
-        "merge",
-        (place, shifts, shift_index, velocity),
-        (source, reaction, *others),
-        [(2, bx, 2 * by, nz)] * chips + [(8, LANES)],
+    onward = [(i, i + step if i % step else i - step) for i in range(gx_size)]
+    onward = [(i, j) for i, j in onward if 0 <= j < gx_size]
+
+    def deal(block, sent):
+        theirs = lax.ppermute(sent, "gy", cores)
+        merged = local_kernel(
+            merge_kernel, "merge", (place,), (block, theirs), [(2, bx, 2 * by, nz)] * chips
+        )
+        return swap_in_plane(merged, 2)
+
+    joined = jnp.concatenate([source, reaction[None]])
+    beside = lax.ppermute(joined, "gx", onward)
+    parts = deal(joined, joined)
+    (sent,) = local_kernel(
+        pack_kernel, "pack", (place,), (beside, *parts[1:]), [(chips + 1, bx, by, nz)]
+    )
+    parts = parts + deal(beside, sent)
+    (scalar_rows,) = local_kernel(
+        scalars_kernel, "scalars", (place, shifts, shift_index, velocity), (), [(8, LANES)]
     )
     scalars = (place, scalar_rows)
-    blocks = swap_in_plane(blocks, 2)
-    halves, beside = [], []
-    for n in range(2):
-        first = n * chips_y
-        (half,) = local_kernel(
-            functools.partial(arrange_kernel, chips_y, first),
-            "arrange",
-            (place,),
-            blocks[first : first + chips_y],
-            [(2, HALO, ny, nz)],
-        )
-        pairs = []
-        for i in range(gx_size):
-            target = i + step if i % step != n else i - step
-            if 0 <= target < gx_size:
-                pairs.append((i, target))
-        halves.append(half)
-        beside.append(lax.ppermute(half, "gx", pairs))
 
     grid, rimmed = (count, ny, nz), (count, ny + 16, nz)
     f, r, w, v1, coarse = local_kernel(
-        functools.partial(pre_kernel, slabs, gy_size),
+        functools.partial(pre_kernel, slabs, chips_y),
         "pre",
         scalars,
-        (pool_matrix(0), pool_matrix(LANES // 2), *halves, *beside),
+        (pool_matrix(0), pool_matrix(LANES // 2), *parts),
         [grid, grid, grid, rimmed, (SLAB // 2, ny // 2, nz)],
         [rimmed, (SLAB, ny, nz), (2, SLAB // 2 * ny // 2, nz)],
     )

time: 59.8 us -> 61.9 us (1.035)
  starting transfers between devices: 25 us -> 26.9 us
  other arithmetic: 0.97 us -> 1.96 us
  waiting for transfers between devices: 24.2 us -> 23.3 us
    ppermute x10 -> x13, starting transfers between devices: 10.8 us -> 16.2 us  [swap_in_plane(): moved.append(lax.ppermute(pieces[k], ('gx', 'gy'), pairs))]
    ppermute x4 -> x3, waiting for transfers between devices: 8.89 us -> 4.09 us  [the longest x1 3.86 us: column_body(): beside = lax.ppermute(joined, 'gx', onward)]
    ppermute x4 -> x3, starting transfers between devices: 5.39 us -> 1.87 us  [the longest x1 1.28 us: column_body(): beside = lax.ppermute(joined, 'gx', onward)]
    ppermute x10 -> x13, waiting for transfers between devices: 11 us -> 13.6 us  [swap_in_plane(): moved.append(lax.ppermute(pieces[k], ('gx', 'gy'), pairs))]
    ppermute x6, waiting for transfers between devices: 4.39 us -> 5.6 us  [swap_slabs(): moved.append(lax.ppermute(piece, 'gx', pairs))]
    concatenate x0 -> x1, other arithmetic: none -> 0.99 us  [column_body(): joined = jnp.concatenate([source, reaction[None]])]
    pallas_call x7 -> x8, Pallas kernels: 7.68 us -> 8.24 us  [local_kernel(): pl.pallas_call(kernel, out_shape=[jax.ShapeDtypeStruct(shape, jnp.float32...]
  transfers between devices with their start and end apart: 20 -> 22, of which waited for: 12 -> 14; matrix products, arithmetic and copies ran while one was open for 0% -> 0% of each run, Pallas kernels for 4% -> 4%
where the time goes in v8:
time: 61.9 us; the launch traced here: 61.8 us
  starting transfers between devices  26.9 us (43%)
  waiting for transfers between devices  23.3 us (38%)
  Pallas kernels  8.24 us (13%)
  other arithmetic  1.96 us (3%)
  between operations  0.79 us (1%)
    ppermute x13, starting transfers between devices, swap_in_plane(): moved.append(lax.ppermute(pieces[k], ('gx', 'gy'), pairs))  16.2 us
    ppermute x13, waiting for transfers between devices, swap_in_plane(): moved.append(lax.ppermute(pieces[k], ('gx', 'gy'), pairs))  13.6 us
    ppermute x6, starting transfers between devices, swap_slabs(): moved.append(lax.ppermute(piece, 'gx', pairs))  8.84 us
    pallas_call x8, Pallas kernels, local_kernel(): pl.pallas_call(kernel, out_shape=[jax.ShapeDtypeStruct(shape, jnp.float32...  8.24 us
    ppermute x6, waiting for transfers between devices, swap_slabs(): moved.append(lax.ppermute(piece, 'gx', pairs))  5.6 us
    ppermute x1, waiting for transfers between devices, column_body(): beside = lax.ppermute(joined, 'gx', onward)  3.86 us
    ppermute x1, starting transfers between devices, column_body(): beside = lax.ppermute(joined, 'gx', onward)  1.28 us
  transfers between devices with their start and end apart: 22, of which 14 were waited for; matrix products, arithmetic and copies ran while one was open for 0% of the time, Pallas kernels for 4%

profile of v8, /device:TPU:0, one launch (start us, length us, event | category | flops | bytes accessed | tf_op | source)
XLA Modules:
  0.0 61.8 jit_solution(9609050008015665119)
XLA Ops:
  2.1 1.3 %collective-permute-start.4 = (f32[9,4,16,128]{3,2,1,0:T(8,128)S(1)}, f32[9,4,16,128]{3,2,1,0:T(8,128)S(1)}, u32[]{:S(2)}, u32[]{:S(2)}) collective-permute-start(f32[9,4,16,128]{3,2,1,0:T(8,128)S(1)} %pad_maximum_fusion.mine_ref), channel_id=1, source_target_pairs={{4,12},{8,0},{12,20},{16,8},{20,28},{24,16},{5,13},{9,1},{13,21},{... | collective-permute-start | bytes 884744 | tf_op jit(solution)/shard_map/ppermute | solution.py:478
  4.1 2.8 %collective-permute-start.1 = (f32[2,4,32,128]{3,2,1,0:T(8,128)S(1)}, f32[2,4,32,128]{3,2,1,0:T(8,128)S(1)}, u32[]{:S(2)}, u32[]{:S(2)}) collective-permute-start(f32[2,4,32,128]{3,2,1,0:T(8,128)S(1)} %get-tuple-element.27), channel_id=1, source_target_pairs={{0,2},{1,3},{2,0},{3,1},{4,6},{5,7},{6,4},{7,5},{8,10},{9,11},{10,... | collective-permute-start | bytes 393224 | tf_op jit(solution)/shard_map/ppermute | solution.py:440
  6.9 3.5 %collective-permute-start.2 = (f32[2,4,32,128]{3,2,1,0:T(8,128)S(1)}, f32[2,4,32,128]{3,2,1,0:T(8,128)S(1)}, u32[]{:S(2)}, u32[]{:S(2)}) collective-permute-start(f32[2,4,32,128]{3,2,1,0:T(8,128)S(1)} %get-tuple-element.28), channel_id=1, source_target_pairs={{0,4},{1,5},{2,6},{3,7},{4,0},{5,1},{6,2},{7,3},{8,12},{9,13},{10,... | collective-permute-start | bytes 393224 | tf_op jit(solution)/shard_map/ppermute | solution.py:440
  10.4 3.9 %collective-permute-done.4.block_ref.mine_ref = f32[9,4,16,128]{3,2,1,0:T(8,128)S(1)} collective-permute-done((f32[9,4,16,128]{3,2,1,0:T(8,128)S(1)}, f32[9,4,16,128]{3,2,1,0:T(8,128)S(1)}, u32[]{:S(2)}, u32[]{:S(2)}) %collective-permute-start.4) | collective-permute-done | bytes 294944 | tf_op jit(solution)/shard_map/ppermute | solution.py:478
  14.7 2.0 %collective-permute-done.3.refs_2_.refs_5_ = f32[2,4,32,128]{3,2,1,0:T(8,128)S(1)} collective-permute-done((f32[2,4,32,128]{3,2,1,0:T(8,128)S(1)}, f32[2,4,32,128]{3,2,1,0:T(8,128)S(1)}, u32[]{:S(2)}, u32[]{:S(2)}) %collective-permute-start.3) | collective-permute-done | bytes 131104 | tf_op jit(solution)/shard_map/ppermute | solution.py:440
  19.4 1.6 %collective-permute-start.6 = (f32[2,4,32,128]{3,2,1,0:T(8,128)S(1)}, f32[2,4,32,128]{3,2,1,0:T(8,128)S(1)}, u32[]{:S(2)}, u32[]{:S(2)}) collective-permute-start(f32[2,4,32,128]{3,2,1,0:T(8,128)S(1)} %get-tuple-element.31), channel_id=1, source_target_pairs={{0,2},{1,3},{2,0},{3,1},{4,6},{5,7},{6,4},{7,5},{8,10},{9,11},{10,... | collective-permute-start | bytes 393224 | tf_op jit(solution)/shard_map/ppermute | solution.py:440
  21.0 1.7 %collective-permute-start.7 = (f32[2,4,32,128]{3,2,1,0:T(8,128)S(1)}, f32[2,4,32,128]{3,2,1,0:T(8,128)S(1)}, u32[]{:S(2)}, u32[]{:S(2)}) collective-permute-start(f32[2,4,32,128]{3,2,1,0:T(8,128)S(1)} %get-tuple-element.32), channel_id=1, source_target_pairs={{0,4},{1,5},{2,6},{3,7},{4,0},{5,1},{6,2},{7,3},{8,12},{9,13},{10,... | collective-permute-start | bytes 393224 | tf_op jit(solution)/shard_map/ppermute | solution.py:440
  23.1 1.9 %collective-permute-done.6.refs_7_ = f32[2,4,32,128]{3,2,1,0:T(8,128)S(1)} collective-permute-done((f32[2,4,32,128]{3,2,1,0:T(8,128)S(1)}, f32[2,4,32,128]{3,2,1,0:T(8,128)S(1)}, u32[]{:S(2)}, u32[]{:S(2)}) %collective-permute-start.6) | collective-permute-done | bytes 131104 | tf_op jit(solution)/shard_map/ppermute | solution.py:440
  25.0 2.4 %collective-permute-done.7.refs_8_ = f32[2,4,32,128]{3,2,1,0:T(8,128)S(1)} collective-permute-done((f32[2,4,32,128]{3,2,1,0:T(8,128)S(1)}, f32[2,4,32,128]{3,2,1,0:T(8,128)S(1)}, u32[]{:S(2)}, u32[]{:S(2)}) %collective-permute-start.7) | collective-permute-done | bytes 131104 | tf_op jit(solution)/shard_map/ppermute | solution.py:440
  27.4 1.6 %collective-permute-done.8.refs_9_ = f32[2,4,32,128]{3,2,1,0:T(8,128)S(1)} collective-permute-done((f32[2,4,32,128]{3,2,1,0:T(8,128)S(1)}, f32[2,4,32,128]{3,2,1,0:T(8,128)S(1)}, u32[]{:S(2)}, u32[]{:S(2)}) %collective-permute-start.8) | collective-permute-done | bytes 131104 | tf_op jit(solution)/shard_map/ppermute | solution.py:440
  29.0 1.4 %pre.1 = (f32[16,64,128]{2,1,0:T(8,128)S(1)}, f32[16,64,128]{2,1,0:T(8,128)S(1)}, f32[16,64,128]{2,1,0:T(8,128)S(1)}, f32[16,80,128]{2,1,0:T(8,128)S(1)}, f32[4,32,128]{2,1,0:T(8,128)S(1)}) custom-call(s32[2]{0:T(128)S(1)} %pad_add_fusion.place_ref, f32[8,128]{1,0:T(8,128)S(1)} %scalars.1.scalar_ref, bf16[128,128]{1,0:T(8,128)(2,1)S(1)} %get-tuple-element.51.refs_0_, ...), custom_call_target="tpu_custom_call" | custom-call | tf_op jit(solution)/shard_map/pre/pallas_call | solution.py:424
  30.4 2.8 %collective-permute-start.11 = (f32[4,32,128]{2,1,0:T(8,128)S(1)}, f32[4,32,128]{2,1,0:T(8,128)S(1)}, u32[]{:S(2)}, u32[]{:S(2)}) collective-permute-start(f32[4,32,128]{2,1,0:T(8,128)S(1)} %get-tuple-element.38.refs_6_), channel_id=1, source_target_pairs={{0,24},{4,28},{8,16},{12,20},{16,8},{20,12},{24,0},{28,4},{1,25},{... | collective-permute-start | bytes 196616 | tf_op jit(solution)/shard_map/ppermute | solution.py:449
  33.5 1.4 %collective-permute-start.9 = (f32[4,32,128]{2,1,0:T(8,128)S(1)}, f32[4,32,128]{2,1,0:T(8,128)S(1)}, u32[]{:S(2)}, u32[]{:S(2)}) collective-permute-start(f32[4,32,128]{2,1,0:T(8,128)S(1)} %get-tuple-element.38.refs_6_), channel_id=1, source_target_pairs={{0,8},{4,12},{8,0},{12,4},{16,24},{20,28},{24,16},{28,20},{1,9},{5... | collective-permute-start | bytes 196616 | tf_op jit(solution)/shard_map/ppermute | solution.py:449
  34.9 2.1 %collective-permute-done.11.refs_9_ = f32[4,32,128]{2,1,0:T(8,128)S(1)} collective-permute-done((f32[4,32,128]{2,1,0:T(8,128)S(1)}, f32[4,32,128]{2,1,0:T(8,128)S(1)}, u32[]{:S(2)}, u32[]{:S(2)}) %collective-permute-start.11) | collective-permute-done | bytes 65568 | tf_op jit(solution)/shard_map/ppermute | solution.py:449
  37.0 2.2 %collective-permute-done.10.refs_8_ = f32[4,32,128]{2,1,0:T(8,128)S(1)} collective-permute-done((f32[4,32,128]{2,1,0:T(8,128)S(1)}, f32[4,32,128]{2,1,0:T(8,128)S(1)}, u32[]{:S(2)}, u32[]{:S(2)}) %collective-permute-start.10) | collective-permute-done | bytes 65568 | tf_op jit(solution)/shard_map/ppermute | solution.py:449
  39.3 3.2 %post.1 = (f32[136,128]{1,0:T(8,128)S(1)}, f32[136,128]{1,0:T(8,128)S(1)}, f32[136,128]{1,0:T(8,128)S(1)}, f32[136,128]{1,0:T(8,128)S(1)}, f32[136,128]{1,0:T(8,...) custom-call(s32[2]{0:T(128)S(1)} %pad_add_fusion.place_ref, ...), custom_call_target="tpu_custom_call" | custom-call | tf_op jit(solution)/shard_map/post/pallas_call | solution.py:424
  42.5 1.6 %collective-permute-start.13 = (f32[136,128]{1,0:T(8,128)S(1)}, f32[136,128]{1,0:T(8,128)S(1)}, u32[]{:S(2)}, u32[]{:S(2)}) collective-permute-start(f32[136,128]{1,0:T(8,128)S(1)} %get-tuple-element.41), channel_id=1, source_target_pairs={{0,2},{1,3},{2,0},{3,1},{4,6},{5,7},{6,4},{7,5},{8,10},{9,11},{10,... | collective-permute-start | bytes 208904 | tf_op jit(solution)/shard_map/ppermute | solution.py:440
  44.4 1.4 %collective-permute-start.15 = (f32[136,128]{1,0:T(8,128)S(1)}, f32[136,128]{1,0:T(8,128)S(1)}, u32[]{:S(2)}, u32[]{:S(2)}) collective-permute-start(f32[136,128]{1,0:T(8,128)S(1)} %get-tuple-element.43), channel_id=1, source_target_pairs={{0,4},{1,5},{2,6},{3,7},{4,0},{5,1},{6,2},{7,3},{8,12},{9,13},{10,... | collective-permute-start | bytes 208904 | tf_op jit(solution)/shard_map/ppermute | solution.py:440
  46.1 2.2 %collective-permute-start.17 = (f32[136,128]{1,0:T(8,128)S(1)}, f32[136,128]{1,0:T(8,128)S(1)}, u32[]{:S(2)}, u32[]{:S(2)}) collective-permute-start(f32[136,128]{1,0:T(8,128)S(1)} %get-tuple-element.45), channel_id=1, source_target_pairs={{0,6},{1,7},{2,4},{3,5},{4,2},{5,3},{6,0},{7,1},{8,14},{9,15},{10,... | collective-permute-start | bytes 208904 | tf_op jit(solution)/shard_map/ppermute | solution.py:440
  48.9 1.2 %collective-permute-done.16.refs_5_ = f32[136,128]{1,0:T(8,128)S(1)} collective-permute-done((f32[136,128]{1,0:T(8,128)S(1)}, f32[136,128]{1,0:T(8,128)S(1)}, u32[]{:S(2)}, u32[]{:S(2)}) %collective-permute-start.16) | collective-permute-done | bytes 69664 | tf_op jit(solution)/shard_map/ppermute | solution.py:440
  50.1 2.8 %collective-permute-done.17.refs_6_ = f32[136,128]{1,0:T(8,128)S(1)} collective-permute-done((f32[136,128]{1,0:T(8,128)S(1)}, f32[136,128]{1,0:T(8,128)S(1)}, u32[]{:S(2)}, u32[]{:S(2)}) %collective-permute-start.17) | collective-permute-done | bytes 69664 | tf_op jit(solution)/shard_map/ppermute | solution.py:440
  54.0 2.5 %collective-permute-start.21 = (f32[8,128]{1,0:T(8,128)S(1)}, f32[8,128]{1,0:T(8,128)S(1)}, u32[]{:S(2)}, u32[]{:S(2)}) collective-permute-start(f32[8,128]{1,0:T(8,128)S(1)} %squares.1), channel_id=1, source_target_pairs={{0,24},{4,28},{8,16},{12,20},{16,8},{20,12},{24,0},{28,4},{1,25},{... | collective-permute-start | bytes 12296 | tf_op jit(solution)/shard_map/ppermute | solution.py:449
  56.5 1.9 %collective-permute-start.19 = (f32[8,128]{1,0:T(8,128)S(1)}, f32[8,128]{1,0:T(8,128)S(1)}, u32[]{:S(2)}, u32[]{:S(2)}) collective-permute-start(f32[8,128]{1,0:T(8,128)S(1)} %squares.1), channel_id=1, source_target_pairs={{0,8},{4,12},{8,0},{12,4},{16,24},{20,28},{24,16},{28,20},{1,9},{5... | collective-permute-start | bytes 12296 | tf_op jit(solution)/shard_map/ppermute | solution.py:449
  58.4 1.4 %collect.1 = (f32[8,4,16,128]{3,2,1,0:T(8,128)}, f32[8,4,16,128]{3,2,1,0:T(8,128)}) custom-call(s32[2]{0:T(128)S(1)} %pad_add_fusion.place_ref, f32[136,128]{1,0:T(8,128)S(1)} %get-tuple-element.39.refs_0_, f32[136,128]{1,0:T(8,128)S(1)} %collective-permute-done.12.refs_1_, f32[136,128]{1,0:T(8,128)S(1)} %collective-permute-done.13.refs_2_, ...), custom_call_target="tpu_custom_call" | custom-call | tf_op jit(solution)/shard_map/collect/pallas_call | solution.py:424
  (43 shorter events, 10.2 us)
Async XLA Ops:
  1.6 1.9 %collective-permute-start = (f32[9,4,16,128]{3,2,1,0:T(8,128)S(1)}, f32[9,4,16,128]{3,2,1,0:T(8,128)S(1)}, u32[]{:S(2)}, u32[]{:S(2)}) collective-permute-start(f32[9,4,16,128]{3,2,1,0:T(8,128)S(1)} %pad_maximum_fusion.mine_ref), channel_id=1, source_target_pairs={{0,1},{1,0},{2,3},{3,2},{4,5},{5,4},{6,7},{7,6},{8,9},{9,8},{10,11... | collective-permute-start | bytes 884744 | tf_op jit(solution)/shard_map/ppermute | solution.py:471
  2.1 12.1 %collective-permute-start.4 = (f32[9,4,16,128]{3,2,1,0:T(8,128)S(1)}, f32[9,4,16,128]{3,2,1,0:T(8,128)S(1)}, u32[]{:S(2)}, u32[]{:S(2)}) collective-permute-start(f32[9,4,16,128]{3,2,1,0:T(8,128)S(1)} %pad_maximum_fusion.mine_ref), channel_id=1, source_target_pairs={{4,12},{8,0},{12,20},{16,8},{20,28},{24,16},{5,13},{9,1},{13,21},{... | collective-permute-start | bytes 884744 | tf_op jit(solution)/shard_map/ppermute | solution.py:478
  4.1 10.2 %collective-permute-start.1 = (f32[2,4,32,128]{3,2,1,0:T(8,128)S(1)}, f32[2,4,32,128]{3,2,1,0:T(8,128)S(1)}, u32[]{:S(2)}, u32[]{:S(2)}) collective-permute-start(f32[2,4,32,128]{3,2,1,0:T(8,128)S(1)} %get-tuple-element.27), channel_id=1, source_target_pairs={{0,2},{1,3},{2,0},{3,1},{4,6},{5,7},{6,4},{7,5},{8,10},{9,11},{10,... | collective-permute-start | bytes 393224 | tf_op jit(solution)/shard_map/ppermute | solution.py:440
  6.9 7.8 %collective-permute-start.2 = (f32[2,4,32,128]{3,2,1,0:T(8,128)S(1)}, f32[2,4,32,128]{3,2,1,0:T(8,128)S(1)}, u32[]{:S(2)}, u32[]{:S(2)}) collective-permute-start(f32[2,4,32,128]{3,2,1,0:T(8,128)S(1)} %get-tuple-element.28), channel_id=1, source_target_pairs={{0,4},{1,5},{2,6},{3,7},{4,0},{5,1},{6,2},{7,3},{8,12},{9,13},{10,... | collective-permute-start | bytes 393224 | tf_op jit(solution)/shard_map/ppermute | solution.py:440
  10.4 6.3 %collective-permute-start.3 = (f32[2,4,32,128]{3,2,1,0:T(8,128)S(1)}, f32[2,4,32,128]{3,2,1,0:T(8,128)S(1)}, u32[]{:S(2)}, u32[]{:S(2)}) collective-permute-start(f32[2,4,32,128]{3,2,1,0:T(8,128)S(1)} %get-tuple-element.29), channel_id=1, source_target_pairs={{0,6},{1,7},{2,4},{3,5},{4,2},{5,3},{6,0},{7,1},{8,14},{9,15},{10,... | collective-permute-start | bytes 393224 | tf_op jit(solution)/shard_map/ppermute | solution.py:440
  17.3 0.7 %copy-start.1 = (s32[8]{0:T(128)S(1)}, s32[8]{0:T(128)}, u32[]{:S(2)}) copy-start(s32[8]{0:T(128)} %index_ref.1) | copy-start | bytes 100
  17.3 0.7 %copy-start.2 = (f32[3]{0:T(128)S(1)}, f32[3]{0:T(128)}, u32[]{:S(2)}) copy-start(f32[3]{0:T(128)} %velocity_ref.1) | copy-start | bytes 40
  17.4 1.5 %collective-permute-start.5 = (f32[5,4,16,128]{3,2,1,0:T(8,128)S(1)}, f32[5,4,16,128]{3,2,1,0:T(8,128)S(1)}, u32[]{:S(2)}, u32[]{:S(2)}) collective-permute-start(f32[5,4,16,128]{3,2,1,0:T(8,128)S(1)} %pack.1), channel_id=1, source_target_pairs={{0,1},{1,0},{2,3},{3,2},{4,5},{5,4},{6,7},{7,6},{8,9},{9,8},{10,11... | collective-permute-start | bytes 491528 | tf_op jit(solution)/shard_map/ppermute | solution.py:471
  19.4 5.6 %collective-permute-start.6 = (f32[2,4,32,128]{3,2,1,0:T(8,128)S(1)}, f32[2,4,32,128]{3,2,1,0:T(8,128)S(1)}, u32[]{:S(2)}, u32[]{:S(2)}) collective-permute-start(f32[2,4,32,128]{3,2,1,0:T(8,128)S(1)} %get-tuple-element.31), channel_id=1, source_target_pairs={{0,2},{1,3},{2,0},{3,1},{4,6},{5,7},{6,4},{7,5},{8,10},{9,11},{10,... | collective-permute-start | bytes 393224 | tf_op jit(solution)/shard_map/ppermute | solution.py:440
  21.0 6.4 %collective-permute-start.7 = (f32[2,4,32,128]{3,2,1,0:T(8,128)S(1)}, f32[2,4,32,128]{3,2,1,0:T(8,128)S(1)}, u32[]{:S(2)}, u32[]{:S(2)}) collective-permute-start(f32[2,4,32,128]{3,2,1,0:T(8,128)S(1)} %get-tuple-element.32), channel_id=1, source_target_pairs={{0,4},{1,5},{2,6},{3,7},{4,0},{5,1},{6,2},{7,3},{8,12},{9,13},{10,... | collective-permute-start | bytes 393224 | tf_op jit(solution)/shard_map/ppermute | solution.py:440
  22.7 6.3 %collective-permute-start.8 = (f32[2,4,32,128]{3,2,1,0:T(8,128)S(1)}, f32[2,4,32,128]{3,2,1,0:T(8,128)S(1)}, u32[]{:S(2)}, u32[]{:S(2)}) collective-permute-start(f32[2,4,32,128]{3,2,1,0:T(8,128)S(1)} %get-tuple-element.33), channel_id=1, source_target_pairs={{0,6},{1,7},{2,4},{3,5},{4,2},{5,3},{6,0},{7,1},{8,14},{9,15},{10,... | collective-permute-start | bytes 393224 | tf_op jit(solution)/shard_map/ppermute | solution.py:440
  30.4 6.6 %collective-permute-start.11 = (f32[4,32,128]{2,1,0:T(8,128)S(1)}, f32[4,32,128]{2,1,0:T(8,128)S(1)}, u32[]{:S(2)}, u32[]{:S(2)}) collective-permute-start(f32[4,32,128]{2,1,0:T(8,128)S(1)} %get-tuple-element.38.refs_6_), channel_id=1, source_target_pairs={{0,24},{4,28},{8,16},{12,20},{16,8},{20,12},{24,0},{28,4},{1,25},{... | collective-permute-start | bytes 196616 | tf_op jit(solution)/shard_map/ppermute | solution.py:449
  33.2 6.0 %collective-permute-start.10 = (f32[4,32,128]{2,1,0:T(8,128)S(1)}, f32[4,32,128]{2,1,0:T(8,128)S(1)}, u32[]{:S(2)}, u32[]{:S(2)}) collective-permute-start(f32[4,32,128]{2,1,0:T(8,128)S(1)} %get-tuple-element.38.refs_6_), channel_id=1, source_target_pairs={{0,16},{4,20},{8,24},{12,28},{16,0},{20,4},{24,8},{28,12},{1,17},{... | collective-permute-start | bytes 196616 | tf_op jit(solution)/shard_map/ppermute | solution.py:449
  33.5 5.8 %collective-permute-start.9 = (f32[4,32,128]{2,1,0:T(8,128)S(1)}, f32[4,32,128]{2,1,0:T(8,128)S(1)}, u32[]{:S(2)}, u32[]{:S(2)}) collective-permute-start(f32[4,32,128]{2,1,0:T(8,128)S(1)} %get-tuple-element.38.refs_6_), channel_id=1, source_target_pairs={{0,8},{4,12},{8,0},{12,4},{16,24},{20,28},{24,16},{28,20},{1,9},{5... | collective-permute-start | bytes 196616 | tf_op jit(solution)/shard_map/ppermute | solution.py:449
  42.5 3.6 %collective-permute-start.12 = (f32[136,128]{1,0:T(8,128)S(1)}, f32[136,128]{1,0:T(8,128)S(1)}, u32[]{:S(2)}, u32[]{:S(2)}) collective-permute-start(f32[136,128]{1,0:T(8,128)S(1)} %get-tuple-element.40), channel_id=1, source_target_pairs={{0,1},{1,0},{2,3},{3,2},{4,5},{5,4},{6,7},{7,6},{8,9},{9,8},{10,11... | collective-permute-start | bytes 208904 | tf_op jit(solution)/shard_map/ppermute | solution.py:440
  42.5 5.8 %collective-permute-start.13 = (f32[136,128]{1,0:T(8,128)S(1)}, f32[136,128]{1,0:T(8,128)S(1)}, u32[]{:S(2)}, u32[]{:S(2)}) collective-permute-start(f32[136,128]{1,0:T(8,128)S(1)} %get-tuple-element.41), channel_id=1, source_target_pairs={{0,2},{1,3},{2,0},{3,1},{4,6},{5,7},{6,4},{7,5},{8,10},{9,11},{10,... | collective-permute-start | bytes 208904 | tf_op jit(solution)/shard_map/ppermute | solution.py:440
  44.1 4.7 %collective-permute-start.14 = (f32[136,128]{1,0:T(8,128)S(1)}, f32[136,128]{1,0:T(8,128)S(1)}, u32[]{:S(2)}, u32[]{:S(2)}) collective-permute-start(f32[136,128]{1,0:T(8,128)S(1)} %get-tuple-element.42), channel_id=1, source_target_pairs={{0,3},{1,2},{2,1},{3,0},{4,7},{5,6},{6,5},{7,4},{8,11},{9,10},{10,... | collective-permute-start | bytes 208904 | tf_op jit(solution)/shard_map/ppermute | solution.py:440
  44.4 4.5 %collective-permute-start.15 = (f32[136,128]{1,0:T(8,128)S(1)}, f32[136,128]{1,0:T(8,128)S(1)}, u32[]{:S(2)}, u32[]{:S(2)}) collective-permute-start(f32[136,128]{1,0:T(8,128)S(1)} %get-tuple-element.43), channel_id=1, source_target_pairs={{0,4},{1,5},{2,6},{3,7},{4,0},{5,1},{6,2},{7,3},{8,12},{9,13},{10,... | collective-permute-start | bytes 208904 | tf_op jit(solution)/shard_map/ppermute | solution.py:440
  45.8 4.4 %collective-permute-start.16 = (f32[136,128]{1,0:T(8,128)S(1)}, f32[136,128]{1,0:T(8,128)S(1)}, u32[]{:S(2)}, u32[]{:S(2)}) collective-permute-start(f32[136,128]{1,0:T(8,128)S(1)} %get-tuple-element.44), channel_id=1, source_target_pairs={{0,5},{1,4},{2,7},{3,6},{4,1},{5,0},{6,3},{7,2},{8,13},{9,12},{10,... | collective-permute-start | bytes 208904 | tf_op jit(solution)/shard_map/ppermute | solution.py:440
  46.1 6.9 %collective-permute-start.17 = (f32[136,128]{1,0:T(8,128)S(1)}, f32[136,128]{1,0:T(8,128)S(1)}, u32[]{:S(2)}, u32[]{:S(2)}) collective-permute-start(f32[136,128]{1,0:T(8,128)S(1)} %get-tuple-element.45), channel_id=1, source_target_pairs={{0,6},{1,7},{2,4},{3,5},{4,2},{5,3},{6,0},{7,1},{8,14},{9,15},{10,... | collective-permute-start | bytes 208904 | tf_op jit(solution)/shard_map/ppermute | solution.py:440
  48.3 5.7 %collective-permute-start.18 = (f32[136,128]{1,0:T(8,128)S(1)}, f32[136,128]{1,0:T(8,128)S(1)}, u32[]{:S(2)}, u32[]{:S(2)}) collective-permute-start(f32[136,128]{1,0:T(8,128)S(1)} %get-tuple-element.46), channel_id=1, source_target_pairs={{0,7},{1,6},{2,5},{3,4},{4,3},{5,2},{6,1},{7,0},{8,15},{9,14},{10,... | collective-permute-start | bytes 208904 | tf_op jit(solution)/shard_map/ppermute | solution.py:440
  54.0 5.8 %collective-permute-start.21 = (f32[8,128]{1,0:T(8,128)S(1)}, f32[8,128]{1,0:T(8,128)S(1)}, u32[]{:S(2)}, u32[]{:S(2)}) collective-permute-start(f32[8,128]{1,0:T(8,128)S(1)} %squares.1), channel_id=1, source_target_pairs={{0,24},{4,28},{8,16},{12,20},{16,8},{20,12},{24,0},{28,4},{1,25},{... | collective-permute-start | bytes 12296 | tf_op jit(solution)/shard_map/ppermute | solution.py:449
  56.5 4.5 %collective-permute-start.20 = (f32[8,128]{1,0:T(8,128)S(1)}, f32[8,128]{1,0:T(8,128)S(1)}, u32[]{:S(2)}, u32[]{:S(2)}) collective-permute-start(f32[8,128]{1,0:T(8,128)S(1)} %squares.1), channel_id=1, source_target_pairs={{0,16},{4,20},{8,24},{12,28},{16,0},{20,4},{24,8},{28,12},{1,17},{... | collective-permute-start | bytes 12296 | tf_op jit(solution)/shard_map/ppermute | solution.py:449
  56.5 4.5 %collective-permute-start.19 = (f32[8,128]{1,0:T(8,128)S(1)}, f32[8,128]{1,0:T(8,128)S(1)}, u32[]{:S(2)}, u32[]{:S(2)}) collective-permute-start(f32[8,128]{1,0:T(8,128)S(1)} %squares.1), channel_id=1, source_target_pairs={{0,8},{4,12},{8,0},{12,4},{16,24},{20,28},{24,16},{28,20},{1,9},{5... | collective-permute-start | bytes 12296 | tf_op jit(solution)/shard_map/ppermute | solution.py:449
  (1 other events, 0.7 us)

commit v9 on v7

--- a/solution.py
+++ b/solution.py
@@ -232,37 +232,49 @@
     return jnp.where(col // 2 == row, 1.0, 0.0).astype(jnp.bfloat16)
 
 
+def keep_kernel(place_ref, source_ref, out_ref):
+    for n in range(out_ref.shape[0]):
+        out_ref[n] = source_ref[2 * n + (place_ref[0] & 1)]
+
+
 def merge_kernel(place_ref, shifts_ref, index_ref, velocity_ref, *refs):
-    source_ref, reaction_ref, other_source_ref, other_reaction_ref = refs[:4]
+    mine_ref, theirs_ref, reaction_ref, beside_ref = refs[:4]
     out_refs, scalar_ref = refs[4:-1], refs[-1]
     chip, core = place_ref[0] // 2, place_ref[0] & 1
-    by = source_ref.shape[2]
+    by = mine_ref.shape[2]
     mine = pl.ds(pl.multiple_of(core * by, 8), by)
     theirs = pl.ds(pl.multiple_of((1 - core) * by, 8), by)
     for m, out_ref in enumerate(out_refs):
-        column = 2 * jnp.bitwise_xor(chip, m) + core
-        out_ref[0, :, mine, :] = source_ref[column]
-        out_ref[0, :, theirs, :] = other_source_ref[column]
-        out_ref[1, :, mine, :] = reaction_ref[...]
-        out_ref[1, :, theirs, :] = other_reaction_ref[...]
+        target = jnp.bitwise_xor(chip, m)
+        out_ref[:, mine, :] = mine_ref[target]
+        out_ref[:, theirs, :] = theirs_ref[2 * target + core]
+        out_ref[:, pl.ds(2 * by, by), :] = reaction_ref[...]
+        out_ref[:, pl.ds(3 * by, by), :] = beside_ref[...]
     scalars = [shifts_ref[index_ref[place_ref[0]]]] + [velocity_ref[d] for d in range(3)]
     for n, scalar in enumerate(scalars):
         scalar_ref[pl.ds(n, 1), :] = jnp.full((1, LANES), scalar, jnp.float32)
 
 
-def arrange_kernel(chips_y, first, place_ref, *refs):
-    half_ref = refs[-1]
-    for m, block in enumerate(refs[:-1]):
-        owner = jnp.bitwise_xor(place_ref[0] // 2, first + m)
-        size = block.shape[2]
-        rows = pl.ds(pl.multiple_of(lax.rem(owner, chips_y) * size, 8), size)
-        half_ref[:, :, rows, :] = block[...]
-
-
-def pre_kernel(slabs, gy_size, place_ref, scalar_ref, *refs):
+def arrange_kernel(chips_y, place_ref, *refs):
+    blocks, (first_ref, second_ref, reaction_ref, halves) = refs[:-4], refs[-4:]
+    by = blocks[0].shape[1] // 4
+    for m, block in enumerate(blocks):
+        owner = jnp.bitwise_xor(place_ref[0] // 2, m)
+        x, y = owner // chips_y, lax.rem(owner, chips_y)
+        rows = pl.ds(pl.multiple_of(2 * y * by, 8), 2 * by)
+        halves[x, :, rows, :] = block[:, pl.ds(0, 2 * by), :]
+        rows = pl.ds(pl.multiple_of(y * by, 8), by)
+        reaction_ref[pl.ds(HALO * (1 + x), HALO), rows, :] = block[:, pl.ds(2 * by, by), :]
+        reaction_ref[pl.ds((HALO + SLAB) * (1 - x), HALO), rows, :] = block[:, pl.ds(3 * by, by), :]
+    even = 1 - (place_ref[1] & 1)
+    first_ref[...] = halves[even]
+    second_ref[...] = halves[1 - even]
+
+
+def pre_kernel(slabs, gy_size, by, place_ref, scalar_ref, *refs):
     pool_ref, pool_up_ref = refs[:2]
-    parts = refs[2:6]
-    f, r, w, v1, coarse_ref, v0, tmp, pooled = refs[6:]
+    parts, reactions = refs[2:6], refs[6:8]
+    f, r, w, v1, coarse_ref, v0, tmp, pooled = refs[8:]
     ny = f.shape[1]
     slab = place_ref[1]
     fine = Level(0, ny, LANES, 0, scalar_ref, f, r, w)
@@ -273,11 +285,15 @@
     inside += [DAMPING] * SLAB
     inside += [jnp.where(slab < slabs - 1, DAMPING, 0.0)] * HALO
 
-    x = place_ref[0] // gy_size
-    firsts = (HALO * (1 + x), HALO * (2 - x), (HALO + SLAB) * (1 - x), (HALO + SLAB) * x)
+    even = 1 - (slab & 1)
+    firsts = (HALO * (1 + even), HALO * (2 - even), (HALO + SLAB) * even, (HALO + SLAB) * (1 - even))
     for part, first in zip(parts, firsts):
-        f[pl.ds(first, HALO)] = part[0]
-        r[pl.ds(first, HALO)] = part[1]
+        f[pl.ds(first, HALO)] = part[...]
+    core = place_ref[0] & 1
+    for n, reaction in enumerate(reactions):
+        for y in range(gy_size // 2):
+            to = pl.multiple_of((2 * y + jnp.bitwise_xor(core, n)) * by, 8)
+            r[:, pl.ds(to, by), :] = reaction[:, pl.ds(y * by, by), :]
 
     def put(x, weight):
         w[x] = weight
@@ -461,40 +477,46 @@
 
     chips, chips_y = columns // 2, gy_size // 2
     cores = [(i, i ^ 1) for i in range(gy_size)]
-    others = [lax.ppermute(source, "gy", cores), lax.ppermute(reaction, "gy", cores)]
+    onward = [(i, i + step if i % step else i - step) for i in range(gx_size)]
+    onward = [(i, j) for i, j in onward if 0 <= j < gx_size]
+    theirs = lax.ppermute(source, "gy", cores)
+    reaction_beside = lax.ppermute(reaction, "gx", onward)
+    (mine,) = local_kernel(keep_kernel, "keep", (place,), (source,), [(chips, bx, by, nz)])
     *blocks, scalar_rows = local_kernel(
         merge_kernel,
         "merge",
         (place, shifts, shift_index, velocity),
-        (source, reaction, *others),
-        [(2, bx, 2 * by, nz)] * chips + [(8, LANES)],
+        (mine, theirs, reaction, reaction_beside),
+        [(bx, 4 * by, nz)] * chips + [(8, LANES)],
     )
     scalars = (place, scalar_rows)
     blocks = swap_in_plane(blocks, 2)
-    halves, beside = [], []
-    for n in range(2):
-        first = n * chips_y
-        (half,) = local_kernel(
-            functools.partial(arrange_kernel, chips_y, first),
-            "arrange",
-            (place,),
-            blocks[first : first + chips_y],
-            [(2, HALO, ny, nz)],
-        )
+
+    half = (HALO, ny, nz)
+    *halves, rows = local_kernel(
+        functools.partial(arrange_kernel, chips_y),
+        "arrange",
+        (place,),
+        blocks,
+        [half, half, (count, ny // 2, nz)],
+        [(2, *half)],
+    )
+    beside = []
+    for n, half in enumerate(halves):
         pairs = []
         for i in range(gx_size):
-            target = i + step if i % step != n else i - step
-            if 0 <= target < gx_size:
-                pairs.append((i, target))
-        halves.append(half)
+            j = i + step if i // step % 2 == n else i - step
+            if 0 <= j < gx_size:
+                pairs.append((i, j))
         beside.append(lax.ppermute(half, "gx", pairs))
+    reactions = [rows, lax.ppermute(rows, "gy", cores)]
 
     grid, rimmed = (count, ny, nz), (count, ny + 16, nz)
     f, r, w, v1, coarse = local_kernel(
-        functools.partial(pre_kernel, slabs, gy_size),
+        functools.partial(pre_kernel, slabs, gy_size, by),
         "pre",
         scalars,
-        (pool_matrix(0), pool_matrix(LANES // 2), *halves, *beside),
+        (pool_matrix(0), pool_matrix(LANES // 2), *halves, *beside, *reactions),
         [grid, grid, grid, rimmed, (SLAB // 2, ny // 2, nz)],
         [rimmed, (SLAB, ny, nz), (2, SLAB // 2 * ny // 2, nz)],
     )

time: 59.8 us -> 60.1 us (level)
    ppermute x2, waiting for transfers between devices: 7.63 us -> 3.3 us  [column_body(): beside.append(lax.ppermute(half, 'gx', pairs))]
    ppermute x2 -> x3, waiting for transfers between devices: 1.26 us -> 3.84 us  [the longest x1 3.83 us: column_body(): reaction_beside = lax.ppermute(reaction, 'gx', onward)]
    ppermute x2, starting transfers between devices: 4.79 us -> 2.53 us  [column_body(): beside.append(lax.ppermute(half, 'gx', pairs))]
    ppermute x6, waiting for transfers between devices: 4.39 us -> 6.35 us  [swap_slabs(): moved.append(lax.ppermute(piece, 'gx', pairs))]
    ppermute x6, starting transfers between devices: 8.84 us -> 10.6 us  [swap_slabs(): moved.append(lax.ppermute(piece, 'gx', pairs))]
    ppermute x2 -> x3, starting transfers between devices: 0.6 us -> 1.87 us  [the longest x1 1.28 us: column_body(): reaction_beside = lax.ppermute(reaction, 'gx', onward)]
    ppermute x10, starting transfers between devices: 10.8 us -> 9.88 us  [swap_in_plane(): moved.append(lax.ppermute(pieces[k], ('gx', 'gy'), pairs))]
  transfers between devices with their start and end apart: 20 -> 21, of which waited for: 12 -> 12; matrix products, arithmetic and copies ran while one was open for 0% -> 0% of each run, Pallas kernels for 4% -> 3%
where the time goes in v9:
time: 60.1 us; the launch traced here: 59.9 us
  starting transfers between devices  24.9 us (41%)
  waiting for transfers between devices  24.5 us (41%)
  Pallas kernels  7.78 us (13%)
  other arithmetic  0.97 us (2%)
  local copies, waits for them, and re-layouts  0.96 us (2%)
  between operations  0.78 us (1%)
    ppermute x10, waiting for transfers between devices, swap_in_plane(): moved.append(lax.ppermute(pieces[k], ('gx', 'gy'), pairs))  11 us
    ppermute x6, starting transfers between devices, swap_slabs(): moved.append(lax.ppermute(piece, 'gx', pairs))  10.6 us
    ppermute x10, starting transfers between devices, swap_in_plane(): moved.append(lax.ppermute(pieces[k], ('gx', 'gy'), pairs))  9.88 us
    pallas_call x7, Pallas kernels, local_kernel(): pl.pallas_call(kernel, out_shape=[jax.ShapeDtypeStruct(shape, jnp.float32...  7.78 us
    ppermute x6, waiting for transfers between devices, swap_slabs(): moved.append(lax.ppermute(piece, 'gx', pairs))  6.35 us
    ppermute x1, waiting for transfers between devices, column_body(): reaction_beside = lax.ppermute(reaction, 'gx', onward)  3.83 us
    ppermute x2, waiting for transfers between devices, column_body(): beside.append(lax.ppermute(half, 'gx', pairs))  3.3 us
    ppermute x2, starting transfers between devices, column_body(): beside.append(lax.ppermute(half, 'gx', pairs))  2.53 us
  transfers between devices with their start and end apart: 21, of which 12 were waited for; matrix products, arithmetic and copies ran while one was open for 0% of the time, Pallas kernels for 3%

profile of v9, /device:TPU:0, one launch (start us, length us, event | category | flops | bytes accessed | tf_op | source)
XLA Modules:
  0.0 59.9 jit_solution(8267976007813358624)
XLA Ops:
  1.1 1.3 %collective-permute-start.1 = (f32[4,16,128]{2,1,0:T(8,128)}, f32[4,16,128]{2,1,0:T(8,128)S(1)}, u32[]{:S(2)}, u32[]{:S(2)}) collective-permute-start(f32[4,16,128]{2,1,0:T(8,128)} %refs_2_.1), channel_id=1, source_target_pairs={{4,12},{8,0},{12,20},{16,8},{20,28},{24,16},{5,13},{9,1},{13,21},{... | collective-permute-start | bytes 98312 | tf_op jit(solution)/shard_map/ppermute | solution.py:483
  2.5 0.9 %copy-done = f32[8,4,16,128]{3,2,1,0:T(8,128)S(1)} copy-done((f32[8,4,16,128]{3,2,1,0:T(8,128)S(1)}, f32[8,4,16,128]{3,2,1,0:T(8,128)}, u32[]{:S(2)}) %copy-start) | copy-done | bytes 262168
  4.1 3.8 %collective-permute-done.1.refs_3_ = f32[4,16,128]{2,1,0:T(8,128)S(1)} collective-permute-done((f32[4,16,128]{2,1,0:T(8,128)}, f32[4,16,128]{2,1,0:T(8,128)S(1)}, u32[]{:S(2)}, u32[]{:S(2)}) %collective-permute-start.1) | collective-permute-done | bytes 32800 | tf_op jit(solution)/shard_map/ppermute | solution.py:483
  8.5 1.9 %collective-permute-start.2 = (f32[4,64,128]{2,1,0:T(8,128)S(1)}, f32[4,64,128]{2,1,0:T(8,128)S(1)}, u32[]{:S(2)}, u32[]{:S(2)}) collective-permute-start(f32[4,64,128]{2,1,0:T(8,128)S(1)} %get-tuple-element.28), channel_id=1, source_target_pairs={{0,2},{1,3},{2,0},{3,1},{4,6},{5,7},{6,4},{7,5},{8,10},{9,11},{10,... | collective-permute-start | bytes 393224 | tf_op jit(solution)/shard_map/ppermute | solution.py:453
  12.1 1.8 %collective-permute-done.2.refs_1_ = f32[4,64,128]{2,1,0:T(8,128)S(1)} collective-permute-done((f32[4,64,128]{2,1,0:T(8,128)S(1)}, f32[4,64,128]{2,1,0:T(8,128)S(1)}, u32[]{:S(2)}, u32[]{:S(2)}) %collective-permute-start.2) | collective-permute-done | bytes 131104 | tf_op jit(solution)/shard_map/ppermute | solution.py:453
  13.9 2.4 %collective-permute-done.3.refs_2_ = f32[4,64,128]{2,1,0:T(8,128)S(1)} collective-permute-done((f32[4,64,128]{2,1,0:T(8,128)S(1)}, f32[4,64,128]{2,1,0:T(8,128)S(1)}, u32[]{:S(2)}, u32[]{:S(2)}) %collective-permute-start.3) | collective-permute-done | bytes 131104 | tf_op jit(solution)/shard_map/ppermute | solution.py:453
  16.3 1.6 %collective-permute-done.4.refs_3_ = f32[4,64,128]{2,1,0:T(8,128)S(1)} collective-permute-done((f32[4,64,128]{2,1,0:T(8,128)S(1)}, f32[4,64,128]{2,1,0:T(8,128)S(1)}, u32[]{:S(2)}, u32[]{:S(2)}) %collective-permute-start.4) | collective-permute-done | bytes 131104 | tf_op jit(solution)/shard_map/ppermute | solution.py:453
  18.6 1.9 %collective-permute-start.5 = (f32[4,64,128]{2,1,0:T(8,128)S(1)}, f32[4,64,128]{2,1,0:T(8,128)S(1)}, u32[]{:S(2)}, u32[]{:S(2)}) collective-permute-start(f32[4,64,128]{2,1,0:T(8,128)S(1)} %get-tuple-element.31.refs_2_), channel_id=1, source_target_pairs={{0,8},{4,12},{8,0},{12,4},{16,24},{20,28},{24,16},{28,20},{1,9},{5... | collective-permute-start | bytes 393224 | tf_op jit(solution)/shard_map/ppermute | solution.py:511
  21.3 3.3 %collective-permute-done.5.refs_4_ = f32[4,64,128]{2,1,0:T(8,128)S(1)} collective-permute-done((f32[4,64,128]{2,1,0:T(8,128)S(1)}, f32[4,64,128]{2,1,0:T(8,128)S(1)}, u32[]{:S(2)}, u32[]{:S(2)}) %collective-permute-start.5) | collective-permute-done | bytes 131104 | tf_op jit(solution)/shard_map/ppermute | solution.py:511
  24.6 1.5 %pre.1 = (f32[16,64,128]{2,1,0:T(8,128)S(1)}, f32[16,64,128]{2,1,0:T(8,128)S(1)}, f32[16,64,128]{2,1,0:T(8,128)S(1)}, f32[16,80,128]{2,1,0:T(8,128)S(1)}, f32[4,32,128]{2,1,0:T(8,128)S(1)}) custom-call(s32[2]{0:T(128)S(1)} %pad_add_fusion.place_ref, f32[8,128]{1,0:T(8,128)S(1)} %get-tuple-element.26.scalar_ref, ...), custom_call_target="tpu_custom_call" | custom-call | tf_op jit(solution)/shard_map/pre/pallas_call | solution.py:437
  26.1 3.5 %collective-permute-start.10 = (f32[4,32,128]{2,1,0:T(8,128)S(1)}, f32[4,32,128]{2,1,0:T(8,128)S(1)}, u32[]{:S(2)}, u32[]{:S(2)}) collective-permute-start(f32[4,32,128]{2,1,0:T(8,128)S(1)} %get-tuple-element.38.refs_6_), channel_id=1, source_target_pairs={{0,24},{4,28},{8,16},{12,20},{16,8},{20,12},{24,0},{28,4},{1,25},{... | collective-permute-start | bytes 196616 | tf_op jit(solution)/shard_map/ppermute | solution.py:462
  29.5 2.5 %collective-permute-start.9 = (f32[4,32,128]{2,1,0:T(8,128)S(1)}, f32[4,32,128]{2,1,0:T(8,128)S(1)}, u32[]{:S(2)}, u32[]{:S(2)}) collective-permute-start(f32[4,32,128]{2,1,0:T(8,128)S(1)} %get-tuple-element.38.refs_6_), channel_id=1, source_target_pairs={{0,16},{4,20},{8,24},{12,28},{16,0},{20,4},{24,8},{28,12},{1,17},{... | collective-permute-start | bytes 196616 | tf_op jit(solution)/shard_map/ppermute | solution.py:462
  32.3 3.5 %collective-permute-done.9.refs_8_ = f32[4,32,128]{2,1,0:T(8,128)S(1)} collective-permute-done((f32[4,32,128]{2,1,0:T(8,128)S(1)}, f32[4,32,128]{2,1,0:T(8,128)S(1)}, u32[]{:S(2)}, u32[]{:S(2)}) %collective-permute-start.9) | collective-permute-done | bytes 65568 | tf_op jit(solution)/shard_map/ppermute | solution.py:462
  36.4 3.2 %post.1 = (f32[136,128]{1,0:T(8,128)S(1)}, f32[136,128]{1,0:T(8,128)S(1)}, f32[136,128]{1,0:T(8,128)S(1)}, f32[136,128]{1,0:T(8,128)S(1)}, f32[136,128]{1,0:T(8,...) custom-call(s32[2]{0:T(128)S(1)} %pad_add_fusion.place_ref, ...), custom_call_target="tpu_custom_call" | custom-call | tf_op jit(solution)/shard_map/post/pallas_call | solution.py:437
  39.7 1.2 %collective-permute-start.12 = (f32[136,128]{1,0:T(8,128)S(1)}, f32[136,128]{1,0:T(8,128)S(1)}, u32[]{:S(2)}, u32[]{:S(2)}) collective-permute-start(f32[136,128]{1,0:T(8,128)S(1)} %get-tuple-element.41), channel_id=1, source_target_pairs={{0,2},{1,3},{2,0},{3,1},{4,6},{5,7},{6,4},{7,5},{8,10},{9,11},{10,... | collective-permute-start | bytes 208904 | tf_op jit(solution)/shard_map/ppermute | solution.py:453
  41.5 1.3 %collective-permute-start.14 = (f32[136,128]{1,0:T(8,128)S(1)}, f32[136,128]{1,0:T(8,128)S(1)}, u32[]{:S(2)}, u32[]{:S(2)}) collective-permute-start(f32[136,128]{1,0:T(8,128)S(1)} %get-tuple-element.43), channel_id=1, source_target_pairs={{0,4},{1,5},{2,6},{3,7},{4,0},{5,1},{6,2},{7,3},{8,12},{9,13},{10,... | collective-permute-start | bytes 208904 | tf_op jit(solution)/shard_map/ppermute | solution.py:453
  43.2 2.3 %collective-permute-start.16 = (f32[136,128]{1,0:T(8,128)S(1)}, f32[136,128]{1,0:T(8,128)S(1)}, u32[]{:S(2)}, u32[]{:S(2)}) collective-permute-start(f32[136,128]{1,0:T(8,128)S(1)} %get-tuple-element.45), channel_id=1, source_target_pairs={{0,6},{1,7},{2,4},{3,5},{4,2},{5,3},{6,0},{7,1},{8,14},{9,15},{10,... | collective-permute-start | bytes 208904 | tf_op jit(solution)/shard_map/ppermute | solution.py:453
  46.1 1.2 %collective-permute-done.15.refs_5_ = f32[136,128]{1,0:T(8,128)S(1)} collective-permute-done((f32[136,128]{1,0:T(8,128)S(1)}, f32[136,128]{1,0:T(8,128)S(1)}, u32[]{:S(2)}, u32[]{:S(2)}) %collective-permute-start.15) | collective-permute-done | bytes 69664 | tf_op jit(solution)/shard_map/ppermute | solution.py:453
  47.3 2.7 %collective-permute-done.16.refs_6_ = f32[136,128]{1,0:T(8,128)S(1)} collective-permute-done((f32[136,128]{1,0:T(8,128)S(1)}, f32[136,128]{1,0:T(8,128)S(1)}, u32[]{:S(2)}, u32[]{:S(2)}) %collective-permute-start.16) | collective-permute-done | bytes 69664 | tf_op jit(solution)/shard_map/ppermute | solution.py:453
  50.0 1.1 %collective-permute-done.17.refs_7_ = f32[136,128]{1,0:T(8,128)S(1)} collective-permute-done((f32[136,128]{1,0:T(8,128)S(1)}, f32[136,128]{1,0:T(8,128)S(1)}, u32[]{:S(2)}, u32[]{:S(2)}) %collective-permute-start.17) | collective-permute-done | bytes 69664 | tf_op jit(solution)/shard_map/ppermute | solution.py:453
  51.1 3.5 %collective-permute-start.20 = (f32[8,128]{1,0:T(8,128)S(1)}, f32[8,128]{1,0:T(8,128)S(1)}, u32[]{:S(2)}, u32[]{:S(2)}) collective-permute-start(f32[8,128]{1,0:T(8,128)S(1)} %squares.1), channel_id=1, source_target_pairs={{0,24},{4,28},{8,16},{12,20},{16,8},{20,12},{24,0},{28,4},{1,25},{... | collective-permute-start | bytes 12296 | tf_op jit(solution)/shard_map/ppermute | solution.py:462
  54.6 0.9 %collective-permute-start.18 = (f32[8,128]{1,0:T(8,128)S(1)}, f32[8,128]{1,0:T(8,128)S(1)}, u32[]{:S(2)}, u32[]{:S(2)}) collective-permute-start(f32[8,128]{1,0:T(8,128)S(1)} %squares.1), channel_id=1, source_target_pairs={{0,8},{4,12},{8,0},{12,4},{16,24},{20,28},{24,16},{28,20},{1,9},{5... | collective-permute-start | bytes 12296 | tf_op jit(solution)/shard_map/ppermute | solution.py:462
  55.5 1.4 %collect.1 = (f32[8,4,16,128]{3,2,1,0:T(8,128)}, f32[8,4,16,128]{3,2,1,0:T(8,128)}) custom-call(s32[2]{0:T(128)S(1)} %pad_add_fusion.place_ref, f32[136,128]{1,0:T(8,128)S(1)} %get-tuple-element.39.refs_0_, f32[136,128]{1,0:T(8,128)S(1)} %collective-permute-done.11.refs_1_, f32[136,128]{1,0:T(8,128)S(1)} %collective-permute-done.12.refs_2_, ...), custom_call_target="tpu_custom_call" | custom-call | tf_op jit(solution)/shard_map/collect/pallas_call | solution.py:437
  56.9 2.2 %collective-permute-done.19 = f32[8,128]{1,0:T(8,128)S(1)} collective-permute-done((f32[8,128]{1,0:T(8,128)S(1)}, f32[8,128]{1,0:T(8,128)S(1)}, u32[]{:S(2)}, u32[]{:S(2)}) %collective-permute-start.19) | collective-permute-done | bytes 4128 | tf_op jit(solution)/shard_map/ppermute | solution.py:462
  (43 shorter events, 8.3 us)
Async XLA Ops:
  0.6 7.3 %collective-permute-start = (f32[8,4,16,128]{3,2,1,0:T(8,128)}, f32[8,4,16,128]{3,2,1,0:T(8,128)S(1)}, u32[]{:S(2)}, u32[]{:S(2)}) collective-permute-start(f32[8,4,16,128]{3,2,1,0:T(8,128)} %source_ref.1), channel_id=1, source_target_pairs={{0,1},{1,0},{2,3},{3,2},{4,5},{5,4},{6,7},{7,6},{8,9},{9,8},{10,11... | collective-permute-start | bytes 786440 | tf_op jit(solution)/shard_map/ppermute | solution.py:482
  1.1 6.7 %collective-permute-start.1 = (f32[4,16,128]{2,1,0:T(8,128)}, f32[4,16,128]{2,1,0:T(8,128)S(1)}, u32[]{:S(2)}, u32[]{:S(2)}) collective-permute-start(f32[4,16,128]{2,1,0:T(8,128)} %refs_2_.1), channel_id=1, source_target_pairs={{4,12},{8,0},{12,20},{16,8},{20,28},{24,16},{5,13},{9,1},{13,21},{... | collective-permute-start | bytes 98312 | tf_op jit(solution)/shard_map/ppermute | solution.py:483
  3.5 4.4 %copy-start.2 = (f32[8]{0:T(128)S(1)}, f32[8]{0:T(128)}, u32[]{:S(2)}) copy-start(f32[8]{0:T(128)} %shifts_ref.1) | copy-start | bytes 100
  3.5 4.4 %copy-start.3 = (s32[8]{0:T(128)S(1)}, s32[8]{0:T(128)}, u32[]{:S(2)}) copy-start(s32[8]{0:T(128)} %index_ref.1) | copy-start | bytes 100
  3.5 4.4 %copy-start.4 = (f32[3]{0:T(128)S(1)}, f32[3]{0:T(128)}, u32[]{:S(2)}) copy-start(f32[3]{0:T(128)} %velocity_ref.1) | copy-start | bytes 40
  8.5 5.4 %collective-permute-start.2 = (f32[4,64,128]{2,1,0:T(8,128)S(1)}, f32[4,64,128]{2,1,0:T(8,128)S(1)}, u32[]{:S(2)}, u32[]{:S(2)}) collective-permute-start(f32[4,64,128]{2,1,0:T(8,128)S(1)} %get-tuple-element.28), channel_id=1, source_target_pairs={{0,2},{1,3},{2,0},{3,1},{4,6},{5,7},{6,4},{7,5},{8,10},{9,11},{10,... | collective-permute-start | bytes 393224 | tf_op jit(solution)/shard_map/ppermute | solution.py:453
  10.4 5.9 %collective-permute-start.3 = (f32[4,64,128]{2,1,0:T(8,128)S(1)}, f32[4,64,128]{2,1,0:T(8,128)S(1)}, u32[]{:S(2)}, u32[]{:S(2)}) collective-permute-start(f32[4,64,128]{2,1,0:T(8,128)S(1)} %get-tuple-element.29), channel_id=1, source_target_pairs={{0,4},{1,5},{2,6},{3,7},{4,0},{5,1},{6,2},{7,3},{8,12},{9,13},{10,... | collective-permute-start | bytes 393224 | tf_op jit(solution)/shard_map/ppermute | solution.py:453
  11.3 6.6 %collective-permute-start.4 = (f32[4,64,128]{2,1,0:T(8,128)S(1)}, f32[4,64,128]{2,1,0:T(8,128)S(1)}, u32[]{:S(2)}, u32[]{:S(2)}) collective-permute-start(f32[4,64,128]{2,1,0:T(8,128)S(1)} %get-tuple-element.30), channel_id=1, source_target_pairs={{0,6},{1,7},{2,4},{3,5},{4,2},{5,3},{6,0},{7,1},{8,14},{9,15},{10,... | collective-permute-start | bytes 393224 | tf_op jit(solution)/shard_map/ppermute | solution.py:453
  18.5 6.1 %collective-permute-start.7 = (f32[16,32,128]{2,1,0:T(8,128)S(1)}, f32[16,32,128]{2,1,0:T(8,128)S(1)}, u32[]{:S(2)}, u32[]{:S(2)}) collective-permute-start(f32[16,32,128]{2,1,0:T(8,128)S(1)} %get-tuple-element.33.refs_6_), channel_id=1, source_target_pairs={{0,1},{1,0},{2,3},{3,2},{4,5},{5,4},{6,7},{7,6},{8,9},{9,8},{10,11... | collective-permute-start | bytes 786440 | tf_op jit(solution)/shard_map/ppermute | solution.py:512
  18.6 6.0 %collective-permute-start.5 = (f32[4,64,128]{2,1,0:T(8,128)S(1)}, f32[4,64,128]{2,1,0:T(8,128)S(1)}, u32[]{:S(2)}, u32[]{:S(2)}) collective-permute-start(f32[4,64,128]{2,1,0:T(8,128)S(1)} %get-tuple-element.31.refs_2_), channel_id=1, source_target_pairs={{0,8},{4,12},{8,0},{12,4},{16,24},{20,28},{24,16},{28,20},{1,9},{5... | collective-permute-start | bytes 393224 | tf_op jit(solution)/shard_map/ppermute | solution.py:511
  20.5 4.1 %collective-permute-start.6 = (f32[4,64,128]{2,1,0:T(8,128)S(1)}, f32[4,64,128]{2,1,0:T(8,128)S(1)}, u32[]{:S(2)}, u32[]{:S(2)}) collective-permute-start(f32[4,64,128]{2,1,0:T(8,128)S(1)} %get-tuple-element.32.refs_3_), channel_id=1, source_target_pairs={{8,16},{12,20},{16,8},{20,12},{9,17},{13,21},{17,9},{21,13},{10,18... | collective-permute-start | bytes 393224 | tf_op jit(solution)/shard_map/ppermute | solution.py:511
  26.1 6.2 %collective-permute-start.10 = (f32[4,32,128]{2,1,0:T(8,128)S(1)}, f32[4,32,128]{2,1,0:T(8,128)S(1)}, u32[]{:S(2)}, u32[]{:S(2)}) collective-permute-start(f32[4,32,128]{2,1,0:T(8,128)S(1)} %get-tuple-element.38.refs_6_), channel_id=1, source_target_pairs={{0,24},{4,28},{8,16},{12,20},{16,8},{20,12},{24,0},{28,4},{1,25},{... | collective-permute-start | bytes 196616 | tf_op jit(solution)/shard_map/ppermute | solution.py:462
  29.5 6.2 %collective-permute-start.9 = (f32[4,32,128]{2,1,0:T(8,128)S(1)}, f32[4,32,128]{2,1,0:T(8,128)S(1)}, u32[]{:S(2)}, u32[]{:S(2)}) collective-permute-start(f32[4,32,128]{2,1,0:T(8,128)S(1)} %get-tuple-element.38.refs_6_), channel_id=1, source_target_pairs={{0,16},{4,20},{8,24},{12,28},{16,0},{20,4},{24,8},{28,12},{1,17},{... | collective-permute-start | bytes 196616 | tf_op jit(solution)/shard_map/ppermute | solution.py:462
  32.0 4.4 %collective-permute-start.8 = (f32[4,32,128]{2,1,0:T(8,128)S(1)}, f32[4,32,128]{2,1,0:T(8,128)S(1)}, u32[]{:S(2)}, u32[]{:S(2)}) collective-permute-start(f32[4,32,128]{2,1,0:T(8,128)S(1)} %get-tuple-element.38.refs_6_), channel_id=1, source_target_pairs={{0,8},{4,12},{8,0},{12,4},{16,24},{20,28},{24,16},{28,20},{1,9},{5... | collective-permute-start | bytes 196616 | tf_op jit(solution)/shard_map/ppermute | solution.py:462
  39.6 3.6 %collective-permute-start.11 = (f32[136,128]{1,0:T(8,128)S(1)}, f32[136,128]{1,0:T(8,128)S(1)}, u32[]{:S(2)}, u32[]{:S(2)}) collective-permute-start(f32[136,128]{1,0:T(8,128)S(1)} %get-tuple-element.40), channel_id=1, source_target_pairs={{0,1},{1,0},{2,3},{3,2},{4,5},{5,4},{6,7},{7,6},{8,9},{9,8},{10,11... | collective-permute-start | bytes 208904 | tf_op jit(solution)/shard_map/ppermute | solution.py:453
  39.7 5.9 %collective-permute-start.12 = (f32[136,128]{1,0:T(8,128)S(1)}, f32[136,128]{1,0:T(8,128)S(1)}, u32[]{:S(2)}, u32[]{:S(2)}) collective-permute-start(f32[136,128]{1,0:T(8,128)S(1)} %get-tuple-element.41), channel_id=1, source_target_pairs={{0,2},{1,3},{2,0},{3,1},{4,6},{5,7},{6,4},{7,5},{8,10},{9,11},{10,... | collective-permute-start | bytes 208904 | tf_op jit(solution)/shard_map/ppermute | solution.py:453
  40.9 5.0 %collective-permute-start.13 = (f32[136,128]{1,0:T(8,128)S(1)}, f32[136,128]{1,0:T(8,128)S(1)}, u32[]{:S(2)}, u32[]{:S(2)}) collective-permute-start(f32[136,128]{1,0:T(8,128)S(1)} %get-tuple-element.42), channel_id=1, source_target_pairs={{0,3},{1,2},{2,1},{3,0},{4,7},{5,6},{6,5},{7,4},{8,11},{9,10},{10,... | collective-permute-start | bytes 208904 | tf_op jit(solution)/shard_map/ppermute | solution.py:453
  41.5 4.6 %collective-permute-start.14 = (f32[136,128]{1,0:T(8,128)S(1)}, f32[136,128]{1,0:T(8,128)S(1)}, u32[]{:S(2)}, u32[]{:S(2)}) collective-permute-start(f32[136,128]{1,0:T(8,128)S(1)} %get-tuple-element.43), channel_id=1, source_target_pairs={{0,4},{1,5},{2,6},{3,7},{4,0},{5,1},{6,2},{7,3},{8,12},{9,13},{10,... | collective-permute-start | bytes 208904 | tf_op jit(solution)/shard_map/ppermute | solution.py:453
  42.9 4.4 %collective-permute-start.15 = (f32[136,128]{1,0:T(8,128)S(1)}, f32[136,128]{1,0:T(8,128)S(1)}, u32[]{:S(2)}, u32[]{:S(2)}) collective-permute-start(f32[136,128]{1,0:T(8,128)S(1)} %get-tuple-element.44), channel_id=1, source_target_pairs={{0,5},{1,4},{2,7},{3,6},{4,1},{5,0},{6,3},{7,2},{8,13},{9,12},{10,... | collective-permute-start | bytes 208904 | tf_op jit(solution)/shard_map/ppermute | solution.py:453
  43.2 6.8 %collective-permute-start.16 = (f32[136,128]{1,0:T(8,128)S(1)}, f32[136,128]{1,0:T(8,128)S(1)}, u32[]{:S(2)}, u32[]{:S(2)}) collective-permute-start(f32[136,128]{1,0:T(8,128)S(1)} %get-tuple-element.45), channel_id=1, source_target_pairs={{0,6},{1,7},{2,4},{3,5},{4,2},{5,3},{6,0},{7,1},{8,14},{9,15},{10,... | collective-permute-start | bytes 208904 | tf_op jit(solution)/shard_map/ppermute | solution.py:453
  45.5 5.6 %collective-permute-start.17 = (f32[136,128]{1,0:T(8,128)S(1)}, f32[136,128]{1,0:T(8,128)S(1)}, u32[]{:S(2)}, u32[]{:S(2)}) collective-permute-start(f32[136,128]{1,0:T(8,128)S(1)} %get-tuple-element.46), channel_id=1, source_target_pairs={{0,7},{1,6},{2,5},{3,4},{4,3},{5,2},{6,1},{7,0},{8,15},{9,14},{10,... | collective-permute-start | bytes 208904 | tf_op jit(solution)/shard_map/ppermute | solution.py:453
  51.1 5.8 %collective-permute-start.20 = (f32[8,128]{1,0:T(8,128)S(1)}, f32[8,128]{1,0:T(8,128)S(1)}, u32[]{:S(2)}, u32[]{:S(2)}) collective-permute-start(f32[8,128]{1,0:T(8,128)S(1)} %squares.1), channel_id=1, source_target_pairs={{0,24},{4,28},{8,16},{12,20},{16,8},{20,12},{24,0},{28,4},{1,25},{... | collective-permute-start | bytes 12296 | tf_op jit(solution)/shard_map/ppermute | solution.py:462
  54.6 4.5 %collective-permute-start.19 = (f32[8,128]{1,0:T(8,128)S(1)}, f32[8,128]{1,0:T(8,128)S(1)}, u32[]{:S(2)}, u32[]{:S(2)}) collective-permute-start(f32[8,128]{1,0:T(8,128)S(1)} %squares.1), channel_id=1, source_target_pairs={{0,16},{4,20},{8,24},{12,28},{16,0},{20,4},{24,8},{28,12},{1,17},{... | collective-permute-start | bytes 12296 | tf_op jit(solution)/shard_map/ppermute | solution.py:462
  54.6 4.5 %collective-permute-start.18 = (f32[8,128]{1,0:T(8,128)S(1)}, f32[8,128]{1,0:T(8,128)S(1)}, u32[]{:S(2)}, u32[]{:S(2)}) collective-permute-start(f32[8,128]{1,0:T(8,128)S(1)} %squares.1), channel_id=1, source_target_pairs={{0,8},{4,12},{8,0},{12,4},{16,24},{20,28},{24,16},{28,20},{1,9},{5... | collective-permute-start | bytes 12296 | tf_op jit(solution)/shard_map/ppermute | solution.py:462
  (2 other events, 5.4 us)

commit v10 on v9

--- a/solution.py
+++ b/solution.py
@@ -238,7 +238,7 @@
 
 
 def merge_kernel(place_ref, shifts_ref, index_ref, velocity_ref, *refs):
-    mine_ref, theirs_ref, reaction_ref, beside_ref = refs[:4]
+    mine_ref, theirs_ref, reaction_ref, other_reaction_ref = refs[:4]
     out_refs, scalar_ref = refs[4:-1], refs[-1]
     chip, core = place_ref[0] // 2, place_ref[0] & 1
     by = mine_ref.shape[2]
@@ -246,35 +246,31 @@
     theirs = pl.ds(pl.multiple_of((1 - core) * by, 8), by)
     for m, out_ref in enumerate(out_refs):
         target = jnp.bitwise_xor(chip, m)
-        out_ref[:, mine, :] = mine_ref[target]
-        out_ref[:, theirs, :] = theirs_ref[2 * target + core]
-        out_ref[:, pl.ds(2 * by, by), :] = reaction_ref[...]
-        out_ref[:, pl.ds(3 * by, by), :] = beside_ref[...]
+        out_ref[0, :, mine, :] = mine_ref[target]
+        out_ref[0, :, theirs, :] = theirs_ref[2 * target + core]
+        out_ref[1, :, mine, :] = reaction_ref[...]
+        out_ref[1, :, theirs, :] = other_reaction_ref[...]
     scalars = [shifts_ref[index_ref[place_ref[0]]]] + [velocity_ref[d] for d in range(3)]
     for n, scalar in enumerate(scalars):
         scalar_ref[pl.ds(n, 1), :] = jnp.full((1, LANES), scalar, jnp.float32)
 
 
 def arrange_kernel(chips_y, place_ref, *refs):
-    blocks, (first_ref, second_ref, reaction_ref, halves) = refs[:-4], refs[-4:]
-    by = blocks[0].shape[1] // 4
+    blocks, (first_ref, second_ref, halves) = refs[:-3], refs[-3:]
     for m, block in enumerate(blocks):
         owner = jnp.bitwise_xor(place_ref[0] // 2, m)
-        x, y = owner // chips_y, lax.rem(owner, chips_y)
-        rows = pl.ds(pl.multiple_of(2 * y * by, 8), 2 * by)
-        halves[x, :, rows, :] = block[:, pl.ds(0, 2 * by), :]
-        rows = pl.ds(pl.multiple_of(y * by, 8), by)
-        reaction_ref[pl.ds(HALO * (1 + x), HALO), rows, :] = block[:, pl.ds(2 * by, by), :]
-        reaction_ref[pl.ds((HALO + SLAB) * (1 - x), HALO), rows, :] = block[:, pl.ds(3 * by, by), :]
+        size = block.shape[2]
+        rows = pl.ds(pl.multiple_of(lax.rem(owner, chips_y) * size, 8), size)
+        halves[owner // chips_y, :, :, rows, :] = block[...]
     even = 1 - (place_ref[1] & 1)
     first_ref[...] = halves[even]
     second_ref[...] = halves[1 - even]
 
 
-def pre_kernel(slabs, gy_size, by, place_ref, scalar_ref, *refs):
+def pre_kernel(slabs, place_ref, scalar_ref, *refs):
     pool_ref, pool_up_ref = refs[:2]
-    parts, reactions = refs[2:6], refs[6:8]
-    f, r, w, v1, coarse_ref, v0, tmp, pooled = refs[8:]
+    parts = refs[2:6]
+    f, r, w, v1, coarse_ref, v0, tmp, pooled = refs[6:]
     ny = f.shape[1]
     slab = place_ref[1]
     fine = Level(0, ny, LANES, 0, scalar_ref, f, r, w)
@@ -288,12 +284,8 @@
     even = 1 - (slab & 1)
     firsts = (HALO * (1 + even), HALO * (2 - even), (HALO + SLAB) * even, (HALO + SLAB) * (1 - even))
     for part, first in zip(parts, firsts):
-        f[pl.ds(first, HALO)] = part[...]
-    core = place_ref[0] & 1
-    for n, reaction in enumerate(reactions):
-        for y in range(gy_size // 2):
-            to = pl.multiple_of((2 * y + jnp.bitwise_xor(core, n)) * by, 8)
-            r[:, pl.ds(to, by), :] = reaction[:, pl.ds(y * by, by), :]
+        f[pl.ds(first, HALO)] = part[0]
+        r[pl.ds(first, HALO)] = part[1]
 
     def put(x, weight):
         w[x] = weight
@@ -316,13 +308,12 @@
     coarse_ref[...] = packed.reshape(coarse_ref.shape)
 
 
-def post_kernel(grid, gy_size, bx, by, place_ref, scalar_ref, *refs):
+def post_kernel(grid, by, place_ref, scalar_ref, *refs):
     slabs, nx, ny, nz = grid
     pool_ref, spread_ref, f, r, w, v1 = refs[:6]
     coarse = refs[6 : 6 + slabs]
-    columns = SLAB // bx * gy_size
-    out_refs = refs[6 + slabs : 6 + slabs + columns]
-    va, vb, f1, r1, w1, v1a, v1b, pooled, tmp = refs[6 + slabs + columns :]
+    kept_ref, sent_ref, squares_ref = refs[6 + slabs : 9 + slabs]
+    va, vb, f1, r1, w1, v1a, v1b, pooled, tmp = refs[9 + slabs :]
     pool, spread = pool_ref[...], spread_ref[...]
     slab = place_ref[1]
     rim = HALO // 2
@@ -403,30 +394,56 @@
         rest = fine.defect(va, HALO + x)
         total = total + jnp.sum((rest * rest).reshape(ny // 8, 8, LANES), axis=0)
         tmp[x] = rest
-    squares = jnp.full((8, LANES), jnp.sum(total), jnp.float32)
+    squares_ref[...] = jnp.full((8, LANES), jnp.sum(total), jnp.float32)
+
+    core = place_ref[0] & 1
+    for ref, first in ((kept_ref, core * by), (sent_ref, (1 - core) * by)):
+        for y in range(ny // (2 * by)):
+            row, to = pl.multiple_of(2 * y * by + first, 8), pl.ds(y * by, by)
+            for x in range(SLAB):
+                ref[0, x, to, :] = va[HALO + x, pl.ds(8 + row, by), :]
+                ref[1, x, to, :] = tmp[x, pl.ds(row, by), :]
+
+
+def merge_back_kernel(bx, by, chips_y, chips, place_ref, kept_ref, got_ref, *refs):
+    squares, out_refs = refs[:-chips], refs[-chips:]
+    total = sum(square[...] for square in squares)
+    chip, core = place_ref[0] // 2, place_ref[0] & 1
     area = bx * by
-    for k, out_ref in enumerate(out_refs):
-        owner = jnp.bitwise_xor(place_ref[0], k)
-        first = (owner // gy_size) * bx
-        row = pl.multiple_of(lax.rem(owner, gy_size) * by, 8)
-        for p in range(bx):
-            out_ref[pl.ds(p * by, by), :] = va[HALO + first + p, pl.ds(8 + row, by), :]
-            out_ref[pl.ds(area + p * by, by), :] = tmp[first + p, pl.ds(row, by), :]
-        out_ref[pl.ds(2 * area, 8), :] = squares
-
-
-def collect_kernel(bx, by, place_ref, *refs):
+    for m, out_ref in enumerate(out_refs):
+        target = jnp.bitwise_xor(chip, m)
+        planes = pl.ds((target // chips_y) * bx, bx)
+        rows = pl.ds(pl.multiple_of(lax.rem(target, chips_y) * by, 8), by)
+        for ref, column in ((kept_ref, core), (got_ref, 1 - core)):
+            for n in range(2):
+                to = pl.multiple_of((2 * column + n) * area, 8)
+                out_ref[pl.ds(to, area), :] = ref[n, planes, rows, :].reshape(area, LANES)
+        out_ref[pl.ds(4 * area, 8), :] = total
+
+
+def collect_kernel(place_ref, *refs):
     parts, (iterate_ref, residual_ref) = refs[:-2], refs[-2:]
+    _, bx, by, _ = iterate_ref.shape
     area = bx * by
-    for k, part in enumerate(parts):
-        column = jnp.bitwise_xor(place_ref[0], k)
-        iterate_ref[column] = part[pl.ds(0, area), :].reshape(bx, by, LANES)
-        residual_ref[column] = part[pl.ds(area, area), :].reshape(bx, by, LANES)
-
-
-def squares_kernel(row, *refs):
-    for k, part in enumerate(refs[:-1]):
-        refs[-1][pl.ds(k, 1), :] = part[pl.ds(row, 1), :]
+    for m, part in enumerate(parts):
+        target = jnp.bitwise_xor(place_ref[0] // 2, m)
+        for n in range(2):
+            for k, ref in enumerate((iterate_ref, residual_ref)):
+                rows = pl.ds((2 * n + k) * area, area)
+                ref[2 * target + n] = part[rows, :].reshape(bx, by, LANES)
+
+
+def totals_kernel(row, *refs):
+    for m, part in enumerate(refs[:-1]):
+        refs[-1][pl.ds(m, 1), :] = part[pl.ds(row, 1), :]
+
+
+def rms_kernel(cells, place_ref, mine_ref, theirs_ref, out_ref):
+    chip, core = place_ref[0] // 2, place_ref[0] & 1
+    for ref, column in ((mine_ref, core), (theirs_ref, 1 - core)):
+        rms = jnp.sqrt(ref[...] / cells + EPSILON)
+        for m in range(out_ref.shape[0] // 2):
+            out_ref[2 * jnp.bitwise_xor(chip, m) + column] = jnp.max(rms[m : m + 1])
 
 
 SMEM = pl.BlockSpec(memory_space=pltpu.SMEM)
@@ -477,29 +494,21 @@
 
     chips, chips_y = columns // 2, gy_size // 2
     cores = [(i, i ^ 1) for i in range(gy_size)]
-    onward = [(i, i + step if i % step else i - step) for i in range(gx_size)]
-    onward = [(i, j) for i, j in onward if 0 <= j < gx_size]
-    theirs = lax.ppermute(source, "gy", cores)
-    reaction_beside = lax.ppermute(reaction, "gx", onward)
+    theirs = [lax.ppermute(source, "gy", cores), lax.ppermute(reaction, "gy", cores)]
     (mine,) = local_kernel(keep_kernel, "keep", (place,), (source,), [(chips, bx, by, nz)])
     *blocks, scalar_rows = local_kernel(
         merge_kernel,
         "merge",
         (place, shifts, shift_index, velocity),
-        (mine, theirs, reaction, reaction_beside),
-        [(bx, 4 * by, nz)] * chips + [(8, LANES)],
+        (mine, theirs[0], reaction, theirs[1]),
+        [(2, bx, 2 * by, nz)] * chips + [(8, LANES)],
     )
     scalars = (place, scalar_rows)
     blocks = swap_in_plane(blocks, 2)
 
-    half = (HALO, ny, nz)
-    *halves, rows = local_kernel(
-        functools.partial(arrange_kernel, chips_y),
-        "arrange",
-        (place,),
-        blocks,
-        [half, half, (count, ny // 2, nz)],
-        [(2, *half)],
+    half = (2, HALO, ny, nz)
+    halves = local_kernel(
+        functools.partial(arrange_kernel, chips_y), "arrange", (place,), blocks, [half] * 2, [(2, *half)]
     )
     beside = []
     for n, half in enumerate(halves):
@@ -509,14 +518,13 @@
             if 0 <= j < gx_size:
                 pairs.append((i, j))
         beside.append(lax.ppermute(half, "gx", pairs))
-    reactions = [rows, lax.ppermute(rows, "gy", cores)]
 
     grid, rimmed = (count, ny, nz), (count, ny + 16, nz)
     f, r, w, v1, coarse = local_kernel(
-        functools.partial(pre_kernel, slabs, gy_size, by),
+        functools.partial(pre_kernel, slabs),
         "pre",
         scalars,
-        (pool_matrix(0), pool_matrix(LANES // 2), *halves, *beside, *reactions),
+        (pool_matrix(0), pool_matrix(LANES // 2), *halves, *beside),
         [grid, grid, grid, rimmed, (SLAB // 2, ny // 2, nz)],
         [rimmed, (SLAB, ny, nz), (2, SLAB // 2 * ny // 2, nz)],
     )
@@ -525,26 +533,38 @@
     coarse_grid = (nx // 2, ny // 2, nz)
     coarse_rimmed = (nx // 2 + HALO, ny // 2 + 16, nz)
     rows = max((SLAB // 2 + HALO) * ny // 2, nx // 4 * ny // 2)
-    results = local_kernel(
-        functools.partial(post_kernel, (slabs, nx, ny, nz), gy_size, bx, by),
+    result = (2, SLAB, ny // 2, nz)
+    kept, sent, squares = local_kernel(
+        functools.partial(post_kernel, (slabs, nx, ny, nz), by),
         "post",
         scalars,
         (pool_matrix(0), spread_matrix(), f, r, w, v1, *gathered),
-        [(2 * area + 8, nz)] * columns,
+        [result, result, (8, nz)],
         [rimmed] * 2 + [coarse_grid] * 3 + [coarse_rimmed] * 2 + [(rows, nz), (nx // 2, ny, nz)],
     )
-    parts = swap_in_plane(results, 1)
-
-    (squares,) = local_kernel(
-        functools.partial(squares_kernel, 2 * area), "squares", (), parts, [(columns, nz)]
-    )
-    total = sum(swap_slabs(squares, step, slabs))
-    rms = jnp.sqrt(total[:, 0] / (nx * ny * nz) + EPSILON)
-    slots = jnp.arange(columns, dtype=jnp.int32)
-    mine = jnp.bitwise_xor(slots, column)[None, :] == slots[:, None]
-    residual_rms = jnp.sum(jnp.where(mine, rms[None, :], 0.0), axis=1)
+
+    got = lax.ppermute(sent, "gy", cores)
+    parts = local_kernel(
+        functools.partial(merge_back_kernel, bx, by, chips_y, chips),
+        "merge_back",
+        (place,),
+        (kept, got, *swap_slabs(squares, step, slabs)),
+        [(4 * area + 8, nz)] * chips,
+    )
+    parts = swap_in_plane(parts, 2)
+    (totals,) = local_kernel(
+        functools.partial(totals_kernel, 4 * area), "totals", (), parts, [(chips, nz)]
+    )
+    other_totals = lax.ppermute(totals, "gy", cores)
+    residual_rms = pl.pallas_call(
+        functools.partial(rms_kernel, nx * ny * nz),
+        out_shape=jax.ShapeDtypeStruct((columns,), jnp.float32),
+        in_specs=[SMEM, VMEM, VMEM],
+        out_specs=SMEM,
+        name="rms",
+    )(place, totals, other_totals)
     iterate, residual = local_kernel(
-        functools.partial(collect_kernel, bx, by), "collect", (place,), parts, [source.shape] * 2
+        collect_kernel, "collect", (place,), parts, [source.shape] * 2
     )
     return iterate, residual, residual_rms
 

time: 60.1 us -> 58.5 us (0.973)
  starting transfers between devices: 24.9 us -> 22.2 us
  Pallas kernels: 7.78 us -> 9.79 us
  waiting for transfers between devices: 24.5 us -> 23.5 us
  other arithmetic: 0.97 us -> 0.21 us
  local copies, waits for them, and re-layouts: 0.96 us -> 1.7 us
    ppermute x3 -> x4, waiting for transfers between devices: 3.84 us -> 0.01 us  [the longest x1 0.01 us: column_body(): lax.ppermute(reaction, 'gy', cores)]
    ppermute x10 -> x6, starting transfers between devices: 9.88 us -> 8.1 us  [swap_in_plane(): moved.append(lax.ppermute(pieces[k], ('gx', 'gy'), pairs))]
    ppermute x2, waiting for transfers between devices: 3.3 us -> 4.9 us  [column_body(): beside.append(lax.ppermute(half, 'gx', pairs))]
    pallas_call x0 -> x1, Pallas kernels: none -> 1.33 us  [column_body(): pl.pallas_call(functools.partial(rms_kernel, nx * ny * nz), out_shape=jax...]
    ppermute x3 -> x4, starting transfers between devices: 1.87 us -> 0.67 us  [the longest x1 0.52 us: column_body(): lax.ppermute(source, 'gy', cores)]
    ppermute x10 -> x6, waiting for transfers between devices: 11 us -> 11.7 us  [swap_in_plane(): moved.append(lax.ppermute(pieces[k], ('gx', 'gy'), pairs))]
    unnamed x10 -> x16, local copies, waits for them, and re-layouts: 0.96 us -> 1.7 us
    pallas_call x7 -> x8, Pallas kernels: 7.78 us -> 8.46 us  [local_kernel(): pl.pallas_call(kernel, out_shape=[jax.ShapeDtypeStruct(shape, jnp.float32...]
  transfers between devices with their start and end apart: 21 -> 18, of which waited for: 12 -> 11; matrix products, arithmetic and copies ran while one was open for 0% -> 0% of each run, Pallas kernels for 3% -> 3%
where the time goes in v10:
time: 58.5 us; the launch traced here: 58.2 us
  waiting for transfers between devices  23.5 us (40%)
  starting transfers between devices  22.2 us (38%)
  Pallas kernels  9.79 us (17%)
  local copies, waits for them, and re-layouts  1.7 us (3%)
  between operations  0.78 us (1%)
    ppermute x6, waiting for transfers between devices, swap_in_plane(): moved.append(lax.ppermute(pieces[k], ('gx', 'gy'), pairs))  11.7 us
    ppermute x6, starting transfers between devices, swap_slabs(): moved.append(lax.ppermute(piece, 'gx', pairs))  11 us
    pallas_call x8, Pallas kernels, local_kernel(): pl.pallas_call(kernel, out_shape=[jax.ShapeDtypeStruct(shape, jnp.float32...  8.46 us
    ppermute x6, starting transfers between devices, swap_in_plane(): moved.append(lax.ppermute(pieces[k], ('gx', 'gy'), pairs))  8.1 us
    ppermute x6, waiting for transfers between devices, swap_slabs(): moved.append(lax.ppermute(piece, 'gx', pairs))  6.88 us
    ppermute x2, waiting for transfers between devices, column_body(): beside.append(lax.ppermute(half, 'gx', pairs))  4.9 us
    ppermute x2, starting transfers between devices, column_body(): beside.append(lax.ppermute(half, 'gx', pairs))  2.45 us
    unnamed x16, local copies, waits for them, and re-layouts  1.7 us
  transfers between devices with their start and end apart: 18, of which 11 were waited for; matrix products, arithmetic and copies ran while one was open for 0% of the time, Pallas kernels for 3%

profile of v10, /device:TPU:0, one launch (start us, length us, event | category | flops | bytes accessed | tf_op | source)
XLA Modules:
  0.0 58.2 jit_solution(10118569231572235575)
XLA Ops:
  3.6 3.0 %collective-permute-start.2 = (f32[2,4,32,128]{3,2,1,0:T(8,128)S(1)}, f32[2,4,32,128]{3,2,1,0:T(8,128)S(1)}, u32[]{:S(2)}, u32[]{:S(2)}) collective-permute-start(f32[2,4,32,128]{3,2,1,0:T(8,128)S(1)} %get-tuple-element.26), channel_id=1, source_target_pairs={{0,2},{1,3},{2,0},{3,1},{4,6},{5,7},{6,4},{7,5},{8,10},{9,11},{10,... | collective-permute-start | bytes 393224 | tf_op jit(solution)/shard_map/ppermute | solution.py:470
  6.6 1.5 %collective-permute-start.3 = (f32[2,4,32,128]{3,2,1,0:T(8,128)S(1)}, f32[2,4,32,128]{3,2,1,0:T(8,128)S(1)}, u32[]{:S(2)}, u32[]{:S(2)}) collective-permute-start(f32[2,4,32,128]{3,2,1,0:T(8,128)S(1)} %get-tuple-element.27), channel_id=1, source_target_pairs={{0,4},{1,5},{2,6},{3,7},{4,0},{5,1},{6,2},{7,3},{8,12},{9,13},{10,... | collective-permute-start | bytes 393224 | tf_op jit(solution)/shard_map/ppermute | solution.py:470
  8.2 2.2 %collective-permute-done.2.refs_1_ = f32[2,4,32,128]{3,2,1,0:T(8,128)S(1)} collective-permute-done((f32[2,4,32,128]{3,2,1,0:T(8,128)S(1)}, f32[2,4,32,128]{3,2,1,0:T(8,128)S(1)}, u32[]{:S(2)}, u32[]{:S(2)}) %collective-permute-start.2) | collective-permute-done | bytes 131104 | tf_op jit(solution)/shard_map/ppermute | solution.py:470
  10.4 2.7 %collective-permute-done.3.refs_2_ = f32[2,4,32,128]{3,2,1,0:T(8,128)S(1)} collective-permute-done((f32[2,4,32,128]{3,2,1,0:T(8,128)S(1)}, f32[2,4,32,128]{3,2,1,0:T(8,128)S(1)}, u32[]{:S(2)}, u32[]{:S(2)}) %collective-permute-start.3) | collective-permute-done | bytes 131104 | tf_op jit(solution)/shard_map/ppermute | solution.py:470
  13.0 1.4 %collective-permute-done.4.refs_3_ = f32[2,4,32,128]{3,2,1,0:T(8,128)S(1)} collective-permute-done((f32[2,4,32,128]{3,2,1,0:T(8,128)S(1)}, f32[2,4,32,128]{3,2,1,0:T(8,128)S(1)}, u32[]{:S(2)}, u32[]{:S(2)}) %collective-permute-start.4) | collective-permute-done | bytes 131104 | tf_op jit(solution)/shard_map/ppermute | solution.py:470
  15.1 1.8 %collective-permute-start.5 = (f32[2,4,64,128]{3,2,1,0:T(8,128)S(1)}, f32[2,4,64,128]{3,2,1,0:T(8,128)S(1)}, u32[]{:S(2)}, u32[]{:S(2)}) collective-permute-start(f32[2,4,64,128]{3,2,1,0:T(8,128)S(1)} %get-tuple-element.29.refs_2_), channel_id=1, source_target_pairs={{0,8},{4,12},{8,0},{12,4},{16,24},{20,28},{24,16},{28,20},{1,9},{5... | collective-permute-start | bytes 786440 | tf_op jit(solution)/shard_map/ppermute | solution.py:520
  17.7 4.9 %collective-permute-done.5.refs_4_ = f32[2,4,64,128]{3,2,1,0:T(8,128)S(1)} collective-permute-done((f32[2,4,64,128]{3,2,1,0:T(8,128)S(1)}, f32[2,4,64,128]{3,2,1,0:T(8,128)S(1)}, u32[]{:S(2)}, u32[]{:S(2)}) %collective-permute-start.5) | collective-permute-done | bytes 262176 | tf_op jit(solution)/shard_map/ppermute | solution.py:520
  22.6 1.5 %pre.1 = (f32[16,64,128]{2,1,0:T(8,128)S(1)}, f32[16,64,128]{2,1,0:T(8,128)S(1)}, f32[16,64,128]{2,1,0:T(8,128)S(1)}, f32[16,80,128]{2,1,0:T(8,128)S(1)}, f32[4,32,128]{2,1,0:T(8,128)S(1)}) custom-call(s32[2]{0:T(128)S(1)} %pad_add_fusion.place_ref, f32[8,128]{1,0:T(8,128)S(1)} %get-tuple-element.24.scalar_ref, ...), custom_call_target="tpu_custom_call" | custom-call | tf_op jit(solution)/shard_map/pre/pallas_call | solution.py:454
  24.1 3.8 %collective-permute-start.9 = (f32[4,32,128]{2,1,0:T(8,128)S(1)}, f32[4,32,128]{2,1,0:T(8,128)S(1)}, u32[]{:S(2)}, u32[]{:S(2)}) collective-permute-start(f32[4,32,128]{2,1,0:T(8,128)S(1)} %get-tuple-element.35.refs_6_), channel_id=1, source_target_pairs={{0,24},{4,28},{8,16},{12,20},{16,8},{20,12},{24,0},{28,4},{1,25},{... | collective-permute-start | bytes 196616 | tf_op jit(solution)/shard_map/ppermute | solution.py:479
  27.9 2.5 %collective-permute-start.8 = (f32[4,32,128]{2,1,0:T(8,128)S(1)}, f32[4,32,128]{2,1,0:T(8,128)S(1)}, u32[]{:S(2)}, u32[]{:S(2)}) collective-permute-start(f32[4,32,128]{2,1,0:T(8,128)S(1)} %get-tuple-element.35.refs_6_), channel_id=1, source_target_pairs={{0,16},{4,20},{8,24},{12,28},{16,0},{20,4},{24,8},{28,12},{1,17},{... | collective-permute-start | bytes 196616 | tf_op jit(solution)/shard_map/ppermute | solution.py:479
  30.6 2.8 %collective-permute-done.8.refs_8_ = f32[4,32,128]{2,1,0:T(8,128)S(1)} collective-permute-done((f32[4,32,128]{2,1,0:T(8,128)S(1)}, f32[4,32,128]{2,1,0:T(8,128)S(1)}, u32[]{:S(2)}, u32[]{:S(2)}) %collective-permute-start.8) | collective-permute-done | bytes 65568 | tf_op jit(solution)/shard_map/ppermute | solution.py:479
  33.5 1.2 %collective-permute-done.7.refs_7_ = f32[4,32,128]{2,1,0:T(8,128)S(1)} collective-permute-done((f32[4,32,128]{2,1,0:T(8,128)S(1)}, f32[4,32,128]{2,1,0:T(8,128)S(1)}, u32[]{:S(2)}, u32[]{:S(2)}) %collective-permute-start.7) | collective-permute-done | bytes 65568 | tf_op jit(solution)/shard_map/ppermute | solution.py:479
  34.6 3.2 %post.1 = (f32[2,8,32,128]{3,2,1,0:T(8,128)S(1)}, f32[2,8,32,128]{3,2,1,0:T(8,128)S(1)}, f32[8,128]{1,0:T(8,128)S(1)}) custom-call(s32[2]{0:T(128)S(1)} %pad_add_fusion.place_ref, f32[8,128]{1,0:T(8,128)S(1)} %get-tuple-element.24.scalar_ref, bf16[128,128]{1,0:T(8,128)(2,1)S(1)} %get-tuple-element.47.refs_0_, ...), custom_call_target="tpu_custom_call" | custom-call | tf_op jit(solution)/shard_map/post/pallas_call | solution.py:454
  37.9 2.8 %collective-permute-start.13 = (f32[8,128]{1,0:T(8,128)S(1)}, f32[8,128]{1,0:T(8,128)S(1)}, u32[]{:S(2)}, u32[]{:S(2)}) collective-permute-start(f32[8,128]{1,0:T(8,128)S(1)} %get-tuple-element.38.refs_0_), channel_id=1, source_target_pairs={{0,24},{4,28},{8,16},{12,20},{16,8},{20,12},{24,0},{28,4},{1,25},{... | collective-permute-start | bytes 12296 | tf_op jit(solution)/shard_map/ppermute | solution.py:479
  40.8 1.6 %collective-permute-start.11 = (f32[8,128]{1,0:T(8,128)S(1)}, f32[8,128]{1,0:T(8,128)S(1)}, u32[]{:S(2)}, u32[]{:S(2)}) collective-permute-start(f32[8,128]{1,0:T(8,128)S(1)} %get-tuple-element.38.refs_0_), channel_id=1, source_target_pairs={{0,8},{4,12},{8,0},{12,4},{16,24},{20,28},{24,16},{28,20},{1,9},{5... | collective-permute-start | bytes 12296 | tf_op jit(solution)/shard_map/ppermute | solution.py:479
  42.4 1.0 %collective-permute-done.13.refs_3_ = f32[8,128]{1,0:T(8,128)S(1)} collective-permute-done((f32[8,128]{1,0:T(8,128)S(1)}, f32[8,128]{1,0:T(8,128)S(1)}, u32[]{:S(2)}, u32[]{:S(2)}) %collective-permute-start.13) | collective-permute-done | bytes 4128 | tf_op jit(solution)/shard_map/ppermute | solution.py:479
  43.4 1.9 %collective-permute-done.12.refs_2_ = f32[8,128]{1,0:T(8,128)S(1)} collective-permute-done((f32[8,128]{1,0:T(8,128)S(1)}, f32[8,128]{1,0:T(8,128)S(1)}, u32[]{:S(2)}, u32[]{:S(2)}) %collective-permute-start.12) | collective-permute-done | bytes 4128 | tf_op jit(solution)/shard_map/ppermute | solution.py:479
  45.9 1.3 %collective-permute-start.14 = (f32[264,128]{1,0:T(8,128)S(1)}, f32[264,128]{1,0:T(8,128)S(1)}, u32[]{:S(2)}, u32[]{:S(2)}) collective-permute-start(f32[264,128]{1,0:T(8,128)S(1)} %get-tuple-element.40), channel_id=1, source_target_pairs={{0,2},{1,3},{2,0},{3,1},{4,6},{5,7},{6,4},{7,5},{8,10},{9,11},{10,... | collective-permute-start | bytes 405512 | tf_op jit(solution)/shard_map/ppermute | solution.py:470
  47.1 1.5 %collective-permute-start.15 = (f32[264,128]{1,0:T(8,128)S(1)}, f32[264,128]{1,0:T(8,128)S(1)}, u32[]{:S(2)}, u32[]{:S(2)}) collective-permute-start(f32[264,128]{1,0:T(8,128)S(1)} %get-tuple-element.41), channel_id=1, source_target_pairs={{0,4},{1,5},{2,6},{3,7},{4,0},{5,1},{6,2},{7,3},{8,12},{9,13},{10,... | collective-permute-start | bytes 405512 | tf_op jit(solution)/shard_map/ppermute | solution.py:470
  49.4 2.2 %collective-permute-done.14.refs_1_ = f32[264,128]{1,0:T(8,128)S(1)} collective-permute-done((f32[264,128]{1,0:T(8,128)S(1)}, f32[264,128]{1,0:T(8,128)S(1)}, u32[]{:S(2)}, u32[]{:S(2)}) %collective-permute-start.14) | collective-permute-done | bytes 135200 | tf_op jit(solution)/shard_map/ppermute | solution.py:470
  51.7 1.2 %collective-permute-done.15.refs_2_ = f32[264,128]{1,0:T(8,128)S(1)} collective-permute-done((f32[264,128]{1,0:T(8,128)S(1)}, f32[264,128]{1,0:T(8,128)S(1)}, u32[]{:S(2)}, u32[]{:S(2)}) %collective-permute-start.15) | collective-permute-done | bytes 135200 | tf_op jit(solution)/shard_map/ppermute | solution.py:470
  52.8 2.1 %collective-permute-done.16.refs_3_ = f32[264,128]{1,0:T(8,128)S(1)} collective-permute-done((f32[264,128]{1,0:T(8,128)S(1)}, f32[264,128]{1,0:T(8,128)S(1)}, u32[]{:S(2)}, u32[]{:S(2)}) %collective-permute-start.16) | collective-permute-done | bytes 135200 | tf_op jit(solution)/shard_map/ppermute | solution.py:470
  55.0 1.4 %collect.1 = (f32[8,4,16,128]{3,2,1,0:T(8,128)}, f32[8,4,16,128]{3,2,1,0:T(8,128)}) custom-call(s32[2]{0:T(128)S(1)} %pad_add_fusion.place_ref, f32[264,128]{1,0:T(8,128)S(1)} %get-tuple-element.39.refs_0_, f32[264,128]{1,0:T(8,128)S(1)} %collective-permute-done.14.refs_1_, f32[264,128]{1,0:T(8,128)S(1)} %collective-permute-done.15.refs_2_, ...), custom_call_target="tpu_custom_call" | custom-call | tf_op jit(solution)/shard_map/collect/pallas_call | solution.py:454
  56.9 1.3 %rms.1 = f32[8]{0:T(128)} custom-call(s32[2]{0:T(128)} %copy-done.2, f32[4,128]{1,0:T(4,128)} %copy-done.3, f32[4,128]{1,0:T(4,128)} %copy-done.7), custom_call_target="tpu_custom_call" | custom-call | tf_op jit(solution)/shard_map/rms/pallas_call | solution.py:559
  (41 shorter events, 6.8 us)
Async XLA Ops:
  0.6 2.2 %collective-permute-start = (f32[8,4,16,128]{3,2,1,0:T(8,128)}, f32[8,4,16,128]{3,2,1,0:T(8,128)S(1)}, u32[]{:S(2)}, u32[]{:S(2)}) collective-permute-start(f32[8,4,16,128]{3,2,1,0:T(8,128)} %source_ref.1), channel_id=1, source_target_pairs={{0,1},{1,0},{2,3},{3,2},{4,5},{5,4},{6,7},{7,6},{8,9},{9,8},{10,11... | collective-permute-start | bytes 786440 | tf_op jit(solution)/shard_map/ppermute | solution.py:497
  1.1 1.7 %collective-permute-start.1 = (f32[4,16,128]{2,1,0:T(8,128)}, f32[4,16,128]{2,1,0:T(8,128)S(1)}, u32[]{:S(2)}, u32[]{:S(2)}) collective-permute-start(f32[4,16,128]{2,1,0:T(8,128)} %refs_2_.1), channel_id=1, source_target_pairs={{0,1},{1,0},{2,3},{3,2},{4,5},{5,4},{6,7},{7,6},{8,9},{9,8},{10,11... | collective-permute-start | bytes 98312 | tf_op jit(solution)/shard_map/ppermute | solution.py:497
  1.3 0.9 %copy-start = (f32[8,4,16,128]{3,2,1,0:T(8,128)S(1)}, f32[8,4,16,128]{3,2,1,0:T(8,128)}, u32[]{:S(2)}) copy-start(f32[8,4,16,128]{3,2,1,0:T(8,128)} %source_ref.1) | copy-start | bytes 786436
  2.3 52.7 %copy-start.2 = (s32[2]{0:T(128)}, s32[2]{0:T(128)S(1)}, u32[]{:S(2)}) copy-start(s32[2]{0:T(128)S(1)} %pad_add_fusion.place_ref) | copy-start | bytes 28
  2.3 0.8 %copy-start.1 = (f32[4,16,128]{2,1,0:T(8,128)S(1)}, f32[4,16,128]{2,1,0:T(8,128)}, u32[]{:S(2)}) copy-start(f32[4,16,128]{2,1,0:T(8,128)} %refs_2_.1) | copy-start | bytes 98308
  2.3 0.8 %copy-start.4 = (f32[8]{0:T(128)S(1)}, f32[8]{0:T(128)}, u32[]{:S(2)}) copy-start(f32[8]{0:T(128)} %shifts_ref.1) | copy-start | bytes 100
  2.3 0.8 %copy-start.5 = (s32[8]{0:T(128)S(1)}, s32[8]{0:T(128)}, u32[]{:S(2)}) copy-start(s32[8]{0:T(128)} %index_ref.1) | copy-start | bytes 100
  3.6 6.8 %collective-permute-start.2 = (f32[2,4,32,128]{3,2,1,0:T(8,128)S(1)}, f32[2,4,32,128]{3,2,1,0:T(8,128)S(1)}, u32[]{:S(2)}, u32[]{:S(2)}) collective-permute-start(f32[2,4,32,128]{3,2,1,0:T(8,128)S(1)} %get-tuple-element.26), channel_id=1, source_target_pairs={{0,2},{1,3},{2,0},{3,1},{4,6},{5,7},{6,4},{7,5},{8,10},{9,11},{10,... | collective-permute-start | bytes 393224 | tf_op jit(solution)/shard_map/ppermute | solution.py:470
  6.6 6.4 %collective-permute-start.3 = (f32[2,4,32,128]{3,2,1,0:T(8,128)S(1)}, f32[2,4,32,128]{3,2,1,0:T(8,128)S(1)}, u32[]{:S(2)}, u32[]{:S(2)}) collective-permute-start(f32[2,4,32,128]{3,2,1,0:T(8,128)S(1)} %get-tuple-element.27), channel_id=1, source_target_pairs={{0,4},{1,5},{2,6},{3,7},{4,0},{5,1},{6,2},{7,3},{8,12},{9,13},{10,... | collective-permute-start | bytes 393224 | tf_op jit(solution)/shard_map/ppermute | solution.py:470
  8.1 6.3 %collective-permute-start.4 = (f32[2,4,32,128]{3,2,1,0:T(8,128)S(1)}, f32[2,4,32,128]{3,2,1,0:T(8,128)S(1)}, u32[]{:S(2)}, u32[]{:S(2)}) collective-permute-start(f32[2,4,32,128]{3,2,1,0:T(8,128)S(1)} %get-tuple-element.28), channel_id=1, source_target_pairs={{0,6},{1,7},{2,4},{3,5},{4,2},{5,3},{6,0},{7,1},{8,14},{9,15},{10,... | collective-permute-start | bytes 393224 | tf_op jit(solution)/shard_map/ppermute | solution.py:470
  15.1 7.5 %collective-permute-start.5 = (f32[2,4,64,128]{3,2,1,0:T(8,128)S(1)}, f32[2,4,64,128]{3,2,1,0:T(8,128)S(1)}, u32[]{:S(2)}, u32[]{:S(2)}) collective-permute-start(f32[2,4,64,128]{3,2,1,0:T(8,128)S(1)} %get-tuple-element.29.refs_2_), channel_id=1, source_target_pairs={{0,8},{4,12},{8,0},{12,4},{16,24},{20,28},{24,16},{28,20},{1,9},{5... | collective-permute-start | bytes 786440 | tf_op jit(solution)/shard_map/ppermute | solution.py:520
  16.9 5.7 %collective-permute-start.6 = (f32[2,4,64,128]{3,2,1,0:T(8,128)S(1)}, f32[2,4,64,128]{3,2,1,0:T(8,128)S(1)}, u32[]{:S(2)}, u32[]{:S(2)}) collective-permute-start(f32[2,4,64,128]{3,2,1,0:T(8,128)S(1)} %get-tuple-element.30.refs_3_), channel_id=1, source_target_pairs={{8,16},{12,20},{16,8},{20,12},{9,17},{13,21},{17,9},{21,13},{10,18... | collective-permute-start | bytes 786440 | tf_op jit(solution)/shard_map/ppermute | solution.py:520
  24.1 6.6 %collective-permute-start.9 = (f32[4,32,128]{2,1,0:T(8,128)S(1)}, f32[4,32,128]{2,1,0:T(8,128)S(1)}, u32[]{:S(2)}, u32[]{:S(2)}) collective-permute-start(f32[4,32,128]{2,1,0:T(8,128)S(1)} %get-tuple-element.35.refs_6_), channel_id=1, source_target_pairs={{0,24},{4,28},{8,16},{12,20},{16,8},{20,12},{24,0},{28,4},{1,25},{... | collective-permute-start | bytes 196616 | tf_op jit(solution)/shard_map/ppermute | solution.py:479
  27.9 5.6 %collective-permute-start.8 = (f32[4,32,128]{2,1,0:T(8,128)S(1)}, f32[4,32,128]{2,1,0:T(8,128)S(1)}, u32[]{:S(2)}, u32[]{:S(2)}) collective-permute-start(f32[4,32,128]{2,1,0:T(8,128)S(1)} %get-tuple-element.35.refs_6_), channel_id=1, source_target_pairs={{0,16},{4,20},{8,24},{12,28},{16,0},{20,4},{24,8},{28,12},{1,17},{... | collective-permute-start | bytes 196616 | tf_op jit(solution)/shard_map/ppermute | solution.py:479
  30.4 4.3 %collective-permute-start.7 = (f32[4,32,128]{2,1,0:T(8,128)S(1)}, f32[4,32,128]{2,1,0:T(8,128)S(1)}, u32[]{:S(2)}, u32[]{:S(2)}) collective-permute-start(f32[4,32,128]{2,1,0:T(8,128)S(1)} %get-tuple-element.35.refs_6_), channel_id=1, source_target_pairs={{0,8},{4,12},{8,0},{12,4},{16,24},{20,28},{24,16},{28,20},{1,9},{5... | collective-permute-start | bytes 196616 | tf_op jit(solution)/shard_map/ppermute | solution.py:479
  37.9 7.4 %collective-permute-start.10 = (f32[2,8,32,128]{3,2,1,0:T(8,128)S(1)}, f32[2,8,32,128]{3,2,1,0:T(8,128)S(1)}, u32[]{:S(2)}, u32[]{:S(2)}) collective-permute-start(f32[2,8,32,128]{3,2,1,0:T(8,128)S(1)} %get-tuple-element.37), channel_id=1, source_target_pairs={{0,1},{1,0},{2,3},{3,2},{4,5},{5,4},{6,7},{7,6},{8,9},{9,8},{10,11... | collective-permute-start | bytes 786440 | tf_op jit(solution)/shard_map/ppermute | solution.py:546
  37.9 5.5 %collective-permute-start.13 = (f32[8,128]{1,0:T(8,128)S(1)}, f32[8,128]{1,0:T(8,128)S(1)}, u32[]{:S(2)}, u32[]{:S(2)}) collective-permute-start(f32[8,128]{1,0:T(8,128)S(1)} %get-tuple-element.38.refs_0_), channel_id=1, source_target_pairs={{0,24},{4,28},{8,16},{12,20},{16,8},{20,12},{24,0},{28,4},{1,25},{... | collective-permute-start | bytes 12296 | tf_op jit(solution)/shard_map/ppermute | solution.py:479
  40.8 4.5 %collective-permute-start.12 = (f32[8,128]{1,0:T(8,128)S(1)}, f32[8,128]{1,0:T(8,128)S(1)}, u32[]{:S(2)}, u32[]{:S(2)}) collective-permute-start(f32[8,128]{1,0:T(8,128)S(1)} %get-tuple-element.38.refs_0_), channel_id=1, source_target_pairs={{0,16},{4,20},{8,24},{12,28},{16,0},{20,4},{24,8},{28,12},{1,17},{... | collective-permute-start | bytes 12296 | tf_op jit(solution)/shard_map/ppermute | solution.py:479
  40.8 4.5 %collective-permute-start.11 = (f32[8,128]{1,0:T(8,128)S(1)}, f32[8,128]{1,0:T(8,128)S(1)}, u32[]{:S(2)}, u32[]{:S(2)}) collective-permute-start(f32[8,128]{1,0:T(8,128)S(1)} %get-tuple-element.38.refs_0_), channel_id=1, source_target_pairs={{0,8},{4,12},{8,0},{12,4},{16,24},{20,28},{24,16},{28,20},{1,9},{5... | collective-permute-start | bytes 12296 | tf_op jit(solution)/shard_map/ppermute | solution.py:479
  45.9 5.8 %collective-permute-start.14 = (f32[264,128]{1,0:T(8,128)S(1)}, f32[264,128]{1,0:T(8,128)S(1)}, u32[]{:S(2)}, u32[]{:S(2)}) collective-permute-start(f32[264,128]{1,0:T(8,128)S(1)} %get-tuple-element.40), channel_id=1, source_target_pairs={{0,2},{1,3},{2,0},{3,1},{4,6},{5,7},{6,4},{7,5},{8,10},{9,11},{10,... | collective-permute-start | bytes 405512 | tf_op jit(solution)/shard_map/ppermute | solution.py:470
  47.1 5.7 %collective-permute-start.15 = (f32[264,128]{1,0:T(8,128)S(1)}, f32[264,128]{1,0:T(8,128)S(1)}, u32[]{:S(2)}, u32[]{:S(2)}) collective-permute-start(f32[264,128]{1,0:T(8,128)S(1)} %get-tuple-element.41), channel_id=1, source_target_pairs={{0,4},{1,5},{2,6},{3,7},{4,0},{5,1},{6,2},{7,3},{8,12},{9,13},{10,... | collective-permute-start | bytes 405512 | tf_op jit(solution)/shard_map/ppermute | solution.py:470
  48.6 6.3 %collective-permute-start.16 = (f32[264,128]{1,0:T(8,128)S(1)}, f32[264,128]{1,0:T(8,128)S(1)}, u32[]{:S(2)}, u32[]{:S(2)}) collective-permute-start(f32[264,128]{1,0:T(8,128)S(1)} %get-tuple-element.42), channel_id=1, source_target_pairs={{0,6},{1,7},{2,4},{3,5},{4,2},{5,3},{6,0},{7,1},{8,14},{9,15},{10,... | collective-permute-start | bytes 405512 | tf_op jit(solution)/shard_map/ppermute | solution.py:470
  54.9 1.4 %copy-start.3 = (f32[4,128]{1,0:T(4,128)}, f32[4,128]{1,0:T(4,128)S(1)}, u32[]{:S(2)}) copy-start(f32[4,128]{1,0:T(4,128)S(1)} %totals.1.mine_ref) | copy-start | bytes 6148
  54.9 1.4 %collective-permute-start.17 = (f32[4,128]{1,0:T(4,128)S(1)}, f32[4,128]{1,0:T(4,128)S(1)}, u32[]{:S(2)}, u32[]{:S(2)}) collective-permute-start(f32[4,128]{1,0:T(4,128)S(1)} %totals.1.mine_ref), channel_id=1, source_target_pairs={{0,1},{1,0},{2,3},{3,2},{4,5},{5,4},{6,7},{7,6},{8,9},{9,8},{10,11... | collective-permute-start | bytes 6152 | tf_op jit(solution)/shard_map/ppermute | solution.py:558
  (2 other events, 1.3 us)

commit v11 on v10

--- a/solution.py
+++ b/solution.py
@@ -17,6 +17,7 @@
 GROUP = 4
 SLAB = 8
 HALO = 4
+NEAR = 2
 
 
 def with_halo(x, sides, width):
@@ -256,43 +257,47 @@
 
 
 def arrange_kernel(chips_y, place_ref, *refs):
-    blocks, (first_ref, second_ref, halves) = refs[:-3], refs[-3:]
+    blocks, (slab_ref, first_ref, second_ref) = refs[:-3], refs[-3:]
     for m, block in enumerate(blocks):
         owner = jnp.bitwise_xor(place_ref[0] // 2, m)
-        size = block.shape[2]
+        _, bx, size, _ = block.shape
+        planes = pl.ds((owner // chips_y) * bx, bx)
         rows = pl.ds(pl.multiple_of(lax.rem(owner, chips_y) * size, 8), size)
-        halves[owner // chips_y, :, :, rows, :] = block[...]
+        slab_ref[:, planes, rows, :] = block[...]
     even = 1 - (place_ref[1] & 1)
-    first_ref[...] = halves[even]
-    second_ref[...] = halves[1 - even]
+    first_ref[...] = slab_ref[:, pl.ds(even * (SLAB - NEAR), NEAR)]
+    second_ref[...] = slab_ref[:, pl.ds((1 - even) * (SLAB - NEAR), NEAR)]
 
 
 def pre_kernel(slabs, place_ref, scalar_ref, *refs):
-    pool_ref, pool_up_ref = refs[:2]
-    parts = refs[2:6]
-    f, r, w, v1, coarse_ref, v0, tmp, pooled = refs[6:]
+    pool_ref, pool_up_ref, slab_ref, first_ref, second_ref = refs[:5]
+    f, r, w, v1, coarse_ref, first_out, second_out, v0, tmp, pooled = refs[5:]
     ny = f.shape[1]
     slab = place_ref[1]
     fine = Level(0, ny, LANES, 0, scalar_ref, f, r, w)
     zero_rows(v0, ny)
     zero_rows(v1, ny)
-    count = SLAB + 2 * HALO
+    after = HALO + SLAB
+    even = 1 - (slab & 1)
+
+    f[pl.ds(HALO, SLAB)], r[pl.ds(HALO, SLAB)] = slab_ref[0], slab_ref[1]
+    for ref, above in ((first_ref, even), (second_ref, 1 - even)):
+        planes = pl.ds((HALO - NEAR) + above * (SLAB + NEAR), NEAR)
+        f[planes], r[planes] = ref[0], ref[1]
+
     inside = [jnp.where(slab > 0, DAMPING, 0.0)] * HALO
     inside += [DAMPING] * SLAB
     inside += [jnp.where(slab < slabs - 1, DAMPING, 0.0)] * HALO
 
-    even = 1 - (slab & 1)
-    firsts = (HALO * (1 + even), HALO * (2 - even), (HALO + SLAB) * even, (HALO + SLAB) * (1 - even))
-    for part, first in zip(parts, firsts):
-        f[pl.ds(first, HALO)] = part[0]
-        r[pl.ds(first, HALO)] = part[1]
-
     def put(x, weight):
         w[x] = weight
         v0[x, pl.ds(8, ny), :] = weight * f[x]
 
-    sweep(range(count), lambda x: inside[x] / (r[x] + fine.centre), put)
-    fine.smooth(v0, v1, range(1, count - 1))
+    known = range(HALO - NEAR, after + NEAR)
+    sweep(known, lambda x: inside[x] / (r[x] + fine.centre), put)
+    fine.smooth(v0, v1, known[1:-1])
+    for ref, above in ((first_out, even), (second_out, 1 - even)):
+        ref[...] = v1[pl.ds(HALO + 1 + above * (SLAB - HALO), NEAR), pl.ds(8, ny), :]
     half = ny // 2
 
     def coarsened(x):
@@ -308,21 +313,17 @@
     coarse_ref[...] = packed.reshape(coarse_ref.shape)
 
 
-def post_kernel(grid, by, place_ref, scalar_ref, *refs):
+def coarse_kernel(grid, place_ref, scalar_ref, *refs):
     slabs, nx, ny, nz = grid
-    pool_ref, spread_ref, f, r, w, v1 = refs[:6]
-    coarse = refs[6 : 6 + slabs]
-    kept_ref, sent_ref, squares_ref = refs[6 + slabs : 9 + slabs]
-    va, vb, f1, r1, w1, v1a, v1b, pooled, tmp = refs[9 + slabs :]
+    pool_ref, spread_ref = refs[:2]
+    coarse, out_ref = refs[2 : 2 + slabs], refs[2 + slabs]
+    f1, r1, w1, v1a, v1b, pooled, tmp = refs[3 + slabs :]
     pool, spread = pool_ref[...], spread_ref[...]
     slab = place_ref[1]
     rim = HALO // 2
     nx1, ny1, nx2, ny2 = nx // 2, ny // 2, nx // 4, ny // 4
-    fine = Level(0, ny, nz, 0, scalar_ref, f, r, w)
     mid = Level(1, ny1, nz // 2, rim, scalar_ref, f1, r1, w1)
     deep = Level(2, ny2, nz // 4, 0, scalar_ref, None, None, None)
-    for v in (va, vb):
-        zero_rows(v, ny)
     for v in (v1a, v1b):
         zero_rows(v, ny1)
         blank = jnp.zeros((rim,) + v.shape[1:], jnp.float32)
@@ -374,16 +375,29 @@
 
     window = own + 2 * rim
     values = v1b[pl.ds(slab * own, window), pl.ds(8, ny1), :].reshape(window * ny1, LANES)
-    pooled[pl.ds(0, window * ny1), :] = split_dot(values, spread)
-    count = SLAB + 2 * HALO
+    out_ref[...] = split_dot(values, spread)
+
+
+def post_kernel(by, place_ref, scalar_ref, *refs):
+    f, r, w, v1, correction, first_ref, second_ref, kept_ref, sent_ref, va, vb, tmp = refs
+    count, ny = f.shape[:2]
+    fine = Level(0, ny, LANES, 0, scalar_ref, f, r, w)
+    for v in (va, vb):
+        zero_rows(v, ny)
+    even, half = 1 - (place_ref[1] & 1), ny // 2
+    window = correction.shape[0] // half
+    for ref, above in ((first_ref, even), (second_ref, 1 - even)):
+        va[pl.ds(1 + above * (SLAB + HALO), NEAR), pl.ds(8, ny), :] = ref[...]
 
     def refined(x):
-        return fine.spread_rows(pooled[pl.ds(x * ny1, ny1), :], tmp.at[x])
+        return fine.spread_rows(correction[pl.ds(x * half, half), :], tmp.at[x])
 
     def put_refined(x, value):
         for at in (2 * x, 2 * x + 1):
             if 0 < at < count - 1:
-                va[at, pl.ds(8, ny), :] = v1[at, pl.ds(8, ny), :] + value
+                known = HALO - NEAR < at < HALO + SLAB + NEAR - 1
+                here = v1 if known else va
+                va[at, pl.ds(8, ny), :] = here[at, pl.ds(8, ny), :] + value
 
     sweep(range(window), refined, put_refined)
     fine.smooth(va, vb, range(2, count - 2))
@@ -394,31 +408,33 @@
         rest = fine.defect(va, HALO + x)
         total = total + jnp.sum((rest * rest).reshape(ny // 8, 8, LANES), axis=0)
         tmp[x] = rest
-    squares_ref[...] = jnp.full((8, LANES), jnp.sum(total), jnp.float32)
-
-    core = place_ref[0] & 1
+    squares = jnp.full((8, LANES), jnp.sum(total), jnp.float32)
+
+    core, area = place_ref[0] & 1, half * SLAB
     for ref, first in ((kept_ref, core * by), (sent_ref, (1 - core) * by)):
-        for y in range(ny // (2 * by)):
-            row, to = pl.multiple_of(2 * y * by + first, 8), pl.ds(y * by, by)
+        for y in range(half // by):
+            row = pl.multiple_of(2 * y * by + first, 8)
             for x in range(SLAB):
-                ref[0, x, to, :] = va[HALO + x, pl.ds(8 + row, by), :]
-                ref[1, x, to, :] = tmp[x, pl.ds(row, by), :]
-
-
-def merge_back_kernel(bx, by, chips_y, chips, place_ref, kept_ref, got_ref, *refs):
-    squares, out_refs = refs[:-chips], refs[-chips:]
-    total = sum(square[...] for square in squares)
+                to = x * half + y * by
+                ref[pl.ds(to, by), :] = va[HALO + x, pl.ds(8 + row, by), :]
+                ref[pl.ds(area + to, by), :] = tmp[x, pl.ds(row, by), :]
+        ref[pl.ds(2 * area, 8), :] = squares
+
+
+def merge_back_kernel(bx, by, chips_y, place_ref, kept_ref, got_ref, *out_refs):
     chip, core = place_ref[0] // 2, place_ref[0] & 1
-    area = bx * by
+    area, half = bx * by, chips_y * by
     for m, out_ref in enumerate(out_refs):
         target = jnp.bitwise_xor(chip, m)
-        planes = pl.ds((target // chips_y) * bx, bx)
-        rows = pl.ds(pl.multiple_of(lax.rem(target, chips_y) * by, 8), by)
+        first = (target // chips_y) * bx * half + lax.rem(target, chips_y) * by
         for ref, column in ((kept_ref, core), (got_ref, 1 - core)):
             for n in range(2):
-                to = pl.multiple_of((2 * column + n) * area, 8)
-                out_ref[pl.ds(to, area), :] = ref[n, planes, rows, :].reshape(area, LANES)
-        out_ref[pl.ds(4 * area, 8), :] = total
+                for p in range(bx):
+                    at = pl.multiple_of(first + (n * SLAB + p) * half, 8)
+                    to = pl.multiple_of((2 * column + n) * area + p * by, 8)
+                    out_ref[pl.ds(to, by), :] = ref[pl.ds(at, by), :]
+            to = pl.multiple_of(4 * area + 8 * column, 8)
+            out_ref[pl.ds(to, 8), :] = ref[pl.ds(2 * SLAB * half, 8), :]
 
 
 def collect_kernel(place_ref, *refs):
@@ -433,17 +449,10 @@
                 ref[2 * target + n] = part[rows, :].reshape(bx, by, LANES)
 
 
-def totals_kernel(row, *refs):
+def squares_kernel(row, *refs):
     for m, part in enumerate(refs[:-1]):
-        refs[-1][pl.ds(m, 1), :] = part[pl.ds(row, 1), :]
-
-
-def rms_kernel(cells, place_ref, mine_ref, theirs_ref, out_ref):
-    chip, core = place_ref[0] // 2, place_ref[0] & 1
-    for ref, column in ((mine_ref, core), (theirs_ref, 1 - core)):
-        rms = jnp.sqrt(ref[...] / cells + EPSILON)
-        for m in range(out_ref.shape[0] // 2):
-            out_ref[2 * jnp.bitwise_xor(chip, m) + column] = jnp.max(rms[m : m + 1])
+        for n in range(2):
+            refs[-1][pl.ds(2 * m + n, 1), :] = part[pl.ds(row + 8 * n, 1), :]
 
 
 SMEM = pl.BlockSpec(memory_space=pltpu.SMEM)
@@ -506,66 +515,74 @@
     scalars = (place, scalar_rows)
     blocks = swap_in_plane(blocks, 2)
 
-    half = (2, HALO, ny, nz)
-    halves = local_kernel(
-        functools.partial(arrange_kernel, chips_y), "arrange", (place,), blocks, [half] * 2, [(2, *half)]
-    )
-    beside = []
-    for n, half in enumerate(halves):
-        pairs = []
-        for i in range(gx_size):
-            j = i + step if i // step % 2 == n else i - step
-            if 0 <= j < gx_size:
-                pairs.append((i, j))
-        beside.append(lax.ppermute(half, "gx", pairs))
+    edge = (2, NEAR, ny, nz)
+    slab, *edges = local_kernel(
+        functools.partial(arrange_kernel, chips_y),
+        "arrange",
+        (place,),
+        blocks,
+        [(2, SLAB, ny, nz), edge, edge],
+    )
+
+    def exchange(pieces):
+        got = []
+        for n, piece in enumerate(pieces):
+            pairs = [(i, i + step if i // step % 2 == n else i - step) for i in range(gx_size)]
+            pairs = [(i, j) for i, j in pairs if 0 <= j < gx_size]
+            got.append(lax.ppermute(piece, "gx", pairs))
+        return got
 
     grid, rimmed = (count, ny, nz), (count, ny + 16, nz)
-    f, r, w, v1, coarse = local_kernel(
+    f, r, w, v1, coarse, *beyond = local_kernel(
         functools.partial(pre_kernel, slabs),
         "pre",
         scalars,
-        (pool_matrix(0), pool_matrix(LANES // 2), *halves, *beside),
-        [grid, grid, grid, rimmed, (SLAB // 2, ny // 2, nz)],
+        (pool_matrix(0), pool_matrix(LANES // 2), slab, *exchange(edges)),
+        [grid, grid, grid, rimmed, (SLAB // 2, ny // 2, nz)] + [(NEAR, ny, nz)] * 2,
         [rimmed, (SLAB, ny, nz), (2, SLAB // 2 * ny // 2, nz)],
     )
     gathered = swap_slabs(coarse, step, slabs)
 
     coarse_grid = (nx // 2, ny // 2, nz)
     coarse_rimmed = (nx // 2 + HALO, ny // 2 + 16, nz)
-    rows = max((SLAB // 2 + HALO) * ny // 2, nx // 4 * ny // 2)
-    result = (2, SLAB, ny // 2, nz)
-    kept, sent, squares = local_kernel(
-        functools.partial(post_kernel, (slabs, nx, ny, nz), by),
+    window = (SLAB // 2 + HALO) * ny // 2
+    (correction,) = local_kernel(
+        functools.partial(coarse_kernel, (slabs, nx, ny, nz)),
+        "coarse",
+        scalars,
+        (pool_matrix(0), spread_matrix(), *gathered),
+        [(window, nz)],
+        [coarse_grid] * 3 + [coarse_rimmed] * 2 + [(nx // 4 * ny // 2, nz), (nx // 2, ny // 2, nz)],
+    )
+    result = (SLAB * ny + 8, nz)
+    kept, sent = local_kernel(
+        functools.partial(post_kernel, by),
         "post",
         scalars,
-        (pool_matrix(0), spread_matrix(), f, r, w, v1, *gathered),
-        [result, result, (8, nz)],
-        [rimmed] * 2 + [coarse_grid] * 3 + [coarse_rimmed] * 2 + [(rows, nz), (nx // 2, ny, nz)],
-    )
-
-    got = lax.ppermute(sent, "gy", cores)
+        (f, r, w, v1, correction, *exchange(beyond)),
+        [result, result],
+        [rimmed] * 2 + [(SLAB, ny, nz)],
+    )
+
     parts = local_kernel(
-        functools.partial(merge_back_kernel, bx, by, chips_y, chips),
+        functools.partial(merge_back_kernel, bx, by, chips_y),
         "merge_back",
         (place,),
-        (kept, got, *swap_slabs(squares, step, slabs)),
-        [(4 * area + 8, nz)] * chips,
+        (kept, lax.ppermute(sent, "gy", cores)),
+        [(4 * area + 16, nz)] * chips,
     )
     parts = swap_in_plane(parts, 2)
-    (totals,) = local_kernel(
-        functools.partial(totals_kernel, 4 * area), "totals", (), parts, [(chips, nz)]
-    )
-    other_totals = lax.ppermute(totals, "gy", cores)
-    residual_rms = pl.pallas_call(
-        functools.partial(rms_kernel, nx * ny * nz),
-        out_shape=jax.ShapeDtypeStruct((columns,), jnp.float32),
-        in_specs=[SMEM, VMEM, VMEM],
-        out_specs=SMEM,
-        name="rms",
-    )(place, totals, other_totals)
+    (squares,) = local_kernel(
+        functools.partial(squares_kernel, 4 * area), "squares", (), parts, [(columns, nz)]
+    )
     iterate, residual = local_kernel(
         collect_kernel, "collect", (place,), parts, [source.shape] * 2
     )
+    total = sum(swap_slabs(squares, step, slabs))
+    rms = jnp.sqrt(total[:, 0] / (nx * ny * nz) + EPSILON)
+    slots = jnp.arange(columns, dtype=jnp.int32)
+    mine = jnp.bitwise_xor(slots, column // 2 * 2)[:, None] == slots[None, :]
+    residual_rms = jnp.sum(jnp.where(mine, rms[None, :], 0.0), axis=1)
     return iterate, residual, residual_rms
 
 

time: 58.5 us -> 56.5 us (0.966)
  waiting for transfers between devices: 23.5 us -> 19.2 us
  starting transfers between devices: 22.2 us -> 25.3 us
  Pallas kernels: 9.79 us -> 8.88 us
  other arithmetic: 0.21 us -> 1.04 us
    ppermute x6, waiting for transfers between devices: 6.88 us -> 2.53 us  [swap_slabs(): moved.append(lax.ppermute(piece, 'gx', pairs))]
    ppermute x4 -> x5, starting transfers between devices: 2.53 us -> 5.19 us  [the longest x4 5.12 us: exchange(): got.append(lax.ppermute(piece, 'gx', pairs))]
    pallas_call x1 -> x0, Pallas kernels: 1.33 us -> none  [column_body(): pl.pallas_call(functools.partial(rms_kernel, nx * ny * nz), out_shape=jax...]
    ppermute x4 -> x5, waiting for transfers between devices: 4.91 us -> 3.99 us  [the longest x4 2.46 us: exchange(): got.append(lax.ppermute(piece, 'gx', pairs))]
    ppermute x6, waiting for transfers between devices: 11.7 us -> 12.6 us  [swap_in_plane(): moved.append(lax.ppermute(pieces[k], ('gx', 'gy'), pairs))]
    reduce_sum x0 -> x1, other arithmetic: none -> 0.7 us  [column_body(): residual_rms = jnp.sum(jnp.where(mine, rms[None, :], 0.0), axis=1)]
    unnamed x16 -> x10, local copies, waits for them, and re-layouts: 1.7 us -> 1.12 us
    pallas_call x8 -> x9, Pallas kernels: 8.46 us -> 8.88 us  [local_kernel(): pl.pallas_call(kernel, out_shape=[jax.ShapeDtypeStruct(shape, jnp.float32...]
  transfers between devices with their start and end apart: 18 -> 19, of which waited for: 11 -> 11; matrix products, arithmetic and copies ran while one was open for 0% -> 0% of each run, Pallas kernels for 3% -> 8%
where the time goes in v11:
time: 56.5 us; the launch traced here: 56.2 us
  starting transfers between devices  25.3 us (45%)
  waiting for transfers between devices  19.2 us (34%)
  Pallas kernels  8.88 us (16%)
  local copies, waits for them, and re-layouts  1.12 us (2%)
  other arithmetic  1.04 us (2%)
  between operations  0.78 us (1%)
    ppermute x6, waiting for transfers between devices, swap_in_plane(): moved.append(lax.ppermute(pieces[k], ('gx', 'gy'), pairs))  12.6 us
    ppermute x6, starting transfers between devices, swap_slabs(): moved.append(lax.ppermute(piece, 'gx', pairs))  11.4 us
    pallas_call x9, Pallas kernels, local_kernel(): pl.pallas_call(kernel, out_shape=[jax.ShapeDtypeStruct(shape, jnp.float32...  8.88 us
    ppermute x6, starting transfers between devices, swap_in_plane(): moved.append(lax.ppermute(pieces[k], ('gx', 'gy'), pairs))  8.1 us
    ppermute x4, starting transfers between devices, exchange(): got.append(lax.ppermute(piece, 'gx', pairs))  5.12 us
    ppermute x6, waiting for transfers between devices, swap_slabs(): moved.append(lax.ppermute(piece, 'gx', pairs))  2.53 us
    ppermute x4, waiting for transfers between devices, exchange(): got.append(lax.ppermute(piece, 'gx', pairs))  2.46 us
    ppermute x1, waiting for transfers between devices, column_body(): lax.ppermute(sent, 'gy', cores)  1.53 us
  transfers between devices with their start and end apart: 19, of which 11 were waited for; matrix products, arithmetic and copies ran while one was open for 0% of the time, Pallas kernels for 8%

profile of v11, /device:TPU:0, one launch (start us, length us, event | category | flops | bytes accessed | tf_op | source)
XLA Modules:
  0.0 56.2 jit_solution(3061383787016675241)
XLA Ops:
  3.6 3.0 %collective-permute-start.2 = (f32[2,4,32,128]{3,2,1,0:T(8,128)S(1)}, f32[2,4,32,128]{3,2,1,0:T(8,128)S(1)}, u32[]{:S(2)}, u32[]{:S(2)}) collective-permute-start(f32[2,4,32,128]{3,2,1,0:T(8,128)S(1)} %get-tuple-element.28), channel_id=1, source_target_pairs={{0,2},{1,3},{2,0},{3,1},{4,6},{5,7},{6,4},{7,5},{8,10},{9,11},{10,... | collective-permute-start | bytes 393224 | tf_op jit(solution)/shard_map/ppermute | solution.py:479
  6.6 1.5 %collective-permute-start.3 = (f32[2,4,32,128]{3,2,1,0:T(8,128)S(1)}, f32[2,4,32,128]{3,2,1,0:T(8,128)S(1)}, u32[]{:S(2)}, u32[]{:S(2)}) collective-permute-start(f32[2,4,32,128]{3,2,1,0:T(8,128)S(1)} %get-tuple-element.29), channel_id=1, source_target_pairs={{0,4},{1,5},{2,6},{3,7},{4,0},{5,1},{6,2},{7,3},{8,12},{9,13},{10,... | collective-permute-start | bytes 393224 | tf_op jit(solution)/shard_map/ppermute | solution.py:479
  8.2 2.2 %collective-permute-done.2.refs_1_ = f32[2,4,32,128]{3,2,1,0:T(8,128)S(1)} collective-permute-done((f32[2,4,32,128]{3,2,1,0:T(8,128)S(1)}, f32[2,4,32,128]{3,2,1,0:T(8,128)S(1)}, u32[]{:S(2)}, u32[]{:S(2)}) %collective-permute-start.2) | collective-permute-done | bytes 131104 | tf_op jit(solution)/shard_map/ppermute | solution.py:479
  10.4 2.7 %collective-permute-done.3.refs_2_ = f32[2,4,32,128]{3,2,1,0:T(8,128)S(1)} collective-permute-done((f32[2,4,32,128]{3,2,1,0:T(8,128)S(1)}, f32[2,4,32,128]{3,2,1,0:T(8,128)S(1)}, u32[]{:S(2)}, u32[]{:S(2)}) %collective-permute-start.3) | collective-permute-done | bytes 131104 | tf_op jit(solution)/shard_map/ppermute | solution.py:479
  13.0 1.4 %collective-permute-done.4.refs_3_ = f32[2,4,32,128]{3,2,1,0:T(8,128)S(1)} collective-permute-done((f32[2,4,32,128]{3,2,1,0:T(8,128)S(1)}, f32[2,4,32,128]{3,2,1,0:T(8,128)S(1)}, u32[]{:S(2)}, u32[]{:S(2)}) %collective-permute-start.4) | collective-permute-done | bytes 131104 | tf_op jit(solution)/shard_map/ppermute | solution.py:479
  15.1 1.8 %collective-permute-start.5 = (f32[2,2,64,128]{3,2,1,0:T(8,128)S(1)}, f32[2,2,64,128]{3,2,1,0:T(8,128)S(1)}, u32[]{:S(2)}, u32[]{:S(2)}) collective-permute-start(f32[2,2,64,128]{3,2,1,0:T(8,128)S(1)} %get-tuple-element.32), channel_id=1, source_target_pairs={{0,8},{4,12},{8,0},{12,4},{16,24},{20,28},{24,16},{28,20},{1,9},{5... | collective-permute-start | bytes 393224 | tf_op jit(solution)/shard_map/ppermute | solution.py:532
  17.6 2.5 %collective-permute-done.5.refs_3_ = f32[2,2,64,128]{3,2,1,0:T(8,128)S(1)} collective-permute-done((f32[2,2,64,128]{3,2,1,0:T(8,128)S(1)}, f32[2,2,64,128]{3,2,1,0:T(8,128)S(1)}, u32[]{:S(2)}, u32[]{:S(2)}) %collective-permute-start.5) | collective-permute-done | bytes 131104 | tf_op jit(solution)/shard_map/ppermute | solution.py:532
  20.1 1.3 %pre.1 = (f32[16,64,128]{2,1,0:T(8,128)S(1)}, f32[16,64,128]{2,1,0:T(8,128)S(1)}, f32[16,64,128]{2,1,0:T(8,128)S(1)}, f32[16,80,128]{2,1,0:T(8,128)S(1)}, f32[4,...) custom-call(s32[2]{0:T(128)S(1)} %pad_add_fusion.place_ref, ...), custom_call_target="tpu_custom_call" | custom-call | tf_op jit(solution)/shard_map/pre/pallas_call | solution.py:463
  21.4 3.8 %collective-permute-start.9 = (f32[4,32,128]{2,1,0:T(8,128)S(1)}, f32[4,32,128]{2,1,0:T(8,128)S(1)}, u32[]{:S(2)}, u32[]{:S(2)}) collective-permute-start(f32[4,32,128]{2,1,0:T(8,128)S(1)} %get-tuple-element.38.refs_2_), channel_id=1, source_target_pairs={{0,24},{4,28},{8,16},{12,20},{16,8},{20,12},{24,0},{28,4},{1,25},{... | collective-permute-start | bytes 196616 | tf_op jit(solution)/shard_map/ppermute | solution.py:488
  25.2 3.2 %collective-permute-start.8 = (f32[4,32,128]{2,1,0:T(8,128)S(1)}, f32[4,32,128]{2,1,0:T(8,128)S(1)}, u32[]{:S(2)}, u32[]{:S(2)}) collective-permute-start(f32[4,32,128]{2,1,0:T(8,128)S(1)} %get-tuple-element.38.refs_2_), channel_id=1, source_target_pairs={{0,16},{4,20},{8,24},{12,28},{16,0},{20,4},{24,8},{28,12},{1,17},{... | collective-permute-start | bytes 196616 | tf_op jit(solution)/shard_map/ppermute | solution.py:488
  28.4 2.0 %collective-permute-start.10 = (f32[2,64,128]{2,1,0:T(8,128)S(1)}, f32[2,64,128]{2,1,0:T(8,128)S(1)}, u32[]{:S(2)}, u32[]{:S(2)}) collective-permute-start(f32[2,64,128]{2,1,0:T(8,128)S(1)} %get-tuple-element.39), channel_id=1, source_target_pairs={{0,8},{4,12},{8,0},{12,4},{16,24},{20,28},{24,16},{28,20},{1,9},{5... | collective-permute-start | bytes 196616 | tf_op jit(solution)/shard_map/ppermute | solution.py:532
  31.5 1.2 %collective-permute-done.7.refs_3_ = f32[4,32,128]{2,1,0:T(8,128)S(1)} collective-permute-done((f32[4,32,128]{2,1,0:T(8,128)S(1)}, f32[4,32,128]{2,1,0:T(8,128)S(1)}, u32[]{:S(2)}, u32[]{:S(2)}) %collective-permute-start.7) | collective-permute-done | bytes 65568 | tf_op jit(solution)/shard_map/ppermute | solution.py:488
  32.6 2.3 %coarse.1.refs_4_ = f32[256,128]{1,0:T(8,128)S(1)} custom-call(s32[2]{0:T(128)S(1)} %pad_add_fusion.place_ref, f32[8,128]{1,0:T(8,128)S(1)} %get-tuple-element.26.scalar_ref, bf16[128,128]{1,0:T(8,128)(2,1)S(1)} %get-tuple-element.50.refs_0_, bf16[128,128]{1,0:T(8,128)(2,1)S(1)} %get-tuple-element.49.refs_1_, f32[4,32,128]{2,1,0:T(8,128)S(1)} %get-tuple-element.38.refs_2_, ...), custom_call_target="tpu_custom_call" | custom-call | tf_op jit(solution)/shard_map/coarse/pallas_call | solution.py:463
  35.0 1.5 %post.1 = (f32[520,128]{1,0:T(8,128)S(1)}, f32[520,128]{1,0:T(8,128)S(1)}) custom-call(s32[2]{0:T(128)S(1)} %pad_add_fusion.place_ref, f32[8,128]{1,0:T(8,128)S(1)} %get-tuple-element.26.scalar_ref, f32[16,64,128]{2,1,0:T(8,128)S(1)} %get-tuple-element.34.refs_0_, f32[16,64,128]{2,1,0:T(8,128)S(1)} %get-tuple-element.35.refs_1_, ...), custom_call_target="tpu_custom_call" | custom-call | tf_op jit(solution)/shard_map/post/pallas_call | solution.py:463
  36.6 1.5 %collective-permute-done.12.got_ref = f32[520,128]{1,0:T(8,128)S(1)} collective-permute-done((f32[520,128]{1,0:T(8,128)S(1)}, f32[520,128]{1,0:T(8,128)S(1)}, u32[]{:S(2)}, u32[]{:S(2)}) %collective-permute-start.12) | collective-permute-done | bytes 266272 | tf_op jit(solution)/shard_map/ppermute | solution.py:571
  38.7 1.6 %collective-permute-start.13 = (f32[272,128]{1,0:T(8,128)S(1)}, f32[272,128]{1,0:T(8,128)S(1)}, u32[]{:S(2)}, u32[]{:S(2)}) collective-permute-start(f32[272,128]{1,0:T(8,128)S(1)} %get-tuple-element.44), channel_id=1, source_target_pairs={{0,2},{1,3},{2,0},{3,1},{4,6},{5,7},{6,4},{7,5},{8,10},{9,11},{10,... | collective-permute-start | bytes 417800 | tf_op jit(solution)/shard_map/ppermute | solution.py:479
  40.3 1.5 %collective-permute-start.14 = (f32[272,128]{1,0:T(8,128)S(1)}, f32[272,128]{1,0:T(8,128)S(1)}, u32[]{:S(2)}, u32[]{:S(2)}) collective-permute-start(f32[272,128]{1,0:T(8,128)S(1)} %get-tuple-element.45), channel_id=1, source_target_pairs={{0,4},{1,5},{2,6},{3,7},{4,0},{5,1},{6,2},{7,3},{8,12},{9,13},{10,... | collective-permute-start | bytes 417800 | tf_op jit(solution)/shard_map/ppermute | solution.py:479
  42.3 2.2 %collective-permute-done.13.refs_1_ = f32[272,128]{1,0:T(8,128)S(1)} collective-permute-done((f32[272,128]{1,0:T(8,128)S(1)}, f32[272,128]{1,0:T(8,128)S(1)}, u32[]{:S(2)}, u32[]{:S(2)}) %collective-permute-start.13) | collective-permute-done | bytes 139296 | tf_op jit(solution)/shard_map/ppermute | solution.py:479
  44.5 2.4 %collective-permute-done.14.refs_2_ = f32[272,128]{1,0:T(8,128)S(1)} collective-permute-done((f32[272,128]{1,0:T(8,128)S(1)}, f32[272,128]{1,0:T(8,128)S(1)}, u32[]{:S(2)}, u32[]{:S(2)}) %collective-permute-start.14) | collective-permute-done | bytes 139296 | tf_op jit(solution)/shard_map/ppermute | solution.py:479
  46.9 1.8 %collective-permute-done.15.refs_3_ = f32[272,128]{1,0:T(8,128)S(1)} collective-permute-done((f32[272,128]{1,0:T(8,128)S(1)}, f32[272,128]{1,0:T(8,128)S(1)}, u32[]{:S(2)}, u32[]{:S(2)}) %collective-permute-start.15) | collective-permute-done | bytes 139296 | tf_op jit(solution)/shard_map/ppermute | solution.py:479
  48.7 2.2 %collective-permute-start.18 = (f32[8,128]{1,0:T(8,128)S(1)}, f32[8,128]{1,0:T(8,128)S(1)}, u32[]{:S(2)}, u32[]{:S(2)}) collective-permute-start(f32[8,128]{1,0:T(8,128)S(1)} %squares.1), channel_id=1, source_target_pairs={{0,24},{4,28},{8,16},{12,20},{16,8},{20,12},{24,0},{28,4},{1,25},{... | collective-permute-start | bytes 12296 | tf_op jit(solution)/shard_map/ppermute | solution.py:488
  51.7 1.4 %collective-permute-start.16 = (f32[8,128]{1,0:T(8,128)S(1)}, f32[8,128]{1,0:T(8,128)S(1)}, u32[]{:S(2)}, u32[]{:S(2)}) collective-permute-start(f32[8,128]{1,0:T(8,128)S(1)} %squares.1), channel_id=1, source_target_pairs={{0,8},{4,12},{8,0},{12,4},{16,24},{20,28},{24,16},{28,20},{1,9},{5... | collective-permute-start | bytes 12296 | tf_op jit(solution)/shard_map/ppermute | solution.py:488
  53.1 1.4 %collect.1 = (f32[8,4,16,128]{3,2,1,0:T(8,128)}, f32[8,4,16,128]{3,2,1,0:T(8,128)}) custom-call(s32[2]{0:T(128)S(1)} %pad_add_fusion.place_ref, f32[272,128]{1,0:T(8,128)S(1)} %get-tuple-element.43.refs_0_, f32[272,128]{1,0:T(8,128)S(1)} %collective-permute-done.13.refs_1_, f32[272,128]{1,0:T(8,128)S(1)} %collective-permute-done.14.refs_2_, ...), custom_call_target="tpu_custom_call" | custom-call | tf_op jit(solution)/shard_map/collect/pallas_call | solution.py:463
  54.5 0.9 %collective-permute-done.17 = f32[8,128]{1,0:T(8,128)S(1)} collective-permute-done((f32[8,128]{1,0:T(8,128)S(1)}, f32[8,128]{1,0:T(8,128)S(1)}, u32[]{:S(2)}, u32[]{:S(2)}) %collective-permute-start.17) | collective-permute-done | bytes 4128 | tf_op jit(solution)/shard_map/ppermute | solution.py:488
  (41 shorter events, 8.3 us)
Async XLA Ops:
  0.6 2.2 %collective-permute-start = (f32[8,4,16,128]{3,2,1,0:T(8,128)}, f32[8,4,16,128]{3,2,1,0:T(8,128)S(1)}, u32[]{:S(2)}, u32[]{:S(2)}) collective-permute-start(f32[8,4,16,128]{3,2,1,0:T(8,128)} %source_ref.1), channel_id=1, source_target_pairs={{0,1},{1,0},{2,3},{3,2},{4,5},{5,4},{6,7},{7,6},{8,9},{9,8},{10,11... | collective-permute-start | bytes 786440 | tf_op jit(solution)/shard_map/ppermute | solution.py:506
  1.1 1.7 %collective-permute-start.1 = (f32[4,16,128]{2,1,0:T(8,128)}, f32[4,16,128]{2,1,0:T(8,128)S(1)}, u32[]{:S(2)}, u32[]{:S(2)}) collective-permute-start(f32[4,16,128]{2,1,0:T(8,128)} %refs_2_.1), channel_id=1, source_target_pairs={{0,1},{1,0},{2,3},{3,2},{4,5},{5,4},{6,7},{7,6},{8,9},{9,8},{10,11... | collective-permute-start | bytes 98312 | tf_op jit(solution)/shard_map/ppermute | solution.py:506
  1.3 0.9 %copy-start = (f32[8,4,16,128]{3,2,1,0:T(8,128)S(1)}, f32[8,4,16,128]{3,2,1,0:T(8,128)}, u32[]{:S(2)}) copy-start(f32[8,4,16,128]{3,2,1,0:T(8,128)} %source_ref.1) | copy-start | bytes 786436
  2.3 0.8 %copy-start.1 = (f32[4,16,128]{2,1,0:T(8,128)S(1)}, f32[4,16,128]{2,1,0:T(8,128)}, u32[]{:S(2)}) copy-start(f32[4,16,128]{2,1,0:T(8,128)} %refs_2_.1) | copy-start | bytes 98308
  2.3 0.8 %copy-start.2 = (f32[8]{0:T(128)S(1)}, f32[8]{0:T(128)}, u32[]{:S(2)}) copy-start(f32[8]{0:T(128)} %shifts_ref.1) | copy-start | bytes 100
  2.3 0.8 %copy-start.3 = (s32[8]{0:T(128)S(1)}, s32[8]{0:T(128)}, u32[]{:S(2)}) copy-start(s32[8]{0:T(128)} %index_ref.1) | copy-start | bytes 100
  2.3 0.8 %copy-start.4 = (f32[3]{0:T(128)S(1)}, f32[3]{0:T(128)}, u32[]{:S(2)}) copy-start(f32[3]{0:T(128)} %velocity_ref.1) | copy-start | bytes 40
  3.6 6.8 %collective-permute-start.2 = (f32[2,4,32,128]{3,2,1,0:T(8,128)S(1)}, f32[2,4,32,128]{3,2,1,0:T(8,128)S(1)}, u32[]{:S(2)}, u32[]{:S(2)}) collective-permute-start(f32[2,4,32,128]{3,2,1,0:T(8,128)S(1)} %get-tuple-element.28), channel_id=1, source_target_pairs={{0,2},{1,3},{2,0},{3,1},{4,6},{5,7},{6,4},{7,5},{8,10},{9,11},{10,... | collective-permute-start | bytes 393224 | tf_op jit(solution)/shard_map/ppermute | solution.py:479
  6.6 6.4 %collective-permute-start.3 = (f32[2,4,32,128]{3,2,1,0:T(8,128)S(1)}, f32[2,4,32,128]{3,2,1,0:T(8,128)S(1)}, u32[]{:S(2)}, u32[]{:S(2)}) collective-permute-start(f32[2,4,32,128]{3,2,1,0:T(8,128)S(1)} %get-tuple-element.29), channel_id=1, source_target_pairs={{0,4},{1,5},{2,6},{3,7},{4,0},{5,1},{6,2},{7,3},{8,12},{9,13},{10,... | collective-permute-start | bytes 393224 | tf_op jit(solution)/shard_map/ppermute | solution.py:479
  8.1 6.3 %collective-permute-start.4 = (f32[2,4,32,128]{3,2,1,0:T(8,128)S(1)}, f32[2,4,32,128]{3,2,1,0:T(8,128)S(1)}, u32[]{:S(2)}, u32[]{:S(2)}) collective-permute-start(f32[2,4,32,128]{3,2,1,0:T(8,128)S(1)} %get-tuple-element.30), channel_id=1, source_target_pairs={{0,6},{1,7},{2,4},{3,5},{4,2},{5,3},{6,0},{7,1},{8,14},{9,15},{10,... | collective-permute-start | bytes 393224 | tf_op jit(solution)/shard_map/ppermute | solution.py:479
  15.1 5.0 %collective-permute-start.5 = (f32[2,2,64,128]{3,2,1,0:T(8,128)S(1)}, f32[2,2,64,128]{3,2,1,0:T(8,128)S(1)}, u32[]{:S(2)}, u32[]{:S(2)}) collective-permute-start(f32[2,2,64,128]{3,2,1,0:T(8,128)S(1)} %get-tuple-element.32), channel_id=1, source_target_pairs={{0,8},{4,12},{8,0},{12,4},{16,24},{20,28},{24,16},{28,20},{1,9},{5... | collective-permute-start | bytes 393224 | tf_op jit(solution)/shard_map/ppermute | solution.py:532
  16.9 3.2 %collective-permute-start.6 = (f32[2,2,64,128]{3,2,1,0:T(8,128)S(1)}, f32[2,2,64,128]{3,2,1,0:T(8,128)S(1)}, u32[]{:S(2)}, u32[]{:S(2)}) collective-permute-start(f32[2,2,64,128]{3,2,1,0:T(8,128)S(1)} %get-tuple-element.33), channel_id=1, source_target_pairs={{8,16},{12,20},{16,8},{20,12},{9,17},{13,21},{17,9},{21,13},{10,18... | collective-permute-start | bytes 393224 | tf_op jit(solution)/shard_map/ppermute | solution.py:532
  21.4 9.7 %collective-permute-start.9 = (f32[4,32,128]{2,1,0:T(8,128)S(1)}, f32[4,32,128]{2,1,0:T(8,128)S(1)}, u32[]{:S(2)}, u32[]{:S(2)}) collective-permute-start(f32[4,32,128]{2,1,0:T(8,128)S(1)} %get-tuple-element.38.refs_2_), channel_id=1, source_target_pairs={{0,24},{4,28},{8,16},{12,20},{16,8},{20,12},{24,0},{28,4},{1,25},{... | collective-permute-start | bytes 196616 | tf_op jit(solution)/shard_map/ppermute | solution.py:488
  25.2 6.2 %collective-permute-start.8 = (f32[4,32,128]{2,1,0:T(8,128)S(1)}, f32[4,32,128]{2,1,0:T(8,128)S(1)}, u32[]{:S(2)}, u32[]{:S(2)}) collective-permute-start(f32[4,32,128]{2,1,0:T(8,128)S(1)} %get-tuple-element.38.refs_2_), channel_id=1, source_target_pairs={{0,16},{4,20},{8,24},{12,28},{16,0},{20,4},{24,8},{28,12},{1,17},{... | collective-permute-start | bytes 196616 | tf_op jit(solution)/shard_map/ppermute | solution.py:488
  28.4 4.3 %collective-permute-start.7 = (f32[4,32,128]{2,1,0:T(8,128)S(1)}, f32[4,32,128]{2,1,0:T(8,128)S(1)}, u32[]{:S(2)}, u32[]{:S(2)}) collective-permute-start(f32[4,32,128]{2,1,0:T(8,128)S(1)} %get-tuple-element.38.refs_2_), channel_id=1, source_target_pairs={{0,8},{4,12},{8,0},{12,4},{16,24},{20,28},{24,16},{28,20},{1,9},{5... | collective-permute-start | bytes 196616 | tf_op jit(solution)/shard_map/ppermute | solution.py:488
  28.4 6.6 %collective-permute-start.10 = (f32[2,64,128]{2,1,0:T(8,128)S(1)}, f32[2,64,128]{2,1,0:T(8,128)S(1)}, u32[]{:S(2)}, u32[]{:S(2)}) collective-permute-start(f32[2,64,128]{2,1,0:T(8,128)S(1)} %get-tuple-element.39), channel_id=1, source_target_pairs={{0,8},{4,12},{8,0},{12,4},{16,24},{20,28},{24,16},{28,20},{1,9},{5... | collective-permute-start | bytes 196616 | tf_op jit(solution)/shard_map/ppermute | solution.py:532
  30.4 4.6 %collective-permute-start.11 = (f32[2,64,128]{2,1,0:T(8,128)S(1)}, f32[2,64,128]{2,1,0:T(8,128)S(1)}, u32[]{:S(2)}, u32[]{:S(2)}) collective-permute-start(f32[2,64,128]{2,1,0:T(8,128)S(1)} %get-tuple-element.40), channel_id=1, source_target_pairs={{8,16},{12,20},{16,8},{20,12},{9,17},{13,21},{17,9},{21,13},{10,18... | collective-permute-start | bytes 196616 | tf_op jit(solution)/shard_map/ppermute | solution.py:532
  36.5 1.6 %collective-permute-start.12 = (f32[520,128]{1,0:T(8,128)S(1)}, f32[520,128]{1,0:T(8,128)S(1)}, u32[]{:S(2)}, u32[]{:S(2)}) collective-permute-start(f32[520,128]{1,0:T(8,128)S(1)} %get-tuple-element.42), channel_id=1, source_target_pairs={{0,1},{1,0},{2,3},{3,2},{4,5},{5,4},{6,7},{7,6},{8,9},{9,8},{10,11... | collective-permute-start | bytes 798728 | tf_op jit(solution)/shard_map/ppermute | solution.py:571
  38.7 5.8 %collective-permute-start.13 = (f32[272,128]{1,0:T(8,128)S(1)}, f32[272,128]{1,0:T(8,128)S(1)}, u32[]{:S(2)}, u32[]{:S(2)}) collective-permute-start(f32[272,128]{1,0:T(8,128)S(1)} %get-tuple-element.44), channel_id=1, source_target_pairs={{0,2},{1,3},{2,0},{3,1},{4,6},{5,7},{6,4},{7,5},{8,10},{9,11},{10,... | collective-permute-start | bytes 417800 | tf_op jit(solution)/shard_map/ppermute | solution.py:479
  40.3 6.6 %collective-permute-start.14 = (f32[272,128]{1,0:T(8,128)S(1)}, f32[272,128]{1,0:T(8,128)S(1)}, u32[]{:S(2)}, u32[]{:S(2)}) collective-permute-start(f32[272,128]{1,0:T(8,128)S(1)} %get-tuple-element.45), channel_id=1, source_target_pairs={{0,4},{1,5},{2,6},{3,7},{4,0},{5,1},{6,2},{7,3},{8,12},{9,13},{10,... | collective-permute-start | bytes 417800 | tf_op jit(solution)/shard_map/ppermute | solution.py:479
  41.8 6.9 %collective-permute-start.15 = (f32[272,128]{1,0:T(8,128)S(1)}, f32[272,128]{1,0:T(8,128)S(1)}, u32[]{:S(2)}, u32[]{:S(2)}) collective-permute-start(f32[272,128]{1,0:T(8,128)S(1)} %get-tuple-element.46), channel_id=1, source_target_pairs={{0,6},{1,7},{2,4},{3,5},{4,2},{5,3},{6,0},{7,1},{8,14},{9,15},{10,... | collective-permute-start | bytes 417800 | tf_op jit(solution)/shard_map/ppermute | solution.py:479
  48.7 5.8 %collective-permute-start.18 = (f32[8,128]{1,0:T(8,128)S(1)}, f32[8,128]{1,0:T(8,128)S(1)}, u32[]{:S(2)}, u32[]{:S(2)}) collective-permute-start(f32[8,128]{1,0:T(8,128)S(1)} %squares.1), channel_id=1, source_target_pairs={{0,24},{4,28},{8,16},{12,20},{16,8},{20,12},{24,0},{28,4},{1,25},{... | collective-permute-start | bytes 12296 | tf_op jit(solution)/shard_map/ppermute | solution.py:488
  50.9 4.5 %collective-permute-start.17 = (f32[8,128]{1,0:T(8,128)S(1)}, f32[8,128]{1,0:T(8,128)S(1)}, u32[]{:S(2)}, u32[]{:S(2)}) collective-permute-start(f32[8,128]{1,0:T(8,128)S(1)} %squares.1), channel_id=1, source_target_pairs={{0,16},{4,20},{8,24},{12,28},{16,0},{20,4},{24,8},{28,12},{1,17},{... | collective-permute-start | bytes 12296 | tf_op jit(solution)/shard_map/ppermute | solution.py:488
  51.7 3.7 %collective-permute-start.16 = (f32[8,128]{1,0:T(8,128)S(1)}, f32[8,128]{1,0:T(8,128)S(1)}, u32[]{:S(2)}, u32[]{:S(2)}) collective-permute-start(f32[8,128]{1,0:T(8,128)S(1)} %squares.1), channel_id=1, source_target_pairs={{0,8},{4,12},{8,0},{12,4},{16,24},{20,28},{24,16},{28,20},{1,9},{5... | collective-permute-start | bytes 12296 | tf_op jit(solution)/shard_map/ppermute | solution.py:488

commit v12 on v11

--- a/solution.py
+++ b/solution.py
@@ -233,6 +233,10 @@
     return jnp.where(col // 2 == row, 1.0, 0.0).astype(jnp.bfloat16)
 
 
+def step_of(k, count):
+    return -k % count
+
+
 def keep_kernel(place_ref, source_ref, out_ref):
     for n in range(out_ref.shape[0]):
         out_ref[n] = source_ref[2 * n + (place_ref[0] & 1)]
@@ -246,7 +250,7 @@
     mine = pl.ds(pl.multiple_of(core * by, 8), by)
     theirs = pl.ds(pl.multiple_of((1 - core) * by, 8), by)
     for m, out_ref in enumerate(out_refs):
-        target = jnp.bitwise_xor(chip, m)
+        target = jnp.bitwise_xor(chip, step_of(m, len(out_refs)))
         out_ref[0, :, mine, :] = mine_ref[target]
         out_ref[0, :, theirs, :] = theirs_ref[2 * target + core]
         out_ref[1, :, mine, :] = reaction_ref[...]
@@ -259,7 +263,7 @@
 def arrange_kernel(chips_y, place_ref, *refs):
     blocks, (slab_ref, first_ref, second_ref) = refs[:-3], refs[-3:]
     for m, block in enumerate(blocks):
-        owner = jnp.bitwise_xor(place_ref[0] // 2, m)
+        owner = jnp.bitwise_xor(place_ref[0] // 2, step_of(m, len(blocks)))
         _, bx, size, _ = block.shape
         planes = pl.ds((owner // chips_y) * bx, bx)
         rows = pl.ds(pl.multiple_of(lax.rem(owner, chips_y) * size, 8), size)
@@ -425,7 +429,7 @@
     chip, core = place_ref[0] // 2, place_ref[0] & 1
     area, half = bx * by, chips_y * by
     for m, out_ref in enumerate(out_refs):
-        target = jnp.bitwise_xor(chip, m)
+        target = jnp.bitwise_xor(chip, step_of(m, len(out_refs)))
         first = (target // chips_y) * bx * half + lax.rem(target, chips_y) * by
         for ref, column in ((kept_ref, core), (got_ref, 1 - core)):
             for n in range(2):
@@ -442,7 +446,7 @@
     _, bx, by, _ = iterate_ref.shape
     area = bx * by
     for m, part in enumerate(parts):
-        target = jnp.bitwise_xor(place_ref[0] // 2, m)
+        target = jnp.bitwise_xor(place_ref[0] // 2, step_of(m, len(parts)))
         for n in range(2):
             for k, ref in enumerate((iterate_ref, residual_ref)):
                 rows = pl.ds((2 * n + k) * area, area)
@@ -475,7 +479,7 @@
     devices = lax.axis_size("gx") * lax.axis_size("gy")
     moved = [pieces[0]]
     for k in range(1, len(pieces)):
-        pairs = [(i, i ^ (k * unit)) for i in range(devices)]
+        pairs = [(i, i ^ (step_of(k, len(pieces)) * unit)) for i in range(devices)]
         moved.append(lax.ppermute(pieces[k], ("gx", "gy"), pairs))
     return moved
 
@@ -581,7 +585,8 @@
     total = sum(swap_slabs(squares, step, slabs))
     rms = jnp.sqrt(total[:, 0] / (nx * ny * nz) + EPSILON)
     slots = jnp.arange(columns, dtype=jnp.int32)
-    mine = jnp.bitwise_xor(slots, column // 2 * 2)[:, None] == slots[None, :]
+    order = jnp.array([2 * step_of(k, chips) + n for k in range(chips) for n in range(2)], jnp.int32)
+    mine = jnp.bitwise_xor(slots, column // 2 * 2)[:, None] == order[None, :]
     residual_rms = jnp.sum(jnp.where(mine, rms[None, :], 0.0), axis=1)
     return iterate, residual, residual_rms
 

time: 56.5 us -> 57.2 us (1.012)
  waiting for transfers between devices: 19.2 us -> 20.2 us
  starting transfers between devices: 25.3 us -> 24.4 us
    ppermute x6, waiting for transfers between devices: 2.53 us -> 3.27 us  [swap_slabs(): moved.append(lax.ppermute(piece, 'gx', pairs))]
    ppermute x4, starting transfers between devices: 5.12 us -> 4.48 us  [exchange(): got.append(lax.ppermute(piece, 'gx', pairs))]
    unnamed x10 -> x12, local copies, waits for them, and re-layouts: 1.12 us -> 1.66 us
  transfers between devices with their start and end apart: 19 -> 19, of which waited for: 11 -> 9; matrix products, arithmetic and copies ran while one was open for 0% -> 0% of each run, Pallas kernels for 8% -> 8%
where the time goes in v12:
time: 57.2 us; the launch traced here: 56.9 us
  starting transfers between devices  24.4 us (43%)
  waiting for transfers between devices  20.2 us (35%)
  Pallas kernels  8.88 us (16%)
  local copies, waits for them, and re-layouts  1.66 us (3%)
  other arithmetic  1.02 us (2%)
  between operations  0.79 us (1%)
    ppermute x6, waiting for transfers between devices, swap_in_plane(): moved.append(lax.ppermute(pieces[k], ('gx', 'gy'), pairs))  12.7 us
    ppermute x6, starting transfers between devices, swap_slabs(): moved.append(lax.ppermute(piece, 'gx', pairs))  11.1 us
    pallas_call x9, Pallas kernels, local_kernel(): pl.pallas_call(kernel, out_shape=[jax.ShapeDtypeStruct(shape, jnp.float32...  8.88 us
    ppermute x6, starting transfers between devices, swap_in_plane(): moved.append(lax.ppermute(pieces[k], ('gx', 'gy'), pairs))  8.14 us
    ppermute x4, starting transfers between devices, exchange(): got.append(lax.ppermute(piece, 'gx', pairs))  4.48 us
    ppermute x6, waiting for transfers between devices, swap_slabs(): moved.append(lax.ppermute(piece, 'gx', pairs))  3.27 us
    ppermute x4, waiting for transfers between devices, exchange(): got.append(lax.ppermute(piece, 'gx', pairs))  2.61 us
    unnamed x12, local copies, waits for them, and re-layouts  1.66 us
  transfers between devices with their start and end apart: 19, of which 9 were waited for; matrix products, arithmetic and copies ran while one was open for 0% of the time, Pallas kernels for 8%

profile of v12, /device:TPU:0, one launch (start us, length us, event | category | flops | bytes accessed | tf_op | source)
XLA Modules:
  0.0 56.9 jit_solution(9655830324570348132)
XLA Ops:
  1.3 0.9 %copy-done = f32[8,4,16,128]{3,2,1,0:T(8,128)S(1)} copy-done((f32[8,4,16,128]{3,2,1,0:T(8,128)S(1)}, f32[8,4,16,128]{3,2,1,0:T(8,128)}, u32[]{:S(2)}) %copy-start) | copy-done | bytes 262168
  3.6 3.9 %collective-permute-start.2 = (f32[2,4,32,128]{3,2,1,0:T(8,128)S(1)}, f32[2,4,32,128]{3,2,1,0:T(8,128)S(1)}, u32[]{:S(2)}, u32[]{:S(2)}) collective-permute-start(f32[2,4,32,128]{3,2,1,0:T(8,128)S(1)} %get-tuple-element.28), channel_id=1, source_target_pairs={{0,6},{1,7},{2,4},{3,5},{4,2},{5,3},{6,0},{7,1},{8,14},{9,15},{10,... | collective-permute-start | bytes 393224 | tf_op jit(solution)/shard_map/ppermute | solution.py:483
  8.2 3.6 %collective-permute-done.2.refs_1_ = f32[2,4,32,128]{3,2,1,0:T(8,128)S(1)} collective-permute-done((f32[2,4,32,128]{3,2,1,0:T(8,128)S(1)}, f32[2,4,32,128]{3,2,1,0:T(8,128)S(1)}, u32[]{:S(2)}, u32[]{:S(2)}) %collective-permute-start.2) | collective-permute-done | bytes 131104 | tf_op jit(solution)/shard_map/ppermute | solution.py:483
  11.9 2.5 %collective-permute-done.3.refs_2_ = f32[2,4,32,128]{3,2,1,0:T(8,128)S(1)} collective-permute-done((f32[2,4,32,128]{3,2,1,0:T(8,128)S(1)}, f32[2,4,32,128]{3,2,1,0:T(8,128)S(1)}, u32[]{:S(2)}, u32[]{:S(2)}) %collective-permute-start.3) | collective-permute-done | bytes 131104 | tf_op jit(solution)/shard_map/ppermute | solution.py:483
  15.0 1.6 %collective-permute-start.5 = (f32[2,2,64,128]{3,2,1,0:T(8,128)S(1)}, f32[2,2,64,128]{3,2,1,0:T(8,128)S(1)}, u32[]{:S(2)}, u32[]{:S(2)}) collective-permute-start(f32[2,2,64,128]{3,2,1,0:T(8,128)S(1)} %get-tuple-element.32), channel_id=1, source_target_pairs={{0,8},{4,12},{8,0},{12,4},{16,24},{20,28},{24,16},{28,20},{1,9},{5... | collective-permute-start | bytes 393224 | tf_op jit(solution)/shard_map/ppermute | solution.py:536
  16.6 0.7 %collective-permute-start.6 = (f32[2,2,64,128]{3,2,1,0:T(8,128)S(1)}, f32[2,2,64,128]{3,2,1,0:T(8,128)S(1)}, u32[]{:S(2)}, u32[]{:S(2)}) collective-permute-start(f32[2,2,64,128]{3,2,1,0:T(8,128)S(1)} %get-tuple-element.33), channel_id=1, source_target_pairs={{8,16},{12,20},{16,8},{20,12},{9,17},{13,21},{17,9},{21,13},{10,18... | collective-permute-start | bytes 393224 | tf_op jit(solution)/shard_map/ppermute | solution.py:536
  17.4 2.6 %collective-permute-done.5.refs_3_ = f32[2,2,64,128]{3,2,1,0:T(8,128)S(1)} collective-permute-done((f32[2,2,64,128]{3,2,1,0:T(8,128)S(1)}, f32[2,2,64,128]{3,2,1,0:T(8,128)S(1)}, u32[]{:S(2)}, u32[]{:S(2)}) %collective-permute-start.5) | collective-permute-done | bytes 131104 | tf_op jit(solution)/shard_map/ppermute | solution.py:536
  20.0 1.3 %pre.1 = (f32[16,64,128]{2,1,0:T(8,128)S(1)}, f32[16,64,128]{2,1,0:T(8,128)S(1)}, f32[16,64,128]{2,1,0:T(8,128)S(1)}, f32[16,80,128]{2,1,0:T(8,128)S(1)}, f32[4,...) custom-call(s32[2]{0:T(128)S(1)} %pad_add_fusion.place_ref, ...), custom_call_target="tpu_custom_call" | custom-call | tf_op jit(solution)/shard_map/pre/pallas_call | solution.py:467
  21.3 3.7 %collective-permute-start.9 = (f32[4,32,128]{2,1,0:T(8,128)S(1)}, f32[4,32,128]{2,1,0:T(8,128)S(1)}, u32[]{:S(2)}, u32[]{:S(2)}) collective-permute-start(f32[4,32,128]{2,1,0:T(8,128)S(1)} %get-tuple-element.38.refs_2_), channel_id=1, source_target_pairs={{0,24},{4,28},{8,16},{12,20},{16,8},{20,12},{24,0},{28,4},{1,25},{... | collective-permute-start | bytes 196616 | tf_op jit(solution)/shard_map/ppermute | solution.py:492
  25.0 2.5 %collective-permute-start.8 = (f32[4,32,128]{2,1,0:T(8,128)S(1)}, f32[4,32,128]{2,1,0:T(8,128)S(1)}, u32[]{:S(2)}, u32[]{:S(2)}) collective-permute-start(f32[4,32,128]{2,1,0:T(8,128)S(1)} %get-tuple-element.38.refs_2_), channel_id=1, source_target_pairs={{0,16},{4,20},{8,24},{12,28},{16,0},{20,4},{24,8},{28,12},{1,17},{... | collective-permute-start | bytes 196616 | tf_op jit(solution)/shard_map/ppermute | solution.py:492
  28.0 1.5 %collective-permute-start.10 = (f32[2,64,128]{2,1,0:T(8,128)S(1)}, f32[2,64,128]{2,1,0:T(8,128)S(1)}, u32[]{:S(2)}, u32[]{:S(2)}) collective-permute-start(f32[2,64,128]{2,1,0:T(8,128)S(1)} %get-tuple-element.39), channel_id=1, source_target_pairs={{0,8},{4,12},{8,0},{12,4},{16,24},{20,28},{24,16},{28,20},{1,9},{5... | collective-permute-start | bytes 196616 | tf_op jit(solution)/shard_map/ppermute | solution.py:536
  29.5 0.7 %collective-permute-start.11 = (f32[2,64,128]{2,1,0:T(8,128)S(1)}, f32[2,64,128]{2,1,0:T(8,128)S(1)}, u32[]{:S(2)}, u32[]{:S(2)}) collective-permute-start(f32[2,64,128]{2,1,0:T(8,128)S(1)} %get-tuple-element.40), channel_id=1, source_target_pairs={{8,16},{12,20},{16,8},{20,12},{9,17},{13,21},{17,9},{21,13},{10,18... | collective-permute-start | bytes 196616 | tf_op jit(solution)/shard_map/ppermute | solution.py:536
  30.8 1.0 %collective-permute-done.7.refs_3_ = f32[4,32,128]{2,1,0:T(8,128)S(1)} collective-permute-done((f32[4,32,128]{2,1,0:T(8,128)S(1)}, f32[4,32,128]{2,1,0:T(8,128)S(1)}, u32[]{:S(2)}, u32[]{:S(2)}) %collective-permute-start.7) | collective-permute-done | bytes 65568 | tf_op jit(solution)/shard_map/ppermute | solution.py:492
  31.8 2.3 %coarse.1.refs_4_ = f32[256,128]{1,0:T(8,128)S(1)} custom-call(s32[2]{0:T(128)S(1)} %pad_add_fusion.place_ref, f32[8,128]{1,0:T(8,128)S(1)} %get-tuple-element.26.scalar_ref, bf16[128,128]{1,0:T(8,128)(2,1)S(1)} %get-tuple-element.50.refs_0_, bf16[128,128]{1,0:T(8,128)(2,1)S(1)} %get-tuple-element.49.refs_1_, f32[4,32,128]{2,1,0:T(8,128)S(1)} %get-tuple-element.38.refs_2_, ...), custom_call_target="tpu_custom_call" | custom-call | tf_op jit(solution)/shard_map/coarse/pallas_call | solution.py:467
  34.2 1.5 %post.1 = (f32[520,128]{1,0:T(8,128)S(1)}, f32[520,128]{1,0:T(8,128)S(1)}) custom-call(s32[2]{0:T(128)S(1)} %pad_add_fusion.place_ref, f32[8,128]{1,0:T(8,128)S(1)} %get-tuple-element.26.scalar_ref, f32[16,64,128]{2,1,0:T(8,128)S(1)} %get-tuple-element.34.refs_0_, f32[16,64,128]{2,1,0:T(8,128)S(1)} %get-tuple-element.35.refs_1_, ...), custom_call_target="tpu_custom_call" | custom-call | tf_op jit(solution)/shard_map/post/pallas_call | solution.py:467
  35.7 1.5 %collective-permute-done.12.got_ref = f32[520,128]{1,0:T(8,128)S(1)} collective-permute-done((f32[520,128]{1,0:T(8,128)S(1)}, f32[520,128]{1,0:T(8,128)S(1)}, u32[]{:S(2)}, u32[]{:S(2)}) %collective-permute-start.12) | collective-permute-done | bytes 266272 | tf_op jit(solution)/shard_map/ppermute | solution.py:575
  37.9 2.9 %collective-permute-start.13 = (f32[272,128]{1,0:T(8,128)S(1)}, f32[272,128]{1,0:T(8,128)S(1)}, u32[]{:S(2)}, u32[]{:S(2)}) collective-permute-start(f32[272,128]{1,0:T(8,128)S(1)} %get-tuple-element.44), channel_id=1, source_target_pairs={{0,6},{1,7},{2,4},{3,5},{4,2},{5,3},{6,0},{7,1},{8,14},{9,15},{10,... | collective-permute-start | bytes 417800 | tf_op jit(solution)/shard_map/ppermute | solution.py:483
  41.4 3.9 %collective-permute-done.13.refs_1_ = f32[272,128]{1,0:T(8,128)S(1)} collective-permute-done((f32[272,128]{1,0:T(8,128)S(1)}, f32[272,128]{1,0:T(8,128)S(1)}, u32[]{:S(2)}, u32[]{:S(2)}) %collective-permute-start.13) | collective-permute-done | bytes 139296 | tf_op jit(solution)/shard_map/ppermute | solution.py:483
  45.3 2.7 %collective-permute-done.14.refs_2_ = f32[272,128]{1,0:T(8,128)S(1)} collective-permute-done((f32[272,128]{1,0:T(8,128)S(1)}, f32[272,128]{1,0:T(8,128)S(1)}, u32[]{:S(2)}, u32[]{:S(2)}) %collective-permute-start.14) | collective-permute-done | bytes 139296 | tf_op jit(solution)/shard_map/ppermute | solution.py:483
  48.0 3.0 %collective-permute-start.18 = (f32[8,128]{1,0:T(8,128)S(1)}, f32[8,128]{1,0:T(8,128)S(1)}, u32[]{:S(2)}, u32[]{:S(2)}) collective-permute-start(f32[8,128]{1,0:T(8,128)S(1)} %squares.1), channel_id=1, source_target_pairs={{0,24},{4,28},{8,16},{12,20},{16,8},{20,12},{24,0},{28,4},{1,25},{... | collective-permute-start | bytes 12296 | tf_op jit(solution)/shard_map/ppermute | solution.py:492
  51.3 1.2 %collective-permute-start.16 = (f32[8,128]{1,0:T(8,128)S(1)}, f32[8,128]{1,0:T(8,128)S(1)}, u32[]{:S(2)}, u32[]{:S(2)}) collective-permute-start(f32[8,128]{1,0:T(8,128)S(1)} %squares.1), channel_id=1, source_target_pairs={{0,8},{4,12},{8,0},{12,4},{16,24},{20,28},{24,16},{28,20},{1,9},{5... | collective-permute-start | bytes 12296 | tf_op jit(solution)/shard_map/ppermute | solution.py:492
  52.5 1.4 %collect.1 = (f32[8,4,16,128]{3,2,1,0:T(8,128)}, f32[8,4,16,128]{3,2,1,0:T(8,128)}) custom-call(s32[2]{0:T(128)S(1)} %pad_add_fusion.place_ref, f32[272,128]{1,0:T(8,128)S(1)} %get-tuple-element.43.refs_0_, f32[272,128]{1,0:T(8,128)S(1)} %collective-permute-done.13.refs_1_, f32[272,128]{1,0:T(8,128)S(1)} %collective-permute-done.14.refs_2_, ...), custom_call_target="tpu_custom_call" | custom-call | tf_op jit(solution)/shard_map/collect/pallas_call | solution.py:467
  53.9 1.7 %collective-permute-done.17 = f32[8,128]{1,0:T(8,128)S(1)} collective-permute-done((f32[8,128]{1,0:T(8,128)S(1)}, f32[8,128]{1,0:T(8,128)S(1)}, u32[]{:S(2)}, u32[]{:S(2)}) %collective-permute-start.17) | collective-permute-done | bytes 4128 | tf_op jit(solution)/shard_map/ppermute | solution.py:492
  56.2 0.7 %select_reduce_fusion = f32[8]{0:T(128)} fusion(f32[8]{0:T(128)S(1)} %sqrt_reduce_fusion, s32[8]{0:T(128)S(1)} %copy-done.5, s32[8]{0:T(128)S(1)} %iota_xor_fusion), kind=kLoop, calls=%fused_computation.7 | loop fusion | flops 184 | bytes 128 | tf_op jit(solution)/shard_map/reduce_sum | solution.py:590
  (43 shorter events, 6.7 us)
Async XLA Ops:
  0.6 2.2 %collective-permute-start = (f32[8,4,16,128]{3,2,1,0:T(8,128)}, f32[8,4,16,128]{3,2,1,0:T(8,128)S(1)}, u32[]{:S(2)}, u32[]{:S(2)}) collective-permute-start(f32[8,4,16,128]{3,2,1,0:T(8,128)} %source_ref.1), channel_id=1, source_target_pairs={{0,1},{1,0},{2,3},{3,2},{4,5},{5,4},{6,7},{7,6},{8,9},{9,8},{10,11... | collective-permute-start | bytes 786440 | tf_op jit(solution)/shard_map/ppermute | solution.py:510
  1.1 1.7 %collective-permute-start.1 = (f32[4,16,128]{2,1,0:T(8,128)}, f32[4,16,128]{2,1,0:T(8,128)S(1)}, u32[]{:S(2)}, u32[]{:S(2)}) collective-permute-start(f32[4,16,128]{2,1,0:T(8,128)} %refs_2_.1), channel_id=1, source_target_pairs={{0,1},{1,0},{2,3},{3,2},{4,5},{5,4},{6,7},{7,6},{8,9},{9,8},{10,11... | collective-permute-start | bytes 98312 | tf_op jit(solution)/shard_map/ppermute | solution.py:510
  1.3 0.9 %copy-start = (f32[8,4,16,128]{3,2,1,0:T(8,128)S(1)}, f32[8,4,16,128]{3,2,1,0:T(8,128)}, u32[]{:S(2)}) copy-start(f32[8,4,16,128]{3,2,1,0:T(8,128)} %source_ref.1) | copy-start | bytes 786436
  2.3 0.8 %copy-start.1 = (f32[4,16,128]{2,1,0:T(8,128)S(1)}, f32[4,16,128]{2,1,0:T(8,128)}, u32[]{:S(2)}) copy-start(f32[4,16,128]{2,1,0:T(8,128)} %refs_2_.1) | copy-start | bytes 98308
  2.3 0.8 %copy-start.2 = (f32[8]{0:T(128)S(1)}, f32[8]{0:T(128)}, u32[]{:S(2)}) copy-start(f32[8]{0:T(128)} %shifts_ref.1) | copy-start | bytes 100
  2.3 0.8 %copy-start.3 = (s32[8]{0:T(128)S(1)}, s32[8]{0:T(128)}, u32[]{:S(2)}) copy-start(s32[8]{0:T(128)} %index_ref.1) | copy-start | bytes 100
  2.3 0.8 %copy-start.4 = (f32[3]{0:T(128)S(1)}, f32[3]{0:T(128)}, u32[]{:S(2)}) copy-start(f32[3]{0:T(128)} %velocity_ref.1) | copy-start | bytes 40
  3.6 8.2 %collective-permute-start.2 = (f32[2,4,32,128]{3,2,1,0:T(8,128)S(1)}, f32[2,4,32,128]{3,2,1,0:T(8,128)S(1)}, u32[]{:S(2)}, u32[]{:S(2)}) collective-permute-start(f32[2,4,32,128]{3,2,1,0:T(8,128)S(1)} %get-tuple-element.28), channel_id=1, source_target_pairs={{0,6},{1,7},{2,4},{3,5},{4,2},{5,3},{6,0},{7,1},{8,14},{9,15},{10,... | collective-permute-start | bytes 393224 | tf_op jit(solution)/shard_map/ppermute | solution.py:483
  7.6 6.8 %collective-permute-start.3 = (f32[2,4,32,128]{3,2,1,0:T(8,128)S(1)}, f32[2,4,32,128]{3,2,1,0:T(8,128)S(1)}, u32[]{:S(2)}, u32[]{:S(2)}) collective-permute-start(f32[2,4,32,128]{3,2,1,0:T(8,128)S(1)} %get-tuple-element.29), channel_id=1, source_target_pairs={{0,4},{1,5},{2,6},{3,7},{4,0},{5,1},{6,2},{7,3},{8,12},{9,13},{10,... | collective-permute-start | bytes 393224 | tf_op jit(solution)/shard_map/ppermute | solution.py:483
  8.1 6.3 %collective-permute-start.4 = (f32[2,4,32,128]{3,2,1,0:T(8,128)S(1)}, f32[2,4,32,128]{3,2,1,0:T(8,128)S(1)}, u32[]{:S(2)}, u32[]{:S(2)}) collective-permute-start(f32[2,4,32,128]{3,2,1,0:T(8,128)S(1)} %get-tuple-element.30), channel_id=1, source_target_pairs={{0,2},{1,3},{2,0},{3,1},{4,6},{5,7},{6,4},{7,5},{8,10},{9,11},{10,... | collective-permute-start | bytes 393224 | tf_op jit(solution)/shard_map/ppermute | solution.py:483
  15.0 5.0 %collective-permute-start.5 = (f32[2,2,64,128]{3,2,1,0:T(8,128)S(1)}, f32[2,2,64,128]{3,2,1,0:T(8,128)S(1)}, u32[]{:S(2)}, u32[]{:S(2)}) collective-permute-start(f32[2,2,64,128]{3,2,1,0:T(8,128)S(1)} %get-tuple-element.32), channel_id=1, source_target_pairs={{0,8},{4,12},{8,0},{12,4},{16,24},{20,28},{24,16},{28,20},{1,9},{5... | collective-permute-start | bytes 393224 | tf_op jit(solution)/shard_map/ppermute | solution.py:536
  16.6 3.4 %collective-permute-start.6 = (f32[2,2,64,128]{3,2,1,0:T(8,128)S(1)}, f32[2,2,64,128]{3,2,1,0:T(8,128)S(1)}, u32[]{:S(2)}, u32[]{:S(2)}) collective-permute-start(f32[2,2,64,128]{3,2,1,0:T(8,128)S(1)} %get-tuple-element.33), channel_id=1, source_target_pairs={{8,16},{12,20},{16,8},{20,12},{9,17},{13,21},{17,9},{21,13},{10,18... | collective-permute-start | bytes 393224 | tf_op jit(solution)/shard_map/ppermute | solution.py:536
  21.3 8.9 %collective-permute-start.9 = (f32[4,32,128]{2,1,0:T(8,128)S(1)}, f32[4,32,128]{2,1,0:T(8,128)S(1)}, u32[]{:S(2)}, u32[]{:S(2)}) collective-permute-start(f32[4,32,128]{2,1,0:T(8,128)S(1)} %get-tuple-element.38.refs_2_), channel_id=1, source_target_pairs={{0,24},{4,28},{8,16},{12,20},{16,8},{20,12},{24,0},{28,4},{1,25},{... | collective-permute-start | bytes 196616 | tf_op jit(solution)/shard_map/ppermute | solution.py:492
  25.0 5.8 %collective-permute-start.8 = (f32[4,32,128]{2,1,0:T(8,128)S(1)}, f32[4,32,128]{2,1,0:T(8,128)S(1)}, u32[]{:S(2)}, u32[]{:S(2)}) collective-permute-start(f32[4,32,128]{2,1,0:T(8,128)S(1)} %get-tuple-element.38.refs_2_), channel_id=1, source_target_pairs={{0,16},{4,20},{8,24},{12,28},{16,0},{20,4},{24,8},{28,12},{1,17},{... | collective-permute-start | bytes 196616 | tf_op jit(solution)/shard_map/ppermute | solution.py:492
  27.5 4.3 %collective-permute-start.7 = (f32[4,32,128]{2,1,0:T(8,128)S(1)}, f32[4,32,128]{2,1,0:T(8,128)S(1)}, u32[]{:S(2)}, u32[]{:S(2)}) collective-permute-start(f32[4,32,128]{2,1,0:T(8,128)S(1)} %get-tuple-element.38.refs_2_), channel_id=1, source_target_pairs={{0,8},{4,12},{8,0},{12,4},{16,24},{20,28},{24,16},{28,20},{1,9},{5... | collective-permute-start | bytes 196616 | tf_op jit(solution)/shard_map/ppermute | solution.py:492
  28.0 6.1 %collective-permute-start.10 = (f32[2,64,128]{2,1,0:T(8,128)S(1)}, f32[2,64,128]{2,1,0:T(8,128)S(1)}, u32[]{:S(2)}, u32[]{:S(2)}) collective-permute-start(f32[2,64,128]{2,1,0:T(8,128)S(1)} %get-tuple-element.39), channel_id=1, source_target_pairs={{0,8},{4,12},{8,0},{12,4},{16,24},{20,28},{24,16},{28,20},{1,9},{5... | collective-permute-start | bytes 196616 | tf_op jit(solution)/shard_map/ppermute | solution.py:536
  29.5 4.6 %collective-permute-start.11 = (f32[2,64,128]{2,1,0:T(8,128)S(1)}, f32[2,64,128]{2,1,0:T(8,128)S(1)}, u32[]{:S(2)}, u32[]{:S(2)}) collective-permute-start(f32[2,64,128]{2,1,0:T(8,128)S(1)} %get-tuple-element.40), channel_id=1, source_target_pairs={{8,16},{12,20},{16,8},{20,12},{9,17},{13,21},{17,9},{21,13},{10,18... | collective-permute-start | bytes 196616 | tf_op jit(solution)/shard_map/ppermute | solution.py:536
  35.7 1.6 %collective-permute-start.12 = (f32[520,128]{1,0:T(8,128)S(1)}, f32[520,128]{1,0:T(8,128)S(1)}, u32[]{:S(2)}, u32[]{:S(2)}) collective-permute-start(f32[520,128]{1,0:T(8,128)S(1)} %get-tuple-element.42), channel_id=1, source_target_pairs={{0,1},{1,0},{2,3},{3,2},{4,5},{5,4},{6,7},{7,6},{8,9},{9,8},{10,11... | collective-permute-start | bytes 798728 | tf_op jit(solution)/shard_map/ppermute | solution.py:575
  37.9 7.5 %collective-permute-start.13 = (f32[272,128]{1,0:T(8,128)S(1)}, f32[272,128]{1,0:T(8,128)S(1)}, u32[]{:S(2)}, u32[]{:S(2)}) collective-permute-start(f32[272,128]{1,0:T(8,128)S(1)} %get-tuple-element.44), channel_id=1, source_target_pairs={{0,6},{1,7},{2,4},{3,5},{4,2},{5,3},{6,0},{7,1},{8,14},{9,15},{10,... | collective-permute-start | bytes 417800 | tf_op jit(solution)/shard_map/ppermute | solution.py:483
  40.8 7.2 %collective-permute-start.14 = (f32[272,128]{1,0:T(8,128)S(1)}, f32[272,128]{1,0:T(8,128)S(1)}, u32[]{:S(2)}, u32[]{:S(2)}) collective-permute-start(f32[272,128]{1,0:T(8,128)S(1)} %get-tuple-element.45), channel_id=1, source_target_pairs={{0,4},{1,5},{2,6},{3,7},{4,0},{5,1},{6,2},{7,3},{8,12},{9,13},{10,... | collective-permute-start | bytes 417800 | tf_op jit(solution)/shard_map/ppermute | solution.py:483
  41.3 6.7 %collective-permute-start.15 = (f32[272,128]{1,0:T(8,128)S(1)}, f32[272,128]{1,0:T(8,128)S(1)}, u32[]{:S(2)}, u32[]{:S(2)}) collective-permute-start(f32[272,128]{1,0:T(8,128)S(1)} %get-tuple-element.46), channel_id=1, source_target_pairs={{0,2},{1,3},{2,0},{3,1},{4,6},{5,7},{6,4},{7,5},{8,10},{9,11},{10,... | collective-permute-start | bytes 417800 | tf_op jit(solution)/shard_map/ppermute | solution.py:483
  48.0 5.8 %collective-permute-start.18 = (f32[8,128]{1,0:T(8,128)S(1)}, f32[8,128]{1,0:T(8,128)S(1)}, u32[]{:S(2)}, u32[]{:S(2)}) collective-permute-start(f32[8,128]{1,0:T(8,128)S(1)} %squares.1), channel_id=1, source_target_pairs={{0,24},{4,28},{8,16},{12,20},{16,8},{20,12},{24,0},{28,4},{1,25},{... | collective-permute-start | bytes 12296 | tf_op jit(solution)/shard_map/ppermute | solution.py:492
  51.1 4.5 %collective-permute-start.17 = (f32[8,128]{1,0:T(8,128)S(1)}, f32[8,128]{1,0:T(8,128)S(1)}, u32[]{:S(2)}, u32[]{:S(2)}) collective-permute-start(f32[8,128]{1,0:T(8,128)S(1)} %squares.1), channel_id=1, source_target_pairs={{0,16},{4,20},{8,24},{12,28},{16,0},{20,4},{24,8},{28,12},{1,17},{... | collective-permute-start | bytes 12296 | tf_op jit(solution)/shard_map/ppermute | solution.py:492
  51.3 4.3 %collective-permute-start.16 = (f32[8,128]{1,0:T(8,128)S(1)}, f32[8,128]{1,0:T(8,128)S(1)}, u32[]{:S(2)}, u32[]{:S(2)}) collective-permute-start(f32[8,128]{1,0:T(8,128)S(1)} %squares.1), channel_id=1, source_target_pairs={{0,8},{4,12},{8,0},{12,4},{16,24},{20,28},{24,16},{28,20},{1,9},{5... | collective-permute-start | bytes 12296 | tf_op jit(solution)/shard_map/ppermute | solution.py:492
  (1 other events, 0.7 us)

commit v13 on v11

--- a/solution.py
+++ b/solution.py
@@ -256,20 +256,29 @@
         scalar_ref[pl.ds(n, 1), :] = jnp.full((1, LANES), scalar, jnp.float32)
 
 
+def edge_kernel(chips_y, place_ref, *refs):
+    blocks, edge_ref = refs[:-1], refs[-1]
+    for m, block in enumerate(blocks):
+        chip = jnp.bitwise_xor(place_ref[0] // 2, m)
+        _, bx, size, _ = block.shape
+        planes = pl.ds((chip // chips_y) * (bx - NEAR), NEAR)
+        rows = pl.ds(pl.multiple_of(lax.rem(chip, chips_y) * size, 8), size)
+        edge_ref[:, :, rows, :] = block[:, planes]
+
+
 def arrange_kernel(chips_y, place_ref, *refs):
-    blocks, (slab_ref, first_ref, second_ref) = refs[:-3], refs[-3:]
+    blocks, (slab_ref, edge_ref) = refs[:-2], refs[-2:]
+    chip = place_ref[0] // 2
     for m, block in enumerate(blocks):
-        owner = jnp.bitwise_xor(place_ref[0] // 2, m)
+        owner = jnp.bitwise_xor(chip, m)
         _, bx, size, _ = block.shape
         planes = pl.ds((owner // chips_y) * bx, bx)
         rows = pl.ds(pl.multiple_of(lax.rem(owner, chips_y) * size, 8), size)
         slab_ref[:, planes, rows, :] = block[...]
-    even = 1 - (place_ref[1] & 1)
-    first_ref[...] = slab_ref[:, pl.ds(even * (SLAB - NEAR), NEAR)]
-    second_ref[...] = slab_ref[:, pl.ds((1 - even) * (SLAB - NEAR), NEAR)]
-
-
-def pre_kernel(slabs, place_ref, scalar_ref, *refs):
+    edge_ref[...] = slab_ref[:, pl.ds((1 - chip // chips_y) * (SLAB - NEAR), NEAR)]
+
+
+def pre_kernel(slabs, chips_y, place_ref, scalar_ref, *refs):
     pool_ref, pool_up_ref, slab_ref, first_ref, second_ref = refs[:5]
     f, r, w, v1, coarse_ref, first_out, second_out, v0, tmp, pooled = refs[5:]
     ny = f.shape[1]
@@ -281,7 +290,8 @@
     even = 1 - (slab & 1)
 
     f[pl.ds(HALO, SLAB)], r[pl.ds(HALO, SLAB)] = slab_ref[0], slab_ref[1]
-    for ref, above in ((first_ref, even), (second_ref, 1 - even)):
+    x = place_ref[0] // 2 // chips_y
+    for ref, above in ((first_ref, 1 - x), (second_ref, x)):
         planes = pl.ds((HALO - NEAR) + above * (SLAB + NEAR), NEAR)
         f[planes], r[planes] = ref[0], ref[1]
 
@@ -516,13 +526,21 @@
     blocks = swap_in_plane(blocks, 2)
 
     edge = (2, NEAR, ny, nz)
-    slab, *edges = local_kernel(
+    (own_edge,) = local_kernel(
+        functools.partial(edge_kernel, chips_y), "edge", (place,), blocks[:chips_y], [edge]
+    )
+    slab, other_edge = local_kernel(
         functools.partial(arrange_kernel, chips_y),
         "arrange",
         (place,),
         blocks,
-        [(2, SLAB, ny, nz), edge, edge],
-    )
+        [(2, SLAB, ny, nz), edge],
+    )
+    beside = []
+    for n, piece in enumerate((own_edge, other_edge)):
+        pairs = [(i, i + step if i % step != n else i - step) for i in range(gx_size)]
+        pairs = [(i, j) for i, j in pairs if 0 <= j < gx_size]
+        beside.append(lax.ppermute(piece, "gx", pairs))
 
     def exchange(pieces):
         got = []
@@ -534,10 +552,10 @@
 
     grid, rimmed = (count, ny, nz), (count, ny + 16, nz)
     f, r, w, v1, coarse, *beyond = local_kernel(
-        functools.partial(pre_kernel, slabs),
+        functools.partial(pre_kernel, slabs, chips_y),
         "pre",
         scalars,
-        (pool_matrix(0), pool_matrix(LANES // 2), slab, *exchange(edges)),
+        (pool_matrix(0), pool_matrix(LANES // 2), slab, *beside),
         [grid, grid, grid, rimmed, (SLAB // 2, ny // 2, nz)] + [(NEAR, ny, nz)] * 2,
         [rimmed, (SLAB, ny, nz), (2, SLAB // 2 * ny // 2, nz)],
     )

time: 56.5 us -> 56.7 us (level)
  Pallas kernels: 8.88 us -> 9.45 us
    ppermute x0 -> x2, starting transfers between devices: none -> 4.93 us  [column_body(): beside.append(lax.ppermute(piece, 'gx', pairs))]
    ppermute x4 -> x2, starting transfers between devices: 5.12 us -> 2.04 us  [exchange(): got.append(lax.ppermute(piece, 'gx', pairs))]
    ppermute x4 -> x2, waiting for transfers between devices: 2.46 us -> 0.01 us  [exchange(): got.append(lax.ppermute(piece, 'gx', pairs))]
    ppermute x0 -> x2, waiting for transfers between devices: none -> 2.36 us  [column_body(): beside.append(lax.ppermute(piece, 'gx', pairs))]
    ppermute x6, waiting for transfers between devices: 12.6 us -> 10.8 us  [swap_in_plane(): moved.append(lax.ppermute(pieces[k], ('gx', 'gy'), pairs))]
    ppermute x6, starting transfers between devices: 11.4 us -> 9.57 us  [swap_slabs(): moved.append(lax.ppermute(piece, 'gx', pairs))]
    ppermute x6, waiting for transfers between devices: 2.53 us -> 4.05 us  [swap_slabs(): moved.append(lax.ppermute(piece, 'gx', pairs))]
    pallas_call x9 -> x10, Pallas kernels: 8.88 us -> 9.45 us  [local_kernel(): pl.pallas_call(kernel, out_shape=[jax.ShapeDtypeStruct(shape, jnp.float32...]
  transfers between devices with their start and end apart: 19 -> 19, of which waited for: 11 -> 10; matrix products, arithmetic and copies ran while one was open for 0% -> 0% of each run, Pallas kernels for 8% -> 10%
where the time goes in v13:
time: 56.7 us; the launch traced here: 56.4 us
  starting transfers between devices  25.3 us (45%)
  waiting for transfers between devices  18.7 us (33%)
  Pallas kernels  9.45 us (17%)
  local copies, waits for them, and re-layouts  1.12 us (2%)
  other arithmetic  1.04 us (2%)
  between operations  0.81 us (1%)
    ppermute x6, waiting for transfers between devices, swap_in_plane(): moved.append(lax.ppermute(pieces[k], ('gx', 'gy'), pairs))  10.8 us
    ppermute x6, starting transfers between devices, swap_slabs(): moved.append(lax.ppermute(piece, 'gx', pairs))  9.57 us
    pallas_call x10, Pallas kernels, local_kernel(): pl.pallas_call(kernel, out_shape=[jax.ShapeDtypeStruct(shape, jnp.float32...  9.45 us
    ppermute x6, starting transfers between devices, swap_in_plane(): moved.append(lax.ppermute(pieces[k], ('gx', 'gy'), pairs))  8.1 us
    ppermute x2, starting transfers between devices, column_body(): beside.append(lax.ppermute(piece, 'gx', pairs))  4.93 us
    ppermute x6, waiting for transfers between devices, swap_slabs(): moved.append(lax.ppermute(piece, 'gx', pairs))  4.05 us
    ppermute x2, waiting for transfers between devices, column_body(): beside.append(lax.ppermute(piece, 'gx', pairs))  2.36 us
    ppermute x2, starting transfers between devices, exchange(): got.append(lax.ppermute(piece, 'gx', pairs))  2.04 us
  transfers between devices with their start and end apart: 19, of which 10 were waited for; matrix products, arithmetic and copies ran while one was open for 0% of the time, Pallas kernels for 10%

profile of v13, /device:TPU:0, one launch (start us, length us, event | category | flops | bytes accessed | tf_op | source)
XLA Modules:
  0.0 56.4 jit_solution(18379136227476370790)
XLA Ops:
  1.3 0.9 %copy-done = f32[8,4,16,128]{3,2,1,0:T(8,128)S(1)} copy-done((f32[8,4,16,128]{3,2,1,0:T(8,128)S(1)}, f32[8,4,16,128]{3,2,1,0:T(8,128)}, u32[]{:S(2)}) %copy-start) | copy-done | bytes 262168
  3.6 3.0 %collective-permute-start.2 = (f32[2,4,32,128]{3,2,1,0:T(8,128)S(1)}, f32[2,4,32,128]{3,2,1,0:T(8,128)S(1)}, u32[]{:S(2)}, u32[]{:S(2)}) collective-permute-start(f32[2,4,32,128]{3,2,1,0:T(8,128)S(1)} %get-tuple-element.27), channel_id=1, source_target_pairs={{0,2},{1,3},{2,0},{3,1},{4,6},{5,7},{6,4},{7,5},{8,10},{9,11},{10,... | collective-permute-start | bytes 393224 | tf_op jit(solution)/shard_map/ppermute | solution.py:489
  6.6 1.5 %collective-permute-start.3 = (f32[2,4,32,128]{3,2,1,0:T(8,128)S(1)}, f32[2,4,32,128]{3,2,1,0:T(8,128)S(1)}, u32[]{:S(2)}, u32[]{:S(2)}) collective-permute-start(f32[2,4,32,128]{3,2,1,0:T(8,128)S(1)} %get-tuple-element.28), channel_id=1, source_target_pairs={{0,4},{1,5},{2,6},{3,7},{4,0},{5,1},{6,2},{7,3},{8,12},{9,13},{10,... | collective-permute-start | bytes 393224 | tf_op jit(solution)/shard_map/ppermute | solution.py:489
  8.2 2.2 %collective-permute-done.2.refs_1_ = f32[2,4,32,128]{3,2,1,0:T(8,128)S(1)} collective-permute-done((f32[2,4,32,128]{3,2,1,0:T(8,128)S(1)}, f32[2,4,32,128]{3,2,1,0:T(8,128)S(1)}, u32[]{:S(2)}, u32[]{:S(2)}) %collective-permute-start.2) | collective-permute-done | bytes 131104 | tf_op jit(solution)/shard_map/ppermute | solution.py:489
  11.0 1.3 %collective-permute-start.5 = (f32[2,2,64,128]{3,2,1,0:T(8,128)S(1)}, f32[2,2,64,128]{3,2,1,0:T(8,128)S(1)}, u32[]{:S(2)}, u32[]{:S(2)}) collective-permute-start(f32[2,2,64,128]{3,2,1,0:T(8,128)S(1)} %edge.1), channel_id=1, source_target_pairs={{4,12},{8,0},{12,20},{16,8},{20,28},{24,16},{5,13},{9,1},{13,21},{... | collective-permute-start | bytes 393224 | tf_op jit(solution)/shard_map/ppermute | solution.py:543
  13.0 1.4 %collective-permute-done.4.refs_3_ = f32[2,4,32,128]{3,2,1,0:T(8,128)S(1)} collective-permute-done((f32[2,4,32,128]{3,2,1,0:T(8,128)S(1)}, f32[2,4,32,128]{3,2,1,0:T(8,128)S(1)}, u32[]{:S(2)}, u32[]{:S(2)}) %collective-permute-start.4) | collective-permute-done | bytes 131104 | tf_op jit(solution)/shard_map/ppermute | solution.py:489
  15.1 3.6 %collective-permute-start.6 = (f32[2,2,64,128]{3,2,1,0:T(8,128)S(1)}, f32[2,2,64,128]{3,2,1,0:T(8,128)S(1)}, u32[]{:S(2)}, u32[]{:S(2)}) collective-permute-start(f32[2,2,64,128]{3,2,1,0:T(8,128)S(1)} %get-tuple-element.31), channel_id=1, source_target_pairs={{0,8},{8,16},{12,4},{16,24},{20,12},{28,20},{1,9},{9,17},{13,5},{1... | collective-permute-start | bytes 393224 | tf_op jit(solution)/shard_map/ppermute | solution.py:543
  18.8 2.4 %collective-permute-done.6.refs_4_ = f32[2,2,64,128]{3,2,1,0:T(8,128)S(1)} collective-permute-done((f32[2,2,64,128]{3,2,1,0:T(8,128)S(1)}, f32[2,2,64,128]{3,2,1,0:T(8,128)S(1)}, u32[]{:S(2)}, u32[]{:S(2)}) %collective-permute-start.6) | collective-permute-done | bytes 131104 | tf_op jit(solution)/shard_map/ppermute | solution.py:543
  21.2 1.3 %pre.1 = (f32[16,64,128]{2,1,0:T(8,128)S(1)}, f32[16,64,128]{2,1,0:T(8,128)S(1)}, f32[16,64,128]{2,1,0:T(8,128)S(1)}, f32[16,80,128]{2,1,0:T(8,128)S(1)}, f32[4,...) custom-call(s32[2]{0:T(128)S(1)} %pad_add_fusion.place_ref, ...), custom_call_target="tpu_custom_call" | custom-call | tf_op jit(solution)/shard_map/pre/pallas_call | solution.py:473
  22.5 4.5 %collective-permute-start.9 = (f32[4,32,128]{2,1,0:T(8,128)S(1)}, f32[4,32,128]{2,1,0:T(8,128)S(1)}, u32[]{:S(2)}, u32[]{:S(2)}) collective-permute-start(f32[4,32,128]{2,1,0:T(8,128)S(1)} %get-tuple-element.36.refs_2_), channel_id=1, source_target_pairs={{0,24},{4,28},{8,16},{12,20},{16,8},{20,12},{24,0},{28,4},{1,25},{... | collective-permute-start | bytes 196616 | tf_op jit(solution)/shard_map/ppermute | solution.py:498
  27.7 1.4 %collective-permute-start.10 = (f32[2,64,128]{2,1,0:T(8,128)S(1)}, f32[2,64,128]{2,1,0:T(8,128)S(1)}, u32[]{:S(2)}, u32[]{:S(2)}) collective-permute-start(f32[2,64,128]{2,1,0:T(8,128)S(1)} %get-tuple-element.37), channel_id=1, source_target_pairs={{0,8},{4,12},{8,0},{12,4},{16,24},{20,28},{24,16},{28,20},{1,9},{5... | collective-permute-start | bytes 196616 | tf_op jit(solution)/shard_map/ppermute | solution.py:550
  29.7 3.2 %collective-permute-done.8.refs_4_ = f32[4,32,128]{2,1,0:T(8,128)S(1)} collective-permute-done((f32[4,32,128]{2,1,0:T(8,128)S(1)}, f32[4,32,128]{2,1,0:T(8,128)S(1)}, u32[]{:S(2)}, u32[]{:S(2)}) %collective-permute-start.8) | collective-permute-done | bytes 65568 | tf_op jit(solution)/shard_map/ppermute | solution.py:498
  33.0 2.3 %coarse.1.refs_4_ = f32[256,128]{1,0:T(8,128)S(1)} custom-call(s32[2]{0:T(128)S(1)} %pad_add_fusion.place_ref, f32[8,128]{1,0:T(8,128)S(1)} %get-tuple-element.25.scalar_ref, bf16[128,128]{1,0:T(8,128)(2,1)S(1)} %get-tuple-element.48.refs_0_, bf16[128,128]{1,0:T(8,128)(2,1)S(1)} %get-tuple-element.47.refs_1_, f32[4,32,128]{2,1,0:T(8,128)S(1)} %get-tuple-element.36.refs_2_, ...), custom_call_target="tpu_custom_call" | custom-call | tf_op jit(solution)/shard_map/coarse/pallas_call | solution.py:473
  35.3 1.5 %post.1 = (f32[520,128]{1,0:T(8,128)S(1)}, f32[520,128]{1,0:T(8,128)S(1)}) custom-call(s32[2]{0:T(128)S(1)} %pad_add_fusion.place_ref, f32[8,128]{1,0:T(8,128)S(1)} %get-tuple-element.25.scalar_ref, f32[16,64,128]{2,1,0:T(8,128)S(1)} %get-tuple-element.32.refs_0_, f32[16,64,128]{2,1,0:T(8,128)S(1)} %get-tuple-element.33.refs_1_, ...), custom_call_target="tpu_custom_call" | custom-call | tf_op jit(solution)/shard_map/post/pallas_call | solution.py:473
  36.9 1.5 %collective-permute-done.12.got_ref = f32[520,128]{1,0:T(8,128)S(1)} collective-permute-done((f32[520,128]{1,0:T(8,128)S(1)}, f32[520,128]{1,0:T(8,128)S(1)}, u32[]{:S(2)}, u32[]{:S(2)}) %collective-permute-start.12) | collective-permute-done | bytes 266272 | tf_op jit(solution)/shard_map/ppermute | solution.py:589
  39.1 1.4 %collective-permute-start.13 = (f32[272,128]{1,0:T(8,128)S(1)}, f32[272,128]{1,0:T(8,128)S(1)}, u32[]{:S(2)}, u32[]{:S(2)}) collective-permute-start(f32[272,128]{1,0:T(8,128)S(1)} %get-tuple-element.42), channel_id=1, source_target_pairs={{0,2},{1,3},{2,0},{3,1},{4,6},{5,7},{6,4},{7,5},{8,10},{9,11},{10,... | collective-permute-start | bytes 417800 | tf_op jit(solution)/shard_map/ppermute | solution.py:489
  40.7 2.0 %collective-permute-start.15 = (f32[272,128]{1,0:T(8,128)S(1)}, f32[272,128]{1,0:T(8,128)S(1)}, u32[]{:S(2)}, u32[]{:S(2)}) collective-permute-start(f32[272,128]{1,0:T(8,128)S(1)} %get-tuple-element.44), channel_id=1, source_target_pairs={{0,6},{1,7},{2,4},{3,5},{4,2},{5,3},{6,0},{7,1},{8,14},{9,15},{10,... | collective-permute-start | bytes 417800 | tf_op jit(solution)/shard_map/ppermute | solution.py:489
  42.6 2.2 %collective-permute-done.13.refs_1_ = f32[272,128]{1,0:T(8,128)S(1)} collective-permute-done((f32[272,128]{1,0:T(8,128)S(1)}, f32[272,128]{1,0:T(8,128)S(1)}, u32[]{:S(2)}, u32[]{:S(2)}) %collective-permute-start.13) | collective-permute-done | bytes 139296 | tf_op jit(solution)/shard_map/ppermute | solution.py:489
  44.8 2.2 %collective-permute-done.14.refs_2_ = f32[272,128]{1,0:T(8,128)S(1)} collective-permute-done((f32[272,128]{1,0:T(8,128)S(1)}, f32[272,128]{1,0:T(8,128)S(1)}, u32[]{:S(2)}, u32[]{:S(2)}) %collective-permute-start.14) | collective-permute-done | bytes 139296 | tf_op jit(solution)/shard_map/ppermute | solution.py:489
  47.0 2.0 %collective-permute-done.15.refs_3_ = f32[272,128]{1,0:T(8,128)S(1)} collective-permute-done((f32[272,128]{1,0:T(8,128)S(1)}, f32[272,128]{1,0:T(8,128)S(1)}, u32[]{:S(2)}, u32[]{:S(2)}) %collective-permute-start.15) | collective-permute-done | bytes 139296 | tf_op jit(solution)/shard_map/ppermute | solution.py:489
  49.0 1.1 %collective-permute-start.18 = (f32[8,128]{1,0:T(8,128)S(1)}, f32[8,128]{1,0:T(8,128)S(1)}, u32[]{:S(2)}, u32[]{:S(2)}) collective-permute-start(f32[8,128]{1,0:T(8,128)S(1)} %squares.1), channel_id=1, source_target_pairs={{0,24},{4,28},{8,16},{12,20},{16,8},{20,12},{24,0},{28,4},{1,25},{... | collective-permute-start | bytes 12296 | tf_op jit(solution)/shard_map/ppermute | solution.py:498
  50.1 1.9 %collective-permute-start.17 = (f32[8,128]{1,0:T(8,128)S(1)}, f32[8,128]{1,0:T(8,128)S(1)}, u32[]{:S(2)}, u32[]{:S(2)}) collective-permute-start(f32[8,128]{1,0:T(8,128)S(1)} %squares.1), channel_id=1, source_target_pairs={{0,16},{4,20},{8,24},{12,28},{16,0},{20,4},{24,8},{28,12},{1,17},{... | collective-permute-start | bytes 12296 | tf_op jit(solution)/shard_map/ppermute | solution.py:498
  52.0 1.4 %collective-permute-start.16 = (f32[8,128]{1,0:T(8,128)S(1)}, f32[8,128]{1,0:T(8,128)S(1)}, u32[]{:S(2)}, u32[]{:S(2)}) collective-permute-start(f32[8,128]{1,0:T(8,128)S(1)} %squares.1), channel_id=1, source_target_pairs={{0,8},{4,12},{8,0},{12,4},{16,24},{20,28},{24,16},{28,20},{1,9},{5... | collective-permute-start | bytes 12296 | tf_op jit(solution)/shard_map/ppermute | solution.py:498
  53.4 1.4 %collect.1 = (f32[8,4,16,128]{3,2,1,0:T(8,128)}, f32[8,4,16,128]{3,2,1,0:T(8,128)}) custom-call(s32[2]{0:T(128)S(1)} %pad_add_fusion.place_ref, f32[272,128]{1,0:T(8,128)S(1)} %get-tuple-element.41.refs_0_, f32[272,128]{1,0:T(8,128)S(1)} %collective-permute-done.13.refs_1_, f32[272,128]{1,0:T(8,128)S(1)} %collective-permute-done.14.refs_2_, ...), custom_call_target="tpu_custom_call" | custom-call | tf_op jit(solution)/shard_map/collect/pallas_call | solution.py:473
  (42 shorter events, 7.9 us)
Async XLA Ops:
  0.6 2.2 %collective-permute-start = (f32[8,4,16,128]{3,2,1,0:T(8,128)}, f32[8,4,16,128]{3,2,1,0:T(8,128)S(1)}, u32[]{:S(2)}, u32[]{:S(2)}) collective-permute-start(f32[8,4,16,128]{3,2,1,0:T(8,128)} %source_ref.1), channel_id=1, source_target_pairs={{0,1},{1,0},{2,3},{3,2},{4,5},{5,4},{6,7},{7,6},{8,9},{9,8},{10,11... | collective-permute-start | bytes 786440 | tf_op jit(solution)/shard_map/ppermute | solution.py:516
  1.1 1.7 %collective-permute-start.1 = (f32[4,16,128]{2,1,0:T(8,128)}, f32[4,16,128]{2,1,0:T(8,128)S(1)}, u32[]{:S(2)}, u32[]{:S(2)}) collective-permute-start(f32[4,16,128]{2,1,0:T(8,128)} %refs_2_.1), channel_id=1, source_target_pairs={{0,1},{1,0},{2,3},{3,2},{4,5},{5,4},{6,7},{7,6},{8,9},{9,8},{10,11... | collective-permute-start | bytes 98312 | tf_op jit(solution)/shard_map/ppermute | solution.py:516
  1.3 0.9 %copy-start = (f32[8,4,16,128]{3,2,1,0:T(8,128)S(1)}, f32[8,4,16,128]{3,2,1,0:T(8,128)}, u32[]{:S(2)}) copy-start(f32[8,4,16,128]{3,2,1,0:T(8,128)} %source_ref.1) | copy-start | bytes 786436
  2.3 0.8 %copy-start.1 = (f32[4,16,128]{2,1,0:T(8,128)S(1)}, f32[4,16,128]{2,1,0:T(8,128)}, u32[]{:S(2)}) copy-start(f32[4,16,128]{2,1,0:T(8,128)} %refs_2_.1) | copy-start | bytes 98308
  2.3 0.8 %copy-start.2 = (f32[8]{0:T(128)S(1)}, f32[8]{0:T(128)}, u32[]{:S(2)}) copy-start(f32[8]{0:T(128)} %shifts_ref.1) | copy-start | bytes 100
  2.3 0.8 %copy-start.3 = (s32[8]{0:T(128)S(1)}, s32[8]{0:T(128)}, u32[]{:S(2)}) copy-start(s32[8]{0:T(128)} %index_ref.1) | copy-start | bytes 100
  2.3 0.8 %copy-start.4 = (f32[3]{0:T(128)S(1)}, f32[3]{0:T(128)}, u32[]{:S(2)}) copy-start(f32[3]{0:T(128)} %velocity_ref.1) | copy-start | bytes 40
  3.6 6.8 %collective-permute-start.2 = (f32[2,4,32,128]{3,2,1,0:T(8,128)S(1)}, f32[2,4,32,128]{3,2,1,0:T(8,128)S(1)}, u32[]{:S(2)}, u32[]{:S(2)}) collective-permute-start(f32[2,4,32,128]{3,2,1,0:T(8,128)S(1)} %get-tuple-element.27), channel_id=1, source_target_pairs={{0,2},{1,3},{2,0},{3,1},{4,6},{5,7},{6,4},{7,5},{8,10},{9,11},{10,... | collective-permute-start | bytes 393224 | tf_op jit(solution)/shard_map/ppermute | solution.py:489
  6.6 6.4 %collective-permute-start.3 = (f32[2,4,32,128]{3,2,1,0:T(8,128)S(1)}, f32[2,4,32,128]{3,2,1,0:T(8,128)S(1)}, u32[]{:S(2)}, u32[]{:S(2)}) collective-permute-start(f32[2,4,32,128]{3,2,1,0:T(8,128)S(1)} %get-tuple-element.28), channel_id=1, source_target_pairs={{0,4},{1,5},{2,6},{3,7},{4,0},{5,1},{6,2},{7,3},{8,12},{9,13},{10,... | collective-permute-start | bytes 393224 | tf_op jit(solution)/shard_map/ppermute | solution.py:489
  8.1 6.3 %collective-permute-start.4 = (f32[2,4,32,128]{3,2,1,0:T(8,128)S(1)}, f32[2,4,32,128]{3,2,1,0:T(8,128)S(1)}, u32[]{:S(2)}, u32[]{:S(2)}) collective-permute-start(f32[2,4,32,128]{3,2,1,0:T(8,128)S(1)} %get-tuple-element.29), channel_id=1, source_target_pairs={{0,6},{1,7},{2,4},{3,5},{4,2},{5,3},{6,0},{7,1},{8,14},{9,15},{10,... | collective-permute-start | bytes 393224 | tf_op jit(solution)/shard_map/ppermute | solution.py:489
  11.0 7.9 %collective-permute-start.5 = (f32[2,2,64,128]{3,2,1,0:T(8,128)S(1)}, f32[2,2,64,128]{3,2,1,0:T(8,128)S(1)}, u32[]{:S(2)}, u32[]{:S(2)}) collective-permute-start(f32[2,2,64,128]{3,2,1,0:T(8,128)S(1)} %edge.1), channel_id=1, source_target_pairs={{4,12},{8,0},{12,20},{16,8},{20,28},{24,16},{5,13},{9,1},{13,21},{... | collective-permute-start | bytes 393224 | tf_op jit(solution)/shard_map/ppermute | solution.py:543
  15.1 6.1 %collective-permute-start.6 = (f32[2,2,64,128]{3,2,1,0:T(8,128)S(1)}, f32[2,2,64,128]{3,2,1,0:T(8,128)S(1)}, u32[]{:S(2)}, u32[]{:S(2)}) collective-permute-start(f32[2,2,64,128]{3,2,1,0:T(8,128)S(1)} %get-tuple-element.31), channel_id=1, source_target_pairs={{0,8},{8,16},{12,4},{16,24},{20,12},{28,20},{1,9},{9,17},{13,5},{1... | collective-permute-start | bytes 393224 | tf_op jit(solution)/shard_map/ppermute | solution.py:543
  22.5 7.2 %collective-permute-start.9 = (f32[4,32,128]{2,1,0:T(8,128)S(1)}, f32[4,32,128]{2,1,0:T(8,128)S(1)}, u32[]{:S(2)}, u32[]{:S(2)}) collective-permute-start(f32[4,32,128]{2,1,0:T(8,128)S(1)} %get-tuple-element.36.refs_2_), channel_id=1, source_target_pairs={{0,24},{4,28},{8,16},{12,20},{16,8},{20,12},{24,0},{28,4},{1,25},{... | collective-permute-start | bytes 196616 | tf_op jit(solution)/shard_map/ppermute | solution.py:498
  27.0 5.9 %collective-permute-start.8 = (f32[4,32,128]{2,1,0:T(8,128)S(1)}, f32[4,32,128]{2,1,0:T(8,128)S(1)}, u32[]{:S(2)}, u32[]{:S(2)}) collective-permute-start(f32[4,32,128]{2,1,0:T(8,128)S(1)} %get-tuple-element.36.refs_2_), channel_id=1, source_target_pairs={{0,16},{4,20},{8,24},{12,28},{16,0},{20,4},{24,8},{28,12},{1,17},{... | collective-permute-start | bytes 196616 | tf_op jit(solution)/shard_map/ppermute | solution.py:498
  27.1 5.9 %collective-permute-start.7 = (f32[4,32,128]{2,1,0:T(8,128)S(1)}, f32[4,32,128]{2,1,0:T(8,128)S(1)}, u32[]{:S(2)}, u32[]{:S(2)}) collective-permute-start(f32[4,32,128]{2,1,0:T(8,128)S(1)} %get-tuple-element.36.refs_2_), channel_id=1, source_target_pairs={{0,8},{4,12},{8,0},{12,4},{16,24},{20,28},{24,16},{28,20},{1,9},{5... | collective-permute-start | bytes 196616 | tf_op jit(solution)/shard_map/ppermute | solution.py:498
  27.7 7.6 %collective-permute-start.10 = (f32[2,64,128]{2,1,0:T(8,128)S(1)}, f32[2,64,128]{2,1,0:T(8,128)S(1)}, u32[]{:S(2)}, u32[]{:S(2)}) collective-permute-start(f32[2,64,128]{2,1,0:T(8,128)S(1)} %get-tuple-element.37), channel_id=1, source_target_pairs={{0,8},{4,12},{8,0},{12,4},{16,24},{20,28},{24,16},{28,20},{1,9},{5... | collective-permute-start | bytes 196616 | tf_op jit(solution)/shard_map/ppermute | solution.py:550
  29.1 6.3 %collective-permute-start.11 = (f32[2,64,128]{2,1,0:T(8,128)S(1)}, f32[2,64,128]{2,1,0:T(8,128)S(1)}, u32[]{:S(2)}, u32[]{:S(2)}) collective-permute-start(f32[2,64,128]{2,1,0:T(8,128)S(1)} %get-tuple-element.38), channel_id=1, source_target_pairs={{8,16},{12,20},{16,8},{20,12},{9,17},{13,21},{17,9},{21,13},{10,18... | collective-permute-start | bytes 196616 | tf_op jit(solution)/shard_map/ppermute | solution.py:550
  36.9 1.6 %collective-permute-start.12 = (f32[520,128]{1,0:T(8,128)S(1)}, f32[520,128]{1,0:T(8,128)S(1)}, u32[]{:S(2)}, u32[]{:S(2)}) collective-permute-start(f32[520,128]{1,0:T(8,128)S(1)} %get-tuple-element.40), channel_id=1, source_target_pairs={{0,1},{1,0},{2,3},{3,2},{4,5},{5,4},{6,7},{7,6},{8,9},{9,8},{10,11... | collective-permute-start | bytes 798728 | tf_op jit(solution)/shard_map/ppermute | solution.py:589
  39.1 5.8 %collective-permute-start.13 = (f32[272,128]{1,0:T(8,128)S(1)}, f32[272,128]{1,0:T(8,128)S(1)}, u32[]{:S(2)}, u32[]{:S(2)}) collective-permute-start(f32[272,128]{1,0:T(8,128)S(1)} %get-tuple-element.42), channel_id=1, source_target_pairs={{0,2},{1,3},{2,0},{3,1},{4,6},{5,7},{6,4},{7,5},{8,10},{9,11},{10,... | collective-permute-start | bytes 417800 | tf_op jit(solution)/shard_map/ppermute | solution.py:489
  40.5 6.6 %collective-permute-start.14 = (f32[272,128]{1,0:T(8,128)S(1)}, f32[272,128]{1,0:T(8,128)S(1)}, u32[]{:S(2)}, u32[]{:S(2)}) collective-permute-start(f32[272,128]{1,0:T(8,128)S(1)} %get-tuple-element.43), channel_id=1, source_target_pairs={{0,4},{1,5},{2,6},{3,7},{4,0},{5,1},{6,2},{7,3},{8,12},{9,13},{10,... | collective-permute-start | bytes 417800 | tf_op jit(solution)/shard_map/ppermute | solution.py:489
  40.7 8.4 %collective-permute-start.15 = (f32[272,128]{1,0:T(8,128)S(1)}, f32[272,128]{1,0:T(8,128)S(1)}, u32[]{:S(2)}, u32[]{:S(2)}) collective-permute-start(f32[272,128]{1,0:T(8,128)S(1)} %get-tuple-element.44), channel_id=1, source_target_pairs={{0,6},{1,7},{2,4},{3,5},{4,2},{5,3},{6,0},{7,1},{8,14},{9,15},{10,... | collective-permute-start | bytes 417800 | tf_op jit(solution)/shard_map/ppermute | solution.py:489
  49.0 5.8 %collective-permute-start.18 = (f32[8,128]{1,0:T(8,128)S(1)}, f32[8,128]{1,0:T(8,128)S(1)}, u32[]{:S(2)}, u32[]{:S(2)}) collective-permute-start(f32[8,128]{1,0:T(8,128)S(1)} %squares.1), channel_id=1, source_target_pairs={{0,24},{4,28},{8,16},{12,20},{16,8},{20,12},{24,0},{28,4},{1,25},{... | collective-permute-start | bytes 12296 | tf_op jit(solution)/shard_map/ppermute | solution.py:498
  50.1 4.7 %collective-permute-start.17 = (f32[8,128]{1,0:T(8,128)S(1)}, f32[8,128]{1,0:T(8,128)S(1)}, u32[]{:S(2)}, u32[]{:S(2)}) collective-permute-start(f32[8,128]{1,0:T(8,128)S(1)} %squares.1), channel_id=1, source_target_pairs={{0,16},{4,20},{8,24},{12,28},{16,0},{20,4},{24,8},{28,12},{1,17},{... | collective-permute-start | bytes 12296 | tf_op jit(solution)/shard_map/ppermute | solution.py:498
  52.0 3.6 %collective-permute-start.16 = (f32[8,128]{1,0:T(8,128)S(1)}, f32[8,128]{1,0:T(8,128)S(1)}, u32[]{:S(2)}, u32[]{:S(2)}) collective-permute-start(f32[8,128]{1,0:T(8,128)S(1)} %squares.1), channel_id=1, source_target_pairs={{0,8},{4,12},{8,0},{12,4},{16,24},{20,28},{24,16},{28,20},{1,9},{5... | collective-permute-start | bytes 12296 | tf_op jit(solution)/shard_map/ppermute | solution.py:498

commit v14 on v13

--- a/solution.py
+++ b/solution.py
@@ -256,18 +256,17 @@
         scalar_ref[pl.ds(n, 1), :] = jnp.full((1, LANES), scalar, jnp.float32)
 
 
-def edge_kernel(chips_y, place_ref, *refs):
-    blocks, edge_ref = refs[:-1], refs[-1]
+def half_kernel(chips_y, place_ref, *refs):
+    blocks, half_ref = refs[:-1], refs[-1]
     for m, block in enumerate(blocks):
+        size = block.shape[2]
         chip = jnp.bitwise_xor(place_ref[0] // 2, m)
-        _, bx, size, _ = block.shape
-        planes = pl.ds((chip // chips_y) * (bx - NEAR), NEAR)
         rows = pl.ds(pl.multiple_of(lax.rem(chip, chips_y) * size, 8), size)
-        edge_ref[:, :, rows, :] = block[:, planes]
+        half_ref[:, :, rows, :] = block[...]
 
 
 def arrange_kernel(chips_y, place_ref, *refs):
-    blocks, (slab_ref, edge_ref) = refs[:-2], refs[-2:]
+    blocks, (slab_ref, near_ref, far_ref) = refs[:-3], refs[-3:]
     chip = place_ref[0] // 2
     for m, block in enumerate(blocks):
         owner = jnp.bitwise_xor(chip, m)
@@ -275,25 +274,49 @@
         planes = pl.ds((owner // chips_y) * bx, bx)
         rows = pl.ds(pl.multiple_of(lax.rem(owner, chips_y) * size, 8), size)
         slab_ref[:, planes, rows, :] = block[...]
-    edge_ref[...] = slab_ref[:, pl.ds((1 - chip // chips_y) * (SLAB - NEAR), NEAR)]
+    other = 1 - chip // chips_y
+    near_ref[...] = slab_ref[:, pl.ds(other * (SLAB - NEAR), NEAR)]
+    far_ref[...] = slab_ref[:, pl.ds(NEAR + other * (SLAB - 3 * NEAR), NEAR)]
+
+
+def beyond_kernel(slabs, chips_y, place_ref, scalar_ref, half_ref, near_ref, far_ref, *refs):
+    out_refs, (f, r, w, v0) = refs[:2], refs[2:]
+    ny, slab = f.shape[1], place_ref[1]
+    x = place_ref[0] // 2 // chips_y
+    fine = Level(0, ny, LANES, 0, scalar_ref, f, r, w)
+    zero_rows(v0, ny)
+    last = NEAR * (1 - x)
+    sides = ((1 - x, ((half_ref, 0, HALO),)), (x, ((near_ref, last, NEAR), (far_ref, NEAR - last, NEAR))))
+    for out_ref, (above, parts) in zip(out_refs, sides):
+        for ref, first, size in parts:
+            f[pl.ds(first, size)], r[pl.ds(first, size)] = ref[0], ref[1]
+        beside = jnp.where(above == 1, slab < slabs - 1, slab > 0)
+        inside = jnp.where(beside, DAMPING, 0.0)
+
+        def put(at, weight):
+            w[at] = weight
+            v0[at, pl.ds(8, ny), :] = weight * f[at]
+
+        sweep(range(HALO), lambda at: inside / (r[at] + fine.centre), put)
+        for n in range(NEAR):
+            out_ref[n] = fine.smoothed(v0, 1 + n)
 
 
 def pre_kernel(slabs, chips_y, place_ref, scalar_ref, *refs):
-    pool_ref, pool_up_ref, slab_ref, first_ref, second_ref = refs[:5]
-    f, r, w, v1, coarse_ref, first_out, second_out, v0, tmp, pooled = refs[5:]
+    pool_ref, pool_up_ref, slab_ref, half_ref, near_ref = refs[:5]
+    f, r, w, v1, coarse_ref, v0, tmp, pooled = refs[5:]
     ny = f.shape[1]
     slab = place_ref[1]
     fine = Level(0, ny, LANES, 0, scalar_ref, f, r, w)
     zero_rows(v0, ny)
     zero_rows(v1, ny)
     after = HALO + SLAB
-    even = 1 - (slab & 1)
 
     f[pl.ds(HALO, SLAB)], r[pl.ds(HALO, SLAB)] = slab_ref[0], slab_ref[1]
     x = place_ref[0] // 2 // chips_y
-    for ref, above in ((first_ref, 1 - x), (second_ref, x)):
+    for above, ref, first in ((1 - x, half_ref, x * NEAR), (x, near_ref, 0)):
         planes = pl.ds((HALO - NEAR) + above * (SLAB + NEAR), NEAR)
-        f[planes], r[planes] = ref[0], ref[1]
+        f[planes], r[planes] = ref[0, pl.ds(first, NEAR)], ref[1, pl.ds(first, NEAR)]
 
     inside = [jnp.where(slab > 0, DAMPING, 0.0)] * HALO
     inside += [DAMPING] * SLAB
@@ -306,8 +329,6 @@
     known = range(HALO - NEAR, after + NEAR)
     sweep(known, lambda x: inside[x] / (r[x] + fine.centre), put)
     fine.smooth(v0, v1, known[1:-1])
-    for ref, above in ((first_out, even), (second_out, 1 - even)):
-        ref[...] = v1[pl.ds(HALO + 1 + above * (SLAB - HALO), NEAR), pl.ds(8, ny), :]
     half = ny // 2
 
     def coarsened(x):
@@ -388,15 +409,15 @@
     out_ref[...] = split_dot(values, spread)
 
 
-def post_kernel(by, place_ref, scalar_ref, *refs):
+def post_kernel(by, chips_y, place_ref, scalar_ref, *refs):
     f, r, w, v1, correction, first_ref, second_ref, kept_ref, sent_ref, va, vb, tmp = refs
     count, ny = f.shape[:2]
     fine = Level(0, ny, LANES, 0, scalar_ref, f, r, w)
     for v in (va, vb):
         zero_rows(v, ny)
-    even, half = 1 - (place_ref[1] & 1), ny // 2
+    x, half = place_ref[0] // 2 // chips_y, ny // 2
     window = correction.shape[0] // half
-    for ref, above in ((first_ref, even), (second_ref, 1 - even)):
+    for ref, above in ((first_ref, 1 - x), (second_ref, x)):
         va[pl.ds(1 + above * (SLAB + HALO), NEAR), pl.ds(8, ny), :] = ref[...]
 
     def refined(x):
@@ -526,40 +547,44 @@
     blocks = swap_in_plane(blocks, 2)
 
     edge = (2, NEAR, ny, nz)
-    (own_edge,) = local_kernel(
-        functools.partial(edge_kernel, chips_y), "edge", (place,), blocks[:chips_y], [edge]
-    )
-    slab, other_edge = local_kernel(
+    (own_half,) = local_kernel(
+        functools.partial(half_kernel, chips_y),
+        "half",
+        (place,),
+        blocks[:chips_y],
+        [(2, HALO, ny, nz)],
+    )
+    slab, near, far = local_kernel(
         functools.partial(arrange_kernel, chips_y),
         "arrange",
         (place,),
         blocks,
-        [(2, SLAB, ny, nz), edge],
-    )
-    beside = []
-    for n, piece in enumerate((own_edge, other_edge)):
-        pairs = [(i, i + step if i % step != n else i - step) for i in range(gx_size)]
-        pairs = [(i, j) for i, j in pairs if 0 <= j < gx_size]
-        beside.append(lax.ppermute(piece, "gx", pairs))
-
-    def exchange(pieces):
-        got = []
-        for n, piece in enumerate(pieces):
-            pairs = [(i, i + step if i // step % 2 == n else i - step) for i in range(gx_size)]
-            pairs = [(i, j) for i, j in pairs if 0 <= j < gx_size]
-            got.append(lax.ppermute(piece, "gx", pairs))
-        return got
-
+        [(2, SLAB, ny, nz), edge, edge],
+    )
+
+    def send_beside(piece, up):
+        pairs = [(i, i + step if i % step == up else i - step) for i in range(gx_size)]
+        return lax.ppermute(piece, "gx", [(i, j) for i, j in pairs if 0 <= j < gx_size])
+
+    beside = [send_beside(own_half, 1), send_beside(near, 0), send_beside(far, 0)]
     grid, rimmed = (count, ny, nz), (count, ny + 16, nz)
-    f, r, w, v1, coarse, *beyond = local_kernel(
+    f, r, w, v1, coarse = local_kernel(
         functools.partial(pre_kernel, slabs, chips_y),
         "pre",
         scalars,
-        (pool_matrix(0), pool_matrix(LANES // 2), slab, *beside),
-        [grid, grid, grid, rimmed, (SLAB // 2, ny // 2, nz)] + [(NEAR, ny, nz)] * 2,
+        (pool_matrix(0), pool_matrix(LANES // 2), slab, *beside[:2]),
+        [grid, grid, grid, rimmed, (SLAB // 2, ny // 2, nz)],
         [rimmed, (SLAB, ny, nz), (2, SLAB // 2 * ny // 2, nz)],
     )
     gathered = swap_slabs(coarse, step, slabs)
+    beyond = local_kernel(
+        functools.partial(beyond_kernel, slabs, chips_y),
+        "beyond",
+        scalars,
+        beside,
+        [(NEAR, ny, nz)] * 2,
+        [(HALO, ny, nz)] * 3 + [(HALO, ny + 16, nz)],
+    )
 
     coarse_grid = (nx // 2, ny // 2, nz)
     coarse_rimmed = (nx // 2 + HALO, ny // 2 + 16, nz)
@@ -574,10 +599,10 @@
     )
     result = (SLAB * ny + 8, nz)
     kept, sent = local_kernel(
-        functools.partial(post_kernel, by),
+        functools.partial(post_kernel, by, chips_y),
         "post",
         scalars,
-        (f, r, w, v1, correction, *exchange(beyond)),
+        (f, r, w, v1, correction, *beyond),
         [result, result],
         [rimmed] * 2 + [(SLAB, ny, nz)],
     )

time: 56.7 us -> 56.7 us (level)
  waiting for transfers between devices: 18.7 us -> 16.4 us
  starting transfers between devices: 25.3 us -> 26.8 us
  Pallas kernels: 9.45 us -> 10.3 us
    ppermute x4 -> x3, waiting for transfers between devices: 2.37 us -> 0.01 us  [send_beside(): lax.ppermute(piece, 'gx', [(i, j) for i, j in pairs if 0 <= j < gx_size])]
    ppermute x4 -> x3, starting transfers between devices: 6.97 us -> 8.41 us  [send_beside(): lax.ppermute(piece, 'gx', [(i, j) for i, j in pairs if 0 <= j < gx_size])]
    pallas_call x10 -> x11, Pallas kernels: 9.45 us -> 10.3 us  [local_kernel(): pl.pallas_call(kernel, out_shape=[jax.ShapeDtypeStruct(shape, jnp.float32...]
  transfers between devices with their start and end apart: 19 -> 18, of which waited for: 10 -> 10; matrix products, arithmetic and copies ran while one was open for 0% -> 0% of each run, Pallas kernels for 10% -> 9%
where the time goes in v14:
time: 56.7 us; the launch traced here: 56.4 us
  starting transfers between devices  26.8 us (47%)
  waiting for transfers between devices  16.4 us (29%)
  Pallas kernels  10.3 us (18%)
  local copies, waits for them, and re-layouts  1.12 us (2%)
  other arithmetic  1.04 us (2%)
  between operations  0.8 us (1%)
    ppermute x6, waiting for transfers between devices, swap_in_plane(): moved.append(lax.ppermute(pieces[k], ('gx', 'gy'), pairs))  10.8 us
    pallas_call x11, Pallas kernels, local_kernel(): pl.pallas_call(kernel, out_shape=[jax.ShapeDtypeStruct(shape, jnp.float32...  10.3 us
    ppermute x6, starting transfers between devices, swap_slabs(): moved.append(lax.ppermute(piece, 'gx', pairs))  9.62 us
    ppermute x3, starting transfers between devices, send_beside(): lax.ppermute(piece, 'gx', [(i, j) for i, j in pairs if 0 <= j < gx_size])  8.41 us
    ppermute x6, starting transfers between devices, swap_in_plane(): moved.append(lax.ppermute(pieces[k], ('gx', 'gy'), pairs))  8.1 us
    ppermute x6, waiting for transfers between devices, swap_slabs(): moved.append(lax.ppermute(piece, 'gx', pairs))  4.06 us
    ppermute x1, waiting for transfers between devices, column_body(): lax.ppermute(sent, 'gy', cores)  1.53 us
  transfers between devices with their start and end apart: 18, of which 10 were waited for; matrix products, arithmetic and copies ran while one was open for 0% of the time, Pallas kernels for 9%

profile of v14, /device:TPU:0, one launch (start us, length us, event | category | flops | bytes accessed | tf_op | source)
XLA Modules:
  0.0 56.4 jit_solution(7455413869617826527)
XLA Ops:
  1.3 0.9 %copy-done = f32[8,4,16,128]{3,2,1,0:T(8,128)S(1)} copy-done((f32[8,4,16,128]{3,2,1,0:T(8,128)S(1)}, f32[8,4,16,128]{3,2,1,0:T(8,128)}, u32[]{:S(2)}) %copy-start) | copy-done | bytes 262168
  3.6 3.0 %collective-permute-start.2 = (f32[2,4,32,128]{3,2,1,0:T(8,128)S(1)}, f32[2,4,32,128]{3,2,1,0:T(8,128)S(1)}, u32[]{:S(2)}, u32[]{:S(2)}) collective-permute-start(f32[2,4,32,128]{3,2,1,0:T(8,128)S(1)} %get-tuple-element.28), channel_id=1, source_target_pairs={{0,2},{1,3},{2,0},{3,1},{4,6},{5,7},{6,4},{7,5},{8,10},{9,11},{10,... | collective-permute-start | bytes 393224 | tf_op jit(solution)/shard_map/ppermute | solution.py:510
  6.6 1.5 %collective-permute-start.3 = (f32[2,4,32,128]{3,2,1,0:T(8,128)S(1)}, f32[2,4,32,128]{3,2,1,0:T(8,128)S(1)}, u32[]{:S(2)}, u32[]{:S(2)}) collective-permute-start(f32[2,4,32,128]{3,2,1,0:T(8,128)S(1)} %get-tuple-element.29), channel_id=1, source_target_pairs={{0,4},{1,5},{2,6},{3,7},{4,0},{5,1},{6,2},{7,3},{8,12},{9,13},{10,... | collective-permute-start | bytes 393224 | tf_op jit(solution)/shard_map/ppermute | solution.py:510
  8.2 2.2 %collective-permute-done.2.refs_1_ = f32[2,4,32,128]{3,2,1,0:T(8,128)S(1)} collective-permute-done((f32[2,4,32,128]{3,2,1,0:T(8,128)S(1)}, f32[2,4,32,128]{3,2,1,0:T(8,128)S(1)}, u32[]{:S(2)}, u32[]{:S(2)}) %collective-permute-start.2) | collective-permute-done | bytes 131104 | tf_op jit(solution)/shard_map/ppermute | solution.py:510
  11.0 1.3 %collective-permute-start.5 = (f32[2,4,64,128]{3,2,1,0:T(8,128)S(1)}, f32[2,4,64,128]{3,2,1,0:T(8,128)S(1)}, u32[]{:S(2)}, u32[]{:S(2)}) collective-permute-start(f32[2,4,64,128]{3,2,1,0:T(8,128)S(1)} %half.1), channel_id=1, source_target_pairs={{4,12},{8,0},{12,20},{16,8},{20,28},{24,16},{5,13},{9,1},{13,21},{... | collective-permute-start | bytes 786440 | tf_op jit(solution)/shard_map/ppermute | solution.py:567
  13.0 1.4 %collective-permute-done.4.refs_3_ = f32[2,4,32,128]{3,2,1,0:T(8,128)S(1)} collective-permute-done((f32[2,4,32,128]{3,2,1,0:T(8,128)S(1)}, f32[2,4,32,128]{3,2,1,0:T(8,128)S(1)}, u32[]{:S(2)}, u32[]{:S(2)}) %collective-permute-start.4) | collective-permute-done | bytes 131104 | tf_op jit(solution)/shard_map/ppermute | solution.py:510
  15.1 3.6 %collective-permute-start.6 = (f32[2,2,64,128]{3,2,1,0:T(8,128)S(1)}, f32[2,2,64,128]{3,2,1,0:T(8,128)S(1)}, u32[]{:S(2)}, u32[]{:S(2)}) collective-permute-start(f32[2,2,64,128]{3,2,1,0:T(8,128)S(1)} %get-tuple-element.32), channel_id=1, source_target_pairs={{0,8},{8,16},{12,4},{16,24},{20,12},{28,20},{1,9},{9,17},{13,5},{1... | collective-permute-start | bytes 393224 | tf_op jit(solution)/shard_map/ppermute | solution.py:567
  18.7 3.5 %collective-permute-start.10 = (f32[2,2,64,128]{3,2,1,0:T(8,128)S(1)}, f32[2,2,64,128]{3,2,1,0:T(8,128)S(1)}, u32[]{:S(2)}, u32[]{:S(2)}) collective-permute-start(f32[2,2,64,128]{3,2,1,0:T(8,128)S(1)} %get-tuple-element.38), channel_id=1, source_target_pairs={{0,8},{8,16},{12,4},{16,24},{20,12},{28,20},{1,9},{9,17},{13,5},{1... | collective-permute-start | bytes 393224 | tf_op jit(solution)/shard_map/ppermute | solution.py:567
  22.4 1.3 %pre.1 = (f32[16,64,128]{2,1,0:T(8,128)S(1)}, f32[16,64,128]{2,1,0:T(8,128)S(1)}, f32[16,64,128]{2,1,0:T(8,128)S(1)}, f32[16,80,128]{2,1,0:T(8,128)S(1)}, f32[4,32,128]{2,1,0:T(8,128)S(1)}) custom-call(s32[2]{0:T(128)S(1)} %pad_add_fusion.place_ref, f32[8,128]{1,0:T(8,128)S(1)} %get-tuple-element.26.scalar_ref, ...), custom_call_target="tpu_custom_call" | custom-call | tf_op jit(solution)/shard_map/pre/pallas_call | solution.py:494
  23.7 4.6 %collective-permute-start.9 = (f32[4,32,128]{2,1,0:T(8,128)S(1)}, f32[4,32,128]{2,1,0:T(8,128)S(1)}, u32[]{:S(2)}, u32[]{:S(2)}) collective-permute-start(f32[4,32,128]{2,1,0:T(8,128)S(1)} %get-tuple-element.37.refs_2_), channel_id=1, source_target_pairs={{0,24},{4,28},{8,16},{12,20},{16,8},{20,12},{24,0},{28,4},{1,25},{... | collective-permute-start | bytes 196616 | tf_op jit(solution)/shard_map/ppermute | solution.py:519
  28.9 0.8 %beyond.1 = (f32[2,64,128]{2,1,0:T(8,128)S(1)}, f32[2,64,128]{2,1,0:T(8,128)S(1)}) custom-call(s32[2]{0:T(128)S(1)} %pad_add_fusion.place_ref, f32[8,128]{1,0:T(8,128)S(1)} %get-tuple-element.26.scalar_ref, f32[2,4,64,128]{3,2,1,0:T(8,128)S(1)} %collective-permute-done.5.refs_3_.half_ref, f32[2,2,64,128]{3,2,1,0:T(8,128)S(1)} %collective-permute-done.6.refs_4_.near_ref, ...), custom_call_target="tpu_custom_call" | custom-call | tf_op jit(solution)/shard_map/beyond/pallas_call | solution.py:494
  29.7 1.2 %collective-permute-done.9.refs_5_ = f32[4,32,128]{2,1,0:T(8,128)S(1)} collective-permute-done((f32[4,32,128]{2,1,0:T(8,128)S(1)}, f32[4,32,128]{2,1,0:T(8,128)S(1)}, u32[]{:S(2)}, u32[]{:S(2)}) %collective-permute-start.9) | collective-permute-done | bytes 65568 | tf_op jit(solution)/shard_map/ppermute | solution.py:519
  30.9 2.5 %collective-permute-done.8.refs_4_ = f32[4,32,128]{2,1,0:T(8,128)S(1)} collective-permute-done((f32[4,32,128]{2,1,0:T(8,128)S(1)}, f32[4,32,128]{2,1,0:T(8,128)S(1)}, u32[]{:S(2)}, u32[]{:S(2)}) %collective-permute-start.8) | collective-permute-done | bytes 65568 | tf_op jit(solution)/shard_map/ppermute | solution.py:519
  33.4 2.3 %coarse.1.refs_4_ = f32[256,128]{1,0:T(8,128)S(1)} custom-call(s32[2]{0:T(128)S(1)} %pad_add_fusion.place_ref, f32[8,128]{1,0:T(8,128)S(1)} %get-tuple-element.26.scalar_ref, bf16[128,128]{1,0:T(8,128)(2,1)S(1)} %get-tuple-element.50.refs_0_, bf16[128,128]{1,0:T(8,128)(2,1)S(1)} %get-tuple-element.49.refs_1_, f32[4,32,128]{2,1,0:T(8,128)S(1)} %get-tuple-element.37.refs_2_, ...), custom_call_target="tpu_custom_call" | custom-call | tf_op jit(solution)/shard_map/coarse/pallas_call | solution.py:494
  35.8 1.5 %post.1 = (f32[520,128]{1,0:T(8,128)S(1)}, f32[520,128]{1,0:T(8,128)S(1)}) custom-call(s32[2]{0:T(128)S(1)} %pad_add_fusion.place_ref, f32[8,128]{1,0:T(8,128)S(1)} %get-tuple-element.26.scalar_ref, f32[16,64,128]{2,1,0:T(8,128)S(1)} %get-tuple-element.33.refs_0_, f32[16,64,128]{2,1,0:T(8,128)S(1)} %get-tuple-element.34.refs_1_, ...), custom_call_target="tpu_custom_call" | custom-call | tf_op jit(solution)/shard_map/post/pallas_call | solution.py:494
  37.4 1.5 %collective-permute-done.11.got_ref = f32[520,128]{1,0:T(8,128)S(1)} collective-permute-done((f32[520,128]{1,0:T(8,128)S(1)}, f32[520,128]{1,0:T(8,128)S(1)}, u32[]{:S(2)}, u32[]{:S(2)}) %collective-permute-start.11) | collective-permute-done | bytes 266272 | tf_op jit(solution)/shard_map/ppermute | solution.py:614
  39.5 1.7 %collective-permute-start.12 = (f32[272,128]{1,0:T(8,128)S(1)}, f32[272,128]{1,0:T(8,128)S(1)}, u32[]{:S(2)}, u32[]{:S(2)}) collective-permute-start(f32[272,128]{1,0:T(8,128)S(1)} %get-tuple-element.44), channel_id=1, source_target_pairs={{0,2},{1,3},{2,0},{3,1},{4,6},{5,7},{6,4},{7,5},{8,10},{9,11},{10,... | collective-permute-start | bytes 417800 | tf_op jit(solution)/shard_map/ppermute | solution.py:510
  41.5 1.5 %collective-permute-start.14 = (f32[272,128]{1,0:T(8,128)S(1)}, f32[272,128]{1,0:T(8,128)S(1)}, u32[]{:S(2)}, u32[]{:S(2)}) collective-permute-start(f32[272,128]{1,0:T(8,128)S(1)} %get-tuple-element.46), channel_id=1, source_target_pairs={{0,6},{1,7},{2,4},{3,5},{4,2},{5,3},{6,0},{7,1},{8,14},{9,15},{10,... | collective-permute-start | bytes 417800 | tf_op jit(solution)/shard_map/ppermute | solution.py:510
  43.1 2.2 %collective-permute-done.12.refs_1_ = f32[272,128]{1,0:T(8,128)S(1)} collective-permute-done((f32[272,128]{1,0:T(8,128)S(1)}, f32[272,128]{1,0:T(8,128)S(1)}, u32[]{:S(2)}, u32[]{:S(2)}) %collective-permute-start.12) | collective-permute-done | bytes 139296 | tf_op jit(solution)/shard_map/ppermute | solution.py:510
  45.3 2.4 %collective-permute-done.13.refs_2_ = f32[272,128]{1,0:T(8,128)S(1)} collective-permute-done((f32[272,128]{1,0:T(8,128)S(1)}, f32[272,128]{1,0:T(8,128)S(1)}, u32[]{:S(2)}, u32[]{:S(2)}) %collective-permute-start.13) | collective-permute-done | bytes 139296 | tf_op jit(solution)/shard_map/ppermute | solution.py:510
  47.7 1.7 %collective-permute-done.14.refs_3_ = f32[272,128]{1,0:T(8,128)S(1)} collective-permute-done((f32[272,128]{1,0:T(8,128)S(1)}, f32[272,128]{1,0:T(8,128)S(1)}, u32[]{:S(2)}, u32[]{:S(2)}) %collective-permute-start.14) | collective-permute-done | bytes 139296 | tf_op jit(solution)/shard_map/ppermute | solution.py:510
  49.4 1.6 %collective-permute-start.17 = (f32[8,128]{1,0:T(8,128)S(1)}, f32[8,128]{1,0:T(8,128)S(1)}, u32[]{:S(2)}, u32[]{:S(2)}) collective-permute-start(f32[8,128]{1,0:T(8,128)S(1)} %squares.1), channel_id=1, source_target_pairs={{0,24},{4,28},{8,16},{12,20},{16,8},{20,12},{24,0},{28,4},{1,25},{... | collective-permute-start | bytes 12296 | tf_op jit(solution)/shard_map/ppermute | solution.py:519
  51.5 2.3 %collective-permute-start.15 = (f32[8,128]{1,0:T(8,128)S(1)}, f32[8,128]{1,0:T(8,128)S(1)}, u32[]{:S(2)}, u32[]{:S(2)}) collective-permute-start(f32[8,128]{1,0:T(8,128)S(1)} %squares.1), channel_id=1, source_target_pairs={{0,8},{4,12},{8,0},{12,4},{16,24},{20,28},{24,16},{28,20},{1,9},{5... | collective-permute-start | bytes 12296 | tf_op jit(solution)/shard_map/ppermute | solution.py:519
  53.8 1.4 %collect.1 = (f32[8,4,16,128]{3,2,1,0:T(8,128)}, f32[8,4,16,128]{3,2,1,0:T(8,128)}) custom-call(s32[2]{0:T(128)S(1)} %pad_add_fusion.place_ref, f32[272,128]{1,0:T(8,128)S(1)} %get-tuple-element.43.refs_0_, f32[272,128]{1,0:T(8,128)S(1)} %collective-permute-done.12.refs_1_, f32[272,128]{1,0:T(8,128)S(1)} %collective-permute-done.13.refs_2_, ...), custom_call_target="tpu_custom_call" | custom-call | tf_op jit(solution)/shard_map/collect/pallas_call | solution.py:494
  (41 shorter events, 7.5 us)
Async XLA Ops:
  0.6 2.2 %collective-permute-start = (f32[8,4,16,128]{3,2,1,0:T(8,128)}, f32[8,4,16,128]{3,2,1,0:T(8,128)S(1)}, u32[]{:S(2)}, u32[]{:S(2)}) collective-permute-start(f32[8,4,16,128]{3,2,1,0:T(8,128)} %source_ref.1), channel_id=1, source_target_pairs={{0,1},{1,0},{2,3},{3,2},{4,5},{5,4},{6,7},{7,6},{8,9},{9,8},{10,11... | collective-permute-start | bytes 786440 | tf_op jit(solution)/shard_map/ppermute | solution.py:537
  1.1 1.7 %collective-permute-start.1 = (f32[4,16,128]{2,1,0:T(8,128)}, f32[4,16,128]{2,1,0:T(8,128)S(1)}, u32[]{:S(2)}, u32[]{:S(2)}) collective-permute-start(f32[4,16,128]{2,1,0:T(8,128)} %refs_2_.1), channel_id=1, source_target_pairs={{0,1},{1,0},{2,3},{3,2},{4,5},{5,4},{6,7},{7,6},{8,9},{9,8},{10,11... | collective-permute-start | bytes 98312 | tf_op jit(solution)/shard_map/ppermute | solution.py:537
  1.3 0.9 %copy-start = (f32[8,4,16,128]{3,2,1,0:T(8,128)S(1)}, f32[8,4,16,128]{3,2,1,0:T(8,128)}, u32[]{:S(2)}) copy-start(f32[8,4,16,128]{3,2,1,0:T(8,128)} %source_ref.1) | copy-start | bytes 786436
  2.3 0.8 %copy-start.1 = (f32[4,16,128]{2,1,0:T(8,128)S(1)}, f32[4,16,128]{2,1,0:T(8,128)}, u32[]{:S(2)}) copy-start(f32[4,16,128]{2,1,0:T(8,128)} %refs_2_.1) | copy-start | bytes 98308
  2.3 0.8 %copy-start.2 = (f32[8]{0:T(128)S(1)}, f32[8]{0:T(128)}, u32[]{:S(2)}) copy-start(f32[8]{0:T(128)} %shifts_ref.1) | copy-start | bytes 100
  2.3 0.8 %copy-start.3 = (s32[8]{0:T(128)S(1)}, s32[8]{0:T(128)}, u32[]{:S(2)}) copy-start(s32[8]{0:T(128)} %index_ref.1) | copy-start | bytes 100
  2.3 0.8 %copy-start.4 = (f32[3]{0:T(128)S(1)}, f32[3]{0:T(128)}, u32[]{:S(2)}) copy-start(f32[3]{0:T(128)} %velocity_ref.1) | copy-start | bytes 40
  3.6 6.8 %collective-permute-start.2 = (f32[2,4,32,128]{3,2,1,0:T(8,128)S(1)}, f32[2,4,32,128]{3,2,1,0:T(8,128)S(1)}, u32[]{:S(2)}, u32[]{:S(2)}) collective-permute-start(f32[2,4,32,128]{3,2,1,0:T(8,128)S(1)} %get-tuple-element.28), channel_id=1, source_target_pairs={{0,2},{1,3},{2,0},{3,1},{4,6},{5,7},{6,4},{7,5},{8,10},{9,11},{10,... | collective-permute-start | bytes 393224 | tf_op jit(solution)/shard_map/ppermute | solution.py:510
  6.6 6.4 %collective-permute-start.3 = (f32[2,4,32,128]{3,2,1,0:T(8,128)S(1)}, f32[2,4,32,128]{3,2,1,0:T(8,128)S(1)}, u32[]{:S(2)}, u32[]{:S(2)}) collective-permute-start(f32[2,4,32,128]{3,2,1,0:T(8,128)S(1)} %get-tuple-element.29), channel_id=1, source_target_pairs={{0,4},{1,5},{2,6},{3,7},{4,0},{5,1},{6,2},{7,3},{8,12},{9,13},{10,... | collective-permute-start | bytes 393224 | tf_op jit(solution)/shard_map/ppermute | solution.py:510
  8.1 6.3 %collective-permute-start.4 = (f32[2,4,32,128]{3,2,1,0:T(8,128)S(1)}, f32[2,4,32,128]{3,2,1,0:T(8,128)S(1)}, u32[]{:S(2)}, u32[]{:S(2)}) collective-permute-start(f32[2,4,32,128]{3,2,1,0:T(8,128)S(1)} %get-tuple-element.30), channel_id=1, source_target_pairs={{0,6},{1,7},{2,4},{3,5},{4,2},{5,3},{6,0},{7,1},{8,14},{9,15},{10,... | collective-permute-start | bytes 393224 | tf_op jit(solution)/shard_map/ppermute | solution.py:510
  11.0 11.4 %collective-permute-start.5 = (f32[2,4,64,128]{3,2,1,0:T(8,128)S(1)}, f32[2,4,64,128]{3,2,1,0:T(8,128)S(1)}, u32[]{:S(2)}, u32[]{:S(2)}) collective-permute-start(f32[2,4,64,128]{3,2,1,0:T(8,128)S(1)} %half.1), channel_id=1, source_target_pairs={{4,12},{8,0},{12,20},{16,8},{20,28},{24,16},{5,13},{9,1},{13,21},{... | collective-permute-start | bytes 786440 | tf_op jit(solution)/shard_map/ppermute | solution.py:567
  15.1 7.3 %collective-permute-start.6 = (f32[2,2,64,128]{3,2,1,0:T(8,128)S(1)}, f32[2,2,64,128]{3,2,1,0:T(8,128)S(1)}, u32[]{:S(2)}, u32[]{:S(2)}) collective-permute-start(f32[2,2,64,128]{3,2,1,0:T(8,128)S(1)} %get-tuple-element.32), channel_id=1, source_target_pairs={{0,8},{8,16},{12,4},{16,24},{20,12},{28,20},{1,9},{9,17},{13,5},{1... | collective-permute-start | bytes 393224 | tf_op jit(solution)/shard_map/ppermute | solution.py:567
  18.7 10.2 %collective-permute-start.10 = (f32[2,2,64,128]{3,2,1,0:T(8,128)S(1)}, f32[2,2,64,128]{3,2,1,0:T(8,128)S(1)}, u32[]{:S(2)}, u32[]{:S(2)}) collective-permute-start(f32[2,2,64,128]{3,2,1,0:T(8,128)S(1)} %get-tuple-element.38), channel_id=1, source_target_pairs={{0,8},{8,16},{12,4},{16,24},{20,12},{28,20},{1,9},{9,17},{13,5},{1... | collective-permute-start | bytes 393224 | tf_op jit(solution)/shard_map/ppermute | solution.py:567
  23.7 7.3 %collective-permute-start.9 = (f32[4,32,128]{2,1,0:T(8,128)S(1)}, f32[4,32,128]{2,1,0:T(8,128)S(1)}, u32[]{:S(2)}, u32[]{:S(2)}) collective-permute-start(f32[4,32,128]{2,1,0:T(8,128)S(1)} %get-tuple-element.37.refs_2_), channel_id=1, source_target_pairs={{0,24},{4,28},{8,16},{12,20},{16,8},{20,12},{24,0},{28,4},{1,25},{... | collective-permute-start | bytes 196616 | tf_op jit(solution)/shard_map/ppermute | solution.py:519
  28.3 5.2 %collective-permute-start.8 = (f32[4,32,128]{2,1,0:T(8,128)S(1)}, f32[4,32,128]{2,1,0:T(8,128)S(1)}, u32[]{:S(2)}, u32[]{:S(2)}) collective-permute-start(f32[4,32,128]{2,1,0:T(8,128)S(1)} %get-tuple-element.37.refs_2_), channel_id=1, source_target_pairs={{0,16},{4,20},{8,24},{12,28},{16,0},{20,4},{24,8},{28,12},{1,17},{... | collective-permute-start | bytes 196616 | tf_op jit(solution)/shard_map/ppermute | solution.py:519
  28.3 5.2 %collective-permute-start.7 = (f32[4,32,128]{2,1,0:T(8,128)S(1)}, f32[4,32,128]{2,1,0:T(8,128)S(1)}, u32[]{:S(2)}, u32[]{:S(2)}) collective-permute-start(f32[4,32,128]{2,1,0:T(8,128)S(1)} %get-tuple-element.37.refs_2_), channel_id=1, source_target_pairs={{0,8},{4,12},{8,0},{12,4},{16,24},{20,28},{24,16},{28,20},{1,9},{5... | collective-permute-start | bytes 196616 | tf_op jit(solution)/shard_map/ppermute | solution.py:519
  37.3 1.6 %collective-permute-start.11 = (f32[520,128]{1,0:T(8,128)S(1)}, f32[520,128]{1,0:T(8,128)S(1)}, u32[]{:S(2)}, u32[]{:S(2)}) collective-permute-start(f32[520,128]{1,0:T(8,128)S(1)} %get-tuple-element.42), channel_id=1, source_target_pairs={{0,1},{1,0},{2,3},{3,2},{4,5},{5,4},{6,7},{7,6},{8,9},{9,8},{10,11... | collective-permute-start | bytes 798728 | tf_op jit(solution)/shard_map/ppermute | solution.py:614
  39.5 5.8 %collective-permute-start.12 = (f32[272,128]{1,0:T(8,128)S(1)}, f32[272,128]{1,0:T(8,128)S(1)}, u32[]{:S(2)}, u32[]{:S(2)}) collective-permute-start(f32[272,128]{1,0:T(8,128)S(1)} %get-tuple-element.44), channel_id=1, source_target_pairs={{0,2},{1,3},{2,0},{3,1},{4,6},{5,7},{6,4},{7,5},{8,10},{9,11},{10,... | collective-permute-start | bytes 417800 | tf_op jit(solution)/shard_map/ppermute | solution.py:510
  41.2 6.6 %collective-permute-start.13 = (f32[272,128]{1,0:T(8,128)S(1)}, f32[272,128]{1,0:T(8,128)S(1)}, u32[]{:S(2)}, u32[]{:S(2)}) collective-permute-start(f32[272,128]{1,0:T(8,128)S(1)} %get-tuple-element.45), channel_id=1, source_target_pairs={{0,4},{1,5},{2,6},{3,7},{4,0},{5,1},{6,2},{7,3},{8,12},{9,13},{10,... | collective-permute-start | bytes 417800 | tf_op jit(solution)/shard_map/ppermute | solution.py:510
  41.5 7.9 %collective-permute-start.14 = (f32[272,128]{1,0:T(8,128)S(1)}, f32[272,128]{1,0:T(8,128)S(1)}, u32[]{:S(2)}, u32[]{:S(2)}) collective-permute-start(f32[272,128]{1,0:T(8,128)S(1)} %get-tuple-element.46), channel_id=1, source_target_pairs={{0,6},{1,7},{2,4},{3,5},{4,2},{5,3},{6,0},{7,1},{8,14},{9,15},{10,... | collective-permute-start | bytes 417800 | tf_op jit(solution)/shard_map/ppermute | solution.py:510
  49.4 5.8 %collective-permute-start.17 = (f32[8,128]{1,0:T(8,128)S(1)}, f32[8,128]{1,0:T(8,128)S(1)}, u32[]{:S(2)}, u32[]{:S(2)}) collective-permute-start(f32[8,128]{1,0:T(8,128)S(1)} %squares.1), channel_id=1, source_target_pairs={{0,24},{4,28},{8,16},{12,20},{16,8},{20,12},{24,0},{28,4},{1,25},{... | collective-permute-start | bytes 12296 | tf_op jit(solution)/shard_map/ppermute | solution.py:519
  51.0 4.5 %collective-permute-start.16 = (f32[8,128]{1,0:T(8,128)S(1)}, f32[8,128]{1,0:T(8,128)S(1)}, u32[]{:S(2)}, u32[]{:S(2)}) collective-permute-start(f32[8,128]{1,0:T(8,128)S(1)} %squares.1), channel_id=1, source_target_pairs={{0,16},{4,20},{8,24},{12,28},{16,0},{20,4},{24,8},{28,12},{1,17},{... | collective-permute-start | bytes 12296 | tf_op jit(solution)/shard_map/ppermute | solution.py:519
  51.5 4.0 %collective-permute-start.15 = (f32[8,128]{1,0:T(8,128)S(1)}, f32[8,128]{1,0:T(8,128)S(1)}, u32[]{:S(2)}, u32[]{:S(2)}) collective-permute-start(f32[8,128]{1,0:T(8,128)S(1)} %squares.1), channel_id=1, source_target_pairs={{0,8},{4,12},{8,0},{12,4},{16,24},{20,28},{24,16},{28,20},{1,9},{5... | collective-permute-start | bytes 12296 | tf_op jit(solution)/shard_map/ppermute | solution.py:519

commit v15 on v13

--- a/solution.py
+++ b/solution.py
@@ -447,16 +447,20 @@
             out_ref[pl.ds(to, 8), :] = ref[pl.ds(2 * SLAB * half, 8), :]
 
 
-def collect_kernel(place_ref, *refs):
-    parts, (iterate_ref, residual_ref) = refs[:-2], refs[-2:]
-    _, bx, by, _ = iterate_ref.shape
+def collect_kernel(which, place_ref, *refs):
+    parts, out_ref = refs[:-1], refs[-1]
+    _, bx, by, _ = out_ref.shape
     area = bx * by
     for m, part in enumerate(parts):
         target = jnp.bitwise_xor(place_ref[0] // 2, m)
         for n in range(2):
-            for k, ref in enumerate((iterate_ref, residual_ref)):
-                rows = pl.ds((2 * n + k) * area, area)
-                ref[2 * target + n] = part[rows, :].reshape(bx, by, LANES)
+            rows = pl.ds((2 * n + which) * area, area)
+            out_ref[2 * target + n] = part[rows, :].reshape(bx, by, LANES)
+
+
+def collect_first_kernel(place_ref, squares_ref, *refs):
+    collect_kernel(0, place_ref, *refs[:-1])
+    refs[-1][...] = squares_ref[...]
 
 
 def squares_kernel(row, *refs):
@@ -593,10 +597,18 @@
     (squares,) = local_kernel(
         functools.partial(squares_kernel, 4 * area), "squares", (), parts, [(columns, nz)]
     )
-    iterate, residual = local_kernel(
-        collect_kernel, "collect", (place,), parts, [source.shape] * 2
-    )
-    total = sum(swap_slabs(squares, step, slabs))
+    total, stride = squares, 1
+    iterate, own = local_kernel(
+        collect_first_kernel, "collect", (place,), (squares, *parts), [source.shape, squares.shape]
+    )
+    while stride < slabs:
+        pairs = [(i, i ^ (stride * step)) for i in range(gx_size)]
+        got = lax.ppermute(total, "gx", pairs)
+        total = (own if stride == 1 else total) + got
+        stride *= 2
+    (residual,) = local_kernel(
+        functools.partial(collect_kernel, 1), "collect", (place,), parts, [source.shape]
+    )
     rms = jnp.sqrt(total[:, 0] / (nx * ny * nz) + EPSILON)
     slots = jnp.arange(columns, dtype=jnp.int32)
     mine = jnp.bitwise_xor(slots, column // 2 * 2)[:, None] == slots[None, :]

time: 56.7 us -> 58.2 us (1.026)
  Pallas kernels: 9.45 us -> 10.6 us
    ppermute x6 -> x3, starting transfers between devices: 9.57 us -> 5.18 us  [swap_slabs(): moved.append(lax.ppermute(piece, 'gx', pairs))]
    ppermute x0 -> x2, starting transfers between devices: none -> 4.32 us  [column_body(): got = lax.ppermute(total, 'gx', pairs)]
    ppermute x0 -> x2, waiting for transfers between devices: none -> 1.24 us  [column_body(): got = lax.ppermute(total, 'gx', pairs)]
    pallas_call x10 -> x11, Pallas kernels: 9.45 us -> 10.6 us  [local_kernel(): pl.pallas_call(kernel, out_shape=[jax.ShapeDtypeStruct(shape, jnp.float32...]
    ppermute x6 -> x3, waiting for transfers between devices: 4.05 us -> 3.23 us  [swap_slabs(): moved.append(lax.ppermute(piece, 'gx', pairs))]
  transfers between devices with their start and end apart: 19 -> 18, of which waited for: 10 -> 11; matrix products, arithmetic and copies ran while one was open for 0% -> 0% of each run, Pallas kernels for 10% -> 11%
where the time goes in v15:
time: 58.2 us; the launch traced here: 58 us
  starting transfers between devices  25.2 us (43%)
  waiting for transfers between devices  19.1 us (33%)
  Pallas kernels  10.6 us (18%)
  local copies, waits for them, and re-layouts  1.12 us (2%)
  other arithmetic  1.04 us (2%)
  between operations  0.81 us (1%)
    ppermute x6, waiting for transfers between devices, swap_in_plane(): moved.append(lax.ppermute(pieces[k], ('gx', 'gy'), pairs))  10.8 us
    pallas_call x11, Pallas kernels, local_kernel(): pl.pallas_call(kernel, out_shape=[jax.ShapeDtypeStruct(shape, jnp.float32...  10.6 us
    ppermute x6, starting transfers between devices, swap_in_plane(): moved.append(lax.ppermute(pieces[k], ('gx', 'gy'), pairs))  8.1 us
    ppermute x3, starting transfers between devices, swap_slabs(): moved.append(lax.ppermute(piece, 'gx', pairs))  5.18 us
    ppermute x2, starting transfers between devices, column_body(): beside.append(lax.ppermute(piece, 'gx', pairs))  4.93 us
    ppermute x2, starting transfers between devices, column_body(): got = lax.ppermute(total, 'gx', pairs)  4.32 us
    ppermute x3, waiting for transfers between devices, swap_slabs(): moved.append(lax.ppermute(piece, 'gx', pairs))  3.23 us
    ppermute x2, waiting for transfers between devices, column_body(): beside.append(lax.ppermute(piece, 'gx', pairs))  2.36 us
  transfers between devices with their start and end apart: 18, of which 11 were waited for; matrix products, arithmetic and copies ran while one was open for 0% of the time, Pallas kernels for 11%

profile of v15, /device:TPU:0, one launch (start us, length us, event | category | flops | bytes accessed | tf_op | source)
XLA Modules:
  0.0 58.0 jit_solution(7445102239148553910)
XLA Ops:
  1.3 0.9 %copy-done = f32[8,4,16,128]{3,2,1,0:T(8,128)S(1)} copy-done((f32[8,4,16,128]{3,2,1,0:T(8,128)S(1)}, f32[8,4,16,128]{3,2,1,0:T(8,128)}, u32[]{:S(2)}) %copy-start) | copy-done | bytes 262168
  3.6 3.0 %collective-permute-start.2 = (f32[2,4,32,128]{3,2,1,0:T(8,128)S(1)}, f32[2,4,32,128]{3,2,1,0:T(8,128)S(1)}, u32[]{:S(2)}, u32[]{:S(2)}) collective-permute-start(f32[2,4,32,128]{3,2,1,0:T(8,128)S(1)} %get-tuple-element.27), channel_id=1, source_target_pairs={{0,2},{1,3},{2,0},{3,1},{4,6},{5,7},{6,4},{7,5},{8,10},{9,11},{10,... | collective-permute-start | bytes 393224 | tf_op jit(solution)/shard_map/ppermute | solution.py:493
  6.6 1.5 %collective-permute-start.3 = (f32[2,4,32,128]{3,2,1,0:T(8,128)S(1)}, f32[2,4,32,128]{3,2,1,0:T(8,128)S(1)}, u32[]{:S(2)}, u32[]{:S(2)}) collective-permute-start(f32[2,4,32,128]{3,2,1,0:T(8,128)S(1)} %get-tuple-element.28), channel_id=1, source_target_pairs={{0,4},{1,5},{2,6},{3,7},{4,0},{5,1},{6,2},{7,3},{8,12},{9,13},{10,... | collective-permute-start | bytes 393224 | tf_op jit(solution)/shard_map/ppermute | solution.py:493
  8.2 2.2 %collective-permute-done.2.refs_1_ = f32[2,4,32,128]{3,2,1,0:T(8,128)S(1)} collective-permute-done((f32[2,4,32,128]{3,2,1,0:T(8,128)S(1)}, f32[2,4,32,128]{3,2,1,0:T(8,128)S(1)}, u32[]{:S(2)}, u32[]{:S(2)}) %collective-permute-start.2) | collective-permute-done | bytes 131104 | tf_op jit(solution)/shard_map/ppermute | solution.py:493
  11.0 1.3 %collective-permute-start.5 = (f32[2,2,64,128]{3,2,1,0:T(8,128)S(1)}, f32[2,2,64,128]{3,2,1,0:T(8,128)S(1)}, u32[]{:S(2)}, u32[]{:S(2)}) collective-permute-start(f32[2,2,64,128]{3,2,1,0:T(8,128)S(1)} %edge.1), channel_id=1, source_target_pairs={{4,12},{8,0},{12,20},{16,8},{20,28},{24,16},{5,13},{9,1},{13,21},{... | collective-permute-start | bytes 393224 | tf_op jit(solution)/shard_map/ppermute | solution.py:547
  13.0 1.4 %collective-permute-done.4.refs_3_ = f32[2,4,32,128]{3,2,1,0:T(8,128)S(1)} collective-permute-done((f32[2,4,32,128]{3,2,1,0:T(8,128)S(1)}, f32[2,4,32,128]{3,2,1,0:T(8,128)S(1)}, u32[]{:S(2)}, u32[]{:S(2)}) %collective-permute-start.4) | collective-permute-done | bytes 131104 | tf_op jit(solution)/shard_map/ppermute | solution.py:493
  15.1 3.6 %collective-permute-start.6 = (f32[2,2,64,128]{3,2,1,0:T(8,128)S(1)}, f32[2,2,64,128]{3,2,1,0:T(8,128)S(1)}, u32[]{:S(2)}, u32[]{:S(2)}) collective-permute-start(f32[2,2,64,128]{3,2,1,0:T(8,128)S(1)} %get-tuple-element.31), channel_id=1, source_target_pairs={{0,8},{8,16},{12,4},{16,24},{20,12},{28,20},{1,9},{9,17},{13,5},{1... | collective-permute-start | bytes 393224 | tf_op jit(solution)/shard_map/ppermute | solution.py:547
  18.8 2.4 %collective-permute-done.6.refs_4_ = f32[2,2,64,128]{3,2,1,0:T(8,128)S(1)} collective-permute-done((f32[2,2,64,128]{3,2,1,0:T(8,128)S(1)}, f32[2,2,64,128]{3,2,1,0:T(8,128)S(1)}, u32[]{:S(2)}, u32[]{:S(2)}) %collective-permute-start.6) | collective-permute-done | bytes 131104 | tf_op jit(solution)/shard_map/ppermute | solution.py:547
  21.2 1.3 %pre.1 = (f32[16,64,128]{2,1,0:T(8,128)S(1)}, f32[16,64,128]{2,1,0:T(8,128)S(1)}, f32[16,64,128]{2,1,0:T(8,128)S(1)}, f32[16,80,128]{2,1,0:T(8,128)S(1)}, f32[4,...) custom-call(s32[2]{0:T(128)S(1)} %pad_add_fusion.place_ref, ...), custom_call_target="tpu_custom_call" | custom-call | tf_op jit(solution)/shard_map/pre/pallas_call | solution.py:477
  22.5 4.5 %collective-permute-start.9 = (f32[4,32,128]{2,1,0:T(8,128)S(1)}, f32[4,32,128]{2,1,0:T(8,128)S(1)}, u32[]{:S(2)}, u32[]{:S(2)}) collective-permute-start(f32[4,32,128]{2,1,0:T(8,128)S(1)} %get-tuple-element.36.refs_2_), channel_id=1, source_target_pairs={{0,24},{4,28},{8,16},{12,20},{16,8},{20,12},{24,0},{28,4},{1,25},{... | collective-permute-start | bytes 196616 | tf_op jit(solution)/shard_map/ppermute | solution.py:502
  27.7 1.4 %collective-permute-start.10 = (f32[2,64,128]{2,1,0:T(8,128)S(1)}, f32[2,64,128]{2,1,0:T(8,128)S(1)}, u32[]{:S(2)}, u32[]{:S(2)}) collective-permute-start(f32[2,64,128]{2,1,0:T(8,128)S(1)} %get-tuple-element.37), channel_id=1, source_target_pairs={{0,8},{4,12},{8,0},{12,4},{16,24},{20,28},{24,16},{28,20},{1,9},{5... | collective-permute-start | bytes 196616 | tf_op jit(solution)/shard_map/ppermute | solution.py:554
  29.7 3.2 %collective-permute-done.8.refs_4_ = f32[4,32,128]{2,1,0:T(8,128)S(1)} collective-permute-done((f32[4,32,128]{2,1,0:T(8,128)S(1)}, f32[4,32,128]{2,1,0:T(8,128)S(1)}, u32[]{:S(2)}, u32[]{:S(2)}) %collective-permute-start.8) | collective-permute-done | bytes 65568 | tf_op jit(solution)/shard_map/ppermute | solution.py:502
  33.0 2.3 %coarse.1.refs_4_ = f32[256,128]{1,0:T(8,128)S(1)} custom-call(s32[2]{0:T(128)S(1)} %pad_add_fusion.place_ref, f32[8,128]{1,0:T(8,128)S(1)} %get-tuple-element.25.scalar_ref, bf16[128,128]{1,0:T(8,128)(2,1)S(1)} %get-tuple-element.48.refs_0_, bf16[128,128]{1,0:T(8,128)(2,1)S(1)} %get-tuple-element.47.refs_1_, f32[4,32,128]{2,1,0:T(8,128)S(1)} %get-tuple-element.36.refs_2_, ...), custom_call_target="tpu_custom_call" | custom-call | tf_op jit(solution)/shard_map/coarse/pallas_call | solution.py:477
  35.3 1.5 %post.1 = (f32[520,128]{1,0:T(8,128)S(1)}, f32[520,128]{1,0:T(8,128)S(1)}) custom-call(s32[2]{0:T(128)S(1)} %pad_add_fusion.place_ref, f32[8,128]{1,0:T(8,128)S(1)} %get-tuple-element.25.scalar_ref, f32[16,64,128]{2,1,0:T(8,128)S(1)} %get-tuple-element.32.refs_0_, f32[16,64,128]{2,1,0:T(8,128)S(1)} %get-tuple-element.33.refs_1_, ...), custom_call_target="tpu_custom_call" | custom-call | tf_op jit(solution)/shard_map/post/pallas_call | solution.py:477
  36.9 1.5 %collective-permute-done.12.got_ref = f32[520,128]{1,0:T(8,128)S(1)} collective-permute-done((f32[520,128]{1,0:T(8,128)S(1)}, f32[520,128]{1,0:T(8,128)S(1)}, u32[]{:S(2)}, u32[]{:S(2)}) %collective-permute-start.12) | collective-permute-done | bytes 266272 | tf_op jit(solution)/shard_map/ppermute | solution.py:593
  39.1 1.4 %collective-permute-start.13 = (f32[272,128]{1,0:T(8,128)S(1)}, f32[272,128]{1,0:T(8,128)S(1)}, u32[]{:S(2)}, u32[]{:S(2)}) collective-permute-start(f32[272,128]{1,0:T(8,128)S(1)} %get-tuple-element.42), channel_id=1, source_target_pairs={{0,2},{1,3},{2,0},{3,1},{4,6},{5,7},{6,4},{7,5},{8,10},{9,11},{10,... | collective-permute-start | bytes 417800 | tf_op jit(solution)/shard_map/ppermute | solution.py:493
  40.7 2.0 %collective-permute-start.15 = (f32[272,128]{1,0:T(8,128)S(1)}, f32[272,128]{1,0:T(8,128)S(1)}, u32[]{:S(2)}, u32[]{:S(2)}) collective-permute-start(f32[272,128]{1,0:T(8,128)S(1)} %get-tuple-element.44), channel_id=1, source_target_pairs={{0,6},{1,7},{2,4},{3,5},{4,2},{5,3},{6,0},{7,1},{8,14},{9,15},{10,... | collective-permute-start | bytes 417800 | tf_op jit(solution)/shard_map/ppermute | solution.py:493
  42.6 2.2 %collective-permute-done.13.refs_1_ = f32[272,128]{1,0:T(8,128)S(1)} collective-permute-done((f32[272,128]{1,0:T(8,128)S(1)}, f32[272,128]{1,0:T(8,128)S(1)}, u32[]{:S(2)}, u32[]{:S(2)}) %collective-permute-start.13) | collective-permute-done | bytes 139296 | tf_op jit(solution)/shard_map/ppermute | solution.py:493
  44.8 2.2 %collective-permute-done.14.refs_2_ = f32[272,128]{1,0:T(8,128)S(1)} collective-permute-done((f32[272,128]{1,0:T(8,128)S(1)}, f32[272,128]{1,0:T(8,128)S(1)}, u32[]{:S(2)}, u32[]{:S(2)}) %collective-permute-start.14) | collective-permute-done | bytes 139296 | tf_op jit(solution)/shard_map/ppermute | solution.py:493
  47.0 2.0 %collective-permute-done.15.refs_3_ = f32[272,128]{1,0:T(8,128)S(1)} collective-permute-done((f32[272,128]{1,0:T(8,128)S(1)}, f32[272,128]{1,0:T(8,128)S(1)}, u32[]{:S(2)}, u32[]{:S(2)}) %collective-permute-start.15) | collective-permute-done | bytes 139296 | tf_op jit(solution)/shard_map/ppermute | solution.py:493
  49.0 1.5 %collective-permute-start.16 = (f32[8,128]{1,0:T(8,128)S(1)}, f32[8,128]{1,0:T(8,128)S(1)}, u32[]{:S(2)}, u32[]{:S(2)}) collective-permute-start(f32[8,128]{1,0:T(8,128)S(1)} %squares.1.squares_ref), channel_id=1, source_target_pairs={{0,8},{4,12},{8,0},{12,4},{16,24},{20,28},{24,16},{28,20},{1,9},{5... | collective-permute-start | bytes 12296 | tf_op jit(solution)/shard_map/ppermute | solution.py:606
  50.5 1.3 %collect.2 = (f32[8,4,16,128]{3,2,1,0:T(8,128)}, f32[8,128]{1,0:T(8,128)S(1)}) custom-call(s32[2]{0:T(128)S(1)} %pad_add_fusion.place_ref, f32[8,128]{1,0:T(8,128)S(1)} %squares.1.squares_ref, f32[272,128]{1,0:T(8,128)S(1)} %get-tuple-element.41.refs_0_, f32[272,128]{1,0:T(8,128)S(1)} %collective-permute-done.13.refs_1_, ...), custom_call_target="tpu_custom_call" | custom-call | tf_op jit(solution)/shard_map/collect/pallas_call | solution.py:477
  52.6 2.8 %collective-permute-start.17 = (f32[8,128]{1,0:T(8,128)S(1)}, f32[8,128]{1,0:T(8,128)S(1)}, u32[]{:S(2)}, u32[]{:S(2)}) collective-permute-start(f32[8,128]{1,0:T(8,128)S(1)} %add.32), channel_id=1, source_target_pairs={{0,16},{4,20},{8,24},{12,28},{16,0},{20,4},{24,8},{28,12},{1,17},{... | collective-permute-start | bytes 12296 | tf_op jit(solution)/shard_map/ppermute | solution.py:606
  55.4 1.3 %collect.3 = f32[8,4,16,128]{3,2,1,0:T(8,128)} custom-call(s32[2]{0:T(128)S(1)} %pad_add_fusion.place_ref, f32[272,128]{1,0:T(8,128)S(1)} %get-tuple-element.41.refs_0_, f32[272,128]{1,0:T(8,128)S(1)} %collective-permute-done.13.refs_1_, f32[272,128]{1,0:T(8,128)S(1)} %collective-permute-done.14.refs_2_, f32[272,128]{1,0:T(8,128)S(1)} %collective-permute-done.15.refs_3_), custom_call_target="tpu_custom_call" | custom-call | tf_op jit(solution)/shard_map/collect/pallas_call | solution.py:477
  (42 shorter events, 8.4 us)
Async XLA Ops:
  0.6 2.2 %collective-permute-start = (f32[8,4,16,128]{3,2,1,0:T(8,128)}, f32[8,4,16,128]{3,2,1,0:T(8,128)S(1)}, u32[]{:S(2)}, u32[]{:S(2)}) collective-permute-start(f32[8,4,16,128]{3,2,1,0:T(8,128)} %source_ref.1), channel_id=1, source_target_pairs={{0,1},{1,0},{2,3},{3,2},{4,5},{5,4},{6,7},{7,6},{8,9},{9,8},{10,11... | collective-permute-start | bytes 786440 | tf_op jit(solution)/shard_map/ppermute | solution.py:520
  1.1 1.7 %collective-permute-start.1 = (f32[4,16,128]{2,1,0:T(8,128)}, f32[4,16,128]{2,1,0:T(8,128)S(1)}, u32[]{:S(2)}, u32[]{:S(2)}) collective-permute-start(f32[4,16,128]{2,1,0:T(8,128)} %refs_2_.1), channel_id=1, source_target_pairs={{0,1},{1,0},{2,3},{3,2},{4,5},{5,4},{6,7},{7,6},{8,9},{9,8},{10,11... | collective-permute-start | bytes 98312 | tf_op jit(solution)/shard_map/ppermute | solution.py:520
  1.3 0.9 %copy-start = (f32[8,4,16,128]{3,2,1,0:T(8,128)S(1)}, f32[8,4,16,128]{3,2,1,0:T(8,128)}, u32[]{:S(2)}) copy-start(f32[8,4,16,128]{3,2,1,0:T(8,128)} %source_ref.1) | copy-start | bytes 786436
  2.3 0.8 %copy-start.1 = (f32[4,16,128]{2,1,0:T(8,128)S(1)}, f32[4,16,128]{2,1,0:T(8,128)}, u32[]{:S(2)}) copy-start(f32[4,16,128]{2,1,0:T(8,128)} %refs_2_.1) | copy-start | bytes 98308
  2.3 0.8 %copy-start.2 = (f32[8]{0:T(128)S(1)}, f32[8]{0:T(128)}, u32[]{:S(2)}) copy-start(f32[8]{0:T(128)} %shifts_ref.1) | copy-start | bytes 100
  2.3 0.8 %copy-start.3 = (s32[8]{0:T(128)S(1)}, s32[8]{0:T(128)}, u32[]{:S(2)}) copy-start(s32[8]{0:T(128)} %index_ref.1) | copy-start | bytes 100
  2.3 0.8 %copy-start.4 = (f32[3]{0:T(128)S(1)}, f32[3]{0:T(128)}, u32[]{:S(2)}) copy-start(f32[3]{0:T(128)} %velocity_ref.1) | copy-start | bytes 40
  3.6 6.8 %collective-permute-start.2 = (f32[2,4,32,128]{3,2,1,0:T(8,128)S(1)}, f32[2,4,32,128]{3,2,1,0:T(8,128)S(1)}, u32[]{:S(2)}, u32[]{:S(2)}) collective-permute-start(f32[2,4,32,128]{3,2,1,0:T(8,128)S(1)} %get-tuple-element.27), channel_id=1, source_target_pairs={{0,2},{1,3},{2,0},{3,1},{4,6},{5,7},{6,4},{7,5},{8,10},{9,11},{10,... | collective-permute-start | bytes 393224 | tf_op jit(solution)/shard_map/ppermute | solution.py:493
  6.6 6.4 %collective-permute-start.3 = (f32[2,4,32,128]{3,2,1,0:T(8,128)S(1)}, f32[2,4,32,128]{3,2,1,0:T(8,128)S(1)}, u32[]{:S(2)}, u32[]{:S(2)}) collective-permute-start(f32[2,4,32,128]{3,2,1,0:T(8,128)S(1)} %get-tuple-element.28), channel_id=1, source_target_pairs={{0,4},{1,5},{2,6},{3,7},{4,0},{5,1},{6,2},{7,3},{8,12},{9,13},{10,... | collective-permute-start | bytes 393224 | tf_op jit(solution)/shard_map/ppermute | solution.py:493
  8.1 6.3 %collective-permute-start.4 = (f32[2,4,32,128]{3,2,1,0:T(8,128)S(1)}, f32[2,4,32,128]{3,2,1,0:T(8,128)S(1)}, u32[]{:S(2)}, u32[]{:S(2)}) collective-permute-start(f32[2,4,32,128]{3,2,1,0:T(8,128)S(1)} %get-tuple-element.29), channel_id=1, source_target_pairs={{0,6},{1,7},{2,4},{3,5},{4,2},{5,3},{6,0},{7,1},{8,14},{9,15},{10,... | collective-permute-start | bytes 393224 | tf_op jit(solution)/shard_map/ppermute | solution.py:493
  11.0 7.9 %collective-permute-start.5 = (f32[2,2,64,128]{3,2,1,0:T(8,128)S(1)}, f32[2,2,64,128]{3,2,1,0:T(8,128)S(1)}, u32[]{:S(2)}, u32[]{:S(2)}) collective-permute-start(f32[2,2,64,128]{3,2,1,0:T(8,128)S(1)} %edge.1), channel_id=1, source_target_pairs={{4,12},{8,0},{12,20},{16,8},{20,28},{24,16},{5,13},{9,1},{13,21},{... | collective-permute-start | bytes 393224 | tf_op jit(solution)/shard_map/ppermute | solution.py:547
  15.1 6.1 %collective-permute-start.6 = (f32[2,2,64,128]{3,2,1,0:T(8,128)S(1)}, f32[2,2,64,128]{3,2,1,0:T(8,128)S(1)}, u32[]{:S(2)}, u32[]{:S(2)}) collective-permute-start(f32[2,2,64,128]{3,2,1,0:T(8,128)S(1)} %get-tuple-element.31), channel_id=1, source_target_pairs={{0,8},{8,16},{12,4},{16,24},{20,12},{28,20},{1,9},{9,17},{13,5},{1... | collective-permute-start | bytes 393224 | tf_op jit(solution)/shard_map/ppermute | solution.py:547
  22.5 7.2 %collective-permute-start.9 = (f32[4,32,128]{2,1,0:T(8,128)S(1)}, f32[4,32,128]{2,1,0:T(8,128)S(1)}, u32[]{:S(2)}, u32[]{:S(2)}) collective-permute-start(f32[4,32,128]{2,1,0:T(8,128)S(1)} %get-tuple-element.36.refs_2_), channel_id=1, source_target_pairs={{0,24},{4,28},{8,16},{12,20},{16,8},{20,12},{24,0},{28,4},{1,25},{... | collective-permute-start | bytes 196616 | tf_op jit(solution)/shard_map/ppermute | solution.py:502
  27.0 5.9 %collective-permute-start.8 = (f32[4,32,128]{2,1,0:T(8,128)S(1)}, f32[4,32,128]{2,1,0:T(8,128)S(1)}, u32[]{:S(2)}, u32[]{:S(2)}) collective-permute-start(f32[4,32,128]{2,1,0:T(8,128)S(1)} %get-tuple-element.36.refs_2_), channel_id=1, source_target_pairs={{0,16},{4,20},{8,24},{12,28},{16,0},{20,4},{24,8},{28,12},{1,17},{... | collective-permute-start | bytes 196616 | tf_op jit(solution)/shard_map/ppermute | solution.py:502
  27.1 5.9 %collective-permute-start.7 = (f32[4,32,128]{2,1,0:T(8,128)S(1)}, f32[4,32,128]{2,1,0:T(8,128)S(1)}, u32[]{:S(2)}, u32[]{:S(2)}) collective-permute-start(f32[4,32,128]{2,1,0:T(8,128)S(1)} %get-tuple-element.36.refs_2_), channel_id=1, source_target_pairs={{0,8},{4,12},{8,0},{12,4},{16,24},{20,28},{24,16},{28,20},{1,9},{5... | collective-permute-start | bytes 196616 | tf_op jit(solution)/shard_map/ppermute | solution.py:502
  27.7 7.6 %collective-permute-start.10 = (f32[2,64,128]{2,1,0:T(8,128)S(1)}, f32[2,64,128]{2,1,0:T(8,128)S(1)}, u32[]{:S(2)}, u32[]{:S(2)}) collective-permute-start(f32[2,64,128]{2,1,0:T(8,128)S(1)} %get-tuple-element.37), channel_id=1, source_target_pairs={{0,8},{4,12},{8,0},{12,4},{16,24},{20,28},{24,16},{28,20},{1,9},{5... | collective-permute-start | bytes 196616 | tf_op jit(solution)/shard_map/ppermute | solution.py:554
  29.1 6.3 %collective-permute-start.11 = (f32[2,64,128]{2,1,0:T(8,128)S(1)}, f32[2,64,128]{2,1,0:T(8,128)S(1)}, u32[]{:S(2)}, u32[]{:S(2)}) collective-permute-start(f32[2,64,128]{2,1,0:T(8,128)S(1)} %get-tuple-element.38), channel_id=1, source_target_pairs={{8,16},{12,20},{16,8},{20,12},{9,17},{13,21},{17,9},{21,13},{10,18... | collective-permute-start | bytes 196616 | tf_op jit(solution)/shard_map/ppermute | solution.py:554
  36.9 1.6 %collective-permute-start.12 = (f32[520,128]{1,0:T(8,128)S(1)}, f32[520,128]{1,0:T(8,128)S(1)}, u32[]{:S(2)}, u32[]{:S(2)}) collective-permute-start(f32[520,128]{1,0:T(8,128)S(1)} %get-tuple-element.40), channel_id=1, source_target_pairs={{0,1},{1,0},{2,3},{3,2},{4,5},{5,4},{6,7},{7,6},{8,9},{9,8},{10,11... | collective-permute-start | bytes 798728 | tf_op jit(solution)/shard_map/ppermute | solution.py:593
  39.1 5.8 %collective-permute-start.13 = (f32[272,128]{1,0:T(8,128)S(1)}, f32[272,128]{1,0:T(8,128)S(1)}, u32[]{:S(2)}, u32[]{:S(2)}) collective-permute-start(f32[272,128]{1,0:T(8,128)S(1)} %get-tuple-element.42), channel_id=1, source_target_pairs={{0,2},{1,3},{2,0},{3,1},{4,6},{5,7},{6,4},{7,5},{8,10},{9,11},{10,... | collective-permute-start | bytes 417800 | tf_op jit(solution)/shard_map/ppermute | solution.py:493
  40.5 6.6 %collective-permute-start.14 = (f32[272,128]{1,0:T(8,128)S(1)}, f32[272,128]{1,0:T(8,128)S(1)}, u32[]{:S(2)}, u32[]{:S(2)}) collective-permute-start(f32[272,128]{1,0:T(8,128)S(1)} %get-tuple-element.43), channel_id=1, source_target_pairs={{0,4},{1,5},{2,6},{3,7},{4,0},{5,1},{6,2},{7,3},{8,12},{9,13},{10,... | collective-permute-start | bytes 417800 | tf_op jit(solution)/shard_map/ppermute | solution.py:493
  40.7 8.4 %collective-permute-start.15 = (f32[272,128]{1,0:T(8,128)S(1)}, f32[272,128]{1,0:T(8,128)S(1)}, u32[]{:S(2)}, u32[]{:S(2)}) collective-permute-start(f32[272,128]{1,0:T(8,128)S(1)} %get-tuple-element.44), channel_id=1, source_target_pairs={{0,6},{1,7},{2,4},{3,5},{4,2},{5,3},{6,0},{7,1},{8,14},{9,15},{10,... | collective-permute-start | bytes 417800 | tf_op jit(solution)/shard_map/ppermute | solution.py:493
  49.0 3.6 %collective-permute-start.16 = (f32[8,128]{1,0:T(8,128)S(1)}, f32[8,128]{1,0:T(8,128)S(1)}, u32[]{:S(2)}, u32[]{:S(2)}) collective-permute-start(f32[8,128]{1,0:T(8,128)S(1)} %squares.1.squares_ref), channel_id=1, source_target_pairs={{0,8},{4,12},{8,0},{12,4},{16,24},{20,28},{24,16},{28,20},{1,9},{5... | collective-permute-start | bytes 12296 | tf_op jit(solution)/shard_map/ppermute | solution.py:606
  52.6 4.5 %collective-permute-start.17 = (f32[8,128]{1,0:T(8,128)S(1)}, f32[8,128]{1,0:T(8,128)S(1)}, u32[]{:S(2)}, u32[]{:S(2)}) collective-permute-start(f32[8,128]{1,0:T(8,128)S(1)} %add.32), channel_id=1, source_target_pairs={{0,16},{4,20},{8,24},{12,28},{16,0},{20,4},{24,8},{28,12},{1,17},{... | collective-permute-start | bytes 12296 | tf_op jit(solution)/shard_map/ppermute | solution.py:606

commit v16 on v14

--- a/solution.py
+++ b/solution.py
@@ -135,9 +135,26 @@
             put(x, value)
 
 
-class Level:
+class Grid:
+    def __init__(self, ny):
+        self.ny = ny
+
+    def pool_rows(self, value, rows):
+        half, ny = self.ny // 2, self.ny
+        rows[pl.ds(0, ny), :] = value
+        return rows[pl.ds(0, half, stride=2), :] + rows[pl.ds(1, half, stride=2), :]
+
+    def spread_rows(self, part, rows):
+        half, ny = self.ny // 2, self.ny
+        rows[pl.ds(0, half, stride=2), :] = part
+        rows[pl.ds(1, half, stride=2), :] = part
+        return rows[pl.ds(0, ny), :]
+
+
+class Level(Grid):
     def __init__(self, index, ny, nz, rim, scalar_ref, f, r, w):
-        self.ny, self.nz, self.rim = ny, nz, rim
+        super().__init__(ny)
+        self.nz, self.rim = nz, rim
         self.f, self.r, self.w = f, r, w
         spacing = 2.0**index
         scale_a = 1.0 / (spacing * spacing)
@@ -183,17 +200,6 @@
         middle = self.plane(v, x)
         pulled = self.f[x] + self.neighbours(v, x, middle)
         return pulled - (self.r[x] + self.centre) * middle
-
-    def pool_rows(self, value, rows):
-        half, ny = self.ny // 2, self.ny
-        rows[pl.ds(0, ny), :] = value
-        return rows[pl.ds(0, half, stride=2), :] + rows[pl.ds(1, half, stride=2), :]
-
-    def spread_rows(self, part, rows):
-        half, ny = self.ny // 2, self.ny
-        rows[pl.ds(0, half, stride=2), :] = part
-        rows[pl.ds(1, half, stride=2), :] = part
-        return rows[pl.ds(0, ny), :]
 
     def solve_in_registers(self, rhs, reaction):
         row = lax.broadcasted_iota(jnp.int32, (self.ny, 1), 0)
@@ -266,7 +272,7 @@
 
 
 def arrange_kernel(chips_y, place_ref, *refs):
-    blocks, (slab_ref, near_ref, far_ref) = refs[:-3], refs[-3:]
+    blocks, (slab_ref, near_ref) = refs[:-2], refs[-2:]
     chip = place_ref[0] // 2
     for m, block in enumerate(blocks):
         owner = jnp.bitwise_xor(chip, m)
@@ -276,35 +282,23 @@
         slab_ref[:, planes, rows, :] = block[...]
     other = 1 - chip // chips_y
     near_ref[...] = slab_ref[:, pl.ds(other * (SLAB - NEAR), NEAR)]
-    far_ref[...] = slab_ref[:, pl.ds(NEAR + other * (SLAB - 3 * NEAR), NEAR)]
-
-
-def beyond_kernel(slabs, chips_y, place_ref, scalar_ref, half_ref, near_ref, far_ref, *refs):
-    out_refs, (f, r, w, v0) = refs[:2], refs[2:]
-    ny, slab = f.shape[1], place_ref[1]
-    x = place_ref[0] // 2 // chips_y
-    fine = Level(0, ny, LANES, 0, scalar_ref, f, r, w)
-    zero_rows(v0, ny)
-    last = NEAR * (1 - x)
-    sides = ((1 - x, ((half_ref, 0, HALO),)), (x, ((near_ref, last, NEAR), (far_ref, NEAR - last, NEAR))))
-    for out_ref, (above, parts) in zip(out_refs, sides):
-        for ref, first, size in parts:
-            f[pl.ds(first, size)], r[pl.ds(first, size)] = ref[0], ref[1]
-        beside = jnp.where(above == 1, slab < slabs - 1, slab > 0)
-        inside = jnp.where(beside, DAMPING, 0.0)
-
-        def put(at, weight):
-            w[at] = weight
-            v0[at, pl.ds(8, ny), :] = weight * f[at]
-
-        sweep(range(HALO), lambda at: inside / (r[at] + fine.centre), put)
-        for n in range(NEAR):
-            out_ref[n] = fine.smoothed(v0, 1 + n)
+
+
+def smooth_beyond(fine, inside, half_ref, v0):
+    f, r, w, ny = fine.f, fine.r, fine.w, fine.ny
+    f[...], r[...] = half_ref[0], half_ref[1]
+
+    def put(at, weight):
+        w[at] = weight
+        v0[at, pl.ds(8, ny), :] = weight * f[at]
+
+    sweep(range(HALO), lambda at: inside / (r[at] + fine.centre), put)
+    return [fine.smoothed(v0, 1 + n) for n in range(NEAR)]
 
 
 def pre_kernel(slabs, chips_y, place_ref, scalar_ref, *refs):
     pool_ref, pool_up_ref, slab_ref, half_ref, near_ref = refs[:5]
-    f, r, w, v1, coarse_ref, v0, tmp, pooled = refs[5:]
+    f, r, w, v1, coarse_ref, beyond_ref, v0, tmp, pooled = refs[5:]
     ny = f.shape[1]
     slab = place_ref[1]
     fine = Level(0, ny, LANES, 0, scalar_ref, f, r, w)
@@ -342,6 +336,8 @@
     sweep(range(SLAB // 2), coarsened, put_pooled)
     packed = split_dot(pooled[0], pool_ref[...]) + split_dot(pooled[1], pool_up_ref[...])
     coarse_ref[...] = packed.reshape(coarse_ref.shape)
+    first = HALO + 1 + (1 - x) * (SLAB - HALO)
+    beyond_ref[...] = v1[pl.ds(first, NEAR), pl.ds(8, ny), :]
 
 
 def coarse_kernel(grid, place_ref, scalar_ref, *refs):
@@ -409,16 +405,23 @@
     out_ref[...] = split_dot(values, spread)
 
 
-def post_kernel(by, chips_y, place_ref, scalar_ref, *refs):
-    f, r, w, v1, correction, first_ref, second_ref, kept_ref, sent_ref, va, vb, tmp = refs
+def post_kernel(slabs, by, chips_y, place_ref, scalar_ref, *refs):
+    f, r, w, v1, correction, half_ref, beyond_ref = refs[:7]
+    kept_ref, sent_ref, va, vb, tmp, f_side, r_side, w_side, v_side = refs[7:]
     count, ny = f.shape[:2]
     fine = Level(0, ny, LANES, 0, scalar_ref, f, r, w)
     for v in (va, vb):
         zero_rows(v, ny)
     x, half = place_ref[0] // 2 // chips_y, ny // 2
     window = correction.shape[0] // half
-    for ref, above in ((first_ref, 1 - x), (second_ref, x)):
-        va[pl.ds(1 + above * (SLAB + HALO), NEAR), pl.ds(8, ny), :] = ref[...]
+    side = Level(0, ny, LANES, 0, scalar_ref, f_side, r_side, w_side)
+    zero_rows(v_side, ny)
+    slab = place_ref[1]
+    beside = jnp.where(x == 0, slab < slabs - 1, slab > 0)
+    planes = smooth_beyond(side, jnp.where(beside, DAMPING, 0.0), half_ref, v_side)
+    for n in range(NEAR):
+        va[1 + (1 - x) * (SLAB + HALO) + n, pl.ds(8, ny), :] = planes[n]
+        va[1 + x * (SLAB + HALO) + n, pl.ds(8, ny), :] = beyond_ref[n]
 
     def refined(x):
         return fine.spread_rows(correction[pl.ds(x * half, half), :], tmp.at[x])
@@ -554,37 +557,29 @@
         blocks[:chips_y],
         [(2, HALO, ny, nz)],
     )
-    slab, near, far = local_kernel(
+    slab, near = local_kernel(
         functools.partial(arrange_kernel, chips_y),
         "arrange",
         (place,),
         blocks,
-        [(2, SLAB, ny, nz), edge, edge],
+        [(2, SLAB, ny, nz), edge],
     )
 
     def send_beside(piece, up):
         pairs = [(i, i + step if i % step == up else i - step) for i in range(gx_size)]
         return lax.ppermute(piece, "gx", [(i, j) for i, j in pairs if 0 <= j < gx_size])
 
-    beside = [send_beside(own_half, 1), send_beside(near, 0), send_beside(far, 0)]
+    beside = [send_beside(own_half, 1), send_beside(near, 0)]
     grid, rimmed = (count, ny, nz), (count, ny + 16, nz)
-    f, r, w, v1, coarse = local_kernel(
+    f, r, w, v1, coarse, beyond = local_kernel(
         functools.partial(pre_kernel, slabs, chips_y),
         "pre",
         scalars,
-        (pool_matrix(0), pool_matrix(LANES // 2), slab, *beside[:2]),
-        [grid, grid, grid, rimmed, (SLAB // 2, ny // 2, nz)],
+        (pool_matrix(0), pool_matrix(LANES // 2), slab, *beside),
+        [grid, grid, grid, rimmed, (SLAB // 2, ny // 2, nz), (NEAR, ny, nz)],
         [rimmed, (SLAB, ny, nz), (2, SLAB // 2 * ny // 2, nz)],
     )
     gathered = swap_slabs(coarse, step, slabs)
-    beyond = local_kernel(
-        functools.partial(beyond_kernel, slabs, chips_y),
-        "beyond",
-        scalars,
-        beside,
-        [(NEAR, ny, nz)] * 2,
-        [(HALO, ny, nz)] * 3 + [(HALO, ny + 16, nz)],
-    )
 
     coarse_grid = (nx // 2, ny // 2, nz)
     coarse_rimmed = (nx // 2 + HALO, ny // 2 + 16, nz)
@@ -599,12 +594,12 @@
     )
     result = (SLAB * ny + 8, nz)
     kept, sent = local_kernel(
-        functools.partial(post_kernel, by, chips_y),
+        functools.partial(post_kernel, slabs, by, chips_y),
         "post",
         scalars,
-        (f, r, w, v1, correction, *beyond),
+        (f, r, w, v1, correction, beside[0], send_beside(beyond, 0)),
         [result, result],
-        [rimmed] * 2 + [(SLAB, ny, nz)],
+        [rimmed] * 2 + [(SLAB, ny, nz)] + [(HALO, ny, nz)] * 3 + [(HALO, ny + 16, nz)],
     )
 
     parts = local_kernel(

time: 56.7 us -> 56.9 us (level)
  waiting for transfers between devices: 16.4 us -> 17.6 us
  Pallas kernels: 10.3 us -> 9.53 us
    ppermute x3, waiting for transfers between devices: 0.01 us -> 2.37 us  [send_beside(): lax.ppermute(piece, 'gx', [(i, j) for i, j in pairs if 0 <= j < gx_size])]
    ppermute x6, waiting for transfers between devices: 4.06 us -> 2.97 us  [swap_slabs(): moved.append(lax.ppermute(piece, 'gx', pairs))]
    pallas_call x11 -> x10, Pallas kernels: 10.3 us -> 9.53 us  [local_kernel(): pl.pallas_call(kernel, out_shape=[jax.ShapeDtypeStruct(shape, jnp.float32...]
  transfers between devices with their start and end apart: 18 -> 18, of which waited for: 10 -> 10; matrix products, arithmetic and copies ran while one was open for 0% -> 0% of each run, Pallas kernels for 9% -> 10%
where the time goes in v16:
time: 56.9 us; the launch traced here: 56.7 us
  starting transfers between devices  26.5 us (47%)
  waiting for transfers between devices  17.6 us (31%)
  Pallas kernels  9.53 us (17%)
  local copies, waits for them, and re-layouts  1.12 us (2%)
  other arithmetic  1.04 us (2%)
  between operations  0.8 us (1%)
    ppermute x6, waiting for transfers between devices, swap_in_plane(): moved.append(lax.ppermute(pieces[k], ('gx', 'gy'), pairs))  10.8 us
    ppermute x6, starting transfers between devices, swap_slabs(): moved.append(lax.ppermute(piece, 'gx', pairs))  9.57 us
    pallas_call x10, Pallas kernels, local_kernel(): pl.pallas_call(kernel, out_shape=[jax.ShapeDtypeStruct(shape, jnp.float32...  9.53 us
    ppermute x3, starting transfers between devices, send_beside(): lax.ppermute(piece, 'gx', [(i, j) for i, j in pairs if 0 <= j < gx_size])  8.21 us
    ppermute x6, starting transfers between devices, swap_in_plane(): moved.append(lax.ppermute(pieces[k], ('gx', 'gy'), pairs))  8.1 us
    ppermute x6, waiting for transfers between devices, swap_slabs(): moved.append(lax.ppermute(piece, 'gx', pairs))  2.97 us
    ppermute x3, waiting for transfers between devices, send_beside(): lax.ppermute(piece, 'gx', [(i, j) for i, j in pairs if 0 <= j < gx_size])  2.37 us
    ppermute x1, waiting for transfers between devices, column_body(): lax.ppermute(sent, 'gy', cores)  1.53 us
  transfers between devices with their start and end apart: 18, of which 10 were waited for; matrix products, arithmetic and copies ran while one was open for 0% of the time, Pallas kernels for 10%

profile of v16, /device:TPU:0, one launch (start us, length us, event | category | flops | bytes accessed | tf_op | source)
XLA Modules:
  0.0 56.7 jit_solution(9656808072533734033)
XLA Ops:
  1.3 0.9 %copy-done = f32[8,4,16,128]{3,2,1,0:T(8,128)S(1)} copy-done((f32[8,4,16,128]{3,2,1,0:T(8,128)S(1)}, f32[8,4,16,128]{3,2,1,0:T(8,128)}, u32[]{:S(2)}) %copy-start) | copy-done | bytes 262168
  3.6 3.0 %collective-permute-start.2 = (f32[2,4,32,128]{3,2,1,0:T(8,128)S(1)}, f32[2,4,32,128]{3,2,1,0:T(8,128)S(1)}, u32[]{:S(2)}, u32[]{:S(2)}) collective-permute-start(f32[2,4,32,128]{3,2,1,0:T(8,128)S(1)} %get-tuple-element.26), channel_id=1, source_target_pairs={{0,2},{1,3},{2,0},{3,1},{4,6},{5,7},{6,4},{7,5},{8,10},{9,11},{10,... | collective-permute-start | bytes 393224 | tf_op jit(solution)/shard_map/ppermute | solution.py:513
  6.6 1.5 %collective-permute-start.3 = (f32[2,4,32,128]{3,2,1,0:T(8,128)S(1)}, f32[2,4,32,128]{3,2,1,0:T(8,128)S(1)}, u32[]{:S(2)}, u32[]{:S(2)}) collective-permute-start(f32[2,4,32,128]{3,2,1,0:T(8,128)S(1)} %get-tuple-element.27), channel_id=1, source_target_pairs={{0,4},{1,5},{2,6},{3,7},{4,0},{5,1},{6,2},{7,3},{8,12},{9,13},{10,... | collective-permute-start | bytes 393224 | tf_op jit(solution)/shard_map/ppermute | solution.py:513
  8.2 2.2 %collective-permute-done.2.refs_1_ = f32[2,4,32,128]{3,2,1,0:T(8,128)S(1)} collective-permute-done((f32[2,4,32,128]{3,2,1,0:T(8,128)S(1)}, f32[2,4,32,128]{3,2,1,0:T(8,128)S(1)}, u32[]{:S(2)}, u32[]{:S(2)}) %collective-permute-start.2) | collective-permute-done | bytes 131104 | tf_op jit(solution)/shard_map/ppermute | solution.py:513
  11.0 1.3 %collective-permute-start.5 = (f32[2,4,64,128]{3,2,1,0:T(8,128)S(1)}, f32[2,4,64,128]{3,2,1,0:T(8,128)S(1)}, u32[]{:S(2)}, u32[]{:S(2)}) collective-permute-start(f32[2,4,64,128]{3,2,1,0:T(8,128)S(1)} %half.1), channel_id=1, source_target_pairs={{4,12},{8,0},{12,20},{16,8},{20,28},{24,16},{5,13},{9,1},{13,21},{... | collective-permute-start | bytes 786440 | tf_op jit(solution)/shard_map/ppermute | solution.py:570
  13.0 1.4 %collective-permute-done.4.refs_3_ = f32[2,4,32,128]{3,2,1,0:T(8,128)S(1)} collective-permute-done((f32[2,4,32,128]{3,2,1,0:T(8,128)S(1)}, f32[2,4,32,128]{3,2,1,0:T(8,128)S(1)}, u32[]{:S(2)}, u32[]{:S(2)}) %collective-permute-start.4) | collective-permute-done | bytes 131104 | tf_op jit(solution)/shard_map/ppermute | solution.py:513
  15.1 3.6 %collective-permute-start.6 = (f32[2,2,64,128]{3,2,1,0:T(8,128)S(1)}, f32[2,2,64,128]{3,2,1,0:T(8,128)S(1)}, u32[]{:S(2)}, u32[]{:S(2)}) collective-permute-start(f32[2,2,64,128]{3,2,1,0:T(8,128)S(1)} %get-tuple-element.30), channel_id=1, source_target_pairs={{0,8},{8,16},{12,4},{16,24},{20,12},{28,20},{1,9},{9,17},{13,5},{1... | collective-permute-start | bytes 393224 | tf_op jit(solution)/shard_map/ppermute | solution.py:570
  18.8 2.4 %collective-permute-done.6.refs_4_ = f32[2,2,64,128]{3,2,1,0:T(8,128)S(1)} collective-permute-done((f32[2,2,64,128]{3,2,1,0:T(8,128)S(1)}, f32[2,2,64,128]{3,2,1,0:T(8,128)S(1)}, u32[]{:S(2)}, u32[]{:S(2)}) %collective-permute-start.6) | collective-permute-done | bytes 131104 | tf_op jit(solution)/shard_map/ppermute | solution.py:570
  21.2 1.3 %pre.1 = (f32[16,64,128]{2,1,0:T(8,128)S(1)}, f32[16,64,128]{2,1,0:T(8,128)S(1)}, f32[16,64,128]{2,1,0:T(8,128)S(1)}, f32[16,80,128]{2,1,0:T(8,128)S(1)}, f32[4,...) custom-call(s32[2]{0:T(128)S(1)} %pad_add_fusion.place_ref, f32[8,128]{1,0:T(8,128)S(1)} %get-tuple-element.24.scalar_ref, ...), custom_call_target="tpu_custom_call" | custom-call | tf_op jit(solution)/shard_map/pre/pallas_call | solution.py:497
  22.5 4.5 %collective-permute-start.9 = (f32[4,32,128]{2,1,0:T(8,128)S(1)}, f32[4,32,128]{2,1,0:T(8,128)S(1)}, u32[]{:S(2)}, u32[]{:S(2)}) collective-permute-start(f32[4,32,128]{2,1,0:T(8,128)S(1)} %get-tuple-element.35.refs_2_), channel_id=1, source_target_pairs={{0,24},{4,28},{8,16},{12,20},{16,8},{20,12},{24,0},{28,4},{1,25},{... | collective-permute-start | bytes 196616 | tf_op jit(solution)/shard_map/ppermute | solution.py:522
  27.7 3.3 %collective-permute-start.10 = (f32[2,64,128]{2,1,0:T(8,128)S(1)}, f32[2,64,128]{2,1,0:T(8,128)S(1)}, u32[]{:S(2)}, u32[]{:S(2)}) collective-permute-start(f32[2,64,128]{2,1,0:T(8,128)S(1)} %get-tuple-element.36), channel_id=1, source_target_pairs={{0,8},{8,16},{12,4},{16,24},{20,12},{28,20},{1,9},{9,17},{13,5},{1... | collective-permute-start | bytes 196616 | tf_op jit(solution)/shard_map/ppermute | solution.py:570
  31.0 1.2 %collective-permute-done.8.refs_4_ = f32[4,32,128]{2,1,0:T(8,128)S(1)} collective-permute-done((f32[4,32,128]{2,1,0:T(8,128)S(1)}, f32[4,32,128]{2,1,0:T(8,128)S(1)}, u32[]{:S(2)}, u32[]{:S(2)}) %collective-permute-start.8) | collective-permute-done | bytes 65568 | tf_op jit(solution)/shard_map/ppermute | solution.py:522
  32.2 2.3 %coarse.1.refs_4_ = f32[256,128]{1,0:T(8,128)S(1)} custom-call(s32[2]{0:T(128)S(1)} %pad_add_fusion.place_ref, f32[8,128]{1,0:T(8,128)S(1)} %get-tuple-element.24.scalar_ref, bf16[128,128]{1,0:T(8,128)(2,1)S(1)} %get-tuple-element.46.refs_0_, bf16[128,128]{1,0:T(8,128)(2,1)S(1)} %get-tuple-element.45.refs_1_, f32[4,32,128]{2,1,0:T(8,128)S(1)} %get-tuple-element.35.refs_2_, ...), custom_call_target="tpu_custom_call" | custom-call | tf_op jit(solution)/shard_map/coarse/pallas_call | solution.py:497
  34.6 1.6 %post.1 = (f32[520,128]{1,0:T(8,128)S(1)}, f32[520,128]{1,0:T(8,128)S(1)}) custom-call(s32[2]{0:T(128)S(1)} %pad_add_fusion.place_ref, f32[8,128]{1,0:T(8,128)S(1)} %get-tuple-element.24.scalar_ref, f32[16,64,128]{2,1,0:T(8,128)S(1)} %get-tuple-element.31.refs_0_, f32[16,64,128]{2,1,0:T(8,128)S(1)} %get-tuple-element.32.refs_1_, ...), custom_call_target="tpu_custom_call" | custom-call | tf_op jit(solution)/shard_map/post/pallas_call | solution.py:497
  36.2 1.5 %collective-permute-done.11.got_ref = f32[520,128]{1,0:T(8,128)S(1)} collective-permute-done((f32[520,128]{1,0:T(8,128)S(1)}, f32[520,128]{1,0:T(8,128)S(1)}, u32[]{:S(2)}, u32[]{:S(2)}) %collective-permute-start.11) | collective-permute-done | bytes 266272 | tf_op jit(solution)/shard_map/ppermute | solution.py:609
  38.4 1.6 %collective-permute-start.12 = (f32[272,128]{1,0:T(8,128)S(1)}, f32[272,128]{1,0:T(8,128)S(1)}, u32[]{:S(2)}, u32[]{:S(2)}) collective-permute-start(f32[272,128]{1,0:T(8,128)S(1)} %get-tuple-element.40), channel_id=1, source_target_pairs={{0,2},{1,3},{2,0},{3,1},{4,6},{5,7},{6,4},{7,5},{8,10},{9,11},{10,... | collective-permute-start | bytes 417800 | tf_op jit(solution)/shard_map/ppermute | solution.py:513
  40.0 1.2 %collective-permute-start.13 = (f32[272,128]{1,0:T(8,128)S(1)}, f32[272,128]{1,0:T(8,128)S(1)}, u32[]{:S(2)}, u32[]{:S(2)}) collective-permute-start(f32[272,128]{1,0:T(8,128)S(1)} %get-tuple-element.41), channel_id=1, source_target_pairs={{0,4},{1,5},{2,6},{3,7},{4,0},{5,1},{6,2},{7,3},{8,12},{9,13},{10,... | collective-permute-start | bytes 417800 | tf_op jit(solution)/shard_map/ppermute | solution.py:513
  41.9 2.2 %collective-permute-done.12.refs_1_ = f32[272,128]{1,0:T(8,128)S(1)} collective-permute-done((f32[272,128]{1,0:T(8,128)S(1)}, f32[272,128]{1,0:T(8,128)S(1)}, u32[]{:S(2)}, u32[]{:S(2)}) %collective-permute-start.12) | collective-permute-done | bytes 139296 | tf_op jit(solution)/shard_map/ppermute | solution.py:513
  44.2 2.4 %collective-permute-done.13.refs_2_ = f32[272,128]{1,0:T(8,128)S(1)} collective-permute-done((f32[272,128]{1,0:T(8,128)S(1)}, f32[272,128]{1,0:T(8,128)S(1)}, u32[]{:S(2)}, u32[]{:S(2)}) %collective-permute-start.13) | collective-permute-done | bytes 139296 | tf_op jit(solution)/shard_map/ppermute | solution.py:513
  46.5 1.8 %collective-permute-done.14.refs_3_ = f32[272,128]{1,0:T(8,128)S(1)} collective-permute-done((f32[272,128]{1,0:T(8,128)S(1)}, f32[272,128]{1,0:T(8,128)S(1)}, u32[]{:S(2)}, u32[]{:S(2)}) %collective-permute-start.14) | collective-permute-done | bytes 139296 | tf_op jit(solution)/shard_map/ppermute | solution.py:513
  48.3 3.0 %collective-permute-start.17 = (f32[8,128]{1,0:T(8,128)S(1)}, f32[8,128]{1,0:T(8,128)S(1)}, u32[]{:S(2)}, u32[]{:S(2)}) collective-permute-start(f32[8,128]{1,0:T(8,128)S(1)} %squares.1), channel_id=1, source_target_pairs={{0,24},{4,28},{8,16},{12,20},{16,8},{20,12},{24,0},{28,4},{1,25},{... | collective-permute-start | bytes 12296 | tf_op jit(solution)/shard_map/ppermute | solution.py:522
  51.3 1.4 %collective-permute-start.15 = (f32[8,128]{1,0:T(8,128)S(1)}, f32[8,128]{1,0:T(8,128)S(1)}, u32[]{:S(2)}, u32[]{:S(2)}) collective-permute-start(f32[8,128]{1,0:T(8,128)S(1)} %squares.1), channel_id=1, source_target_pairs={{0,8},{4,12},{8,0},{12,4},{16,24},{20,28},{24,16},{28,20},{1,9},{5... | collective-permute-start | bytes 12296 | tf_op jit(solution)/shard_map/ppermute | solution.py:522
  52.7 1.4 %collect.1 = (f32[8,4,16,128]{3,2,1,0:T(8,128)}, f32[8,4,16,128]{3,2,1,0:T(8,128)}) custom-call(s32[2]{0:T(128)S(1)} %pad_add_fusion.place_ref, f32[272,128]{1,0:T(8,128)S(1)} %get-tuple-element.39.refs_0_, f32[272,128]{1,0:T(8,128)S(1)} %collective-permute-done.12.refs_1_, f32[272,128]{1,0:T(8,128)S(1)} %collective-permute-done.13.refs_2_, ...), custom_call_target="tpu_custom_call" | custom-call | tf_op jit(solution)/shard_map/collect/pallas_call | solution.py:497
  54.1 1.7 %collective-permute-done.16 = f32[8,128]{1,0:T(8,128)S(1)} collective-permute-done((f32[8,128]{1,0:T(8,128)S(1)}, f32[8,128]{1,0:T(8,128)S(1)}, u32[]{:S(2)}, u32[]{:S(2)}) %collective-permute-start.16) | collective-permute-done | bytes 4128 | tf_op jit(solution)/shard_map/ppermute | solution.py:522
  (40 shorter events, 7.0 us)
Async XLA Ops:
  0.6 2.2 %collective-permute-start = (f32[8,4,16,128]{3,2,1,0:T(8,128)}, f32[8,4,16,128]{3,2,1,0:T(8,128)S(1)}, u32[]{:S(2)}, u32[]{:S(2)}) collective-permute-start(f32[8,4,16,128]{3,2,1,0:T(8,128)} %source_ref.1), channel_id=1, source_target_pairs={{0,1},{1,0},{2,3},{3,2},{4,5},{5,4},{6,7},{7,6},{8,9},{9,8},{10,11... | collective-permute-start | bytes 786440 | tf_op jit(solution)/shard_map/ppermute | solution.py:540
  1.1 1.7 %collective-permute-start.1 = (f32[4,16,128]{2,1,0:T(8,128)}, f32[4,16,128]{2,1,0:T(8,128)S(1)}, u32[]{:S(2)}, u32[]{:S(2)}) collective-permute-start(f32[4,16,128]{2,1,0:T(8,128)} %refs_2_.1), channel_id=1, source_target_pairs={{0,1},{1,0},{2,3},{3,2},{4,5},{5,4},{6,7},{7,6},{8,9},{9,8},{10,11... | collective-permute-start | bytes 98312 | tf_op jit(solution)/shard_map/ppermute | solution.py:540
  1.3 0.9 %copy-start = (f32[8,4,16,128]{3,2,1,0:T(8,128)S(1)}, f32[8,4,16,128]{3,2,1,0:T(8,128)}, u32[]{:S(2)}) copy-start(f32[8,4,16,128]{3,2,1,0:T(8,128)} %source_ref.1) | copy-start | bytes 786436
  2.3 0.8 %copy-start.1 = (f32[4,16,128]{2,1,0:T(8,128)S(1)}, f32[4,16,128]{2,1,0:T(8,128)}, u32[]{:S(2)}) copy-start(f32[4,16,128]{2,1,0:T(8,128)} %refs_2_.1) | copy-start | bytes 98308
  2.3 0.8 %copy-start.2 = (f32[8]{0:T(128)S(1)}, f32[8]{0:T(128)}, u32[]{:S(2)}) copy-start(f32[8]{0:T(128)} %shifts_ref.1) | copy-start | bytes 100
  2.3 0.8 %copy-start.3 = (s32[8]{0:T(128)S(1)}, s32[8]{0:T(128)}, u32[]{:S(2)}) copy-start(s32[8]{0:T(128)} %index_ref.1) | copy-start | bytes 100
  2.3 0.8 %copy-start.4 = (f32[3]{0:T(128)S(1)}, f32[3]{0:T(128)}, u32[]{:S(2)}) copy-start(f32[3]{0:T(128)} %velocity_ref.1) | copy-start | bytes 40
  3.6 6.8 %collective-permute-start.2 = (f32[2,4,32,128]{3,2,1,0:T(8,128)S(1)}, f32[2,4,32,128]{3,2,1,0:T(8,128)S(1)}, u32[]{:S(2)}, u32[]{:S(2)}) collective-permute-start(f32[2,4,32,128]{3,2,1,0:T(8,128)S(1)} %get-tuple-element.26), channel_id=1, source_target_pairs={{0,2},{1,3},{2,0},{3,1},{4,6},{5,7},{6,4},{7,5},{8,10},{9,11},{10,... | collective-permute-start | bytes 393224 | tf_op jit(solution)/shard_map/ppermute | solution.py:513
  6.6 6.4 %collective-permute-start.3 = (f32[2,4,32,128]{3,2,1,0:T(8,128)S(1)}, f32[2,4,32,128]{3,2,1,0:T(8,128)S(1)}, u32[]{:S(2)}, u32[]{:S(2)}) collective-permute-start(f32[2,4,32,128]{3,2,1,0:T(8,128)S(1)} %get-tuple-element.27), channel_id=1, source_target_pairs={{0,4},{1,5},{2,6},{3,7},{4,0},{5,1},{6,2},{7,3},{8,12},{9,13},{10,... | collective-permute-start | bytes 393224 | tf_op jit(solution)/shard_map/ppermute | solution.py:513
  8.1 6.3 %collective-permute-start.4 = (f32[2,4,32,128]{3,2,1,0:T(8,128)S(1)}, f32[2,4,32,128]{3,2,1,0:T(8,128)S(1)}, u32[]{:S(2)}, u32[]{:S(2)}) collective-permute-start(f32[2,4,32,128]{3,2,1,0:T(8,128)S(1)} %get-tuple-element.28), channel_id=1, source_target_pairs={{0,6},{1,7},{2,4},{3,5},{4,2},{5,3},{6,0},{7,1},{8,14},{9,15},{10,... | collective-permute-start | bytes 393224 | tf_op jit(solution)/shard_map/ppermute | solution.py:513
  11.0 10.2 %collective-permute-start.5 = (f32[2,4,64,128]{3,2,1,0:T(8,128)S(1)}, f32[2,4,64,128]{3,2,1,0:T(8,128)S(1)}, u32[]{:S(2)}, u32[]{:S(2)}) collective-permute-start(f32[2,4,64,128]{3,2,1,0:T(8,128)S(1)} %half.1), channel_id=1, source_target_pairs={{4,12},{8,0},{12,20},{16,8},{20,28},{24,16},{5,13},{9,1},{13,21},{... | collective-permute-start | bytes 786440 | tf_op jit(solution)/shard_map/ppermute | solution.py:570
  15.1 6.1 %collective-permute-start.6 = (f32[2,2,64,128]{3,2,1,0:T(8,128)S(1)}, f32[2,2,64,128]{3,2,1,0:T(8,128)S(1)}, u32[]{:S(2)}, u32[]{:S(2)}) collective-permute-start(f32[2,2,64,128]{3,2,1,0:T(8,128)S(1)} %get-tuple-element.30), channel_id=1, source_target_pairs={{0,8},{8,16},{12,4},{16,24},{20,12},{28,20},{1,9},{9,17},{13,5},{1... | collective-permute-start | bytes 393224 | tf_op jit(solution)/shard_map/ppermute | solution.py:570
  22.5 8.5 %collective-permute-start.9 = (f32[4,32,128]{2,1,0:T(8,128)S(1)}, f32[4,32,128]{2,1,0:T(8,128)S(1)}, u32[]{:S(2)}, u32[]{:S(2)}) collective-permute-start(f32[4,32,128]{2,1,0:T(8,128)S(1)} %get-tuple-element.35.refs_2_), channel_id=1, source_target_pairs={{0,24},{4,28},{8,16},{12,20},{16,8},{20,12},{24,0},{28,4},{1,25},{... | collective-permute-start | bytes 196616 | tf_op jit(solution)/shard_map/ppermute | solution.py:522
  27.0 5.2 %collective-permute-start.8 = (f32[4,32,128]{2,1,0:T(8,128)S(1)}, f32[4,32,128]{2,1,0:T(8,128)S(1)}, u32[]{:S(2)}, u32[]{:S(2)}) collective-permute-start(f32[4,32,128]{2,1,0:T(8,128)S(1)} %get-tuple-element.35.refs_2_), channel_id=1, source_target_pairs={{0,16},{4,20},{8,24},{12,28},{16,0},{20,4},{24,8},{28,12},{1,17},{... | collective-permute-start | bytes 196616 | tf_op jit(solution)/shard_map/ppermute | solution.py:522
  27.0 5.2 %collective-permute-start.7 = (f32[4,32,128]{2,1,0:T(8,128)S(1)}, f32[4,32,128]{2,1,0:T(8,128)S(1)}, u32[]{:S(2)}, u32[]{:S(2)}) collective-permute-start(f32[4,32,128]{2,1,0:T(8,128)S(1)} %get-tuple-element.35.refs_2_), channel_id=1, source_target_pairs={{0,8},{4,12},{8,0},{12,4},{16,24},{20,28},{24,16},{28,20},{1,9},{5... | collective-permute-start | bytes 196616 | tf_op jit(solution)/shard_map/ppermute | solution.py:522
  27.7 6.9 %collective-permute-start.10 = (f32[2,64,128]{2,1,0:T(8,128)S(1)}, f32[2,64,128]{2,1,0:T(8,128)S(1)}, u32[]{:S(2)}, u32[]{:S(2)}) collective-permute-start(f32[2,64,128]{2,1,0:T(8,128)S(1)} %get-tuple-element.36), channel_id=1, source_target_pairs={{0,8},{8,16},{12,4},{16,24},{20,12},{28,20},{1,9},{9,17},{13,5},{1... | collective-permute-start | bytes 196616 | tf_op jit(solution)/shard_map/ppermute | solution.py:570
  36.2 1.6 %collective-permute-start.11 = (f32[520,128]{1,0:T(8,128)S(1)}, f32[520,128]{1,0:T(8,128)S(1)}, u32[]{:S(2)}, u32[]{:S(2)}) collective-permute-start(f32[520,128]{1,0:T(8,128)S(1)} %get-tuple-element.38), channel_id=1, source_target_pairs={{0,1},{1,0},{2,3},{3,2},{4,5},{5,4},{6,7},{7,6},{8,9},{9,8},{10,11... | collective-permute-start | bytes 798728 | tf_op jit(solution)/shard_map/ppermute | solution.py:609
  38.4 5.8 %collective-permute-start.12 = (f32[272,128]{1,0:T(8,128)S(1)}, f32[272,128]{1,0:T(8,128)S(1)}, u32[]{:S(2)}, u32[]{:S(2)}) collective-permute-start(f32[272,128]{1,0:T(8,128)S(1)} %get-tuple-element.40), channel_id=1, source_target_pairs={{0,2},{1,3},{2,0},{3,1},{4,6},{5,7},{6,4},{7,5},{8,10},{9,11},{10,... | collective-permute-start | bytes 417800 | tf_op jit(solution)/shard_map/ppermute | solution.py:513
  40.0 6.6 %collective-permute-start.13 = (f32[272,128]{1,0:T(8,128)S(1)}, f32[272,128]{1,0:T(8,128)S(1)}, u32[]{:S(2)}, u32[]{:S(2)}) collective-permute-start(f32[272,128]{1,0:T(8,128)S(1)} %get-tuple-element.41), channel_id=1, source_target_pairs={{0,4},{1,5},{2,6},{3,7},{4,0},{5,1},{6,2},{7,3},{8,12},{9,13},{10,... | collective-permute-start | bytes 417800 | tf_op jit(solution)/shard_map/ppermute | solution.py:513
  41.2 7.1 %collective-permute-start.14 = (f32[272,128]{1,0:T(8,128)S(1)}, f32[272,128]{1,0:T(8,128)S(1)}, u32[]{:S(2)}, u32[]{:S(2)}) collective-permute-start(f32[272,128]{1,0:T(8,128)S(1)} %get-tuple-element.42), channel_id=1, source_target_pairs={{0,6},{1,7},{2,4},{3,5},{4,2},{5,3},{6,0},{7,1},{8,14},{9,15},{10,... | collective-permute-start | bytes 417800 | tf_op jit(solution)/shard_map/ppermute | solution.py:513
  48.3 5.8 %collective-permute-start.17 = (f32[8,128]{1,0:T(8,128)S(1)}, f32[8,128]{1,0:T(8,128)S(1)}, u32[]{:S(2)}, u32[]{:S(2)}) collective-permute-start(f32[8,128]{1,0:T(8,128)S(1)} %squares.1), channel_id=1, source_target_pairs={{0,24},{4,28},{8,16},{12,20},{16,8},{20,12},{24,0},{28,4},{1,25},{... | collective-permute-start | bytes 12296 | tf_op jit(solution)/shard_map/ppermute | solution.py:522
  51.3 4.5 %collective-permute-start.16 = (f32[8,128]{1,0:T(8,128)S(1)}, f32[8,128]{1,0:T(8,128)S(1)}, u32[]{:S(2)}, u32[]{:S(2)}) collective-permute-start(f32[8,128]{1,0:T(8,128)S(1)} %squares.1), channel_id=1, source_target_pairs={{0,16},{4,20},{8,24},{12,28},{16,0},{20,4},{24,8},{28,12},{1,17},{... | collective-permute-start | bytes 12296 | tf_op jit(solution)/shard_map/ppermute | solution.py:522
  51.3 4.5 %collective-permute-start.15 = (f32[8,128]{1,0:T(8,128)S(1)}, f32[8,128]{1,0:T(8,128)S(1)}, u32[]{:S(2)}, u32[]{:S(2)}) collective-permute-start(f32[8,128]{1,0:T(8,128)S(1)} %squares.1), channel_id=1, source_target_pairs={{0,8},{4,12},{8,0},{12,4},{16,24},{20,28},{24,16},{28,20},{1,9},{5... | collective-permute-start | bytes 12296 | tf_op jit(solution)/shard_map/ppermute | solution.py:522

commit v17 on v16

--- a/solution.py
+++ b/solution.py
@@ -152,15 +152,14 @@
 
 
 class Level(Grid):
-    def __init__(self, index, ny, nz, rim, scalar_ref, f, r, w):
+    def __init__(self, index, ny, nz, rim, scalars, f, r, w):
         super().__init__(ny)
         self.nz, self.rim = nz, rim
         self.f, self.r, self.w = f, r, w
         spacing = 2.0**index
         scale_a = 1.0 / (spacing * spacing)
         inverse = 1.0 / spacing
-        shift = scalar_ref[0, 0]
-        speed = [scalar_ref[1 + d, 0] for d in range(3)]
+        shift, speed = scalars
         self.backward = [scale_a + jnp.maximum(v, 0.0) * inverse for v in speed]
         self.forward = [scale_a - jnp.minimum(v, 0.0) * inverse for v in speed]
         total = jnp.abs(speed[0]) + jnp.abs(speed[1]) + jnp.abs(speed[2])
@@ -221,6 +220,10 @@
         return jnp.concatenate(v, axis=0)
 
 
+def scalars_of(scalar_ref):
+    return scalar_ref[0, 0], [scalar_ref[1 + d, 0] for d in range(3)]
+
+
 def zero_rows(v, ny):
     edge = jnp.zeros((v.shape[0], 8, LANES), jnp.float32)
     v[:, pl.ds(0, 8), :] = edge
@@ -301,7 +304,7 @@
     f, r, w, v1, coarse_ref, beyond_ref, v0, tmp, pooled = refs[5:]
     ny = f.shape[1]
     slab = place_ref[1]
-    fine = Level(0, ny, LANES, 0, scalar_ref, f, r, w)
+    fine = Level(0, ny, LANES, 0, scalars_of(scalar_ref), f, r, w)
     zero_rows(v0, ny)
     zero_rows(v1, ny)
     after = HALO + SLAB
@@ -349,8 +352,8 @@
     slab = place_ref[1]
     rim = HALO // 2
     nx1, ny1, nx2, ny2 = nx // 2, ny // 2, nx // 4, ny // 4
-    mid = Level(1, ny1, nz // 2, rim, scalar_ref, f1, r1, w1)
-    deep = Level(2, ny2, nz // 4, 0, scalar_ref, None, None, None)
+    mid = Level(1, ny1, nz // 2, rim, scalars_of(scalar_ref), f1, r1, w1)
+    deep = Level(2, ny2, nz // 4, 0, scalars_of(scalar_ref), None, None, None)
     for v in (v1a, v1b):
         zero_rows(v, ny1)
         blank = jnp.zeros((rim,) + v.shape[1:], jnp.float32)
@@ -409,12 +412,12 @@
     f, r, w, v1, correction, half_ref, beyond_ref = refs[:7]
     kept_ref, sent_ref, va, vb, tmp, f_side, r_side, w_side, v_side = refs[7:]
     count, ny = f.shape[:2]
-    fine = Level(0, ny, LANES, 0, scalar_ref, f, r, w)
+    fine = Level(0, ny, LANES, 0, scalars_of(scalar_ref), f, r, w)
     for v in (va, vb):
         zero_rows(v, ny)
     x, half = place_ref[0] // 2 // chips_y, ny // 2
     window = correction.shape[0] // half
-    side = Level(0, ny, LANES, 0, scalar_ref, f_side, r_side, w_side)
+    side = Level(0, ny, LANES, 0, scalars_of(scalar_ref), f_side, r_side, w_side)
     zero_rows(v_side, ny)
     slab = place_ref[1]
     beside = jnp.where(x == 0, slab < slabs - 1, slab > 0)
@@ -455,38 +458,68 @@
         ref[pl.ds(2 * area, 8), :] = squares
 
 
+def part_rows(bx, by):
+    outer = bx * by
+    edges = outer + 2 * by
+    squares = edges + 2 * (bx - 2)
+    return outer, edges, squares, (squares + 8) // 8 * 8
+
+
 def merge_back_kernel(bx, by, chips_y, place_ref, kept_ref, got_ref, *out_refs):
     chip, core = place_ref[0] // 2, place_ref[0] & 1
-    area, half = bx * by, chips_y * by
+    half = chips_y * by
+    outer, edges, squares, size = part_rows(bx, by)
     for m, out_ref in enumerate(out_refs):
         target = jnp.bitwise_xor(chip, m)
         first = (target // chips_y) * bx * half + lax.rem(target, chips_y) * by
         for ref, column in ((kept_ref, core), (got_ref, 1 - core)):
-            for n in range(2):
-                for p in range(bx):
-                    at = pl.multiple_of(first + (n * SLAB + p) * half, 8)
-                    to = pl.multiple_of((2 * column + n) * area + p * by, 8)
-                    out_ref[pl.ds(to, by), :] = ref[pl.ds(at, by), :]
-            to = pl.multiple_of(4 * area + 8 * column, 8)
-            out_ref[pl.ds(to, 8), :] = ref[pl.ds(2 * SLAB * half, 8), :]
-
-
-def collect_kernel(place_ref, *refs):
+            base = pl.multiple_of(column * size, 8)
+            for p in range(bx):
+                at = pl.multiple_of(first + p * half, 8)
+                out_ref[pl.ds(base + p * by, by), :] = ref[pl.ds(at, by), :]
+                at = pl.multiple_of(at + SLAB * half, 8)
+                if p in (0, bx - 1):
+                    out_ref[pl.ds(base + outer + (p > 0) * by, by), :] = ref[pl.ds(at, by), :]
+                else:
+                    rows = ref[pl.ds(at, by), :]
+                    to = base + edges + 2 * (p - 1)
+                    out_ref[pl.ds(to, 1), :] = rows[:1]
+                    out_ref[pl.ds(to + 1, 1), :] = rows[by - 1 :]
+            out_ref[pl.ds(base + squares, 1), :] = ref[pl.ds(2 * SLAB * half, 1), :]
+
+
+def collect_kernel(place_ref, shifts_ref, index_ref, velocity_ref, source_ref, reaction_ref, *refs):
     parts, (iterate_ref, residual_ref) = refs[:-2], refs[-2:]
-    _, bx, by, _ = iterate_ref.shape
-    area = bx * by
+    _, bx, by, nz = iterate_ref.shape
+    outer, edges, _, size = part_rows(bx, by)
+    fine = Level(0, by, nz, 0, (0.0, [velocity_ref[d] for d in range(3)]), None, None, None)
+    reaction = [reaction_ref[p] + fine.centre for p in range(1, bx - 1)]
     for m, part in enumerate(parts):
         target = jnp.bitwise_xor(place_ref[0] // 2, m)
         for n in range(2):
-            for k, ref in enumerate((iterate_ref, residual_ref)):
-                rows = pl.ds((2 * n + k) * area, area)
-                ref[2 * target + n] = part[rows, :].reshape(bx, by, LANES)
-
-
-def squares_kernel(row, *refs):
+            base, column = n * size, 2 * target + n
+            shift = shifts_ref[index_ref[column]]
+            planes = [part[pl.ds(base + p * by, by), :] for p in range(bx)]
+            for p in range(bx):
+                iterate_ref[column, p] = planes[p]
+            for p in (0, bx - 1):
+                residual_ref[column, p] = part[pl.ds(base + outer + (p > 0) * by, by), :]
+            for p in range(1, bx - 1):
+                here = planes[p]
+                pulled = source_ref[column, p] + fine.along_z(here)
+                pulled += fine.backward[0] * planes[p - 1] + fine.forward[0] * planes[p + 1]
+                pulled += fine.backward[1] * pltpu.roll(here, 1, 0) + fine.forward[1] * pltpu.roll(here, by - 1, 0)
+                residual_ref[column, p] = pulled - (reaction[p - 1] + shift) * here
+                at = base + edges + 2 * (p - 1)
+                residual_ref[column, p, pl.ds(0, 1), :] = part[pl.ds(at, 1), :]
+                residual_ref[column, p, pl.ds(by - 1, 1), :] = part[pl.ds(at + 1, 1), :]
+
+
+def squares_kernel(bx, by, *refs):
+    _, _, squares, size = part_rows(bx, by)
     for m, part in enumerate(refs[:-1]):
         for n in range(2):
-            refs[-1][pl.ds(2 * m + n, 1), :] = part[pl.ds(row + 8 * n, 1), :]
+            refs[-1][pl.ds(2 * m + n, 1), :] = part[pl.ds(n * size + squares, 1), :]
 
 
 SMEM = pl.BlockSpec(memory_space=pltpu.SMEM)
@@ -607,14 +640,18 @@
         "merge_back",
         (place,),
         (kept, lax.ppermute(sent, "gy", cores)),
-        [(4 * area + 16, nz)] * chips,
+        [(2 * part_rows(bx, by)[3], nz)] * chips,
     )
     parts = swap_in_plane(parts, 2)
     (squares,) = local_kernel(
-        functools.partial(squares_kernel, 4 * area), "squares", (), parts, [(columns, nz)]
+        functools.partial(squares_kernel, bx, by), "squares", (), parts, [(columns, nz)]
     )
     iterate, residual = local_kernel(
-        collect_kernel, "collect", (place,), parts, [source.shape] * 2
+        collect_kernel,
+        "collect",
+        (place, shifts, shift_index, velocity),
+        (source, reaction, *parts),
+        [source.shape] * 2,
     )
     total = sum(swap_slabs(squares, step, slabs))
     rms = jnp.sqrt(total[:, 0] / (nx * ny * nz) + EPSILON)

time: 56.9 us -> 55.5 us (0.975)
  waiting for transfers between devices: 17.6 us -> 16.2 us
    ppermute x6, waiting for transfers between devices: 10.8 us -> 9.35 us  [swap_in_plane(): moved.append(lax.ppermute(pieces[k], ('gx', 'gy'), pairs))]
where the time goes in v17:
time: 55.5 us; the launch traced here: 55.3 us
  starting transfers between devices  26.5 us (48%)
  waiting for transfers between devices  16.2 us (29%)
  Pallas kernels  9.56 us (17%)
  local copies, waits for them, and re-layouts  1.13 us (2%)
  other arithmetic  1.04 us (2%)
  between operations  0.81 us (1%)
    ppermute x6, starting transfers between devices, swap_slabs(): moved.append(lax.ppermute(piece, 'gx', pairs))  9.57 us
    pallas_call x10, Pallas kernels, local_kernel(): pl.pallas_call(kernel, out_shape=[jax.ShapeDtypeStruct(shape, jnp.float32...  9.56 us
    ppermute x6, waiting for transfers between devices, swap_in_plane(): moved.append(lax.ppermute(pieces[k], ('gx', 'gy'), pairs))  9.35 us
    ppermute x3, starting transfers between devices, send_beside(): lax.ppermute(piece, 'gx', [(i, j) for i, j in pairs if 0 <= j < gx_size])  8.21 us
    ppermute x6, starting transfers between devices, swap_in_plane(): moved.append(lax.ppermute(pieces[k], ('gx', 'gy'), pairs))  8.1 us
    ppermute x6, waiting for transfers between devices, swap_slabs(): moved.append(lax.ppermute(piece, 'gx', pairs))  2.93 us
    ppermute x3, waiting for transfers between devices, send_beside(): lax.ppermute(piece, 'gx', [(i, j) for i, j in pairs if 0 <= j < gx_size])  2.37 us
    ppermute x1, waiting for transfers between devices, column_body(): lax.ppermute(sent, 'gy', cores)  1.53 us
  transfers between devices with their start and end apart: 18, of which 10 were waited for; matrix products, arithmetic and copies ran while one was open for 0% of the time, Pallas kernels for 10%

profile of v17, /device:TPU:0, one launch (start us, length us, event | category | flops | bytes accessed | tf_op | source)
XLA Modules:
  0.0 55.3 jit_solution(8493349237567557302)
XLA Ops:
  1.3 0.9 %copy-done = f32[8,4,16,128]{3,2,1,0:T(8,128)S(1)} copy-done((f32[8,4,16,128]{3,2,1,0:T(8,128)S(1)}, f32[8,4,16,128]{3,2,1,0:T(8,128)}, u32[]{:S(2)}) %copy-start) | copy-done | bytes 262168
  3.6 3.0 %collective-permute-start.2 = (f32[2,4,32,128]{3,2,1,0:T(8,128)S(1)}, f32[2,4,32,128]{3,2,1,0:T(8,128)S(1)}, u32[]{:S(2)}, u32[]{:S(2)}) collective-permute-start(f32[2,4,32,128]{3,2,1,0:T(8,128)S(1)} %get-tuple-element.26), channel_id=1, source_target_pairs={{0,2},{1,3},{2,0},{3,1},{4,6},{5,7},{6,4},{7,5},{8,10},{9,11},{10,... | collective-permute-start | bytes 393224 | tf_op jit(solution)/shard_map/ppermute | solution.py:546
  6.6 1.5 %collective-permute-start.3 = (f32[2,4,32,128]{3,2,1,0:T(8,128)S(1)}, f32[2,4,32,128]{3,2,1,0:T(8,128)S(1)}, u32[]{:S(2)}, u32[]{:S(2)}) collective-permute-start(f32[2,4,32,128]{3,2,1,0:T(8,128)S(1)} %get-tuple-element.27), channel_id=1, source_target_pairs={{0,4},{1,5},{2,6},{3,7},{4,0},{5,1},{6,2},{7,3},{8,12},{9,13},{10,... | collective-permute-start | bytes 393224 | tf_op jit(solution)/shard_map/ppermute | solution.py:546
  8.2 2.2 %collective-permute-done.2.refs_1_ = f32[2,4,32,128]{3,2,1,0:T(8,128)S(1)} collective-permute-done((f32[2,4,32,128]{3,2,1,0:T(8,128)S(1)}, f32[2,4,32,128]{3,2,1,0:T(8,128)S(1)}, u32[]{:S(2)}, u32[]{:S(2)}) %collective-permute-start.2) | collective-permute-done | bytes 131104 | tf_op jit(solution)/shard_map/ppermute | solution.py:546
  11.0 1.3 %collective-permute-start.5 = (f32[2,4,64,128]{3,2,1,0:T(8,128)S(1)}, f32[2,4,64,128]{3,2,1,0:T(8,128)S(1)}, u32[]{:S(2)}, u32[]{:S(2)}) collective-permute-start(f32[2,4,64,128]{3,2,1,0:T(8,128)S(1)} %half.1), channel_id=1, source_target_pairs={{4,12},{8,0},{12,20},{16,8},{20,28},{24,16},{5,13},{9,1},{13,21},{... | collective-permute-start | bytes 786440 | tf_op jit(solution)/shard_map/ppermute | solution.py:603
  13.0 1.4 %collective-permute-done.4.refs_3_ = f32[2,4,32,128]{3,2,1,0:T(8,128)S(1)} collective-permute-done((f32[2,4,32,128]{3,2,1,0:T(8,128)S(1)}, f32[2,4,32,128]{3,2,1,0:T(8,128)S(1)}, u32[]{:S(2)}, u32[]{:S(2)}) %collective-permute-start.4) | collective-permute-done | bytes 131104 | tf_op jit(solution)/shard_map/ppermute | solution.py:546
  15.1 3.6 %collective-permute-start.6 = (f32[2,2,64,128]{3,2,1,0:T(8,128)S(1)}, f32[2,2,64,128]{3,2,1,0:T(8,128)S(1)}, u32[]{:S(2)}, u32[]{:S(2)}) collective-permute-start(f32[2,2,64,128]{3,2,1,0:T(8,128)S(1)} %get-tuple-element.30), channel_id=1, source_target_pairs={{0,8},{8,16},{12,4},{16,24},{20,12},{28,20},{1,9},{9,17},{13,5},{1... | collective-permute-start | bytes 393224 | tf_op jit(solution)/shard_map/ppermute | solution.py:603
  18.8 2.4 %collective-permute-done.6.refs_4_ = f32[2,2,64,128]{3,2,1,0:T(8,128)S(1)} collective-permute-done((f32[2,2,64,128]{3,2,1,0:T(8,128)S(1)}, f32[2,2,64,128]{3,2,1,0:T(8,128)S(1)}, u32[]{:S(2)}, u32[]{:S(2)}) %collective-permute-start.6) | collective-permute-done | bytes 131104 | tf_op jit(solution)/shard_map/ppermute | solution.py:603
  21.2 1.3 %pre.1 = (f32[16,64,128]{2,1,0:T(8,128)S(1)}, f32[16,64,128]{2,1,0:T(8,128)S(1)}, f32[16,64,128]{2,1,0:T(8,128)S(1)}, f32[16,80,128]{2,1,0:T(8,128)S(1)}, f32[4,...) custom-call(s32[2]{0:T(128)S(1)} %pad_add_fusion.place_ref, f32[8,128]{1,0:T(8,128)S(1)} %get-tuple-element.24.scalar_ref, ...), custom_call_target="tpu_custom_call" | custom-call | tf_op jit(solution)/shard_map/pre/pallas_call | solution.py:530
  22.5 4.5 %collective-permute-start.9 = (f32[4,32,128]{2,1,0:T(8,128)S(1)}, f32[4,32,128]{2,1,0:T(8,128)S(1)}, u32[]{:S(2)}, u32[]{:S(2)}) collective-permute-start(f32[4,32,128]{2,1,0:T(8,128)S(1)} %get-tuple-element.35.refs_2_), channel_id=1, source_target_pairs={{0,24},{4,28},{8,16},{12,20},{16,8},{20,12},{24,0},{28,4},{1,25},{... | collective-permute-start | bytes 196616 | tf_op jit(solution)/shard_map/ppermute | solution.py:555
  27.7 3.3 %collective-permute-start.10 = (f32[2,64,128]{2,1,0:T(8,128)S(1)}, f32[2,64,128]{2,1,0:T(8,128)S(1)}, u32[]{:S(2)}, u32[]{:S(2)}) collective-permute-start(f32[2,64,128]{2,1,0:T(8,128)S(1)} %get-tuple-element.36), channel_id=1, source_target_pairs={{0,8},{8,16},{12,4},{16,24},{20,12},{28,20},{1,9},{9,17},{13,5},{1... | collective-permute-start | bytes 196616 | tf_op jit(solution)/shard_map/ppermute | solution.py:603
  31.0 1.2 %collective-permute-done.8.refs_4_ = f32[4,32,128]{2,1,0:T(8,128)S(1)} collective-permute-done((f32[4,32,128]{2,1,0:T(8,128)S(1)}, f32[4,32,128]{2,1,0:T(8,128)S(1)}, u32[]{:S(2)}, u32[]{:S(2)}) %collective-permute-start.8) | collective-permute-done | bytes 65568 | tf_op jit(solution)/shard_map/ppermute | solution.py:555
  32.2 2.3 %coarse.1.refs_4_ = f32[256,128]{1,0:T(8,128)S(1)} custom-call(s32[2]{0:T(128)S(1)} %pad_add_fusion.place_ref, f32[8,128]{1,0:T(8,128)S(1)} %get-tuple-element.24.scalar_ref, bf16[128,128]{1,0:T(8,128)(2,1)S(1)} %get-tuple-element.46.refs_0_, bf16[128,128]{1,0:T(8,128)(2,1)S(1)} %get-tuple-element.45.refs_1_, f32[4,32,128]{2,1,0:T(8,128)S(1)} %get-tuple-element.35.refs_2_, ...), custom_call_target="tpu_custom_call" | custom-call | tf_op jit(solution)/shard_map/coarse/pallas_call | solution.py:530
  34.6 1.6 %post.1 = (f32[520,128]{1,0:T(8,128)S(1)}, f32[520,128]{1,0:T(8,128)S(1)}) custom-call(s32[2]{0:T(128)S(1)} %pad_add_fusion.place_ref, f32[8,128]{1,0:T(8,128)S(1)} %get-tuple-element.24.scalar_ref, f32[16,64,128]{2,1,0:T(8,128)S(1)} %get-tuple-element.31.refs_0_, f32[16,64,128]{2,1,0:T(8,128)S(1)} %get-tuple-element.32.refs_1_, ...), custom_call_target="tpu_custom_call" | custom-call | tf_op jit(solution)/shard_map/post/pallas_call | solution.py:530
  36.2 1.5 %collective-permute-done.11.got_ref = f32[520,128]{1,0:T(8,128)S(1)} collective-permute-done((f32[520,128]{1,0:T(8,128)S(1)}, f32[520,128]{1,0:T(8,128)S(1)}, u32[]{:S(2)}, u32[]{:S(2)}) %collective-permute-start.11) | collective-permute-done | bytes 266272 | tf_op jit(solution)/shard_map/ppermute | solution.py:642
  38.4 1.6 %collective-permute-start.12 = (f32[208,128]{1,0:T(8,128)S(1)}, f32[208,128]{1,0:T(8,128)S(1)}, u32[]{:S(2)}, u32[]{:S(2)}) collective-permute-start(f32[208,128]{1,0:T(8,128)S(1)} %get-tuple-element.40), channel_id=1, source_target_pairs={{0,2},{1,3},{2,0},{3,1},{4,6},{5,7},{6,4},{7,5},{8,10},{9,11},{10,... | collective-permute-start | bytes 319496 | tf_op jit(solution)/shard_map/ppermute | solution.py:546
  40.0 1.2 %collective-permute-start.13 = (f32[208,128]{1,0:T(8,128)S(1)}, f32[208,128]{1,0:T(8,128)S(1)}, u32[]{:S(2)}, u32[]{:S(2)}) collective-permute-start(f32[208,128]{1,0:T(8,128)S(1)} %get-tuple-element.41), channel_id=1, source_target_pairs={{0,4},{1,5},{2,6},{3,7},{4,0},{5,1},{6,2},{7,3},{8,12},{9,13},{10,... | collective-permute-start | bytes 319496 | tf_op jit(solution)/shard_map/ppermute | solution.py:546
  41.9 1.5 %collective-permute-done.12.refs_1_ = f32[208,128]{1,0:T(8,128)S(1)} collective-permute-done((f32[208,128]{1,0:T(8,128)S(1)}, f32[208,128]{1,0:T(8,128)S(1)}, u32[]{:S(2)}, u32[]{:S(2)}) %collective-permute-start.12) | collective-permute-done | bytes 106528 | tf_op jit(solution)/shard_map/ppermute | solution.py:546
  43.5 2.4 %collective-permute-done.13.refs_2_ = f32[208,128]{1,0:T(8,128)S(1)} collective-permute-done((f32[208,128]{1,0:T(8,128)S(1)}, f32[208,128]{1,0:T(8,128)S(1)}, u32[]{:S(2)}, u32[]{:S(2)}) %collective-permute-start.13) | collective-permute-done | bytes 106528 | tf_op jit(solution)/shard_map/ppermute | solution.py:546
  45.8 1.1 %collective-permute-done.14.refs_3_ = f32[208,128]{1,0:T(8,128)S(1)} collective-permute-done((f32[208,128]{1,0:T(8,128)S(1)}, f32[208,128]{1,0:T(8,128)S(1)}, u32[]{:S(2)}, u32[]{:S(2)}) %collective-permute-start.14) | collective-permute-done | bytes 106528 | tf_op jit(solution)/shard_map/ppermute | solution.py:546
  46.9 3.0 %collective-permute-start.17 = (f32[8,128]{1,0:T(8,128)S(1)}, f32[8,128]{1,0:T(8,128)S(1)}, u32[]{:S(2)}, u32[]{:S(2)}) collective-permute-start(f32[8,128]{1,0:T(8,128)S(1)} %squares.1), channel_id=1, source_target_pairs={{0,24},{4,28},{8,16},{12,20},{16,8},{20,12},{24,0},{28,4},{1,25},{... | collective-permute-start | bytes 12296 | tf_op jit(solution)/shard_map/ppermute | solution.py:555
  49.9 1.4 %collective-permute-start.15 = (f32[8,128]{1,0:T(8,128)S(1)}, f32[8,128]{1,0:T(8,128)S(1)}, u32[]{:S(2)}, u32[]{:S(2)}) collective-permute-start(f32[8,128]{1,0:T(8,128)S(1)} %squares.1), channel_id=1, source_target_pairs={{0,8},{4,12},{8,0},{12,4},{16,24},{20,28},{24,16},{28,20},{1,9},{5... | collective-permute-start | bytes 12296 | tf_op jit(solution)/shard_map/ppermute | solution.py:555
  51.3 1.4 %collect.1 = (f32[8,4,16,128]{3,2,1,0:T(8,128)}, f32[8,4,16,128]{3,2,1,0:T(8,128)}) custom-call(s32[2]{0:T(128)S(1)} %pad_add_fusion.place_ref, f32[8]{0:T(128)S(1)} %copy-done.3, s32[8]{0:T(128)S(1)} %copy-done.4, f32[3]{0:T(128)S(1)} %copy-done.5, f32[8,4,16,128]{3,2,1,0:T(8,128)S(1)} %copy-done.1, f32[4,16,128]{2,1,0:T(8,128)S(1)} %copy-done.2, ...), custom_call_target="tpu_custom_call" | custom-call | tf_op jit(solution)/shard_map/collect/pallas_call | solution.py:530
  52.7 1.7 %collective-permute-done.16 = f32[8,128]{1,0:T(8,128)S(1)} collective-permute-done((f32[8,128]{1,0:T(8,128)S(1)}, f32[8,128]{1,0:T(8,128)S(1)}, u32[]{:S(2)}, u32[]{:S(2)}) %collective-permute-start.16) | collective-permute-done | bytes 4128 | tf_op jit(solution)/shard_map/ppermute | solution.py:555
  (42 shorter events, 7.0 us)
Async XLA Ops:
  0.6 2.2 %collective-permute-start = (f32[8,4,16,128]{3,2,1,0:T(8,128)}, f32[8,4,16,128]{3,2,1,0:T(8,128)S(1)}, u32[]{:S(2)}, u32[]{:S(2)}) collective-permute-start(f32[8,4,16,128]{3,2,1,0:T(8,128)} %source_ref.3), channel_id=1, source_target_pairs={{0,1},{1,0},{2,3},{3,2},{4,5},{5,4},{6,7},{7,6},{8,9},{9,8},{10,11... | collective-permute-start | bytes 786440 | tf_op jit(solution)/shard_map/ppermute | solution.py:573
  1.1 1.7 %collective-permute-start.1 = (f32[4,16,128]{2,1,0:T(8,128)}, f32[4,16,128]{2,1,0:T(8,128)S(1)}, u32[]{:S(2)}, u32[]{:S(2)}) collective-permute-start(f32[4,16,128]{2,1,0:T(8,128)} %reaction_ref.1), channel_id=1, source_target_pairs={{0,1},{1,0},{2,3},{3,2},{4,5},{5,4},{6,7},{7,6},{8,9},{9,8},{10,11... | collective-permute-start | bytes 98312 | tf_op jit(solution)/shard_map/ppermute | solution.py:573
  1.3 0.9 %copy-start = (f32[8,4,16,128]{3,2,1,0:T(8,128)S(1)}, f32[8,4,16,128]{3,2,1,0:T(8,128)}, u32[]{:S(2)}) copy-start(f32[8,4,16,128]{3,2,1,0:T(8,128)} %source_ref.3) | copy-start | bytes 786436
  2.3 0.8 %copy-start.2 = (f32[4,16,128]{2,1,0:T(8,128)S(1)}, f32[4,16,128]{2,1,0:T(8,128)}, u32[]{:S(2)}) copy-start(f32[4,16,128]{2,1,0:T(8,128)} %reaction_ref.1) | copy-start | bytes 98308
  2.3 0.8 %copy-start.3 = (f32[8]{0:T(128)S(1)}, f32[8]{0:T(128)}, u32[]{:S(2)}) copy-start(f32[8]{0:T(128)} %shifts_ref.3) | copy-start | bytes 100
  2.3 0.8 %copy-start.4 = (s32[8]{0:T(128)S(1)}, s32[8]{0:T(128)}, u32[]{:S(2)}) copy-start(s32[8]{0:T(128)} %index_ref.3) | copy-start | bytes 100
  2.3 0.8 %copy-start.5 = (f32[3]{0:T(128)S(1)}, f32[3]{0:T(128)}, u32[]{:S(2)}) copy-start(f32[3]{0:T(128)} %velocity_ref.3) | copy-start | bytes 40
  3.6 6.8 %collective-permute-start.2 = (f32[2,4,32,128]{3,2,1,0:T(8,128)S(1)}, f32[2,4,32,128]{3,2,1,0:T(8,128)S(1)}, u32[]{:S(2)}, u32[]{:S(2)}) collective-permute-start(f32[2,4,32,128]{3,2,1,0:T(8,128)S(1)} %get-tuple-element.26), channel_id=1, source_target_pairs={{0,2},{1,3},{2,0},{3,1},{4,6},{5,7},{6,4},{7,5},{8,10},{9,11},{10,... | collective-permute-start | bytes 393224 | tf_op jit(solution)/shard_map/ppermute | solution.py:546
  6.6 6.4 %collective-permute-start.3 = (f32[2,4,32,128]{3,2,1,0:T(8,128)S(1)}, f32[2,4,32,128]{3,2,1,0:T(8,128)S(1)}, u32[]{:S(2)}, u32[]{:S(2)}) collective-permute-start(f32[2,4,32,128]{3,2,1,0:T(8,128)S(1)} %get-tuple-element.27), channel_id=1, source_target_pairs={{0,4},{1,5},{2,6},{3,7},{4,0},{5,1},{6,2},{7,3},{8,12},{9,13},{10,... | collective-permute-start | bytes 393224 | tf_op jit(solution)/shard_map/ppermute | solution.py:546
  8.1 6.3 %collective-permute-start.4 = (f32[2,4,32,128]{3,2,1,0:T(8,128)S(1)}, f32[2,4,32,128]{3,2,1,0:T(8,128)S(1)}, u32[]{:S(2)}, u32[]{:S(2)}) collective-permute-start(f32[2,4,32,128]{3,2,1,0:T(8,128)S(1)} %get-tuple-element.28), channel_id=1, source_target_pairs={{0,6},{1,7},{2,4},{3,5},{4,2},{5,3},{6,0},{7,1},{8,14},{9,15},{10,... | collective-permute-start | bytes 393224 | tf_op jit(solution)/shard_map/ppermute | solution.py:546
  11.0 10.2 %collective-permute-start.5 = (f32[2,4,64,128]{3,2,1,0:T(8,128)S(1)}, f32[2,4,64,128]{3,2,1,0:T(8,128)S(1)}, u32[]{:S(2)}, u32[]{:S(2)}) collective-permute-start(f32[2,4,64,128]{3,2,1,0:T(8,128)S(1)} %half.1), channel_id=1, source_target_pairs={{4,12},{8,0},{12,20},{16,8},{20,28},{24,16},{5,13},{9,1},{13,21},{... | collective-permute-start | bytes 786440 | tf_op jit(solution)/shard_map/ppermute | solution.py:603
  15.1 6.1 %collective-permute-start.6 = (f32[2,2,64,128]{3,2,1,0:T(8,128)S(1)}, f32[2,2,64,128]{3,2,1,0:T(8,128)S(1)}, u32[]{:S(2)}, u32[]{:S(2)}) collective-permute-start(f32[2,2,64,128]{3,2,1,0:T(8,128)S(1)} %get-tuple-element.30), channel_id=1, source_target_pairs={{0,8},{8,16},{12,4},{16,24},{20,12},{28,20},{1,9},{9,17},{13,5},{1... | collective-permute-start | bytes 393224 | tf_op jit(solution)/shard_map/ppermute | solution.py:603
  22.5 8.5 %collective-permute-start.9 = (f32[4,32,128]{2,1,0:T(8,128)S(1)}, f32[4,32,128]{2,1,0:T(8,128)S(1)}, u32[]{:S(2)}, u32[]{:S(2)}) collective-permute-start(f32[4,32,128]{2,1,0:T(8,128)S(1)} %get-tuple-element.35.refs_2_), channel_id=1, source_target_pairs={{0,24},{4,28},{8,16},{12,20},{16,8},{20,12},{24,0},{28,4},{1,25},{... | collective-permute-start | bytes 196616 | tf_op jit(solution)/shard_map/ppermute | solution.py:555
  27.0 5.2 %collective-permute-start.8 = (f32[4,32,128]{2,1,0:T(8,128)S(1)}, f32[4,32,128]{2,1,0:T(8,128)S(1)}, u32[]{:S(2)}, u32[]{:S(2)}) collective-permute-start(f32[4,32,128]{2,1,0:T(8,128)S(1)} %get-tuple-element.35.refs_2_), channel_id=1, source_target_pairs={{0,16},{4,20},{8,24},{12,28},{16,0},{20,4},{24,8},{28,12},{1,17},{... | collective-permute-start | bytes 196616 | tf_op jit(solution)/shard_map/ppermute | solution.py:555
  27.0 5.2 %collective-permute-start.7 = (f32[4,32,128]{2,1,0:T(8,128)S(1)}, f32[4,32,128]{2,1,0:T(8,128)S(1)}, u32[]{:S(2)}, u32[]{:S(2)}) collective-permute-start(f32[4,32,128]{2,1,0:T(8,128)S(1)} %get-tuple-element.35.refs_2_), channel_id=1, source_target_pairs={{0,8},{4,12},{8,0},{12,4},{16,24},{20,28},{24,16},{28,20},{1,9},{5... | collective-permute-start | bytes 196616 | tf_op jit(solution)/shard_map/ppermute | solution.py:555
  27.7 6.9 %collective-permute-start.10 = (f32[2,64,128]{2,1,0:T(8,128)S(1)}, f32[2,64,128]{2,1,0:T(8,128)S(1)}, u32[]{:S(2)}, u32[]{:S(2)}) collective-permute-start(f32[2,64,128]{2,1,0:T(8,128)S(1)} %get-tuple-element.36), channel_id=1, source_target_pairs={{0,8},{8,16},{12,4},{16,24},{20,12},{28,20},{1,9},{9,17},{13,5},{1... | collective-permute-start | bytes 196616 | tf_op jit(solution)/shard_map/ppermute | solution.py:603
  36.2 1.6 %collective-permute-start.11 = (f32[520,128]{1,0:T(8,128)S(1)}, f32[520,128]{1,0:T(8,128)S(1)}, u32[]{:S(2)}, u32[]{:S(2)}) collective-permute-start(f32[520,128]{1,0:T(8,128)S(1)} %get-tuple-element.38), channel_id=1, source_target_pairs={{0,1},{1,0},{2,3},{3,2},{4,5},{5,4},{6,7},{7,6},{8,9},{9,8},{10,11... | collective-permute-start | bytes 798728 | tf_op jit(solution)/shard_map/ppermute | solution.py:642
  38.4 13.0 %copy-start.1 = (f32[8,4,16,128]{3,2,1,0:T(8,128)S(1)}, f32[8,4,16,128]{3,2,1,0:T(8,128)}, u32[]{:S(2)}) copy-start(f32[8,4,16,128]{3,2,1,0:T(8,128)} %source_ref.3) | copy-start | bytes 786436
  38.4 5.1 %collective-permute-start.12 = (f32[208,128]{1,0:T(8,128)S(1)}, f32[208,128]{1,0:T(8,128)S(1)}, u32[]{:S(2)}, u32[]{:S(2)}) collective-permute-start(f32[208,128]{1,0:T(8,128)S(1)} %get-tuple-element.40), channel_id=1, source_target_pairs={{0,2},{1,3},{2,0},{3,1},{4,6},{5,7},{6,4},{7,5},{8,10},{9,11},{10,... | collective-permute-start | bytes 319496 | tf_op jit(solution)/shard_map/ppermute | solution.py:546
  40.0 5.9 %collective-permute-start.13 = (f32[208,128]{1,0:T(8,128)S(1)}, f32[208,128]{1,0:T(8,128)S(1)}, u32[]{:S(2)}, u32[]{:S(2)}) collective-permute-start(f32[208,128]{1,0:T(8,128)S(1)} %get-tuple-element.41), channel_id=1, source_target_pairs={{0,4},{1,5},{2,6},{3,7},{4,0},{5,1},{6,2},{7,3},{8,12},{9,13},{10,... | collective-permute-start | bytes 319496 | tf_op jit(solution)/shard_map/ppermute | solution.py:546
  41.2 5.7 %collective-permute-start.14 = (f32[208,128]{1,0:T(8,128)S(1)}, f32[208,128]{1,0:T(8,128)S(1)}, u32[]{:S(2)}, u32[]{:S(2)}) collective-permute-start(f32[208,128]{1,0:T(8,128)S(1)} %get-tuple-element.42), channel_id=1, source_target_pairs={{0,6},{1,7},{2,4},{3,5},{4,2},{5,3},{6,0},{7,1},{8,14},{9,15},{10,... | collective-permute-start | bytes 319496 | tf_op jit(solution)/shard_map/ppermute | solution.py:546
  46.9 5.8 %collective-permute-start.17 = (f32[8,128]{1,0:T(8,128)S(1)}, f32[8,128]{1,0:T(8,128)S(1)}, u32[]{:S(2)}, u32[]{:S(2)}) collective-permute-start(f32[8,128]{1,0:T(8,128)S(1)} %squares.1), channel_id=1, source_target_pairs={{0,24},{4,28},{8,16},{12,20},{16,8},{20,12},{24,0},{28,4},{1,25},{... | collective-permute-start | bytes 12296 | tf_op jit(solution)/shard_map/ppermute | solution.py:555
  49.9 4.5 %collective-permute-start.16 = (f32[8,128]{1,0:T(8,128)S(1)}, f32[8,128]{1,0:T(8,128)S(1)}, u32[]{:S(2)}, u32[]{:S(2)}) collective-permute-start(f32[8,128]{1,0:T(8,128)S(1)} %squares.1), channel_id=1, source_target_pairs={{0,16},{4,20},{8,24},{12,28},{16,0},{20,4},{24,8},{28,12},{1,17},{... | collective-permute-start | bytes 12296 | tf_op jit(solution)/shard_map/ppermute | solution.py:555
  49.9 4.5 %collective-permute-start.15 = (f32[8,128]{1,0:T(8,128)S(1)}, f32[8,128]{1,0:T(8,128)S(1)}, u32[]{:S(2)}, u32[]{:S(2)}) collective-permute-start(f32[8,128]{1,0:T(8,128)S(1)} %squares.1), channel_id=1, source_target_pairs={{0,8},{4,12},{8,0},{12,4},{16,24},{20,28},{24,16},{28,20},{1,9},{5... | collective-permute-start | bytes 12296 | tf_op jit(solution)/shard_map/ppermute | solution.py:555

commit v18 on v17

--- a/solution.py
+++ b/solution.py
@@ -287,45 +287,63 @@
     near_ref[...] = slab_ref[:, pl.ds(other * (SLAB - NEAR), NEAR)]
 
 
-def smooth_beyond(fine, inside, half_ref, v0):
-    f, r, w, ny = fine.f, fine.r, fine.w, fine.ny
+def beyond_kernel(slabs, chips_y, place_ref, scalar_ref, half_ref, out_ref, f, r, w, v0):
+    ny, slab = f.shape[1], place_ref[1]
+    x = place_ref[0] // 2 // chips_y
+    fine = Level(0, ny, LANES, 0, scalars_of(scalar_ref), f, r, w)
+    zero_rows(v0, ny)
     f[...], r[...] = half_ref[0], half_ref[1]
+    beside = jnp.where(x == 0, slab < slabs - 1, slab > 0)
+    inside = jnp.where(beside, DAMPING, 0.0)
 
     def put(at, weight):
         w[at] = weight
         v0[at, pl.ds(8, ny), :] = weight * f[at]
 
     sweep(range(HALO), lambda at: inside / (r[at] + fine.centre), put)
-    return [fine.smoothed(v0, 1 + n) for n in range(NEAR)]
+    for n in range(NEAR):
+        out_ref[n] = fine.smoothed(v0, 1 + n)
+
+
+def begin_kernel(scalar_ref, slab_ref, f, r, w, v0, v1):
+    ny = f.shape[1]
+    fine = Level(0, ny, LANES, 0, scalars_of(scalar_ref), f, r, w)
+    zero_rows(v0, ny)
+    zero_rows(v1, ny)
+    own = range(HALO, HALO + SLAB)
+    f[pl.ds(HALO, SLAB)], r[pl.ds(HALO, SLAB)] = slab_ref[0], slab_ref[1]
+
+    def put(at, weight):
+        w[at] = weight
+        v0[at, pl.ds(8, ny), :] = weight * f[at]
+
+    sweep(own, lambda at: DAMPING / (r[at] + fine.centre), put)
+    fine.smooth(v0, v1, own[1:-1])
 
 
 def pre_kernel(slabs, chips_y, place_ref, scalar_ref, *refs):
-    pool_ref, pool_up_ref, slab_ref, half_ref, near_ref = refs[:5]
-    f, r, w, v1, coarse_ref, beyond_ref, v0, tmp, pooled = refs[5:]
+    half_ref, near_ref, pool_ref, pool_up_ref = refs[5:9]
+    f, r, w, v0, v1, coarse_ref, beyond_ref, tmp, pooled = refs[9:]
     ny = f.shape[1]
     slab = place_ref[1]
     fine = Level(0, ny, LANES, 0, scalars_of(scalar_ref), f, r, w)
-    zero_rows(v0, ny)
-    zero_rows(v1, ny)
     after = HALO + SLAB
 
-    f[pl.ds(HALO, SLAB)], r[pl.ds(HALO, SLAB)] = slab_ref[0], slab_ref[1]
     x = place_ref[0] // 2 // chips_y
     for above, ref, first in ((1 - x, half_ref, x * NEAR), (x, near_ref, 0)):
         planes = pl.ds((HALO - NEAR) + above * (SLAB + NEAR), NEAR)
         f[planes], r[planes] = ref[0, pl.ds(first, NEAR)], ref[1, pl.ds(first, NEAR)]
 
-    inside = [jnp.where(slab > 0, DAMPING, 0.0)] * HALO
-    inside += [DAMPING] * SLAB
-    inside += [jnp.where(slab < slabs - 1, DAMPING, 0.0)] * HALO
-
-    def put(x, weight):
-        w[x] = weight
-        v0[x, pl.ds(8, ny), :] = weight * f[x]
-
-    known = range(HALO - NEAR, after + NEAR)
-    sweep(known, lambda x: inside[x] / (r[x] + fine.centre), put)
-    fine.smooth(v0, v1, known[1:-1])
+    below = jnp.where(slab > 0, DAMPING, 0.0)
+    above = jnp.where(slab < slabs - 1, DAMPING, 0.0)
+
+    def put(at, weight):
+        w[at] = weight
+        v0[at, pl.ds(8, ny), :] = weight * f[at]
+
+    beside = [*range(HALO - NEAR, HALO), *range(after, after + NEAR)]
+    sweep(beside, lambda at: (below if at < HALO else above) / (r[at] + fine.centre), put)
+    fine.smooth(v0, v1, (HALO - 1, HALO, after - 1, after))
     half = ny // 2
 
     def coarsened(x):
@@ -408,23 +426,16 @@
     out_ref[...] = split_dot(values, spread)
 
 
-def post_kernel(slabs, by, chips_y, place_ref, scalar_ref, *refs):
-    f, r, w, v1, correction, half_ref, beyond_ref = refs[:7]
-    kept_ref, sent_ref, va, vb, tmp, f_side, r_side, w_side, v_side = refs[7:]
+def post_kernel(by, chips_y, place_ref, scalar_ref, *refs):
+    f, r, w, v1, correction, first_ref, second_ref, kept_ref, sent_ref, va, vb, tmp = refs
     count, ny = f.shape[:2]
     fine = Level(0, ny, LANES, 0, scalars_of(scalar_ref), f, r, w)
     for v in (va, vb):
         zero_rows(v, ny)
     x, half = place_ref[0] // 2 // chips_y, ny // 2
     window = correction.shape[0] // half
-    side = Level(0, ny, LANES, 0, scalars_of(scalar_ref), f_side, r_side, w_side)
-    zero_rows(v_side, ny)
-    slab = place_ref[1]
-    beside = jnp.where(x == 0, slab < slabs - 1, slab > 0)
-    planes = smooth_beyond(side, jnp.where(beside, DAMPING, 0.0), half_ref, v_side)
-    for n in range(NEAR):
-        va[1 + (1 - x) * (SLAB + HALO) + n, pl.ds(8, ny), :] = planes[n]
-        va[1 + x * (SLAB + HALO) + n, pl.ds(8, ny), :] = beyond_ref[n]
+    for ref, above in ((first_ref, 1 - x), (second_ref, x)):
+        va[pl.ds(1 + above * (SLAB + HALO), NEAR), pl.ds(8, ny), :] = ref[...]
 
     def refined(x):
         return fine.spread_rows(correction[pl.ds(x * half, half), :], tmp.at[x])
@@ -526,13 +537,14 @@
 VMEM = pl.BlockSpec(memory_space=pltpu.VMEM)
 
 
-def local_kernel(kernel, name, scalars, arrays, outs, scratch=()):
+def local_kernel(kernel, name, scalars, arrays, outs, scratch=(), in_place=0):
     return pl.pallas_call(
         kernel,
         out_shape=[jax.ShapeDtypeStruct(shape, jnp.float32) for shape in outs],
         in_specs=[SMEM] * len(scalars) + [VMEM] * len(arrays),
         out_specs=[VMEM] * len(outs),
         scratch_shapes=[pltpu.VMEM(shape, jnp.float32) for shape in scratch],
+        input_output_aliases={len(scalars) + n: n for n in range(in_place)},
         compiler_params=pltpu.CompilerParams(vmem_limit_bytes=VMEM_LIMIT),
         name=name,
     )(*scalars, *arrays)
@@ -604,13 +616,24 @@
 
     beside = [send_beside(own_half, 1), send_beside(near, 0)]
     grid, rimmed = (count, ny, nz), (count, ny + 16, nz)
-    f, r, w, v1, coarse, beyond = local_kernel(
+    fields = [grid, grid, grid, rimmed, rimmed]
+    fields_own = local_kernel(begin_kernel, "begin", (scalar_rows,), (slab,), fields)
+    f, r, w, _, v1, coarse, beyond = local_kernel(
         functools.partial(pre_kernel, slabs, chips_y),
         "pre",
         scalars,
-        (pool_matrix(0), pool_matrix(LANES // 2), slab, *beside),
-        [grid, grid, grid, rimmed, (SLAB // 2, ny // 2, nz), (NEAR, ny, nz)],
-        [rimmed, (SLAB, ny, nz), (2, SLAB // 2 * ny // 2, nz)],
+        (*fields_own, *beside, pool_matrix(0), pool_matrix(LANES // 2)),
+        fields + [(SLAB // 2, ny // 2, nz), (NEAR, ny, nz)],
+        [(SLAB, ny, nz), (2, SLAB // 2 * ny // 2, nz)],
+        in_place=len(fields),
+    )
+    (own_beyond,) = local_kernel(
+        functools.partial(beyond_kernel, slabs, chips_y),
+        "beyond",
+        scalars,
+        beside[:1],
+        [(NEAR, ny, nz)],
+        [(HALO, ny, nz)] * 3 + [(HALO, ny + 16, nz)],
     )
     gathered = swap_slabs(coarse, step, slabs)
 
@@ -627,12 +650,12 @@
     )
     result = (SLAB * ny + 8, nz)
     kept, sent = local_kernel(
-        functools.partial(post_kernel, slabs, by, chips_y),
+        functools.partial(post_kernel, by, chips_y),
         "post",
         scalars,
-        (f, r, w, v1, correction, beside[0], send_beside(beyond, 0)),
+        (f, r, w, v1, correction, own_beyond, send_beside(beyond, 0)),
         [result, result],
-        [rimmed] * 2 + [(SLAB, ny, nz)] + [(HALO, ny, nz)] * 3 + [(HALO, ny + 16, nz)],
+        [rimmed] * 2 + [(SLAB, ny, nz)],
     )
 
     parts = local_kernel(

time: 55.5 us -> 56.8 us (1.023)
  Pallas kernels: 9.56 us -> 10.9 us
    pallas_call x10 -> x12, Pallas kernels: 9.56 us -> 10.9 us  [local_kernel(): pl.pallas_call(kernel, out_shape=[jax.ShapeDtypeStruct(shape, jnp.float32...]
    ppermute x6, waiting for transfers between devices: 2.93 us -> 4.19 us  [swap_slabs(): moved.append(lax.ppermute(piece, 'gx', pairs))]
    ppermute x3, waiting for transfers between devices: 2.37 us -> 1.55 us  [send_beside(): lax.ppermute(piece, 'gx', [(i, j) for i, j in pairs if 0 <= j < gx_size])]
  transfers between devices with their start and end apart: 18 -> 18, of which waited for: 10 -> 11; matrix products, arithmetic and copies ran while one was open for 0% -> 0% of each run, Pallas kernels for 10% -> 12%
where the time goes in v18:
time: 56.8 us; the launch traced here: 56.5 us
  starting transfers between devices  26 us (46%)
  waiting for transfers between devices  16.6 us (29%)
  Pallas kernels  10.9 us (19%)
  local copies, waits for them, and re-layouts  1.13 us (2%)
  other arithmetic  1.04 us (2%)
  between operations  0.81 us (1%)
    pallas_call x12, Pallas kernels, local_kernel(): pl.pallas_call(kernel, out_shape=[jax.ShapeDtypeStruct(shape, jnp.float32...  10.9 us
    ppermute x6, starting transfers between devices, swap_slabs(): moved.append(lax.ppermute(piece, 'gx', pairs))  9.49 us
    ppermute x6, waiting for transfers between devices, swap_in_plane(): moved.append(lax.ppermute(pieces[k], ('gx', 'gy'), pairs))  9.35 us
    ppermute x6, starting transfers between devices, swap_in_plane(): moved.append(lax.ppermute(pieces[k], ('gx', 'gy'), pairs))  8.1 us
    ppermute x3, starting transfers between devices, send_beside(): lax.ppermute(piece, 'gx', [(i, j) for i, j in pairs if 0 <= j < gx_size])  7.74 us
    ppermute x6, waiting for transfers between devices, swap_slabs(): moved.append(lax.ppermute(piece, 'gx', pairs))  4.19 us
    ppermute x3, waiting for transfers between devices, send_beside(): lax.ppermute(piece, 'gx', [(i, j) for i, j in pairs if 0 <= j < gx_size])  1.55 us
    ppermute x1, waiting for transfers between devices, column_body(): lax.ppermute(sent, 'gy', cores)  1.53 us
  transfers between devices with their start and end apart: 18, of which 11 were waited for; matrix products, arithmetic and copies ran while one was open for 0% of the time, Pallas kernels for 12%

profile of v18, /device:TPU:0, one launch (start us, length us, event | category | flops | bytes accessed | tf_op | source)
XLA Modules:
  0.0 56.5 jit_solution(14820166778062285265)
XLA Ops:
  3.6 3.0 %collective-permute-start.2 = (f32[2,4,32,128]{3,2,1,0:T(8,128)S(1)}, f32[2,4,32,128]{3,2,1,0:T(8,128)S(1)}, u32[]{:S(2)}, u32[]{:S(2)}) collective-permute-start(f32[2,4,32,128]{3,2,1,0:T(8,128)S(1)} %get-tuple-element.31), channel_id=1, source_target_pairs={{0,2},{1,3},{2,0},{3,1},{4,6},{5,7},{6,4},{7,5},{8,10},{9,11},{10,... | collective-permute-start | bytes 393224 | tf_op jit(solution)/shard_map/ppermute | solution.py:558
  6.6 1.5 %collective-permute-start.3 = (f32[2,4,32,128]{3,2,1,0:T(8,128)S(1)}, f32[2,4,32,128]{3,2,1,0:T(8,128)S(1)}, u32[]{:S(2)}, u32[]{:S(2)}) collective-permute-start(f32[2,4,32,128]{3,2,1,0:T(8,128)S(1)} %get-tuple-element.32), channel_id=1, source_target_pairs={{0,4},{1,5},{2,6},{3,7},{4,0},{5,1},{6,2},{7,3},{8,12},{9,13},{10,... | collective-permute-start | bytes 393224 | tf_op jit(solution)/shard_map/ppermute | solution.py:558
  8.2 2.2 %collective-permute-done.2.refs_1_ = f32[2,4,32,128]{3,2,1,0:T(8,128)S(1)} collective-permute-done((f32[2,4,32,128]{3,2,1,0:T(8,128)S(1)}, f32[2,4,32,128]{3,2,1,0:T(8,128)S(1)}, u32[]{:S(2)}, u32[]{:S(2)}) %collective-permute-start.2) | collective-permute-done | bytes 131104 | tf_op jit(solution)/shard_map/ppermute | solution.py:558
  11.0 1.3 %collective-permute-start.5 = (f32[2,4,64,128]{3,2,1,0:T(8,128)S(1)}, f32[2,4,64,128]{3,2,1,0:T(8,128)S(1)}, u32[]{:S(2)}, u32[]{:S(2)}) collective-permute-start(f32[2,4,64,128]{3,2,1,0:T(8,128)S(1)} %half.1), channel_id=1, source_target_pairs={{4,12},{8,0},{12,20},{16,8},{20,28},{24,16},{5,13},{9,1},{13,21},{... | collective-permute-start | bytes 786440 | tf_op jit(solution)/shard_map/ppermute | solution.py:615
  13.0 1.4 %collective-permute-done.4.refs_3_ = f32[2,4,32,128]{3,2,1,0:T(8,128)S(1)} collective-permute-done((f32[2,4,32,128]{3,2,1,0:T(8,128)S(1)}, f32[2,4,32,128]{3,2,1,0:T(8,128)S(1)}, u32[]{:S(2)}, u32[]{:S(2)}) %collective-permute-start.4) | collective-permute-done | bytes 131104 | tf_op jit(solution)/shard_map/ppermute | solution.py:558
  15.1 3.6 %collective-permute-start.6 = (f32[2,2,64,128]{3,2,1,0:T(8,128)S(1)}, f32[2,2,64,128]{3,2,1,0:T(8,128)S(1)}, u32[]{:S(2)}, u32[]{:S(2)}) collective-permute-start(f32[2,2,64,128]{3,2,1,0:T(8,128)S(1)} %get-tuple-element.40), channel_id=1, source_target_pairs={{0,8},{8,16},{12,4},{16,24},{20,12},{28,20},{1,9},{9,17},{13,5},{1... | collective-permute-start | bytes 393224 | tf_op jit(solution)/shard_map/ppermute | solution.py:615
  19.6 1.5 %collective-permute-done.6.refs_6_ = f32[2,2,64,128]{3,2,1,0:T(8,128)S(1)} collective-permute-done((f32[2,2,64,128]{3,2,1,0:T(8,128)S(1)}, f32[2,2,64,128]{3,2,1,0:T(8,128)S(1)}, u32[]{:S(2)}, u32[]{:S(2)}) %collective-permute-start.6) | collective-permute-done | bytes 131104 | tf_op jit(solution)/shard_map/ppermute | solution.py:615
  21.2 1.1 %pre.1 = (f32[16,64,128]{2,1,0:T(8,128)S(1)}, f32[16,64,128]{2,1,0:T(8,128)S(1)}, f32[16,64,128]{2,1,0:T(8,128)S(1)}, f32[16,80,128]{2,1,0:T(8,128)S(1)}, f32[16...) custom-call(s32[2]{0:T(128)S(1)} %pad_add_fusion.place_ref, ...), custom_call_target="tpu_custom_call", output_to_operand_aliasing={{0}: (2, {}), {1}: (3, {}), {2}: (4, {}), {3}: (5, {}), {4}... | custom-call | tf_op jit(solution)/shard_map/pre/pallas_call | solution.py:541
  22.3 2.5 %collective-permute-start.7 = (f32[4,32,128]{2,1,0:T(8,128)S(1)}, f32[4,32,128]{2,1,0:T(8,128)S(1)}, u32[]{:S(2)}, u32[]{:S(2)}) collective-permute-start(f32[4,32,128]{2,1,0:T(8,128)S(1)} %get-tuple-element.45.refs_2_), channel_id=1, source_target_pairs={{0,8},{4,12},{8,0},{12,4},{16,24},{20,28},{24,16},{28,20},{1,9},{5... | collective-permute-start | bytes 196616 | tf_op jit(solution)/shard_map/ppermute | solution.py:567
  24.8 2.6 %collective-permute-start.8 = (f32[4,32,128]{2,1,0:T(8,128)S(1)}, f32[4,32,128]{2,1,0:T(8,128)S(1)}, u32[]{:S(2)}, u32[]{:S(2)}) collective-permute-start(f32[4,32,128]{2,1,0:T(8,128)S(1)} %get-tuple-element.45.refs_2_), channel_id=1, source_target_pairs={{0,16},{4,20},{8,24},{12,28},{16,0},{20,4},{24,8},{28,12},{1,17},{... | collective-permute-start | bytes 196616 | tf_op jit(solution)/shard_map/ppermute | solution.py:567
  27.4 2.8 %collective-permute-start.10 = (f32[2,64,128]{2,1,0:T(8,128)S(1)}, f32[2,64,128]{2,1,0:T(8,128)S(1)}, u32[]{:S(2)}, u32[]{:S(2)}) collective-permute-start(f32[2,64,128]{2,1,0:T(8,128)S(1)} %get-tuple-element.46), channel_id=1, source_target_pairs={{0,8},{8,16},{12,4},{16,24},{20,12},{28,20},{1,9},{9,17},{13,5},{1... | collective-permute-start | bytes 196616 | tf_op jit(solution)/shard_map/ppermute | solution.py:615
  31.4 2.1 %collective-permute-done.9.refs_5_ = f32[4,32,128]{2,1,0:T(8,128)S(1)} collective-permute-done((f32[4,32,128]{2,1,0:T(8,128)S(1)}, f32[4,32,128]{2,1,0:T(8,128)S(1)}, u32[]{:S(2)}, u32[]{:S(2)}) %collective-permute-start.9) | collective-permute-done | bytes 65568 | tf_op jit(solution)/shard_map/ppermute | solution.py:567
  33.5 2.3 %coarse.1.refs_4_ = f32[256,128]{1,0:T(8,128)S(1)} custom-call(s32[2]{0:T(128)S(1)} %pad_add_fusion.place_ref, f32[8,128]{1,0:T(8,128)S(1)} %get-tuple-element.29.scalar_ref, bf16[128,128]{1,0:T(8,128)(2,1)S(1)} %get-tuple-element.56.refs_7_.refs_0_, bf16[128,128]{1,0:T(8,128)(2,1)S(1)} %get-tuple-element.55.refs_1_, ...), custom_call_target="tpu_custom_call" | custom-call | tf_op jit(solution)/shard_map/coarse/pallas_call | solution.py:541
  35.8 1.5 %post.1 = (f32[520,128]{1,0:T(8,128)S(1)}, f32[520,128]{1,0:T(8,128)S(1)}) custom-call(s32[2]{0:T(128)S(1)} %pad_add_fusion.place_ref, f32[8,128]{1,0:T(8,128)S(1)} %get-tuple-element.29.scalar_ref, f32[16,64,128]{2,1,0:T(8,128)S(1)} %get-tuple-element.41.refs_0_, f32[16,64,128]{2,1,0:T(8,128)S(1)} %get-tuple-element.42.refs_1_, ...), custom_call_target="tpu_custom_call" | custom-call | tf_op jit(solution)/shard_map/post/pallas_call | solution.py:541
  37.4 1.5 %collective-permute-done.11.got_ref = f32[520,128]{1,0:T(8,128)S(1)} collective-permute-done((f32[520,128]{1,0:T(8,128)S(1)}, f32[520,128]{1,0:T(8,128)S(1)}, u32[]{:S(2)}, u32[]{:S(2)}) %collective-permute-start.11) | collective-permute-done | bytes 266272 | tf_op jit(solution)/shard_map/ppermute | solution.py:665
  39.6 1.6 %collective-permute-start.12 = (f32[208,128]{1,0:T(8,128)S(1)}, f32[208,128]{1,0:T(8,128)S(1)}, u32[]{:S(2)}, u32[]{:S(2)}) collective-permute-start(f32[208,128]{1,0:T(8,128)S(1)} %get-tuple-element.50), channel_id=1, source_target_pairs={{0,2},{1,3},{2,0},{3,1},{4,6},{5,7},{6,4},{7,5},{8,10},{9,11},{10,... | collective-permute-start | bytes 319496 | tf_op jit(solution)/shard_map/ppermute | solution.py:558
  41.4 1.7 %collective-permute-start.14 = (f32[208,128]{1,0:T(8,128)S(1)}, f32[208,128]{1,0:T(8,128)S(1)}, u32[]{:S(2)}, u32[]{:S(2)}) collective-permute-start(f32[208,128]{1,0:T(8,128)S(1)} %get-tuple-element.52), channel_id=1, source_target_pairs={{0,6},{1,7},{2,4},{3,5},{4,2},{5,3},{6,0},{7,1},{8,14},{9,15},{10,... | collective-permute-start | bytes 319496 | tf_op jit(solution)/shard_map/ppermute | solution.py:558
  43.1 1.5 %collective-permute-done.12.refs_1_ = f32[208,128]{1,0:T(8,128)S(1)} collective-permute-done((f32[208,128]{1,0:T(8,128)S(1)}, f32[208,128]{1,0:T(8,128)S(1)}, u32[]{:S(2)}, u32[]{:S(2)}) %collective-permute-start.12) | collective-permute-done | bytes 106528 | tf_op jit(solution)/shard_map/ppermute | solution.py:558
  44.7 2.4 %collective-permute-done.13.refs_2_ = f32[208,128]{1,0:T(8,128)S(1)} collective-permute-done((f32[208,128]{1,0:T(8,128)S(1)}, f32[208,128]{1,0:T(8,128)S(1)}, u32[]{:S(2)}, u32[]{:S(2)}) %collective-permute-start.13) | collective-permute-done | bytes 106528 | tf_op jit(solution)/shard_map/ppermute | solution.py:558
  47.0 1.1 %collective-permute-done.14.refs_3_ = f32[208,128]{1,0:T(8,128)S(1)} collective-permute-done((f32[208,128]{1,0:T(8,128)S(1)}, f32[208,128]{1,0:T(8,128)S(1)}, u32[]{:S(2)}, u32[]{:S(2)}) %collective-permute-start.14) | collective-permute-done | bytes 106528 | tf_op jit(solution)/shard_map/ppermute | solution.py:558
  48.3 2.0 %collective-permute-start.16 = (f32[8,128]{1,0:T(8,128)S(1)}, f32[8,128]{1,0:T(8,128)S(1)}, u32[]{:S(2)}, u32[]{:S(2)}) collective-permute-start(f32[8,128]{1,0:T(8,128)S(1)} %squares.1), channel_id=1, source_target_pairs={{0,16},{4,20},{8,24},{12,28},{16,0},{20,4},{24,8},{28,12},{1,17},{... | collective-permute-start | bytes 12296 | tf_op jit(solution)/shard_map/ppermute | solution.py:567
  50.2 2.3 %collective-permute-start.17 = (f32[8,128]{1,0:T(8,128)S(1)}, f32[8,128]{1,0:T(8,128)S(1)}, u32[]{:S(2)}, u32[]{:S(2)}) collective-permute-start(f32[8,128]{1,0:T(8,128)S(1)} %squares.1), channel_id=1, source_target_pairs={{0,24},{4,28},{8,16},{12,20},{16,8},{20,12},{24,0},{28,4},{1,25},{... | collective-permute-start | bytes 12296 | tf_op jit(solution)/shard_map/ppermute | solution.py:567
  52.5 1.4 %collect.1 = (f32[8,4,16,128]{3,2,1,0:T(8,128)}, f32[8,4,16,128]{3,2,1,0:T(8,128)}) custom-call(s32[2]{0:T(128)S(1)} %pad_add_fusion.place_ref, f32[8]{0:T(128)S(1)} %copy-done.3, s32[8]{0:T(128)S(1)} %copy-done.4, f32[3]{0:T(128)S(1)} %copy-done.5, f32[8,4,16,128]{3,2,1,0:T(8,128)S(1)} %copy-done.1, f32[4,16,128]{2,1,0:T(8,128)S(1)} %copy-done.2, ...), custom_call_target="tpu_custom_call" | custom-call | tf_op jit(solution)/shard_map/collect/pallas_call | solution.py:541
  54.0 1.7 %collective-permute-done.17 = f32[8,128]{1,0:T(8,128)S(1)} collective-permute-done((f32[8,128]{1,0:T(8,128)S(1)}, f32[8,128]{1,0:T(8,128)S(1)}, u32[]{:S(2)}, u32[]{:S(2)}) %collective-permute-start.17) | collective-permute-done | bytes 4128 | tf_op jit(solution)/shard_map/ppermute | solution.py:567
  (44 shorter events, 8.9 us)
Async XLA Ops:
  0.6 2.2 %collective-permute-start = (f32[8,4,16,128]{3,2,1,0:T(8,128)}, f32[8,4,16,128]{3,2,1,0:T(8,128)S(1)}, u32[]{:S(2)}, u32[]{:S(2)}) collective-permute-start(f32[8,4,16,128]{3,2,1,0:T(8,128)} %source_ref.3), channel_id=1, source_target_pairs={{0,1},{1,0},{2,3},{3,2},{4,5},{5,4},{6,7},{7,6},{8,9},{9,8},{10,11... | collective-permute-start | bytes 786440 | tf_op jit(solution)/shard_map/ppermute | solution.py:585
  1.1 1.7 %collective-permute-start.1 = (f32[4,16,128]{2,1,0:T(8,128)}, f32[4,16,128]{2,1,0:T(8,128)S(1)}, u32[]{:S(2)}, u32[]{:S(2)}) collective-permute-start(f32[4,16,128]{2,1,0:T(8,128)} %reaction_ref.1), channel_id=1, source_target_pairs={{0,1},{1,0},{2,3},{3,2},{4,5},{5,4},{6,7},{7,6},{8,9},{9,8},{10,11... | collective-permute-start | bytes 98312 | tf_op jit(solution)/shard_map/ppermute | solution.py:585
  1.3 0.9 %copy-start = (f32[8,4,16,128]{3,2,1,0:T(8,128)S(1)}, f32[8,4,16,128]{3,2,1,0:T(8,128)}, u32[]{:S(2)}) copy-start(f32[8,4,16,128]{3,2,1,0:T(8,128)} %source_ref.3) | copy-start | bytes 786436
  2.3 0.8 %copy-start.2 = (f32[4,16,128]{2,1,0:T(8,128)S(1)}, f32[4,16,128]{2,1,0:T(8,128)}, u32[]{:S(2)}) copy-start(f32[4,16,128]{2,1,0:T(8,128)} %reaction_ref.1) | copy-start | bytes 98308
  2.3 0.8 %copy-start.3 = (f32[8]{0:T(128)S(1)}, f32[8]{0:T(128)}, u32[]{:S(2)}) copy-start(f32[8]{0:T(128)} %shifts_ref.3) | copy-start | bytes 100
  2.3 0.8 %copy-start.4 = (s32[8]{0:T(128)S(1)}, s32[8]{0:T(128)}, u32[]{:S(2)}) copy-start(s32[8]{0:T(128)} %index_ref.3) | copy-start | bytes 100
  2.3 0.8 %copy-start.5 = (f32[3]{0:T(128)S(1)}, f32[3]{0:T(128)}, u32[]{:S(2)}) copy-start(f32[3]{0:T(128)} %velocity_ref.3) | copy-start | bytes 40
  3.6 6.8 %collective-permute-start.2 = (f32[2,4,32,128]{3,2,1,0:T(8,128)S(1)}, f32[2,4,32,128]{3,2,1,0:T(8,128)S(1)}, u32[]{:S(2)}, u32[]{:S(2)}) collective-permute-start(f32[2,4,32,128]{3,2,1,0:T(8,128)S(1)} %get-tuple-element.31), channel_id=1, source_target_pairs={{0,2},{1,3},{2,0},{3,1},{4,6},{5,7},{6,4},{7,5},{8,10},{9,11},{10,... | collective-permute-start | bytes 393224 | tf_op jit(solution)/shard_map/ppermute | solution.py:558
  6.6 6.4 %collective-permute-start.3 = (f32[2,4,32,128]{3,2,1,0:T(8,128)S(1)}, f32[2,4,32,128]{3,2,1,0:T(8,128)S(1)}, u32[]{:S(2)}, u32[]{:S(2)}) collective-permute-start(f32[2,4,32,128]{3,2,1,0:T(8,128)S(1)} %get-tuple-element.32), channel_id=1, source_target_pairs={{0,4},{1,5},{2,6},{3,7},{4,0},{5,1},{6,2},{7,3},{8,12},{9,13},{10,... | collective-permute-start | bytes 393224 | tf_op jit(solution)/shard_map/ppermute | solution.py:558
  8.1 6.3 %collective-permute-start.4 = (f32[2,4,32,128]{3,2,1,0:T(8,128)S(1)}, f32[2,4,32,128]{3,2,1,0:T(8,128)S(1)}, u32[]{:S(2)}, u32[]{:S(2)}) collective-permute-start(f32[2,4,32,128]{3,2,1,0:T(8,128)S(1)} %get-tuple-element.33), channel_id=1, source_target_pairs={{0,6},{1,7},{2,4},{3,5},{4,2},{5,3},{6,0},{7,1},{8,14},{9,15},{10,... | collective-permute-start | bytes 393224 | tf_op jit(solution)/shard_map/ppermute | solution.py:558
  11.0 10.2 %collective-permute-start.5 = (f32[2,4,64,128]{3,2,1,0:T(8,128)S(1)}, f32[2,4,64,128]{3,2,1,0:T(8,128)S(1)}, u32[]{:S(2)}, u32[]{:S(2)}) collective-permute-start(f32[2,4,64,128]{3,2,1,0:T(8,128)S(1)} %half.1), channel_id=1, source_target_pairs={{4,12},{8,0},{12,20},{16,8},{20,28},{24,16},{5,13},{9,1},{13,21},{... | collective-permute-start | bytes 786440 | tf_op jit(solution)/shard_map/ppermute | solution.py:615
  15.1 6.1 %collective-permute-start.6 = (f32[2,2,64,128]{3,2,1,0:T(8,128)S(1)}, f32[2,2,64,128]{3,2,1,0:T(8,128)S(1)}, u32[]{:S(2)}, u32[]{:S(2)}) collective-permute-start(f32[2,2,64,128]{3,2,1,0:T(8,128)S(1)} %get-tuple-element.40), channel_id=1, source_target_pairs={{0,8},{8,16},{12,4},{16,24},{20,12},{28,20},{1,9},{9,17},{13,5},{1... | collective-permute-start | bytes 393224 | tf_op jit(solution)/shard_map/ppermute | solution.py:615
  22.3 8.7 %collective-permute-start.7 = (f32[4,32,128]{2,1,0:T(8,128)S(1)}, f32[4,32,128]{2,1,0:T(8,128)S(1)}, u32[]{:S(2)}, u32[]{:S(2)}) collective-permute-start(f32[4,32,128]{2,1,0:T(8,128)S(1)} %get-tuple-element.45.refs_2_), channel_id=1, source_target_pairs={{0,8},{4,12},{8,0},{12,4},{16,24},{20,28},{24,16},{28,20},{1,9},{5... | collective-permute-start | bytes 196616 | tf_op jit(solution)/shard_map/ppermute | solution.py:567
  24.8 6.6 %collective-permute-start.8 = (f32[4,32,128]{2,1,0:T(8,128)S(1)}, f32[4,32,128]{2,1,0:T(8,128)S(1)}, u32[]{:S(2)}, u32[]{:S(2)}) collective-permute-start(f32[4,32,128]{2,1,0:T(8,128)S(1)} %get-tuple-element.45.refs_2_), channel_id=1, source_target_pairs={{0,16},{4,20},{8,24},{12,28},{16,0},{20,4},{24,8},{28,12},{1,17},{... | collective-permute-start | bytes 196616 | tf_op jit(solution)/shard_map/ppermute | solution.py:567
  27.4 6.1 %collective-permute-start.9 = (f32[4,32,128]{2,1,0:T(8,128)S(1)}, f32[4,32,128]{2,1,0:T(8,128)S(1)}, u32[]{:S(2)}, u32[]{:S(2)}) collective-permute-start(f32[4,32,128]{2,1,0:T(8,128)S(1)} %get-tuple-element.45.refs_2_), channel_id=1, source_target_pairs={{0,24},{4,28},{8,16},{12,20},{16,8},{20,12},{24,0},{28,4},{1,25},{... | collective-permute-start | bytes 196616 | tf_op jit(solution)/shard_map/ppermute | solution.py:567
  27.4 8.4 %collective-permute-start.10 = (f32[2,64,128]{2,1,0:T(8,128)S(1)}, f32[2,64,128]{2,1,0:T(8,128)S(1)}, u32[]{:S(2)}, u32[]{:S(2)}) collective-permute-start(f32[2,64,128]{2,1,0:T(8,128)S(1)} %get-tuple-element.46), channel_id=1, source_target_pairs={{0,8},{8,16},{12,4},{16,24},{20,12},{28,20},{1,9},{9,17},{13,5},{1... | collective-permute-start | bytes 196616 | tf_op jit(solution)/shard_map/ppermute | solution.py:615
  37.4 1.6 %collective-permute-start.11 = (f32[520,128]{1,0:T(8,128)S(1)}, f32[520,128]{1,0:T(8,128)S(1)}, u32[]{:S(2)}, u32[]{:S(2)}) collective-permute-start(f32[520,128]{1,0:T(8,128)S(1)} %get-tuple-element.48), channel_id=1, source_target_pairs={{0,1},{1,0},{2,3},{3,2},{4,5},{5,4},{6,7},{7,6},{8,9},{9,8},{10,11... | collective-permute-start | bytes 798728 | tf_op jit(solution)/shard_map/ppermute | solution.py:665
  39.6 13.0 %copy-start.1 = (f32[8,4,16,128]{3,2,1,0:T(8,128)S(1)}, f32[8,4,16,128]{3,2,1,0:T(8,128)}, u32[]{:S(2)}) copy-start(f32[8,4,16,128]{3,2,1,0:T(8,128)} %source_ref.3) | copy-start | bytes 786436
  39.6 5.1 %collective-permute-start.12 = (f32[208,128]{1,0:T(8,128)S(1)}, f32[208,128]{1,0:T(8,128)S(1)}, u32[]{:S(2)}, u32[]{:S(2)}) collective-permute-start(f32[208,128]{1,0:T(8,128)S(1)} %get-tuple-element.50), channel_id=1, source_target_pairs={{0,2},{1,3},{2,0},{3,1},{4,6},{5,7},{6,4},{7,5},{8,10},{9,11},{10,... | collective-permute-start | bytes 319496 | tf_op jit(solution)/shard_map/ppermute | solution.py:558
  41.2 5.9 %collective-permute-start.13 = (f32[208,128]{1,0:T(8,128)S(1)}, f32[208,128]{1,0:T(8,128)S(1)}, u32[]{:S(2)}, u32[]{:S(2)}) collective-permute-start(f32[208,128]{1,0:T(8,128)S(1)} %get-tuple-element.51), channel_id=1, source_target_pairs={{0,4},{1,5},{2,6},{3,7},{4,0},{5,1},{6,2},{7,3},{8,12},{9,13},{10,... | collective-permute-start | bytes 319496 | tf_op jit(solution)/shard_map/ppermute | solution.py:558
  41.4 6.7 %collective-permute-start.14 = (f32[208,128]{1,0:T(8,128)S(1)}, f32[208,128]{1,0:T(8,128)S(1)}, u32[]{:S(2)}, u32[]{:S(2)}) collective-permute-start(f32[208,128]{1,0:T(8,128)S(1)} %get-tuple-element.52), channel_id=1, source_target_pairs={{0,6},{1,7},{2,4},{3,5},{4,2},{5,3},{6,0},{7,1},{8,14},{9,15},{10,... | collective-permute-start | bytes 319496 | tf_op jit(solution)/shard_map/ppermute | solution.py:558
  48.1 5.8 %collective-permute-start.15 = (f32[8,128]{1,0:T(8,128)S(1)}, f32[8,128]{1,0:T(8,128)S(1)}, u32[]{:S(2)}, u32[]{:S(2)}) collective-permute-start(f32[8,128]{1,0:T(8,128)S(1)} %squares.1), channel_id=1, source_target_pairs={{0,8},{4,12},{8,0},{12,4},{16,24},{20,28},{24,16},{28,20},{1,9},{5... | collective-permute-start | bytes 12296 | tf_op jit(solution)/shard_map/ppermute | solution.py:567
  48.3 5.7 %collective-permute-start.16 = (f32[8,128]{1,0:T(8,128)S(1)}, f32[8,128]{1,0:T(8,128)S(1)}, u32[]{:S(2)}, u32[]{:S(2)}) collective-permute-start(f32[8,128]{1,0:T(8,128)S(1)} %squares.1), channel_id=1, source_target_pairs={{0,16},{4,20},{8,24},{12,28},{16,0},{20,4},{24,8},{28,12},{1,17},{... | collective-permute-start | bytes 12296 | tf_op jit(solution)/shard_map/ppermute | solution.py:567
  50.2 5.4 %collective-permute-start.17 = (f32[8,128]{1,0:T(8,128)S(1)}, f32[8,128]{1,0:T(8,128)S(1)}, u32[]{:S(2)}, u32[]{:S(2)}) collective-permute-start(f32[8,128]{1,0:T(8,128)S(1)} %squares.1), channel_id=1, source_target_pairs={{0,24},{4,28},{8,16},{12,20},{16,8},{20,12},{24,0},{28,4},{1,25},{... | collective-permute-start | bytes 12296 | tf_op jit(solution)/shard_map/ppermute | solution.py:567

commit v19 on v18

--- a/solution.py
+++ b/solution.py
@@ -242,6 +242,10 @@
     return jnp.where(col // 2 == row, 1.0, 0.0).astype(jnp.bfloat16)
 
 
+def step_of(k, count):
+    return -k % count
+
+
 def keep_kernel(place_ref, source_ref, out_ref):
     for n in range(out_ref.shape[0]):
         out_ref[n] = source_ref[2 * n + (place_ref[0] & 1)]
@@ -381,7 +385,7 @@
     lower = lax.broadcasted_iota(jnp.int32, (1, LANES), 1) < LANES // 2
     own = SLAB // 2
     for k in range(slabs):
-        first = jnp.bitwise_xor(slab, k) * own
+        first = jnp.bitwise_xor(slab, step_of(k, slabs)) * own
         both = coarse[k][...]
         f1[pl.ds(first, own)] = jnp.where(lower, both, 0.0)
         r1[pl.ds(first, own)] = jnp.where(lower, pltpu.roll(both, LANES // 2, 2), 0.0)
@@ -563,7 +567,7 @@
     size = lax.axis_size("gx")
     moved = [piece]
     for k in range(1, slabs):
-        pairs = [(i, i ^ (k * step)) for i in range(size)]
+        pairs = [(i, i ^ (step_of(k, slabs) * step)) for i in range(size)]
         moved.append(lax.ppermute(piece, "gx", pairs))
     return moved
 

time: 56.8 us -> 55.3 us (0.974)
  waiting for transfers between devices: 16.6 us -> 14.6 us
    ppermute x6, waiting for transfers between devices: 4.19 us -> 2.19 us  [swap_slabs(): moved.append(lax.ppermute(piece, 'gx', pairs))]
  transfers between devices with their start and end apart: 18 -> 18, of which waited for: 11 -> 10; matrix products, arithmetic and copies ran while one was open for 0% -> 0% of each run, Pallas kernels for 12% -> 13%
where the time goes in v19:
time: 55.3 us; the launch traced here: 55 us
  starting transfers between devices  26.5 us (48%)
  waiting for transfers between devices  14.6 us (26%)
  Pallas kernels  10.9 us (20%)
  local copies, waits for them, and re-layouts  1.13 us (2%)
  other arithmetic  1.04 us (2%)
  between operations  0.81 us (1%)
    pallas_call x12, Pallas kernels, local_kernel(): pl.pallas_call(kernel, out_shape=[jax.ShapeDtypeStruct(shape, jnp.float32...  10.9 us
    ppermute x6, starting transfers between devices, swap_slabs(): moved.append(lax.ppermute(piece, 'gx', pairs))  9.57 us
    ppermute x6, waiting for transfers between devices, swap_in_plane(): moved.append(lax.ppermute(pieces[k], ('gx', 'gy'), pairs))  9.35 us
    ppermute x3, starting transfers between devices, send_beside(): lax.ppermute(piece, 'gx', [(i, j) for i, j in pairs if 0 <= j < gx_size])  8.21 us
    ppermute x6, starting transfers between devices, swap_in_plane(): moved.append(lax.ppermute(pieces[k], ('gx', 'gy'), pairs))  8.1 us
    ppermute x6, waiting for transfers between devices, swap_slabs(): moved.append(lax.ppermute(piece, 'gx', pairs))  2.19 us
    ppermute x3, waiting for transfers between devices, send_beside(): lax.ppermute(piece, 'gx', [(i, j) for i, j in pairs if 0 <= j < gx_size])  1.55 us
    ppermute x1, waiting for transfers between devices, column_body(): lax.ppermute(sent, 'gy', cores)  1.53 us
  transfers between devices with their start and end apart: 18, of which 10 were waited for; matrix products, arithmetic and copies ran while one was open for 0% of the time, Pallas kernels for 13%

profile of v19, /device:TPU:0, one launch (start us, length us, event | category | flops | bytes accessed | tf_op | source)
XLA Modules:
  0.0 55.0 jit_solution(5835555430386756919)
XLA Ops:
  1.3 0.9 %copy-done = f32[8,4,16,128]{3,2,1,0:T(8,128)S(1)} copy-done((f32[8,4,16,128]{3,2,1,0:T(8,128)S(1)}, f32[8,4,16,128]{3,2,1,0:T(8,128)}, u32[]{:S(2)}) %copy-start) | copy-done | bytes 262168
  3.6 3.0 %collective-permute-start.2 = (f32[2,4,32,128]{3,2,1,0:T(8,128)S(1)}, f32[2,4,32,128]{3,2,1,0:T(8,128)S(1)}, u32[]{:S(2)}, u32[]{:S(2)}) collective-permute-start(f32[2,4,32,128]{3,2,1,0:T(8,128)S(1)} %get-tuple-element.31), channel_id=1, source_target_pairs={{0,2},{1,3},{2,0},{3,1},{4,6},{5,7},{6,4},{7,5},{8,10},{9,11},{10,... | collective-permute-start | bytes 393224 | tf_op jit(solution)/shard_map/ppermute | solution.py:562
  6.6 1.5 %collective-permute-start.3 = (f32[2,4,32,128]{3,2,1,0:T(8,128)S(1)}, f32[2,4,32,128]{3,2,1,0:T(8,128)S(1)}, u32[]{:S(2)}, u32[]{:S(2)}) collective-permute-start(f32[2,4,32,128]{3,2,1,0:T(8,128)S(1)} %get-tuple-element.32), channel_id=1, source_target_pairs={{0,4},{1,5},{2,6},{3,7},{4,0},{5,1},{6,2},{7,3},{8,12},{9,13},{10,... | collective-permute-start | bytes 393224 | tf_op jit(solution)/shard_map/ppermute | solution.py:562
  8.2 2.2 %collective-permute-done.2.refs_1_ = f32[2,4,32,128]{3,2,1,0:T(8,128)S(1)} collective-permute-done((f32[2,4,32,128]{3,2,1,0:T(8,128)S(1)}, f32[2,4,32,128]{3,2,1,0:T(8,128)S(1)}, u32[]{:S(2)}, u32[]{:S(2)}) %collective-permute-start.2) | collective-permute-done | bytes 131104 | tf_op jit(solution)/shard_map/ppermute | solution.py:562
  11.0 1.3 %collective-permute-start.5 = (f32[2,4,64,128]{3,2,1,0:T(8,128)S(1)}, f32[2,4,64,128]{3,2,1,0:T(8,128)S(1)}, u32[]{:S(2)}, u32[]{:S(2)}) collective-permute-start(f32[2,4,64,128]{3,2,1,0:T(8,128)S(1)} %half.1), channel_id=1, source_target_pairs={{4,12},{8,0},{12,20},{16,8},{20,28},{24,16},{5,13},{9,1},{13,21},{... | collective-permute-start | bytes 786440 | tf_op jit(solution)/shard_map/ppermute | solution.py:619
  13.0 1.4 %collective-permute-done.4.refs_3_ = f32[2,4,32,128]{3,2,1,0:T(8,128)S(1)} collective-permute-done((f32[2,4,32,128]{3,2,1,0:T(8,128)S(1)}, f32[2,4,32,128]{3,2,1,0:T(8,128)S(1)}, u32[]{:S(2)}, u32[]{:S(2)}) %collective-permute-start.4) | collective-permute-done | bytes 131104 | tf_op jit(solution)/shard_map/ppermute | solution.py:562
  15.1 3.6 %collective-permute-start.6 = (f32[2,2,64,128]{3,2,1,0:T(8,128)S(1)}, f32[2,2,64,128]{3,2,1,0:T(8,128)S(1)}, u32[]{:S(2)}, u32[]{:S(2)}) collective-permute-start(f32[2,2,64,128]{3,2,1,0:T(8,128)S(1)} %get-tuple-element.40), channel_id=1, source_target_pairs={{0,8},{8,16},{12,4},{16,24},{20,12},{28,20},{1,9},{9,17},{13,5},{1... | collective-permute-start | bytes 393224 | tf_op jit(solution)/shard_map/ppermute | solution.py:619
  18.8 0.8 %begin.1 = (f32[16,64,128]{2,1,0:T(8,128)S(1)}, f32[16,64,128]{2,1,0:T(8,128)S(1)}, f32[16,64,128]{2,1,0:T(8,128)S(1)}, f32[16,80,128]{2,1,0:T(8,128)S(1)}, f32[16,80,128]{2,1,0:T(8,128)S(1)}) custom-call(f32[8,128]{1,0:T(8,128)S(1)} %get-tuple-element.29.scalar_ref, f32[2,8,64,128]{3,2,1,0:T(8,128)S(1)} %get-tuple-element.34.slab_ref), custom_call_target="tpu_custom_call" | custom-call | tf_op jit(solution)/shard_map/begin/pallas_call | solution.py:545
  19.6 1.5 %collective-permute-done.6.refs_6_ = f32[2,2,64,128]{3,2,1,0:T(8,128)S(1)} collective-permute-done((f32[2,2,64,128]{3,2,1,0:T(8,128)S(1)}, f32[2,2,64,128]{3,2,1,0:T(8,128)S(1)}, u32[]{:S(2)}, u32[]{:S(2)}) %collective-permute-start.6) | collective-permute-done | bytes 131104 | tf_op jit(solution)/shard_map/ppermute | solution.py:619
  21.2 1.1 %pre.1 = (f32[16,64,128]{2,1,0:T(8,128)S(1)}, f32[16,64,128]{2,1,0:T(8,128)S(1)}, f32[16,64,128]{2,1,0:T(8,128)S(1)}, f32[16,80,128]{2,1,0:T(8,128)S(1)}, f32[16...) custom-call(s32[2]{0:T(128)S(1)} %pad_add_fusion.place_ref, ...), custom_call_target="tpu_custom_call", output_to_operand_aliasing={{0}: (2, {}), {1}: (3, {}), {2}: (4, {}), {3}: (5, {}), {4}... | custom-call | tf_op jit(solution)/shard_map/pre/pallas_call | solution.py:545
  22.3 4.5 %collective-permute-start.7 = (f32[4,32,128]{2,1,0:T(8,128)S(1)}, f32[4,32,128]{2,1,0:T(8,128)S(1)}, u32[]{:S(2)}, u32[]{:S(2)}) collective-permute-start(f32[4,32,128]{2,1,0:T(8,128)S(1)} %get-tuple-element.45.refs_2_), channel_id=1, source_target_pairs={{0,24},{4,28},{8,16},{12,20},{16,8},{20,12},{24,0},{28,4},{1,25},{... | collective-permute-start | bytes 196616 | tf_op jit(solution)/shard_map/ppermute | solution.py:571
  27.5 3.3 %collective-permute-start.10 = (f32[2,64,128]{2,1,0:T(8,128)S(1)}, f32[2,64,128]{2,1,0:T(8,128)S(1)}, u32[]{:S(2)}, u32[]{:S(2)}) collective-permute-start(f32[2,64,128]{2,1,0:T(8,128)S(1)} %get-tuple-element.46), channel_id=1, source_target_pairs={{0,8},{8,16},{12,4},{16,24},{20,12},{28,20},{1,9},{9,17},{13,5},{1... | collective-permute-start | bytes 196616 | tf_op jit(solution)/shard_map/ppermute | solution.py:619
  32.0 2.3 %coarse.1.refs_4_ = f32[256,128]{1,0:T(8,128)S(1)} custom-call(s32[2]{0:T(128)S(1)} %pad_add_fusion.place_ref, f32[8,128]{1,0:T(8,128)S(1)} %get-tuple-element.29.scalar_ref, bf16[128,128]{1,0:T(8,128)(2,1)S(1)} %get-tuple-element.56.refs_7_.refs_0_, bf16[128,128]{1,0:T(8,128)(2,1)S(1)} %get-tuple-element.55.refs_1_, ...), custom_call_target="tpu_custom_call" | custom-call | tf_op jit(solution)/shard_map/coarse/pallas_call | solution.py:545
  34.4 1.5 %post.1 = (f32[520,128]{1,0:T(8,128)S(1)}, f32[520,128]{1,0:T(8,128)S(1)}) custom-call(s32[2]{0:T(128)S(1)} %pad_add_fusion.place_ref, f32[8,128]{1,0:T(8,128)S(1)} %get-tuple-element.29.scalar_ref, f32[16,64,128]{2,1,0:T(8,128)S(1)} %get-tuple-element.41.refs_0_, f32[16,64,128]{2,1,0:T(8,128)S(1)} %get-tuple-element.42.refs_1_, ...), custom_call_target="tpu_custom_call" | custom-call | tf_op jit(solution)/shard_map/post/pallas_call | solution.py:545
  36.0 1.5 %collective-permute-done.11.got_ref = f32[520,128]{1,0:T(8,128)S(1)} collective-permute-done((f32[520,128]{1,0:T(8,128)S(1)}, f32[520,128]{1,0:T(8,128)S(1)}, u32[]{:S(2)}, u32[]{:S(2)}) %collective-permute-start.11) | collective-permute-done | bytes 266272 | tf_op jit(solution)/shard_map/ppermute | solution.py:669
  38.1 1.6 %collective-permute-start.12 = (f32[208,128]{1,0:T(8,128)S(1)}, f32[208,128]{1,0:T(8,128)S(1)}, u32[]{:S(2)}, u32[]{:S(2)}) collective-permute-start(f32[208,128]{1,0:T(8,128)S(1)} %get-tuple-element.50), channel_id=1, source_target_pairs={{0,2},{1,3},{2,0},{3,1},{4,6},{5,7},{6,4},{7,5},{8,10},{9,11},{10,... | collective-permute-start | bytes 319496 | tf_op jit(solution)/shard_map/ppermute | solution.py:562
  39.7 1.2 %collective-permute-start.13 = (f32[208,128]{1,0:T(8,128)S(1)}, f32[208,128]{1,0:T(8,128)S(1)}, u32[]{:S(2)}, u32[]{:S(2)}) collective-permute-start(f32[208,128]{1,0:T(8,128)S(1)} %get-tuple-element.51), channel_id=1, source_target_pairs={{0,4},{1,5},{2,6},{3,7},{4,0},{5,1},{6,2},{7,3},{8,12},{9,13},{10,... | collective-permute-start | bytes 319496 | tf_op jit(solution)/shard_map/ppermute | solution.py:562
  41.7 1.5 %collective-permute-done.12.refs_1_ = f32[208,128]{1,0:T(8,128)S(1)} collective-permute-done((f32[208,128]{1,0:T(8,128)S(1)}, f32[208,128]{1,0:T(8,128)S(1)}, u32[]{:S(2)}, u32[]{:S(2)}) %collective-permute-start.12) | collective-permute-done | bytes 106528 | tf_op jit(solution)/shard_map/ppermute | solution.py:562
  43.2 2.4 %collective-permute-done.13.refs_2_ = f32[208,128]{1,0:T(8,128)S(1)} collective-permute-done((f32[208,128]{1,0:T(8,128)S(1)}, f32[208,128]{1,0:T(8,128)S(1)}, u32[]{:S(2)}, u32[]{:S(2)}) %collective-permute-start.13) | collective-permute-done | bytes 106528 | tf_op jit(solution)/shard_map/ppermute | solution.py:562
  45.6 1.1 %collective-permute-done.14.refs_3_ = f32[208,128]{1,0:T(8,128)S(1)} collective-permute-done((f32[208,128]{1,0:T(8,128)S(1)}, f32[208,128]{1,0:T(8,128)S(1)}, u32[]{:S(2)}, u32[]{:S(2)}) %collective-permute-start.14) | collective-permute-done | bytes 106528 | tf_op jit(solution)/shard_map/ppermute | solution.py:562
  46.7 3.0 %collective-permute-start.15 = (f32[8,128]{1,0:T(8,128)S(1)}, f32[8,128]{1,0:T(8,128)S(1)}, u32[]{:S(2)}, u32[]{:S(2)}) collective-permute-start(f32[8,128]{1,0:T(8,128)S(1)} %squares.1), channel_id=1, source_target_pairs={{0,24},{4,28},{8,16},{12,20},{16,8},{20,12},{24,0},{28,4},{1,25},{... | collective-permute-start | bytes 12296 | tf_op jit(solution)/shard_map/ppermute | solution.py:571
  49.7 1.4 %collective-permute-start.17 = (f32[8,128]{1,0:T(8,128)S(1)}, f32[8,128]{1,0:T(8,128)S(1)}, u32[]{:S(2)}, u32[]{:S(2)}) collective-permute-start(f32[8,128]{1,0:T(8,128)S(1)} %squares.1), channel_id=1, source_target_pairs={{0,8},{4,12},{8,0},{12,4},{16,24},{20,28},{24,16},{28,20},{1,9},{5... | collective-permute-start | bytes 12296 | tf_op jit(solution)/shard_map/ppermute | solution.py:571
  51.1 1.4 %collect.1 = (f32[8,4,16,128]{3,2,1,0:T(8,128)}, f32[8,4,16,128]{3,2,1,0:T(8,128)}) custom-call(s32[2]{0:T(128)S(1)} %pad_add_fusion.place_ref, f32[8]{0:T(128)S(1)} %copy-done.3, s32[8]{0:T(128)S(1)} %copy-done.4, f32[3]{0:T(128)S(1)} %copy-done.5, f32[8,4,16,128]{3,2,1,0:T(8,128)S(1)} %copy-done.1, f32[4,16,128]{2,1,0:T(8,128)S(1)} %copy-done.2, ...), custom_call_target="tpu_custom_call" | custom-call | tf_op jit(solution)/shard_map/collect/pallas_call | solution.py:545
  52.5 1.7 %collective-permute-done.16 = f32[8,128]{1,0:T(8,128)S(1)} collective-permute-done((f32[8,128]{1,0:T(8,128)S(1)}, f32[8,128]{1,0:T(8,128)S(1)}, u32[]{:S(2)}, u32[]{:S(2)}) %collective-permute-start.16) | collective-permute-done | bytes 4128 | tf_op jit(solution)/shard_map/ppermute | solution.py:571
  (44 shorter events, 8.3 us)
Async XLA Ops:
  0.6 2.2 %collective-permute-start = (f32[8,4,16,128]{3,2,1,0:T(8,128)}, f32[8,4,16,128]{3,2,1,0:T(8,128)S(1)}, u32[]{:S(2)}, u32[]{:S(2)}) collective-permute-start(f32[8,4,16,128]{3,2,1,0:T(8,128)} %source_ref.3), channel_id=1, source_target_pairs={{0,1},{1,0},{2,3},{3,2},{4,5},{5,4},{6,7},{7,6},{8,9},{9,8},{10,11... | collective-permute-start | bytes 786440 | tf_op jit(solution)/shard_map/ppermute | solution.py:589
  1.1 1.7 %collective-permute-start.1 = (f32[4,16,128]{2,1,0:T(8,128)}, f32[4,16,128]{2,1,0:T(8,128)S(1)}, u32[]{:S(2)}, u32[]{:S(2)}) collective-permute-start(f32[4,16,128]{2,1,0:T(8,128)} %reaction_ref.1), channel_id=1, source_target_pairs={{0,1},{1,0},{2,3},{3,2},{4,5},{5,4},{6,7},{7,6},{8,9},{9,8},{10,11... | collective-permute-start | bytes 98312 | tf_op jit(solution)/shard_map/ppermute | solution.py:589
  1.3 0.9 %copy-start = (f32[8,4,16,128]{3,2,1,0:T(8,128)S(1)}, f32[8,4,16,128]{3,2,1,0:T(8,128)}, u32[]{:S(2)}) copy-start(f32[8,4,16,128]{3,2,1,0:T(8,128)} %source_ref.3) | copy-start | bytes 786436
  2.3 0.8 %copy-start.2 = (f32[4,16,128]{2,1,0:T(8,128)S(1)}, f32[4,16,128]{2,1,0:T(8,128)}, u32[]{:S(2)}) copy-start(f32[4,16,128]{2,1,0:T(8,128)} %reaction_ref.1) | copy-start | bytes 98308
  2.3 0.8 %copy-start.3 = (f32[8]{0:T(128)S(1)}, f32[8]{0:T(128)}, u32[]{:S(2)}) copy-start(f32[8]{0:T(128)} %shifts_ref.3) | copy-start | bytes 100
  2.3 0.8 %copy-start.4 = (s32[8]{0:T(128)S(1)}, s32[8]{0:T(128)}, u32[]{:S(2)}) copy-start(s32[8]{0:T(128)} %index_ref.3) | copy-start | bytes 100
  2.3 0.8 %copy-start.5 = (f32[3]{0:T(128)S(1)}, f32[3]{0:T(128)}, u32[]{:S(2)}) copy-start(f32[3]{0:T(128)} %velocity_ref.3) | copy-start | bytes 40
  3.6 6.8 %collective-permute-start.2 = (f32[2,4,32,128]{3,2,1,0:T(8,128)S(1)}, f32[2,4,32,128]{3,2,1,0:T(8,128)S(1)}, u32[]{:S(2)}, u32[]{:S(2)}) collective-permute-start(f32[2,4,32,128]{3,2,1,0:T(8,128)S(1)} %get-tuple-element.31), channel_id=1, source_target_pairs={{0,2},{1,3},{2,0},{3,1},{4,6},{5,7},{6,4},{7,5},{8,10},{9,11},{10,... | collective-permute-start | bytes 393224 | tf_op jit(solution)/shard_map/ppermute | solution.py:562
  6.6 6.4 %collective-permute-start.3 = (f32[2,4,32,128]{3,2,1,0:T(8,128)S(1)}, f32[2,4,32,128]{3,2,1,0:T(8,128)S(1)}, u32[]{:S(2)}, u32[]{:S(2)}) collective-permute-start(f32[2,4,32,128]{3,2,1,0:T(8,128)S(1)} %get-tuple-element.32), channel_id=1, source_target_pairs={{0,4},{1,5},{2,6},{3,7},{4,0},{5,1},{6,2},{7,3},{8,12},{9,13},{10,... | collective-permute-start | bytes 393224 | tf_op jit(solution)/shard_map/ppermute | solution.py:562
  8.1 6.3 %collective-permute-start.4 = (f32[2,4,32,128]{3,2,1,0:T(8,128)S(1)}, f32[2,4,32,128]{3,2,1,0:T(8,128)S(1)}, u32[]{:S(2)}, u32[]{:S(2)}) collective-permute-start(f32[2,4,32,128]{3,2,1,0:T(8,128)S(1)} %get-tuple-element.33), channel_id=1, source_target_pairs={{0,6},{1,7},{2,4},{3,5},{4,2},{5,3},{6,0},{7,1},{8,14},{9,15},{10,... | collective-permute-start | bytes 393224 | tf_op jit(solution)/shard_map/ppermute | solution.py:562
  11.0 10.2 %collective-permute-start.5 = (f32[2,4,64,128]{3,2,1,0:T(8,128)S(1)}, f32[2,4,64,128]{3,2,1,0:T(8,128)S(1)}, u32[]{:S(2)}, u32[]{:S(2)}) collective-permute-start(f32[2,4,64,128]{3,2,1,0:T(8,128)S(1)} %half.1), channel_id=1, source_target_pairs={{4,12},{8,0},{12,20},{16,8},{20,28},{24,16},{5,13},{9,1},{13,21},{... | collective-permute-start | bytes 786440 | tf_op jit(solution)/shard_map/ppermute | solution.py:619
  15.1 6.1 %collective-permute-start.6 = (f32[2,2,64,128]{3,2,1,0:T(8,128)S(1)}, f32[2,2,64,128]{3,2,1,0:T(8,128)S(1)}, u32[]{:S(2)}, u32[]{:S(2)}) collective-permute-start(f32[2,2,64,128]{3,2,1,0:T(8,128)S(1)} %get-tuple-element.40), channel_id=1, source_target_pairs={{0,8},{8,16},{12,4},{16,24},{20,12},{28,20},{1,9},{9,17},{13,5},{1... | collective-permute-start | bytes 393224 | tf_op jit(solution)/shard_map/ppermute | solution.py:619
  22.3 9.2 %collective-permute-start.7 = (f32[4,32,128]{2,1,0:T(8,128)S(1)}, f32[4,32,128]{2,1,0:T(8,128)S(1)}, u32[]{:S(2)}, u32[]{:S(2)}) collective-permute-start(f32[4,32,128]{2,1,0:T(8,128)S(1)} %get-tuple-element.45.refs_2_), channel_id=1, source_target_pairs={{0,24},{4,28},{8,16},{12,20},{16,8},{20,12},{24,0},{28,4},{1,25},{... | collective-permute-start | bytes 196616 | tf_op jit(solution)/shard_map/ppermute | solution.py:571
  26.9 5.2 %collective-permute-start.8 = (f32[4,32,128]{2,1,0:T(8,128)S(1)}, f32[4,32,128]{2,1,0:T(8,128)S(1)}, u32[]{:S(2)}, u32[]{:S(2)}) collective-permute-start(f32[4,32,128]{2,1,0:T(8,128)S(1)} %get-tuple-element.45.refs_2_), channel_id=1, source_target_pairs={{0,16},{4,20},{8,24},{12,28},{16,0},{20,4},{24,8},{28,12},{1,17},{... | collective-permute-start | bytes 196616 | tf_op jit(solution)/shard_map/ppermute | solution.py:571
  26.9 5.2 %collective-permute-start.9 = (f32[4,32,128]{2,1,0:T(8,128)S(1)}, f32[4,32,128]{2,1,0:T(8,128)S(1)}, u32[]{:S(2)}, u32[]{:S(2)}) collective-permute-start(f32[4,32,128]{2,1,0:T(8,128)S(1)} %get-tuple-element.45.refs_2_), channel_id=1, source_target_pairs={{0,8},{4,12},{8,0},{12,4},{16,24},{20,28},{24,16},{28,20},{1,9},{5... | collective-permute-start | bytes 196616 | tf_op jit(solution)/shard_map/ppermute | solution.py:571
  27.5 6.9 %collective-permute-start.10 = (f32[2,64,128]{2,1,0:T(8,128)S(1)}, f32[2,64,128]{2,1,0:T(8,128)S(1)}, u32[]{:S(2)}, u32[]{:S(2)}) collective-permute-start(f32[2,64,128]{2,1,0:T(8,128)S(1)} %get-tuple-element.46), channel_id=1, source_target_pairs={{0,8},{8,16},{12,4},{16,24},{20,12},{28,20},{1,9},{9,17},{13,5},{1... | collective-permute-start | bytes 196616 | tf_op jit(solution)/shard_map/ppermute | solution.py:619
  35.9 1.6 %collective-permute-start.11 = (f32[520,128]{1,0:T(8,128)S(1)}, f32[520,128]{1,0:T(8,128)S(1)}, u32[]{:S(2)}, u32[]{:S(2)}) collective-permute-start(f32[520,128]{1,0:T(8,128)S(1)} %get-tuple-element.48), channel_id=1, source_target_pairs={{0,1},{1,0},{2,3},{3,2},{4,5},{5,4},{6,7},{7,6},{8,9},{9,8},{10,11... | collective-permute-start | bytes 798728 | tf_op jit(solution)/shard_map/ppermute | solution.py:669
  38.1 13.0 %copy-start.1 = (f32[8,4,16,128]{3,2,1,0:T(8,128)S(1)}, f32[8,4,16,128]{3,2,1,0:T(8,128)}, u32[]{:S(2)}) copy-start(f32[8,4,16,128]{3,2,1,0:T(8,128)} %source_ref.3) | copy-start | bytes 786436
  38.1 5.1 %collective-permute-start.12 = (f32[208,128]{1,0:T(8,128)S(1)}, f32[208,128]{1,0:T(8,128)S(1)}, u32[]{:S(2)}, u32[]{:S(2)}) collective-permute-start(f32[208,128]{1,0:T(8,128)S(1)} %get-tuple-element.50), channel_id=1, source_target_pairs={{0,2},{1,3},{2,0},{3,1},{4,6},{5,7},{6,4},{7,5},{8,10},{9,11},{10,... | collective-permute-start | bytes 319496 | tf_op jit(solution)/shard_map/ppermute | solution.py:562
  39.7 5.9 %collective-permute-start.13 = (f32[208,128]{1,0:T(8,128)S(1)}, f32[208,128]{1,0:T(8,128)S(1)}, u32[]{:S(2)}, u32[]{:S(2)}) collective-permute-start(f32[208,128]{1,0:T(8,128)S(1)} %get-tuple-element.51), channel_id=1, source_target_pairs={{0,4},{1,5},{2,6},{3,7},{4,0},{5,1},{6,2},{7,3},{8,12},{9,13},{10,... | collective-permute-start | bytes 319496 | tf_op jit(solution)/shard_map/ppermute | solution.py:562
  40.9 5.7 %collective-permute-start.14 = (f32[208,128]{1,0:T(8,128)S(1)}, f32[208,128]{1,0:T(8,128)S(1)}, u32[]{:S(2)}, u32[]{:S(2)}) collective-permute-start(f32[208,128]{1,0:T(8,128)S(1)} %get-tuple-element.52), channel_id=1, source_target_pairs={{0,6},{1,7},{2,4},{3,5},{4,2},{5,3},{6,0},{7,1},{8,14},{9,15},{10,... | collective-permute-start | bytes 319496 | tf_op jit(solution)/shard_map/ppermute | solution.py:562
  46.7 5.8 %collective-permute-start.15 = (f32[8,128]{1,0:T(8,128)S(1)}, f32[8,128]{1,0:T(8,128)S(1)}, u32[]{:S(2)}, u32[]{:S(2)}) collective-permute-start(f32[8,128]{1,0:T(8,128)S(1)} %squares.1), channel_id=1, source_target_pairs={{0,24},{4,28},{8,16},{12,20},{16,8},{20,12},{24,0},{28,4},{1,25},{... | collective-permute-start | bytes 12296 | tf_op jit(solution)/shard_map/ppermute | solution.py:571
  49.7 4.5 %collective-permute-start.16 = (f32[8,128]{1,0:T(8,128)S(1)}, f32[8,128]{1,0:T(8,128)S(1)}, u32[]{:S(2)}, u32[]{:S(2)}) collective-permute-start(f32[8,128]{1,0:T(8,128)S(1)} %squares.1), channel_id=1, source_target_pairs={{0,16},{4,20},{8,24},{12,28},{16,0},{20,4},{24,8},{28,12},{1,17},{... | collective-permute-start | bytes 12296 | tf_op jit(solution)/shard_map/ppermute | solution.py:571
  49.7 4.5 %collective-permute-start.17 = (f32[8,128]{1,0:T(8,128)S(1)}, f32[8,128]{1,0:T(8,128)S(1)}, u32[]{:S(2)}, u32[]{:S(2)}) collective-permute-start(f32[8,128]{1,0:T(8,128)S(1)} %squares.1), channel_id=1, source_target_pairs={{0,8},{4,12},{8,0},{12,4},{16,24},{20,28},{24,16},{28,20},{1,9},{5... | collective-permute-start | bytes 12296 | tf_op jit(solution)/shard_map/ppermute | solution.py:571

commit v20 on v19

--- a/solution.py
+++ b/solution.py
@@ -530,11 +530,13 @@
                 residual_ref[column, p, pl.ds(by - 1, 1), :] = part[pl.ds(at + 1, 1), :]
 
 
-def squares_kernel(bx, by, *refs):
+def squares_kernel(bx, by, place_ref, *refs):
+    parts, out_ref = refs[:-1], refs[-1]
     _, _, squares, size = part_rows(bx, by)
-    for m, part in enumerate(refs[:-1]):
+    for m, part in enumerate(parts):
+        target = jnp.bitwise_xor(place_ref[0] // 2, m)
         for n in range(2):
-            refs[-1][pl.ds(2 * m + n, 1), :] = part[pl.ds(n * size + squares, 1), :]
+            out_ref[pl.ds(2 * target + n, 1), :] = part[pl.ds(n * size + squares, 1), :]
 
 
 SMEM = pl.BlockSpec(memory_space=pltpu.SMEM)
@@ -671,7 +673,7 @@
     )
     parts = swap_in_plane(parts, 2)
     (squares,) = local_kernel(
-        functools.partial(squares_kernel, bx, by), "squares", (), parts, [(columns, nz)]
+        functools.partial(squares_kernel, bx, by), "squares", (place,), parts, [(columns, nz)]
     )
     iterate, residual = local_kernel(
         collect_kernel,
@@ -680,11 +682,12 @@
         (source, reaction, *parts),
         [source.shape] * 2,
     )
-    total = sum(swap_slabs(squares, step, slabs))
-    rms = jnp.sqrt(total[:, 0] / (nx * ny * nz) + EPSILON)
-    slots = jnp.arange(columns, dtype=jnp.int32)
-    mine = jnp.bitwise_xor(slots, column // 2 * 2)[:, None] == slots[None, :]
-    residual_rms = jnp.sum(jnp.where(mine, rms[None, :], 0.0), axis=1)
+    sums = swap_slabs(squares, step, slabs)
+    sums = [*sums[1:], sums[0]]
+    while len(sums) > 1:
+        sums = [first + second for first, second in zip(sums[::2], sums[1::2])]
+    (total,) = sums
+    residual_rms = jnp.sqrt(total[:, 0] / (nx * ny * nz) + EPSILON)
     return iterate, residual, residual_rms
 
 

time: 55.3 us -> 55.7 us (level)
    reduce_sum x1 -> x0, other arithmetic: 0.7 us -> none  [column_body(): residual_rms = jnp.sum(jnp.where(mine, rms[None, :], 0.0), axis=1)]
where the time goes in v20:
time: 55.7 us; the launch traced here: 55.5 us
  starting transfers between devices  26.6 us (48%)
  waiting for transfers between devices  14.6 us (26%)
  Pallas kernels  11.4 us (20%)
  local copies, waits for them, and re-layouts  1.13 us (2%)
  other arithmetic  0.85 us (2%)
  between operations  0.82 us (1%)
    pallas_call x12, Pallas kernels, local_kernel(): pl.pallas_call(kernel, out_shape=[jax.ShapeDtypeStruct(shape, jnp.float32...  11.4 us
    ppermute x6, starting transfers between devices, swap_slabs(): moved.append(lax.ppermute(piece, 'gx', pairs))  9.63 us
    ppermute x6, waiting for transfers between devices, swap_in_plane(): moved.append(lax.ppermute(pieces[k], ('gx', 'gy'), pairs))  9.35 us
    ppermute x3, starting transfers between devices, send_beside(): lax.ppermute(piece, 'gx', [(i, j) for i, j in pairs if 0 <= j < gx_size])  8.21 us
    ppermute x6, starting transfers between devices, swap_in_plane(): moved.append(lax.ppermute(pieces[k], ('gx', 'gy'), pairs))  8.1 us
    ppermute x6, waiting for transfers between devices, swap_slabs(): moved.append(lax.ppermute(piece, 'gx', pairs))  2.19 us
    ppermute x3, waiting for transfers between devices, send_beside(): lax.ppermute(piece, 'gx', [(i, j) for i, j in pairs if 0 <= j < gx_size])  1.55 us
    ppermute x1, waiting for transfers between devices, column_body(): lax.ppermute(sent, 'gy', cores)  1.53 us
  transfers between devices with their start and end apart: 18, of which 10 were waited for; matrix products, arithmetic and copies ran while one was open for 0% of the time, Pallas kernels for 13%

profile of v20, /device:TPU:0, one launch (start us, length us, event | category | flops | bytes accessed | tf_op | source)
XLA Modules:
  0.0 55.5 jit_solution(603258405538288494)
XLA Ops:
  1.3 0.9 %copy-done = f32[8,4,16,128]{3,2,1,0:T(8,128)S(1)} copy-done((f32[8,4,16,128]{3,2,1,0:T(8,128)S(1)}, f32[8,4,16,128]{3,2,1,0:T(8,128)}, u32[]{:S(2)}) %copy-start) | copy-done | bytes 262168
  3.6 3.0 %collective-permute-start.2 = (f32[2,4,32,128]{3,2,1,0:T(8,128)S(1)}, f32[2,4,32,128]{3,2,1,0:T(8,128)S(1)}, u32[]{:S(2)}, u32[]{:S(2)}) collective-permute-start(f32[2,4,32,128]{3,2,1,0:T(8,128)S(1)} %get-tuple-element.31), channel_id=1, source_target_pairs={{0,2},{1,3},{2,0},{3,1},{4,6},{5,7},{6,4},{7,5},{8,10},{9,11},{10,... | collective-permute-start | bytes 393224 | tf_op jit(solution)/shard_map/ppermute | solution.py:564
  6.6 1.5 %collective-permute-start.3 = (f32[2,4,32,128]{3,2,1,0:T(8,128)S(1)}, f32[2,4,32,128]{3,2,1,0:T(8,128)S(1)}, u32[]{:S(2)}, u32[]{:S(2)}) collective-permute-start(f32[2,4,32,128]{3,2,1,0:T(8,128)S(1)} %get-tuple-element.32), channel_id=1, source_target_pairs={{0,4},{1,5},{2,6},{3,7},{4,0},{5,1},{6,2},{7,3},{8,12},{9,13},{10,... | collective-permute-start | bytes 393224 | tf_op jit(solution)/shard_map/ppermute | solution.py:564
  8.2 2.2 %collective-permute-done.2.refs_1_ = f32[2,4,32,128]{3,2,1,0:T(8,128)S(1)} collective-permute-done((f32[2,4,32,128]{3,2,1,0:T(8,128)S(1)}, f32[2,4,32,128]{3,2,1,0:T(8,128)S(1)}, u32[]{:S(2)}, u32[]{:S(2)}) %collective-permute-start.2) | collective-permute-done | bytes 131104 | tf_op jit(solution)/shard_map/ppermute | solution.py:564
  11.0 1.3 %collective-permute-start.5 = (f32[2,4,64,128]{3,2,1,0:T(8,128)S(1)}, f32[2,4,64,128]{3,2,1,0:T(8,128)S(1)}, u32[]{:S(2)}, u32[]{:S(2)}) collective-permute-start(f32[2,4,64,128]{3,2,1,0:T(8,128)S(1)} %half.1), channel_id=1, source_target_pairs={{4,12},{8,0},{12,20},{16,8},{20,28},{24,16},{5,13},{9,1},{13,21},{... | collective-permute-start | bytes 786440 | tf_op jit(solution)/shard_map/ppermute | solution.py:621
  13.0 1.4 %collective-permute-done.4.refs_3_ = f32[2,4,32,128]{3,2,1,0:T(8,128)S(1)} collective-permute-done((f32[2,4,32,128]{3,2,1,0:T(8,128)S(1)}, f32[2,4,32,128]{3,2,1,0:T(8,128)S(1)}, u32[]{:S(2)}, u32[]{:S(2)}) %collective-permute-start.4) | collective-permute-done | bytes 131104 | tf_op jit(solution)/shard_map/ppermute | solution.py:564
  15.1 3.6 %collective-permute-start.6 = (f32[2,2,64,128]{3,2,1,0:T(8,128)S(1)}, f32[2,2,64,128]{3,2,1,0:T(8,128)S(1)}, u32[]{:S(2)}, u32[]{:S(2)}) collective-permute-start(f32[2,2,64,128]{3,2,1,0:T(8,128)S(1)} %get-tuple-element.40), channel_id=1, source_target_pairs={{0,8},{8,16},{12,4},{16,24},{20,12},{28,20},{1,9},{9,17},{13,5},{1... | collective-permute-start | bytes 393224 | tf_op jit(solution)/shard_map/ppermute | solution.py:621
  18.8 0.8 %begin.1 = (f32[16,64,128]{2,1,0:T(8,128)S(1)}, f32[16,64,128]{2,1,0:T(8,128)S(1)}, f32[16,64,128]{2,1,0:T(8,128)S(1)}, f32[16,80,128]{2,1,0:T(8,128)S(1)}, f32[16,80,128]{2,1,0:T(8,128)S(1)}) custom-call(f32[8,128]{1,0:T(8,128)S(1)} %get-tuple-element.29.scalar_ref, f32[2,8,64,128]{3,2,1,0:T(8,128)S(1)} %get-tuple-element.34.slab_ref), custom_call_target="tpu_custom_call" | custom-call | tf_op jit(solution)/shard_map/begin/pallas_call | solution.py:547
  19.6 1.5 %collective-permute-done.6.refs_6_ = f32[2,2,64,128]{3,2,1,0:T(8,128)S(1)} collective-permute-done((f32[2,2,64,128]{3,2,1,0:T(8,128)S(1)}, f32[2,2,64,128]{3,2,1,0:T(8,128)S(1)}, u32[]{:S(2)}, u32[]{:S(2)}) %collective-permute-start.6) | collective-permute-done | bytes 131104 | tf_op jit(solution)/shard_map/ppermute | solution.py:621
  21.2 1.1 %pre.1 = (f32[16,64,128]{2,1,0:T(8,128)S(1)}, f32[16,64,128]{2,1,0:T(8,128)S(1)}, f32[16,64,128]{2,1,0:T(8,128)S(1)}, f32[16,80,128]{2,1,0:T(8,128)S(1)}, f32[16...) custom-call(s32[2]{0:T(128)S(1)} %pad_add_fusion.place_ref, ...), custom_call_target="tpu_custom_call", output_to_operand_aliasing={{0}: (2, {}), {1}: (3, {}), {2}: (4, {}), {3}: (5, {}), {4}... | custom-call | tf_op jit(solution)/shard_map/pre/pallas_call | solution.py:547
  22.3 4.5 %collective-permute-start.7 = (f32[4,32,128]{2,1,0:T(8,128)S(1)}, f32[4,32,128]{2,1,0:T(8,128)S(1)}, u32[]{:S(2)}, u32[]{:S(2)}) collective-permute-start(f32[4,32,128]{2,1,0:T(8,128)S(1)} %get-tuple-element.45.refs_2_), channel_id=1, source_target_pairs={{0,24},{4,28},{8,16},{12,20},{16,8},{20,12},{24,0},{28,4},{1,25},{... | collective-permute-start | bytes 196616 | tf_op jit(solution)/shard_map/ppermute | solution.py:573
  27.5 3.3 %collective-permute-start.10 = (f32[2,64,128]{2,1,0:T(8,128)S(1)}, f32[2,64,128]{2,1,0:T(8,128)S(1)}, u32[]{:S(2)}, u32[]{:S(2)}) collective-permute-start(f32[2,64,128]{2,1,0:T(8,128)S(1)} %get-tuple-element.46), channel_id=1, source_target_pairs={{0,8},{8,16},{12,4},{16,24},{20,12},{28,20},{1,9},{9,17},{13,5},{1... | collective-permute-start | bytes 196616 | tf_op jit(solution)/shard_map/ppermute | solution.py:621
  32.0 2.3 %coarse.1.refs_4_ = f32[256,128]{1,0:T(8,128)S(1)} custom-call(s32[2]{0:T(128)S(1)} %pad_add_fusion.place_ref, f32[8,128]{1,0:T(8,128)S(1)} %get-tuple-element.29.scalar_ref, bf16[128,128]{1,0:T(8,128)(2,1)S(1)} %get-tuple-element.56.refs_7_.refs_0_, bf16[128,128]{1,0:T(8,128)(2,1)S(1)} %get-tuple-element.55.refs_1_, ...), custom_call_target="tpu_custom_call" | custom-call | tf_op jit(solution)/shard_map/coarse/pallas_call | solution.py:547
  34.4 1.5 %post.1 = (f32[520,128]{1,0:T(8,128)S(1)}, f32[520,128]{1,0:T(8,128)S(1)}) custom-call(s32[2]{0:T(128)S(1)} %pad_add_fusion.place_ref, f32[8,128]{1,0:T(8,128)S(1)} %get-tuple-element.29.scalar_ref, f32[16,64,128]{2,1,0:T(8,128)S(1)} %get-tuple-element.41.refs_0_, f32[16,64,128]{2,1,0:T(8,128)S(1)} %get-tuple-element.42.refs_1_, ...), custom_call_target="tpu_custom_call" | custom-call | tf_op jit(solution)/shard_map/post/pallas_call | solution.py:547
  36.0 1.5 %collective-permute-done.11.got_ref = f32[520,128]{1,0:T(8,128)S(1)} collective-permute-done((f32[520,128]{1,0:T(8,128)S(1)}, f32[520,128]{1,0:T(8,128)S(1)}, u32[]{:S(2)}, u32[]{:S(2)}) %collective-permute-start.11) | collective-permute-done | bytes 266272 | tf_op jit(solution)/shard_map/ppermute | solution.py:671
  38.1 1.6 %collective-permute-start.12 = (f32[208,128]{1,0:T(8,128)S(1)}, f32[208,128]{1,0:T(8,128)S(1)}, u32[]{:S(2)}, u32[]{:S(2)}) collective-permute-start(f32[208,128]{1,0:T(8,128)S(1)} %get-tuple-element.50), channel_id=1, source_target_pairs={{0,2},{1,3},{2,0},{3,1},{4,6},{5,7},{6,4},{7,5},{8,10},{9,11},{10,... | collective-permute-start | bytes 319496 | tf_op jit(solution)/shard_map/ppermute | solution.py:564
  39.7 1.2 %collective-permute-start.13 = (f32[208,128]{1,0:T(8,128)S(1)}, f32[208,128]{1,0:T(8,128)S(1)}, u32[]{:S(2)}, u32[]{:S(2)}) collective-permute-start(f32[208,128]{1,0:T(8,128)S(1)} %get-tuple-element.51), channel_id=1, source_target_pairs={{0,4},{1,5},{2,6},{3,7},{4,0},{5,1},{6,2},{7,3},{8,12},{9,13},{10,... | collective-permute-start | bytes 319496 | tf_op jit(solution)/shard_map/ppermute | solution.py:564
  41.7 1.5 %collective-permute-done.12.refs_1_ = f32[208,128]{1,0:T(8,128)S(1)} collective-permute-done((f32[208,128]{1,0:T(8,128)S(1)}, f32[208,128]{1,0:T(8,128)S(1)}, u32[]{:S(2)}, u32[]{:S(2)}) %collective-permute-start.12) | collective-permute-done | bytes 106528 | tf_op jit(solution)/shard_map/ppermute | solution.py:564
  43.2 2.4 %collective-permute-done.13.refs_2_ = f32[208,128]{1,0:T(8,128)S(1)} collective-permute-done((f32[208,128]{1,0:T(8,128)S(1)}, f32[208,128]{1,0:T(8,128)S(1)}, u32[]{:S(2)}, u32[]{:S(2)}) %collective-permute-start.13) | collective-permute-done | bytes 106528 | tf_op jit(solution)/shard_map/ppermute | solution.py:564
  45.6 1.1 %collective-permute-done.14.refs_3_ = f32[208,128]{1,0:T(8,128)S(1)} collective-permute-done((f32[208,128]{1,0:T(8,128)S(1)}, f32[208,128]{1,0:T(8,128)S(1)}, u32[]{:S(2)}, u32[]{:S(2)}) %collective-permute-start.14) | collective-permute-done | bytes 106528 | tf_op jit(solution)/shard_map/ppermute | solution.py:564
  47.2 3.1 %collective-permute-start.15 = (f32[8,128]{1,0:T(8,128)S(1)}, f32[8,128]{1,0:T(8,128)S(1)}, u32[]{:S(2)}, u32[]{:S(2)}) collective-permute-start(f32[8,128]{1,0:T(8,128)S(1)} %squares.1), channel_id=1, source_target_pairs={{0,24},{4,28},{8,16},{12,20},{16,8},{20,12},{24,0},{28,4},{1,25},{... | collective-permute-start | bytes 12296 | tf_op jit(solution)/shard_map/ppermute | solution.py:573
  50.3 1.4 %collective-permute-start.17 = (f32[8,128]{1,0:T(8,128)S(1)}, f32[8,128]{1,0:T(8,128)S(1)}, u32[]{:S(2)}, u32[]{:S(2)}) collective-permute-start(f32[8,128]{1,0:T(8,128)S(1)} %squares.1), channel_id=1, source_target_pairs={{0,8},{4,12},{8,0},{12,4},{16,24},{20,28},{24,16},{28,20},{1,9},{5... | collective-permute-start | bytes 12296 | tf_op jit(solution)/shard_map/ppermute | solution.py:573
  51.7 1.4 %collect.1 = (f32[8,4,16,128]{3,2,1,0:T(8,128)}, f32[8,4,16,128]{3,2,1,0:T(8,128)}) custom-call(s32[2]{0:T(128)S(1)} %pad_add_fusion.place_ref, f32[8]{0:T(128)S(1)} %copy-done.3, s32[8]{0:T(128)S(1)} %copy-done.4, f32[3]{0:T(128)S(1)} %copy-done.5, f32[8,4,16,128]{3,2,1,0:T(8,128)S(1)} %copy-done.1, f32[4,16,128]{2,1,0:T(8,128)S(1)} %copy-done.2, ...), custom_call_target="tpu_custom_call" | custom-call | tf_op jit(solution)/shard_map/collect/pallas_call | solution.py:547
  53.1 1.7 %collective-permute-done.16 = f32[8,128]{1,0:T(8,128)S(1)} collective-permute-done((f32[8,128]{1,0:T(8,128)S(1)}, f32[8,128]{1,0:T(8,128)S(1)}, u32[]{:S(2)}, u32[]{:S(2)}) %collective-permute-start.16) | collective-permute-done | bytes 4128 | tf_op jit(solution)/shard_map/ppermute | solution.py:573
  (42 shorter events, 8.6 us)
Async XLA Ops:
  0.6 2.2 %collective-permute-start = (f32[8,4,16,128]{3,2,1,0:T(8,128)}, f32[8,4,16,128]{3,2,1,0:T(8,128)S(1)}, u32[]{:S(2)}, u32[]{:S(2)}) collective-permute-start(f32[8,4,16,128]{3,2,1,0:T(8,128)} %source_ref.3), channel_id=1, source_target_pairs={{0,1},{1,0},{2,3},{3,2},{4,5},{5,4},{6,7},{7,6},{8,9},{9,8},{10,11... | collective-permute-start | bytes 786440 | tf_op jit(solution)/shard_map/ppermute | solution.py:591
  1.1 1.7 %collective-permute-start.1 = (f32[4,16,128]{2,1,0:T(8,128)}, f32[4,16,128]{2,1,0:T(8,128)S(1)}, u32[]{:S(2)}, u32[]{:S(2)}) collective-permute-start(f32[4,16,128]{2,1,0:T(8,128)} %reaction_ref.1), channel_id=1, source_target_pairs={{0,1},{1,0},{2,3},{3,2},{4,5},{5,4},{6,7},{7,6},{8,9},{9,8},{10,11... | collective-permute-start | bytes 98312 | tf_op jit(solution)/shard_map/ppermute | solution.py:591
  1.3 0.9 %copy-start = (f32[8,4,16,128]{3,2,1,0:T(8,128)S(1)}, f32[8,4,16,128]{3,2,1,0:T(8,128)}, u32[]{:S(2)}) copy-start(f32[8,4,16,128]{3,2,1,0:T(8,128)} %source_ref.3) | copy-start | bytes 786436
  2.3 0.8 %copy-start.2 = (f32[4,16,128]{2,1,0:T(8,128)S(1)}, f32[4,16,128]{2,1,0:T(8,128)}, u32[]{:S(2)}) copy-start(f32[4,16,128]{2,1,0:T(8,128)} %reaction_ref.1) | copy-start | bytes 98308
  2.3 0.8 %copy-start.3 = (f32[8]{0:T(128)S(1)}, f32[8]{0:T(128)}, u32[]{:S(2)}) copy-start(f32[8]{0:T(128)} %shifts_ref.3) | copy-start | bytes 100
  2.3 0.8 %copy-start.4 = (s32[8]{0:T(128)S(1)}, s32[8]{0:T(128)}, u32[]{:S(2)}) copy-start(s32[8]{0:T(128)} %index_ref.3) | copy-start | bytes 100
  2.3 0.8 %copy-start.5 = (f32[3]{0:T(128)S(1)}, f32[3]{0:T(128)}, u32[]{:S(2)}) copy-start(f32[3]{0:T(128)} %velocity_ref.3) | copy-start | bytes 40
  3.6 6.8 %collective-permute-start.2 = (f32[2,4,32,128]{3,2,1,0:T(8,128)S(1)}, f32[2,4,32,128]{3,2,1,0:T(8,128)S(1)}, u32[]{:S(2)}, u32[]{:S(2)}) collective-permute-start(f32[2,4,32,128]{3,2,1,0:T(8,128)S(1)} %get-tuple-element.31), channel_id=1, source_target_pairs={{0,2},{1,3},{2,0},{3,1},{4,6},{5,7},{6,4},{7,5},{8,10},{9,11},{10,... | collective-permute-start | bytes 393224 | tf_op jit(solution)/shard_map/ppermute | solution.py:564
  6.6 6.4 %collective-permute-start.3 = (f32[2,4,32,128]{3,2,1,0:T(8,128)S(1)}, f32[2,4,32,128]{3,2,1,0:T(8,128)S(1)}, u32[]{:S(2)}, u32[]{:S(2)}) collective-permute-start(f32[2,4,32,128]{3,2,1,0:T(8,128)S(1)} %get-tuple-element.32), channel_id=1, source_target_pairs={{0,4},{1,5},{2,6},{3,7},{4,0},{5,1},{6,2},{7,3},{8,12},{9,13},{10,... | collective-permute-start | bytes 393224 | tf_op jit(solution)/shard_map/ppermute | solution.py:564
  8.1 6.3 %collective-permute-start.4 = (f32[2,4,32,128]{3,2,1,0:T(8,128)S(1)}, f32[2,4,32,128]{3,2,1,0:T(8,128)S(1)}, u32[]{:S(2)}, u32[]{:S(2)}) collective-permute-start(f32[2,4,32,128]{3,2,1,0:T(8,128)S(1)} %get-tuple-element.33), channel_id=1, source_target_pairs={{0,6},{1,7},{2,4},{3,5},{4,2},{5,3},{6,0},{7,1},{8,14},{9,15},{10,... | collective-permute-start | bytes 393224 | tf_op jit(solution)/shard_map/ppermute | solution.py:564
  11.0 10.2 %collective-permute-start.5 = (f32[2,4,64,128]{3,2,1,0:T(8,128)S(1)}, f32[2,4,64,128]{3,2,1,0:T(8,128)S(1)}, u32[]{:S(2)}, u32[]{:S(2)}) collective-permute-start(f32[2,4,64,128]{3,2,1,0:T(8,128)S(1)} %half.1), channel_id=1, source_target_pairs={{4,12},{8,0},{12,20},{16,8},{20,28},{24,16},{5,13},{9,1},{13,21},{... | collective-permute-start | bytes 786440 | tf_op jit(solution)/shard_map/ppermute | solution.py:621
  15.1 6.1 %collective-permute-start.6 = (f32[2,2,64,128]{3,2,1,0:T(8,128)S(1)}, f32[2,2,64,128]{3,2,1,0:T(8,128)S(1)}, u32[]{:S(2)}, u32[]{:S(2)}) collective-permute-start(f32[2,2,64,128]{3,2,1,0:T(8,128)S(1)} %get-tuple-element.40), channel_id=1, source_target_pairs={{0,8},{8,16},{12,4},{16,24},{20,12},{28,20},{1,9},{9,17},{13,5},{1... | collective-permute-start | bytes 393224 | tf_op jit(solution)/shard_map/ppermute | solution.py:621
  22.3 9.2 %collective-permute-start.7 = (f32[4,32,128]{2,1,0:T(8,128)S(1)}, f32[4,32,128]{2,1,0:T(8,128)S(1)}, u32[]{:S(2)}, u32[]{:S(2)}) collective-permute-start(f32[4,32,128]{2,1,0:T(8,128)S(1)} %get-tuple-element.45.refs_2_), channel_id=1, source_target_pairs={{0,24},{4,28},{8,16},{12,20},{16,8},{20,12},{24,0},{28,4},{1,25},{... | collective-permute-start | bytes 196616 | tf_op jit(solution)/shard_map/ppermute | solution.py:573
  26.9 5.2 %collective-permute-start.8 = (f32[4,32,128]{2,1,0:T(8,128)S(1)}, f32[4,32,128]{2,1,0:T(8,128)S(1)}, u32[]{:S(2)}, u32[]{:S(2)}) collective-permute-start(f32[4,32,128]{2,1,0:T(8,128)S(1)} %get-tuple-element.45.refs_2_), channel_id=1, source_target_pairs={{0,16},{4,20},{8,24},{12,28},{16,0},{20,4},{24,8},{28,12},{1,17},{... | collective-permute-start | bytes 196616 | tf_op jit(solution)/shard_map/ppermute | solution.py:573
  26.9 5.2 %collective-permute-start.9 = (f32[4,32,128]{2,1,0:T(8,128)S(1)}, f32[4,32,128]{2,1,0:T(8,128)S(1)}, u32[]{:S(2)}, u32[]{:S(2)}) collective-permute-start(f32[4,32,128]{2,1,0:T(8,128)S(1)} %get-tuple-element.45.refs_2_), channel_id=1, source_target_pairs={{0,8},{4,12},{8,0},{12,4},{16,24},{20,28},{24,16},{28,20},{1,9},{5... | collective-permute-start | bytes 196616 | tf_op jit(solution)/shard_map/ppermute | solution.py:573
  27.5 6.9 %collective-permute-start.10 = (f32[2,64,128]{2,1,0:T(8,128)S(1)}, f32[2,64,128]{2,1,0:T(8,128)S(1)}, u32[]{:S(2)}, u32[]{:S(2)}) collective-permute-start(f32[2,64,128]{2,1,0:T(8,128)S(1)} %get-tuple-element.46), channel_id=1, source_target_pairs={{0,8},{8,16},{12,4},{16,24},{20,12},{28,20},{1,9},{9,17},{13,5},{1... | collective-permute-start | bytes 196616 | tf_op jit(solution)/shard_map/ppermute | solution.py:621
  35.9 1.6 %collective-permute-start.11 = (f32[520,128]{1,0:T(8,128)S(1)}, f32[520,128]{1,0:T(8,128)S(1)}, u32[]{:S(2)}, u32[]{:S(2)}) collective-permute-start(f32[520,128]{1,0:T(8,128)S(1)} %get-tuple-element.48), channel_id=1, source_target_pairs={{0,1},{1,0},{2,3},{3,2},{4,5},{5,4},{6,7},{7,6},{8,9},{9,8},{10,11... | collective-permute-start | bytes 798728 | tf_op jit(solution)/shard_map/ppermute | solution.py:671
  38.1 13.6 %copy-start.1 = (f32[8,4,16,128]{3,2,1,0:T(8,128)S(1)}, f32[8,4,16,128]{3,2,1,0:T(8,128)}, u32[]{:S(2)}) copy-start(f32[8,4,16,128]{3,2,1,0:T(8,128)} %source_ref.3) | copy-start | bytes 786436
  38.1 5.1 %collective-permute-start.12 = (f32[208,128]{1,0:T(8,128)S(1)}, f32[208,128]{1,0:T(8,128)S(1)}, u32[]{:S(2)}, u32[]{:S(2)}) collective-permute-start(f32[208,128]{1,0:T(8,128)S(1)} %get-tuple-element.50), channel_id=1, source_target_pairs={{0,2},{1,3},{2,0},{3,1},{4,6},{5,7},{6,4},{7,5},{8,10},{9,11},{10,... | collective-permute-start | bytes 319496 | tf_op jit(solution)/shard_map/ppermute | solution.py:564
  39.7 5.9 %collective-permute-start.13 = (f32[208,128]{1,0:T(8,128)S(1)}, f32[208,128]{1,0:T(8,128)S(1)}, u32[]{:S(2)}, u32[]{:S(2)}) collective-permute-start(f32[208,128]{1,0:T(8,128)S(1)} %get-tuple-element.51), channel_id=1, source_target_pairs={{0,4},{1,5},{2,6},{3,7},{4,0},{5,1},{6,2},{7,3},{8,12},{9,13},{10,... | collective-permute-start | bytes 319496 | tf_op jit(solution)/shard_map/ppermute | solution.py:564
  40.9 5.7 %collective-permute-start.14 = (f32[208,128]{1,0:T(8,128)S(1)}, f32[208,128]{1,0:T(8,128)S(1)}, u32[]{:S(2)}, u32[]{:S(2)}) collective-permute-start(f32[208,128]{1,0:T(8,128)S(1)} %get-tuple-element.52), channel_id=1, source_target_pairs={{0,6},{1,7},{2,4},{3,5},{4,2},{5,3},{6,0},{7,1},{8,14},{9,15},{10,... | collective-permute-start | bytes 319496 | tf_op jit(solution)/shard_map/ppermute | solution.py:564
  47.2 5.9 %collective-permute-start.15 = (f32[8,128]{1,0:T(8,128)S(1)}, f32[8,128]{1,0:T(8,128)S(1)}, u32[]{:S(2)}, u32[]{:S(2)}) collective-permute-start(f32[8,128]{1,0:T(8,128)S(1)} %squares.1), channel_id=1, source_target_pairs={{0,24},{4,28},{8,16},{12,20},{16,8},{20,12},{24,0},{28,4},{1,25},{... | collective-permute-start | bytes 12296 | tf_op jit(solution)/shard_map/ppermute | solution.py:573
  50.3 4.5 %collective-permute-start.16 = (f32[8,128]{1,0:T(8,128)S(1)}, f32[8,128]{1,0:T(8,128)S(1)}, u32[]{:S(2)}, u32[]{:S(2)}) collective-permute-start(f32[8,128]{1,0:T(8,128)S(1)} %squares.1), channel_id=1, source_target_pairs={{0,16},{4,20},{8,24},{12,28},{16,0},{20,4},{24,8},{28,12},{1,17},{... | collective-permute-start | bytes 12296 | tf_op jit(solution)/shard_map/ppermute | solution.py:573
  50.3 4.5 %collective-permute-start.17 = (f32[8,128]{1,0:T(8,128)S(1)}, f32[8,128]{1,0:T(8,128)S(1)}, u32[]{:S(2)}, u32[]{:S(2)}) collective-permute-start(f32[8,128]{1,0:T(8,128)S(1)} %squares.1), channel_id=1, source_target_pairs={{0,8},{4,12},{8,0},{12,4},{16,24},{20,28},{24,16},{28,20},{1,9},{5... | collective-permute-start | bytes 12296 | tf_op jit(solution)/shard_map/ppermute | solution.py:573

commit v21 on v20

--- a/solution.py
+++ b/solution.py
@@ -221,7 +221,7 @@
 
 
 def scalars_of(scalar_ref):
-    return scalar_ref[0, 0], [scalar_ref[1 + d, 0] for d in range(3)]
+    return scalar_ref[pl.ds(0, 1), :], [scalar_ref[pl.ds(1 + d, 1), :] for d in range(3)]
 
 
 def zero_rows(v, ny):
@@ -246,15 +246,19 @@
     return -k % count
 
 
-def keep_kernel(place_ref, source_ref, out_ref):
+def keep_kernel(place, source_ref, out_ref):
     for n in range(out_ref.shape[0]):
-        out_ref[n] = source_ref[2 * n + (place_ref[0] & 1)]
-
-
-def merge_kernel(place_ref, shifts_ref, index_ref, velocity_ref, *refs):
-    mine_ref, theirs_ref, reaction_ref, other_reaction_ref = refs[:4]
-    out_refs, scalar_ref = refs[4:-1], refs[-1]
-    chip, core = place_ref[0] // 2, place_ref[0] & 1
+        out_ref[n] = source_ref[2 * n + (place[0] & 1)]
+
+
+def scalars_kernel(place, shifts_ref, index_ref, velocity_ref, scalar_ref):
+    scalars = [shifts_ref[index_ref[place[0]]]] + [velocity_ref[d] for d in range(3)]
+    for n, scalar in enumerate(scalars):
+        scalar_ref[pl.ds(n, 1), :] = jnp.full((1, LANES), scalar, jnp.float32)
+
+
+def merge_kernel(place, mine_ref, theirs_ref, reaction_ref, other_reaction_ref, *out_refs):
+    chip, core = place[0] // 2, place[0] & 1
     by = mine_ref.shape[2]
     mine = pl.ds(pl.multiple_of(core * by, 8), by)
     theirs = pl.ds(pl.multiple_of((1 - core) * by, 8), by)
@@ -264,23 +268,20 @@
         out_ref[0, :, theirs, :] = theirs_ref[2 * target + core]
         out_ref[1, :, mine, :] = reaction_ref[...]
         out_ref[1, :, theirs, :] = other_reaction_ref[...]
-    scalars = [shifts_ref[index_ref[place_ref[0]]]] + [velocity_ref[d] for d in range(3)]
-    for n, scalar in enumerate(scalars):
-        scalar_ref[pl.ds(n, 1), :] = jnp.full((1, LANES), scalar, jnp.float32)
-
-
-def half_kernel(chips_y, place_ref, *refs):
+
+
+def half_kernel(chips_y, place, *refs):
     blocks, half_ref = refs[:-1], refs[-1]
     for m, block in enumerate(blocks):
         size = block.shape[2]
-        chip = jnp.bitwise_xor(place_ref[0] // 2, m)
+        chip = jnp.bitwise_xor(place[0] // 2, m)
         rows = pl.ds(pl.multiple_of(lax.rem(chip, chips_y) * size, 8), size)
         half_ref[:, :, rows, :] = block[...]
 
 
-def arrange_kernel(chips_y, place_ref, *refs):
+def arrange_kernel(chips_y, place, *refs):
     blocks, (slab_ref, near_ref) = refs[:-2], refs[-2:]
-    chip = place_ref[0] // 2
+    chip = place[0] // 2
     for m, block in enumerate(blocks):
         owner = jnp.bitwise_xor(chip, m)
         _, bx, size, _ = block.shape
@@ -291,9 +292,9 @@
     near_ref[...] = slab_ref[:, pl.ds(other * (SLAB - NEAR), NEAR)]
 
 
-def beyond_kernel(slabs, chips_y, place_ref, scalar_ref, half_ref, out_ref, f, r, w, v0):
-    ny, slab = f.shape[1], place_ref[1]
-    x = place_ref[0] // 2 // chips_y
+def beyond_kernel(slabs, chips_y, place, scalar_ref, half_ref, out_ref, f, r, w, v0):
+    ny, slab = f.shape[1], place[1]
+    x = place[0] // 2 // chips_y
     fine = Level(0, ny, LANES, 0, scalars_of(scalar_ref), f, r, w)
     zero_rows(v0, ny)
     f[...], r[...] = half_ref[0], half_ref[1]
@@ -309,7 +310,7 @@
         out_ref[n] = fine.smoothed(v0, 1 + n)
 
 
-def begin_kernel(scalar_ref, slab_ref, f, r, w, v0, v1):
+def begin_kernel(_, scalar_ref, slab_ref, f, r, w, v0, v1):
     ny = f.shape[1]
     fine = Level(0, ny, LANES, 0, scalars_of(scalar_ref), f, r, w)
     zero_rows(v0, ny)
@@ -325,15 +326,15 @@
     fine.smooth(v0, v1, own[1:-1])
 
 
-def pre_kernel(slabs, chips_y, place_ref, scalar_ref, *refs):
+def pre_kernel(slabs, chips_y, place, scalar_ref, *refs):
     half_ref, near_ref, pool_ref, pool_up_ref = refs[5:9]
     f, r, w, v0, v1, coarse_ref, beyond_ref, tmp, pooled = refs[9:]
     ny = f.shape[1]
-    slab = place_ref[1]
+    slab = place[1]
     fine = Level(0, ny, LANES, 0, scalars_of(scalar_ref), f, r, w)
     after = HALO + SLAB
 
-    x = place_ref[0] // 2 // chips_y
+    x = place[0] // 2 // chips_y
     for above, ref, first in ((1 - x, half_ref, x * NEAR), (x, near_ref, 0)):
         planes = pl.ds((HALO - NEAR) + above * (SLAB + NEAR), NEAR)
         f[planes], r[planes] = ref[0, pl.ds(first, NEAR)], ref[1, pl.ds(first, NEAR)]
@@ -365,13 +366,13 @@
     beyond_ref[...] = v1[pl.ds(first, NEAR), pl.ds(8, ny), :]
 
 
-def coarse_kernel(grid, place_ref, scalar_ref, *refs):
+def coarse_kernel(grid, place, scalar_ref, *refs):
     slabs, nx, ny, nz = grid
     pool_ref, spread_ref = refs[:2]
     coarse, out_ref = refs[2 : 2 + slabs], refs[2 + slabs]
     f1, r1, w1, v1a, v1b, pooled, tmp = refs[3 + slabs :]
     pool, spread = pool_ref[...], spread_ref[...]
-    slab = place_ref[1]
+    slab = place[1]
     rim = HALO // 2
     nx1, ny1, nx2, ny2 = nx // 2, ny // 2, nx // 4, ny // 4
     mid = Level(1, ny1, nz // 2, rim, scalars_of(scalar_ref), f1, r1, w1)
@@ -430,13 +431,13 @@
     out_ref[...] = split_dot(values, spread)
 
 
-def post_kernel(by, chips_y, place_ref, scalar_ref, *refs):
+def post_kernel(by, chips_y, place, scalar_ref, *refs):
     f, r, w, v1, correction, first_ref, second_ref, kept_ref, sent_ref, va, vb, tmp = refs
     count, ny = f.shape[:2]
     fine = Level(0, ny, LANES, 0, scalars_of(scalar_ref), f, r, w)
     for v in (va, vb):
         zero_rows(v, ny)
-    x, half = place_ref[0] // 2 // chips_y, ny // 2
+    x, half = place[0] // 2 // chips_y, ny // 2
     window = correction.shape[0] // half
     for ref, above in ((first_ref, 1 - x), (second_ref, x)):
         va[pl.ds(1 + above * (SLAB + HALO), NEAR), pl.ds(8, ny), :] = ref[...]
@@ -462,7 +463,7 @@
         tmp[x] = rest
     squares = jnp.full((8, LANES), jnp.sum(total), jnp.float32)
 
-    core, area = place_ref[0] & 1, half * SLAB
+    core, area = place[0] & 1, half * SLAB
     for ref, first in ((kept_ref, core * by), (sent_ref, (1 - core) * by)):
         for y in range(half // by):
             row = pl.multiple_of(2 * y * by + first, 8)
@@ -480,8 +481,8 @@
     return outer, edges, squares, (squares + 8) // 8 * 8
 
 
-def merge_back_kernel(bx, by, chips_y, place_ref, kept_ref, got_ref, *out_refs):
-    chip, core = place_ref[0] // 2, place_ref[0] & 1
+def merge_back_kernel(bx, by, chips_y, place, kept_ref, got_ref, *out_refs):
+    chip, core = place[0] // 2, place[0] & 1
     half = chips_y * by
     outer, edges, squares, size = part_rows(bx, by)
     for m, out_ref in enumerate(out_refs):
@@ -503,14 +504,14 @@
             out_ref[pl.ds(base + squares, 1), :] = ref[pl.ds(2 * SLAB * half, 1), :]
 
 
-def collect_kernel(place_ref, shifts_ref, index_ref, velocity_ref, source_ref, reaction_ref, *refs):
+def collect_kernel(place, shifts_ref, index_ref, velocity_ref, source_ref, reaction_ref, *refs):
     parts, (iterate_ref, residual_ref) = refs[:-2], refs[-2:]
     _, bx, by, nz = iterate_ref.shape
     outer, edges, _, size = part_rows(bx, by)
     fine = Level(0, by, nz, 0, (0.0, [velocity_ref[d] for d in range(3)]), None, None, None)
     reaction = [reaction_ref[p] + fine.centre for p in range(1, bx - 1)]
     for m, part in enumerate(parts):
-        target = jnp.bitwise_xor(place_ref[0] // 2, m)
+        target = jnp.bitwise_xor(place[0] // 2, m)
         for n in range(2):
             base, column = n * size, 2 * target + n
             shift = shifts_ref[index_ref[column]]
@@ -530,11 +531,11 @@
                 residual_ref[column, p, pl.ds(by - 1, 1), :] = part[pl.ds(at + 1, 1), :]
 
 
-def squares_kernel(bx, by, place_ref, *refs):
+def squares_kernel(bx, by, place, *refs):
     parts, out_ref = refs[:-1], refs[-1]
     _, _, squares, size = part_rows(bx, by)
     for m, part in enumerate(parts):
-        target = jnp.bitwise_xor(place_ref[0] // 2, m)
+        target = jnp.bitwise_xor(place[0] // 2, m)
         for n in range(2):
             out_ref[pl.ds(2 * target + n, 1), :] = part[pl.ds(n * size + squares, 1), :]
 
@@ -543,14 +544,21 @@
 VMEM = pl.BlockSpec(memory_space=pltpu.VMEM)
 
 
-def local_kernel(kernel, name, scalars, arrays, outs, scratch=(), in_place=0):
+def local_kernel(kernel, name, scalars, arrays, outs, scratch=(), in_place=()):
+    gy_size = lax.axis_size("gy")
+    step = SLAB // HALO
+
+    def placed(*refs):
+        along, across = lax.axis_index("gx"), lax.axis_index("gy")
+        kernel((lax.rem(along, step) * gy_size + across, along // step), *refs)
+
     return pl.pallas_call(
-        kernel,
+        placed,
         out_shape=[jax.ShapeDtypeStruct(shape, jnp.float32) for shape in outs],
         in_specs=[SMEM] * len(scalars) + [VMEM] * len(arrays),
         out_specs=[VMEM] * len(outs),
         scratch_shapes=[pltpu.VMEM(shape, jnp.float32) for shape in scratch],
-        input_output_aliases={len(scalars) + n: n for n in range(in_place)},
+        input_output_aliases={len(scalars) + n: k for k, n in enumerate(in_place)},
         compiler_params=pltpu.CompilerParams(vmem_limit_bytes=VMEM_LIMIT),
         name=name,
     )(*scalars, *arrays)
@@ -580,38 +588,37 @@
     nx, ny = bx * gx_size, by * gy_size
     step = columns // gy_size
     slabs = gx_size // step
-    along, across = lax.axis_index("gx"), lax.axis_index("gy")
-    column = lax.rem(along, step) * gy_size + across
-    place = jnp.stack([column, along // step]).astype(jnp.int32)
     count = SLAB + 2 * HALO
     area = bx * by
 
     chips, chips_y = columns // 2, gy_size // 2
     cores = [(i, i ^ 1) for i in range(gy_size)]
     theirs = [lax.ppermute(source, "gy", cores), lax.ppermute(reaction, "gy", cores)]
-    (mine,) = local_kernel(keep_kernel, "keep", (place,), (source,), [(chips, bx, by, nz)])
-    *blocks, scalar_rows = local_kernel(
+    (mine,) = local_kernel(keep_kernel, "keep", (), (source,), [(chips, bx, by, nz)])
+    (scalar_rows,) = local_kernel(
+        scalars_kernel, "scalars", (shifts, shift_index, velocity), (), [(8, LANES)]
+    )
+    blocks = local_kernel(
         merge_kernel,
         "merge",
-        (place, shifts, shift_index, velocity),
+        (),
         (mine, theirs[0], reaction, theirs[1]),
-        [(2, bx, 2 * by, nz)] * chips + [(8, LANES)],
-    )
-    scalars = (place, scalar_rows)
+        [(2, bx, 2 * by, nz)] * chips,
+    )
     blocks = swap_in_plane(blocks, 2)
 
     edge = (2, NEAR, ny, nz)
     (own_half,) = local_kernel(
         functools.partial(half_kernel, chips_y),
         "half",
-        (place,),
+        (),
         blocks[:chips_y],
         [(2, HALO, ny, nz)],
     )
     slab, near = local_kernel(
         functools.partial(arrange_kernel, chips_y),
         "arrange",
-        (place,),
+        (),
         blocks,
         [(2, SLAB, ny, nz), edge],
     )
@@ -623,21 +630,21 @@
     beside = [send_beside(own_half, 1), send_beside(near, 0)]
     grid, rimmed = (count, ny, nz), (count, ny + 16, nz)
     fields = [grid, grid, grid, rimmed, rimmed]
-    fields_own = local_kernel(begin_kernel, "begin", (scalar_rows,), (slab,), fields)
+    fields_own = local_kernel(begin_kernel, "begin", (), (scalar_rows, slab), fields)
     f, r, w, _, v1, coarse, beyond = local_kernel(
         functools.partial(pre_kernel, slabs, chips_y),
         "pre",
-        scalars,
-        (*fields_own, *beside, pool_matrix(0), pool_matrix(LANES // 2)),
+        (),
+        (scalar_rows, *fields_own, *beside, pool_matrix(0), pool_matrix(LANES // 2)),
         fields + [(SLAB // 2, ny // 2, nz), (NEAR, ny, nz)],
         [(SLAB, ny, nz), (2, SLAB // 2 * ny // 2, nz)],
-        in_place=len(fields),
+        in_place=range(1, 1 + len(fields)),
     )
     (own_beyond,) = local_kernel(
         functools.partial(beyond_kernel, slabs, chips_y),
         "beyond",
-        scalars,
-        beside[:1],
+        (),
+        (scalar_rows, beside[0]),
         [(NEAR, ny, nz)],
         [(HALO, ny, nz)] * 3 + [(HALO, ny + 16, nz)],
     )
@@ -649,8 +656,8 @@
     (correction,) = local_kernel(
         functools.partial(coarse_kernel, (slabs, nx, ny, nz)),
         "coarse",
-        scalars,
-        (pool_matrix(0), spread_matrix(), *gathered),
+        (),
+        (scalar_rows, pool_matrix(0), spread_matrix(), *gathered),
         [(window, nz)],
         [coarse_grid] * 3 + [coarse_rimmed] * 2 + [(nx // 4 * ny // 2, nz), (nx // 2, ny // 2, nz)],
     )
@@ -658,8 +665,8 @@
     kept, sent = local_kernel(
         functools.partial(post_kernel, by, chips_y),
         "post",
-        scalars,
-        (f, r, w, v1, correction, own_beyond, send_beside(beyond, 0)),
+        (),
+        (scalar_rows, f, r, w, v1, correction, own_beyond, send_beside(beyond, 0)),
         [result, result],
         [rimmed] * 2 + [(SLAB, ny, nz)],
     )
@@ -667,18 +674,18 @@
     parts = local_kernel(
         functools.partial(merge_back_kernel, bx, by, chips_y),
         "merge_back",
-        (place,),
+        (),
         (kept, lax.ppermute(sent, "gy", cores)),
         [(2 * part_rows(bx, by)[3], nz)] * chips,
     )
     parts = swap_in_plane(parts, 2)
     (squares,) = local_kernel(
-        functools.partial(squares_kernel, bx, by), "squares", (place,), parts, [(columns, nz)]
+        functools.partial(squares_kernel, bx, by), "squares", (), parts, [(columns, nz)]
     )
     iterate, residual = local_kernel(
         collect_kernel,
         "collect",
-        (place, shifts, shift_index, velocity),
+        (shifts, shift_index, velocity),
         (source, reaction, *parts),
         [source.shape] * 2,
     )

time: 55.7 us -> 52.1 us (0.935)
  Pallas kernels: 11.4 us -> 5.67 us
  waiting for transfers between devices: 14.6 us -> 16.6 us
    pallas_call x12 -> x13, Pallas kernels: 11.4 us -> 5.67 us  [local_kernel(): pl.pallas_call(placed, out_shape=[jax.ShapeDtypeStruct(shape, jnp.float32...]
    ppermute x6, waiting for transfers between devices: 2.19 us -> 2.88 us  [swap_slabs(): moved.append(lax.ppermute(piece, 'gx', pairs))]
    ppermute x3, waiting for transfers between devices: 1.55 us -> 2.15 us  [send_beside(): lax.ppermute(piece, 'gx', [(i, j) for i, j in pairs if 0 <= j < gx_size])]
  transfers between devices with their start and end apart: 18 -> 18, of which waited for: 10 -> 11; matrix products, arithmetic and copies ran while one was open for 0% -> 0% of each run, Pallas kernels for 13% -> 8%
where the time goes in v21:
time: 52.1 us; the launch traced here: 51.9 us
  starting transfers between devices  26.7 us (51%)
  waiting for transfers between devices  16.6 us (32%)
  Pallas kernels  5.67 us (11%)
  local copies, waits for them, and re-layouts  1.34 us (3%)
  between operations  0.84 us (2%)
  other arithmetic  0.77 us (1%)
    ppermute x6, waiting for transfers between devices, swap_in_plane(): moved.append(lax.ppermute(pieces[k], ('gx', 'gy'), pairs))  9.63 us
    ppermute x6, starting transfers between devices, swap_slabs(): moved.append(lax.ppermute(piece, 'gx', pairs))  9.57 us
    ppermute x3, starting transfers between devices, send_beside(): lax.ppermute(piece, 'gx', [(i, j) for i, j in pairs if 0 <= j < gx_size])  8.34 us
    ppermute x6, starting transfers between devices, swap_in_plane(): moved.append(lax.ppermute(pieces[k], ('gx', 'gy'), pairs))  8.1 us
    pallas_call x13, Pallas kernels, local_kernel(): pl.pallas_call(placed, out_shape=[jax.ShapeDtypeStruct(shape, jnp.float32...  5.67 us
    ppermute x6, waiting for transfers between devices, swap_slabs(): moved.append(lax.ppermute(piece, 'gx', pairs))  2.88 us
    ppermute x3, waiting for transfers between devices, send_beside(): lax.ppermute(piece, 'gx', [(i, j) for i, j in pairs if 0 <= j < gx_size])  2.15 us
    ppermute x1, waiting for transfers between devices, column_body(): lax.ppermute(sent, 'gy', cores)  1.53 us
  transfers between devices with their start and end apart: 18, of which 11 were waited for; matrix products, arithmetic and copies ran while one was open for 0% of the time, Pallas kernels for 8%

profile of v21, /device:TPU:0, one launch (start us, length us, event | category | flops | bytes accessed | tf_op | source)
XLA Modules:
  0.0 51.9 jit_solution(18224647918725752694)
XLA Ops:
  1.2 0.9 %copy-done = f32[8,4,16,128]{3,2,1,0:T(8,128)S(1)} copy-done((f32[8,4,16,128]{3,2,1,0:T(8,128)S(1)}, f32[8,4,16,128]{3,2,1,0:T(8,128)}, u32[]{:S(2)}) %copy-start) | copy-done | bytes 262168
  3.0 3.0 %collective-permute-start.2 = (f32[2,4,32,128]{3,2,1,0:T(8,128)S(1)}, f32[2,4,32,128]{3,2,1,0:T(8,128)S(1)}, u32[]{:S(2)}, u32[]{:S(2)}) collective-permute-start(f32[2,4,32,128]{3,2,1,0:T(8,128)S(1)} %get-tuple-element.29), channel_id=1, source_target_pairs={{0,2},{1,3},{2,0},{3,1},{4,6},{5,7},{6,4},{7,5},{8,10},{9,11},{10,... | collective-permute-start | bytes 393224 | tf_op jit(solution)/shard_map/ppermute | solution.py:572
  6.0 1.5 %collective-permute-start.3 = (f32[2,4,32,128]{3,2,1,0:T(8,128)S(1)}, f32[2,4,32,128]{3,2,1,0:T(8,128)S(1)}, u32[]{:S(2)}, u32[]{:S(2)}) collective-permute-start(f32[2,4,32,128]{3,2,1,0:T(8,128)S(1)} %get-tuple-element.30), channel_id=1, source_target_pairs={{0,4},{1,5},{2,6},{3,7},{4,0},{5,1},{6,2},{7,3},{8,12},{9,13},{10,... | collective-permute-start | bytes 393224 | tf_op jit(solution)/shard_map/ppermute | solution.py:572
  7.5 2.2 %collective-permute-done.2.refs_1_ = f32[2,4,32,128]{3,2,1,0:T(8,128)S(1)} collective-permute-done((f32[2,4,32,128]{3,2,1,0:T(8,128)S(1)}, f32[2,4,32,128]{3,2,1,0:T(8,128)S(1)}, u32[]{:S(2)}, u32[]{:S(2)}) %collective-permute-start.2) | collective-permute-done | bytes 131104 | tf_op jit(solution)/shard_map/ppermute | solution.py:572
  9.8 1.4 %collective-permute-start.5 = (f32[2,4,64,128]{3,2,1,0:T(8,128)S(1)}, f32[2,4,64,128]{3,2,1,0:T(8,128)S(1)}, u32[]{:S(2)}, u32[]{:S(2)}) collective-permute-start(f32[2,4,64,128]{3,2,1,0:T(8,128)S(1)} %half.1), channel_id=1, source_target_pairs={{4,12},{8,0},{12,20},{16,8},{20,28},{24,16},{5,13},{9,1},{13,21},{... | collective-permute-start | bytes 786440 | tf_op jit(solution)/shard_map/ppermute | solution.py:628
  12.4 1.4 %collective-permute-done.4.refs_3_ = f32[2,4,32,128]{3,2,1,0:T(8,128)S(1)} collective-permute-done((f32[2,4,32,128]{3,2,1,0:T(8,128)S(1)}, f32[2,4,32,128]{3,2,1,0:T(8,128)S(1)}, u32[]{:S(2)}, u32[]{:S(2)}) %collective-permute-start.4) | collective-permute-done | bytes 131104 | tf_op jit(solution)/shard_map/ppermute | solution.py:572
  13.9 3.6 %collective-permute-start.6 = (f32[2,2,64,128]{3,2,1,0:T(8,128)S(1)}, f32[2,2,64,128]{3,2,1,0:T(8,128)S(1)}, u32[]{:S(2)}, u32[]{:S(2)}) collective-permute-start(f32[2,2,64,128]{3,2,1,0:T(8,128)S(1)} %get-tuple-element.38), channel_id=1, source_target_pairs={{0,8},{8,16},{12,4},{16,24},{20,12},{28,20},{1,9},{9,17},{13,5},{1... | collective-permute-start | bytes 393224 | tf_op jit(solution)/shard_map/ppermute | solution.py:628
  17.9 2.1 %collective-permute-done.6.refs_7_ = f32[2,2,64,128]{3,2,1,0:T(8,128)S(1)} collective-permute-done((f32[2,2,64,128]{3,2,1,0:T(8,128)S(1)}, f32[2,2,64,128]{3,2,1,0:T(8,128)S(1)}, u32[]{:S(2)}, u32[]{:S(2)}) %collective-permute-start.6) | collective-permute-done | bytes 131104 | tf_op jit(solution)/shard_map/ppermute | solution.py:628
  20.5 4.5 %collective-permute-start.7 = (f32[4,32,128]{2,1,0:T(8,128)S(1)}, f32[4,32,128]{2,1,0:T(8,128)S(1)}, u32[]{:S(2)}, u32[]{:S(2)}) collective-permute-start(f32[4,32,128]{2,1,0:T(8,128)S(1)} %get-tuple-element.43.refs_3_), channel_id=1, source_target_pairs={{0,24},{4,28},{8,16},{12,20},{16,8},{20,12},{24,0},{28,4},{1,25},{... | collective-permute-start | bytes 196616 | tf_op jit(solution)/shard_map/ppermute | solution.py:581
  25.1 0.6 %collective-permute-start.9 = (f32[4,32,128]{2,1,0:T(8,128)S(1)}, f32[4,32,128]{2,1,0:T(8,128)S(1)}, u32[]{:S(2)}, u32[]{:S(2)}) collective-permute-start(f32[4,32,128]{2,1,0:T(8,128)S(1)} %get-tuple-element.43.refs_3_), channel_id=1, source_target_pairs={{0,8},{4,12},{8,0},{12,4},{16,24},{20,28},{24,16},{28,20},{1,9},{5... | collective-permute-start | bytes 196616 | tf_op jit(solution)/shard_map/ppermute | solution.py:581
  25.7 3.3 %collective-permute-start.10 = (f32[2,64,128]{2,1,0:T(8,128)S(1)}, f32[2,64,128]{2,1,0:T(8,128)S(1)}, u32[]{:S(2)}, u32[]{:S(2)}) collective-permute-start(f32[2,64,128]{2,1,0:T(8,128)S(1)} %get-tuple-element.44), channel_id=1, source_target_pairs={{0,8},{8,16},{12,4},{16,24},{20,12},{28,20},{1,9},{9,17},{13,5},{1... | collective-permute-start | bytes 196616 | tf_op jit(solution)/shard_map/ppermute | solution.py:628
  29.2 1.1 %collective-permute-done.8.refs_5_ = f32[4,32,128]{2,1,0:T(8,128)S(1)} collective-permute-done((f32[4,32,128]{2,1,0:T(8,128)S(1)}, f32[4,32,128]{2,1,0:T(8,128)S(1)}, u32[]{:S(2)}, u32[]{:S(2)}) %collective-permute-start.8) | collective-permute-done | bytes 65568 | tf_op jit(solution)/shard_map/ppermute | solution.py:581
  30.2 1.7 %coarse.1.refs_5_ = f32[256,128]{1,0:T(8,128)S(1)} custom-call(f32[8,128]{1,0:T(8,128)S(1)} %scalars.1.refs_0_, bf16[128,128]{1,0:T(8,128)(2,1)S(1)} %get-tuple-element.54.refs_8_.refs_1_, bf16[128,128]{1,0:T(8,128)(2,1)S(1)} %get-tuple-element.53.refs_2_, f32[4,32,128]{2,1,0:T(8,128)S(1)} %get-tuple-element.43.refs_3_, ...), custom_call_target="tpu_custom_call" | custom-call | tf_op jit(solution)/shard_map/coarse/pallas_call | solution.py:555
  32.0 0.9 %post.1 = (f32[520,128]{1,0:T(8,128)S(1)}, f32[520,128]{1,0:T(8,128)S(1)}) custom-call(f32[8,128]{1,0:T(8,128)S(1)} %scalars.1.refs_0_, f32[16,64,128]{2,1,0:T(8,128)S(1)} %get-tuple-element.39.refs_1_, f32[16,64,128]{2,1,0:T(8,128)S(1)} %get-tuple-element.40.refs_2_, f32[16,64,128]{2,1,0:T(8,128)S(1)} %get-tuple-element.41.refs_3_, ...), custom_call_target="tpu_custom_call" | custom-call | tf_op jit(solution)/shard_map/post/pallas_call | solution.py:555
  33.0 1.5 %collective-permute-done.11.refs_1_ = f32[520,128]{1,0:T(8,128)S(1)} collective-permute-done((f32[520,128]{1,0:T(8,128)S(1)}, f32[520,128]{1,0:T(8,128)S(1)}, u32[]{:S(2)}, u32[]{:S(2)}) %collective-permute-start.11) | collective-permute-done | bytes 266272 | tf_op jit(solution)/shard_map/ppermute | solution.py:678
  34.6 1.6 %collective-permute-start.12 = (f32[208,128]{1,0:T(8,128)S(1)}, f32[208,128]{1,0:T(8,128)S(1)}, u32[]{:S(2)}, u32[]{:S(2)}) collective-permute-start(f32[208,128]{1,0:T(8,128)S(1)} %get-tuple-element.48), channel_id=1, source_target_pairs={{0,2},{1,3},{2,0},{3,1},{4,6},{5,7},{6,4},{7,5},{8,10},{9,11},{10,... | collective-permute-start | bytes 319496 | tf_op jit(solution)/shard_map/ppermute | solution.py:572
  36.2 1.9 %collective-permute-start.13 = (f32[208,128]{1,0:T(8,128)S(1)}, f32[208,128]{1,0:T(8,128)S(1)}, u32[]{:S(2)}, u32[]{:S(2)}) collective-permute-start(f32[208,128]{1,0:T(8,128)S(1)} %get-tuple-element.49), channel_id=1, source_target_pairs={{0,4},{1,5},{2,6},{3,7},{4,0},{5,1},{6,2},{7,3},{8,12},{9,13},{10,... | collective-permute-start | bytes 319496 | tf_op jit(solution)/shard_map/ppermute | solution.py:572
  38.1 1.5 %collective-permute-done.12.refs_6_.refs_1_ = f32[208,128]{1,0:T(8,128)S(1)} collective-permute-done((f32[208,128]{1,0:T(8,128)S(1)}, f32[208,128]{1,0:T(8,128)S(1)}, u32[]{:S(2)}, u32[]{:S(2)}) %collective-permute-start.12) | collective-permute-done | bytes 106528 | tf_op jit(solution)/shard_map/ppermute | solution.py:572
  39.6 2.2 %collective-permute-done.13.refs_7_.refs_2_ = f32[208,128]{1,0:T(8,128)S(1)} collective-permute-done((f32[208,128]{1,0:T(8,128)S(1)}, f32[208,128]{1,0:T(8,128)S(1)}, u32[]{:S(2)}, u32[]{:S(2)}) %collective-permute-start.13) | collective-permute-done | bytes 106528 | tf_op jit(solution)/shard_map/ppermute | solution.py:572
  41.9 1.7 %collective-permute-done.14.refs_8_.refs_3_ = f32[208,128]{1,0:T(8,128)S(1)} collective-permute-done((f32[208,128]{1,0:T(8,128)S(1)}, f32[208,128]{1,0:T(8,128)S(1)}, u32[]{:S(2)}, u32[]{:S(2)}) %collective-permute-start.14) | collective-permute-done | bytes 106528 | tf_op jit(solution)/shard_map/ppermute | solution.py:572
  43.6 3.1 %collective-permute-start.15 = (f32[8,128]{1,0:T(8,128)S(1)}, f32[8,128]{1,0:T(8,128)S(1)}, u32[]{:S(2)}, u32[]{:S(2)}) collective-permute-start(f32[8,128]{1,0:T(8,128)S(1)} %squares.1), channel_id=1, source_target_pairs={{0,24},{4,28},{8,16},{12,20},{16,8},{20,12},{24,0},{28,4},{1,25},{... | collective-permute-start | bytes 12296 | tf_op jit(solution)/shard_map/ppermute | solution.py:581
  46.7 1.3 %collective-permute-start.17 = (f32[8,128]{1,0:T(8,128)S(1)}, f32[8,128]{1,0:T(8,128)S(1)}, u32[]{:S(2)}, u32[]{:S(2)}) collective-permute-start(f32[8,128]{1,0:T(8,128)S(1)} %squares.1), channel_id=1, source_target_pairs={{0,8},{4,12},{8,0},{12,4},{16,24},{20,28},{24,16},{28,20},{1,9},{5... | collective-permute-start | bytes 12296 | tf_op jit(solution)/shard_map/ppermute | solution.py:581
  48.0 1.4 %collect.1 = (f32[8,4,16,128]{3,2,1,0:T(8,128)}, f32[8,4,16,128]{3,2,1,0:T(8,128)}) custom-call(f32[8]{0:T(128)S(1)} %copy-done.3, s32[8]{0:T(128)S(1)} %copy-done.4, f32[3]{0:T(128)S(1)} %copy-done.5, f32[8,4,16,128]{3,2,1,0:T(8,128)S(1)} %copy-done.1, f32[4,16,128]{2,1,0:T(8,128)S(1)} %copy-done.2, f32[208,128]{1,0:T(8,128)S(1)} %get-tuple-element.47.refs_5_.refs_0_, ...), custom_call_target="tpu_custom_call" | custom-call | tf_op jit(solution)/shard_map/collect/pallas_call | solution.py:555
  49.4 1.8 %collective-permute-done.16 = f32[8,128]{1,0:T(8,128)S(1)} collective-permute-done((f32[8,128]{1,0:T(8,128)S(1)}, f32[8,128]{1,0:T(8,128)S(1)}, u32[]{:S(2)}, u32[]{:S(2)}) %collective-permute-start.16) | collective-permute-done | bytes 4128 | tf_op jit(solution)/shard_map/ppermute | solution.py:581
  (42 shorter events, 4.5 us)
Async XLA Ops:
  0.6 1.9 %collective-permute-start = (f32[8,4,16,128]{3,2,1,0:T(8,128)}, f32[8,4,16,128]{3,2,1,0:T(8,128)S(1)}, u32[]{:S(2)}, u32[]{:S(2)}) collective-permute-start(f32[8,4,16,128]{3,2,1,0:T(8,128)} %refs_3_.1), channel_id=1, source_target_pairs={{0,1},{1,0},{2,3},{3,2},{4,5},{5,4},{6,7},{7,6},{8,9},{9,8},{10,11... | collective-permute-start | bytes 786440 | tf_op jit(solution)/shard_map/ppermute | solution.py:596
  1.1 1.4 %collective-permute-start.1 = (f32[4,16,128]{2,1,0:T(8,128)}, f32[4,16,128]{2,1,0:T(8,128)S(1)}, u32[]{:S(2)}, u32[]{:S(2)}) collective-permute-start(f32[4,16,128]{2,1,0:T(8,128)} %refs_4_.1), channel_id=1, source_target_pairs={{0,1},{1,0},{2,3},{3,2},{4,5},{5,4},{6,7},{7,6},{8,9},{9,8},{10,11... | collective-permute-start | bytes 98312 | tf_op jit(solution)/shard_map/ppermute | solution.py:596
  1.2 0.9 %copy-start = (f32[8,4,16,128]{3,2,1,0:T(8,128)S(1)}, f32[8,4,16,128]{3,2,1,0:T(8,128)}, u32[]{:S(2)}) copy-start(f32[8,4,16,128]{3,2,1,0:T(8,128)} %refs_3_.1) | copy-start | bytes 786436
  2.2 0.8 %copy-start.2 = (f32[4,16,128]{2,1,0:T(8,128)S(1)}, f32[4,16,128]{2,1,0:T(8,128)}, u32[]{:S(2)}) copy-start(f32[4,16,128]{2,1,0:T(8,128)} %refs_4_.1) | copy-start | bytes 98308
  3.0 6.8 %collective-permute-start.2 = (f32[2,4,32,128]{3,2,1,0:T(8,128)S(1)}, f32[2,4,32,128]{3,2,1,0:T(8,128)S(1)}, u32[]{:S(2)}, u32[]{:S(2)}) collective-permute-start(f32[2,4,32,128]{3,2,1,0:T(8,128)S(1)} %get-tuple-element.29), channel_id=1, source_target_pairs={{0,2},{1,3},{2,0},{3,1},{4,6},{5,7},{6,4},{7,5},{8,10},{9,11},{10,... | collective-permute-start | bytes 393224 | tf_op jit(solution)/shard_map/ppermute | solution.py:572
  6.0 6.4 %collective-permute-start.3 = (f32[2,4,32,128]{3,2,1,0:T(8,128)S(1)}, f32[2,4,32,128]{3,2,1,0:T(8,128)S(1)}, u32[]{:S(2)}, u32[]{:S(2)}) collective-permute-start(f32[2,4,32,128]{3,2,1,0:T(8,128)S(1)} %get-tuple-element.30), channel_id=1, source_target_pairs={{0,4},{1,5},{2,6},{3,7},{4,0},{5,1},{6,2},{7,3},{8,12},{9,13},{10,... | collective-permute-start | bytes 393224 | tf_op jit(solution)/shard_map/ppermute | solution.py:572
  7.5 6.3 %collective-permute-start.4 = (f32[2,4,32,128]{3,2,1,0:T(8,128)S(1)}, f32[2,4,32,128]{3,2,1,0:T(8,128)S(1)}, u32[]{:S(2)}, u32[]{:S(2)}) collective-permute-start(f32[2,4,32,128]{3,2,1,0:T(8,128)S(1)} %get-tuple-element.31), channel_id=1, source_target_pairs={{0,6},{1,7},{2,4},{3,5},{4,2},{5,3},{6,0},{7,1},{8,14},{9,15},{10,... | collective-permute-start | bytes 393224 | tf_op jit(solution)/shard_map/ppermute | solution.py:572
  9.8 1.5 %copy-start.3 = (f32[8]{0:T(128)S(1)}, f32[8]{0:T(128)}, u32[]{:S(2)}) copy-start(f32[8]{0:T(128)} %refs_0_.5) | copy-start | bytes 100
  9.8 1.5 %copy-start.4 = (s32[8]{0:T(128)S(1)}, s32[8]{0:T(128)}, u32[]{:S(2)}) copy-start(s32[8]{0:T(128)} %refs_1_.3) | copy-start | bytes 100
  9.8 1.5 %copy-start.5 = (f32[3]{0:T(128)S(1)}, f32[3]{0:T(128)}, u32[]{:S(2)}) copy-start(f32[3]{0:T(128)} %refs_2_.5) | copy-start | bytes 40
  9.8 10.2 %collective-permute-start.5 = (f32[2,4,64,128]{3,2,1,0:T(8,128)S(1)}, f32[2,4,64,128]{3,2,1,0:T(8,128)S(1)}, u32[]{:S(2)}, u32[]{:S(2)}) collective-permute-start(f32[2,4,64,128]{3,2,1,0:T(8,128)S(1)} %half.1), channel_id=1, source_target_pairs={{4,12},{8,0},{12,20},{16,8},{20,28},{24,16},{5,13},{9,1},{13,21},{... | collective-permute-start | bytes 786440 | tf_op jit(solution)/shard_map/ppermute | solution.py:628
  13.9 6.1 %collective-permute-start.6 = (f32[2,2,64,128]{3,2,1,0:T(8,128)S(1)}, f32[2,2,64,128]{3,2,1,0:T(8,128)S(1)}, u32[]{:S(2)}, u32[]{:S(2)}) collective-permute-start(f32[2,2,64,128]{3,2,1,0:T(8,128)S(1)} %get-tuple-element.38), channel_id=1, source_target_pairs={{0,8},{8,16},{12,4},{16,24},{20,12},{28,20},{1,9},{9,17},{13,5},{1... | collective-permute-start | bytes 393224 | tf_op jit(solution)/shard_map/ppermute | solution.py:628
  20.5 8.6 %collective-permute-start.7 = (f32[4,32,128]{2,1,0:T(8,128)S(1)}, f32[4,32,128]{2,1,0:T(8,128)S(1)}, u32[]{:S(2)}, u32[]{:S(2)}) collective-permute-start(f32[4,32,128]{2,1,0:T(8,128)S(1)} %get-tuple-element.43.refs_3_), channel_id=1, source_target_pairs={{0,24},{4,28},{8,16},{12,20},{16,8},{20,12},{24,0},{28,4},{1,25},{... | collective-permute-start | bytes 196616 | tf_op jit(solution)/shard_map/ppermute | solution.py:581
  25.1 5.2 %collective-permute-start.8 = (f32[4,32,128]{2,1,0:T(8,128)S(1)}, f32[4,32,128]{2,1,0:T(8,128)S(1)}, u32[]{:S(2)}, u32[]{:S(2)}) collective-permute-start(f32[4,32,128]{2,1,0:T(8,128)S(1)} %get-tuple-element.43.refs_3_), channel_id=1, source_target_pairs={{0,16},{4,20},{8,24},{12,28},{16,0},{20,4},{24,8},{28,12},{1,17},{... | collective-permute-start | bytes 196616 | tf_op jit(solution)/shard_map/ppermute | solution.py:581
  25.1 5.2 %collective-permute-start.9 = (f32[4,32,128]{2,1,0:T(8,128)S(1)}, f32[4,32,128]{2,1,0:T(8,128)S(1)}, u32[]{:S(2)}, u32[]{:S(2)}) collective-permute-start(f32[4,32,128]{2,1,0:T(8,128)S(1)} %get-tuple-element.43.refs_3_), channel_id=1, source_target_pairs={{0,8},{4,12},{8,0},{12,4},{16,24},{20,28},{24,16},{28,20},{1,9},{5... | collective-permute-start | bytes 196616 | tf_op jit(solution)/shard_map/ppermute | solution.py:581
  25.7 6.3 %collective-permute-start.10 = (f32[2,64,128]{2,1,0:T(8,128)S(1)}, f32[2,64,128]{2,1,0:T(8,128)S(1)}, u32[]{:S(2)}, u32[]{:S(2)}) collective-permute-start(f32[2,64,128]{2,1,0:T(8,128)S(1)} %get-tuple-element.44), channel_id=1, source_target_pairs={{0,8},{8,16},{12,4},{16,24},{20,12},{28,20},{1,9},{9,17},{13,5},{1... | collective-permute-start | bytes 196616 | tf_op jit(solution)/shard_map/ppermute | solution.py:628
  32.9 1.6 %collective-permute-start.11 = (f32[520,128]{1,0:T(8,128)S(1)}, f32[520,128]{1,0:T(8,128)S(1)}, u32[]{:S(2)}, u32[]{:S(2)}) collective-permute-start(f32[520,128]{1,0:T(8,128)S(1)} %get-tuple-element.46), channel_id=1, source_target_pairs={{0,1},{1,0},{2,3},{3,2},{4,5},{5,4},{6,7},{7,6},{8,9},{9,8},{10,11... | collective-permute-start | bytes 798728 | tf_op jit(solution)/shard_map/ppermute | solution.py:678
  34.6 13.5 %copy-start.1 = (f32[8,4,16,128]{3,2,1,0:T(8,128)S(1)}, f32[8,4,16,128]{3,2,1,0:T(8,128)}, u32[]{:S(2)}) copy-start(f32[8,4,16,128]{3,2,1,0:T(8,128)} %refs_3_.1) | copy-start | bytes 786436
  34.6 5.1 %collective-permute-start.12 = (f32[208,128]{1,0:T(8,128)S(1)}, f32[208,128]{1,0:T(8,128)S(1)}, u32[]{:S(2)}, u32[]{:S(2)}) collective-permute-start(f32[208,128]{1,0:T(8,128)S(1)} %get-tuple-element.48), channel_id=1, source_target_pairs={{0,2},{1,3},{2,0},{3,1},{4,6},{5,7},{6,4},{7,5},{8,10},{9,11},{10,... | collective-permute-start | bytes 319496 | tf_op jit(solution)/shard_map/ppermute | solution.py:572
  36.2 5.7 %collective-permute-start.13 = (f32[208,128]{1,0:T(8,128)S(1)}, f32[208,128]{1,0:T(8,128)S(1)}, u32[]{:S(2)}, u32[]{:S(2)}) collective-permute-start(f32[208,128]{1,0:T(8,128)S(1)} %get-tuple-element.49), channel_id=1, source_target_pairs={{0,4},{1,5},{2,6},{3,7},{4,0},{5,1},{6,2},{7,3},{8,12},{9,13},{10,... | collective-permute-start | bytes 319496 | tf_op jit(solution)/shard_map/ppermute | solution.py:572
  38.0 5.6 %collective-permute-start.14 = (f32[208,128]{1,0:T(8,128)S(1)}, f32[208,128]{1,0:T(8,128)S(1)}, u32[]{:S(2)}, u32[]{:S(2)}) collective-permute-start(f32[208,128]{1,0:T(8,128)S(1)} %get-tuple-element.50), channel_id=1, source_target_pairs={{0,6},{1,7},{2,4},{3,5},{4,2},{5,3},{6,0},{7,1},{8,14},{9,15},{10,... | collective-permute-start | bytes 319496 | tf_op jit(solution)/shard_map/ppermute | solution.py:572
  43.6 5.8 %collective-permute-start.15 = (f32[8,128]{1,0:T(8,128)S(1)}, f32[8,128]{1,0:T(8,128)S(1)}, u32[]{:S(2)}, u32[]{:S(2)}) collective-permute-start(f32[8,128]{1,0:T(8,128)S(1)} %squares.1), channel_id=1, source_target_pairs={{0,24},{4,28},{8,16},{12,20},{16,8},{20,12},{24,0},{28,4},{1,25},{... | collective-permute-start | bytes 12296 | tf_op jit(solution)/shard_map/ppermute | solution.py:581
  46.7 4.5 %collective-permute-start.16 = (f32[8,128]{1,0:T(8,128)S(1)}, f32[8,128]{1,0:T(8,128)S(1)}, u32[]{:S(2)}, u32[]{:S(2)}) collective-permute-start(f32[8,128]{1,0:T(8,128)S(1)} %squares.1), channel_id=1, source_target_pairs={{0,16},{4,20},{8,24},{12,28},{16,0},{20,4},{24,8},{28,12},{1,17},{... | collective-permute-start | bytes 12296 | tf_op jit(solution)/shard_map/ppermute | solution.py:581
  46.7 4.5 %collective-permute-start.17 = (f32[8,128]{1,0:T(8,128)S(1)}, f32[8,128]{1,0:T(8,128)S(1)}, u32[]{:S(2)}, u32[]{:S(2)}) collective-permute-start(f32[8,128]{1,0:T(8,128)S(1)} %squares.1), channel_id=1, source_target_pairs={{0,8},{4,12},{8,0},{12,4},{16,24},{20,28},{24,16},{28,20},{1,9},{5... | collective-permute-start | bytes 12296 | tf_op jit(solution)/shard_map/ppermute | solution.py:581

commit v22 on v21

--- a/solution.py
+++ b/solution.py
@@ -252,8 +252,10 @@
 
 
 def scalars_kernel(place, shifts_ref, index_ref, velocity_ref, scalar_ref):
-    scalars = [shifts_ref[index_ref[place[0]]]] + [velocity_ref[d] for d in range(3)]
-    for n, scalar in enumerate(scalars):
+    rows = {0: shifts_ref[index_ref[place[0]]]}
+    rows.update({1 + d: velocity_ref[d] for d in range(3)})
+    rows.update({8 + c: shifts_ref[index_ref[c]] for c in range(index_ref.shape[0])})
+    for n, scalar in rows.items():
         scalar_ref[pl.ds(n, 1), :] = jnp.full((1, LANES), scalar, jnp.float32)
 
 
@@ -504,17 +506,18 @@
             out_ref[pl.ds(base + squares, 1), :] = ref[pl.ds(2 * SLAB * half, 1), :]
 
 
-def collect_kernel(place, shifts_ref, index_ref, velocity_ref, source_ref, reaction_ref, *refs):
+def collect_kernel(place, scalar_ref, source_ref, reaction_ref, *refs):
     parts, (iterate_ref, residual_ref) = refs[:-2], refs[-2:]
     _, bx, by, nz = iterate_ref.shape
     outer, edges, _, size = part_rows(bx, by)
-    fine = Level(0, by, nz, 0, (0.0, [velocity_ref[d] for d in range(3)]), None, None, None)
+    _, speed = scalars_of(scalar_ref)
+    fine = Level(0, by, nz, 0, (0.0, speed), None, None, None)
     reaction = [reaction_ref[p] + fine.centre for p in range(1, bx - 1)]
     for m, part in enumerate(parts):
         target = jnp.bitwise_xor(place[0] // 2, m)
         for n in range(2):
             base, column = n * size, 2 * target + n
-            shift = shifts_ref[index_ref[column]]
+            shift = scalar_ref[pl.ds(8 + column, 1), :]
             planes = [part[pl.ds(base + p * by, by), :] for p in range(bx)]
             for p in range(bx):
                 iterate_ref[column, p] = planes[p]
@@ -534,10 +537,13 @@
 def squares_kernel(bx, by, place, *refs):
     parts, out_ref = refs[:-1], refs[-1]
     _, _, squares, size = part_rows(bx, by)
+    lane = lax.broadcasted_iota(jnp.int32, (1, LANES), 1)
+    row = jnp.zeros((1, LANES), jnp.float32)
     for m, part in enumerate(parts):
         target = jnp.bitwise_xor(place[0] // 2, m)
         for n in range(2):
-            out_ref[pl.ds(2 * target + n, 1), :] = part[pl.ds(n * size + squares, 1), :]
+            row = jnp.where(lane == 2 * target + n, part[pl.ds(n * size + squares, 1), :], row)
+    out_ref[...] = row
 
 
 SMEM = pl.BlockSpec(memory_space=pltpu.SMEM)
@@ -596,7 +602,7 @@
     theirs = [lax.ppermute(source, "gy", cores), lax.ppermute(reaction, "gy", cores)]
     (mine,) = local_kernel(keep_kernel, "keep", (), (source,), [(chips, bx, by, nz)])
     (scalar_rows,) = local_kernel(
-        scalars_kernel, "scalars", (shifts, shift_index, velocity), (), [(8, LANES)]
+        scalars_kernel, "scalars", (shifts, shift_index, velocity), (), [(8 + columns, LANES)]
     )
     blocks = local_kernel(
         merge_kernel,
@@ -680,13 +686,13 @@
     )
     parts = swap_in_plane(parts, 2)
     (squares,) = local_kernel(
-        functools.partial(squares_kernel, bx, by), "squares", (), parts, [(columns, nz)]
+        functools.partial(squares_kernel, bx, by), "squares", (), parts, [(1, nz)]
     )
     iterate, residual = local_kernel(
         collect_kernel,
         "collect",
-        (shifts, shift_index, velocity),
-        (source, reaction, *parts),
+        (),
+        (scalar_rows, source, reaction, *parts),
         [source.shape] * 2,
     )
     sums = swap_slabs(squares, step, slabs)
@@ -694,7 +700,7 @@
     while len(sums) > 1:
         sums = [first + second for first, second in zip(sums[::2], sums[1::2])]
     (total,) = sums
-    residual_rms = jnp.sqrt(total[:, 0] / (nx * ny * nz) + EPSILON)
+    residual_rms = jnp.sqrt(total[0, :columns] / (nx * ny * nz) + EPSILON)
     return iterate, residual, residual_rms
 
 

time: 52.1 us -> 52 us (level)
  Pallas kernels: 5.67 us -> 5.14 us
    pallas_call x13, Pallas kernels: 5.67 us -> 5.14 us  [local_kernel(): pl.pallas_call(placed, out_shape=[jax.ShapeDtypeStruct(shape, jnp.float32...]
  transfers between devices with their start and end apart: 18 -> 18, of which waited for: 11 -> 12; matrix products, arithmetic and copies ran while one was open for 0% -> 0% of each run, Pallas kernels for 8% -> 7%
where the time goes in v22:
time: 52 us; the launch traced here: 51.8 us
  starting transfers between devices  26.7 us (51%)
  waiting for transfers between devices  17.1 us (33%)
  Pallas kernels  5.14 us (10%)
  local copies, waits for them, and re-layouts  1.34 us (3%)
  between operations  0.84 us (2%)
  other arithmetic  0.66 us (1%)
    ppermute x6, waiting for transfers between devices, swap_in_plane(): moved.append(lax.ppermute(pieces[k], ('gx', 'gy'), pairs))  9.63 us
    ppermute x6, starting transfers between devices, swap_slabs(): moved.append(lax.ppermute(piece, 'gx', pairs))  9.63 us
    ppermute x3, starting transfers between devices, send_beside(): lax.ppermute(piece, 'gx', [(i, j) for i, j in pairs if 0 <= j < gx_size])  8.34 us
    ppermute x6, starting transfers between devices, swap_in_plane(): moved.append(lax.ppermute(pieces[k], ('gx', 'gy'), pairs))  8.1 us
    pallas_call x13, Pallas kernels, local_kernel(): pl.pallas_call(placed, out_shape=[jax.ShapeDtypeStruct(shape, jnp.float32...  5.14 us
    ppermute x6, waiting for transfers between devices, swap_slabs(): moved.append(lax.ppermute(piece, 'gx', pairs))  3.36 us
    ppermute x3, waiting for transfers between devices, send_beside(): lax.ppermute(piece, 'gx', [(i, j) for i, j in pairs if 0 <= j < gx_size])  2.16 us
    ppermute x1, waiting for transfers between devices, column_body(): lax.ppermute(sent, 'gy', cores)  1.53 us
  transfers between devices with their start and end apart: 18, of which 12 were waited for; matrix products, arithmetic and copies ran while one was open for 0% of the time, Pallas kernels for 7%

profile of v22, /device:TPU:0, one launch (start us, length us, event | category | flops | bytes accessed | tf_op | source)
XLA Modules:
  0.0 51.8 jit_solution(10762852775046056803)
XLA Ops:
  1.2 0.9 %copy-done = f32[8,4,16,128]{3,2,1,0:T(8,128)S(1)} copy-done((f32[8,4,16,128]{3,2,1,0:T(8,128)S(1)}, f32[8,4,16,128]{3,2,1,0:T(8,128)}, u32[]{:S(2)}) %copy-start) | copy-done | bytes 262168
  3.0 3.0 %collective-permute-start.2 = (f32[2,4,32,128]{3,2,1,0:T(8,128)S(1)}, f32[2,4,32,128]{3,2,1,0:T(8,128)S(1)}, u32[]{:S(2)}, u32[]{:S(2)}) collective-permute-start(f32[2,4,32,128]{3,2,1,0:T(8,128)S(1)} %get-tuple-element.29), channel_id=1, source_target_pairs={{0,2},{1,3},{2,0},{3,1},{4,6},{5,7},{6,4},{7,5},{8,10},{9,11},{10,... | collective-permute-start | bytes 393224 | tf_op jit(solution)/shard_map/ppermute | solution.py:578
  6.0 1.5 %collective-permute-start.3 = (f32[2,4,32,128]{3,2,1,0:T(8,128)S(1)}, f32[2,4,32,128]{3,2,1,0:T(8,128)S(1)}, u32[]{:S(2)}, u32[]{:S(2)}) collective-permute-start(f32[2,4,32,128]{3,2,1,0:T(8,128)S(1)} %get-tuple-element.30), channel_id=1, source_target_pairs={{0,4},{1,5},{2,6},{3,7},{4,0},{5,1},{6,2},{7,3},{8,12},{9,13},{10,... | collective-permute-start | bytes 393224 | tf_op jit(solution)/shard_map/ppermute | solution.py:578
  7.5 2.2 %collective-permute-done.2.refs_1_ = f32[2,4,32,128]{3,2,1,0:T(8,128)S(1)} collective-permute-done((f32[2,4,32,128]{3,2,1,0:T(8,128)S(1)}, f32[2,4,32,128]{3,2,1,0:T(8,128)S(1)}, u32[]{:S(2)}, u32[]{:S(2)}) %collective-permute-start.2) | collective-permute-done | bytes 131104 | tf_op jit(solution)/shard_map/ppermute | solution.py:578
  9.8 1.4 %collective-permute-start.5 = (f32[2,4,64,128]{3,2,1,0:T(8,128)S(1)}, f32[2,4,64,128]{3,2,1,0:T(8,128)S(1)}, u32[]{:S(2)}, u32[]{:S(2)}) collective-permute-start(f32[2,4,64,128]{3,2,1,0:T(8,128)S(1)} %half.1), channel_id=1, source_target_pairs={{4,12},{8,0},{12,20},{16,8},{20,28},{24,16},{5,13},{9,1},{13,21},{... | collective-permute-start | bytes 786440 | tf_op jit(solution)/shard_map/ppermute | solution.py:634
  12.4 1.4 %collective-permute-done.4.refs_3_ = f32[2,4,32,128]{3,2,1,0:T(8,128)S(1)} collective-permute-done((f32[2,4,32,128]{3,2,1,0:T(8,128)S(1)}, f32[2,4,32,128]{3,2,1,0:T(8,128)S(1)}, u32[]{:S(2)}, u32[]{:S(2)}) %collective-permute-start.4) | collective-permute-done | bytes 131104 | tf_op jit(solution)/shard_map/ppermute | solution.py:578
  13.9 3.6 %collective-permute-start.6 = (f32[2,2,64,128]{3,2,1,0:T(8,128)S(1)}, f32[2,2,64,128]{3,2,1,0:T(8,128)S(1)}, u32[]{:S(2)}, u32[]{:S(2)}) collective-permute-start(f32[2,2,64,128]{3,2,1,0:T(8,128)S(1)} %get-tuple-element.38), channel_id=1, source_target_pairs={{0,8},{8,16},{12,4},{16,24},{20,12},{28,20},{1,9},{9,17},{13,5},{1... | collective-permute-start | bytes 393224 | tf_op jit(solution)/shard_map/ppermute | solution.py:634
  17.9 2.2 %collective-permute-done.6.refs_7_ = f32[2,2,64,128]{3,2,1,0:T(8,128)S(1)} collective-permute-done((f32[2,2,64,128]{3,2,1,0:T(8,128)S(1)}, f32[2,2,64,128]{3,2,1,0:T(8,128)S(1)}, u32[]{:S(2)}, u32[]{:S(2)}) %collective-permute-start.6) | collective-permute-done | bytes 131104 | tf_op jit(solution)/shard_map/ppermute | solution.py:634
  20.5 4.5 %collective-permute-start.7 = (f32[4,32,128]{2,1,0:T(8,128)S(1)}, f32[4,32,128]{2,1,0:T(8,128)S(1)}, u32[]{:S(2)}, u32[]{:S(2)}) collective-permute-start(f32[4,32,128]{2,1,0:T(8,128)S(1)} %get-tuple-element.43.refs_3_), channel_id=1, source_target_pairs={{0,24},{4,28},{8,16},{12,20},{16,8},{20,12},{24,0},{28,4},{1,25},{... | collective-permute-start | bytes 196616 | tf_op jit(solution)/shard_map/ppermute | solution.py:587
  25.1 0.6 %collective-permute-start.9 = (f32[4,32,128]{2,1,0:T(8,128)S(1)}, f32[4,32,128]{2,1,0:T(8,128)S(1)}, u32[]{:S(2)}, u32[]{:S(2)}) collective-permute-start(f32[4,32,128]{2,1,0:T(8,128)S(1)} %get-tuple-element.43.refs_3_), channel_id=1, source_target_pairs={{0,8},{4,12},{8,0},{12,4},{16,24},{20,28},{24,16},{28,20},{1,9},{5... | collective-permute-start | bytes 196616 | tf_op jit(solution)/shard_map/ppermute | solution.py:587
  25.7 3.3 %collective-permute-start.10 = (f32[2,64,128]{2,1,0:T(8,128)S(1)}, f32[2,64,128]{2,1,0:T(8,128)S(1)}, u32[]{:S(2)}, u32[]{:S(2)}) collective-permute-start(f32[2,64,128]{2,1,0:T(8,128)S(1)} %get-tuple-element.44), channel_id=1, source_target_pairs={{0,8},{8,16},{12,4},{16,24},{20,12},{28,20},{1,9},{9,17},{13,5},{1... | collective-permute-start | bytes 196616 | tf_op jit(solution)/shard_map/ppermute | solution.py:634
  29.2 1.1 %collective-permute-done.8.refs_5_ = f32[4,32,128]{2,1,0:T(8,128)S(1)} collective-permute-done((f32[4,32,128]{2,1,0:T(8,128)S(1)}, f32[4,32,128]{2,1,0:T(8,128)S(1)}, u32[]{:S(2)}, u32[]{:S(2)}) %collective-permute-start.8) | collective-permute-done | bytes 65568 | tf_op jit(solution)/shard_map/ppermute | solution.py:587
  30.2 1.7 %coarse.1.refs_5_ = f32[256,128]{1,0:T(8,128)S(1)} custom-call(f32[16,128]{1,0:T(8,128)S(1)} %scalars.1.refs_0_, bf16[128,128]{1,0:T(8,128)(2,1)S(1)} %get-tuple-element.54.refs_8_.refs_1_, bf16[128,128]{1,0:T(8,128)(2,1)S(1)} %get-tuple-element.53.refs_2_, f32[4,32,128]{2,1,0:T(8,128)S(1)} %get-tuple-element.43.refs_3_, ...), custom_call_target="tpu_custom_call" | custom-call | tf_op jit(solution)/shard_map/coarse/pallas_call | solution.py:561
  32.0 0.9 %post.1 = (f32[520,128]{1,0:T(8,128)S(1)}, f32[520,128]{1,0:T(8,128)S(1)}) custom-call(f32[16,128]{1,0:T(8,128)S(1)} %scalars.1.refs_0_, f32[16,64,128]{2,1,0:T(8,128)S(1)} %get-tuple-element.39.refs_1_, f32[16,64,128]{2,1,0:T(8,128)S(1)} %get-tuple-element.40.refs_2_, f32[16,64,128]{2,1,0:T(8,128)S(1)} %get-tuple-element.41.refs_3_, ...), custom_call_target="tpu_custom_call" | custom-call | tf_op jit(solution)/shard_map/post/pallas_call | solution.py:561
  33.0 1.5 %collective-permute-done.11.refs_1_ = f32[520,128]{1,0:T(8,128)S(1)} collective-permute-done((f32[520,128]{1,0:T(8,128)S(1)}, f32[520,128]{1,0:T(8,128)S(1)}, u32[]{:S(2)}, u32[]{:S(2)}) %collective-permute-start.11) | collective-permute-done | bytes 266272 | tf_op jit(solution)/shard_map/ppermute | solution.py:684
  34.6 1.6 %collective-permute-start.12 = (f32[208,128]{1,0:T(8,128)S(1)}, f32[208,128]{1,0:T(8,128)S(1)}, u32[]{:S(2)}, u32[]{:S(2)}) collective-permute-start(f32[208,128]{1,0:T(8,128)S(1)} %get-tuple-element.48), channel_id=1, source_target_pairs={{0,2},{1,3},{2,0},{3,1},{4,6},{5,7},{6,4},{7,5},{8,10},{9,11},{10,... | collective-permute-start | bytes 319496 | tf_op jit(solution)/shard_map/ppermute | solution.py:578
  36.2 1.9 %collective-permute-start.13 = (f32[208,128]{1,0:T(8,128)S(1)}, f32[208,128]{1,0:T(8,128)S(1)}, u32[]{:S(2)}, u32[]{:S(2)}) collective-permute-start(f32[208,128]{1,0:T(8,128)S(1)} %get-tuple-element.49), channel_id=1, source_target_pairs={{0,4},{1,5},{2,6},{3,7},{4,0},{5,1},{6,2},{7,3},{8,12},{9,13},{10,... | collective-permute-start | bytes 319496 | tf_op jit(solution)/shard_map/ppermute | solution.py:578
  38.1 1.5 %collective-permute-done.12.refs_4_.refs_1_ = f32[208,128]{1,0:T(8,128)S(1)} collective-permute-done((f32[208,128]{1,0:T(8,128)S(1)}, f32[208,128]{1,0:T(8,128)S(1)}, u32[]{:S(2)}, u32[]{:S(2)}) %collective-permute-start.12) | collective-permute-done | bytes 106528 | tf_op jit(solution)/shard_map/ppermute | solution.py:578
  39.7 2.2 %collective-permute-done.13.refs_5_.refs_2_ = f32[208,128]{1,0:T(8,128)S(1)} collective-permute-done((f32[208,128]{1,0:T(8,128)S(1)}, f32[208,128]{1,0:T(8,128)S(1)}, u32[]{:S(2)}, u32[]{:S(2)}) %collective-permute-start.13) | collective-permute-done | bytes 106528 | tf_op jit(solution)/shard_map/ppermute | solution.py:578
  41.9 1.7 %collective-permute-done.14.refs_6_.refs_3_ = f32[208,128]{1,0:T(8,128)S(1)} collective-permute-done((f32[208,128]{1,0:T(8,128)S(1)}, f32[208,128]{1,0:T(8,128)S(1)}, u32[]{:S(2)}, u32[]{:S(2)}) %collective-permute-start.14) | collective-permute-done | bytes 106528 | tf_op jit(solution)/shard_map/ppermute | solution.py:578
  43.7 3.1 %collective-permute-start.15 = (f32[1,128]{1,0:T(1,128)S(1)}, f32[1,128]{1,0:T(1,128)S(1)}, u32[]{:S(2)}, u32[]{:S(2)}) collective-permute-start(f32[1,128]{1,0:T(1,128)S(1)} %squares.1), channel_id=1, source_target_pairs={{0,24},{4,28},{8,16},{12,20},{16,8},{20,12},{24,0},{28,4},{1,25},{... | collective-permute-start | bytes 1544 | tf_op jit(solution)/shard_map/ppermute | solution.py:587
  46.8 1.3 %collective-permute-start.17 = (f32[1,128]{1,0:T(1,128)S(1)}, f32[1,128]{1,0:T(1,128)S(1)}, u32[]{:S(2)}, u32[]{:S(2)}) collective-permute-start(f32[1,128]{1,0:T(1,128)S(1)} %squares.1), channel_id=1, source_target_pairs={{0,8},{4,12},{8,0},{12,4},{16,24},{20,28},{24,16},{28,20},{1,9},{5... | collective-permute-start | bytes 1544 | tf_op jit(solution)/shard_map/ppermute | solution.py:587
  48.1 0.9 %collect.1 = (f32[8,4,16,128]{3,2,1,0:T(8,128)}, f32[8,4,16,128]{3,2,1,0:T(8,128)}) custom-call(f32[16,128]{1,0:T(8,128)S(1)} %scalars.1.refs_0_, f32[8,4,16,128]{3,2,1,0:T(8,128)S(1)} %copy-done.1, f32[4,16,128]{2,1,0:T(8,128)S(1)} %copy-done.2, f32[208,128]{1,0:T(8,128)S(1)} %get-tuple-element.47.refs_3_.refs_0_, ...), custom_call_target="tpu_custom_call" | custom-call | tf_op jit(solution)/shard_map/collect/pallas_call | solution.py:561
  49.1 2.2 %collective-permute-done.16 = f32[1,128]{1,0:T(1,128)S(1)} collective-permute-done((f32[1,128]{1,0:T(1,128)S(1)}, f32[1,128]{1,0:T(1,128)S(1)}, u32[]{:S(2)}, u32[]{:S(2)}) %collective-permute-start.16) | collective-permute-done | bytes 544 | tf_op jit(solution)/shard_map/ppermute | solution.py:587
  (42 shorter events, 4.5 us)
Async XLA Ops:
  0.6 1.9 %collective-permute-start = (f32[8,4,16,128]{3,2,1,0:T(8,128)}, f32[8,4,16,128]{3,2,1,0:T(8,128)S(1)}, u32[]{:S(2)}, u32[]{:S(2)}) collective-permute-start(f32[8,4,16,128]{3,2,1,0:T(8,128)} %refs_1_.3), channel_id=1, source_target_pairs={{0,1},{1,0},{2,3},{3,2},{4,5},{5,4},{6,7},{7,6},{8,9},{9,8},{10,11... | collective-permute-start | bytes 786440 | tf_op jit(solution)/shard_map/ppermute | solution.py:602
  1.1 1.4 %collective-permute-start.1 = (f32[4,16,128]{2,1,0:T(8,128)}, f32[4,16,128]{2,1,0:T(8,128)S(1)}, u32[]{:S(2)}, u32[]{:S(2)}) collective-permute-start(f32[4,16,128]{2,1,0:T(8,128)} %refs_2_.5), channel_id=1, source_target_pairs={{0,1},{1,0},{2,3},{3,2},{4,5},{5,4},{6,7},{7,6},{8,9},{9,8},{10,11... | collective-permute-start | bytes 98312 | tf_op jit(solution)/shard_map/ppermute | solution.py:602
  1.2 0.9 %copy-start = (f32[8,4,16,128]{3,2,1,0:T(8,128)S(1)}, f32[8,4,16,128]{3,2,1,0:T(8,128)}, u32[]{:S(2)}) copy-start(f32[8,4,16,128]{3,2,1,0:T(8,128)} %refs_1_.3) | copy-start | bytes 786436
  2.2 0.8 %copy-start.2 = (f32[4,16,128]{2,1,0:T(8,128)S(1)}, f32[4,16,128]{2,1,0:T(8,128)}, u32[]{:S(2)}) copy-start(f32[4,16,128]{2,1,0:T(8,128)} %refs_2_.5) | copy-start | bytes 98308
  3.0 6.8 %collective-permute-start.2 = (f32[2,4,32,128]{3,2,1,0:T(8,128)S(1)}, f32[2,4,32,128]{3,2,1,0:T(8,128)S(1)}, u32[]{:S(2)}, u32[]{:S(2)}) collective-permute-start(f32[2,4,32,128]{3,2,1,0:T(8,128)S(1)} %get-tuple-element.29), channel_id=1, source_target_pairs={{0,2},{1,3},{2,0},{3,1},{4,6},{5,7},{6,4},{7,5},{8,10},{9,11},{10,... | collective-permute-start | bytes 393224 | tf_op jit(solution)/shard_map/ppermute | solution.py:578
  6.0 6.4 %collective-permute-start.3 = (f32[2,4,32,128]{3,2,1,0:T(8,128)S(1)}, f32[2,4,32,128]{3,2,1,0:T(8,128)S(1)}, u32[]{:S(2)}, u32[]{:S(2)}) collective-permute-start(f32[2,4,32,128]{3,2,1,0:T(8,128)S(1)} %get-tuple-element.30), channel_id=1, source_target_pairs={{0,4},{1,5},{2,6},{3,7},{4,0},{5,1},{6,2},{7,3},{8,12},{9,13},{10,... | collective-permute-start | bytes 393224 | tf_op jit(solution)/shard_map/ppermute | solution.py:578
  7.5 6.3 %collective-permute-start.4 = (f32[2,4,32,128]{3,2,1,0:T(8,128)S(1)}, f32[2,4,32,128]{3,2,1,0:T(8,128)S(1)}, u32[]{:S(2)}, u32[]{:S(2)}) collective-permute-start(f32[2,4,32,128]{3,2,1,0:T(8,128)S(1)} %get-tuple-element.31), channel_id=1, source_target_pairs={{0,6},{1,7},{2,4},{3,5},{4,2},{5,3},{6,0},{7,1},{8,14},{9,15},{10,... | collective-permute-start | bytes 393224 | tf_op jit(solution)/shard_map/ppermute | solution.py:578
  9.8 1.5 %copy-start.3 = (f32[8]{0:T(128)S(1)}, f32[8]{0:T(128)}, u32[]{:S(2)}) copy-start(f32[8]{0:T(128)} %refs_0_.2) | copy-start | bytes 100
  9.8 1.5 %copy-start.4 = (s32[8]{0:T(128)S(1)}, s32[8]{0:T(128)}, u32[]{:S(2)}) copy-start(s32[8]{0:T(128)} %refs_1_.2) | copy-start | bytes 100
  9.8 1.5 %copy-start.5 = (f32[3]{0:T(128)S(1)}, f32[3]{0:T(128)}, u32[]{:S(2)}) copy-start(f32[3]{0:T(128)} %refs_2_.3) | copy-start | bytes 40
  9.8 10.2 %collective-permute-start.5 = (f32[2,4,64,128]{3,2,1,0:T(8,128)S(1)}, f32[2,4,64,128]{3,2,1,0:T(8,128)S(1)}, u32[]{:S(2)}, u32[]{:S(2)}) collective-permute-start(f32[2,4,64,128]{3,2,1,0:T(8,128)S(1)} %half.1), channel_id=1, source_target_pairs={{4,12},{8,0},{12,20},{16,8},{20,28},{24,16},{5,13},{9,1},{13,21},{... | collective-permute-start | bytes 786440 | tf_op jit(solution)/shard_map/ppermute | solution.py:634
  13.9 6.1 %collective-permute-start.6 = (f32[2,2,64,128]{3,2,1,0:T(8,128)S(1)}, f32[2,2,64,128]{3,2,1,0:T(8,128)S(1)}, u32[]{:S(2)}, u32[]{:S(2)}) collective-permute-start(f32[2,2,64,128]{3,2,1,0:T(8,128)S(1)} %get-tuple-element.38), channel_id=1, source_target_pairs={{0,8},{8,16},{12,4},{16,24},{20,12},{28,20},{1,9},{9,17},{13,5},{1... | collective-permute-start | bytes 393224 | tf_op jit(solution)/shard_map/ppermute | solution.py:634
  20.5 8.6 %collective-permute-start.7 = (f32[4,32,128]{2,1,0:T(8,128)S(1)}, f32[4,32,128]{2,1,0:T(8,128)S(1)}, u32[]{:S(2)}, u32[]{:S(2)}) collective-permute-start(f32[4,32,128]{2,1,0:T(8,128)S(1)} %get-tuple-element.43.refs_3_), channel_id=1, source_target_pairs={{0,24},{4,28},{8,16},{12,20},{16,8},{20,12},{24,0},{28,4},{1,25},{... | collective-permute-start | bytes 196616 | tf_op jit(solution)/shard_map/ppermute | solution.py:587
  25.1 5.2 %collective-permute-start.8 = (f32[4,32,128]{2,1,0:T(8,128)S(1)}, f32[4,32,128]{2,1,0:T(8,128)S(1)}, u32[]{:S(2)}, u32[]{:S(2)}) collective-permute-start(f32[4,32,128]{2,1,0:T(8,128)S(1)} %get-tuple-element.43.refs_3_), channel_id=1, source_target_pairs={{0,16},{4,20},{8,24},{12,28},{16,0},{20,4},{24,8},{28,12},{1,17},{... | collective-permute-start | bytes 196616 | tf_op jit(solution)/shard_map/ppermute | solution.py:587
  25.1 5.2 %collective-permute-start.9 = (f32[4,32,128]{2,1,0:T(8,128)S(1)}, f32[4,32,128]{2,1,0:T(8,128)S(1)}, u32[]{:S(2)}, u32[]{:S(2)}) collective-permute-start(f32[4,32,128]{2,1,0:T(8,128)S(1)} %get-tuple-element.43.refs_3_), channel_id=1, source_target_pairs={{0,8},{4,12},{8,0},{12,4},{16,24},{20,28},{24,16},{28,20},{1,9},{5... | collective-permute-start | bytes 196616 | tf_op jit(solution)/shard_map/ppermute | solution.py:587
  25.7 6.3 %collective-permute-start.10 = (f32[2,64,128]{2,1,0:T(8,128)S(1)}, f32[2,64,128]{2,1,0:T(8,128)S(1)}, u32[]{:S(2)}, u32[]{:S(2)}) collective-permute-start(f32[2,64,128]{2,1,0:T(8,128)S(1)} %get-tuple-element.44), channel_id=1, source_target_pairs={{0,8},{8,16},{12,4},{16,24},{20,12},{28,20},{1,9},{9,17},{13,5},{1... | collective-permute-start | bytes 196616 | tf_op jit(solution)/shard_map/ppermute | solution.py:634
  32.9 1.6 %collective-permute-start.11 = (f32[520,128]{1,0:T(8,128)S(1)}, f32[520,128]{1,0:T(8,128)S(1)}, u32[]{:S(2)}, u32[]{:S(2)}) collective-permute-start(f32[520,128]{1,0:T(8,128)S(1)} %get-tuple-element.46), channel_id=1, source_target_pairs={{0,1},{1,0},{2,3},{3,2},{4,5},{5,4},{6,7},{7,6},{8,9},{9,8},{10,11... | collective-permute-start | bytes 798728 | tf_op jit(solution)/shard_map/ppermute | solution.py:684
  34.6 13.5 %copy-start.1 = (f32[8,4,16,128]{3,2,1,0:T(8,128)S(1)}, f32[8,4,16,128]{3,2,1,0:T(8,128)}, u32[]{:S(2)}) copy-start(f32[8,4,16,128]{3,2,1,0:T(8,128)} %refs_1_.3) | copy-start | bytes 786436
  34.6 5.1 %collective-permute-start.12 = (f32[208,128]{1,0:T(8,128)S(1)}, f32[208,128]{1,0:T(8,128)S(1)}, u32[]{:S(2)}, u32[]{:S(2)}) collective-permute-start(f32[208,128]{1,0:T(8,128)S(1)} %get-tuple-element.48), channel_id=1, source_target_pairs={{0,2},{1,3},{2,0},{3,1},{4,6},{5,7},{6,4},{7,5},{8,10},{9,11},{10,... | collective-permute-start | bytes 319496 | tf_op jit(solution)/shard_map/ppermute | solution.py:578
  36.2 5.7 %collective-permute-start.13 = (f32[208,128]{1,0:T(8,128)S(1)}, f32[208,128]{1,0:T(8,128)S(1)}, u32[]{:S(2)}, u32[]{:S(2)}) collective-permute-start(f32[208,128]{1,0:T(8,128)S(1)} %get-tuple-element.49), channel_id=1, source_target_pairs={{0,4},{1,5},{2,6},{3,7},{4,0},{5,1},{6,2},{7,3},{8,12},{9,13},{10,... | collective-permute-start | bytes 319496 | tf_op jit(solution)/shard_map/ppermute | solution.py:578
  38.0 5.6 %collective-permute-start.14 = (f32[208,128]{1,0:T(8,128)S(1)}, f32[208,128]{1,0:T(8,128)S(1)}, u32[]{:S(2)}, u32[]{:S(2)}) collective-permute-start(f32[208,128]{1,0:T(8,128)S(1)} %get-tuple-element.50), channel_id=1, source_target_pairs={{0,6},{1,7},{2,4},{3,5},{4,2},{5,3},{6,0},{7,1},{8,14},{9,15},{10,... | collective-permute-start | bytes 319496 | tf_op jit(solution)/shard_map/ppermute | solution.py:578
  43.7 5.4 %collective-permute-start.15 = (f32[1,128]{1,0:T(1,128)S(1)}, f32[1,128]{1,0:T(1,128)S(1)}, u32[]{:S(2)}, u32[]{:S(2)}) collective-permute-start(f32[1,128]{1,0:T(1,128)S(1)} %squares.1), channel_id=1, source_target_pairs={{0,24},{4,28},{8,16},{12,20},{16,8},{20,12},{24,0},{28,4},{1,25},{... | collective-permute-start | bytes 1544 | tf_op jit(solution)/shard_map/ppermute | solution.py:587
  46.8 4.4 %collective-permute-start.16 = (f32[1,128]{1,0:T(1,128)S(1)}, f32[1,128]{1,0:T(1,128)S(1)}, u32[]{:S(2)}, u32[]{:S(2)}) collective-permute-start(f32[1,128]{1,0:T(1,128)S(1)} %squares.1), channel_id=1, source_target_pairs={{0,16},{4,20},{8,24},{12,28},{16,0},{20,4},{24,8},{28,12},{1,17},{... | collective-permute-start | bytes 1544 | tf_op jit(solution)/shard_map/ppermute | solution.py:587
  46.8 4.4 %collective-permute-start.17 = (f32[1,128]{1,0:T(1,128)S(1)}, f32[1,128]{1,0:T(1,128)S(1)}, u32[]{:S(2)}, u32[]{:S(2)}) collective-permute-start(f32[1,128]{1,0:T(1,128)S(1)} %squares.1), channel_id=1, source_target_pairs={{0,8},{4,12},{8,0},{12,4},{16,24},{20,28},{24,16},{28,20},{1,9},{5... | collective-permute-start | bytes 1544 | tf_op jit(solution)/shard_map/ppermute | solution.py:587

commit v23 on v22

--- a/solution.py
+++ b/solution.py
@@ -126,10 +126,10 @@
     )
 
 
-def sweep(planes, get, put):
+def sweep(planes, get, put, size=GROUP):
     planes = list(planes)
-    for first in range(0, len(planes), GROUP):
-        group = planes[first : first + GROUP]
+    for first in range(0, len(planes), size):
+        group = planes[first : first + size]
         values = [get(x) for x in group]
         for x, value in zip(group, values):
             put(x, value)
@@ -193,7 +193,7 @@
         return (1.0 - DAMPING) * middle + self.w[x] * pulled
 
     def smooth(self, src, dst, planes):
-        sweep(planes, lambda x: self.smoothed(src, x), self.put(dst))
+        sweep(planes, lambda x: self.smoothed(src, x), self.put(dst), GROUP * 64 // self.ny)
 
     def defect(self, v, x):
         middle = self.plane(v, x)
@@ -246,7 +246,8 @@
     return -k % count
 
 
-def keep_kernel(place, source_ref, out_ref):
+def keep_kernel(place, source_ref, reaction_ref, out_ref, kept_ref):
+    kept_ref[...] = reaction_ref[...]
     for n in range(out_ref.shape[0]):
         out_ref[n] = source_ref[2 * n + (place[0] & 1)]
 
@@ -397,7 +398,7 @@
         w1[x] = weight
         v1a[x + rim, pl.ds(8, ny1), :] = weight * f1[x]
 
-    sweep(range(nx1), lambda x: DAMPING / (r1[x] + mid.centre), put_start)
+    sweep(range(nx1), lambda x: DAMPING / (r1[x] + mid.centre), put_start, 2 * GROUP)
     mid.smooth(v1a, v1b, range(nx1))
 
     def coarsened(x):
@@ -600,7 +601,9 @@
     chips, chips_y = columns // 2, gy_size // 2
     cores = [(i, i ^ 1) for i in range(gy_size)]
     theirs = [lax.ppermute(source, "gy", cores), lax.ppermute(reaction, "gy", cores)]
-    (mine,) = local_kernel(keep_kernel, "keep", (), (source,), [(chips, bx, by, nz)])
+    mine, kept = local_kernel(
+        keep_kernel, "keep", (), (source, reaction), [(chips, bx, by, nz), reaction.shape]
+    )
     (scalar_rows,) = local_kernel(
         scalars_kernel, "scalars", (shifts, shift_index, velocity), (), [(8 + columns, LANES)]
     )
@@ -608,7 +611,7 @@
         merge_kernel,
         "merge",
         (),
-        (mine, theirs[0], reaction, theirs[1]),
+        (mine, theirs[0], kept, theirs[1]),
         [(2, bx, 2 * by, nz)] * chips,
     )
     blocks = swap_in_plane(blocks, 2)

time: 52 us -> 52.1 us (level)
    unnamed x12 -> x14, local copies, waits for them, and re-layouts: 1.34 us -> 1.74 us
  transfers between devices with their start and end apart: 18 -> 18, of which waited for: 12 -> 11; matrix products, arithmetic and copies ran while one was open for 0% -> 0% of each run, Pallas kernels for 7% -> 7%
where the time goes in v23:
time: 52.1 us; the launch traced here: 51.8 us
  starting transfers between devices  26.7 us (51%)
  waiting for transfers between devices  16.7 us (32%)
  Pallas kernels  5.16 us (10%)
  local copies, waits for them, and re-layouts  1.74 us (3%)
  between operations  0.86 us (2%)
  other arithmetic  0.66 us (1%)
    ppermute x6, starting transfers between devices, swap_slabs(): moved.append(lax.ppermute(piece, 'gx', pairs))  9.63 us
    ppermute x6, waiting for transfers between devices, swap_in_plane(): moved.append(lax.ppermute(pieces[k], ('gx', 'gy'), pairs))  9.63 us
    ppermute x3, starting transfers between devices, send_beside(): lax.ppermute(piece, 'gx', [(i, j) for i, j in pairs if 0 <= j < gx_size])  8.34 us
    ppermute x6, starting transfers between devices, swap_in_plane(): moved.append(lax.ppermute(pieces[k], ('gx', 'gy'), pairs))  8.1 us
    pallas_call x13, Pallas kernels, local_kernel(): pl.pallas_call(placed, out_shape=[jax.ShapeDtypeStruct(shape, jnp.float32...  5.16 us
    ppermute x6, waiting for transfers between devices, swap_slabs(): moved.append(lax.ppermute(piece, 'gx', pairs))  3.36 us
    ppermute x3, waiting for transfers between devices, send_beside(): lax.ppermute(piece, 'gx', [(i, j) for i, j in pairs if 0 <= j < gx_size])  2.16 us
    unnamed x14, local copies, waits for them, and re-layouts  1.74 us
  transfers between devices with their start and end apart: 18, of which 11 were waited for; matrix products, arithmetic and copies ran while one was open for 0% of the time, Pallas kernels for 7%

profile of v23, /device:TPU:0, one launch (start us, length us, event | category | flops | bytes accessed | tf_op | source)
XLA Modules:
  0.0 51.8 jit_solution(17574775512324378967)
XLA Ops:
  1.2 0.9 %copy-done = f32[8,4,16,128]{3,2,1,0:T(8,128)S(1)} copy-done((f32[8,4,16,128]{3,2,1,0:T(8,128)S(1)}, f32[8,4,16,128]{3,2,1,0:T(8,128)}, u32[]{:S(2)}) %copy-start) | copy-done | bytes 262168
  2.2 0.8 %copy-done.2 = f32[4,16,128]{2,1,0:T(8,128)S(1)} copy-done((f32[4,16,128]{2,1,0:T(8,128)S(1)}, f32[4,16,128]{2,1,0:T(8,128)}, u32[]{:S(2)}) %copy-start.2) | copy-done | bytes 32792
  3.0 3.0 %collective-permute-start.2 = (f32[2,4,32,128]{3,2,1,0:T(8,128)S(1)}, f32[2,4,32,128]{3,2,1,0:T(8,128)S(1)}, u32[]{:S(2)}, u32[]{:S(2)}) collective-permute-start(f32[2,4,32,128]{3,2,1,0:T(8,128)S(1)} %get-tuple-element.33), channel_id=1, source_target_pairs={{0,2},{1,3},{2,0},{3,1},{4,6},{5,7},{6,4},{7,5},{8,10},{9,11},{10,... | collective-permute-start | bytes 393224 | tf_op jit(solution)/shard_map/ppermute | solution.py:579
  6.0 1.5 %collective-permute-start.3 = (f32[2,4,32,128]{3,2,1,0:T(8,128)S(1)}, f32[2,4,32,128]{3,2,1,0:T(8,128)S(1)}, u32[]{:S(2)}, u32[]{:S(2)}) collective-permute-start(f32[2,4,32,128]{3,2,1,0:T(8,128)S(1)} %get-tuple-element.34), channel_id=1, source_target_pairs={{0,4},{1,5},{2,6},{3,7},{4,0},{5,1},{6,2},{7,3},{8,12},{9,13},{10,... | collective-permute-start | bytes 393224 | tf_op jit(solution)/shard_map/ppermute | solution.py:579
  7.6 2.2 %collective-permute-done.2.refs_1_ = f32[2,4,32,128]{3,2,1,0:T(8,128)S(1)} collective-permute-done((f32[2,4,32,128]{3,2,1,0:T(8,128)S(1)}, f32[2,4,32,128]{3,2,1,0:T(8,128)S(1)}, u32[]{:S(2)}, u32[]{:S(2)}) %collective-permute-start.2) | collective-permute-done | bytes 131104 | tf_op jit(solution)/shard_map/ppermute | solution.py:579
  9.9 1.4 %collective-permute-start.5 = (f32[2,4,64,128]{3,2,1,0:T(8,128)S(1)}, f32[2,4,64,128]{3,2,1,0:T(8,128)S(1)}, u32[]{:S(2)}, u32[]{:S(2)}) collective-permute-start(f32[2,4,64,128]{3,2,1,0:T(8,128)S(1)} %half.1), channel_id=1, source_target_pairs={{4,12},{8,0},{12,20},{16,8},{20,28},{24,16},{5,13},{9,1},{13,21},{... | collective-permute-start | bytes 786440 | tf_op jit(solution)/shard_map/ppermute | solution.py:637
  12.4 1.4 %collective-permute-done.4.refs_3_ = f32[2,4,32,128]{3,2,1,0:T(8,128)S(1)} collective-permute-done((f32[2,4,32,128]{3,2,1,0:T(8,128)S(1)}, f32[2,4,32,128]{3,2,1,0:T(8,128)S(1)}, u32[]{:S(2)}, u32[]{:S(2)}) %collective-permute-start.4) | collective-permute-done | bytes 131104 | tf_op jit(solution)/shard_map/ppermute | solution.py:579
  13.9 3.6 %collective-permute-start.6 = (f32[2,2,64,128]{3,2,1,0:T(8,128)S(1)}, f32[2,2,64,128]{3,2,1,0:T(8,128)S(1)}, u32[]{:S(2)}, u32[]{:S(2)}) collective-permute-start(f32[2,2,64,128]{3,2,1,0:T(8,128)S(1)} %get-tuple-element.42), channel_id=1, source_target_pairs={{0,8},{8,16},{12,4},{16,24},{20,12},{28,20},{1,9},{9,17},{13,5},{1... | collective-permute-start | bytes 393224 | tf_op jit(solution)/shard_map/ppermute | solution.py:637
  17.9 2.2 %collective-permute-done.6.refs_7_ = f32[2,2,64,128]{3,2,1,0:T(8,128)S(1)} collective-permute-done((f32[2,2,64,128]{3,2,1,0:T(8,128)S(1)}, f32[2,2,64,128]{3,2,1,0:T(8,128)S(1)}, u32[]{:S(2)}, u32[]{:S(2)}) %collective-permute-start.6) | collective-permute-done | bytes 131104 | tf_op jit(solution)/shard_map/ppermute | solution.py:637
  20.6 4.5 %collective-permute-start.7 = (f32[4,32,128]{2,1,0:T(8,128)S(1)}, f32[4,32,128]{2,1,0:T(8,128)S(1)}, u32[]{:S(2)}, u32[]{:S(2)}) collective-permute-start(f32[4,32,128]{2,1,0:T(8,128)S(1)} %get-tuple-element.47.refs_3_), channel_id=1, source_target_pairs={{0,24},{4,28},{8,16},{12,20},{16,8},{20,12},{24,0},{28,4},{1,25},{... | collective-permute-start | bytes 196616 | tf_op jit(solution)/shard_map/ppermute | solution.py:588
  25.8 3.3 %collective-permute-start.10 = (f32[2,64,128]{2,1,0:T(8,128)S(1)}, f32[2,64,128]{2,1,0:T(8,128)S(1)}, u32[]{:S(2)}, u32[]{:S(2)}) collective-permute-start(f32[2,64,128]{2,1,0:T(8,128)S(1)} %get-tuple-element.48), channel_id=1, source_target_pairs={{0,8},{8,16},{12,4},{16,24},{20,12},{28,20},{1,9},{9,17},{13,5},{1... | collective-permute-start | bytes 196616 | tf_op jit(solution)/shard_map/ppermute | solution.py:637
  29.2 1.1 %collective-permute-done.8.refs_5_ = f32[4,32,128]{2,1,0:T(8,128)S(1)} collective-permute-done((f32[4,32,128]{2,1,0:T(8,128)S(1)}, f32[4,32,128]{2,1,0:T(8,128)S(1)}, u32[]{:S(2)}, u32[]{:S(2)}) %collective-permute-start.8) | collective-permute-done | bytes 65568 | tf_op jit(solution)/shard_map/ppermute | solution.py:588
  30.3 1.7 %coarse.1.refs_5_ = f32[256,128]{1,0:T(8,128)S(1)} custom-call(f32[16,128]{1,0:T(8,128)S(1)} %scalars.1.refs_0_, bf16[128,128]{1,0:T(8,128)(2,1)S(1)} %get-tuple-element.58.refs_8_.refs_1_, bf16[128,128]{1,0:T(8,128)(2,1)S(1)} %get-tuple-element.57.refs_2_, f32[4,32,128]{2,1,0:T(8,128)S(1)} %get-tuple-element.47.refs_3_, ...), custom_call_target="tpu_custom_call" | custom-call | tf_op jit(solution)/shard_map/coarse/pallas_call | solution.py:562
  32.1 0.9 %post.1 = (f32[520,128]{1,0:T(8,128)S(1)}, f32[520,128]{1,0:T(8,128)S(1)}) custom-call(f32[16,128]{1,0:T(8,128)S(1)} %scalars.1.refs_0_, f32[16,64,128]{2,1,0:T(8,128)S(1)} %get-tuple-element.43.refs_1_, f32[16,64,128]{2,1,0:T(8,128)S(1)} %get-tuple-element.44.refs_2_, f32[16,64,128]{2,1,0:T(8,128)S(1)} %get-tuple-element.45.refs_3_, ...), custom_call_target="tpu_custom_call" | custom-call | tf_op jit(solution)/shard_map/post/pallas_call | solution.py:562
  33.1 1.5 %collective-permute-done.11.refs_1_ = f32[520,128]{1,0:T(8,128)S(1)} collective-permute-done((f32[520,128]{1,0:T(8,128)S(1)}, f32[520,128]{1,0:T(8,128)S(1)}, u32[]{:S(2)}, u32[]{:S(2)}) %collective-permute-start.11) | collective-permute-done | bytes 266272 | tf_op jit(solution)/shard_map/ppermute | solution.py:687
  34.6 1.6 %collective-permute-start.12 = (f32[208,128]{1,0:T(8,128)S(1)}, f32[208,128]{1,0:T(8,128)S(1)}, u32[]{:S(2)}, u32[]{:S(2)}) collective-permute-start(f32[208,128]{1,0:T(8,128)S(1)} %get-tuple-element.52), channel_id=1, source_target_pairs={{0,2},{1,3},{2,0},{3,1},{4,6},{5,7},{6,4},{7,5},{8,10},{9,11},{10,... | collective-permute-start | bytes 319496 | tf_op jit(solution)/shard_map/ppermute | solution.py:579
  36.2 1.9 %collective-permute-start.13 = (f32[208,128]{1,0:T(8,128)S(1)}, f32[208,128]{1,0:T(8,128)S(1)}, u32[]{:S(2)}, u32[]{:S(2)}) collective-permute-start(f32[208,128]{1,0:T(8,128)S(1)} %get-tuple-element.53), channel_id=1, source_target_pairs={{0,4},{1,5},{2,6},{3,7},{4,0},{5,1},{6,2},{7,3},{8,12},{9,13},{10,... | collective-permute-start | bytes 319496 | tf_op jit(solution)/shard_map/ppermute | solution.py:579
  38.2 1.5 %collective-permute-done.12.refs_4_.refs_1_ = f32[208,128]{1,0:T(8,128)S(1)} collective-permute-done((f32[208,128]{1,0:T(8,128)S(1)}, f32[208,128]{1,0:T(8,128)S(1)}, u32[]{:S(2)}, u32[]{:S(2)}) %collective-permute-start.12) | collective-permute-done | bytes 106528 | tf_op jit(solution)/shard_map/ppermute | solution.py:579
  39.7 2.2 %collective-permute-done.13.refs_5_.refs_2_ = f32[208,128]{1,0:T(8,128)S(1)} collective-permute-done((f32[208,128]{1,0:T(8,128)S(1)}, f32[208,128]{1,0:T(8,128)S(1)}, u32[]{:S(2)}, u32[]{:S(2)}) %collective-permute-start.13) | collective-permute-done | bytes 106528 | tf_op jit(solution)/shard_map/ppermute | solution.py:579
  42.0 1.7 %collective-permute-done.14.refs_6_.refs_3_ = f32[208,128]{1,0:T(8,128)S(1)} collective-permute-done((f32[208,128]{1,0:T(8,128)S(1)}, f32[208,128]{1,0:T(8,128)S(1)}, u32[]{:S(2)}, u32[]{:S(2)}) %collective-permute-start.14) | collective-permute-done | bytes 106528 | tf_op jit(solution)/shard_map/ppermute | solution.py:579
  43.7 3.1 %collective-permute-start.15 = (f32[1,128]{1,0:T(1,128)S(1)}, f32[1,128]{1,0:T(1,128)S(1)}, u32[]{:S(2)}, u32[]{:S(2)}) collective-permute-start(f32[1,128]{1,0:T(1,128)S(1)} %squares.1), channel_id=1, source_target_pairs={{0,24},{4,28},{8,16},{12,20},{16,8},{20,12},{24,0},{28,4},{1,25},{... | collective-permute-start | bytes 1544 | tf_op jit(solution)/shard_map/ppermute | solution.py:588
  46.9 1.3 %collective-permute-start.17 = (f32[1,128]{1,0:T(1,128)S(1)}, f32[1,128]{1,0:T(1,128)S(1)}, u32[]{:S(2)}, u32[]{:S(2)}) collective-permute-start(f32[1,128]{1,0:T(1,128)S(1)} %squares.1), channel_id=1, source_target_pairs={{0,8},{4,12},{8,0},{12,4},{16,24},{20,28},{24,16},{28,20},{1,9},{5... | collective-permute-start | bytes 1544 | tf_op jit(solution)/shard_map/ppermute | solution.py:588
  48.2 0.9 %collect.1 = (f32[8,4,16,128]{3,2,1,0:T(8,128)}, f32[8,4,16,128]{3,2,1,0:T(8,128)}) custom-call(f32[16,128]{1,0:T(8,128)S(1)} %scalars.1.refs_0_, f32[8,4,16,128]{3,2,1,0:T(8,128)S(1)} %copy-done.1, f32[4,16,128]{2,1,0:T(8,128)S(1)} %copy-done.3, f32[208,128]{1,0:T(8,128)S(1)} %get-tuple-element.51.refs_3_.refs_0_, ...), custom_call_target="tpu_custom_call" | custom-call | tf_op jit(solution)/shard_map/collect/pallas_call | solution.py:562
  49.1 2.2 %collective-permute-done.16 = f32[1,128]{1,0:T(1,128)S(1)} collective-permute-done((f32[1,128]{1,0:T(1,128)S(1)}, f32[1,128]{1,0:T(1,128)S(1)}, u32[]{:S(2)}, u32[]{:S(2)}) %collective-permute-start.16) | collective-permute-done | bytes 544 | tf_op jit(solution)/shard_map/ppermute | solution.py:588
  (44 shorter events, 4.4 us)
Async XLA Ops:
  0.6 2.3 %collective-permute-start = (f32[8,4,16,128]{3,2,1,0:T(8,128)}, f32[8,4,16,128]{3,2,1,0:T(8,128)S(1)}, u32[]{:S(2)}, u32[]{:S(2)}) collective-permute-start(f32[8,4,16,128]{3,2,1,0:T(8,128)} %refs_1_.5), channel_id=1, source_target_pairs={{0,1},{1,0},{2,3},{3,2},{4,5},{5,4},{6,7},{7,6},{8,9},{9,8},{10,11... | collective-permute-start | bytes 786440 | tf_op jit(solution)/shard_map/ppermute | solution.py:603
  1.1 1.8 %collective-permute-start.1 = (f32[4,16,128]{2,1,0:T(8,128)}, f32[4,16,128]{2,1,0:T(8,128)S(1)}, u32[]{:S(2)}, u32[]{:S(2)}) collective-permute-start(f32[4,16,128]{2,1,0:T(8,128)} %refs_2_.3), channel_id=1, source_target_pairs={{0,1},{1,0},{2,3},{3,2},{4,5},{5,4},{6,7},{7,6},{8,9},{9,8},{10,11... | collective-permute-start | bytes 98312 | tf_op jit(solution)/shard_map/ppermute | solution.py:603
  1.2 0.9 %copy-start = (f32[8,4,16,128]{3,2,1,0:T(8,128)S(1)}, f32[8,4,16,128]{3,2,1,0:T(8,128)}, u32[]{:S(2)}) copy-start(f32[8,4,16,128]{3,2,1,0:T(8,128)} %refs_1_.5) | copy-start | bytes 786436
  3.0 6.8 %collective-permute-start.2 = (f32[2,4,32,128]{3,2,1,0:T(8,128)S(1)}, f32[2,4,32,128]{3,2,1,0:T(8,128)S(1)}, u32[]{:S(2)}, u32[]{:S(2)}) collective-permute-start(f32[2,4,32,128]{3,2,1,0:T(8,128)S(1)} %get-tuple-element.33), channel_id=1, source_target_pairs={{0,2},{1,3},{2,0},{3,1},{4,6},{5,7},{6,4},{7,5},{8,10},{9,11},{10,... | collective-permute-start | bytes 393224 | tf_op jit(solution)/shard_map/ppermute | solution.py:579
  6.0 6.4 %collective-permute-start.3 = (f32[2,4,32,128]{3,2,1,0:T(8,128)S(1)}, f32[2,4,32,128]{3,2,1,0:T(8,128)S(1)}, u32[]{:S(2)}, u32[]{:S(2)}) collective-permute-start(f32[2,4,32,128]{3,2,1,0:T(8,128)S(1)} %get-tuple-element.34), channel_id=1, source_target_pairs={{0,4},{1,5},{2,6},{3,7},{4,0},{5,1},{6,2},{7,3},{8,12},{9,13},{10,... | collective-permute-start | bytes 393224 | tf_op jit(solution)/shard_map/ppermute | solution.py:579
  7.5 6.3 %collective-permute-start.4 = (f32[2,4,32,128]{3,2,1,0:T(8,128)S(1)}, f32[2,4,32,128]{3,2,1,0:T(8,128)S(1)}, u32[]{:S(2)}, u32[]{:S(2)}) collective-permute-start(f32[2,4,32,128]{3,2,1,0:T(8,128)S(1)} %get-tuple-element.35), channel_id=1, source_target_pairs={{0,6},{1,7},{2,4},{3,5},{4,2},{5,3},{6,0},{7,1},{8,14},{9,15},{10,... | collective-permute-start | bytes 393224 | tf_op jit(solution)/shard_map/ppermute | solution.py:579
  9.8 1.5 %copy-start.4 = (f32[8]{0:T(128)S(1)}, f32[8]{0:T(128)}, u32[]{:S(2)}) copy-start(f32[8]{0:T(128)} %refs_0_.2) | copy-start | bytes 100
  9.8 1.5 %copy-start.5 = (s32[8]{0:T(128)S(1)}, s32[8]{0:T(128)}, u32[]{:S(2)}) copy-start(s32[8]{0:T(128)} %refs_1_.3) | copy-start | bytes 100
  9.9 1.5 %copy-start.6 = (f32[3]{0:T(128)S(1)}, f32[3]{0:T(128)}, u32[]{:S(2)}) copy-start(f32[3]{0:T(128)} %refs_2_.2) | copy-start | bytes 40
  9.9 10.2 %collective-permute-start.5 = (f32[2,4,64,128]{3,2,1,0:T(8,128)S(1)}, f32[2,4,64,128]{3,2,1,0:T(8,128)S(1)}, u32[]{:S(2)}, u32[]{:S(2)}) collective-permute-start(f32[2,4,64,128]{3,2,1,0:T(8,128)S(1)} %half.1), channel_id=1, source_target_pairs={{4,12},{8,0},{12,20},{16,8},{20,28},{24,16},{5,13},{9,1},{13,21},{... | collective-permute-start | bytes 786440 | tf_op jit(solution)/shard_map/ppermute | solution.py:637
  13.9 6.1 %collective-permute-start.6 = (f32[2,2,64,128]{3,2,1,0:T(8,128)S(1)}, f32[2,2,64,128]{3,2,1,0:T(8,128)S(1)}, u32[]{:S(2)}, u32[]{:S(2)}) collective-permute-start(f32[2,2,64,128]{3,2,1,0:T(8,128)S(1)} %get-tuple-element.42), channel_id=1, source_target_pairs={{0,8},{8,16},{12,4},{16,24},{20,12},{28,20},{1,9},{9,17},{13,5},{1... | collective-permute-start | bytes 393224 | tf_op jit(solution)/shard_map/ppermute | solution.py:637
  20.6 8.6 %collective-permute-start.7 = (f32[4,32,128]{2,1,0:T(8,128)S(1)}, f32[4,32,128]{2,1,0:T(8,128)S(1)}, u32[]{:S(2)}, u32[]{:S(2)}) collective-permute-start(f32[4,32,128]{2,1,0:T(8,128)S(1)} %get-tuple-element.47.refs_3_), channel_id=1, source_target_pairs={{0,24},{4,28},{8,16},{12,20},{16,8},{20,12},{24,0},{28,4},{1,25},{... | collective-permute-start | bytes 196616 | tf_op jit(solution)/shard_map/ppermute | solution.py:588
  25.1 5.2 %collective-permute-start.8 = (f32[4,32,128]{2,1,0:T(8,128)S(1)}, f32[4,32,128]{2,1,0:T(8,128)S(1)}, u32[]{:S(2)}, u32[]{:S(2)}) collective-permute-start(f32[4,32,128]{2,1,0:T(8,128)S(1)} %get-tuple-element.47.refs_3_), channel_id=1, source_target_pairs={{0,16},{4,20},{8,24},{12,28},{16,0},{20,4},{24,8},{28,12},{1,17},{... | collective-permute-start | bytes 196616 | tf_op jit(solution)/shard_map/ppermute | solution.py:588
  25.1 5.2 %collective-permute-start.9 = (f32[4,32,128]{2,1,0:T(8,128)S(1)}, f32[4,32,128]{2,1,0:T(8,128)S(1)}, u32[]{:S(2)}, u32[]{:S(2)}) collective-permute-start(f32[4,32,128]{2,1,0:T(8,128)S(1)} %get-tuple-element.47.refs_3_), channel_id=1, source_target_pairs={{0,8},{4,12},{8,0},{12,4},{16,24},{20,28},{24,16},{28,20},{1,9},{5... | collective-permute-start | bytes 196616 | tf_op jit(solution)/shard_map/ppermute | solution.py:588
  25.8 6.3 %collective-permute-start.10 = (f32[2,64,128]{2,1,0:T(8,128)S(1)}, f32[2,64,128]{2,1,0:T(8,128)S(1)}, u32[]{:S(2)}, u32[]{:S(2)}) collective-permute-start(f32[2,64,128]{2,1,0:T(8,128)S(1)} %get-tuple-element.48), channel_id=1, source_target_pairs={{0,8},{8,16},{12,4},{16,24},{20,12},{28,20},{1,9},{9,17},{13,5},{1... | collective-permute-start | bytes 196616 | tf_op jit(solution)/shard_map/ppermute | solution.py:637
  33.0 1.6 %collective-permute-start.11 = (f32[520,128]{1,0:T(8,128)S(1)}, f32[520,128]{1,0:T(8,128)S(1)}, u32[]{:S(2)}, u32[]{:S(2)}) collective-permute-start(f32[520,128]{1,0:T(8,128)S(1)} %get-tuple-element.50), channel_id=1, source_target_pairs={{0,1},{1,0},{2,3},{3,2},{4,5},{5,4},{6,7},{7,6},{8,9},{9,8},{10,11... | collective-permute-start | bytes 798728 | tf_op jit(solution)/shard_map/ppermute | solution.py:687
  34.6 13.5 %copy-start.1 = (f32[8,4,16,128]{3,2,1,0:T(8,128)S(1)}, f32[8,4,16,128]{3,2,1,0:T(8,128)}, u32[]{:S(2)}) copy-start(f32[8,4,16,128]{3,2,1,0:T(8,128)} %refs_1_.5) | copy-start | bytes 786436
  34.6 5.1 %collective-permute-start.12 = (f32[208,128]{1,0:T(8,128)S(1)}, f32[208,128]{1,0:T(8,128)S(1)}, u32[]{:S(2)}, u32[]{:S(2)}) collective-permute-start(f32[208,128]{1,0:T(8,128)S(1)} %get-tuple-element.52), channel_id=1, source_target_pairs={{0,2},{1,3},{2,0},{3,1},{4,6},{5,7},{6,4},{7,5},{8,10},{9,11},{10,... | collective-permute-start | bytes 319496 | tf_op jit(solution)/shard_map/ppermute | solution.py:579
  36.2 5.7 %collective-permute-start.13 = (f32[208,128]{1,0:T(8,128)S(1)}, f32[208,128]{1,0:T(8,128)S(1)}, u32[]{:S(2)}, u32[]{:S(2)}) collective-permute-start(f32[208,128]{1,0:T(8,128)S(1)} %get-tuple-element.53), channel_id=1, source_target_pairs={{0,4},{1,5},{2,6},{3,7},{4,0},{5,1},{6,2},{7,3},{8,12},{9,13},{10,... | collective-permute-start | bytes 319496 | tf_op jit(solution)/shard_map/ppermute | solution.py:579
  38.1 5.6 %collective-permute-start.14 = (f32[208,128]{1,0:T(8,128)S(1)}, f32[208,128]{1,0:T(8,128)S(1)}, u32[]{:S(2)}, u32[]{:S(2)}) collective-permute-start(f32[208,128]{1,0:T(8,128)S(1)} %get-tuple-element.54), channel_id=1, source_target_pairs={{0,6},{1,7},{2,4},{3,5},{4,2},{5,3},{6,0},{7,1},{8,14},{9,15},{10,... | collective-permute-start | bytes 319496 | tf_op jit(solution)/shard_map/ppermute | solution.py:579
  43.7 4.5 %copy-start.3 = (f32[4,16,128]{2,1,0:T(8,128)S(1)}, f32[4,16,128]{2,1,0:T(8,128)}, u32[]{:S(2)}) copy-start(f32[4,16,128]{2,1,0:T(8,128)} %refs_2_.3) | copy-start | bytes 98308
  43.7 5.4 %collective-permute-start.15 = (f32[1,128]{1,0:T(1,128)S(1)}, f32[1,128]{1,0:T(1,128)S(1)}, u32[]{:S(2)}, u32[]{:S(2)}) collective-permute-start(f32[1,128]{1,0:T(1,128)S(1)} %squares.1), channel_id=1, source_target_pairs={{0,24},{4,28},{8,16},{12,20},{16,8},{20,12},{24,0},{28,4},{1,25},{... | collective-permute-start | bytes 1544 | tf_op jit(solution)/shard_map/ppermute | solution.py:588
  46.9 4.4 %collective-permute-start.16 = (f32[1,128]{1,0:T(1,128)S(1)}, f32[1,128]{1,0:T(1,128)S(1)}, u32[]{:S(2)}, u32[]{:S(2)}) collective-permute-start(f32[1,128]{1,0:T(1,128)S(1)} %squares.1), channel_id=1, source_target_pairs={{0,16},{4,20},{8,24},{12,28},{16,0},{20,4},{24,8},{28,12},{1,17},{... | collective-permute-start | bytes 1544 | tf_op jit(solution)/shard_map/ppermute | solution.py:588
  46.9 4.4 %collective-permute-start.17 = (f32[1,128]{1,0:T(1,128)S(1)}, f32[1,128]{1,0:T(1,128)S(1)}, u32[]{:S(2)}, u32[]{:S(2)}) collective-permute-start(f32[1,128]{1,0:T(1,128)S(1)} %squares.1), channel_id=1, source_target_pairs={{0,8},{4,12},{8,0},{12,4},{16,24},{20,28},{24,16},{28,20},{1,9},{5... | collective-permute-start | bytes 1544 | tf_op jit(solution)/shard_map/ppermute | solution.py:588
  (1 other events, 0.8 us)

commit v24 on v23

--- a/solution.py
+++ b/solution.py
@@ -246,12 +246,6 @@
     return -k % count
 
 
-def keep_kernel(place, source_ref, reaction_ref, out_ref, kept_ref):
-    kept_ref[...] = reaction_ref[...]
-    for n in range(out_ref.shape[0]):
-        out_ref[n] = source_ref[2 * n + (place[0] & 1)]
-
-
 def scalars_kernel(place, shifts_ref, index_ref, velocity_ref, scalar_ref):
     rows = {0: shifts_ref[index_ref[place[0]]]}
     rows.update({1 + d: velocity_ref[d] for d in range(3)})
@@ -260,16 +254,16 @@
         scalar_ref[pl.ds(n, 1), :] = jnp.full((1, LANES), scalar, jnp.float32)
 
 
-def merge_kernel(place, mine_ref, theirs_ref, reaction_ref, other_reaction_ref, *out_refs):
+def merge_kernel(place, mine_ref, theirs_ref, other_reaction_ref, *out_refs):
     chip, core = place[0] // 2, place[0] & 1
-    by = mine_ref.shape[2]
+    columns, by = theirs_ref.shape[0], theirs_ref.shape[2]
     mine = pl.ds(pl.multiple_of(core * by, 8), by)
     theirs = pl.ds(pl.multiple_of((1 - core) * by, 8), by)
     for m, out_ref in enumerate(out_refs):
-        target = jnp.bitwise_xor(chip, m)
-        out_ref[0, :, mine, :] = mine_ref[target]
-        out_ref[0, :, theirs, :] = theirs_ref[2 * target + core]
-        out_ref[1, :, mine, :] = reaction_ref[...]
+        column = 2 * jnp.bitwise_xor(chip, m) + core
+        out_ref[0, :, mine, :] = mine_ref[column]
+        out_ref[0, :, theirs, :] = theirs_ref[column]
+        out_ref[1, :, mine, :] = mine_ref[columns]
         out_ref[1, :, theirs, :] = other_reaction_ref[...]
 
 
@@ -601,9 +595,7 @@
     chips, chips_y = columns // 2, gy_size // 2
     cores = [(i, i ^ 1) for i in range(gy_size)]
     theirs = [lax.ppermute(source, "gy", cores), lax.ppermute(reaction, "gy", cores)]
-    mine, kept = local_kernel(
-        keep_kernel, "keep", (), (source, reaction), [(chips, bx, by, nz), reaction.shape]
-    )
+    mine = jnp.concatenate([source, reaction[None]])
     (scalar_rows,) = local_kernel(
         scalars_kernel, "scalars", (shifts, shift_index, velocity), (), [(8 + columns, LANES)]
     )
@@ -611,7 +603,7 @@
         merge_kernel,
         "merge",
         (),
-        (mine, theirs[0], kept, theirs[1]),
+        (mine, *theirs),
         [(2, bx, 2 * by, nz)] * chips,
     )
     blocks = swap_in_plane(blocks, 2)

time: 52.1 us -> 51.6 us (level)
  local copies, waits for them, and re-layouts: 1.74 us -> 0.03 us
  other arithmetic: 0.66 us -> 1.65 us
    unnamed x14 -> x10, local copies, waits for them, and re-layouts: 1.74 us -> 0.03 us
    concatenate x0 -> x1, other arithmetic: none -> 0.99 us  [column_body(): mine = jnp.concatenate([source, reaction[None]])]
    pallas_call x13 -> x12, Pallas kernels: 5.16 us -> 5.13 us  [local_kernel(): pl.pallas_call(placed, out_shape=[jax.ShapeDtypeStruct(shape, jnp.float32...]
  transfers between devices with their start and end apart: 18 -> 18, of which waited for: 11 -> 12; matrix products, arithmetic and copies ran while one was open for 0% -> 2% of each run, Pallas kernels for 7% -> 7%
where the time goes in v24:
time: 51.6 us; the launch traced here: 51.4 us
  starting transfers between devices  26.7 us (52%)
  waiting for transfers between devices  17.1 us (33%)
  Pallas kernels  5.13 us (10%)
  other arithmetic  1.65 us (3%)
  between operations  0.84 us (2%)
    ppermute x6, waiting for transfers between devices, swap_in_plane(): moved.append(lax.ppermute(pieces[k], ('gx', 'gy'), pairs))  9.68 us
    ppermute x6, starting transfers between devices, swap_slabs(): moved.append(lax.ppermute(piece, 'gx', pairs))  9.63 us
    ppermute x3, starting transfers between devices, send_beside(): lax.ppermute(piece, 'gx', [(i, j) for i, j in pairs if 0 <= j < gx_size])  8.34 us
    ppermute x6, starting transfers between devices, swap_in_plane(): moved.append(lax.ppermute(pieces[k], ('gx', 'gy'), pairs))  8.05 us
    pallas_call x12, Pallas kernels, local_kernel(): pl.pallas_call(placed, out_shape=[jax.ShapeDtypeStruct(shape, jnp.float32...  5.13 us
    ppermute x6, waiting for transfers between devices, swap_slabs(): moved.append(lax.ppermute(piece, 'gx', pairs))  3.36 us
    ppermute x3, waiting for transfers between devices, send_beside(): lax.ppermute(piece, 'gx', [(i, j) for i, j in pairs if 0 <= j < gx_size])  2.16 us
    ppermute x1, waiting for transfers between devices, column_body(): lax.ppermute(sent, 'gy', cores)  1.53 us
  transfers between devices with their start and end apart: 18, of which 12 were waited for; matrix products, arithmetic and copies ran while one was open for 2% of the time, Pallas kernels for 7%

profile of v24, /device:TPU:0, one launch (start us, length us, event | category | flops | bytes accessed | tf_op | source)
XLA Modules:
  0.0 51.4 jit_solution(2559399162342599884)
XLA Ops:
  1.2 1.0 %pad_maximum_fusion.refs_0_ = f32[9,4,16,128]{3,2,1,0:T(8,128)S(1)} fusion(f32[1,4,16,128]{3,2,1,0:T(8,128)} %bitcast.3, f32[8,4,16,128]{3,2,1,0:T(8,128)} %refs_1_.3), kind=kLoop, calls=%fused_computation | loop fusion | flops 73728 | bytes 589824 | tf_op jit(solution)/shard_map/concatenate | solution.py:598
  2.6 3.0 %collective-permute-start.2 = (f32[2,4,32,128]{3,2,1,0:T(8,128)S(1)}, f32[2,4,32,128]{3,2,1,0:T(8,128)S(1)}, u32[]{:S(2)}, u32[]{:S(2)}) collective-permute-start(f32[2,4,32,128]{3,2,1,0:T(8,128)S(1)} %get-tuple-element.29), channel_id=1, source_target_pairs={{0,2},{1,3},{2,0},{3,1},{4,6},{5,7},{6,4},{7,5},{8,10},{9,11},{10,... | collective-permute-start | bytes 393224 | tf_op jit(solution)/shard_map/ppermute | solution.py:573
  5.6 1.5 %collective-permute-start.3 = (f32[2,4,32,128]{3,2,1,0:T(8,128)S(1)}, f32[2,4,32,128]{3,2,1,0:T(8,128)S(1)}, u32[]{:S(2)}, u32[]{:S(2)}) collective-permute-start(f32[2,4,32,128]{3,2,1,0:T(8,128)S(1)} %get-tuple-element.30), channel_id=1, source_target_pairs={{0,4},{1,5},{2,6},{3,7},{4,0},{5,1},{6,2},{7,3},{8,12},{9,13},{10,... | collective-permute-start | bytes 393224 | tf_op jit(solution)/shard_map/ppermute | solution.py:573
  7.1 2.3 %collective-permute-done.2.refs_1_ = f32[2,4,32,128]{3,2,1,0:T(8,128)S(1)} collective-permute-done((f32[2,4,32,128]{3,2,1,0:T(8,128)S(1)}, f32[2,4,32,128]{3,2,1,0:T(8,128)S(1)}, u32[]{:S(2)}, u32[]{:S(2)}) %collective-permute-start.2) | collective-permute-done | bytes 131104 | tf_op jit(solution)/shard_map/ppermute | solution.py:573
  9.4 1.4 %collective-permute-start.5 = (f32[2,4,64,128]{3,2,1,0:T(8,128)S(1)}, f32[2,4,64,128]{3,2,1,0:T(8,128)S(1)}, u32[]{:S(2)}, u32[]{:S(2)}) collective-permute-start(f32[2,4,64,128]{3,2,1,0:T(8,128)S(1)} %half.1), channel_id=1, source_target_pairs={{4,12},{8,0},{12,20},{16,8},{20,28},{24,16},{5,13},{9,1},{13,21},{... | collective-permute-start | bytes 786440 | tf_op jit(solution)/shard_map/ppermute | solution.py:629
  11.9 1.5 %collective-permute-done.4.refs_3_ = f32[2,4,32,128]{3,2,1,0:T(8,128)S(1)} collective-permute-done((f32[2,4,32,128]{3,2,1,0:T(8,128)S(1)}, f32[2,4,32,128]{3,2,1,0:T(8,128)S(1)}, u32[]{:S(2)}, u32[]{:S(2)}) %collective-permute-start.4) | collective-permute-done | bytes 131104 | tf_op jit(solution)/shard_map/ppermute | solution.py:573
  13.5 3.6 %collective-permute-start.6 = (f32[2,2,64,128]{3,2,1,0:T(8,128)S(1)}, f32[2,2,64,128]{3,2,1,0:T(8,128)S(1)}, u32[]{:S(2)}, u32[]{:S(2)}) collective-permute-start(f32[2,2,64,128]{3,2,1,0:T(8,128)S(1)} %get-tuple-element.38), channel_id=1, source_target_pairs={{0,8},{8,16},{12,4},{16,24},{20,12},{28,20},{1,9},{9,17},{13,5},{1... | collective-permute-start | bytes 393224 | tf_op jit(solution)/shard_map/ppermute | solution.py:629
  17.5 2.2 %collective-permute-done.6.refs_7_ = f32[2,2,64,128]{3,2,1,0:T(8,128)S(1)} collective-permute-done((f32[2,2,64,128]{3,2,1,0:T(8,128)S(1)}, f32[2,2,64,128]{3,2,1,0:T(8,128)S(1)}, u32[]{:S(2)}, u32[]{:S(2)}) %collective-permute-start.6) | collective-permute-done | bytes 131104 | tf_op jit(solution)/shard_map/ppermute | solution.py:629
  20.2 4.5 %collective-permute-start.7 = (f32[4,32,128]{2,1,0:T(8,128)S(1)}, f32[4,32,128]{2,1,0:T(8,128)S(1)}, u32[]{:S(2)}, u32[]{:S(2)}) collective-permute-start(f32[4,32,128]{2,1,0:T(8,128)S(1)} %get-tuple-element.43.refs_3_), channel_id=1, source_target_pairs={{0,24},{4,28},{8,16},{12,20},{16,8},{20,12},{24,0},{28,4},{1,25},{... | collective-permute-start | bytes 196616 | tf_op jit(solution)/shard_map/ppermute | solution.py:582
  24.7 0.6 %collective-permute-start.9 = (f32[4,32,128]{2,1,0:T(8,128)S(1)}, f32[4,32,128]{2,1,0:T(8,128)S(1)}, u32[]{:S(2)}, u32[]{:S(2)}) collective-permute-start(f32[4,32,128]{2,1,0:T(8,128)S(1)} %get-tuple-element.43.refs_3_), channel_id=1, source_target_pairs={{0,8},{4,12},{8,0},{12,4},{16,24},{20,28},{24,16},{28,20},{1,9},{5... | collective-permute-start | bytes 196616 | tf_op jit(solution)/shard_map/ppermute | solution.py:582
  25.4 3.3 %collective-permute-start.10 = (f32[2,64,128]{2,1,0:T(8,128)S(1)}, f32[2,64,128]{2,1,0:T(8,128)S(1)}, u32[]{:S(2)}, u32[]{:S(2)}) collective-permute-start(f32[2,64,128]{2,1,0:T(8,128)S(1)} %get-tuple-element.44), channel_id=1, source_target_pairs={{0,8},{8,16},{12,4},{16,24},{20,12},{28,20},{1,9},{9,17},{13,5},{1... | collective-permute-start | bytes 196616 | tf_op jit(solution)/shard_map/ppermute | solution.py:629
  28.8 1.1 %collective-permute-done.8.refs_5_ = f32[4,32,128]{2,1,0:T(8,128)S(1)} collective-permute-done((f32[4,32,128]{2,1,0:T(8,128)S(1)}, f32[4,32,128]{2,1,0:T(8,128)S(1)}, u32[]{:S(2)}, u32[]{:S(2)}) %collective-permute-start.8) | collective-permute-done | bytes 65568 | tf_op jit(solution)/shard_map/ppermute | solution.py:582
  29.9 1.7 %coarse.1.refs_5_ = f32[256,128]{1,0:T(8,128)S(1)} custom-call(f32[16,128]{1,0:T(8,128)S(1)} %scalars.1.refs_0_, bf16[128,128]{1,0:T(8,128)(2,1)S(1)} %get-tuple-element.54.refs_8_.refs_1_, bf16[128,128]{1,0:T(8,128)(2,1)S(1)} %get-tuple-element.53.refs_2_, f32[4,32,128]{2,1,0:T(8,128)S(1)} %get-tuple-element.43.refs_3_, ...), custom_call_target="tpu_custom_call" | custom-call | tf_op jit(solution)/shard_map/coarse/pallas_call | solution.py:556
  31.6 0.9 %post.1 = (f32[520,128]{1,0:T(8,128)S(1)}, f32[520,128]{1,0:T(8,128)S(1)}) custom-call(f32[16,128]{1,0:T(8,128)S(1)} %scalars.1.refs_0_, f32[16,64,128]{2,1,0:T(8,128)S(1)} %get-tuple-element.39.refs_1_, f32[16,64,128]{2,1,0:T(8,128)S(1)} %get-tuple-element.40.refs_2_, f32[16,64,128]{2,1,0:T(8,128)S(1)} %get-tuple-element.41.refs_3_, ...), custom_call_target="tpu_custom_call" | custom-call | tf_op jit(solution)/shard_map/post/pallas_call | solution.py:556
  32.6 1.5 %collective-permute-done.11.refs_1_ = f32[520,128]{1,0:T(8,128)S(1)} collective-permute-done((f32[520,128]{1,0:T(8,128)S(1)}, f32[520,128]{1,0:T(8,128)S(1)}, u32[]{:S(2)}, u32[]{:S(2)}) %collective-permute-start.11) | collective-permute-done | bytes 266272 | tf_op jit(solution)/shard_map/ppermute | solution.py:679
  34.2 1.6 %collective-permute-start.12 = (f32[208,128]{1,0:T(8,128)S(1)}, f32[208,128]{1,0:T(8,128)S(1)}, u32[]{:S(2)}, u32[]{:S(2)}) collective-permute-start(f32[208,128]{1,0:T(8,128)S(1)} %get-tuple-element.48), channel_id=1, source_target_pairs={{0,2},{1,3},{2,0},{3,1},{4,6},{5,7},{6,4},{7,5},{8,10},{9,11},{10,... | collective-permute-start | bytes 319496 | tf_op jit(solution)/shard_map/ppermute | solution.py:573
  35.8 1.9 %collective-permute-start.13 = (f32[208,128]{1,0:T(8,128)S(1)}, f32[208,128]{1,0:T(8,128)S(1)}, u32[]{:S(2)}, u32[]{:S(2)}) collective-permute-start(f32[208,128]{1,0:T(8,128)S(1)} %get-tuple-element.49), channel_id=1, source_target_pairs={{0,4},{1,5},{2,6},{3,7},{4,0},{5,1},{6,2},{7,3},{8,12},{9,13},{10,... | collective-permute-start | bytes 319496 | tf_op jit(solution)/shard_map/ppermute | solution.py:573
  37.8 1.5 %collective-permute-done.12.refs_4_.refs_1_ = f32[208,128]{1,0:T(8,128)S(1)} collective-permute-done((f32[208,128]{1,0:T(8,128)S(1)}, f32[208,128]{1,0:T(8,128)S(1)}, u32[]{:S(2)}, u32[]{:S(2)}) %collective-permute-start.12) | collective-permute-done | bytes 106528 | tf_op jit(solution)/shard_map/ppermute | solution.py:573
  39.3 2.2 %collective-permute-done.13.refs_5_.refs_2_ = f32[208,128]{1,0:T(8,128)S(1)} collective-permute-done((f32[208,128]{1,0:T(8,128)S(1)}, f32[208,128]{1,0:T(8,128)S(1)}, u32[]{:S(2)}, u32[]{:S(2)}) %collective-permute-start.13) | collective-permute-done | bytes 106528 | tf_op jit(solution)/shard_map/ppermute | solution.py:573
  41.5 1.7 %collective-permute-done.14.refs_6_.refs_3_ = f32[208,128]{1,0:T(8,128)S(1)} collective-permute-done((f32[208,128]{1,0:T(8,128)S(1)}, f32[208,128]{1,0:T(8,128)S(1)}, u32[]{:S(2)}, u32[]{:S(2)}) %collective-permute-start.14) | collective-permute-done | bytes 106528 | tf_op jit(solution)/shard_map/ppermute | solution.py:573
  43.3 3.2 %collective-permute-start.15 = (f32[1,128]{1,0:T(1,128)S(1)}, f32[1,128]{1,0:T(1,128)S(1)}, u32[]{:S(2)}, u32[]{:S(2)}) collective-permute-start(f32[1,128]{1,0:T(1,128)S(1)} %squares.1), channel_id=1, source_target_pairs={{0,24},{4,28},{8,16},{12,20},{16,8},{20,12},{24,0},{28,4},{1,25},{... | collective-permute-start | bytes 1544 | tf_op jit(solution)/shard_map/ppermute | solution.py:582
  46.4 1.3 %collective-permute-start.17 = (f32[1,128]{1,0:T(1,128)S(1)}, f32[1,128]{1,0:T(1,128)S(1)}, u32[]{:S(2)}, u32[]{:S(2)}) collective-permute-start(f32[1,128]{1,0:T(1,128)S(1)} %squares.1), channel_id=1, source_target_pairs={{0,8},{4,12},{8,0},{12,4},{16,24},{20,28},{24,16},{28,20},{1,9},{5... | collective-permute-start | bytes 1544 | tf_op jit(solution)/shard_map/ppermute | solution.py:582
  47.7 0.9 %collect.1 = (f32[8,4,16,128]{3,2,1,0:T(8,128)}, f32[8,4,16,128]{3,2,1,0:T(8,128)}) custom-call(f32[16,128]{1,0:T(8,128)S(1)} %scalars.1.refs_0_, f32[8,4,16,128]{3,2,1,0:T(8,128)S(1)} %copy-done, f32[4,16,128]{2,1,0:T(8,128)S(1)} %copy-done.1, f32[208,128]{1,0:T(8,128)S(1)} %get-tuple-element.47.refs_3_.refs_0_, ...), custom_call_target="tpu_custom_call" | custom-call | tf_op jit(solution)/shard_map/collect/pallas_call | solution.py:556
  48.7 2.2 %collective-permute-done.16 = f32[1,128]{1,0:T(1,128)S(1)} collective-permute-done((f32[1,128]{1,0:T(1,128)S(1)}, f32[1,128]{1,0:T(1,128)S(1)}, u32[]{:S(2)}, u32[]{:S(2)}) %collective-permute-start.16) | collective-permute-done | bytes 544 | tf_op jit(solution)/shard_map/ppermute | solution.py:582
  (40 shorter events, 4.0 us)
Async XLA Ops:
  0.6 1.9 %collective-permute-start = (f32[8,4,16,128]{3,2,1,0:T(8,128)}, f32[8,4,16,128]{3,2,1,0:T(8,128)S(1)}, u32[]{:S(2)}, u32[]{:S(2)}) collective-permute-start(f32[8,4,16,128]{3,2,1,0:T(8,128)} %refs_1_.3), channel_id=1, source_target_pairs={{0,1},{1,0},{2,3},{3,2},{4,5},{5,4},{6,7},{7,6},{8,9},{9,8},{10,11... | collective-permute-start | bytes 786440 | tf_op jit(solution)/shard_map/ppermute | solution.py:597
  1.1 1.4 %collective-permute-start.1 = (f32[4,16,128]{2,1,0:T(8,128)}, f32[4,16,128]{2,1,0:T(8,128)S(1)}, u32[]{:S(2)}, u32[]{:S(2)}) collective-permute-start(f32[4,16,128]{2,1,0:T(8,128)} %refs_2_.3), channel_id=1, source_target_pairs={{0,1},{1,0},{2,3},{3,2},{4,5},{5,4},{6,7},{7,6},{8,9},{9,8},{10,11... | collective-permute-start | bytes 98312 | tf_op jit(solution)/shard_map/ppermute | solution.py:597
  2.6 6.8 %collective-permute-start.2 = (f32[2,4,32,128]{3,2,1,0:T(8,128)S(1)}, f32[2,4,32,128]{3,2,1,0:T(8,128)S(1)}, u32[]{:S(2)}, u32[]{:S(2)}) collective-permute-start(f32[2,4,32,128]{3,2,1,0:T(8,128)S(1)} %get-tuple-element.29), channel_id=1, source_target_pairs={{0,2},{1,3},{2,0},{3,1},{4,6},{5,7},{6,4},{7,5},{8,10},{9,11},{10,... | collective-permute-start | bytes 393224 | tf_op jit(solution)/shard_map/ppermute | solution.py:573
  5.6 6.4 %collective-permute-start.3 = (f32[2,4,32,128]{3,2,1,0:T(8,128)S(1)}, f32[2,4,32,128]{3,2,1,0:T(8,128)S(1)}, u32[]{:S(2)}, u32[]{:S(2)}) collective-permute-start(f32[2,4,32,128]{3,2,1,0:T(8,128)S(1)} %get-tuple-element.30), channel_id=1, source_target_pairs={{0,4},{1,5},{2,6},{3,7},{4,0},{5,1},{6,2},{7,3},{8,12},{9,13},{10,... | collective-permute-start | bytes 393224 | tf_op jit(solution)/shard_map/ppermute | solution.py:573
  7.1 6.4 %collective-permute-start.4 = (f32[2,4,32,128]{3,2,1,0:T(8,128)S(1)}, f32[2,4,32,128]{3,2,1,0:T(8,128)S(1)}, u32[]{:S(2)}, u32[]{:S(2)}) collective-permute-start(f32[2,4,32,128]{3,2,1,0:T(8,128)S(1)} %get-tuple-element.31), channel_id=1, source_target_pairs={{0,6},{1,7},{2,4},{3,5},{4,2},{5,3},{6,0},{7,1},{8,14},{9,15},{10,... | collective-permute-start | bytes 393224 | tf_op jit(solution)/shard_map/ppermute | solution.py:573
  9.4 1.5 %copy-start.2 = (f32[8]{0:T(128)S(1)}, f32[8]{0:T(128)}, u32[]{:S(2)}) copy-start(f32[8]{0:T(128)} %refs_0_.1) | copy-start | bytes 100
  9.4 1.5 %copy-start.3 = (s32[8]{0:T(128)S(1)}, s32[8]{0:T(128)}, u32[]{:S(2)}) copy-start(s32[8]{0:T(128)} %refs_1_.2) | copy-start | bytes 100
  9.4 1.5 %copy-start.4 = (f32[3]{0:T(128)S(1)}, f32[3]{0:T(128)}, u32[]{:S(2)}) copy-start(f32[3]{0:T(128)} %refs_2_.2) | copy-start | bytes 40
  9.4 10.2 %collective-permute-start.5 = (f32[2,4,64,128]{3,2,1,0:T(8,128)S(1)}, f32[2,4,64,128]{3,2,1,0:T(8,128)S(1)}, u32[]{:S(2)}, u32[]{:S(2)}) collective-permute-start(f32[2,4,64,128]{3,2,1,0:T(8,128)S(1)} %half.1), channel_id=1, source_target_pairs={{4,12},{8,0},{12,20},{16,8},{20,28},{24,16},{5,13},{9,1},{13,21},{... | collective-permute-start | bytes 786440 | tf_op jit(solution)/shard_map/ppermute | solution.py:629
  13.5 6.1 %collective-permute-start.6 = (f32[2,2,64,128]{3,2,1,0:T(8,128)S(1)}, f32[2,2,64,128]{3,2,1,0:T(8,128)S(1)}, u32[]{:S(2)}, u32[]{:S(2)}) collective-permute-start(f32[2,2,64,128]{3,2,1,0:T(8,128)S(1)} %get-tuple-element.38), channel_id=1, source_target_pairs={{0,8},{8,16},{12,4},{16,24},{20,12},{28,20},{1,9},{9,17},{13,5},{1... | collective-permute-start | bytes 393224 | tf_op jit(solution)/shard_map/ppermute | solution.py:629
  20.2 8.6 %collective-permute-start.7 = (f32[4,32,128]{2,1,0:T(8,128)S(1)}, f32[4,32,128]{2,1,0:T(8,128)S(1)}, u32[]{:S(2)}, u32[]{:S(2)}) collective-permute-start(f32[4,32,128]{2,1,0:T(8,128)S(1)} %get-tuple-element.43.refs_3_), channel_id=1, source_target_pairs={{0,24},{4,28},{8,16},{12,20},{16,8},{20,12},{24,0},{28,4},{1,25},{... | collective-permute-start | bytes 196616 | tf_op jit(solution)/shard_map/ppermute | solution.py:582
  24.7 5.2 %collective-permute-start.8 = (f32[4,32,128]{2,1,0:T(8,128)S(1)}, f32[4,32,128]{2,1,0:T(8,128)S(1)}, u32[]{:S(2)}, u32[]{:S(2)}) collective-permute-start(f32[4,32,128]{2,1,0:T(8,128)S(1)} %get-tuple-element.43.refs_3_), channel_id=1, source_target_pairs={{0,16},{4,20},{8,24},{12,28},{16,0},{20,4},{24,8},{28,12},{1,17},{... | collective-permute-start | bytes 196616 | tf_op jit(solution)/shard_map/ppermute | solution.py:582
  24.7 5.2 %collective-permute-start.9 = (f32[4,32,128]{2,1,0:T(8,128)S(1)}, f32[4,32,128]{2,1,0:T(8,128)S(1)}, u32[]{:S(2)}, u32[]{:S(2)}) collective-permute-start(f32[4,32,128]{2,1,0:T(8,128)S(1)} %get-tuple-element.43.refs_3_), channel_id=1, source_target_pairs={{0,8},{4,12},{8,0},{12,4},{16,24},{20,28},{24,16},{28,20},{1,9},{5... | collective-permute-start | bytes 196616 | tf_op jit(solution)/shard_map/ppermute | solution.py:582
  25.4 6.3 %collective-permute-start.10 = (f32[2,64,128]{2,1,0:T(8,128)S(1)}, f32[2,64,128]{2,1,0:T(8,128)S(1)}, u32[]{:S(2)}, u32[]{:S(2)}) collective-permute-start(f32[2,64,128]{2,1,0:T(8,128)S(1)} %get-tuple-element.44), channel_id=1, source_target_pairs={{0,8},{8,16},{12,4},{16,24},{20,12},{28,20},{1,9},{9,17},{13,5},{1... | collective-permute-start | bytes 196616 | tf_op jit(solution)/shard_map/ppermute | solution.py:629
  32.5 1.6 %collective-permute-start.11 = (f32[520,128]{1,0:T(8,128)S(1)}, f32[520,128]{1,0:T(8,128)S(1)}, u32[]{:S(2)}, u32[]{:S(2)}) collective-permute-start(f32[520,128]{1,0:T(8,128)S(1)} %get-tuple-element.46), channel_id=1, source_target_pairs={{0,1},{1,0},{2,3},{3,2},{4,5},{5,4},{6,7},{7,6},{8,9},{9,8},{10,11... | collective-permute-start | bytes 798728 | tf_op jit(solution)/shard_map/ppermute | solution.py:679
  34.2 13.5 %copy-start = (f32[8,4,16,128]{3,2,1,0:T(8,128)S(1)}, f32[8,4,16,128]{3,2,1,0:T(8,128)}, u32[]{:S(2)}) copy-start(f32[8,4,16,128]{3,2,1,0:T(8,128)} %refs_1_.3) | copy-start | bytes 786436
  34.2 5.1 %collective-permute-start.12 = (f32[208,128]{1,0:T(8,128)S(1)}, f32[208,128]{1,0:T(8,128)S(1)}, u32[]{:S(2)}, u32[]{:S(2)}) collective-permute-start(f32[208,128]{1,0:T(8,128)S(1)} %get-tuple-element.48), channel_id=1, source_target_pairs={{0,2},{1,3},{2,0},{3,1},{4,6},{5,7},{6,4},{7,5},{8,10},{9,11},{10,... | collective-permute-start | bytes 319496 | tf_op jit(solution)/shard_map/ppermute | solution.py:573
  35.8 5.7 %collective-permute-start.13 = (f32[208,128]{1,0:T(8,128)S(1)}, f32[208,128]{1,0:T(8,128)S(1)}, u32[]{:S(2)}, u32[]{:S(2)}) collective-permute-start(f32[208,128]{1,0:T(8,128)S(1)} %get-tuple-element.49), channel_id=1, source_target_pairs={{0,4},{1,5},{2,6},{3,7},{4,0},{5,1},{6,2},{7,3},{8,12},{9,13},{10,... | collective-permute-start | bytes 319496 | tf_op jit(solution)/shard_map/ppermute | solution.py:573
  37.7 5.6 %collective-permute-start.14 = (f32[208,128]{1,0:T(8,128)S(1)}, f32[208,128]{1,0:T(8,128)S(1)}, u32[]{:S(2)}, u32[]{:S(2)}) collective-permute-start(f32[208,128]{1,0:T(8,128)S(1)} %get-tuple-element.50), channel_id=1, source_target_pairs={{0,6},{1,7},{2,4},{3,5},{4,2},{5,3},{6,0},{7,1},{8,14},{9,15},{10,... | collective-permute-start | bytes 319496 | tf_op jit(solution)/shard_map/ppermute | solution.py:573
  43.3 4.5 %copy-start.1 = (f32[4,16,128]{2,1,0:T(8,128)S(1)}, f32[4,16,128]{2,1,0:T(8,128)}, u32[]{:S(2)}) copy-start(f32[4,16,128]{2,1,0:T(8,128)} %refs_2_.3) | copy-start | bytes 98308
  43.3 5.4 %collective-permute-start.15 = (f32[1,128]{1,0:T(1,128)S(1)}, f32[1,128]{1,0:T(1,128)S(1)}, u32[]{:S(2)}, u32[]{:S(2)}) collective-permute-start(f32[1,128]{1,0:T(1,128)S(1)} %squares.1), channel_id=1, source_target_pairs={{0,24},{4,28},{8,16},{12,20},{16,8},{20,12},{24,0},{28,4},{1,25},{... | collective-permute-start | bytes 1544 | tf_op jit(solution)/shard_map/ppermute | solution.py:582
  46.4 4.4 %collective-permute-start.16 = (f32[1,128]{1,0:T(1,128)S(1)}, f32[1,128]{1,0:T(1,128)S(1)}, u32[]{:S(2)}, u32[]{:S(2)}) collective-permute-start(f32[1,128]{1,0:T(1,128)S(1)} %squares.1), channel_id=1, source_target_pairs={{0,16},{4,20},{8,24},{12,28},{16,0},{20,4},{24,8},{28,12},{1,17},{... | collective-permute-start | bytes 1544 | tf_op jit(solution)/shard_map/ppermute | solution.py:582
  46.4 4.4 %collective-permute-start.17 = (f32[1,128]{1,0:T(1,128)S(1)}, f32[1,128]{1,0:T(1,128)S(1)}, u32[]{:S(2)}, u32[]{:S(2)}) collective-permute-start(f32[1,128]{1,0:T(1,128)S(1)} %squares.1), channel_id=1, source_target_pairs={{0,8},{4,12},{8,0},{12,4},{16,24},{20,28},{24,16},{28,20},{1,9},{5... | collective-permute-start | bytes 1544 | tf_op jit(solution)/shard_map/ppermute | solution.py:582

commit v25 on v24

--- a/solution.py
+++ b/solution.py
@@ -277,7 +277,7 @@
 
 
 def arrange_kernel(chips_y, place, *refs):
-    blocks, (slab_ref, near_ref) = refs[:-2], refs[-2:]
+    blocks, (slab_ref, near_ref, far_ref) = refs[:-3], refs[-3:]
     chip = place[0] // 2
     for m, block in enumerate(blocks):
         owner = jnp.bitwise_xor(chip, m)
@@ -287,24 +287,30 @@
         slab_ref[:, planes, rows, :] = block[...]
     other = 1 - chip // chips_y
     near_ref[...] = slab_ref[:, pl.ds(other * (SLAB - NEAR), NEAR)]
-
-
-def beyond_kernel(slabs, chips_y, place, scalar_ref, half_ref, out_ref, f, r, w, v0):
+    far_ref[...] = slab_ref[:, pl.ds(NEAR + other * (SLAB - 3 * NEAR), NEAR)]
+
+
+def beyond_kernel(slabs, chips_y, place, scalar_ref, half_ref, near_ref, far_ref, *refs):
+    out_refs, (f, r, w, v0) = refs[:2], refs[2:]
     ny, slab = f.shape[1], place[1]
     x = place[0] // 2 // chips_y
     fine = Level(0, ny, LANES, 0, scalars_of(scalar_ref), f, r, w)
     zero_rows(v0, ny)
-    f[...], r[...] = half_ref[0], half_ref[1]
-    beside = jnp.where(x == 0, slab < slabs - 1, slab > 0)
-    inside = jnp.where(beside, DAMPING, 0.0)
-
-    def put(at, weight):
-        w[at] = weight
-        v0[at, pl.ds(8, ny), :] = weight * f[at]
-
-    sweep(range(HALO), lambda at: inside / (r[at] + fine.centre), put)
-    for n in range(NEAR):
-        out_ref[n] = fine.smoothed(v0, 1 + n)
+    last = NEAR * (1 - x)
+    sides = ((1 - x, ((half_ref, 0, HALO),)), (x, ((near_ref, last, NEAR), (far_ref, NEAR - last, NEAR))))
+    for out_ref, (above, parts) in zip(out_refs, sides):
+        for ref, first, size in parts:
+            f[pl.ds(first, size)], r[pl.ds(first, size)] = ref[0], ref[1]
+        beside = jnp.where(above == 1, slab < slabs - 1, slab > 0)
+        inside = jnp.where(beside, DAMPING, 0.0)
+
+        def put(at, weight):
+            w[at] = weight
+            v0[at, pl.ds(8, ny), :] = weight * f[at]
+
+        sweep(range(HALO), lambda at: inside / (r[at] + fine.centre), put)
+        for n in range(NEAR):
+            out_ref[n] = fine.smoothed(v0, 1 + n)
 
 
 def begin_kernel(_, scalar_ref, slab_ref, f, r, w, v0, v1):
@@ -325,7 +331,7 @@
 
 def pre_kernel(slabs, chips_y, place, scalar_ref, *refs):
     half_ref, near_ref, pool_ref, pool_up_ref = refs[5:9]
-    f, r, w, v0, v1, coarse_ref, beyond_ref, tmp, pooled = refs[9:]
+    f, r, w, v0, v1, coarse_ref, tmp, pooled = refs[9:]
     ny = f.shape[1]
     slab = place[1]
     fine = Level(0, ny, LANES, 0, scalars_of(scalar_ref), f, r, w)
@@ -359,8 +365,6 @@
     sweep(range(SLAB // 2), coarsened, put_pooled)
     packed = split_dot(pooled[0], pool_ref[...]) + split_dot(pooled[1], pool_up_ref[...])
     coarse_ref[...] = packed.reshape(coarse_ref.shape)
-    first = HALO + 1 + (1 - x) * (SLAB - HALO)
-    beyond_ref[...] = v1[pl.ds(first, NEAR), pl.ds(8, ny), :]
 
 
 def coarse_kernel(grid, place, scalar_ref, *refs):
@@ -616,37 +620,37 @@
         blocks[:chips_y],
         [(2, HALO, ny, nz)],
     )
-    slab, near = local_kernel(
+    slab, near, far = local_kernel(
         functools.partial(arrange_kernel, chips_y),
         "arrange",
         (),
         blocks,
-        [(2, SLAB, ny, nz), edge],
+        [(2, SLAB, ny, nz), edge, edge],
     )
 
     def send_beside(piece, up):
         pairs = [(i, i + step if i % step == up else i - step) for i in range(gx_size)]
         return lax.ppermute(piece, "gx", [(i, j) for i, j in pairs if 0 <= j < gx_size])
 
-    beside = [send_beside(own_half, 1), send_beside(near, 0)]
+    beside = [send_beside(own_half, 1), send_beside(near, 0), send_beside(far, 0)]
     grid, rimmed = (count, ny, nz), (count, ny + 16, nz)
     fields = [grid, grid, grid, rimmed, rimmed]
     fields_own = local_kernel(begin_kernel, "begin", (), (scalar_rows, slab), fields)
-    f, r, w, _, v1, coarse, beyond = local_kernel(
+    f, r, w, _, v1, coarse = local_kernel(
         functools.partial(pre_kernel, slabs, chips_y),
         "pre",
         (),
-        (scalar_rows, *fields_own, *beside, pool_matrix(0), pool_matrix(LANES // 2)),
-        fields + [(SLAB // 2, ny // 2, nz), (NEAR, ny, nz)],
+        (scalar_rows, *fields_own, *beside[:2], pool_matrix(0), pool_matrix(LANES // 2)),
+        fields + [(SLAB // 2, ny // 2, nz)],
         [(SLAB, ny, nz), (2, SLAB // 2 * ny // 2, nz)],
         in_place=range(1, 1 + len(fields)),
     )
-    (own_beyond,) = local_kernel(
+    beyond = local_kernel(
         functools.partial(beyond_kernel, slabs, chips_y),
         "beyond",
         (),
-        (scalar_rows, beside[0]),
-        [(NEAR, ny, nz)],
+        (scalar_rows, *beside),
+        [(NEAR, ny, nz)] * 2,
         [(HALO, ny, nz)] * 3 + [(HALO, ny + 16, nz)],
     )
     gathered = swap_slabs(coarse, step, slabs)
@@ -667,7 +671,7 @@
         functools.partial(post_kernel, by, chips_y),
         "post",
         (),
-        (scalar_rows, f, r, w, v1, correction, own_beyond, send_beside(beyond, 0)),
+        (scalar_rows, f, r, w, v1, correction, *beyond),
         [result, result],
         [rimmed] * 2 + [(SLAB, ny, nz)],
     )

time: 51.6 us -> 53 us (1.027)
  waiting for transfers between devices: 17.1 us -> 18.5 us
  starting transfers between devices: 26.7 us -> 26 us
    ppermute x6, waiting for transfers between devices: 3.36 us -> 6.6 us  [swap_slabs(): moved.append(lax.ppermute(piece, 'gx', pairs))]
    ppermute x3, waiting for transfers between devices: 2.16 us -> 0.01 us  [send_beside(): lax.ppermute(piece, 'gx', [(i, j) for i, j in pairs if 0 <= j < gx_size])]
    ppermute x6, starting transfers between devices: 9.63 us -> 8.9 us  [swap_slabs(): moved.append(lax.ppermute(piece, 'gx', pairs))]
  transfers between devices with their start and end apart: 18 -> 18, of which waited for: 12 -> 12; matrix products, arithmetic and copies ran while one was open for 2% -> 2% of each run, Pallas kernels for 7% -> 5%
where the time goes in v25:
time: 53 us; the launch traced here: 52.8 us
  starting transfers between devices  26 us (49%)
  waiting for transfers between devices  18.5 us (35%)
  Pallas kernels  5.19 us (10%)
  other arithmetic  1.65 us (3%)
  between operations  0.82 us (2%)
  local copies, waits for them, and re-layouts  0.55 us (1%)
    ppermute x6, waiting for transfers between devices, swap_in_plane(): moved.append(lax.ppermute(pieces[k], ('gx', 'gy'), pairs))  10.1 us
    ppermute x6, starting transfers between devices, swap_slabs(): moved.append(lax.ppermute(piece, 'gx', pairs))  8.9 us
    ppermute x3, starting transfers between devices, send_beside(): lax.ppermute(piece, 'gx', [(i, j) for i, j in pairs if 0 <= j < gx_size])  8.41 us
    ppermute x6, starting transfers between devices, swap_in_plane(): moved.append(lax.ppermute(pieces[k], ('gx', 'gy'), pairs))  8.05 us
    ppermute x6, waiting for transfers between devices, swap_slabs(): moved.append(lax.ppermute(piece, 'gx', pairs))  6.6 us
    pallas_call x12, Pallas kernels, local_kernel(): pl.pallas_call(placed, out_shape=[jax.ShapeDtypeStruct(shape, jnp.float32...  5.19 us
    ppermute x1, waiting for transfers between devices, column_body(): lax.ppermute(sent, 'gy', cores)  1.53 us
  transfers between devices with their start and end apart: 18, of which 12 were waited for; matrix products, arithmetic and copies ran while one was open for 2% of the time, Pallas kernels for 5%

profile of v25, /device:TPU:0, one launch (start us, length us, event | category | flops | bytes accessed | tf_op | source)
XLA Modules:
  0.0 52.8 jit_solution(14076709237418625840)
XLA Ops:
  1.2 1.0 %pad_maximum_fusion.refs_0_ = f32[9,4,16,128]{3,2,1,0:T(8,128)S(1)} fusion(f32[1,4,16,128]{3,2,1,0:T(8,128)} %bitcast.3, f32[8,4,16,128]{3,2,1,0:T(8,128)} %refs_1_.3), kind=kLoop, calls=%fused_computation | loop fusion | flops 73728 | bytes 589824 | tf_op jit(solution)/shard_map/concatenate | solution.py:602
  2.6 3.0 %collective-permute-start.2 = (f32[2,4,32,128]{3,2,1,0:T(8,128)S(1)}, f32[2,4,32,128]{3,2,1,0:T(8,128)S(1)}, u32[]{:S(2)}, u32[]{:S(2)}) collective-permute-start(f32[2,4,32,128]{3,2,1,0:T(8,128)S(1)} %get-tuple-element.31), channel_id=1, source_target_pairs={{0,2},{1,3},{2,0},{3,1},{4,6},{5,7},{6,4},{7,5},{8,10},{9,11},{10,... | collective-permute-start | bytes 393224 | tf_op jit(solution)/shard_map/ppermute | solution.py:577
  5.6 1.5 %collective-permute-start.3 = (f32[2,4,32,128]{3,2,1,0:T(8,128)S(1)}, f32[2,4,32,128]{3,2,1,0:T(8,128)S(1)}, u32[]{:S(2)}, u32[]{:S(2)}) collective-permute-start(f32[2,4,32,128]{3,2,1,0:T(8,128)S(1)} %get-tuple-element.32), channel_id=1, source_target_pairs={{0,4},{1,5},{2,6},{3,7},{4,0},{5,1},{6,2},{7,3},{8,12},{9,13},{10,... | collective-permute-start | bytes 393224 | tf_op jit(solution)/shard_map/ppermute | solution.py:577
  7.1 2.3 %collective-permute-done.2.refs_1_ = f32[2,4,32,128]{3,2,1,0:T(8,128)S(1)} collective-permute-done((f32[2,4,32,128]{3,2,1,0:T(8,128)S(1)}, f32[2,4,32,128]{3,2,1,0:T(8,128)S(1)}, u32[]{:S(2)}, u32[]{:S(2)}) %collective-permute-start.2) | collective-permute-done | bytes 131104 | tf_op jit(solution)/shard_map/ppermute | solution.py:577
  9.4 1.3 %collective-permute-start.5 = (f32[2,4,64,128]{3,2,1,0:T(8,128)S(1)}, f32[2,4,64,128]{3,2,1,0:T(8,128)S(1)}, u32[]{:S(2)}, u32[]{:S(2)}) collective-permute-start(f32[2,4,64,128]{3,2,1,0:T(8,128)S(1)} %half.1), channel_id=1, source_target_pairs={{4,12},{8,0},{12,20},{16,8},{20,28},{24,16},{5,13},{9,1},{13,21},{... | collective-permute-start | bytes 786440 | tf_op jit(solution)/shard_map/ppermute | solution.py:633
  10.7 1.2 %collective-permute-done.3.refs_2_ = f32[2,4,32,128]{3,2,1,0:T(8,128)S(1)} collective-permute-done((f32[2,4,32,128]{3,2,1,0:T(8,128)S(1)}, f32[2,4,32,128]{3,2,1,0:T(8,128)S(1)}, u32[]{:S(2)}, u32[]{:S(2)}) %collective-permute-start.3) | collective-permute-done | bytes 131104 | tf_op jit(solution)/shard_map/ppermute | solution.py:577
  11.9 1.5 %collective-permute-done.4.refs_3_ = f32[2,4,32,128]{3,2,1,0:T(8,128)S(1)} collective-permute-done((f32[2,4,32,128]{3,2,1,0:T(8,128)S(1)}, f32[2,4,32,128]{3,2,1,0:T(8,128)S(1)}, u32[]{:S(2)}, u32[]{:S(2)}) %collective-permute-start.4) | collective-permute-done | bytes 131104 | tf_op jit(solution)/shard_map/ppermute | solution.py:577
  13.5 3.6 %collective-permute-start.6 = (f32[2,2,64,128]{3,2,1,0:T(8,128)S(1)}, f32[2,2,64,128]{3,2,1,0:T(8,128)S(1)}, u32[]{:S(2)}, u32[]{:S(2)}) collective-permute-start(f32[2,2,64,128]{3,2,1,0:T(8,128)S(1)} %get-tuple-element.40), channel_id=1, source_target_pairs={{0,8},{8,16},{12,4},{16,24},{20,12},{28,20},{1,9},{9,17},{13,5},{1... | collective-permute-start | bytes 393224 | tf_op jit(solution)/shard_map/ppermute | solution.py:633
  17.2 3.5 %collective-permute-start.10 = (f32[2,2,64,128]{3,2,1,0:T(8,128)S(1)}, f32[2,2,64,128]{3,2,1,0:T(8,128)S(1)}, u32[]{:S(2)}, u32[]{:S(2)}) collective-permute-start(f32[2,2,64,128]{3,2,1,0:T(8,128)S(1)} %get-tuple-element.46), channel_id=1, source_target_pairs={{0,8},{8,16},{12,4},{16,24},{20,12},{28,20},{1,9},{9,17},{13,5},{1... | collective-permute-start | bytes 393224 | tf_op jit(solution)/shard_map/ppermute | solution.py:633
  22.7 1.6 %collective-permute-start.9 = (f32[4,32,128]{2,1,0:T(8,128)S(1)}, f32[4,32,128]{2,1,0:T(8,128)S(1)}, u32[]{:S(2)}, u32[]{:S(2)}) collective-permute-start(f32[4,32,128]{2,1,0:T(8,128)S(1)} %get-tuple-element.45.refs_3_), channel_id=1, source_target_pairs={{0,8},{4,12},{8,0},{12,4},{16,24},{20,28},{24,16},{28,20},{1,9},{5... | collective-permute-start | bytes 196616 | tf_op jit(solution)/shard_map/ppermute | solution.py:586
  24.3 2.1 %collective-permute-start.8 = (f32[4,32,128]{2,1,0:T(8,128)S(1)}, f32[4,32,128]{2,1,0:T(8,128)S(1)}, u32[]{:S(2)}, u32[]{:S(2)}) collective-permute-start(f32[4,32,128]{2,1,0:T(8,128)S(1)} %get-tuple-element.45.refs_3_), channel_id=1, source_target_pairs={{0,16},{4,20},{8,24},{12,28},{16,0},{20,4},{24,8},{28,12},{1,17},{... | collective-permute-start | bytes 196616 | tf_op jit(solution)/shard_map/ppermute | solution.py:586
  27.3 0.9 %collective-permute-done.9.refs_6_ = f32[4,32,128]{2,1,0:T(8,128)S(1)} collective-permute-done((f32[4,32,128]{2,1,0:T(8,128)S(1)}, f32[4,32,128]{2,1,0:T(8,128)S(1)}, u32[]{:S(2)}, u32[]{:S(2)}) %collective-permute-start.9) | collective-permute-done | bytes 65568 | tf_op jit(solution)/shard_map/ppermute | solution.py:586
  28.3 2.1 %collective-permute-done.8.refs_5_ = f32[4,32,128]{2,1,0:T(8,128)S(1)} collective-permute-done((f32[4,32,128]{2,1,0:T(8,128)S(1)}, f32[4,32,128]{2,1,0:T(8,128)S(1)}, u32[]{:S(2)}, u32[]{:S(2)}) %collective-permute-start.8) | collective-permute-done | bytes 65568 | tf_op jit(solution)/shard_map/ppermute | solution.py:586
  30.4 2.1 %collective-permute-done.7.refs_4_ = f32[4,32,128]{2,1,0:T(8,128)S(1)} collective-permute-done((f32[4,32,128]{2,1,0:T(8,128)S(1)}, f32[4,32,128]{2,1,0:T(8,128)S(1)}, u32[]{:S(2)}, u32[]{:S(2)}) %collective-permute-start.7) | collective-permute-done | bytes 65568 | tf_op jit(solution)/shard_map/ppermute | solution.py:586
  32.5 1.7 %coarse.1.refs_5_ = f32[256,128]{1,0:T(8,128)S(1)} custom-call(f32[16,128]{1,0:T(8,128)S(1)} %scalars.1.refs_0_, bf16[128,128]{1,0:T(8,128)(2,1)S(1)} %get-tuple-element.58.refs_8_.refs_1_, bf16[128,128]{1,0:T(8,128)(2,1)S(1)} %get-tuple-element.57.refs_2_, f32[4,32,128]{2,1,0:T(8,128)S(1)} %get-tuple-element.45.refs_3_, ...), custom_call_target="tpu_custom_call" | custom-call | tf_op jit(solution)/shard_map/coarse/pallas_call | solution.py:560
  35.2 1.5 %collective-permute-done.11.refs_1_ = f32[520,128]{1,0:T(8,128)S(1)} collective-permute-done((f32[520,128]{1,0:T(8,128)S(1)}, f32[520,128]{1,0:T(8,128)S(1)}, u32[]{:S(2)}, u32[]{:S(2)}) %collective-permute-start.11) | collective-permute-done | bytes 266272 | tf_op jit(solution)/shard_map/ppermute | solution.py:683
  36.8 1.8 %collective-permute-start.12 = (f32[208,128]{1,0:T(8,128)S(1)}, f32[208,128]{1,0:T(8,128)S(1)}, u32[]{:S(2)}, u32[]{:S(2)}) collective-permute-start(f32[208,128]{1,0:T(8,128)S(1)} %get-tuple-element.52), channel_id=1, source_target_pairs={{0,2},{1,3},{2,0},{3,1},{4,6},{5,7},{6,4},{7,5},{8,10},{9,11},{10,... | collective-permute-start | bytes 319496 | tf_op jit(solution)/shard_map/ppermute | solution.py:577
  38.6 1.7 %collective-permute-start.14 = (f32[208,128]{1,0:T(8,128)S(1)}, f32[208,128]{1,0:T(8,128)S(1)}, u32[]{:S(2)}, u32[]{:S(2)}) collective-permute-start(f32[208,128]{1,0:T(8,128)S(1)} %get-tuple-element.54), channel_id=1, source_target_pairs={{0,6},{1,7},{2,4},{3,5},{4,2},{5,3},{6,0},{7,1},{8,14},{9,15},{10,... | collective-permute-start | bytes 319496 | tf_op jit(solution)/shard_map/ppermute | solution.py:577
  40.4 1.6 %collective-permute-done.12.refs_4_.refs_1_ = f32[208,128]{1,0:T(8,128)S(1)} collective-permute-done((f32[208,128]{1,0:T(8,128)S(1)}, f32[208,128]{1,0:T(8,128)S(1)}, u32[]{:S(2)}, u32[]{:S(2)}) %collective-permute-start.12) | collective-permute-done | bytes 106528 | tf_op jit(solution)/shard_map/ppermute | solution.py:577
  41.9 2.6 %collective-permute-done.13.refs_5_.refs_2_ = f32[208,128]{1,0:T(8,128)S(1)} collective-permute-done((f32[208,128]{1,0:T(8,128)S(1)}, f32[208,128]{1,0:T(8,128)S(1)}, u32[]{:S(2)}, u32[]{:S(2)}) %collective-permute-start.13) | collective-permute-done | bytes 106528 | tf_op jit(solution)/shard_map/ppermute | solution.py:577
  44.5 0.9 %collective-permute-done.14.refs_6_.refs_3_ = f32[208,128]{1,0:T(8,128)S(1)} collective-permute-done((f32[208,128]{1,0:T(8,128)S(1)}, f32[208,128]{1,0:T(8,128)S(1)}, u32[]{:S(2)}, u32[]{:S(2)}) %collective-permute-start.14) | collective-permute-done | bytes 106528 | tf_op jit(solution)/shard_map/ppermute | solution.py:577
  45.5 1.4 %collective-permute-start.16 = (f32[1,128]{1,0:T(1,128)S(1)}, f32[1,128]{1,0:T(1,128)S(1)}, u32[]{:S(2)}, u32[]{:S(2)}) collective-permute-start(f32[1,128]{1,0:T(1,128)S(1)} %squares.1), channel_id=1, source_target_pairs={{0,16},{4,20},{8,24},{12,28},{16,0},{20,4},{24,8},{28,12},{1,17},{... | collective-permute-start | bytes 1544 | tf_op jit(solution)/shard_map/ppermute | solution.py:586
  46.9 3.0 %collective-permute-start.15 = (f32[1,128]{1,0:T(1,128)S(1)}, f32[1,128]{1,0:T(1,128)S(1)}, u32[]{:S(2)}, u32[]{:S(2)}) collective-permute-start(f32[1,128]{1,0:T(1,128)S(1)} %squares.1), channel_id=1, source_target_pairs={{0,24},{4,28},{8,16},{12,20},{16,8},{20,12},{24,0},{28,4},{1,25},{... | collective-permute-start | bytes 1544 | tf_op jit(solution)/shard_map/ppermute | solution.py:586
  50.8 1.5 %collective-permute-done.15 = f32[1,128]{1,0:T(1,128)S(1)} collective-permute-done((f32[1,128]{1,0:T(1,128)S(1)}, f32[1,128]{1,0:T(1,128)S(1)}, u32[]{:S(2)}, u32[]{:S(2)}) %collective-permute-start.15) | collective-permute-done | bytes 544 | tf_op jit(solution)/shard_map/ppermute | solution.py:586
  (40 shorter events, 6.5 us)
Async XLA Ops:
  0.6 1.9 %collective-permute-start = (f32[8,4,16,128]{3,2,1,0:T(8,128)}, f32[8,4,16,128]{3,2,1,0:T(8,128)S(1)}, u32[]{:S(2)}, u32[]{:S(2)}) collective-permute-start(f32[8,4,16,128]{3,2,1,0:T(8,128)} %refs_1_.3), channel_id=1, source_target_pairs={{0,1},{1,0},{2,3},{3,2},{4,5},{5,4},{6,7},{7,6},{8,9},{9,8},{10,11... | collective-permute-start | bytes 786440 | tf_op jit(solution)/shard_map/ppermute | solution.py:601
  1.1 1.4 %collective-permute-start.1 = (f32[4,16,128]{2,1,0:T(8,128)}, f32[4,16,128]{2,1,0:T(8,128)S(1)}, u32[]{:S(2)}, u32[]{:S(2)}) collective-permute-start(f32[4,16,128]{2,1,0:T(8,128)} %refs_2_.3), channel_id=1, source_target_pairs={{0,1},{1,0},{2,3},{3,2},{4,5},{5,4},{6,7},{7,6},{8,9},{9,8},{10,11... | collective-permute-start | bytes 98312 | tf_op jit(solution)/shard_map/ppermute | solution.py:601
  2.6 6.8 %collective-permute-start.2 = (f32[2,4,32,128]{3,2,1,0:T(8,128)S(1)}, f32[2,4,32,128]{3,2,1,0:T(8,128)S(1)}, u32[]{:S(2)}, u32[]{:S(2)}) collective-permute-start(f32[2,4,32,128]{3,2,1,0:T(8,128)S(1)} %get-tuple-element.31), channel_id=1, source_target_pairs={{0,2},{1,3},{2,0},{3,1},{4,6},{5,7},{6,4},{7,5},{8,10},{9,11},{10,... | collective-permute-start | bytes 393224 | tf_op jit(solution)/shard_map/ppermute | solution.py:577
  5.6 6.4 %collective-permute-start.3 = (f32[2,4,32,128]{3,2,1,0:T(8,128)S(1)}, f32[2,4,32,128]{3,2,1,0:T(8,128)S(1)}, u32[]{:S(2)}, u32[]{:S(2)}) collective-permute-start(f32[2,4,32,128]{3,2,1,0:T(8,128)S(1)} %get-tuple-element.32), channel_id=1, source_target_pairs={{0,4},{1,5},{2,6},{3,7},{4,0},{5,1},{6,2},{7,3},{8,12},{9,13},{10,... | collective-permute-start | bytes 393224 | tf_op jit(solution)/shard_map/ppermute | solution.py:577
  7.1 6.4 %collective-permute-start.4 = (f32[2,4,32,128]{3,2,1,0:T(8,128)S(1)}, f32[2,4,32,128]{3,2,1,0:T(8,128)S(1)}, u32[]{:S(2)}, u32[]{:S(2)}) collective-permute-start(f32[2,4,32,128]{3,2,1,0:T(8,128)S(1)} %get-tuple-element.33), channel_id=1, source_target_pairs={{0,6},{1,7},{2,4},{3,5},{4,2},{5,3},{6,0},{7,1},{8,14},{9,15},{10,... | collective-permute-start | bytes 393224 | tf_op jit(solution)/shard_map/ppermute | solution.py:577
  9.4 12.7 %collective-permute-start.5 = (f32[2,4,64,128]{3,2,1,0:T(8,128)S(1)}, f32[2,4,64,128]{3,2,1,0:T(8,128)S(1)}, u32[]{:S(2)}, u32[]{:S(2)}) collective-permute-start(f32[2,4,64,128]{3,2,1,0:T(8,128)S(1)} %half.1), channel_id=1, source_target_pairs={{4,12},{8,0},{12,20},{16,8},{20,28},{24,16},{5,13},{9,1},{13,21},{... | collective-permute-start | bytes 786440 | tf_op jit(solution)/shard_map/ppermute | solution.py:633
  13.5 8.6 %collective-permute-start.6 = (f32[2,2,64,128]{3,2,1,0:T(8,128)S(1)}, f32[2,2,64,128]{3,2,1,0:T(8,128)S(1)}, u32[]{:S(2)}, u32[]{:S(2)}) collective-permute-start(f32[2,2,64,128]{3,2,1,0:T(8,128)S(1)} %get-tuple-element.40), channel_id=1, source_target_pairs={{0,8},{8,16},{12,4},{16,24},{20,12},{28,20},{1,9},{9,17},{13,5},{1... | collective-permute-start | bytes 393224 | tf_op jit(solution)/shard_map/ppermute | solution.py:633
  17.2 10.0 %collective-permute-start.10 = (f32[2,2,64,128]{3,2,1,0:T(8,128)S(1)}, f32[2,2,64,128]{3,2,1,0:T(8,128)S(1)}, u32[]{:S(2)}, u32[]{:S(2)}) collective-permute-start(f32[2,2,64,128]{3,2,1,0:T(8,128)S(1)} %get-tuple-element.46), channel_id=1, source_target_pairs={{0,8},{8,16},{12,4},{16,24},{20,12},{28,20},{1,9},{9,17},{13,5},{1... | collective-permute-start | bytes 393224 | tf_op jit(solution)/shard_map/ppermute | solution.py:633
  20.6 0.7 %copy-start.2 = (f32[8]{0:T(128)S(1)}, f32[8]{0:T(128)}, u32[]{:S(2)}) copy-start(f32[8]{0:T(128)} %refs_0_.1) | copy-start | bytes 100
  20.7 0.7 %copy-start.3 = (s32[8]{0:T(128)S(1)}, s32[8]{0:T(128)}, u32[]{:S(2)}) copy-start(s32[8]{0:T(128)} %refs_1_.2) | copy-start | bytes 100
  20.7 0.7 %copy-start.4 = (f32[3]{0:T(128)S(1)}, f32[3]{0:T(128)}, u32[]{:S(2)}) copy-start(f32[3]{0:T(128)} %refs_2_.2) | copy-start | bytes 40
  22.7 5.6 %collective-permute-start.9 = (f32[4,32,128]{2,1,0:T(8,128)S(1)}, f32[4,32,128]{2,1,0:T(8,128)S(1)}, u32[]{:S(2)}, u32[]{:S(2)}) collective-permute-start(f32[4,32,128]{2,1,0:T(8,128)S(1)} %get-tuple-element.45.refs_3_), channel_id=1, source_target_pairs={{0,8},{4,12},{8,0},{12,4},{16,24},{20,28},{24,16},{28,20},{1,9},{5... | collective-permute-start | bytes 196616 | tf_op jit(solution)/shard_map/ppermute | solution.py:586
  24.3 6.1 %collective-permute-start.8 = (f32[4,32,128]{2,1,0:T(8,128)S(1)}, f32[4,32,128]{2,1,0:T(8,128)S(1)}, u32[]{:S(2)}, u32[]{:S(2)}) collective-permute-start(f32[4,32,128]{2,1,0:T(8,128)S(1)} %get-tuple-element.45.refs_3_), channel_id=1, source_target_pairs={{0,16},{4,20},{8,24},{12,28},{16,0},{20,4},{24,8},{28,12},{1,17},{... | collective-permute-start | bytes 196616 | tf_op jit(solution)/shard_map/ppermute | solution.py:586
  26.4 6.1 %collective-permute-start.7 = (f32[4,32,128]{2,1,0:T(8,128)S(1)}, f32[4,32,128]{2,1,0:T(8,128)S(1)}, u32[]{:S(2)}, u32[]{:S(2)}) collective-permute-start(f32[4,32,128]{2,1,0:T(8,128)S(1)} %get-tuple-element.45.refs_3_), channel_id=1, source_target_pairs={{0,24},{4,28},{8,16},{12,20},{16,8},{20,12},{24,0},{28,4},{1,25},{... | collective-permute-start | bytes 196616 | tf_op jit(solution)/shard_map/ppermute | solution.py:586
  35.1 1.6 %collective-permute-start.11 = (f32[520,128]{1,0:T(8,128)S(1)}, f32[520,128]{1,0:T(8,128)S(1)}, u32[]{:S(2)}, u32[]{:S(2)}) collective-permute-start(f32[520,128]{1,0:T(8,128)S(1)} %get-tuple-element.50), channel_id=1, source_target_pairs={{0,1},{1,0},{2,3},{3,2},{4,5},{5,4},{6,7},{7,6},{8,9},{9,8},{10,11... | collective-permute-start | bytes 798728 | tf_op jit(solution)/shard_map/ppermute | solution.py:683
  36.8 13.1 %copy-start = (f32[8,4,16,128]{3,2,1,0:T(8,128)S(1)}, f32[8,4,16,128]{3,2,1,0:T(8,128)}, u32[]{:S(2)}) copy-start(f32[8,4,16,128]{3,2,1,0:T(8,128)} %refs_1_.3) | copy-start | bytes 786436
  36.8 5.1 %collective-permute-start.12 = (f32[208,128]{1,0:T(8,128)S(1)}, f32[208,128]{1,0:T(8,128)S(1)}, u32[]{:S(2)}, u32[]{:S(2)}) collective-permute-start(f32[208,128]{1,0:T(8,128)S(1)} %get-tuple-element.52), channel_id=1, source_target_pairs={{0,2},{1,3},{2,0},{3,1},{4,6},{5,7},{6,4},{7,5},{8,10},{9,11},{10,... | collective-permute-start | bytes 319496 | tf_op jit(solution)/shard_map/ppermute | solution.py:577
  38.6 5.9 %collective-permute-start.13 = (f32[208,128]{1,0:T(8,128)S(1)}, f32[208,128]{1,0:T(8,128)S(1)}, u32[]{:S(2)}, u32[]{:S(2)}) collective-permute-start(f32[208,128]{1,0:T(8,128)S(1)} %get-tuple-element.53), channel_id=1, source_target_pairs={{0,4},{1,5},{2,6},{3,7},{4,0},{5,1},{6,2},{7,3},{8,12},{9,13},{10,... | collective-permute-start | bytes 319496 | tf_op jit(solution)/shard_map/ppermute | solution.py:577
  38.6 6.8 %collective-permute-start.14 = (f32[208,128]{1,0:T(8,128)S(1)}, f32[208,128]{1,0:T(8,128)S(1)}, u32[]{:S(2)}, u32[]{:S(2)}) collective-permute-start(f32[208,128]{1,0:T(8,128)S(1)} %get-tuple-element.54), channel_id=1, source_target_pairs={{0,6},{1,7},{2,4},{3,5},{4,2},{5,3},{6,0},{7,1},{8,14},{9,15},{10,... | collective-permute-start | bytes 319496 | tf_op jit(solution)/shard_map/ppermute | solution.py:577
  45.5 4.5 %copy-start.1 = (f32[4,16,128]{2,1,0:T(8,128)S(1)}, f32[4,16,128]{2,1,0:T(8,128)}, u32[]{:S(2)}) copy-start(f32[4,16,128]{2,1,0:T(8,128)} %refs_2_.3) | copy-start | bytes 98308
  45.5 5.3 %collective-permute-start.17 = (f32[1,128]{1,0:T(1,128)S(1)}, f32[1,128]{1,0:T(1,128)S(1)}, u32[]{:S(2)}, u32[]{:S(2)}) collective-permute-start(f32[1,128]{1,0:T(1,128)S(1)} %squares.1), channel_id=1, source_target_pairs={{0,8},{4,12},{8,0},{12,4},{16,24},{20,28},{24,16},{28,20},{1,9},{5... | collective-permute-start | bytes 1544 | tf_op jit(solution)/shard_map/ppermute | solution.py:586
  45.5 5.2 %collective-permute-start.16 = (f32[1,128]{1,0:T(1,128)S(1)}, f32[1,128]{1,0:T(1,128)S(1)}, u32[]{:S(2)}, u32[]{:S(2)}) collective-permute-start(f32[1,128]{1,0:T(1,128)S(1)} %squares.1), channel_id=1, source_target_pairs={{0,16},{4,20},{8,24},{12,28},{16,0},{20,4},{24,8},{28,12},{1,17},{... | collective-permute-start | bytes 1544 | tf_op jit(solution)/shard_map/ppermute | solution.py:586
  46.9 5.3 %collective-permute-start.15 = (f32[1,128]{1,0:T(1,128)S(1)}, f32[1,128]{1,0:T(1,128)S(1)}, u32[]{:S(2)}, u32[]{:S(2)}) collective-permute-start(f32[1,128]{1,0:T(1,128)S(1)} %squares.1), channel_id=1, source_target_pairs={{0,24},{4,28},{8,16},{12,20},{16,8},{20,12},{24,0},{28,4},{1,25},{... | collective-permute-start | bytes 1544 | tf_op jit(solution)/shard_map/ppermute | solution.py:586

commit v26 on v24

--- a/solution.py
+++ b/solution.py
@@ -509,7 +509,7 @@
     fine = Level(0, by, nz, 0, (0.0, speed), None, None, None)
     reaction = [reaction_ref[p] + fine.centre for p in range(1, bx - 1)]
     for m, part in enumerate(parts):
-        target = jnp.bitwise_xor(place[0] // 2, m)
+        target = jnp.bitwise_xor(place[0] // 2, step_of(m, len(parts)))
         for n in range(2):
             base, column = n * size, 2 * target + n
             shift = scalar_ref[pl.ds(8 + column, 1), :]
@@ -535,7 +535,7 @@
     lane = lax.broadcasted_iota(jnp.int32, (1, LANES), 1)
     row = jnp.zeros((1, LANES), jnp.float32)
     for m, part in enumerate(parts):
-        target = jnp.bitwise_xor(place[0] // 2, m)
+        target = jnp.bitwise_xor(place[0] // 2, step_of(m, len(parts)))
         for n in range(2):
             row = jnp.where(lane == 2 * target + n, part[pl.ds(n * size + squares, 1), :], row)
     out_ref[...] = row
@@ -680,6 +680,7 @@
         [(2 * part_rows(bx, by)[3], nz)] * chips,
     )
     parts = swap_in_plane(parts, 2)
+    parts = [parts[step_of(k, chips)] for k in range(chips)]
     (squares,) = local_kernel(
         functools.partial(squares_kernel, bx, by), "squares", (), parts, [(1, nz)]
     )

time: 51.6 us -> 51.4 us (level)
    ppermute x6, waiting for transfers between devices: 9.68 us -> 9.06 us  [swap_in_plane(): moved.append(lax.ppermute(pieces[k], ('gx', 'gy'), pairs))]
where the time goes in v26:
time: 51.4 us; the launch traced here: 51.2 us
  starting transfers between devices  26.7 us (52%)
  waiting for transfers between devices  16.9 us (33%)
  Pallas kernels  5.13 us (10%)
  other arithmetic  1.65 us (3%)
  between operations  0.84 us (2%)
    ppermute x6, starting transfers between devices, swap_slabs(): moved.append(lax.ppermute(piece, 'gx', pairs))  9.63 us
    ppermute x6, waiting for transfers between devices, swap_in_plane(): moved.append(lax.ppermute(pieces[k], ('gx', 'gy'), pairs))  9.06 us
    ppermute x3, starting transfers between devices, send_beside(): lax.ppermute(piece, 'gx', [(i, j) for i, j in pairs if 0 <= j < gx_size])  8.34 us
    ppermute x6, starting transfers between devices, swap_in_plane(): moved.append(lax.ppermute(pieces[k], ('gx', 'gy'), pairs))  8.05 us
    pallas_call x12, Pallas kernels, local_kernel(): pl.pallas_call(placed, out_shape=[jax.ShapeDtypeStruct(shape, jnp.float32...  5.13 us
    ppermute x6, waiting for transfers between devices, swap_slabs(): moved.append(lax.ppermute(piece, 'gx', pairs))  3.77 us
    ppermute x3, waiting for transfers between devices, send_beside(): lax.ppermute(piece, 'gx', [(i, j) for i, j in pairs if 0 <= j < gx_size])  2.16 us
    ppermute x1, waiting for transfers between devices, column_body(): lax.ppermute(sent, 'gy', cores)  1.53 us
  transfers between devices with their start and end apart: 18, of which 12 were waited for; matrix products, arithmetic and copies ran while one was open for 2% of the time, Pallas kernels for 7%

profile of v26, /device:TPU:0, one launch (start us, length us, event | category | flops | bytes accessed | tf_op | source)
XLA Modules:
  0.0 51.2 jit_solution(17522680265384506998)
XLA Ops:
  1.2 1.0 %pad_maximum_fusion.refs_0_ = f32[9,4,16,128]{3,2,1,0:T(8,128)S(1)} fusion(f32[1,4,16,128]{3,2,1,0:T(8,128)} %bitcast.3, f32[8,4,16,128]{3,2,1,0:T(8,128)} %refs_1_.3), kind=kLoop, calls=%fused_computation | loop fusion | flops 73728 | bytes 589824 | tf_op jit(solution)/shard_map/concatenate | solution.py:598
  2.6 3.0 %collective-permute-start.2 = (f32[2,4,32,128]{3,2,1,0:T(8,128)S(1)}, f32[2,4,32,128]{3,2,1,0:T(8,128)S(1)}, u32[]{:S(2)}, u32[]{:S(2)}) collective-permute-start(f32[2,4,32,128]{3,2,1,0:T(8,128)S(1)} %get-tuple-element.29), channel_id=1, source_target_pairs={{0,2},{1,3},{2,0},{3,1},{4,6},{5,7},{6,4},{7,5},{8,10},{9,11},{10,... | collective-permute-start | bytes 393224 | tf_op jit(solution)/shard_map/ppermute | solution.py:573
  5.6 1.5 %collective-permute-start.3 = (f32[2,4,32,128]{3,2,1,0:T(8,128)S(1)}, f32[2,4,32,128]{3,2,1,0:T(8,128)S(1)}, u32[]{:S(2)}, u32[]{:S(2)}) collective-permute-start(f32[2,4,32,128]{3,2,1,0:T(8,128)S(1)} %get-tuple-element.30), channel_id=1, source_target_pairs={{0,4},{1,5},{2,6},{3,7},{4,0},{5,1},{6,2},{7,3},{8,12},{9,13},{10,... | collective-permute-start | bytes 393224 | tf_op jit(solution)/shard_map/ppermute | solution.py:573
  7.1 2.3 %collective-permute-done.2.refs_1_ = f32[2,4,32,128]{3,2,1,0:T(8,128)S(1)} collective-permute-done((f32[2,4,32,128]{3,2,1,0:T(8,128)S(1)}, f32[2,4,32,128]{3,2,1,0:T(8,128)S(1)}, u32[]{:S(2)}, u32[]{:S(2)}) %collective-permute-start.2) | collective-permute-done | bytes 131104 | tf_op jit(solution)/shard_map/ppermute | solution.py:573
  9.4 1.4 %collective-permute-start.5 = (f32[2,4,64,128]{3,2,1,0:T(8,128)S(1)}, f32[2,4,64,128]{3,2,1,0:T(8,128)S(1)}, u32[]{:S(2)}, u32[]{:S(2)}) collective-permute-start(f32[2,4,64,128]{3,2,1,0:T(8,128)S(1)} %half.1), channel_id=1, source_target_pairs={{4,12},{8,0},{12,20},{16,8},{20,28},{24,16},{5,13},{9,1},{13,21},{... | collective-permute-start | bytes 786440 | tf_op jit(solution)/shard_map/ppermute | solution.py:629
  10.9 0.6 %scalars.1.refs_0_ = f32[16,128]{1,0:T(8,128)S(1)} custom-call(f32[8]{0:T(128)S(1)} %copy-done.2, s32[8]{0:T(128)S(1)} %copy-done.3, f32[3]{0:T(128)S(1)} %copy-done.4), custom_call_target="tpu_custom_call" | custom-call | tf_op jit(solution)/shard_map/scalars/pallas_call | solution.py:556
  11.9 1.5 %collective-permute-done.4.refs_3_ = f32[2,4,32,128]{3,2,1,0:T(8,128)S(1)} collective-permute-done((f32[2,4,32,128]{3,2,1,0:T(8,128)S(1)}, f32[2,4,32,128]{3,2,1,0:T(8,128)S(1)}, u32[]{:S(2)}, u32[]{:S(2)}) %collective-permute-start.4) | collective-permute-done | bytes 131104 | tf_op jit(solution)/shard_map/ppermute | solution.py:573
  13.5 3.6 %collective-permute-start.6 = (f32[2,2,64,128]{3,2,1,0:T(8,128)S(1)}, f32[2,2,64,128]{3,2,1,0:T(8,128)S(1)}, u32[]{:S(2)}, u32[]{:S(2)}) collective-permute-start(f32[2,2,64,128]{3,2,1,0:T(8,128)S(1)} %get-tuple-element.38), channel_id=1, source_target_pairs={{0,8},{8,16},{12,4},{16,24},{20,12},{28,20},{1,9},{9,17},{13,5},{1... | collective-permute-start | bytes 393224 | tf_op jit(solution)/shard_map/ppermute | solution.py:629
  17.5 2.2 %collective-permute-done.6.refs_7_ = f32[2,2,64,128]{3,2,1,0:T(8,128)S(1)} collective-permute-done((f32[2,2,64,128]{3,2,1,0:T(8,128)S(1)}, f32[2,2,64,128]{3,2,1,0:T(8,128)S(1)}, u32[]{:S(2)}, u32[]{:S(2)}) %collective-permute-start.6) | collective-permute-done | bytes 131104 | tf_op jit(solution)/shard_map/ppermute | solution.py:629
  20.2 4.5 %collective-permute-start.7 = (f32[4,32,128]{2,1,0:T(8,128)S(1)}, f32[4,32,128]{2,1,0:T(8,128)S(1)}, u32[]{:S(2)}, u32[]{:S(2)}) collective-permute-start(f32[4,32,128]{2,1,0:T(8,128)S(1)} %get-tuple-element.43.refs_3_), channel_id=1, source_target_pairs={{0,24},{4,28},{8,16},{12,20},{16,8},{20,12},{24,0},{28,4},{1,25},{... | collective-permute-start | bytes 196616 | tf_op jit(solution)/shard_map/ppermute | solution.py:582
  24.7 0.6 %collective-permute-start.9 = (f32[4,32,128]{2,1,0:T(8,128)S(1)}, f32[4,32,128]{2,1,0:T(8,128)S(1)}, u32[]{:S(2)}, u32[]{:S(2)}) collective-permute-start(f32[4,32,128]{2,1,0:T(8,128)S(1)} %get-tuple-element.43.refs_3_), channel_id=1, source_target_pairs={{0,8},{4,12},{8,0},{12,4},{16,24},{20,28},{24,16},{28,20},{1,9},{5... | collective-permute-start | bytes 196616 | tf_op jit(solution)/shard_map/ppermute | solution.py:582
  25.4 3.3 %collective-permute-start.10 = (f32[2,64,128]{2,1,0:T(8,128)S(1)}, f32[2,64,128]{2,1,0:T(8,128)S(1)}, u32[]{:S(2)}, u32[]{:S(2)}) collective-permute-start(f32[2,64,128]{2,1,0:T(8,128)S(1)} %get-tuple-element.44), channel_id=1, source_target_pairs={{0,8},{8,16},{12,4},{16,24},{20,12},{28,20},{1,9},{9,17},{13,5},{1... | collective-permute-start | bytes 196616 | tf_op jit(solution)/shard_map/ppermute | solution.py:629
  28.8 1.1 %collective-permute-done.8.refs_5_ = f32[4,32,128]{2,1,0:T(8,128)S(1)} collective-permute-done((f32[4,32,128]{2,1,0:T(8,128)S(1)}, f32[4,32,128]{2,1,0:T(8,128)S(1)}, u32[]{:S(2)}, u32[]{:S(2)}) %collective-permute-start.8) | collective-permute-done | bytes 65568 | tf_op jit(solution)/shard_map/ppermute | solution.py:582
  29.9 1.7 %coarse.1.refs_5_ = f32[256,128]{1,0:T(8,128)S(1)} custom-call(f32[16,128]{1,0:T(8,128)S(1)} %scalars.1.refs_0_, bf16[128,128]{1,0:T(8,128)(2,1)S(1)} %get-tuple-element.54.refs_8_.refs_1_, bf16[128,128]{1,0:T(8,128)(2,1)S(1)} %get-tuple-element.53.refs_2_, f32[4,32,128]{2,1,0:T(8,128)S(1)} %get-tuple-element.43.refs_3_, ...), custom_call_target="tpu_custom_call" | custom-call | tf_op jit(solution)/shard_map/coarse/pallas_call | solution.py:556
  31.6 0.9 %post.1 = (f32[520,128]{1,0:T(8,128)S(1)}, f32[520,128]{1,0:T(8,128)S(1)}) custom-call(f32[16,128]{1,0:T(8,128)S(1)} %scalars.1.refs_0_, f32[16,64,128]{2,1,0:T(8,128)S(1)} %get-tuple-element.39.refs_1_, f32[16,64,128]{2,1,0:T(8,128)S(1)} %get-tuple-element.40.refs_2_, f32[16,64,128]{2,1,0:T(8,128)S(1)} %get-tuple-element.41.refs_3_, ...), custom_call_target="tpu_custom_call" | custom-call | tf_op jit(solution)/shard_map/post/pallas_call | solution.py:556
  32.6 1.5 %collective-permute-done.11.refs_1_ = f32[520,128]{1,0:T(8,128)S(1)} collective-permute-done((f32[520,128]{1,0:T(8,128)S(1)}, f32[520,128]{1,0:T(8,128)S(1)}, u32[]{:S(2)}, u32[]{:S(2)}) %collective-permute-start.11) | collective-permute-done | bytes 266272 | tf_op jit(solution)/shard_map/ppermute | solution.py:679
  34.2 2.9 %collective-permute-start.12 = (f32[208,128]{1,0:T(8,128)S(1)}, f32[208,128]{1,0:T(8,128)S(1)}, u32[]{:S(2)}, u32[]{:S(2)}) collective-permute-start(f32[208,128]{1,0:T(8,128)S(1)} %get-tuple-element.48), channel_id=1, source_target_pairs={{0,6},{1,7},{2,4},{3,5},{4,2},{5,3},{6,0},{7,1},{8,14},{9,15},{10,... | collective-permute-start | bytes 319496 | tf_op jit(solution)/shard_map/ppermute | solution.py:573
  37.8 3.2 %collective-permute-done.12.refs_4_.refs_1_ = f32[208,128]{1,0:T(8,128)S(1)} collective-permute-done((f32[208,128]{1,0:T(8,128)S(1)}, f32[208,128]{1,0:T(8,128)S(1)}, u32[]{:S(2)}, u32[]{:S(2)}) %collective-permute-start.12) | collective-permute-done | bytes 106528 | tf_op jit(solution)/shard_map/ppermute | solution.py:573
  41.0 1.6 %collective-permute-done.13.refs_5_.refs_2_ = f32[208,128]{1,0:T(8,128)S(1)} collective-permute-done((f32[208,128]{1,0:T(8,128)S(1)}, f32[208,128]{1,0:T(8,128)S(1)}, u32[]{:S(2)}, u32[]{:S(2)}) %collective-permute-start.13) | collective-permute-done | bytes 106528 | tf_op jit(solution)/shard_map/ppermute | solution.py:573
  42.7 3.6 %collective-permute-start.15 = (f32[1,128]{1,0:T(1,128)S(1)}, f32[1,128]{1,0:T(1,128)S(1)}, u32[]{:S(2)}, u32[]{:S(2)}) collective-permute-start(f32[1,128]{1,0:T(1,128)S(1)} %squares.1), channel_id=1, source_target_pairs={{0,24},{4,28},{8,16},{12,20},{16,8},{20,12},{24,0},{28,4},{1,25},{... | collective-permute-start | bytes 1544 | tf_op jit(solution)/shard_map/ppermute | solution.py:582
  46.2 0.9 %collective-permute-start.17 = (f32[1,128]{1,0:T(1,128)S(1)}, f32[1,128]{1,0:T(1,128)S(1)}, u32[]{:S(2)}, u32[]{:S(2)}) collective-permute-start(f32[1,128]{1,0:T(1,128)S(1)} %squares.1), channel_id=1, source_target_pairs={{0,8},{4,12},{8,0},{12,4},{16,24},{20,28},{24,16},{28,20},{1,9},{5... | collective-permute-start | bytes 1544 | tf_op jit(solution)/shard_map/ppermute | solution.py:582
  47.1 0.9 %collect.1 = (f32[8,4,16,128]{3,2,1,0:T(8,128)}, f32[8,4,16,128]{3,2,1,0:T(8,128)}) custom-call(f32[16,128]{1,0:T(8,128)S(1)} %scalars.1.refs_0_, f32[8,4,16,128]{3,2,1,0:T(8,128)S(1)} %copy-done, f32[4,16,128]{2,1,0:T(8,128)S(1)} %copy-done.1, f32[208,128]{1,0:T(8,128)S(1)} %get-tuple-element.47.refs_3_.refs_0_, ...), custom_call_target="tpu_custom_call" | custom-call | tf_op jit(solution)/shard_map/collect/pallas_call | solution.py:556
  48.1 2.6 %collective-permute-done.16 = f32[1,128]{1,0:T(1,128)S(1)} collective-permute-done((f32[1,128]{1,0:T(1,128)S(1)}, f32[1,128]{1,0:T(1,128)S(1)}, u32[]{:S(2)}, u32[]{:S(2)}) %collective-permute-start.16) | collective-permute-done | bytes 544 | tf_op jit(solution)/shard_map/ppermute | solution.py:582
  50.7 0.5 %sqrt_bitcast_fusion = f32[8]{0:T(128)} fusion(f32[1,128]{1,0:T(1,128)S(1)} %add_add_fusion), kind=kLoop, calls=%fused_computation.12 | loop fusion | flops 16 | bytes 64 | tf_op jit(solution)/shard_map/sqrt | solution.py:699
  (40 shorter events, 3.6 us)
Async XLA Ops:
  0.6 1.9 %collective-permute-start = (f32[8,4,16,128]{3,2,1,0:T(8,128)}, f32[8,4,16,128]{3,2,1,0:T(8,128)S(1)}, u32[]{:S(2)}, u32[]{:S(2)}) collective-permute-start(f32[8,4,16,128]{3,2,1,0:T(8,128)} %refs_1_.3), channel_id=1, source_target_pairs={{0,1},{1,0},{2,3},{3,2},{4,5},{5,4},{6,7},{7,6},{8,9},{9,8},{10,11... | collective-permute-start | bytes 786440 | tf_op jit(solution)/shard_map/ppermute | solution.py:597
  1.1 1.4 %collective-permute-start.1 = (f32[4,16,128]{2,1,0:T(8,128)}, f32[4,16,128]{2,1,0:T(8,128)S(1)}, u32[]{:S(2)}, u32[]{:S(2)}) collective-permute-start(f32[4,16,128]{2,1,0:T(8,128)} %refs_2_.3), channel_id=1, source_target_pairs={{0,1},{1,0},{2,3},{3,2},{4,5},{5,4},{6,7},{7,6},{8,9},{9,8},{10,11... | collective-permute-start | bytes 98312 | tf_op jit(solution)/shard_map/ppermute | solution.py:597
  2.6 6.8 %collective-permute-start.2 = (f32[2,4,32,128]{3,2,1,0:T(8,128)S(1)}, f32[2,4,32,128]{3,2,1,0:T(8,128)S(1)}, u32[]{:S(2)}, u32[]{:S(2)}) collective-permute-start(f32[2,4,32,128]{3,2,1,0:T(8,128)S(1)} %get-tuple-element.29), channel_id=1, source_target_pairs={{0,2},{1,3},{2,0},{3,1},{4,6},{5,7},{6,4},{7,5},{8,10},{9,11},{10,... | collective-permute-start | bytes 393224 | tf_op jit(solution)/shard_map/ppermute | solution.py:573
  5.6 6.4 %collective-permute-start.3 = (f32[2,4,32,128]{3,2,1,0:T(8,128)S(1)}, f32[2,4,32,128]{3,2,1,0:T(8,128)S(1)}, u32[]{:S(2)}, u32[]{:S(2)}) collective-permute-start(f32[2,4,32,128]{3,2,1,0:T(8,128)S(1)} %get-tuple-element.30), channel_id=1, source_target_pairs={{0,4},{1,5},{2,6},{3,7},{4,0},{5,1},{6,2},{7,3},{8,12},{9,13},{10,... | collective-permute-start | bytes 393224 | tf_op jit(solution)/shard_map/ppermute | solution.py:573
  7.1 6.4 %collective-permute-start.4 = (f32[2,4,32,128]{3,2,1,0:T(8,128)S(1)}, f32[2,4,32,128]{3,2,1,0:T(8,128)S(1)}, u32[]{:S(2)}, u32[]{:S(2)}) collective-permute-start(f32[2,4,32,128]{3,2,1,0:T(8,128)S(1)} %get-tuple-element.31), channel_id=1, source_target_pairs={{0,6},{1,7},{2,4},{3,5},{4,2},{5,3},{6,0},{7,1},{8,14},{9,15},{10,... | collective-permute-start | bytes 393224 | tf_op jit(solution)/shard_map/ppermute | solution.py:573
  9.4 1.5 %copy-start.2 = (f32[8]{0:T(128)S(1)}, f32[8]{0:T(128)}, u32[]{:S(2)}) copy-start(f32[8]{0:T(128)} %refs_0_.1) | copy-start | bytes 100
  9.4 1.5 %copy-start.3 = (s32[8]{0:T(128)S(1)}, s32[8]{0:T(128)}, u32[]{:S(2)}) copy-start(s32[8]{0:T(128)} %refs_1_.2) | copy-start | bytes 100
  9.4 1.5 %copy-start.4 = (f32[3]{0:T(128)S(1)}, f32[3]{0:T(128)}, u32[]{:S(2)}) copy-start(f32[3]{0:T(128)} %refs_2_.2) | copy-start | bytes 40
  9.4 10.2 %collective-permute-start.5 = (f32[2,4,64,128]{3,2,1,0:T(8,128)S(1)}, f32[2,4,64,128]{3,2,1,0:T(8,128)S(1)}, u32[]{:S(2)}, u32[]{:S(2)}) collective-permute-start(f32[2,4,64,128]{3,2,1,0:T(8,128)S(1)} %half.1), channel_id=1, source_target_pairs={{4,12},{8,0},{12,20},{16,8},{20,28},{24,16},{5,13},{9,1},{13,21},{... | collective-permute-start | bytes 786440 | tf_op jit(solution)/shard_map/ppermute | solution.py:629
  13.5 6.1 %collective-permute-start.6 = (f32[2,2,64,128]{3,2,1,0:T(8,128)S(1)}, f32[2,2,64,128]{3,2,1,0:T(8,128)S(1)}, u32[]{:S(2)}, u32[]{:S(2)}) collective-permute-start(f32[2,2,64,128]{3,2,1,0:T(8,128)S(1)} %get-tuple-element.38), channel_id=1, source_target_pairs={{0,8},{8,16},{12,4},{16,24},{20,12},{28,20},{1,9},{9,17},{13,5},{1... | collective-permute-start | bytes 393224 | tf_op jit(solution)/shard_map/ppermute | solution.py:629
  20.2 8.6 %collective-permute-start.7 = (f32[4,32,128]{2,1,0:T(8,128)S(1)}, f32[4,32,128]{2,1,0:T(8,128)S(1)}, u32[]{:S(2)}, u32[]{:S(2)}) collective-permute-start(f32[4,32,128]{2,1,0:T(8,128)S(1)} %get-tuple-element.43.refs_3_), channel_id=1, source_target_pairs={{0,24},{4,28},{8,16},{12,20},{16,8},{20,12},{24,0},{28,4},{1,25},{... | collective-permute-start | bytes 196616 | tf_op jit(solution)/shard_map/ppermute | solution.py:582
  24.7 5.2 %collective-permute-start.8 = (f32[4,32,128]{2,1,0:T(8,128)S(1)}, f32[4,32,128]{2,1,0:T(8,128)S(1)}, u32[]{:S(2)}, u32[]{:S(2)}) collective-permute-start(f32[4,32,128]{2,1,0:T(8,128)S(1)} %get-tuple-element.43.refs_3_), channel_id=1, source_target_pairs={{0,16},{4,20},{8,24},{12,28},{16,0},{20,4},{24,8},{28,12},{1,17},{... | collective-permute-start | bytes 196616 | tf_op jit(solution)/shard_map/ppermute | solution.py:582
  24.7 5.2 %collective-permute-start.9 = (f32[4,32,128]{2,1,0:T(8,128)S(1)}, f32[4,32,128]{2,1,0:T(8,128)S(1)}, u32[]{:S(2)}, u32[]{:S(2)}) collective-permute-start(f32[4,32,128]{2,1,0:T(8,128)S(1)} %get-tuple-element.43.refs_3_), channel_id=1, source_target_pairs={{0,8},{4,12},{8,0},{12,4},{16,24},{20,28},{24,16},{28,20},{1,9},{5... | collective-permute-start | bytes 196616 | tf_op jit(solution)/shard_map/ppermute | solution.py:582
  25.4 6.3 %collective-permute-start.10 = (f32[2,64,128]{2,1,0:T(8,128)S(1)}, f32[2,64,128]{2,1,0:T(8,128)S(1)}, u32[]{:S(2)}, u32[]{:S(2)}) collective-permute-start(f32[2,64,128]{2,1,0:T(8,128)S(1)} %get-tuple-element.44), channel_id=1, source_target_pairs={{0,8},{8,16},{12,4},{16,24},{20,12},{28,20},{1,9},{9,17},{13,5},{1... | collective-permute-start | bytes 196616 | tf_op jit(solution)/shard_map/ppermute | solution.py:629
  32.5 1.6 %collective-permute-start.11 = (f32[520,128]{1,0:T(8,128)S(1)}, f32[520,128]{1,0:T(8,128)S(1)}, u32[]{:S(2)}, u32[]{:S(2)}) collective-permute-start(f32[520,128]{1,0:T(8,128)S(1)} %get-tuple-element.46), channel_id=1, source_target_pairs={{0,1},{1,0},{2,3},{3,2},{4,5},{5,4},{6,7},{7,6},{8,9},{9,8},{10,11... | collective-permute-start | bytes 798728 | tf_op jit(solution)/shard_map/ppermute | solution.py:679
  34.2 12.9 %copy-start = (f32[8,4,16,128]{3,2,1,0:T(8,128)S(1)}, f32[8,4,16,128]{3,2,1,0:T(8,128)}, u32[]{:S(2)}) copy-start(f32[8,4,16,128]{3,2,1,0:T(8,128)} %refs_1_.3) | copy-start | bytes 786436
  34.2 6.8 %collective-permute-start.12 = (f32[208,128]{1,0:T(8,128)S(1)}, f32[208,128]{1,0:T(8,128)S(1)}, u32[]{:S(2)}, u32[]{:S(2)}) collective-permute-start(f32[208,128]{1,0:T(8,128)S(1)} %get-tuple-element.48), channel_id=1, source_target_pairs={{0,6},{1,7},{2,4},{3,5},{4,2},{5,3},{6,0},{7,1},{8,14},{9,15},{10,... | collective-permute-start | bytes 319496 | tf_op jit(solution)/shard_map/ppermute | solution.py:573
  37.1 5.4 %collective-permute-start.13 = (f32[208,128]{1,0:T(8,128)S(1)}, f32[208,128]{1,0:T(8,128)S(1)}, u32[]{:S(2)}, u32[]{:S(2)}) collective-permute-start(f32[208,128]{1,0:T(8,128)S(1)} %get-tuple-element.49), channel_id=1, source_target_pairs={{0,4},{1,5},{2,6},{3,7},{4,0},{5,1},{6,2},{7,3},{8,12},{9,13},{10,... | collective-permute-start | bytes 319496 | tf_op jit(solution)/shard_map/ppermute | solution.py:573
  37.3 5.4 %collective-permute-start.14 = (f32[208,128]{1,0:T(8,128)S(1)}, f32[208,128]{1,0:T(8,128)S(1)}, u32[]{:S(2)}, u32[]{:S(2)}) collective-permute-start(f32[208,128]{1,0:T(8,128)S(1)} %get-tuple-element.50), channel_id=1, source_target_pairs={{0,2},{1,3},{2,0},{3,1},{4,6},{5,7},{6,4},{7,5},{8,10},{9,11},{10,... | collective-permute-start | bytes 319496 | tf_op jit(solution)/shard_map/ppermute | solution.py:573
  42.7 4.5 %copy-start.1 = (f32[4,16,128]{2,1,0:T(8,128)S(1)}, f32[4,16,128]{2,1,0:T(8,128)}, u32[]{:S(2)}) copy-start(f32[4,16,128]{2,1,0:T(8,128)} %refs_2_.3) | copy-start | bytes 98308
  42.7 5.4 %collective-permute-start.15 = (f32[1,128]{1,0:T(1,128)S(1)}, f32[1,128]{1,0:T(1,128)S(1)}, u32[]{:S(2)}, u32[]{:S(2)}) collective-permute-start(f32[1,128]{1,0:T(1,128)S(1)} %squares.1), channel_id=1, source_target_pairs={{0,24},{4,28},{8,16},{12,20},{16,8},{20,12},{24,0},{28,4},{1,25},{... | collective-permute-start | bytes 1544 | tf_op jit(solution)/shard_map/ppermute | solution.py:582
  46.2 4.4 %collective-permute-start.16 = (f32[1,128]{1,0:T(1,128)S(1)}, f32[1,128]{1,0:T(1,128)S(1)}, u32[]{:S(2)}, u32[]{:S(2)}) collective-permute-start(f32[1,128]{1,0:T(1,128)S(1)} %squares.1), channel_id=1, source_target_pairs={{0,16},{4,20},{8,24},{12,28},{16,0},{20,4},{24,8},{28,12},{1,17},{... | collective-permute-start | bytes 1544 | tf_op jit(solution)/shard_map/ppermute | solution.py:582
  46.2 4.4 %collective-permute-start.17 = (f32[1,128]{1,0:T(1,128)S(1)}, f32[1,128]{1,0:T(1,128)S(1)}, u32[]{:S(2)}, u32[]{:S(2)}) collective-permute-start(f32[1,128]{1,0:T(1,128)S(1)} %squares.1), channel_id=1, source_target_pairs={{0,8},{4,12},{8,0},{12,4},{16,24},{20,28},{24,16},{28,20},{1,9},{5... | collective-permute-start | bytes 1544 | tf_op jit(solution)/shard_map/ppermute | solution.py:582

commit v27 on v26

--- a/solution.py
+++ b/solution.py
@@ -280,7 +280,7 @@
     blocks, (slab_ref, near_ref) = refs[:-2], refs[-2:]
     chip = place[0] // 2
     for m, block in enumerate(blocks):
-        owner = jnp.bitwise_xor(chip, m)
+        owner = jnp.bitwise_xor(chip, m ^ (m >> 1))
         _, bx, size, _ = block.shape
         planes = pl.ds((owner // chips_y) * bx, bx)
         rows = pl.ds(pl.multiple_of(lax.rem(owner, chips_y) * size, 8), size)
@@ -620,7 +620,7 @@
         functools.partial(arrange_kernel, chips_y),
         "arrange",
         (),
-        blocks,
+        [blocks[m ^ (m >> 1)] for m in range(chips)],
         [(2, SLAB, ny, nz), edge],
     )
 

time: 51.4 us -> 53.5 us (1.041)
  starting transfers between devices: 26.7 us -> 29.2 us
  waiting for transfers between devices: 16.9 us -> 16.3 us
    ppermute x6, starting transfers between devices: 8.05 us -> 9.24 us  [swap_in_plane(): moved.append(lax.ppermute(pieces[k], ('gx', 'gy'), pairs))]
    ppermute x3, starting transfers between devices: 8.34 us -> 9.26 us  [send_beside(): lax.ppermute(piece, 'gx', [(i, j) for i, j in pairs if 0 <= j < gx_size])]
    ppermute x6, waiting for transfers between devices: 3.77 us -> 3.02 us  [swap_slabs(): moved.append(lax.ppermute(piece, 'gx', pairs))]
  transfers between devices with their start and end apart: 18 -> 18, of which waited for: 12 -> 10; matrix products, arithmetic and copies ran while one was open for 2% -> 2% of each run, Pallas kernels for 7% -> 7%
where the time goes in v27:
time: 53.5 us; the launch traced here: 53.3 us
  starting transfers between devices  29.2 us (55%)
  waiting for transfers between devices  16.3 us (30%)
  Pallas kernels  5.14 us (10%)
  other arithmetic  1.65 us (3%)
  between operations  0.85 us (2%)
    ppermute x6, starting transfers between devices, swap_slabs(): moved.append(lax.ppermute(piece, 'gx', pairs))  10.1 us
    ppermute x6, waiting for transfers between devices, swap_in_plane(): moved.append(lax.ppermute(pieces[k], ('gx', 'gy'), pairs))  9.29 us
    ppermute x3, starting transfers between devices, send_beside(): lax.ppermute(piece, 'gx', [(i, j) for i, j in pairs if 0 <= j < gx_size])  9.26 us
    ppermute x6, starting transfers between devices, swap_in_plane(): moved.append(lax.ppermute(pieces[k], ('gx', 'gy'), pairs))  9.24 us
    pallas_call x12, Pallas kernels, local_kernel(): pl.pallas_call(placed, out_shape=[jax.ShapeDtypeStruct(shape, jnp.float32...  5.14 us
    ppermute x6, waiting for transfers between devices, swap_slabs(): moved.append(lax.ppermute(piece, 'gx', pairs))  3.02 us
    ppermute x3, waiting for transfers between devices, send_beside(): lax.ppermute(piece, 'gx', [(i, j) for i, j in pairs if 0 <= j < gx_size])  2.16 us
    ppermute x1, waiting for transfers between devices, column_body(): lax.ppermute(sent, 'gy', cores)  1.53 us
  transfers between devices with their start and end apart: 18, of which 10 were waited for; matrix products, arithmetic and copies ran while one was open for 2% of the time, Pallas kernels for 7%

profile of v27, /device:TPU:0, one launch (start us, length us, event | category | flops | bytes accessed | tf_op | source)
XLA Modules:
  0.0 53.3 jit_solution(9634487515360544898)
XLA Ops:
  1.2 1.0 %pad_maximum_fusion.refs_0_ = f32[9,4,16,128]{3,2,1,0:T(8,128)S(1)} fusion(f32[1,4,16,128]{3,2,1,0:T(8,128)} %bitcast.3, f32[8,4,16,128]{3,2,1,0:T(8,128)} %refs_1_.3), kind=kLoop, calls=%fused_computation | loop fusion | flops 73728 | bytes 589824 | tf_op jit(solution)/shard_map/concatenate | solution.py:598
  2.6 3.0 %collective-permute-start.2 = (f32[2,4,32,128]{3,2,1,0:T(8,128)S(1)}, f32[2,4,32,128]{3,2,1,0:T(8,128)S(1)}, u32[]{:S(2)}, u32[]{:S(2)}) collective-permute-start(f32[2,4,32,128]{3,2,1,0:T(8,128)S(1)} %get-tuple-element.29), channel_id=1, source_target_pairs={{0,2},{1,3},{2,0},{3,1},{4,6},{5,7},{6,4},{7,5},{8,10},{9,11},{10,... | collective-permute-start | bytes 393224 | tf_op jit(solution)/shard_map/ppermute | solution.py:573
  5.6 1.4 %collective-permute-start.3 = (f32[2,4,32,128]{3,2,1,0:T(8,128)S(1)}, f32[2,4,32,128]{3,2,1,0:T(8,128)S(1)}, u32[]{:S(2)}, u32[]{:S(2)}) collective-permute-start(f32[2,4,32,128]{3,2,1,0:T(8,128)S(1)} %get-tuple-element.30), channel_id=1, source_target_pairs={{0,6},{1,7},{2,4},{3,5},{4,2},{5,3},{6,0},{7,1},{8,14},{9,15},{10,... | collective-permute-start | bytes 393224 | tf_op jit(solution)/shard_map/ppermute | solution.py:573
  7.1 4.4 %collective-permute-done.2.refs_1_ = f32[2,4,32,128]{3,2,1,0:T(8,128)S(1)} collective-permute-done((f32[2,4,32,128]{3,2,1,0:T(8,128)S(1)}, f32[2,4,32,128]{3,2,1,0:T(8,128)S(1)}, u32[]{:S(2)}, u32[]{:S(2)}) %collective-permute-start.2) | collective-permute-done | bytes 131104 | tf_op jit(solution)/shard_map/ppermute | solution.py:573
  11.6 1.4 %collective-permute-start.5 = (f32[2,4,64,128]{3,2,1,0:T(8,128)S(1)}, f32[2,4,64,128]{3,2,1,0:T(8,128)S(1)}, u32[]{:S(2)}, u32[]{:S(2)}) collective-permute-start(f32[2,4,64,128]{3,2,1,0:T(8,128)S(1)} %half.1), channel_id=1, source_target_pairs={{4,12},{8,0},{12,20},{16,8},{20,28},{24,16},{5,13},{9,1},{13,21},{... | collective-permute-start | bytes 786440 | tf_op jit(solution)/shard_map/ppermute | solution.py:629
  13.0 0.6 %scalars.1.refs_0_ = f32[16,128]{1,0:T(8,128)S(1)} custom-call(f32[8]{0:T(128)S(1)} %copy-done.2, s32[8]{0:T(128)S(1)} %copy-done.3, f32[3]{0:T(128)S(1)} %copy-done.4), custom_call_target="tpu_custom_call" | custom-call | tf_op jit(solution)/shard_map/scalars/pallas_call | solution.py:556
  13.7 4.6 %collective-permute-start.6 = (f32[2,2,64,128]{3,2,1,0:T(8,128)S(1)}, f32[2,2,64,128]{3,2,1,0:T(8,128)S(1)}, u32[]{:S(2)}, u32[]{:S(2)}) collective-permute-start(f32[2,2,64,128]{3,2,1,0:T(8,128)S(1)} %get-tuple-element.38), channel_id=1, source_target_pairs={{0,8},{8,16},{12,4},{16,24},{20,12},{28,20},{1,9},{9,17},{13,5},{1... | collective-permute-start | bytes 393224 | tf_op jit(solution)/shard_map/ppermute | solution.py:629
  18.6 2.2 %collective-permute-done.6.refs_7_ = f32[2,2,64,128]{3,2,1,0:T(8,128)S(1)} collective-permute-done((f32[2,2,64,128]{3,2,1,0:T(8,128)S(1)}, f32[2,2,64,128]{3,2,1,0:T(8,128)S(1)}, u32[]{:S(2)}, u32[]{:S(2)}) %collective-permute-start.6) | collective-permute-done | bytes 131104 | tf_op jit(solution)/shard_map/ppermute | solution.py:629
  21.3 5.0 %collective-permute-start.7 = (f32[4,32,128]{2,1,0:T(8,128)S(1)}, f32[4,32,128]{2,1,0:T(8,128)S(1)}, u32[]{:S(2)}, u32[]{:S(2)}) collective-permute-start(f32[4,32,128]{2,1,0:T(8,128)S(1)} %get-tuple-element.43.refs_3_), channel_id=1, source_target_pairs={{0,24},{4,28},{8,16},{12,20},{16,8},{20,12},{24,0},{28,4},{1,25},{... | collective-permute-start | bytes 196616 | tf_op jit(solution)/shard_map/ppermute | solution.py:582
  26.3 0.6 %collective-permute-start.9 = (f32[4,32,128]{2,1,0:T(8,128)S(1)}, f32[4,32,128]{2,1,0:T(8,128)S(1)}, u32[]{:S(2)}, u32[]{:S(2)}) collective-permute-start(f32[4,32,128]{2,1,0:T(8,128)S(1)} %get-tuple-element.43.refs_3_), channel_id=1, source_target_pairs={{0,8},{4,12},{8,0},{12,4},{16,24},{20,28},{24,16},{28,20},{1,9},{5... | collective-permute-start | bytes 196616 | tf_op jit(solution)/shard_map/ppermute | solution.py:582
  26.9 3.3 %collective-permute-start.10 = (f32[2,64,128]{2,1,0:T(8,128)S(1)}, f32[2,64,128]{2,1,0:T(8,128)S(1)}, u32[]{:S(2)}, u32[]{:S(2)}) collective-permute-start(f32[2,64,128]{2,1,0:T(8,128)S(1)} %get-tuple-element.44), channel_id=1, source_target_pairs={{0,8},{8,16},{12,4},{16,24},{20,12},{28,20},{1,9},{9,17},{13,5},{1... | collective-permute-start | bytes 196616 | tf_op jit(solution)/shard_map/ppermute | solution.py:629
  30.4 1.1 %collective-permute-done.8.refs_5_ = f32[4,32,128]{2,1,0:T(8,128)S(1)} collective-permute-done((f32[4,32,128]{2,1,0:T(8,128)S(1)}, f32[4,32,128]{2,1,0:T(8,128)S(1)}, u32[]{:S(2)}, u32[]{:S(2)}) %collective-permute-start.8) | collective-permute-done | bytes 65568 | tf_op jit(solution)/shard_map/ppermute | solution.py:582
  31.5 1.7 %coarse.1.refs_5_ = f32[256,128]{1,0:T(8,128)S(1)} custom-call(f32[16,128]{1,0:T(8,128)S(1)} %scalars.1.refs_0_, bf16[128,128]{1,0:T(8,128)(2,1)S(1)} %get-tuple-element.54.refs_8_.refs_1_, bf16[128,128]{1,0:T(8,128)(2,1)S(1)} %get-tuple-element.53.refs_2_, f32[4,32,128]{2,1,0:T(8,128)S(1)} %get-tuple-element.43.refs_3_, ...), custom_call_target="tpu_custom_call" | custom-call | tf_op jit(solution)/shard_map/coarse/pallas_call | solution.py:556
  33.2 0.9 %post.1 = (f32[520,128]{1,0:T(8,128)S(1)}, f32[520,128]{1,0:T(8,128)S(1)}) custom-call(f32[16,128]{1,0:T(8,128)S(1)} %scalars.1.refs_0_, f32[16,64,128]{2,1,0:T(8,128)S(1)} %get-tuple-element.39.refs_1_, f32[16,64,128]{2,1,0:T(8,128)S(1)} %get-tuple-element.40.refs_2_, f32[16,64,128]{2,1,0:T(8,128)S(1)} %get-tuple-element.41.refs_3_, ...), custom_call_target="tpu_custom_call" | custom-call | tf_op jit(solution)/shard_map/post/pallas_call | solution.py:556
  34.2 1.5 %collective-permute-done.11.refs_1_ = f32[520,128]{1,0:T(8,128)S(1)} collective-permute-done((f32[520,128]{1,0:T(8,128)S(1)}, f32[520,128]{1,0:T(8,128)S(1)}, u32[]{:S(2)}, u32[]{:S(2)}) %collective-permute-start.11) | collective-permute-done | bytes 266272 | tf_op jit(solution)/shard_map/ppermute | solution.py:679
  35.8 4.1 %collective-permute-start.12 = (f32[208,128]{1,0:T(8,128)S(1)}, f32[208,128]{1,0:T(8,128)S(1)}, u32[]{:S(2)}, u32[]{:S(2)}) collective-permute-start(f32[208,128]{1,0:T(8,128)S(1)} %get-tuple-element.48), channel_id=1, source_target_pairs={{0,6},{1,7},{2,4},{3,5},{4,2},{5,3},{6,0},{7,1},{8,14},{9,15},{10,... | collective-permute-start | bytes 319496 | tf_op jit(solution)/shard_map/ppermute | solution.py:573
  39.9 0.6 %collective-permute-start.14 = (f32[208,128]{1,0:T(8,128)S(1)}, f32[208,128]{1,0:T(8,128)S(1)}, u32[]{:S(2)}, u32[]{:S(2)}) collective-permute-start(f32[208,128]{1,0:T(8,128)S(1)} %get-tuple-element.50), channel_id=1, source_target_pairs={{0,2},{1,3},{2,0},{3,1},{4,6},{5,7},{6,4},{7,5},{8,10},{9,11},{10,... | collective-permute-start | bytes 319496 | tf_op jit(solution)/shard_map/ppermute | solution.py:573
  40.6 3.1 %collective-permute-done.12.refs_4_.refs_1_ = f32[208,128]{1,0:T(8,128)S(1)} collective-permute-done((f32[208,128]{1,0:T(8,128)S(1)}, f32[208,128]{1,0:T(8,128)S(1)}, u32[]{:S(2)}, u32[]{:S(2)}) %collective-permute-start.12) | collective-permute-done | bytes 106528 | tf_op jit(solution)/shard_map/ppermute | solution.py:573
  43.7 1.1 %collective-permute-done.13.refs_5_.refs_2_ = f32[208,128]{1,0:T(8,128)S(1)} collective-permute-done((f32[208,128]{1,0:T(8,128)S(1)}, f32[208,128]{1,0:T(8,128)S(1)}, u32[]{:S(2)}, u32[]{:S(2)}) %collective-permute-start.13) | collective-permute-done | bytes 106528 | tf_op jit(solution)/shard_map/ppermute | solution.py:573
  44.7 0.7 %collective-permute-done.14.refs_6_.refs_3_ = f32[208,128]{1,0:T(8,128)S(1)} collective-permute-done((f32[208,128]{1,0:T(8,128)S(1)}, f32[208,128]{1,0:T(8,128)S(1)}, u32[]{:S(2)}, u32[]{:S(2)}) %collective-permute-start.14) | collective-permute-done | bytes 106528 | tf_op jit(solution)/shard_map/ppermute | solution.py:573
  45.5 2.8 %collective-permute-start.15 = (f32[1,128]{1,0:T(1,128)S(1)}, f32[1,128]{1,0:T(1,128)S(1)}, u32[]{:S(2)}, u32[]{:S(2)}) collective-permute-start(f32[1,128]{1,0:T(1,128)S(1)} %squares.1), channel_id=1, source_target_pairs={{0,24},{4,28},{8,16},{12,20},{16,8},{20,12},{24,0},{28,4},{1,25},{... | collective-permute-start | bytes 1544 | tf_op jit(solution)/shard_map/ppermute | solution.py:582
  48.3 1.6 %collective-permute-start.17 = (f32[1,128]{1,0:T(1,128)S(1)}, f32[1,128]{1,0:T(1,128)S(1)}, u32[]{:S(2)}, u32[]{:S(2)}) collective-permute-start(f32[1,128]{1,0:T(1,128)S(1)} %squares.1), channel_id=1, source_target_pairs={{0,8},{4,12},{8,0},{12,4},{16,24},{20,28},{24,16},{28,20},{1,9},{5... | collective-permute-start | bytes 1544 | tf_op jit(solution)/shard_map/ppermute | solution.py:582
  49.9 0.9 %collect.1 = (f32[8,4,16,128]{3,2,1,0:T(8,128)}, f32[8,4,16,128]{3,2,1,0:T(8,128)}) custom-call(f32[16,128]{1,0:T(8,128)S(1)} %scalars.1.refs_0_, f32[8,4,16,128]{3,2,1,0:T(8,128)S(1)} %copy-done, f32[4,16,128]{2,1,0:T(8,128)S(1)} %copy-done.1, f32[208,128]{1,0:T(8,128)S(1)} %get-tuple-element.47.refs_3_.refs_0_, ...), custom_call_target="tpu_custom_call" | custom-call | tf_op jit(solution)/shard_map/collect/pallas_call | solution.py:556
  50.9 1.8 %collective-permute-done.16 = f32[1,128]{1,0:T(1,128)S(1)} collective-permute-done((f32[1,128]{1,0:T(1,128)S(1)}, f32[1,128]{1,0:T(1,128)S(1)}, u32[]{:S(2)}, u32[]{:S(2)}) %collective-permute-start.16) | collective-permute-done | bytes 544 | tf_op jit(solution)/shard_map/ppermute | solution.py:582
  (40 shorter events, 3.0 us)
Async XLA Ops:
  0.6 1.9 %collective-permute-start = (f32[8,4,16,128]{3,2,1,0:T(8,128)}, f32[8,4,16,128]{3,2,1,0:T(8,128)S(1)}, u32[]{:S(2)}, u32[]{:S(2)}) collective-permute-start(f32[8,4,16,128]{3,2,1,0:T(8,128)} %refs_1_.3), channel_id=1, source_target_pairs={{0,1},{1,0},{2,3},{3,2},{4,5},{5,4},{6,7},{7,6},{8,9},{9,8},{10,11... | collective-permute-start | bytes 786440 | tf_op jit(solution)/shard_map/ppermute | solution.py:597
  1.1 1.4 %collective-permute-start.1 = (f32[4,16,128]{2,1,0:T(8,128)}, f32[4,16,128]{2,1,0:T(8,128)S(1)}, u32[]{:S(2)}, u32[]{:S(2)}) collective-permute-start(f32[4,16,128]{2,1,0:T(8,128)} %refs_2_.3), channel_id=1, source_target_pairs={{0,1},{1,0},{2,3},{3,2},{4,5},{5,4},{6,7},{7,6},{8,9},{9,8},{10,11... | collective-permute-start | bytes 98312 | tf_op jit(solution)/shard_map/ppermute | solution.py:597
  2.6 8.9 %collective-permute-start.2 = (f32[2,4,32,128]{3,2,1,0:T(8,128)S(1)}, f32[2,4,32,128]{3,2,1,0:T(8,128)S(1)}, u32[]{:S(2)}, u32[]{:S(2)}) collective-permute-start(f32[2,4,32,128]{3,2,1,0:T(8,128)S(1)} %get-tuple-element.29), channel_id=1, source_target_pairs={{0,2},{1,3},{2,0},{3,1},{4,6},{5,7},{6,4},{7,5},{8,10},{9,11},{10,... | collective-permute-start | bytes 393224 | tf_op jit(solution)/shard_map/ppermute | solution.py:573
  5.6 8.1 %collective-permute-start.3 = (f32[2,4,32,128]{3,2,1,0:T(8,128)S(1)}, f32[2,4,32,128]{3,2,1,0:T(8,128)S(1)}, u32[]{:S(2)}, u32[]{:S(2)}) collective-permute-start(f32[2,4,32,128]{3,2,1,0:T(8,128)S(1)} %get-tuple-element.30), channel_id=1, source_target_pairs={{0,6},{1,7},{2,4},{3,5},{4,2},{5,3},{6,0},{7,1},{8,14},{9,15},{10,... | collective-permute-start | bytes 393224 | tf_op jit(solution)/shard_map/ppermute | solution.py:573
  7.0 6.6 %collective-permute-start.4 = (f32[2,4,32,128]{3,2,1,0:T(8,128)S(1)}, f32[2,4,32,128]{3,2,1,0:T(8,128)S(1)}, u32[]{:S(2)}, u32[]{:S(2)}) collective-permute-start(f32[2,4,32,128]{3,2,1,0:T(8,128)S(1)} %get-tuple-element.31), channel_id=1, source_target_pairs={{0,4},{1,5},{2,6},{3,7},{4,0},{5,1},{6,2},{7,3},{8,12},{9,13},{10,... | collective-permute-start | bytes 393224 | tf_op jit(solution)/shard_map/ppermute | solution.py:573
  11.5 1.5 %copy-start.2 = (f32[8]{0:T(128)S(1)}, f32[8]{0:T(128)}, u32[]{:S(2)}) copy-start(f32[8]{0:T(128)} %refs_0_.1) | copy-start | bytes 100
  11.5 1.5 %copy-start.3 = (s32[8]{0:T(128)S(1)}, s32[8]{0:T(128)}, u32[]{:S(2)}) copy-start(s32[8]{0:T(128)} %refs_1_.2) | copy-start | bytes 100
  11.6 1.5 %copy-start.4 = (f32[3]{0:T(128)S(1)}, f32[3]{0:T(128)}, u32[]{:S(2)}) copy-start(f32[3]{0:T(128)} %refs_2_.2) | copy-start | bytes 40
  11.6 9.2 %collective-permute-start.5 = (f32[2,4,64,128]{3,2,1,0:T(8,128)S(1)}, f32[2,4,64,128]{3,2,1,0:T(8,128)S(1)}, u32[]{:S(2)}, u32[]{:S(2)}) collective-permute-start(f32[2,4,64,128]{3,2,1,0:T(8,128)S(1)} %half.1), channel_id=1, source_target_pairs={{4,12},{8,0},{12,20},{16,8},{20,28},{24,16},{5,13},{9,1},{13,21},{... | collective-permute-start | bytes 786440 | tf_op jit(solution)/shard_map/ppermute | solution.py:629
  13.7 7.1 %collective-permute-start.6 = (f32[2,2,64,128]{3,2,1,0:T(8,128)S(1)}, f32[2,2,64,128]{3,2,1,0:T(8,128)S(1)}, u32[]{:S(2)}, u32[]{:S(2)}) collective-permute-start(f32[2,2,64,128]{3,2,1,0:T(8,128)S(1)} %get-tuple-element.38), channel_id=1, source_target_pairs={{0,8},{8,16},{12,4},{16,24},{20,12},{28,20},{1,9},{9,17},{13,5},{1... | collective-permute-start | bytes 393224 | tf_op jit(solution)/shard_map/ppermute | solution.py:629
  21.3 9.1 %collective-permute-start.7 = (f32[4,32,128]{2,1,0:T(8,128)S(1)}, f32[4,32,128]{2,1,0:T(8,128)S(1)}, u32[]{:S(2)}, u32[]{:S(2)}) collective-permute-start(f32[4,32,128]{2,1,0:T(8,128)S(1)} %get-tuple-element.43.refs_3_), channel_id=1, source_target_pairs={{0,24},{4,28},{8,16},{12,20},{16,8},{20,12},{24,0},{28,4},{1,25},{... | collective-permute-start | bytes 196616 | tf_op jit(solution)/shard_map/ppermute | solution.py:582
  26.3 5.2 %collective-permute-start.8 = (f32[4,32,128]{2,1,0:T(8,128)S(1)}, f32[4,32,128]{2,1,0:T(8,128)S(1)}, u32[]{:S(2)}, u32[]{:S(2)}) collective-permute-start(f32[4,32,128]{2,1,0:T(8,128)S(1)} %get-tuple-element.43.refs_3_), channel_id=1, source_target_pairs={{0,16},{4,20},{8,24},{12,28},{16,0},{20,4},{24,8},{28,12},{1,17},{... | collective-permute-start | bytes 196616 | tf_op jit(solution)/shard_map/ppermute | solution.py:582
  26.3 5.2 %collective-permute-start.9 = (f32[4,32,128]{2,1,0:T(8,128)S(1)}, f32[4,32,128]{2,1,0:T(8,128)S(1)}, u32[]{:S(2)}, u32[]{:S(2)}) collective-permute-start(f32[4,32,128]{2,1,0:T(8,128)S(1)} %get-tuple-element.43.refs_3_), channel_id=1, source_target_pairs={{0,8},{4,12},{8,0},{12,4},{16,24},{20,28},{24,16},{28,20},{1,9},{5... | collective-permute-start | bytes 196616 | tf_op jit(solution)/shard_map/ppermute | solution.py:582
  26.9 6.3 %collective-permute-start.10 = (f32[2,64,128]{2,1,0:T(8,128)S(1)}, f32[2,64,128]{2,1,0:T(8,128)S(1)}, u32[]{:S(2)}, u32[]{:S(2)}) collective-permute-start(f32[2,64,128]{2,1,0:T(8,128)S(1)} %get-tuple-element.44), channel_id=1, source_target_pairs={{0,8},{8,16},{12,4},{16,24},{20,12},{28,20},{1,9},{9,17},{13,5},{1... | collective-permute-start | bytes 196616 | tf_op jit(solution)/shard_map/ppermute | solution.py:629
  34.1 1.6 %collective-permute-start.11 = (f32[520,128]{1,0:T(8,128)S(1)}, f32[520,128]{1,0:T(8,128)S(1)}, u32[]{:S(2)}, u32[]{:S(2)}) collective-permute-start(f32[520,128]{1,0:T(8,128)S(1)} %get-tuple-element.46), channel_id=1, source_target_pairs={{0,1},{1,0},{2,3},{3,2},{4,5},{5,4},{6,7},{7,6},{8,9},{9,8},{10,11... | collective-permute-start | bytes 798728 | tf_op jit(solution)/shard_map/ppermute | solution.py:679
  35.8 14.1 %copy-start = (f32[8,4,16,128]{3,2,1,0:T(8,128)S(1)}, f32[8,4,16,128]{3,2,1,0:T(8,128)}, u32[]{:S(2)}) copy-start(f32[8,4,16,128]{3,2,1,0:T(8,128)} %refs_1_.3) | copy-start | bytes 786436
  35.8 7.9 %collective-permute-start.12 = (f32[208,128]{1,0:T(8,128)S(1)}, f32[208,128]{1,0:T(8,128)S(1)}, u32[]{:S(2)}, u32[]{:S(2)}) collective-permute-start(f32[208,128]{1,0:T(8,128)S(1)} %get-tuple-element.48), channel_id=1, source_target_pairs={{0,6},{1,7},{2,4},{3,5},{4,2},{5,3},{6,0},{7,1},{8,14},{9,15},{10,... | collective-permute-start | bytes 319496 | tf_op jit(solution)/shard_map/ppermute | solution.py:573
  39.9 4.8 %collective-permute-start.13 = (f32[208,128]{1,0:T(8,128)S(1)}, f32[208,128]{1,0:T(8,128)S(1)}, u32[]{:S(2)}, u32[]{:S(2)}) collective-permute-start(f32[208,128]{1,0:T(8,128)S(1)} %get-tuple-element.49), channel_id=1, source_target_pairs={{0,4},{1,5},{2,6},{3,7},{4,0},{5,1},{6,2},{7,3},{8,12},{9,13},{10,... | collective-permute-start | bytes 319496 | tf_op jit(solution)/shard_map/ppermute | solution.py:573
  39.9 5.5 %collective-permute-start.14 = (f32[208,128]{1,0:T(8,128)S(1)}, f32[208,128]{1,0:T(8,128)S(1)}, u32[]{:S(2)}, u32[]{:S(2)}) collective-permute-start(f32[208,128]{1,0:T(8,128)S(1)} %get-tuple-element.50), channel_id=1, source_target_pairs={{0,2},{1,3},{2,0},{3,1},{4,6},{5,7},{6,4},{7,5},{8,10},{9,11},{10,... | collective-permute-start | bytes 319496 | tf_op jit(solution)/shard_map/ppermute | solution.py:573
  45.5 4.5 %copy-start.1 = (f32[4,16,128]{2,1,0:T(8,128)S(1)}, f32[4,16,128]{2,1,0:T(8,128)}, u32[]{:S(2)}) copy-start(f32[4,16,128]{2,1,0:T(8,128)} %refs_2_.3) | copy-start | bytes 98308
  45.5 5.4 %collective-permute-start.15 = (f32[1,128]{1,0:T(1,128)S(1)}, f32[1,128]{1,0:T(1,128)S(1)}, u32[]{:S(2)}, u32[]{:S(2)}) collective-permute-start(f32[1,128]{1,0:T(1,128)S(1)} %squares.1), channel_id=1, source_target_pairs={{0,24},{4,28},{8,16},{12,20},{16,8},{20,12},{24,0},{28,4},{1,25},{... | collective-permute-start | bytes 1544 | tf_op jit(solution)/shard_map/ppermute | solution.py:582
  48.3 4.4 %collective-permute-start.16 = (f32[1,128]{1,0:T(1,128)S(1)}, f32[1,128]{1,0:T(1,128)S(1)}, u32[]{:S(2)}, u32[]{:S(2)}) collective-permute-start(f32[1,128]{1,0:T(1,128)S(1)} %squares.1), channel_id=1, source_target_pairs={{0,16},{4,20},{8,24},{12,28},{16,0},{20,4},{24,8},{28,12},{1,17},{... | collective-permute-start | bytes 1544 | tf_op jit(solution)/shard_map/ppermute | solution.py:582
  48.3 4.4 %collective-permute-start.17 = (f32[1,128]{1,0:T(1,128)S(1)}, f32[1,128]{1,0:T(1,128)S(1)}, u32[]{:S(2)}, u32[]{:S(2)}) collective-permute-start(f32[1,128]{1,0:T(1,128)S(1)} %squares.1), channel_id=1, source_target_pairs={{0,8},{4,12},{8,0},{12,4},{16,24},{20,28},{24,16},{28,20},{1,9},{5... | collective-permute-start | bytes 1544 | tf_op jit(solution)/shard_map/ppermute | solution.py:582
